TPU v7x, 32 devices: a whole 2x2x4 slice. The times are simulated.
32 devices in a mesh: rep: 2 (over y), expert: 8 (over z, x), group: 2 (over core).
Axes of the slice: x: 2, y: 2, z: 4, core: 2. Of those that a mesh axis runs over, the one named last changes fastest.
Arguments:
- tokens: bfloat16 [4096, 1024], P(('rep', 'expert', 'group')), parts along dimension 0, may hold values from -6 to 6
- w_gate: bfloat16 [16, 1024, 384], P('expert', 'group'), may hold values from -0.1875 to 0.1875
- w_up: bfloat16 [16, 1024, 384], P('expert', 'group'), may hold values from -0.1875 to 0.1875
- w_down: bfloat16 [16, 384, 1024], P('expert', 'group'), may hold values from -0.45927933 to 0.45927933
- route_ids: int32 [4096, 8], P(('rep', 'expert', 'group')), parts along dimension 0, may hold values from 0 to 15, all different within a row; in each aligned block of 128 rows (0 to 127, 128 to 255, ...) at most 80 rows name the same one
- route_scores: float32 [4096, 8], P(('rep', 'expert', 'group')), parts along dimension 0, may hold values from 0.05 to 1
- norm_gain: float32 [1024], replicated, may hold values from 0.5 to 1.5
- class_head: bfloat16 [1024, 2000], P(None, 'expert'), may hold values from -0.59765625 to 0.59765625
- targets: int32 [16, 2, 2000], P('rep', 'group', 'expert'), parts along dimension 0, may hold values 0 or 1
Outputs:
- token_grad: bfloat16 [4096, 1024], P(('rep', 'expert', 'group')), parts along dimension 0
- head_grad: float32 [2048, 2000], P('rep', 'expert'), parts along dimension 0
There are 2 independent parts, one for each index of `rep`. A program takes and returns all parts, laid end to end along the dimension named above; an argument that names none is the same for every part. Nothing has to cross between parts.
Inputs may be any that keep to these rules, and one draw needn't show every extreme that they name: `route_ids`: each row names 8 different experts; among the 128 tokens of one sequence no expert is named by more than 80 tokens, and in some sequences one expert is named by exactly 80.
All inputs are finite; a program needn't handle non-finite values. No bound on the sum of `targets` on one device may be relied on, other than what follows from the above.
Results may differ from a plain program's by a relative error of at most 0.022.
Values may be sent and summed in bfloat16 or wider, within the bound.
No kernel may reach another device: no remote copies, remote signals or barrier semaphores. Data moves between devices by JAX's collectives and lax.ppermute only.
A program may use at most 64 MiB of HBM per device.

v0:
```python
import jax
import jax.numpy as jnp
from jax import lax
from jax.sharding import PartitionSpec as P

LOSS_SCALE = 8.0
NORM_EPS = 1e-06


def body(tokens, w_gate, w_up, w_down, route_ids, route_scores, norm_gain, class_head, targets):
    rows_here, feature_dim = tokens.shape
    top_count = route_ids.shape[1]
    expert_count = lax.axis_size("expert")
    local_experts = w_gate.shape[0]
    experts_all = expert_count * local_experts
    capacity = min(rows_here, rows_here * top_count * 5 // (4 * experts_all))
    route_weight = route_scores / jnp.sum(route_scores, axis=-1, keepdims=True)
    expert_iota = jnp.arange(experts_all, dtype=jnp.int32)
    named_count = jnp.zeros((rows_here, experts_all), jnp.int32)
    for choice_k in range(top_count):
        named_count = named_count + (
            route_ids[:, choice_k][:, None] == expert_iota[None, :]
        ).astype(jnp.int32)
    before = jnp.cumsum(named_count, axis=0) - named_count
    position_cols = []
    for choice_k in range(top_count):
        hit_expert = route_ids[:, choice_k][:, None] == expert_iota[None, :]
        position_cols.append(jnp.sum(jnp.where(hit_expert, before, 0), axis=1))
    position = jnp.stack(position_cols, axis=1)
    slot_index = route_ids * capacity + position
    slot_iota = jnp.arange(experts_all * capacity, dtype=jnp.int32)
    place_rows = jnp.zeros((experts_all * capacity, rows_here), jnp.float32)
    place_weight = jnp.zeros((experts_all * capacity, rows_here), jnp.float32)
    for choice_k in range(top_count):
        slot_hit = slot_iota[:, None] == slot_index[:, choice_k][None, :]
        place_rows = place_rows + slot_hit.astype(jnp.float32)
        place_weight = place_weight + jnp.where(slot_hit, route_weight[:, choice_k][None, :], 0.0)
    place_rows = place_rows.astype(jnp.bfloat16)
    slot_shape = (expert_count, local_experts, capacity, feature_dim)
    outgoing = (
        jnp.dot(place_rows, tokens, preferred_element_type=jnp.float32)
        .astype(jnp.bfloat16)
        .reshape(slot_shape)
    )
    gate_full, up_full, down_full = (
        lax.all_gather(w_gate, "group", axis=1, tiled=True),
        lax.all_gather(w_up, "group", axis=1, tiled=True),
        lax.all_gather(w_down, "group", axis=1, tiled=True),
    )
    incoming = lax.all_to_all(outgoing, "expert", split_axis=0, concat_axis=0, tiled=True)
    gate_list = []
    up_list = []
    hidden_list = []
    for local in range(local_experts):
        expert_rows = incoming[:, local].reshape(-1, feature_dim)
        gate_act = jnp.dot(expert_rows, gate_full[local], preferred_element_type=jnp.float32)
        up_act = jnp.dot(expert_rows, up_full[local], preferred_element_type=jnp.float32)
        hidden = (gate_act * jax.nn.sigmoid(gate_act) * up_act).astype(jnp.bfloat16)
        gate_list.append(gate_act)
        up_list.append(up_act)
        hidden_list.append(hidden)
    out_list = []
    for local in range(local_experts):
        expert_out = jnp.dot(
            hidden_list[local], down_full[local], preferred_element_type=jnp.float32
        ).astype(jnp.bfloat16)
        out_list.append(expert_out.reshape(expert_count, capacity, feature_dim))
    expert_out_all = jnp.stack(out_list, axis=1)
    returned = lax.all_to_all(
        expert_out_all, "expert", split_axis=0, concat_axis=0, tiled=True
    ).reshape(-1, feature_dim)
    picked = jnp.take(returned, slot_index.reshape(-1), axis=0).reshape(
        rows_here, top_count, feature_dim
    )
    moe_out = jnp.einsum("tk,tkd->td", route_weight, picked.astype(jnp.float32))
    residual = tokens.astype(jnp.float32) + moe_out
    inv_rms = lax.rsqrt(jnp.mean(residual * residual, axis=-1, keepdims=True) + NORM_EPS)
    normed = residual * inv_rms * norm_gain
    pooled = jnp.mean(normed, axis=0, keepdims=True).astype(jnp.bfloat16)
    pooled_all = lax.all_gather(pooled, "expert", axis=0, tiled=True)
    logits = jnp.dot(pooled_all, class_head, preferred_element_type=jnp.float32)
    target_rows = targets.reshape(expert_count, -1).astype(jnp.float32)
    logit_grad = (LOSS_SCALE * (jax.nn.sigmoid(logits) - target_rows)).astype(jnp.bfloat16)
    head_part = lax.dot_general(
        pooled_all, logit_grad, (((0,), (0,)), ((), ())), preferred_element_type=jnp.float32
    )
    head_grad = lax.psum(head_part.astype(jnp.bfloat16), "group").astype(jnp.float32)
    pooled_terms = lax.dot_general(
        logit_grad, class_head, (((1,), (1,)), ((), ())), preferred_element_type=jnp.float32
    )
    pooled_grad = lax.psum_scatter(
        pooled_terms.astype(jnp.bfloat16), "expert", scatter_dimension=0, tiled=True
    ).astype(jnp.float32)
    scaled = norm_gain * pooled_grad / rows_here
    cube = inv_rms * inv_rms * inv_rms
    resid_grad = inv_rms * scaled - residual * cube * jnp.mean(
        residual * scaled, axis=-1, keepdims=True
    )
    slot_grad = jnp.dot(
        place_weight,
        resid_grad,
        precision=lax.Precision.HIGHEST,
        preferred_element_type=jnp.float32,
    )
    slot_grad = slot_grad.astype(jnp.bfloat16).reshape(slot_shape)
    grad_in = lax.all_to_all(slot_grad, "expert", split_axis=0, concat_axis=0, tiled=True)
    back_list = []
    for local in range(local_experts):
        grad_rows = grad_in[:, local].reshape(-1, feature_dim)
        gate_act = gate_list[local]
        sigmoid_gate = jax.nn.sigmoid(gate_act)
        down_back = lax.dot_general(
            grad_rows,
            down_full[local],
            (((1,), (1,)), ((), ())),
            preferred_element_type=jnp.float32,
        )
        silu_slope = sigmoid_gate * (1.0 + gate_act * (1.0 - sigmoid_gate))
        gate_grad = (down_back * up_list[local] * silu_slope).astype(jnp.bfloat16)
        up_grad = (down_back * gate_act * sigmoid_gate).astype(jnp.bfloat16)
        input_grad = lax.dot_general(
            gate_grad,
            gate_full[local],
            (((1,), (1,)), ((), ())),
            preferred_element_type=jnp.float32,
        )
        input_grad = input_grad + lax.dot_general(
            up_grad, up_full[local], (((1,), (1,)), ((), ())), preferred_element_type=jnp.float32
        )
        back_list.append(
            input_grad.astype(jnp.bfloat16).reshape(expert_count, capacity, feature_dim)
        )
    input_grad_all = jnp.stack(back_list, axis=1)
    grad_back = lax.all_to_all(
        input_grad_all, "expert", split_axis=0, concat_axis=0, tiled=True
    ).reshape(-1, feature_dim)
    grad_pick = jnp.take(grad_back, slot_index.reshape(-1), axis=0).reshape(
        rows_here, top_count, feature_dim
    )
    token_grad = (resid_grad + jnp.sum(grad_pick.astype(jnp.float32), axis=1)).astype(jnp.bfloat16)
    return (token_grad, head_grad)


def solution(mesh):
    in_specs = (
        P(("rep", "expert", "group"), None),
        P("expert", "group", None),
        P("expert", "group", None),
        P("expert", "group", None),
        P(("rep", "expert", "group"), None),
        P(("rep", "expert", "group"), None),
        P(),
        P(None, "expert"),
        P("rep", "group", "expert"),
    )
    out_specs = (P(("rep", "expert", "group"), None), P("rep", "expert"))
    return jax.shard_map(body, mesh=mesh, in_specs=in_specs, out_specs=out_specs, check_vma=False)
```

profile of v0, /device:TPU:0, one launch (start us, length us, event | category | flops | bytes accessed | tf_op | source)
XLA Modules:
  0.0 371.7 jit_solution(3693473801401391951)
XLA Ops:
  9.7 3.5 convolution_convert_fusion.1
  13.2 7.2 %all-to-all-start = ((bf16[8,2,80,1024]{3,2,1,0:T(8,128)(2,1)}), bf16[8,2,80,1024]{3,2,1,0:T(8,128)(2,1)S(1)}, u32[]{:S(2)}, u32[]{:S(2)}) async-start(bf16[8,2,80,1024]{3,2,1,0:T(8,128)(2,1)} %bitcast.142), calls=%async_computation | async-start | bytes 5242880 | tf_op jit(solution)/shard_map/all_to_all | solution.py:50
  22.7 57.3 %all-to-all-done = bf16[8,2,80,1024]{3,2,1,0:T(8,128)(2,1)S(1)} async-done(((bf16[8,2,80,1024]{3,2,1,0:T(8,128)(2,1)}), bf16[8,2,80,1024]{3,2,1,0:T(8,128)(2,1)S(1)}, u32[]{:S(2)}, u32[]{:S(2)}) %all-to-all-start) | async-done | bytes 2621472 | tf_op jit(solution)/shard_map/all_to_all | solution.py:50
  79.9 1.9 fusion.82
  81.8 3.4 fusion.12
  85.2 3.1 fusion.13
  88.3 1.9 fusion.17
  91.1 3.0 convolution_convert_fusion.3
  95.0 1.7 pad_maximum_fusion
  96.7 3.8 %all-to-all-start.1 = ((bf16[8,2,80,1024]{3,2,1,0:T(8,128)(2,1)}), bf16[8,2,80,1024]{3,2,1,0:T(8,128)(2,1)S(1)}, u32[]{:S(2)}, u32[]{:S(2)}) async-start(bf16[8,2,80,1024]{3,2,1,0:T(8,128)(2,1)} %pad_maximum_fusion), calls=%async_computation.1 | async-start | bytes 5242880 | tf_op jit(solution)/shard_map/all_to_all | solution.py:69
  101.5 58.6 %all-to-all-done.1 = bf16[8,2,80,1024]{3,2,1,0:T(8,128)(2,1)S(1)} async-done(((bf16[8,2,80,1024]{3,2,1,0:T(8,128)(2,1)}), bf16[8,2,80,1024]{3,2,1,0:T(8,128)(2,1)S(1)}, u32[]{:S(2)}, u32[]{:S(2)}) %all-to-all-start.1) | async-done | bytes 2621472 | tf_op jit(solution)/shard_map/all_to_all | solution.py:69
  160.1 5.4 %gather_fusion = bf16[1024,1024]{1,0:T(8,128)(2,1)} fusion(bf16[1280,1024]{1,0:T(8,128)(2,1)S(1)} %bitcast.140, s32[1024]{0:T(1024)S(1)} %fusion.71), kind=kCustom, calls=%fused_computation.clone | custom fusion | bytes 4198400 | tf_op jit(solution)/shard_map/jit(_take)/gather | solution.py:72
  165.5 2.4 fusion
  168.3 26.0 %all-gather = bf16[8192]{0:T(1024)(128)(2,1)S(1)} all-gather(bf16[1024]{0:T(1024)(128)(2,1)S(1)} %multiply_convert_fusion.12), channel_id=2, replica_groups=mesh['rep'=2,'expert'=8,'group'=2] {'expert'}, dimensions={0}, use_global_device_ids=true | all-gather | bytes 18432 | tf_op jit(solution)/shard_map/all_gather | solution.py:80
  194.8 33.8 %all-reduce = bf16[8,1024]{1,0:T(8,128)(2,1)S(1)} all-reduce(bf16[8,1024]{1,0:T(8,128)(2,1)S(1)} %convolution_convert_fusion.5), channel_id=3, replica_groups=mesh['rep'=2,'expert'=8,'group'=2] {'expert'}, use_global_device_ids=true, to_apply=%region_12.14.clone | all-reduce | flops 8192 | bytes 32768
  229.4 5.3 %convolution_convert_fusion = bf16[1280,1024]{1,0:T(8,128)(2,1)S(1)} fusion(f32[128]{0:T(128)S(1)} %get-tuple-element.16, f32[128]{0:T(128)S(1)} %get-tuple-element.17, f32[128]{0:T(128)S(1)} %get-tuple-element.18, f32[128]{0:T(128)S(1)} %get-tuple-element.19, f32[128]{0:T(128)S(1)} %get-tuple-element.20, f32[128]{0:T(128)S(1)} %get-tuple-element.21, ...), kind=kOutput, calls=%fused_computation.3 | convolution fusion | flops 2019131392 | bytes 3421696 | tf_op jit(solution)/shard_map/dot_general | solution.py:99
  234.7 51.1 %all_to_all.20 = bf16[8,2,80,1024]{3,2,1,0:T(8,128)(2,1)S(1)} all-to-all(bf16[8,2,80,1024]{3,2,1,0:T(8,128)(2,1)S(1)} %bitcast.143), channel_id=1, replica_groups=mesh['rep'=2,'expert'=8,'group'=2] {'expert'}, dimensions={0} | all-to-all | bytes 5242880 | tf_op jit(solution)/shard_map/all_to_all | solution.py:106
  294.7 1.7 pad_maximum_fusion.1
  296.5 3.7 all-to-all-start.3
  301.4 22.4 %all-reduce.3.cloned.1.call-done = bf16[1024,250]{1,0:T(8,128)(2,1)} async-done(((bf16[1024,250]{1,0:T(8,128)(2,1)}), bf16[1024,250]{1,0:T(8,128)(2,1)}) %all-reduce.3.cloned.1.call-update) | async-done | bytes 512016 | tf_op jit(solution)/shard_map/psum | solution.py:87
  323.8 2.1 convert_element_type.176
  325.9 30.0 %all-to-all-done.3 = bf16[8,2,80,1024]{3,2,1,0:T(8,128)(2,1)S(1)} async-done(((bf16[8,2,80,1024]{3,2,1,0:T(8,128)(2,1)}), bf16[8,2,80,1024]{3,2,1,0:T(8,128)(2,1)S(1)}, u32[]{:S(2)}, u32[]{:S(2)}) %all-to-all-start.3) | async-done | bytes 2621472 | tf_op jit(solution)/shard_map/all_to_all | solution.py:134
  355.9 5.4 %gather_fusion.1 = bf16[1024,1024]{1,0:T(8,128)(2,1)} fusion(bf16[1280,1024]{1,0:T(8,128)(2,1)S(1)} %bitcast.141, s32[1024]{0:T(1024)S(1)} %fusion.71), kind=kCustom, calls=%fused_computation.1.clone | custom fusion | bytes 4198400 | tf_op jit(solution)/shard_map/jit(_take)/gather | solution.py:137
  361.2 3.0 convert_reduce_fusion
  (93 shorter events, 20.0 us)
Async XLA Ops:
  7.2 187.2 %copy-start = (bf16[1024,250]{1,0:T(8,128)(2,1)S(1)}, bf16[1024,250]{1,0:T(8,128)(2,1)}, u32[]{:S(2)}) copy-start(bf16[1024,250]{1,0:T(8,128)(2,1)} %param.18) | copy-start | bytes 1536004
  13.2 66.7 %all-to-all-start = ((bf16[8,2,80,1024]{3,2,1,0:T(8,128)(2,1)}), bf16[8,2,80,1024]{3,2,1,0:T(8,128)(2,1)S(1)}, u32[]{:S(2)}, u32[]{:S(2)}) async-start(bf16[8,2,80,1024]{3,2,1,0:T(8,128)(2,1)} %bitcast.142), calls=%async_computation | async-start | bytes 5242880 | tf_op jit(solution)/shard_map/all_to_all | solution.py:50
  20.4 61.4 %all-gather.5.cloned.1.call-start = ((), (), s32[]{:S(2)}) async-start(), calls=%async_computation.4 | async-start | bytes 2359296 | tf_op jit(solution)/shard_map/all_gather | solution.py:46
  21.2 64.1 %all-gather.7.cloned.1.call-start = ((), (), s32[]{:S(2)}) async-start(), calls=%async_computation.5 | async-start | bytes 2359296 | tf_op jit(solution)/shard_map/all_gather | solution.py:47
  21.9 69.1 %all-gather.9.cloned.1.call-start = ((), (), s32[]{:S(2)}) async-start(), calls=%async_computation.6 | async-start | bytes 2359296 | tf_op jit(solution)/shard_map/all_gather | solution.py:48
  81.8 3.4 copy-start.5
  85.2 3.1 copy-start.4
  85.2 3.1 copy-start.11
  88.3 1.9 copy-start.9
  91.0 3.0 copy-start.16
  91.0 3.0 copy-start.18
  91.1 3.0 copy-start.13
  96.7 4.0 %copy-start.6 = (f32[128,8]{0,1:T(8,128)S(1)}, f32[128,8]{0,1:T(8,128)}, u32[]{:S(2)}) copy-start(f32[128,8]{0,1:T(8,128)} %param.16) | copy-start | bytes 12292
  96.7 4.2 %copy-start.15 = (u32[32]{0:T(128)S(1)}, u32[32]{0:T(128)}, u32[]{:S(2)}) copy-start(u32[32]{0:T(128)} %constant.41) | copy-start | bytes 388
  96.7 63.4 %all-to-all-start.1 = ((bf16[8,2,80,1024]{3,2,1,0:T(8,128)(2,1)}), bf16[8,2,80,1024]{3,2,1,0:T(8,128)(2,1)S(1)}, u32[]{:S(2)}, u32[]{:S(2)}) async-start(bf16[8,2,80,1024]{3,2,1,0:T(8,128)(2,1)} %pad_maximum_fusion), calls=%async_computation.1 | async-start | bytes 5242880 | tf_op jit(solution)/shard_map/all_to_all | solution.py:69
  165.5 2.4 copy-start.3
  165.5 2.6 copy-start.7
  167.9 61.5 %copy-start.1 = (f32[128,1,1024]{2,1,0:T(1,128)}, f32[128,1,1024]{2,1,0:T(1,128)S(1)}, u32[]{:S(2)}) copy-start(f32[128,1,1024]{2,1,0:T(1,128)S(1)} %fusion) | copy-start | bytes 1572868
  167.9 26.4 %copy-start.8 = (s32[8,1,250]{2,1,0:T(1,128)S(1)}, s32[8,1,250]{2,1,0:T(1,128)}, u32[]{:S(2)}) copy-start(s32[8,1,250]{2,1,0:T(1,128)} %param.19) | copy-start | bytes 24004
  285.8 2.3 copy-start.21
  287.2 1.7 copy-start.20
  296.5 59.4 %all-to-all-start.3 = ((bf16[8,2,80,1024]{3,2,1,0:T(8,128)(2,1)}), bf16[8,2,80,1024]{3,2,1,0:T(8,128)(2,1)S(1)}, u32[]{:S(2)}, u32[]{:S(2)}) async-start(bf16[8,2,80,1024]{3,2,1,0:T(8,128)(2,1)} %pad_maximum_fusion.1), calls=%async_computation.3 | async-start | bytes 5242880 | tf_op jit(solution)/shard_map/all_to_all | solution.py:134
  300.1 23.6 %all-reduce.3.cloned.1.call-start = ((), (), s32[]{:S(2)}) async-start(), calls=%async_computation.7 | async-start | bytes 1048576 | tf_op jit(solution)/shard_map/psum | solution.py:87
  361.2 3.0 copy-start.2
  (5 other events, 7.0 us)
Sparse Core Ops, SparseCore 0:
  22.8 11.2 all-gather.4
  35.6 10.9 all-gather.6
  48.2 10.9 all-gather.8
  303.6 20.1 all-reduce.2
where the time goes:
time: 372 us
  waiting for transfers between devices  170 us (46%)
  blocking collectives  111 us (30%)
  matrix products  31.4 us (8%)
  local copies, waits for them, and re-layouts  17.9 us (5%)
  starting transfers between devices  14.8 us (4%)
  between operations  14.1 us (4%)
  other arithmetic  12.2 us (3%)
    all_to_all x1, waiting for transfers between devices, body(): lax.all_to_all(expert_out_all, 'expert', split_axis=0, concat_axis=0, til...  58.6 us
    all_to_all x1, waiting for transfers between devices, body(): lax.all_to_all(outgoing, 'expert', split_axis=0, concat_axis=0, tiled=True)  57.3 us
    all_to_all x1, blocking collectives, body(): lax.all_to_all(slot_grad, 'expert', split_axis=0, concat_axis=0, tiled=True)  51.1 us
    unnamed x1, blocking collectives  33.8 us
    all_to_all x1, waiting for transfers between devices, body(): lax.all_to_all(input_grad_all, 'expert', split_axis=0, concat_axis=0, til...  30 us
    all_gather x1, blocking collectives, body(): pooled_all = lax.all_gather(pooled, 'expert', axis=0, tiled=True)  26 us
    psum x1, waiting for transfers between devices, body(): lax.psum(head_part.astype(jnp.bfloat16), 'group').astype(jnp.float32)  22.4 us
  transfers between devices with their start and end apart: 7, of which 4 were waited for; matrix products, arithmetic and copies ran while one was open for 4% of the time, Pallas kernels for 0%

commit v1 on v0

v1 whole, which is shorter than its diff:
```python
import jax
import jax.numpy as jnp
from jax import lax
from jax.sharding import PartitionSpec as P

LOSS_SCALE = 8.0
NORM_EPS = 1e-06
F32 = jnp.float32
BF16 = jnp.bfloat16


def dot(left, right):
    return jnp.dot(left, right, preferred_element_type=F32)


def dot_t(left, right):
    return lax.dot_general(left, right, (((1,), (1,)), ((), ())), preferred_element_type=F32)


def joined(shard, group_count, axis):
    if group_count != 2:
        return lax.all_gather(shard, "group", axis=axis, tiled=True)
    other = lax.ppermute(shard, "group", [(0, 1), (1, 0)])
    first = lax.axis_index("group") == 0
    return jnp.concatenate(
        [jnp.where(first, shard, other), jnp.where(first, other, shard)], axis=axis
    )


def body(tokens, w_gate, w_up, w_down, route_ids, route_scores, norm_gain, class_head, targets):
    rows_here, feature_dim = tokens.shape
    top_count = route_ids.shape[1]
    expert_count = lax.axis_size("expert")
    group_count = lax.axis_size("group")
    local_experts = w_gate.shape[0]
    experts_all = expert_count * local_experts

    route_weight = route_scores / jnp.sum(route_scores, axis=-1, keepdims=True)
    expert_iota = jnp.arange(experts_all, dtype=jnp.int32)
    weight_by = jnp.zeros((rows_here, experts_all), F32)
    for choice_k in range(top_count):
        hit = route_ids[:, choice_k][:, None] == expert_iota[None, :]
        weight_by = weight_by + jnp.where(hit, route_weight[:, choice_k][:, None], 0.0)
    weight_out = weight_by.reshape(rows_here, expert_count, local_experts).transpose(1, 0, 2)
    weight_in = lax.all_to_all(weight_out, "expert", split_axis=0, concat_axis=0, tiled=True)
    weight_in = weight_in.reshape(expert_count * rows_here, local_experts)

    tokens_all = lax.all_gather(tokens, "expert", axis=0, tiled=True)
    gate_full = joined(w_gate, group_count, 1)
    up_full = joined(w_up, group_count, 1)
    down_full = joined(w_down, group_count, 1)

    gate_list = []
    up_list = []
    part = None
    for local in range(local_experts):
        gate_act = dot(tokens_all, gate_full[local])
        up_act = dot(tokens_all, up_full[local])
        gate_list.append(gate_act)
        up_list.append(up_act)
        hidden = gate_act * jax.nn.sigmoid(gate_act) * up_act * weight_in[:, local][:, None]
        term = dot(hidden.astype(BF16), down_full[local])
        part = term if part is None else part + term
    moe_out = lax.psum_scatter(part.astype(BF16), "expert", scatter_dimension=0, tiled=True)
    moe_all = lax.all_gather(moe_out, "expert", axis=0, tiled=True)

    residual = tokens_all.astype(F32) + moe_all.astype(F32)
    inv_rms = lax.rsqrt(jnp.mean(residual * residual, axis=-1, keepdims=True) + NORM_EPS)
    normed = residual * inv_rms * norm_gain
    pooled = jnp.mean(normed.reshape(expert_count, rows_here, feature_dim), axis=1).astype(BF16)
    logits = dot(pooled, class_head)
    target_rows = targets.reshape(expert_count, -1).astype(F32)
    logit_grad = (LOSS_SCALE * (jax.nn.sigmoid(logits) - target_rows)).astype(BF16)
    pooled_terms = dot_t(logit_grad, class_head)
    pooled_grad = lax.psum(pooled_terms.astype(BF16), "expert").astype(F32)

    both = jnp.concatenate([pooled, logit_grad], axis=1)
    if group_count == 2:
        both = jnp.concatenate([both, lax.ppermute(both, "group", [(0, 1), (1, 0)])], axis=0)
    else:
        both = lax.all_gather(both, "group", axis=0, tiled=True)
    head_grad = lax.dot_general(
        both[:, :feature_dim],
        both[:, feature_dim:],
        (((0,), (0,)), ((), ())),
        preferred_element_type=F32,
    )

    scaled = jnp.repeat(norm_gain * pooled_grad / rows_here, rows_here, axis=0)
    cube = inv_rms * inv_rms * inv_rms
    slope = cube * jnp.mean(residual * scaled, axis=-1, keepdims=True)
    resid_grad = inv_rms * scaled - residual * slope
    grad_rows = resid_grad.astype(BF16)

    back = None
    for local in range(local_experts):
        gate_act = gate_list[local]
        sigmoid_gate = jax.nn.sigmoid(gate_act)
        down_back = dot_t(grad_rows, down_full[local]) * weight_in[:, local][:, None]
        silu_slope = sigmoid_gate * (1.0 + gate_act * (1.0 - sigmoid_gate))
        gate_grad = (down_back * up_list[local] * silu_slope).astype(BF16)
        up_grad = (down_back * gate_act * sigmoid_gate).astype(BF16)
        term = dot_t(gate_grad, gate_full[local]) + dot_t(up_grad, up_full[local])
        back = term if back is None else back + term
    input_grad = lax.psum_scatter(back.astype(BF16), "expert", scatter_dimension=0, tiled=True)
    own = lax.dynamic_slice_in_dim(
        resid_grad, lax.axis_index("expert") * rows_here, rows_here, axis=0
    )
    token_grad = (own + input_grad.astype(F32)).astype(BF16)
    return (token_grad, head_grad)


def solution(mesh):
    in_specs = (
        P(("rep", "expert", "group"), None),
        P("expert", "group", None),
        P("expert", "group", None),
        P("expert", "group", None),
        P(("rep", "expert", "group"), None),
        P(("rep", "expert", "group"), None),
        P(),
        P(None, "expert"),
        P("rep", "group", "expert"),
    )
    out_specs = (P(("rep", "expert", "group"), None), P("rep", "expert"))
    return jax.shard_map(body, mesh=mesh, in_specs=in_specs, out_specs=out_specs, check_vma=False)
```

time: 372 us -> 320 us (0.86)
  blocking collectives: 111 us -> 34.7 us
  waiting for transfers between devices: 170 us -> 218 us
  local copies, waits for them, and re-layouts: 17.9 us -> 5.84 us
  matrix products: 31.4 us -> 21.2 us
  starting transfers between devices: 14.8 us -> 8.13 us
  other arithmetic: 12.2 us -> 16.8 us
    all_to_all x3 -> x1, waiting for transfers between devices: 146 us -> 6.47 us  [body(): lax.all_to_all(weight_out, 'expert', split_axis=0, concat_axis=0, tiled=T...]
    reduce_scatter x0 -> x2, waiting for transfers between devices: none -> 129 us  [the longest x1 66.2 us: body(): lax.psum_scatter(part.astype(BF16), 'expert', scatter_dimension=0, tiled=...]
    all_gather x3 -> x2, waiting for transfers between devices: 0.02 us -> 81.2 us  [the longest x1 50.5 us: body(): moe_all = lax.all_gather(moe_out, 'expert', axis=0, tiled=True)]
    all_to_all x1 -> x0, blocking collectives: 51.1 us -> none  [body(): lax.all_to_all(slot_grad, 'expert', split_axis=0, concat_axis=0, tiled=True)]
    psum x0 -> x1, blocking collectives: none -> 34.7 us  [body(): pooled_grad = lax.psum(pooled_terms.astype(BF16), 'expert').astype(F32)]
    unnamed x1 -> x0, blocking collectives: 33.8 us -> none
    all_gather x1 -> x0, blocking collectives: 26 us -> none  [body(): pooled_all = lax.all_gather(pooled, 'expert', axis=0, tiled=True)]
    psum x1 -> x0, waiting for transfers between devices: 22.4 us -> none  [body(): lax.psum(head_part.astype(jnp.bfloat16), 'group').astype(jnp.float32)]
  transfers between devices with their start and end apart: 7 -> 9, of which waited for: 4 -> 6; matrix products, arithmetic and copies ran while one was open for 4% -> 3% of each run, Pallas kernels for 0% -> 0%
where the time goes in v1:
time: 320 us; the launch traced here: 319 us
  waiting for transfers between devices  218 us (68%)
  blocking collectives  34.7 us (11%)
  matrix products  21.2 us (7%)
  other arithmetic  16.8 us (5%)
  between operations  14.1 us (4%)
  starting transfers between devices  8.13 us (3%)
  local copies, waits for them, and re-layouts  5.84 us (2%)
    reduce_scatter x1, waiting for transfers between devices, body(): lax.psum_scatter(part.astype(BF16), 'expert', scatter_dimension=0, tiled=...  66.2 us
    reduce_scatter x1, waiting for transfers between devices, body(): lax.psum_scatter(back.astype(BF16), 'expert', scatter_dimension=0, tiled=...  62.6 us
    all_gather x1, waiting for transfers between devices, body(): moe_all = lax.all_gather(moe_out, 'expert', axis=0, tiled=True)  50.5 us
    psum x1, blocking collectives, body(): pooled_grad = lax.psum(pooled_terms.astype(BF16), 'expert').astype(F32)  34.7 us
    all_gather x1, waiting for transfers between devices, body(): tokens_all = lax.all_gather(tokens, 'expert', axis=0, tiled=True)  30.7 us
    dot_general x7, matrix products, dot(): return jnp.dot(left, right, preferred_element_type=F32)  10.3 us
    dot_general x7, matrix products, dot_t(): lax.dot_general(left, right, (((1,), (1,)), ((), ())), preferred_element_...  9.62 us
    all_to_all x1, starting transfers between devices, body(): lax.all_to_all(weight_out, 'expert', split_axis=0, concat_axis=0, tiled=T...  7.23 us
  transfers between devices with their start and end apart: 9, of which 6 were waited for; matrix products, arithmetic and copies ran while one was open for 3% of the time, Pallas kernels for 0%

profile of v1, /device:TPU:0, one launch (start us, length us, event | category | flops | bytes accessed | tf_op | source)
XLA Modules:
  0.0 319.2 jit_solution(13226647802396808278)
XLA Ops:
  11.6 7.2 %all-to-all-start = ((f32[8,128,2]{1,2,0:T(2,128)}), f32[8,128,2]{1,2,0:T(2,128)S(1)}, u32[]{:S(2)}, u32[]{:S(2)}) async-start(f32[8,128,2]{1,2,0:T(2,128)} %fusion.75), calls=%async_computation | async-start | bytes 16384 | tf_op jit(solution)/shard_map/all_to_all | solution.py:45
  19.0 6.5 %all-to-all-done = f32[8,128,2]{1,2,0:T(2,128)S(1)} async-done(((f32[8,128,2]{1,2,0:T(2,128)}), f32[8,128,2]{1,2,0:T(2,128)S(1)}, u32[]{:S(2)}, u32[]{:S(2)}) %all-to-all-start) | async-done | bytes 8224 | tf_op jit(solution)/shard_map/all_to_all | solution.py:45
  25.5 2.2 broadcast_select_fusion.4
  27.7 1.3 broadcast_select_fusion.2
  29.1 2.4 broadcast_select_fusion
  31.4 30.7 %all-gather.3.cloned.1.call-done = bf16[1024,1024]{1,0:T(8,128)(2,1)} async-done(((bf16[128,1024]{1,0:T(8,128)(2,1)}), bf16[1024,1024]{1,0:T(8,128)(2,1)}) %all-gather.3.cloned.1.call-update) | async-done | bytes 2097168 | tf_op jit(solution)/shard_map/all_gather | solution.py:48
  62.2 2.9 fusion.96
  67.0 1.4 fusion.36
  69.5 1.0 fusion.63
  70.6 1.1 copy-done.13
  71.7 2.7 add_convert_fusion.1
  74.5 66.2 %reduce-scatter.3.cloned.1.call-done = bf16[128,1024]{1,0:T(8,128)(2,1)} async-done(((bf16[1024,1024]{1,0:T(8,128)(2,1)}), bf16[128,1024]{1,0:T(8,128)(2,1)}) %reduce-scatter.3.cloned.1.call-update) | async-done | bytes 262160 | tf_op jit(solution)/shard_map/reduce_scatter | solution.py:64
  140.8 50.5 %all-gather.5.cloned.1.call-done = bf16[1024,1024]{1,0:T(8,128)(2,1)} async-done(((bf16[128,1024]{1,0:T(8,128)(2,1)}), bf16[1024,1024]{1,0:T(8,128)(2,1)}) %all-gather.5.cloned.1.call-update) | async-done | bytes 2097168 | tf_op jit(solution)/shard_map/all_gather | solution.py:65
  191.4 2.5 multiply_reduce_fusion
  195.4 34.7 %psum.7 = bf16[8,1024]{1,0:T(8,128)(2,1)S(1)} all-reduce(bf16[8,1024]{1,0:T(8,128)(2,1)S(1)} %convolution_convert_fusion), channel_id=1, replica_groups=mesh['rep'=2,'expert'=8,'group'=2] {'expert'}, use_global_device_ids=true, to_apply=%region_4.5 | all-reduce | flops 8192 | bytes 32768 | tf_op jit(solution)/shard_map/psum | solution.py:75
  230.1 2.5 fusion.1
  238.0 1.6 fusion.34
  239.7 1.3 fusion.32
  241.1 1.3 fusion.38
  242.5 3.1 add_convert_fusion
  245.7 1.2 collective-permute-done.3
  246.9 1.3 fusion.67
  248.2 62.6 %reduce-scatter.5.cloned.1.call-done = bf16[128,1024]{1,0:T(8,128)(2,1)} async-done(((bf16[1024,1024]{1,0:T(8,128)(2,1)}), bf16[128,1024]{1,0:T(8,128)(2,1)}) %reduce-scatter.5.cloned.1.call-update) | async-done | bytes 262160 | tf_op jit(solution)/shard_map/reduce_scatter | solution.py:105
  310.8 1.9 add_convert_fusion.2
  (89 shorter events, 14.9 us)
Async XLA Ops:
  7.2 187.8 %copy-start = (bf16[1024,250]{1,0:T(8,128)(2,1)S(1)}, bf16[1024,250]{1,0:T(8,128)(2,1)}, u32[]{:S(2)}) copy-start(bf16[1024,250]{1,0:T(8,128)(2,1)} %param.16) | copy-start | bytes 1536004
  7.2 55.0 %all-gather.3.cloned.1.call-start = ((), (), s32[]{:S(2)}) async-start(), calls=%async_computation.3 | async-start | bytes 2359296 | tf_op jit(solution)/shard_map/all_gather | solution.py:48
  7.9 17.6 %collective-permute-start = (bf16[2,512,384]{2,1,0:T(8,128)(2,1)}, bf16[2,512,384]{2,1,0:T(8,128)(2,1)S(1)}, u32[]{:S(2)}, u32[]{:S(2)}) collective-permute-start(bf16[2,512,384]{2,1,0:T(8,128)(2,1)} %param.10), channel_id=1, source_target_pairs={{0,1},{1,0},{2,3},{3,2},{4,5},{5,4},{6,7},{7,6},{8,9},{9,8},{10,11... | collective-permute-start | bytes 2359304 | tf_op jit(solution)/shard_map/ppermute | solution.py:23
  8.4 19.3 %collective-permute-start.1 = (bf16[2,512,384]{2,1,0:T(8,128)(2,1)}, bf16[2,512,384]{2,1,0:T(8,128)(2,1)S(1)}, u32[]{:S(2)}, u32[]{:S(2)}) collective-permute-start(bf16[2,512,384]{2,1,0:T(8,128)(2,1)} %param.11), channel_id=1, source_target_pairs={{0,1},{1,0},{2,3},{3,2},{4,5},{5,4},{6,7},{7,6},{8,9},{9,8},{10,11... | collective-permute-start | bytes 2359304 | tf_op jit(solution)/shard_map/ppermute | solution.py:23
  11.6 13.8 %all-to-all-start = ((f32[8,128,2]{1,2,0:T(2,128)}), f32[8,128,2]{1,2,0:T(2,128)S(1)}, u32[]{:S(2)}, u32[]{:S(2)}) async-start(f32[8,128,2]{1,2,0:T(2,128)} %fusion.75), calls=%async_computation | async-start | bytes 16384 | tf_op jit(solution)/shard_map/all_to_all | solution.py:45
  18.8 121.9 %reduce-scatter.3.cloned.1.call-start = ((), (), s32[]{:S(2)}) async-start(), calls=%async_computation.4 | async-start | bytes 2359296 | tf_op jit(solution)/shard_map/reduce_scatter | solution.py:64
  18.9 10.2 %collective-permute-start.2 = (bf16[2,192,1024]{2,1,0:T(8,128)(2,1)}, bf16[2,192,1024]{2,1,0:T(8,128)(2,1)}, u32[]{:S(2)}, u32[]{:S(2)}) collective-permute-start(bf16[2,192,1024]{2,1,0:T(8,128)(2,1)} %param.12), channel_id=1, source_target_pairs={{0,1},{1,0},{2,3},{3,2},{4,5},{5,4},{6,7},{7,6},{8,9},{9,8},{10,11... | collective-permute-start | bytes 2359304 | tf_op jit(solution)/shard_map/ppermute | solution.py:23
  25.5 2.3 copy-start.19
  62.2 2.9 copy-start.1
  62.2 2.9 copy-start.15
  62.2 2.9 copy-start.17
  65.1 1.7 copy-start.7
  65.1 1.9 copy-start.9
  66.2 2.2 copy-start.25
  74.5 116.9 %all-gather.5.cloned.1.call-start = ((), (), s32[]{:S(2)}) async-start(), calls=%async_computation.5 | async-start | bytes 2359296 | tf_op jit(solution)/shard_map/all_gather | solution.py:65
  140.8 53.1 %copy-start.21 = (f32[1024]{0:T(1024)S(1)}, f32[1024]{0:T(1024)}, u32[]{:S(2)}) copy-start(f32[1024]{0:T(1024)} %param.15) | copy-start | bytes 12292
  140.8 170.0 %reduce-scatter.5.cloned.1.call-start = ((), (), s32[]{:S(2)}) async-start(), calls=%async_computation.6 | async-start | bytes 2359296 | tf_op jit(solution)/shard_map/reduce_scatter | solution.py:105
  191.4 2.5 copy-start.3
  230.1 2.5 copy-start.4
  234.0 2.0 copy-start.2
  235.9 1.7 copy-start.24
  235.9 2.1 copy-start.26
  238.0 1.6 copy-start.18
  245.6 1.3 collective-permute-start.3
  (12 other events, 15.4 us)
Sparse Core Ops, SparseCore 0:
  10.1 51.9 all-gather.2
  74.6 66.1 reduce-scatter.2
  142.9 48.4 all-gather.4
  245.7 65.0 reduce-scatter.4

commit v2 on v1

v2 whole, which is shorter than its diff:
```python
import functools

import jax
import jax.numpy as jnp
from jax import lax
from jax.experimental import pallas as pl
from jax.experimental.pallas import tpu as pltpu
from jax.sharding import PartitionSpec as P

LOSS_SCALE = 8.0
NORM_EPS = 1e-06
F32 = jnp.float32
BF16 = jnp.bfloat16
LANES = 128
VMEM_LIMIT = 32 * 1024 * 1024


def dot(left, right):
    return jnp.dot(left, right, preferred_element_type=F32)


def dot_t(left, right):
    return lax.dot_general(left, right, (((1,), (1,)), ((), ())), preferred_element_type=F32)


def call(kernel, outs, *args, flops=0, scratch=(), in_any=False):
    if in_any:
        specs = [pl.BlockSpec(memory_space=pl.ANY)] * len(args)
    else:
        specs = [pl.BlockSpec(memory_space=pltpu.VMEM)] * len(args)
        args = [pltpu.with_memory_space_constraint(a, pltpu.VMEM) for a in args]
    size = sum(a.size * a.dtype.itemsize for a in args)
    return pl.pallas_call(
        kernel,
        out_shape=[pltpu.VMEM(shape, dtype) for shape, dtype in outs],
        in_specs=specs,
        out_specs=[pl.BlockSpec(memory_space=pltpu.VMEM)] * len(outs),
        scratch_shapes=list(scratch),
        compiler_params=pltpu.CompilerParams(vmem_limit_bytes=VMEM_LIMIT),
        cost_estimate=pl.CostEstimate(flops=flops, bytes_accessed=size, transcendentals=0),
    )(*args)


class Ring:
    def __init__(self, expert_count, group_count):
        self.count = expert_count
        self.half = expert_count // 2
        self.snake = group_count == 2
        if self.snake:
            self.order = list(range(0, expert_count, 2)) + list(range(expert_count - 1, 0, -2))
        else:
            self.order = list(range(expert_count))

    def send(self, value, distance):
        pairs = [
            (self.order[i], self.order[(i + distance) % self.count]) for i in range(self.count)
        ]
        return lax.ppermute(value, "expert", pairs)

    def device_at(self, distance):
        here = lax.axis_index("expert")
        count = self.count
        if self.snake:
            here = jnp.where(here % 2 == 0, here // 2, count - 1 - here // 2)
        there = lax.rem(here + distance % count, count)
        if self.snake:
            there = jnp.where(there < self.half, 2 * there, 2 * (count - 1 - there) + 1)
        return there

    def gather(self, block, use):
        mid = block.shape[0] // 2
        from_left = from_right = block
        use((0,), (block,))
        for step in range(1, self.half):
            from_left = self.send(from_left, 1)
            from_right = self.send(from_right, -1)
            use((-step, step), (from_left, from_right))
        top = self.send(from_left[:mid], 1)
        bottom = self.send(from_right[mid:], -1)
        use((self.half,), (top, bottom))

    def scatter(self, ends, partial):
        from_left = self.send(ends[0], 1)
        from_right = self.send(ends[1], -1)
        for step in range(self.half - 1, 0, -1):
            right = add_rows(partial(step), from_left, 0)
            left = add_rows(partial(-step), from_right, 1)
            from_left = self.send(right, 1)
            from_right = self.send(left, -1)
        return from_left, from_right


def add_rows(block, arrived, at_end):
    rows, cols = block.shape
    some = arrived.shape[0]

    def kernel(block_ref, arrived_ref, out_ref):
        if some == rows:
            out_ref[...] = (block_ref[...] + arrived_ref[...].astype(F32)).astype(BF16)
            return
        begin = rows - some if at_end else 0
        rest = 0 if at_end else some
        own = pl.ds(begin, some)
        other = pl.ds(rest, rows - some)
        out_ref[own, :] = (block_ref[own, :] + arrived_ref[...].astype(F32)).astype(BF16)
        out_ref[other, :] = block_ref[other, :].astype(BF16)

    return call(kernel, [((rows, cols), BF16)], block, arrived)[0]


def pack_kernel(ids_ref, scores_ref, tokens_ref, out_ref):
    rows, cols = tokens_ref.shape
    scores = scores_ref[...]
    ids = ids_ref[...]
    route_weight = scores / jnp.sum(scores, axis=-1, keepdims=True)
    lane = lax.broadcasted_iota(jnp.int32, (rows, LANES), 1)
    weight_by = jnp.zeros((rows, LANES), F32)
    for choice_k in range(scores.shape[1]):
        one = slice(choice_k, choice_k + 1)
        weight_by = weight_by + jnp.where(ids[:, one] == lane, route_weight[:, one], 0.0)
    high = weight_by.astype(BF16).astype(F32)
    low = pltpu.roll(weight_by - high, LANES // 2, 1)
    out_ref[:, :cols] = tokens_ref[...]
    out_ref[:, cols:] = (high + low).astype(BF16)


def assemble_kernel(shards, local_experts, *refs):
    gates, ups, downs = refs[:shards], refs[shards : 2 * shards], refs[2 * shards : 3 * shards]
    wide_ref, down_ref, sems = refs[3 * shards :]
    hidden_dim = gates[0].shape[2]
    copies = []

    def start(source, target):
        copies.append(pltpu.make_async_copy(source, target, sems.at[len(copies)]))
        copies[-1].start()

    for i in range(shards):
        place = 0
        if shards == 2:
            group = lax.axis_index("group")
            place = group if i == 0 else 1 - group
        depth, height = gates[i].shape[1], downs[i].shape[1]
        rows = pl.ds(pl.multiple_of(place * depth, 16), depth)
        for local in range(local_experts):
            begin = local * 2 * hidden_dim
            start(gates[i].at[local], wide_ref.at[rows, pl.ds(begin, hidden_dim)])
            start(ups[i].at[local], wide_ref.at[rows, pl.ds(begin + hidden_dim, hidden_dim)])
            top = pl.multiple_of(local * hidden_dim + place * height, 16)
            start(downs[i].at[local], down_ref.at[pl.ds(top, height), :])
    for copy in copies:
        copy.wait()


def full_weights(w_gate, w_up, w_down, group_count):
    local_experts, _, hidden_dim = w_gate.shape
    feature_dim = w_down.shape[2]
    shards = []
    for shard in (w_gate, w_up, w_down):
        if group_count == 2:
            shards += [shard, lax.ppermute(shard, "group", [(0, 1), (1, 0)])]
        else:
            shards += [lax.all_gather(shard, "group", axis=1, tiled=True)]
    count = len(shards) // 3
    return call(
        functools.partial(assemble_kernel, count, local_experts),
        [
            ((feature_dim, 2 * local_experts * hidden_dim), BF16),
            ((local_experts * hidden_dim, feature_dim), BF16),
        ],
        *shards,
        scratch=[pltpu.SemaphoreType.DMA((3 * count * local_experts,))],
        in_any=True,
    )


def body(tokens, w_gate, w_up, w_down, route_ids, route_scores, norm_gain, class_head, targets):
    rows_here, feature_dim = tokens.shape
    expert_count = lax.axis_size("expert")
    group_count = lax.axis_size("group")
    local_experts, _, hidden_dim = w_gate.shape
    pair_dim = 2 * hidden_dim
    ring = Ring(expert_count, group_count)
    block = (rows_here, feature_dim)
    mid = rows_here // 2

    packed = call(
        pack_kernel,
        [((rows_here, feature_dim + LANES), BF16)],
        route_ids,
        route_scores,
        tokens,
    )[0]
    wide, down = full_weights(w_gate, w_up, w_down, group_count)

    def rows_of(refs):
        return jnp.concatenate([ref[...] for ref in refs], axis=0) if len(refs) > 1 else refs[0][...]

    def forward_kernel(halves, count, *refs):
        token_refs, (wide_ref, down_ref), outs = refs[:count], refs[count : count + 2], refs[count + 2 :]
        x = rows_of([ref.at[:, :feature_dim] for ref in token_refs])
        weights = rows_of([ref.at[:, feature_dim:] for ref in token_refs]).astype(F32)
        lane = lax.broadcasted_iota(jnp.int32, weights.shape, 1)
        total = None
        for local in range(local_experts):
            expert = lax.axis_index("expert") * local_experts + local
            mine = (lane == expert) | (lane == expert + LANES // 2)
            scale = jnp.sum(jnp.where(mine, weights, 0.0), axis=1, keepdims=True)
            act = dot(x, wide_ref[:, pl.ds(local * pair_dim, pair_dim)])
            gate_act, up_act = act[:, :hidden_dim], act[:, hidden_dim:]
            sigmoid_gate = jax.nn.sigmoid(gate_act)
            silu = gate_act * sigmoid_gate * scale
            slope = sigmoid_gate * (1.0 + gate_act * (1.0 - sigmoid_gate)) * scale
            cols = pl.ds(local * hidden_dim, hidden_dim)
            outs[0][:, cols] = (up_act * slope).astype(BF16)
            outs[1][:, cols] = silu.astype(BF16)
            hidden = (silu * up_act).astype(BF16)
            term = dot(hidden, down_ref[cols, :])
            total = term if total is None else total + term
        rows = total.shape[0] // len(outs[2:])
        for i, out in enumerate(outs[2:]):
            out[...] = total[i * rows : (i + 1) * rows].astype(out.dtype)

    tokens_at, saved_at, part_at = {}, {}, {}
    flops = 2 * rows_here * feature_dim * hidden_dim * local_experts * 3

    def forward(distances, blocks):
        ends = distances == (ring.half,)
        rows = sum(b.shape[0] for b in blocks)
        outs = [((rows, local_experts * hidden_dim), BF16)] * 2
        outs += [((mid, feature_dim), BF16)] * 2 if ends else [(block, F32)] * len(blocks)
        result = call(
            functools.partial(forward_kernel, ends, len(blocks)),
            outs,
            *blocks,
            wide,
            down,
            flops=flops * rows // rows_here,
        )
        tokens_at[distances] = blocks
        saved_at[distances] = result[:2]
        if ends:
            part_at["ends"] = result[2:]
        else:
            part_at.update(zip(distances, result[2:]))

    ring.gather(packed, forward)
    from_left, from_right = ring.scatter(part_at["ends"], lambda k: part_at[k])

    def moe_kernel(part_ref, left_ref, right_ref, out_ref):
        arrived = left_ref[...].astype(F32) + right_ref[...].astype(F32)
        out_ref[...] = (part_ref[...] + arrived).astype(BF16)

    moe_out = call(moe_kernel, [(block, BF16)], part_at[0], from_left, from_right)[0]

    gain = norm_gain.reshape(1, feature_dim)
    moe_at, mean_at = {}, {}

    def residual_of(token_refs, moe_refs):
        token_rows = rows_of([ref.at[:, :feature_dim] for ref in token_refs]).astype(F32)
        return token_rows + rows_of(moe_refs).astype(F32)

    def inv_rms_of(residual):
        return lax.rsqrt(jnp.mean(residual * residual, axis=-1, keepdims=True) + NORM_EPS)

    def norm_kernel(distances, count, *refs):
        residual = residual_of(refs[:count], refs[count : 2 * count])
        gain_ref, so_far, out_ref = refs[2 * count :]
        normed = residual * inv_rms_of(residual) * gain_ref[...]
        pooled = so_far[...]
        row = lax.broadcasted_iota(jnp.int32, pooled.shape, 0)
        for i, k in enumerate(distances):
            part = normed[i * rows_here : (i + 1) * rows_here]
            mean = jnp.mean(part, axis=0, keepdims=True)
            pooled = jnp.where(row == ring.device_at(k), mean, pooled)
        out_ref[...] = pooled

    pooled_shape = (expert_count, feature_dim)
    mean_at["pooled"] = jnp.zeros(pooled_shape, F32)

    def norm(distances, blocks):
        moe_at[distances] = blocks
        mean_at["pooled"] = call(
            functools.partial(norm_kernel, distances, len(blocks)),
            [(pooled_shape, F32)],
            *tokens_at[distances],
            *blocks,
            gain,
            mean_at["pooled"],
        )[0]

    ring.gather(moe_out, norm)
    pooled = mean_at["pooled"].astype(BF16)
    logits = dot(pooled, class_head)
    target_rows = targets.reshape(expert_count, -1).astype(F32)
    logit_grad = (LOSS_SCALE * (jax.nn.sigmoid(logits) - target_rows)).astype(BF16)
    pooled_grad = dot_t(logit_grad, class_head)
    distance = 1
    while distance < expert_count:
        pairs = [(e, e ^ distance) for e in range(expert_count)]
        mine = pooled_grad.astype(BF16)
        other = lax.ppermute(mine, "expert", pairs)
        pooled_grad = mine.astype(F32) + other.astype(F32)
        distance *= 2

    both = jnp.concatenate([pooled, logit_grad], axis=1)
    if group_count == 2:
        both = jnp.concatenate([both, lax.ppermute(both, "group", [(0, 1), (1, 0)])], axis=0)
    else:
        both = lax.all_gather(both, "group", axis=0, tiled=True)
    head_grad = lax.dot_general(
        both[:, :feature_dim],
        both[:, feature_dim:],
        (((0,), (0,)), ((), ())),
        preferred_element_type=F32,
    )

    def backward_kernel(distances, count, *refs):
        residual = residual_of(refs[:count], refs[count : 2 * count])
        gate_save, up_save, grad_ref, gain_ref, wide_ref, down_ref = refs[2 * count : 2 * count + 6]
        outs = refs[2 * count + 6 :]
        inv_rms = inv_rms_of(residual)
        cube = inv_rms * inv_rms * inv_rms
        parts = []
        for i, k in enumerate(distances):
            rows = slice(i * rows_here, (i + 1) * rows_here)
            scaled = gain_ref[...] * grad_ref[pl.ds(ring.device_at(k), 1), :] / rows_here
            slope = cube[rows] * jnp.mean(residual[rows] * scaled, axis=-1, keepdims=True)
            parts.append(inv_rms[rows] * scaled - residual[rows] * slope)
        resid_grad = jnp.concatenate(parts, axis=0) if len(parts) > 1 else parts[0]
        down_back = dot_t(resid_grad.astype(BF16), down_ref[...])
        total = resid_grad if distances == (0,) else None
        for local in range(local_experts):
            cols = slice(local * hidden_dim, (local + 1) * hidden_dim)
            gate_grad = (down_back[:, cols] * gate_save[:, cols].astype(F32)).astype(BF16)
            up_grad = (down_back[:, cols] * up_save[:, cols].astype(F32)).astype(BF16)
            grads = jnp.concatenate([gate_grad, up_grad], axis=1)
            term = dot_t(grads, wide_ref[:, pl.ds(local * pair_dim, pair_dim)])
            total = term if total is None else total + term
        rows = total.shape[0] // len(outs)
        for i, out in enumerate(outs):
            out[...] = total[i * rows : (i + 1) * rows].astype(out.dtype)

    back_at = {}

    def backward(distances):
        blocks = tokens_at[distances]
        ends = distances == (ring.half,)
        outs = [((mid, feature_dim), BF16)] * 2 if ends else [(block, F32)] * len(blocks)
        result = call(
            functools.partial(backward_kernel, distances, len(blocks)),
            outs,
            *blocks,
            *moe_at[distances],
            *saved_at[distances],
            pooled_grad,
            gain,
            wide,
            down,
            flops=flops * len(distances),
        )
        if ends:
            back_at["ends"] = result
        else:
            back_at.update(zip(distances, result))

    for step in range(ring.half, 0, -1):
        backward((step,) if step == ring.half else (-step, step))
    backward((0,))
    from_left, from_right = ring.scatter(back_at["ends"], lambda k: back_at[k])
    token_grad = call(moe_kernel, [(block, BF16)], back_at[0], from_left, from_right)[0]
    return (token_grad, head_grad)


def solution(mesh):
    in_specs = (
        P(("rep", "expert", "group"), None),
        P("expert", "group", None),
        P("expert", "group", None),
        P("expert", "group", None),
        P(("rep", "expert", "group"), None),
        P(("rep", "expert", "group"), None),
        P(),
        P(None, "expert"),
        P("rep", "group", "expert"),
    )
    out_specs = (P(("rep", "expert", "group"), None), P("rep", "expert"))
    return jax.shard_map(body, mesh=mesh, in_specs=in_specs, out_specs=out_specs, check_vma=False)
```

time: 320 us -> 141 us (0.44)
  waiting for transfers between devices: 218 us -> 71.3 us
  blocking collectives: 34.7 us -> 0 us
  starting transfers between devices: 8.13 us -> 37 us
  Pallas kernels: 0 us -> 22.9 us
  matrix products: 21.2 us -> 1.71 us
  other arithmetic: 16.8 us -> 0.04 us
  between operations: 14.1 us -> 0.97 us
    reduce_scatter x2 -> x0, waiting for transfers between devices: 129 us -> none  [the longest x1 66.2 us: body(): lax.psum_scatter(part.astype(BF16), 'expert', scatter_dimension=0, tiled=...]
    all_gather x2 -> x0, waiting for transfers between devices: 81.2 us -> none  [the longest x1 50.5 us: body(): moe_all = lax.all_gather(moe_out, 'expert', axis=0, tiled=True)]
    ppermute x3 -> x38, waiting for transfers between devices: 0.01 us -> 71.3 us  [the longest x32 59.3 us: send(): return lax.ppermute(value, 'expert', pairs)]
    ppermute x3 -> x38, starting transfers between devices: 0.67 us -> 37 us  [the longest x32 35.9 us: send(): return lax.ppermute(value, 'expert', pairs)]
    psum x1 -> x0, blocking collectives: 34.7 us -> none  [body(): pooled_grad = lax.psum(pooled_terms.astype(BF16), 'expert').astype(F32)]
    pallas_call x0 -> x31, Pallas kernels: none -> 22.9 us  [call(): pl.pallas_call(kernel, out_shape=[pltpu.VMEM(shape, dtype) for shape, dty...]
    dot_general x7 -> x1, matrix products: 10.3 us -> 0.19 us  [dot(): return jnp.dot(left, right, preferred_element_type=F32)]
    dot_general x7 -> x1, matrix products: 9.62 us -> 0.22 us  [dot_t(): lax.dot_general(left, right, (((1,), (1,)), ((), ())), preferred_element_...]
  transfers between devices with their start and end apart: 9 -> 39, of which waited for: 6 -> 21; matrix products, arithmetic and copies ran while one was open for 3% -> 1% of each run, Pallas kernels for 0% -> 13%
where the time goes in v2:
time: 141 us
  waiting for transfers between devices  71.3 us (51%)
  starting transfers between devices  37 us (26%)
  Pallas kernels  22.9 us (16%)
  local copies, waits for them, and re-layouts  6.74 us (5%)
  matrix products  1.71 us (1%)
    ppermute x32, waiting for transfers between devices, send(): return lax.ppermute(value, 'expert', pairs)  59.3 us
    ppermute x32, starting transfers between devices, send(): return lax.ppermute(value, 'expert', pairs)  35.9 us
    pallas_call x31, Pallas kernels, call(): pl.pallas_call(kernel, out_shape=[pltpu.VMEM(shape, dtype) for shape, dty...  22.9 us
    ppermute x3, waiting for transfers between devices, body(): other = lax.ppermute(mine, 'expert', pairs)  12 us
    unnamed x17, local copies, waits for them, and re-layouts  6.69 us
  transfers between devices with their start and end apart: 39, of which 21 were waited for; matrix products, arithmetic and copies ran while one was open for 1% of the time, Pallas kernels for 13%

profile of v2, /device:TPU:0, one launch (start us, length us, event | category | flops | bytes accessed | tf_op | source)
XLA Modules:
  0.0 140.7 jit_solution(7549233672005319748)
XLA Ops:
  3.7 3.0 %collective-permute-start.4 = (bf16[128,1152]{1,0:T(8,128)(2,1)S(1)}, bf16[128,1152]{1,0:T(8,128)(2,1)S(1)}, u32[]{:S(2)}, u32[]{:S(2)}) collective-permute-start(bf16[128,1152]{1,0:T(8,128)(2,1)S(1)} %shard_map.104.refs_0_), channel_id=1, source_target_pairs={{0,2},{4,0},{8,4},{12,8},{14,12},{10,14},{6,10},{2,6},{1,3},{5,1},... | collective-permute-start | bytes 884744 | tf_op jit(solution)/shard_map/ppermute | solution.py:58
  7.4 6.4 %collective-permute-done.4.refs_1_ = bf16[128,1152]{1,0:T(8,128)(2,1)S(1)} collective-permute-done((bf16[128,1152]{1,0:T(8,128)(2,1)S(1)}, bf16[128,1152]{1,0:T(8,128)(2,1)S(1)}, u32[]{:S(2)}, u32[]{:S(2)}) %collective-permute-start.4) | collective-permute-done | bytes 294944 | tf_op jit(solution)/shard_map/ppermute | solution.py:58
  15.8 6.2 %collective-permute-done.6.refs_1_ = bf16[128,1152]{1,0:T(8,128)(2,1)S(1)} collective-permute-done((bf16[128,1152]{1,0:T(8,128)(2,1)S(1)}, bf16[128,1152]{1,0:T(8,128)(2,1)S(1)}, u32[]{:S(2)}, u32[]{:S(2)}) %collective-permute-start.6) | collective-permute-done | bytes 294944 | tf_op jit(solution)/shard_map/ppermute | solution.py:58
  24.0 5.2 %collective-permute-done.8.refs_1_ = bf16[128,1152]{1,0:T(8,128)(2,1)S(1)} collective-permute-done((bf16[128,1152]{1,0:T(8,128)(2,1)S(1)}, bf16[128,1152]{1,0:T(8,128)(2,1)S(1)}, u32[]{:S(2)}, u32[]{:S(2)}) %collective-permute-start.8) | collective-permute-done | bytes 294944 | tf_op jit(solution)/shard_map/ppermute | solution.py:58
  40.9 2.7 %collective-permute-done.15.arrived_ref = bf16[64,1024]{1,0:T(8,128)(2,1)S(1)} collective-permute-done((bf16[64,1024]{1,0:T(8,128)(2,1)S(1)}, bf16[64,1024]{1,0:T(8,128)(2,1)S(1)}, u32[]{:S(2)}, u32[]{:S(2)}) %collective-permute-start.15) | collective-permute-done | bytes 131104 | tf_op jit(solution)/shard_map/ppermute | solution.py:58
  47.5 5.1 %collective-permute-done.16.arrived_ref = bf16[128,1024]{1,0:T(8,128)(2,1)S(1)} collective-permute-done((bf16[128,1024]{1,0:T(8,128)(2,1)S(1)}, bf16[128,1024]{1,0:T(8,128)(2,1)S(1)}, u32[]{:S(2)}, u32[]{:S(2)}) %collective-permute-start.16) | collective-permute-done | bytes 262176 | tf_op jit(solution)/shard_map/ppermute | solution.py:58
  56.7 4.6 %collective-permute-done.17.arrived_ref = bf16[128,1024]{1,0:T(8,128)(2,1)S(1)} collective-permute-done((bf16[128,1024]{1,0:T(8,128)(2,1)S(1)}, bf16[128,1024]{1,0:T(8,128)(2,1)S(1)}, u32[]{:S(2)}, u32[]{:S(2)}) %collective-permute-start.17) | collective-permute-done | bytes 262176 | tf_op jit(solution)/shard_map/ppermute | solution.py:58
  64.6 4.8 %collective-permute-done.18.right_ref = bf16[128,1024]{1,0:T(8,128)(2,1)S(1)} collective-permute-done((bf16[128,1024]{1,0:T(8,128)(2,1)S(1)}, bf16[128,1024]{1,0:T(8,128)(2,1)S(1)}, u32[]{:S(2)}, u32[]{:S(2)}) %collective-permute-start.18) | collective-permute-done | bytes 262176 | tf_op jit(solution)/shard_map/ppermute | solution.py:58
  72.8 4.3 %collective-permute-done.23.refs_3_ = bf16[128,1024]{1,0:T(8,128)(2,1)S(1)} collective-permute-done((bf16[128,1024]{1,0:T(8,128)(2,1)S(1)}, bf16[128,1024]{1,0:T(8,128)(2,1)S(1)}, u32[]{:S(2)}, u32[]{:S(2)}) %collective-permute-start.23) | collective-permute-done | bytes 262176 | tf_op jit(solution)/shard_map/ppermute | solution.py:58
  77.1 2.0 %collective-permute-start.24 = (bf16[128,1024]{1,0:T(8,128)(2,1)S(1)}, bf16[128,1024]{1,0:T(8,128)(2,1)S(1)}, u32[]{:S(2)}, u32[]{:S(2)}) collective-permute-start(bf16[128,1024]{1,0:T(8,128)(2,1)S(1)} %collective-permute-done.23.refs_3_), channel_id=1, source_target_pairs={{0,2},{4,0},{8,4},{12,8},{14,12},{10,14},{6,10},{2,6},{1,3},{5,1},... | collective-permute-start | bytes 786440 | tf_op jit(solution)/shard_map/ppermute | solution.py:58
  79.2 5.1 %collective-permute-done.24.refs_3_ = bf16[128,1024]{1,0:T(8,128)(2,1)S(1)} collective-permute-done((bf16[128,1024]{1,0:T(8,128)(2,1)S(1)}, bf16[128,1024]{1,0:T(8,128)(2,1)S(1)}, u32[]{:S(2)}, u32[]{:S(2)}) %collective-permute-start.24) | collective-permute-done | bytes 262176 | tf_op jit(solution)/shard_map/ppermute | solution.py:58
  84.2 2.5 %collective-permute-start.25 = (bf16[128,1024]{1,0:T(8,128)(2,1)S(1)}, bf16[128,1024]{1,0:T(8,128)(2,1)S(1)}, u32[]{:S(2)}, u32[]{:S(2)}) collective-permute-start(bf16[128,1024]{1,0:T(8,128)(2,1)S(1)} %collective-permute-done.24.refs_3_), channel_id=1, source_target_pairs={{0,2},{4,0},{8,4},{12,8},{14,12},{10,14},{6,10},{2,6},{1,3},{5,1},... | collective-permute-start | bytes 786440 | tf_op jit(solution)/shard_map/ppermute | solution.py:58
  86.7 4.1 %collective-permute-done.25.refs_3_ = bf16[128,1024]{1,0:T(8,128)(2,1)S(1)} collective-permute-done((bf16[128,1024]{1,0:T(8,128)(2,1)S(1)}, bf16[128,1024]{1,0:T(8,128)(2,1)S(1)}, u32[]{:S(2)}, u32[]{:S(2)}) %collective-permute-start.25) | collective-permute-done | bytes 262176 | tf_op jit(solution)/shard_map/ppermute | solution.py:58
  90.8 2.5 %collective-permute-start.26 = (bf16[64,1024]{1,0:T(8,128)(2,1)S(1)}, bf16[64,1024]{1,0:T(8,128)(2,1)S(1)}, u32[]{:S(2)}, u32[]{:S(2)}) collective-permute-start(bf16[64,1024]{1,0:T(8,128)(2,1)S(1)} %slice.27), channel_id=1, source_target_pairs={{0,2},{4,0},{8,4},{12,8},{14,12},{10,14},{6,10},{2,6},{1,3},{5,1},... | collective-permute-start | bytes 393224 | tf_op jit(solution)/shard_map/ppermute | solution.py:58
  95.9 2.7 %collective-permute-done.22.refs_2_ = bf16[64,1024]{1,0:T(8,128)(2,1)S(1)} collective-permute-done((bf16[64,1024]{1,0:T(8,128)(2,1)S(1)}, bf16[64,1024]{1,0:T(8,128)(2,1)S(1)}, u32[]{:S(2)}, u32[]{:S(2)}) %collective-permute-start.22) | collective-permute-done | bytes 131104 | tf_op jit(solution)/shard_map/ppermute | solution.py:58
  99.7 3.5 %collective-permute-done.27 = bf16[8,1024]{1,0:T(8,128)(2,1)S(1)} collective-permute-done((bf16[8,1024]{1,0:T(8,128)(2,1)S(1)}, bf16[8,1024]{1,0:T(8,128)(2,1)S(1)}, u32[]{:S(2)}, u32[]{:S(2)}) %collective-permute-start.27) | collective-permute-done | bytes 16416 | tf_op jit(solution)/shard_map/ppermute | solution.py:301
  103.2 3.9 %collective-permute-done.28 = bf16[8,1024]{1,0:T(8,128)(2,1)S(1)} collective-permute-done((bf16[8,1024]{1,0:T(8,128)(2,1)S(1)}, bf16[8,1024]{1,0:T(8,128)(2,1)S(1)}, u32[]{:S(2)}, u32[]{:S(2)}) %collective-permute-start.28) | collective-permute-done | bytes 16416 | tf_op jit(solution)/shard_map/ppermute | solution.py:301
  107.2 4.6 %collective-permute-done.29 = bf16[8,1024]{1,0:T(8,128)(2,1)S(1)} collective-permute-done((bf16[8,1024]{1,0:T(8,128)(2,1)S(1)}, bf16[8,1024]{1,0:T(8,128)(2,1)S(1)}, u32[]{:S(2)}, u32[]{:S(2)}) %collective-permute-start.29) | collective-permute-done | bytes 16416 | tf_op jit(solution)/shard_map/ppermute | solution.py:301
  111.8 2.5 %shard_map.127 = (bf16[64,1024]{1,0:T(8,128)(2,1)S(1)}, bf16[64,1024]{1,0:T(8,128)(2,1)S(1)}) custom-call(bf16[64,1152]{1,0:T(8,128)(2,1)S(1)} %collective-permute-done.9.refs_0_, bf16[64,1152]{1,0:T(8,128)(2,1)S(1)} %collective-permute-done.10.refs_1_, bf16[64,1024]{1,0:T(8,128)(2,1)S(1)} %collective-permute-done.22.refs_2_, ...), custom_call_target="tpu_custom_call" | custom-call | flops 603979776 | bytes 5705728 | tf_op jit(solution)/shard_map/pallas_call | solution.py:33
  116.4 2.5 %shard_map.126 = (f32[128,1024]{1,0:T(8,128)S(1)}, f32[128,1024]{1,0:T(8,128)S(1)}) custom-call(bf16[128,1152]{1,0:T(8,128)(2,1)S(1)} %collective-permute-done.7.refs_0_, bf16[128,1152]{1,0:T(8,128)(2,1)S(1)} %collective-permute-done.8.refs_1_, bf16[128,1024]{1,0:T(8,128)(2,1)S(1)} %collective-permute-done.21.refs_2_, ...), custom_call_target="tpu_custom_call" | custom-call | flops 1207959552 | bytes 6656000 | tf_op jit(solution)/shard_map/pallas_call | solution.py:33
  121.5 2.5 %shard_map.125 = (f32[128,1024]{1,0:T(8,128)S(1)}, f32[128,1024]{1,0:T(8,128)S(1)}) custom-call(bf16[128,1152]{1,0:T(8,128)(2,1)S(1)} %collective-permute-done.5.refs_0_, bf16[128,1152]{1,0:T(8,128)(2,1)S(1)} %collective-permute-done.6.refs_1_, bf16[128,1024]{1,0:T(8,128)(2,1)S(1)} %collective-permute-done.20.refs_2_, ...), custom_call_target="tpu_custom_call" | custom-call | flops 1207959552 | bytes 6656000 | tf_op jit(solution)/shard_map/pallas_call | solution.py:33
  128.0 2.5 %shard_map.124 = (f32[128,1024]{1,0:T(8,128)S(1)}, f32[128,1024]{1,0:T(8,128)S(1)}) custom-call(bf16[128,1152]{1,0:T(8,128)(2,1)S(1)} %collective-permute-done.3.refs_0_, bf16[128,1152]{1,0:T(8,128)(2,1)S(1)} %collective-permute-done.4.refs_1_, bf16[128,1024]{1,0:T(8,128)(2,1)S(1)} %collective-permute-done.19.refs_2_, ...), custom_call_target="tpu_custom_call" | custom-call | flops 1207959552 | bytes 6656000 | tf_op jit(solution)/shard_map/pallas_call | solution.py:33
  130.6 2.3 %collective-permute-done.36.arrived_ref = bf16[128,1024]{1,0:T(8,128)(2,1)S(1)} collective-permute-done((bf16[128,1024]{1,0:T(8,128)(2,1)S(1)}, bf16[128,1024]{1,0:T(8,128)(2,1)S(1)}, u32[]{:S(2)}, u32[]{:S(2)}) %collective-permute-start.36) | collective-permute-done | bytes 262176 | tf_op jit(solution)/shard_map/ppermute | solution.py:58
  136.5 2.0 %shard_map.123.part_ref = f32[128,1024]{1,0:T(8,128)S(1)} custom-call(bf16[128,1152]{1,0:T(8,128)(2,1)S(1)} %shard_map.104.refs_0_, bf16[128,1024]{1,0:T(8,128)(2,1)S(1)} %shard_map.117.refs_1_, bf16[128,768]{1,0:T(8,128)(2,1)S(1)} %get-tuple-element.42.refs_2_, bf16[128,768]{1,0:T(8,128)(2,1)S(1)} %get-tuple-element.43.refs_3_, ...), custom_call_target="tpu_custom_call" | custom-call | flops 603979776 | bytes 5705728 | tf_op jit(solution)/shard_map/pallas_call | solution.py:33
  (116 shorter events, 52.1 us)
Async XLA Ops:
  3.7 10.1 %collective-permute-start.4 = (bf16[128,1152]{1,0:T(8,128)(2,1)S(1)}, bf16[128,1152]{1,0:T(8,128)(2,1)S(1)}, u32[]{:S(2)}, u32[]{:S(2)}) collective-permute-start(bf16[128,1152]{1,0:T(8,128)(2,1)S(1)} %shard_map.104.refs_0_), channel_id=1, source_target_pairs={{0,2},{4,0},{8,4},{12,8},{14,12},{10,14},{6,10},{2,6},{1,3},{5,1},... | collective-permute-start | bytes 884744 | tf_op jit(solution)/shard_map/ppermute | solution.py:58
  6.7 8.8 %collective-permute-start.3 = (bf16[128,1152]{1,0:T(8,128)(2,1)S(1)}, bf16[128,1152]{1,0:T(8,128)(2,1)S(1)}, u32[]{:S(2)}, u32[]{:S(2)}) collective-permute-start(bf16[128,1152]{1,0:T(8,128)(2,1)S(1)} %shard_map.104.refs_0_), channel_id=1, source_target_pairs={{0,4},{4,8},{8,12},{12,14},{14,10},{10,6},{6,2},{2,0},{1,5},{5,9},... | collective-permute-start | bytes 884744 | tf_op jit(solution)/shard_map/ppermute | solution.py:58
  6.9 24.6 %collective-permute-start = (bf16[2,512,384]{2,1,0:T(8,128)(2,1)}, bf16[2,512,384]{2,1,0:T(8,128)(2,1)S(1)}, u32[]{:S(2)}, u32[]{:S(2)}) collective-permute-start(bf16[2,512,384]{2,1,0:T(8,128)(2,1)} %refs_0_.1), channel_id=1, source_target_pairs={{0,1},{1,0},{2,3},{3,2},{4,5},{5,4},{6,7},{7,6},{8,9},{9,8},{10,11... | collective-permute-start | bytes 2359304 | tf_op jit(solution)/shard_map/ppermute | solution.py:160
  6.9 24.6 %collective-permute-start.1 = (bf16[2,512,384]{2,1,0:T(8,128)(2,1)}, bf16[2,512,384]{2,1,0:T(8,128)(2,1)S(1)}, u32[]{:S(2)}, u32[]{:S(2)}) collective-permute-start(bf16[2,512,384]{2,1,0:T(8,128)(2,1)} %refs_2_.1), channel_id=1, source_target_pairs={{0,1},{1,0},{2,3},{3,2},{4,5},{5,4},{6,7},{7,6},{8,9},{9,8},{10,11... | collective-permute-start | bytes 2359304 | tf_op jit(solution)/shard_map/ppermute | solution.py:160
  7.4 24.1 %collective-permute-start.2 = (bf16[2,192,1024]{2,1,0:T(8,128)(2,1)}, bf16[2,192,1024]{2,1,0:T(8,128)(2,1)S(1)}, u32[]{:S(2)}, u32[]{:S(2)}) collective-permute-start(bf16[2,192,1024]{2,1,0:T(8,128)(2,1)} %refs_4_.1), channel_id=1, source_target_pairs={{0,1},{1,0},{2,3},{3,2},{4,5},{5,4},{6,7},{7,6},{8,9},{9,8},{10,11... | collective-permute-start | bytes 2359304 | tf_op jit(solution)/shard_map/ppermute | solution.py:160
  13.8 8.2 %collective-permute-start.6 = (bf16[128,1152]{1,0:T(8,128)(2,1)S(1)}, bf16[128,1152]{1,0:T(8,128)(2,1)S(1)}, u32[]{:S(2)}, u32[]{:S(2)}) collective-permute-start(bf16[128,1152]{1,0:T(8,128)(2,1)S(1)} %collective-permute-done.4.refs_1_), channel_id=1, source_target_pairs={{0,2},{4,0},{8,4},{12,8},{14,12},{10,14},{6,10},{2,6},{1,3},{5,1},... | collective-permute-start | bytes 884744 | tf_op jit(solution)/shard_map/ppermute | solution.py:58
  15.5 7.9 %collective-permute-start.5 = (bf16[128,1152]{1,0:T(8,128)(2,1)S(1)}, bf16[128,1152]{1,0:T(8,128)(2,1)S(1)}, u32[]{:S(2)}, u32[]{:S(2)}) collective-permute-start(bf16[128,1152]{1,0:T(8,128)(2,1)S(1)} %collective-permute-done.3.refs_0_), channel_id=1, source_target_pairs={{0,4},{4,8},{8,12},{12,14},{14,10},{10,6},{6,2},{2,0},{1,5},{5,9},... | collective-permute-start | bytes 884744 | tf_op jit(solution)/shard_map/ppermute | solution.py:58
  22.0 7.3 %collective-permute-start.8 = (bf16[128,1152]{1,0:T(8,128)(2,1)S(1)}, bf16[128,1152]{1,0:T(8,128)(2,1)S(1)}, u32[]{:S(2)}, u32[]{:S(2)}) collective-permute-start(bf16[128,1152]{1,0:T(8,128)(2,1)S(1)} %collective-permute-done.6.refs_1_), channel_id=1, source_target_pairs={{0,2},{4,0},{8,4},{12,8},{14,12},{10,14},{6,10},{2,6},{1,3},{5,1},... | collective-permute-start | bytes 884744 | tf_op jit(solution)/shard_map/ppermute | solution.py:58
  23.3 7.2 %collective-permute-start.7 = (bf16[128,1152]{1,0:T(8,128)(2,1)S(1)}, bf16[128,1152]{1,0:T(8,128)(2,1)S(1)}, u32[]{:S(2)}, u32[]{:S(2)}) collective-permute-start(bf16[128,1152]{1,0:T(8,128)(2,1)S(1)} %collective-permute-done.5.refs_0_), channel_id=1, source_target_pairs={{0,4},{4,8},{8,12},{12,14},{14,10},{10,6},{6,2},{2,0},{1,5},{5,9},... | collective-permute-start | bytes 884744 | tf_op jit(solution)/shard_map/ppermute | solution.py:58
  29.3 6.8 %collective-permute-start.10 = (bf16[64,1152]{1,0:T(8,128)(2,1)S(1)}, bf16[64,1152]{1,0:T(8,128)(2,1)S(1)}, u32[]{:S(2)}, u32[]{:S(2)}) collective-permute-start(bf16[64,1152]{1,0:T(8,128)(2,1)S(1)} %slice.25), channel_id=1, source_target_pairs={{0,2},{4,0},{8,4},{12,8},{14,12},{10,14},{6,10},{2,6},{1,3},{5,1},... | collective-permute-start | bytes 442376 | tf_op jit(solution)/shard_map/ppermute | solution.py:58
  43.6 8.9 %collective-permute-start.16 = (bf16[128,1024]{1,0:T(8,128)(2,1)S(1)}, bf16[128,1024]{1,0:T(8,128)(2,1)S(1)}, u32[]{:S(2)}, u32[]{:S(2)}) collective-permute-start(bf16[128,1024]{1,0:T(8,128)(2,1)S(1)} %shard_map.114), channel_id=1, source_target_pairs={{0,2},{4,0},{8,4},{12,8},{14,12},{10,14},{6,10},{2,6},{1,3},{5,1},... | collective-permute-start | bytes 786440 | tf_op jit(solution)/shard_map/ppermute | solution.py:58
  44.9 9.2 %collective-permute-start.12 = (bf16[128,1024]{1,0:T(8,128)(2,1)S(1)}, bf16[128,1024]{1,0:T(8,128)(2,1)S(1)}, u32[]{:S(2)}, u32[]{:S(2)}) collective-permute-start(bf16[128,1024]{1,0:T(8,128)(2,1)S(1)} %shard_map.111), channel_id=1, source_target_pairs={{0,4},{4,8},{8,12},{12,14},{14,10},{10,6},{6,2},{2,0},{1,5},{5,9},... | collective-permute-start | bytes 786440 | tf_op jit(solution)/shard_map/ppermute | solution.py:58
  52.6 8.7 %collective-permute-start.17 = (bf16[128,1024]{1,0:T(8,128)(2,1)S(1)}, bf16[128,1024]{1,0:T(8,128)(2,1)S(1)}, u32[]{:S(2)}, u32[]{:S(2)}) collective-permute-start(bf16[128,1024]{1,0:T(8,128)(2,1)S(1)} %shard_map.115), channel_id=1, source_target_pairs={{0,2},{4,0},{8,4},{12,8},{14,12},{10,14},{6,10},{2,6},{1,3},{5,1},... | collective-permute-start | bytes 786440 | tf_op jit(solution)/shard_map/ppermute | solution.py:58
  54.1 8.3 %collective-permute-start.13 = (bf16[128,1024]{1,0:T(8,128)(2,1)S(1)}, bf16[128,1024]{1,0:T(8,128)(2,1)S(1)}, u32[]{:S(2)}, u32[]{:S(2)}) collective-permute-start(bf16[128,1024]{1,0:T(8,128)(2,1)S(1)} %shard_map.112), channel_id=1, source_target_pairs={{0,4},{4,8},{8,12},{12,14},{14,10},{10,6},{6,2},{2,0},{1,5},{5,9},... | collective-permute-start | bytes 786440 | tf_op jit(solution)/shard_map/ppermute | solution.py:58
  61.4 8.1 %collective-permute-start.18 = (bf16[128,1024]{1,0:T(8,128)(2,1)S(1)}, bf16[128,1024]{1,0:T(8,128)(2,1)S(1)}, u32[]{:S(2)}, u32[]{:S(2)}) collective-permute-start(bf16[128,1024]{1,0:T(8,128)(2,1)S(1)} %shard_map.116), channel_id=1, source_target_pairs={{0,2},{4,0},{8,4},{12,8},{14,12},{10,14},{6,10},{2,6},{1,3},{5,1},... | collective-permute-start | bytes 786440 | tf_op jit(solution)/shard_map/ppermute | solution.py:58
  62.5 8.1 %collective-permute-start.14 = (bf16[128,1024]{1,0:T(8,128)(2,1)S(1)}, bf16[128,1024]{1,0:T(8,128)(2,1)S(1)}, u32[]{:S(2)}, u32[]{:S(2)}) collective-permute-start(bf16[128,1024]{1,0:T(8,128)(2,1)S(1)} %shard_map.113), channel_id=1, source_target_pairs={{0,4},{4,8},{8,12},{12,14},{14,10},{10,6},{6,2},{2,0},{1,5},{5,9},... | collective-permute-start | bytes 786440 | tf_op jit(solution)/shard_map/ppermute | solution.py:58
  72.3 6.8 %collective-permute-start.19 = (bf16[128,1024]{1,0:T(8,128)(2,1)S(1)}, bf16[128,1024]{1,0:T(8,128)(2,1)S(1)}, u32[]{:S(2)}, u32[]{:S(2)}) collective-permute-start(bf16[128,1024]{1,0:T(8,128)(2,1)S(1)} %shard_map.117.refs_1_), channel_id=1, source_target_pairs={{0,4},{4,8},{8,12},{12,14},{14,10},{10,6},{6,2},{2,0},{1,5},{5,9},... | collective-permute-start | bytes 786440 | tf_op jit(solution)/shard_map/ppermute | solution.py:58
  77.1 7.1 %collective-permute-start.24 = (bf16[128,1024]{1,0:T(8,128)(2,1)S(1)}, bf16[128,1024]{1,0:T(8,128)(2,1)S(1)}, u32[]{:S(2)}, u32[]{:S(2)}) collective-permute-start(bf16[128,1024]{1,0:T(8,128)(2,1)S(1)} %collective-permute-done.23.refs_3_), channel_id=1, source_target_pairs={{0,2},{4,0},{8,4},{12,8},{14,12},{10,14},{6,10},{2,6},{1,3},{5,1},... | collective-permute-start | bytes 786440 | tf_op jit(solution)/shard_map/ppermute | solution.py:58
  79.2 7.6 %collective-permute-start.20 = (bf16[128,1024]{1,0:T(8,128)(2,1)S(1)}, bf16[128,1024]{1,0:T(8,128)(2,1)S(1)}, u32[]{:S(2)}, u32[]{:S(2)}) collective-permute-start(bf16[128,1024]{1,0:T(8,128)(2,1)S(1)} %collective-permute-done.19.refs_2_), channel_id=1, source_target_pairs={{0,4},{4,8},{8,12},{12,14},{14,10},{10,6},{6,2},{2,0},{1,5},{5,9},... | collective-permute-start | bytes 786440 | tf_op jit(solution)/shard_map/ppermute | solution.py:58
  84.2 6.5 %collective-permute-start.25 = (bf16[128,1024]{1,0:T(8,128)(2,1)S(1)}, bf16[128,1024]{1,0:T(8,128)(2,1)S(1)}, u32[]{:S(2)}, u32[]{:S(2)}) collective-permute-start(bf16[128,1024]{1,0:T(8,128)(2,1)S(1)} %collective-permute-done.24.refs_3_), channel_id=1, source_target_pairs={{0,2},{4,0},{8,4},{12,8},{14,12},{10,14},{6,10},{2,6},{1,3},{5,1},... | collective-permute-start | bytes 786440 | tf_op jit(solution)/shard_map/ppermute | solution.py:58
  86.7 6.6 %collective-permute-start.21 = (bf16[128,1024]{1,0:T(8,128)(2,1)S(1)}, bf16[128,1024]{1,0:T(8,128)(2,1)S(1)}, u32[]{:S(2)}, u32[]{:S(2)}) collective-permute-start(bf16[128,1024]{1,0:T(8,128)(2,1)S(1)} %collective-permute-done.20.refs_2_), channel_id=1, source_target_pairs={{0,4},{4,8},{8,12},{12,14},{14,10},{10,6},{6,2},{2,0},{1,5},{5,9},... | collective-permute-start | bytes 786440 | tf_op jit(solution)/shard_map/ppermute | solution.py:58
  121.5 6.5 %collective-permute-start.38 = (bf16[8,1274]{1,0:T(8,128)(2,1)S(1)}, bf16[8,1274]{1,0:T(8,128)(2,1)S(1)}, u32[]{:S(2)}, u32[]{:S(2)}) collective-permute-start(bf16[8,1274]{1,0:T(8,128)(2,1)S(1)} %pad_maximum_fusion.1), channel_id=1, source_target_pairs={{0,1},{1,0},{2,3},{3,2},{4,5},{5,4},{6,7},{7,6},{8,9},{9,8},{10,11... | collective-permute-start | bytes 61160 | tf_op jit(solution)/shard_map/ppermute | solution.py:307
  125.8 7.1 %collective-permute-start.36 = (bf16[128,1024]{1,0:T(8,128)(2,1)S(1)}, bf16[128,1024]{1,0:T(8,128)(2,1)S(1)}, u32[]{:S(2)}, u32[]{:S(2)}) collective-permute-start(bf16[128,1024]{1,0:T(8,128)(2,1)S(1)} %shard_map.132), channel_id=1, source_target_pairs={{0,2},{4,0},{8,4},{12,8},{14,12},{10,14},{6,10},{2,6},{1,3},{5,1},... | collective-permute-start | bytes 786440 | tf_op jit(solution)/shard_map/ppermute | solution.py:58
  126.3 7.1 %collective-permute-start.32 = (bf16[128,1024]{1,0:T(8,128)(2,1)S(1)}, bf16[128,1024]{1,0:T(8,128)(2,1)S(1)}, u32[]{:S(2)}, u32[]{:S(2)}) collective-permute-start(bf16[128,1024]{1,0:T(8,128)(2,1)S(1)} %shard_map.129), channel_id=1, source_target_pairs={{0,4},{4,8},{8,12},{12,14},{14,10},{10,6},{6,2},{2,0},{1,5},{5,9},... | collective-permute-start | bytes 786440 | tf_op jit(solution)/shard_map/ppermute | solution.py:58
  (22 other events, 245.2 us)

commit v3 on v2

--- a/solution.py
+++ b/solution.py
@@ -23,19 +23,14 @@
     return lax.dot_general(left, right, (((1,), (1,)), ((), ())), preferred_element_type=F32)
 
 
-def call(kernel, outs, *args, flops=0, scratch=(), in_any=False):
-    if in_any:
-        specs = [pl.BlockSpec(memory_space=pl.ANY)] * len(args)
-    else:
-        specs = [pl.BlockSpec(memory_space=pltpu.VMEM)] * len(args)
-        args = [pltpu.with_memory_space_constraint(a, pltpu.VMEM) for a in args]
+def call(kernel, outs, *args, flops=0):
+    args = [pltpu.with_memory_space_constraint(a, pltpu.VMEM) for a in args]
     size = sum(a.size * a.dtype.itemsize for a in args)
     return pl.pallas_call(
         kernel,
         out_shape=[pltpu.VMEM(shape, dtype) for shape, dtype in outs],
-        in_specs=specs,
+        in_specs=[pl.BlockSpec(memory_space=pltpu.VMEM)] * len(args),
         out_specs=[pl.BlockSpec(memory_space=pltpu.VMEM)] * len(outs),
-        scratch_shapes=list(scratch),
         compiler_params=pltpu.CompilerParams(vmem_limit_bytes=VMEM_LIMIT),
         cost_estimate=pl.CostEstimate(flops=flops, bytes_accessed=size, transcendentals=0),
     )(*args)
@@ -67,66 +62,87 @@
             there = jnp.where(there < self.half, 2 * there, 2 * (count - 1 - there) + 1)
         return there
 
-    def gather(self, block, use):
-        mid = block.shape[0] // 2
-        from_left = from_right = block
-        use((0,), (block,))
+    def gather(self, top, bottom, use, first=None):
+        top_left = top_right = top
+        bottom_left = bottom_right = bottom
+        use((0,), (top, bottom))
         for step in range(1, self.half):
-            from_left = self.send(from_left, 1)
-            from_right = self.send(from_right, -1)
-            use((-step, step), (from_left, from_right))
-        top = self.send(from_left[:mid], 1)
-        bottom = self.send(from_right[mid:], -1)
-        use((self.half,), (top, bottom))
-
-    def scatter(self, ends, partial):
-        from_left = self.send(ends[0], 1)
-        from_right = self.send(ends[1], -1)
-        for step in range(self.half - 1, 0, -1):
-            right = add_rows(partial(step), from_left, 0)
-            left = add_rows(partial(-step), from_right, 1)
-            from_left = self.send(right, 1)
-            from_right = self.send(left, -1)
-        return from_left, from_right
-
-
-def add_rows(block, arrived, at_end):
-    rows, cols = block.shape
-    some = arrived.shape[0]
-
-    def kernel(block_ref, arrived_ref, out_ref):
-        if some == rows:
-            out_ref[...] = (block_ref[...] + arrived_ref[...].astype(F32)).astype(BF16)
-            return
-        begin = rows - some if at_end else 0
-        rest = 0 if at_end else some
-        own = pl.ds(begin, some)
-        other = pl.ds(rest, rows - some)
-        out_ref[own, :] = (block_ref[own, :] + arrived_ref[...].astype(F32)).astype(BF16)
-        out_ref[other, :] = block_ref[other, :].astype(BF16)
-
-    return call(kernel, [((rows, cols), BF16)], block, arrived)[0]
-
-
-def pack_kernel(ids_ref, scores_ref, tokens_ref, out_ref):
+            top_left = self.send(top_left, 1)
+            top_right = self.send(top_right, -1)
+            bottom_left = self.send(bottom_left, 1)
+            bottom_right = self.send(bottom_right, -1)
+            if first is not None and step == min(2, self.half - 1):
+                bottom_left = first(bottom_left)
+            use((-step, step), (top_left, bottom_left, top_right, bottom_right))
+        use((self.half,), (self.send(top_left, 1), self.send(bottom_right, -1)))
+
+    def scatter(self, parts):
+        most = self.half - 1
+        top_left = self.send(parts[self.half][0], 1)
+        bottom_right = self.send(parts[self.half][1], -1)
+        bottom_left = self.send(parts[most][1], 1)
+        top_right = self.send(parts[-most][0], -1)
+        for step in range(most, 0, -1):
+            top_left = self.send(add(parts[step][0], top_left), 1)
+            bottom_right = self.send(add(parts[-step][1], bottom_right), -1)
+            if step > 1:
+                bottom_left = self.send(add(parts[step - 1][1], bottom_left), 1)
+                top_right = self.send(add(parts[1 - step][0], top_right), -1)
+        return (top_left, top_right), (bottom_left, bottom_right)
+
+    def part_types(self, distances):
+        types = []
+        for k in distances:
+            first = BF16 if k == self.half or k == 1 - self.half else F32
+            second = BF16 if k == self.half or k == self.half - 1 else F32
+            types += [first, second]
+        return types
+
+
+def add_kernel(block_ref, arrived_ref, out_ref):
+    out_ref[...] = (block_ref[...] + arrived_ref[...].astype(F32)).astype(BF16)
+
+
+def add(block, arrived):
+    return call(add_kernel, [(block.shape, BF16)], block, arrived)[0]
+
+
+def sum_kernel(*refs):
+    out_ref = refs[-1]
+    rows = refs[0].shape[0]
+    for i in range(len(refs) // 3):
+        own, left, right = refs[3 * i : 3 * i + 3]
+        arrived = left[...].astype(F32) + right[...].astype(F32)
+        out_ref[pl.ds(i * rows, rows), :] = (own[...] + arrived).astype(BF16)
+
+
+def pack_kernel(ids_ref, scores_ref, tokens_ref, top_ref, bottom_ref, sems):
     rows, cols = tokens_ref.shape
+    mid = rows // 2
+    copies = []
+    for i, ref in enumerate((top_ref, bottom_ref)):
+        source = tokens_ref.at[pl.ds(i * mid, mid), :]
+        copies.append(pltpu.make_async_copy(source, ref.at[:, pl.ds(0, cols)], sems.at[i]))
+        copies[-1].start()
     scores = scores_ref[...]
     ids = ids_ref[...]
-    route_weight = scores / jnp.sum(scores, axis=-1, keepdims=True)
-    lane = lax.broadcasted_iota(jnp.int32, (rows, LANES), 1)
-    weight_by = jnp.zeros((rows, LANES), F32)
-    for choice_k in range(scores.shape[1]):
+    route_weight = scores / jnp.sum(scores, axis=0, keepdims=True)
+    expert = lax.broadcasted_iota(jnp.int32, (LANES // 2, rows), 0)
+    weight_by = jnp.zeros((LANES // 2, rows), F32)
+    for choice_k in range(scores.shape[0]):
         one = slice(choice_k, choice_k + 1)
-        weight_by = weight_by + jnp.where(ids[:, one] == lane, route_weight[:, one], 0.0)
+        weight_by = weight_by + jnp.where(ids[one] == expert, route_weight[one], 0.0)
     high = weight_by.astype(BF16).astype(F32)
-    low = pltpu.roll(weight_by - high, LANES // 2, 1)
-    out_ref[:, :cols] = tokens_ref[...]
-    out_ref[:, cols:] = (high + low).astype(BF16)
+    weights = jnp.concatenate([high, weight_by - high], axis=0).T.astype(BF16)
+    top_ref[:, cols:] = weights[:mid]
+    bottom_ref[:, cols:] = weights[mid:]
+    for copy in copies:
+        copy.wait()
 
 
 def assemble_kernel(shards, local_experts, *refs):
     gates, ups, downs = refs[:shards], refs[shards : 2 * shards], refs[2 * shards : 3 * shards]
-    wide_ref, down_ref, sems = refs[3 * shards :]
+    wide_ref, down_ref, _, sems = refs[3 * shards + 1 :]
     hidden_dim = gates[0].shape[2]
     copies = []
 
@@ -151,26 +167,42 @@
         copy.wait()
 
 
-def full_weights(w_gate, w_up, w_down, group_count):
-    local_experts, _, hidden_dim = w_gate.shape
-    feature_dim = w_down.shape[2]
+def exchange_shards(w_gate, w_up, w_down, group_count):
     shards = []
     for shard in (w_gate, w_up, w_down):
         if group_count == 2:
             shards += [shard, lax.ppermute(shard, "group", [(0, 1), (1, 0)])]
         else:
             shards += [lax.all_gather(shard, "group", axis=1, tiled=True)]
+    return shards
+
+
+def assemble(shards, local_experts, passed):
     count = len(shards) // 3
-    return call(
+    hidden_dim = shards[0].shape[2]
+    feature_dim = shards[-1].shape[2]
+    if count == 2:
+        shards = [
+            pltpu.with_memory_space_constraint(w, pltpu.VMEM) if i % 2 else w
+            for i, w in enumerate(shards)
+        ]
+    return pl.pallas_call(
         functools.partial(assemble_kernel, count, local_experts),
-        [
-            ((feature_dim, 2 * local_experts * hidden_dim), BF16),
-            ((local_experts * hidden_dim, feature_dim), BF16),
+        out_shape=[
+            pltpu.VMEM((feature_dim, 2 * local_experts * hidden_dim), BF16),
+            pltpu.VMEM((local_experts * hidden_dim, feature_dim), BF16),
+            pltpu.VMEM(passed.shape, passed.dtype),
         ],
-        *shards,
-        scratch=[pltpu.SemaphoreType.DMA((3 * count * local_experts,))],
-        in_any=True,
-    )
+        in_specs=[
+            pl.BlockSpec(memory_space=pltpu.VMEM if count == 2 and i % 2 else pl.ANY)
+            for i in range(len(shards))
+        ]
+        + [pl.BlockSpec(memory_space=pltpu.VMEM)],
+        out_specs=[pl.BlockSpec(memory_space=pltpu.VMEM)] * 3,
+        scratch_shapes=[pltpu.SemaphoreType.DMA((3 * count * local_experts,))],
+        input_output_aliases={len(shards): 2},
+        compiler_params=pltpu.CompilerParams(vmem_limit_bytes=VMEM_LIMIT),
+    )(*shards, pltpu.with_memory_space_constraint(passed, pltpu.VMEM))
 
 
 def body(tokens, w_gate, w_up, w_down, route_ids, route_scores, norm_gain, class_head, targets):
@@ -183,19 +215,26 @@
     block = (rows_here, feature_dim)
     mid = rows_here // 2
 
-    packed = call(
+    shards = exchange_shards(w_gate, w_up, w_down, group_count)
+    top, bottom = pl.pallas_call(
         pack_kernel,
-        [((rows_here, feature_dim + LANES), BF16)],
-        route_ids,
-        route_scores,
-        tokens,
-    )[0]
-    wide, down = full_weights(w_gate, w_up, w_down, group_count)
+        out_shape=[pltpu.VMEM((mid, feature_dim + LANES), BF16)] * 2,
+        in_specs=[pl.BlockSpec(memory_space=pltpu.VMEM)] * 2 + [pl.BlockSpec(memory_space=pl.ANY)],
+        out_specs=[pl.BlockSpec(memory_space=pltpu.VMEM)] * 2,
+        scratch_shapes=[pltpu.SemaphoreType.DMA((2,))],
+        compiler_params=pltpu.CompilerParams(vmem_limit_bytes=VMEM_LIMIT),
+    )(route_ids.T, route_scores.T, tokens)
+    weights_at = []
+
+    def assemble_now(passed):
+        wide, down, passed = assemble(shards, local_experts, passed)
+        weights_at.extend([wide, down])
+        return passed
 
     def rows_of(refs):
         return jnp.concatenate([ref[...] for ref in refs], axis=0) if len(refs) > 1 else refs[0][...]
 
-    def forward_kernel(halves, count, *refs):
+    def forward_kernel(count, *refs):
         token_refs, (wide_ref, down_ref), outs = refs[:count], refs[count : count + 2], refs[count + 2 :]
         x = rows_of([ref.at[:, :feature_dim] for ref in token_refs])
         weights = rows_of([ref.at[:, feature_dim:] for ref in token_refs]).astype(F32)
@@ -216,43 +255,45 @@
             hidden = (silu * up_act).astype(BF16)
             term = dot(hidden, down_ref[cols, :])
             total = term if total is None else total + term
-        rows = total.shape[0] // len(outs[2:])
         for i, out in enumerate(outs[2:]):
-            out[...] = total[i * rows : (i + 1) * rows].astype(out.dtype)
+            out[...] = total[i * mid : (i + 1) * mid].astype(out.dtype)
 
     tokens_at, saved_at, part_at = {}, {}, {}
     flops = 2 * rows_here * feature_dim * hidden_dim * local_experts * 3
 
-    def forward(distances, blocks):
-        ends = distances == (ring.half,)
-        rows = sum(b.shape[0] for b in blocks)
-        outs = [((rows, local_experts * hidden_dim), BF16)] * 2
-        outs += [((mid, feature_dim), BF16)] * 2 if ends else [(block, F32)] * len(blocks)
+    def hold(distances, blocks):
+        tokens_at[distances] = blocks
+
+    def keep_parts(parts, distances, halves):
+        parts.update({k: halves[2 * i : 2 * i + 2] for i, k in enumerate(distances)})
+
+    def part_outs(distances):
+        return [((mid, feature_dim), dtype) for dtype in ring.part_types(distances)]
+
+    def forward(distances):
+        blocks = tokens_at[distances]
+        rows = mid * len(blocks)
         result = call(
-            functools.partial(forward_kernel, ends, len(blocks)),
-            outs,
+            functools.partial(forward_kernel, len(blocks)),
+            [((rows, local_experts * hidden_dim), BF16)] * 2 + part_outs(distances),
             *blocks,
-            wide,
-            down,
+            *weights_at,
             flops=flops * rows // rows_here,
         )
-        tokens_at[distances] = blocks
         saved_at[distances] = result[:2]
-        if ends:
-            part_at["ends"] = result[2:]
-        else:
-            part_at.update(zip(distances, result[2:]))
-
-    ring.gather(packed, forward)
-    from_left, from_right = ring.scatter(part_at["ends"], lambda k: part_at[k])
-
-    def moe_kernel(part_ref, left_ref, right_ref, out_ref):
-        arrived = left_ref[...].astype(F32) + right_ref[...].astype(F32)
-        out_ref[...] = (part_ref[...] + arrived).astype(BF16)
-
-    moe_out = call(moe_kernel, [(block, BF16)], part_at[0], from_left, from_right)[0]
-
+        keep_parts(part_at, distances, result[2:])
+
+    ring.gather(top, bottom, hold, assemble_now)
+    wide, down = weights_at
+    for distances in tokens_at:
+        forward(distances)
     gain = norm_gain.reshape(1, feature_dim)
+    half_shape = (mid, feature_dim)
+    moe_top, moe_bottom = [
+        call(sum_kernel, [(half_shape, BF16)], own, *arrived)[0]
+        for own, arrived in zip(part_at[0], ring.scatter(part_at))
+    ]
+
     moe_at, mean_at = {}, {}
 
     def residual_of(token_refs, moe_refs):
@@ -288,7 +329,7 @@
             mean_at["pooled"],
         )[0]
 
-    ring.gather(moe_out, norm)
+    ring.gather(moe_top, moe_bottom, norm)
     pooled = mean_at["pooled"].astype(BF16)
     logits = dot(pooled, class_head)
     target_rows = targets.reshape(expert_count, -1).astype(F32)
@@ -336,19 +377,16 @@
             grads = jnp.concatenate([gate_grad, up_grad], axis=1)
             term = dot_t(grads, wide_ref[:, pl.ds(local * pair_dim, pair_dim)])
             total = term if total is None else total + term
-        rows = total.shape[0] // len(outs)
         for i, out in enumerate(outs):
-            out[...] = total[i * rows : (i + 1) * rows].astype(out.dtype)
+            out[...] = total[i * mid : (i + 1) * mid].astype(out.dtype)
 
     back_at = {}
 
     def backward(distances):
         blocks = tokens_at[distances]
-        ends = distances == (ring.half,)
-        outs = [((mid, feature_dim), BF16)] * 2 if ends else [(block, F32)] * len(blocks)
         result = call(
             functools.partial(backward_kernel, distances, len(blocks)),
-            outs,
+            part_outs(distances),
             *blocks,
             *moe_at[distances],
             *saved_at[distances],
@@ -358,16 +396,18 @@
             down,
             flops=flops * len(distances),
         )
-        if ends:
-            back_at["ends"] = result
-        else:
-            back_at.update(zip(distances, result))
-
-    for step in range(ring.half, 0, -1):
-        backward((step,) if step == ring.half else (-step, step))
-    backward((0,))
-    from_left, from_right = ring.scatter(back_at["ends"], lambda k: back_at[k])
-    token_grad = call(moe_kernel, [(block, BF16)], back_at[0], from_left, from_right)[0]
+        keep_parts(back_at, distances, result)
+
+    for distances in reversed(list(tokens_at)):
+        backward(distances)
+    (top_left, top_right), (bottom_left, bottom_right) = ring.scatter(back_at)
+    token_grad = pl.pallas_call(
+        sum_kernel,
+        out_shape=jax.ShapeDtypeStruct(block, BF16),
+        in_specs=[pl.BlockSpec(memory_space=pltpu.VMEM)] * 6,
+        out_specs=pl.BlockSpec(memory_space=pltpu.VMEM),
+        compiler_params=pltpu.CompilerParams(vmem_limit_bytes=VMEM_LIMIT),
+    )(back_at[0][0], top_left, top_right, back_at[0][1], bottom_left, bottom_right)
     return (token_grad, head_grad)
 
 

time: 141 us -> 141 us (level)
  starting transfers between devices: 37 us -> 70.7 us
  waiting for transfers between devices: 71.3 us -> 37.7 us
    ppermute x32 -> x56, starting transfers between devices: 35.9 us -> 64.2 us  [send(): return lax.ppermute(value, 'expert', pairs)]
    ppermute x32 -> x56, waiting for transfers between devices: 59.3 us -> 31.3 us  [send(): return lax.ppermute(value, 'expert', pairs)]
    ppermute x3, waiting for transfers between devices: 12 us -> 6.37 us  [body(): other = lax.ppermute(mine, 'expert', pairs)]
    ppermute x3, starting transfers between devices: 0.61 us -> 5.91 us  [body(): other = lax.ppermute(mine, 'expert', pairs)]
    pallas_call x0 -> x3, Pallas kernels: none -> 2.18 us  [the longest x1 1.2 us: assemble(): pl.pallas_call(functools.partial(assemble_kernel, count, local_experts),...]
    pallas_call x31 -> x37, Pallas kernels: 22.9 us -> 21.3 us  [call(): pl.pallas_call(kernel, out_shape=[pltpu.VMEM(shape, dtype) for shape, dty...]
    unnamed x17 -> x18, local copies, waits for them, and re-layouts: 6.69 us -> 5.79 us
  transfers between devices with their start and end apart: 39 -> 63, of which waited for: 21 -> 24; matrix products, arithmetic and copies ran while one was open for 1% -> 1% of each run, Pallas kernels for 13% -> 14%
where the time goes in v3:
time: 141 us; the launch traced here: 140 us
  starting transfers between devices  70.7 us (50%)
  waiting for transfers between devices  37.7 us (27%)
  Pallas kernels  23.5 us (17%)
  local copies, waits for them, and re-layouts  5.8 us (4%)
  matrix products  1.71 us (1%)
    ppermute x56, starting transfers between devices, send(): return lax.ppermute(value, 'expert', pairs)  64.2 us
    ppermute x56, waiting for transfers between devices, send(): return lax.ppermute(value, 'expert', pairs)  31.3 us
    pallas_call x37, Pallas kernels, call(): pl.pallas_call(kernel, out_shape=[pltpu.VMEM(shape, dtype) for shape, dty...  21.3 us
    ppermute x3, waiting for transfers between devices, body(): other = lax.ppermute(mine, 'expert', pairs)  6.37 us
    ppermute x3, starting transfers between devices, body(): other = lax.ppermute(mine, 'expert', pairs)  5.91 us
    unnamed x18, local copies, waits for them, and re-layouts  5.79 us
  transfers between devices with their start and end apart: 63, of which 24 were waited for; matrix products, arithmetic and copies ran while one was open for 1% of the time, Pallas kernels for 14%

profile of v3, /device:TPU:0, one launch (start us, length us, event | category | flops | bytes accessed | tf_op | source)
XLA Modules:
  0.0 140.4 jit_solution(13599231732142953519)
XLA Ops:
  3.2 3.0 %collective-permute-start.6 = (bf16[64,1152]{1,0:T(8,128)(2,1)S(1)}, bf16[64,1152]{1,0:T(8,128)(2,1)S(1)}, u32[]{:S(2)}, u32[]{:S(2)}) collective-permute-start(bf16[64,1152]{1,0:T(8,128)(2,1)S(1)} %get-tuple-element.49.refs_0_), channel_id=1, source_target_pairs={{0,2},{4,0},{8,4},{12,8},{14,12},{10,14},{6,10},{2,6},{1,3},{5,1},... | collective-permute-start | bytes 442376 | tf_op jit(solution)/shard_map/ppermute | solution.py:53
  6.9 3.3 %collective-permute-done.6.refs_2_ = bf16[64,1152]{1,0:T(8,128)(2,1)S(1)} collective-permute-done((bf16[64,1152]{1,0:T(8,128)(2,1)S(1)}, bf16[64,1152]{1,0:T(8,128)(2,1)S(1)}, u32[]{:S(2)}, u32[]{:S(2)}) %collective-permute-start.6) | collective-permute-done | bytes 147488 | tf_op jit(solution)/shard_map/ppermute | solution.py:53
  12.2 3.1 %collective-permute-done.7.refs_3_ = bf16[64,1152]{1,0:T(8,128)(2,1)S(1)} collective-permute-done((bf16[64,1152]{1,0:T(8,128)(2,1)S(1)}, bf16[64,1152]{1,0:T(8,128)(2,1)S(1)}, u32[]{:S(2)}, u32[]{:S(2)}) %collective-permute-start.7) | collective-permute-done | bytes 147488 | tf_op jit(solution)/shard_map/ppermute | solution.py:53
  17.3 3.5 %collective-permute-done.9.refs_2_ = bf16[64,1152]{1,0:T(8,128)(2,1)S(1)} collective-permute-done((bf16[64,1152]{1,0:T(8,128)(2,1)S(1)}, bf16[64,1152]{1,0:T(8,128)(2,1)S(1)}, u32[]{:S(2)}, u32[]{:S(2)}) %collective-permute-start.9) | collective-permute-done | bytes 147488 | tf_op jit(solution)/shard_map/ppermute | solution.py:53
  23.0 3.1 %collective-permute-done.10.refs_3_ = bf16[64,1152]{1,0:T(8,128)(2,1)S(1)} collective-permute-done((bf16[64,1152]{1,0:T(8,128)(2,1)S(1)}, bf16[64,1152]{1,0:T(8,128)(2,1)S(1)}, u32[]{:S(2)}, u32[]{:S(2)}) %collective-permute-start.10) | collective-permute-done | bytes 147488 | tf_op jit(solution)/shard_map/ppermute | solution.py:53
  26.1 2.4 %collective-permute-start.11 = (bf16[64,1152]{1,0:T(8,128)(2,1)S(1)}, bf16[64,1152]{1,0:T(8,128)(2,1)S(1)}, u32[]{:S(2)}, u32[]{:S(2)}) collective-permute-start(bf16[64,1152]{1,0:T(8,128)(2,1)S(1)} %collective-permute-done.8.refs_0_), channel_id=1, source_target_pairs={{0,4},{4,8},{8,12},{12,14},{14,10},{10,6},{6,2},{2,0},{1,5},{5,9},... | collective-permute-start | bytes 442376 | tf_op jit(solution)/shard_map/ppermute | solution.py:53
  29.6 2.8 %collective-permute-done.11.refs_0_ = bf16[64,1152]{1,0:T(8,128)(2,1)S(1)} collective-permute-done((bf16[64,1152]{1,0:T(8,128)(2,1)S(1)}, bf16[64,1152]{1,0:T(8,128)(2,1)S(1)}, u32[]{:S(2)}, u32[]{:S(2)}) %collective-permute-start.11) | collective-permute-done | bytes 147488 | tf_op jit(solution)/shard_map/ppermute | solution.py:53
  32.4 2.5 %collective-permute-start.15 = (bf16[64,1152]{1,0:T(8,128)(2,1)S(1)}, bf16[64,1152]{1,0:T(8,128)(2,1)S(1)}, u32[]{:S(2)}, u32[]{:S(2)}) collective-permute-start(bf16[64,1152]{1,0:T(8,128)(2,1)S(1)} %collective-permute-done.11.refs_0_), channel_id=1, source_target_pairs={{0,4},{4,8},{8,12},{12,14},{14,10},{10,6},{6,2},{2,0},{1,5},{5,9},... | collective-permute-start | bytes 442376 | tf_op jit(solution)/shard_map/ppermute | solution.py:53
  46.1 3.1 %collective-permute-done.12.refs_1_ = bf16[64,1152]{1,0:T(8,128)(2,1)S(1)} collective-permute-done((bf16[64,1152]{1,0:T(8,128)(2,1)S(1)}, bf16[64,1152]{1,0:T(8,128)(2,1)S(1)}, u32[]{:S(2)}, u32[]{:S(2)}) %collective-permute-start.12) | collective-permute-done | bytes 147488 | tf_op jit(solution)/shard_map/ppermute | solution.py:53
  64.0 2.5 %collective-permute-start.23 = (bf16[64,1024]{1,0:T(8,128)(2,1)S(1)}, bf16[64,1024]{1,0:T(8,128)(2,1)S(1)}, u32[]{:S(2)}, u32[]{:S(2)}) collective-permute-start(bf16[64,1024]{1,0:T(8,128)(2,1)S(1)} %shard_map.115), channel_id=1, source_target_pairs={{0,2},{4,0},{8,4},{12,8},{14,12},{10,14},{6,10},{2,6},{1,3},{5,1},... | collective-permute-start | bytes 393224 | tf_op jit(solution)/shard_map/ppermute | solution.py:53
  73.6 2.3 %collective-permute-start.35 = (bf16[64,1024]{1,0:T(8,128)(2,1)S(1)}, bf16[64,1024]{1,0:T(8,128)(2,1)S(1)}, u32[]{:S(2)}, u32[]{:S(2)}) collective-permute-start(bf16[64,1024]{1,0:T(8,128)(2,1)S(1)} %shard_map.122.refs_3_), channel_id=1, source_target_pairs={{0,2},{4,0},{8,4},{12,8},{14,12},{10,14},{6,10},{2,6},{1,3},{5,1},... | collective-permute-start | bytes 393224 | tf_op jit(solution)/shard_map/ppermute | solution.py:53
  79.3 2.1 %collective-permute-start.36 = (bf16[64,1024]{1,0:T(8,128)(2,1)S(1)}, bf16[64,1024]{1,0:T(8,128)(2,1)S(1)}, u32[]{:S(2)}, u32[]{:S(2)}) collective-permute-start(bf16[64,1024]{1,0:T(8,128)(2,1)S(1)} %collective-permute-done.35.refs_7_), channel_id=1, source_target_pairs={{0,2},{4,0},{8,4},{12,8},{14,12},{10,14},{6,10},{2,6},{1,3},{5,1},... | collective-permute-start | bytes 393224 | tf_op jit(solution)/shard_map/ppermute | solution.py:53
  82.0 2.1 %collective-permute-start.43 = (bf16[64,1024]{1,0:T(8,128)(2,1)S(1)}, bf16[64,1024]{1,0:T(8,128)(2,1)S(1)}, u32[]{:S(2)}, u32[]{:S(2)}) collective-permute-start(bf16[64,1024]{1,0:T(8,128)(2,1)S(1)} %collective-permute-done.42.refs_6_), channel_id=1, source_target_pairs={{0,2},{4,0},{8,4},{12,8},{14,12},{10,14},{6,10},{2,6},{1,3},{5,1},... | collective-permute-start | bytes 393224 | tf_op jit(solution)/shard_map/ppermute | solution.py:53
  84.3 2.1 %collective-permute-start.37 = (bf16[64,1024]{1,0:T(8,128)(2,1)S(1)}, bf16[64,1024]{1,0:T(8,128)(2,1)S(1)}, u32[]{:S(2)}, u32[]{:S(2)}) collective-permute-start(bf16[64,1024]{1,0:T(8,128)(2,1)S(1)} %collective-permute-done.36.refs_7_), channel_id=1, source_target_pairs={{0,2},{4,0},{8,4},{12,8},{14,12},{10,14},{6,10},{2,6},{1,3},{5,1},... | collective-permute-start | bytes 393224 | tf_op jit(solution)/shard_map/ppermute | solution.py:53
  86.9 2.1 %collective-permute-start.44 = (bf16[64,1024]{1,0:T(8,128)(2,1)S(1)}, bf16[64,1024]{1,0:T(8,128)(2,1)S(1)}, u32[]{:S(2)}, u32[]{:S(2)}) collective-permute-start(bf16[64,1024]{1,0:T(8,128)(2,1)S(1)} %collective-permute-done.43.refs_6_), channel_id=1, source_target_pairs={{0,2},{4,0},{8,4},{12,8},{14,12},{10,14},{6,10},{2,6},{1,3},{5,1},... | collective-permute-start | bytes 393224 | tf_op jit(solution)/shard_map/ppermute | solution.py:53
  103.9 2.0 %collective-permute-start.47 = (bf16[8,1024]{1,0:T(8,128)(2,1)S(1)}, bf16[8,1024]{1,0:T(8,128)(2,1)S(1)}, u32[]{:S(2)}, u32[]{:S(2)}) collective-permute-start(bf16[8,1024]{1,0:T(8,128)(2,1)S(1)} %add_convert_fusion), channel_id=1, source_target_pairs={{0,8},{2,10},{4,12},{6,14},{8,0},{10,2},{12,4},{14,6},{1,9},{3,11}... | collective-permute-start | bytes 49160 | tf_op jit(solution)/shard_map/ppermute | solution.py:342
  105.9 2.7 %collective-permute-done.47 = bf16[8,1024]{1,0:T(8,128)(2,1)S(1)} collective-permute-done((bf16[8,1024]{1,0:T(8,128)(2,1)S(1)}, bf16[8,1024]{1,0:T(8,128)(2,1)S(1)}, u32[]{:S(2)}, u32[]{:S(2)}) %collective-permute-start.47) | collective-permute-done | bytes 16416 | tf_op jit(solution)/shard_map/ppermute | solution.py:342
  108.6 2.5 %shard_map.132 = (bf16[64,1024]{1,0:T(8,128)(2,1)S(1)}, bf16[64,1024]{1,0:T(8,128)(2,1)S(1)}) custom-call(bf16[64,1152]{1,0:T(8,128)(2,1)S(1)} %collective-permute-done.15.refs_0_, bf16[64,1152]{1,0:T(8,128)(2,1)S(1)} %collective-permute-done.16.refs_1_, bf16[64,1024]{1,0:T(8,128)(2,1)S(1)} %collective-permute-done.34.refs_2_, ...), custom_call_target="tpu_custom_call" | custom-call | flops 603979776 | bytes 5705728 | tf_op jit(solution)/shard_map/pallas_call | solution.py:29
  111.1 2.2 %collective-permute-start.48 = (bf16[64,1024]{1,0:T(8,128)(2,1)S(1)}, bf16[64,1024]{1,0:T(8,128)(2,1)S(1)}, u32[]{:S(2)}, u32[]{:S(2)}) collective-permute-start(bf16[64,1024]{1,0:T(8,128)(2,1)S(1)} %get-tuple-element.84), channel_id=1, source_target_pairs={{0,4},{4,8},{8,12},{12,14},{14,10},{10,6},{6,2},{2,0},{1,5},{5,9},... | collective-permute-start | bytes 393224 | tf_op jit(solution)/shard_map/ppermute | solution.py:53
  113.2 2.5 %shard_map.131 = (bf16[64,1024]{1,0:T(8,128)(2,1)S(1)}, f32[64,1024]{1,0:T(8,128)S(1)}, f32[64,1024]{1,0:T(8,128)S(1)}, bf16[64,1024]{1,0:T(8,128)(2,1)S(1)}) custom-call(bf16[64,1152]{1,0:T(8,128)(2,1)S(1)} %collective-permute-done.11.refs_0_, bf16[64,1152]{1,0:T(8,128)(2,1)S(1)} %collective-permute-done.12.refs_1_, ...), custom_call_target="tpu_custom_call" | custom-call | flops 1207959552 | bytes 6656000 | tf_op jit(solution)/shard_map/pallas_call | solution.py:29
  115.8 2.1 %collective-permute-start.52 = (bf16[64,1024]{1,0:T(8,128)(2,1)S(1)}, bf16[64,1024]{1,0:T(8,128)(2,1)S(1)}, u32[]{:S(2)}, u32[]{:S(2)}) collective-permute-start(bf16[64,1024]{1,0:T(8,128)(2,1)S(1)} %get-tuple-element.87), channel_id=1, source_target_pairs={{0,2},{4,0},{8,4},{12,8},{14,12},{10,14},{6,10},{2,6},{1,3},{5,1},... | collective-permute-start | bytes 393224 | tf_op jit(solution)/shard_map/ppermute | solution.py:53
  120.2 2.5 %shard_map.130 = (f32[64,1024]{1,0:T(8,128)S(1)}, f32[64,1024]{1,0:T(8,128)S(1)}, f32[64,1024]{1,0:T(8,128)S(1)}, f32[64,1024]{1,0:T(8,128)S(1)}) custom-call(bf16[64,1152]{1,0:T(8,128)(2,1)S(1)} %collective-permute-done.8.refs_0_, bf16[64,1152]{1,0:T(8,128)(2,1)S(1)} %get-tuple-element.55.refs_1_, bf16[64,1152]{1,0:T(8,128)(2,1)S(1)} %collective-permute-done.9.refs_2_, ...), custom_call_target="tpu_custom_call" | custom-call | flops 1207959552 | bytes 6656000 | tf_op jit(solution)/shard_map/pallas_call | solution.py:29
  127.1 2.5 %shard_map.129 = (f32[64,1024]{1,0:T(8,128)S(1)}, f32[64,1024]{1,0:T(8,128)S(1)}, f32[64,1024]{1,0:T(8,128)S(1)}, f32[64,1024]{1,0:T(8,128)S(1)}) custom-call(bf16[64,1152]{1,0:T(8,128)(2,1)S(1)} %collective-permute-done.5.refs_0_, bf16[64,1152]{1,0:T(8,128)(2,1)S(1)} %collective-permute-done.3.refs_1_, bf16[64,1152]{1,0:T(8,128)(2,1)S(1)} %collective-permute-done.6.refs_2_, ...), custom_call_target="tpu_custom_call" | custom-call | flops 1207959552 | bytes 6656000 | tf_op jit(solution)/shard_map/pallas_call | solution.py:29
  137.0 2.1 %shard_map.128 = (f32[64,1024]{1,0:T(8,128)S(1)}, f32[64,1024]{1,0:T(8,128)S(1)}) custom-call(bf16[64,1152]{1,0:T(8,128)(2,1)S(1)} %get-tuple-element.49.refs_0_, bf16[64,1152]{1,0:T(8,128)(2,1)S(1)} %get-tuple-element.50.refs_1_, bf16[64,1024]{1,0:T(8,128)(2,1)S(1)} %shard_map.116.refs_2_, bf16[64,1024]{1,0:T(8,128)(2,1)S(1)} %shard_map.122.refs_3_, ...), custom_call_target="tpu_custom_call" | custom-call | flops 603979776 | bytes 5705728 | tf_op jit(solution)/shard_map/pallas_call | solution.py:29
  (170 shorter events, 78.2 us)
Async XLA Ops:
  3.2 6.9 %collective-permute-start.6 = (bf16[64,1152]{1,0:T(8,128)(2,1)S(1)}, bf16[64,1152]{1,0:T(8,128)(2,1)S(1)}, u32[]{:S(2)}, u32[]{:S(2)}) collective-permute-start(bf16[64,1152]{1,0:T(8,128)(2,1)S(1)} %get-tuple-element.49.refs_0_), channel_id=1, source_target_pairs={{0,2},{4,0},{8,4},{12,8},{14,12},{10,14},{6,10},{2,6},{1,3},{5,1},... | collective-permute-start | bytes 442376 | tf_op jit(solution)/shard_map/ppermute | solution.py:53
  6.4 29.9 %collective-permute-start = (bf16[2,512,384]{2,1,0:T(8,128)(2,1)}, bf16[2,512,384]{2,1,0:T(8,128)(2,1)S(1)}, u32[]{:S(2)}, u32[]{:S(2)}) collective-permute-start(bf16[2,512,384]{2,1,0:T(8,128)(2,1)} %refs_0_.1), channel_id=1, source_target_pairs={{0,1},{1,0},{2,3},{3,2},{4,5},{5,4},{6,7},{7,6},{8,9},{9,8},{10,11... | collective-permute-start | bytes 2359304 | tf_op jit(solution)/shard_map/ppermute | solution.py:174
  6.4 31.5 %collective-permute-start.1 = (bf16[2,512,384]{2,1,0:T(8,128)(2,1)}, bf16[2,512,384]{2,1,0:T(8,128)(2,1)S(1)}, u32[]{:S(2)}, u32[]{:S(2)}) collective-permute-start(bf16[2,512,384]{2,1,0:T(8,128)(2,1)} %refs_2_.1), channel_id=1, source_target_pairs={{0,1},{1,0},{2,3},{3,2},{4,5},{5,4},{6,7},{7,6},{8,9},{9,8},{10,11... | collective-permute-start | bytes 2359304 | tf_op jit(solution)/shard_map/ppermute | solution.py:174
  6.9 31.0 %collective-permute-start.2 = (bf16[2,192,1024]{2,1,0:T(8,128)(2,1)}, bf16[2,192,1024]{2,1,0:T(8,128)(2,1)S(1)}, u32[]{:S(2)}, u32[]{:S(2)}) collective-permute-start(bf16[2,192,1024]{2,1,0:T(8,128)(2,1)} %refs_4_.1), channel_id=1, source_target_pairs={{0,1},{1,0},{2,3},{3,2},{4,5},{5,4},{6,7},{7,6},{8,9},{9,8},{10,11... | collective-permute-start | bytes 2359304 | tf_op jit(solution)/shard_map/ppermute | solution.py:174
  32.4 10.6 %collective-permute-start.15 = (bf16[64,1152]{1,0:T(8,128)(2,1)S(1)}, bf16[64,1152]{1,0:T(8,128)(2,1)S(1)}, u32[]{:S(2)}, u32[]{:S(2)}) collective-permute-start(bf16[64,1152]{1,0:T(8,128)(2,1)S(1)} %collective-permute-done.11.refs_0_), channel_id=1, source_target_pairs={{0,4},{4,8},{8,12},{12,14},{14,10},{10,6},{6,2},{2,0},{1,5},{5,9},... | collective-permute-start | bytes 442376 | tf_op jit(solution)/shard_map/ppermute | solution.py:53
  35.1 7.9 %collective-permute-start.16 = (bf16[64,1152]{1,0:T(8,128)(2,1)S(1)}, bf16[64,1152]{1,0:T(8,128)(2,1)S(1)}, u32[]{:S(2)}, u32[]{:S(2)}) collective-permute-start(bf16[64,1152]{1,0:T(8,128)(2,1)S(1)} %collective-permute-done.14.refs_3_), channel_id=1, source_target_pairs={{0,2},{4,0},{8,4},{12,8},{14,12},{10,14},{6,10},{2,6},{1,3},{5,1},... | collective-permute-start | bytes 442376 | tf_op jit(solution)/shard_map/ppermute | solution.py:53
  36.3 9.8 %collective-permute-start.13 = (bf16[64,1152]{1,0:T(8,128)(2,1)S(1)}, bf16[64,1152]{1,0:T(8,128)(2,1)S(1)}, u32[]{:S(2)}, u32[]{:S(2)}) collective-permute-start(bf16[64,1152]{1,0:T(8,128)(2,1)S(1)} %collective-permute-done.9.refs_2_), channel_id=1, source_target_pairs={{0,2},{4,0},{8,4},{12,8},{14,12},{10,14},{6,10},{2,6},{1,3},{5,1},... | collective-permute-start | bytes 442376 | tf_op jit(solution)/shard_map/ppermute | solution.py:53
  44.0 8.5 %collective-permute-start.17 = (bf16[64,1024]{1,0:T(8,128)(2,1)S(1)}, bf16[64,1024]{1,0:T(8,128)(2,1)S(1)}, u32[]{:S(2)}, u32[]{:S(2)}) collective-permute-start(bf16[64,1024]{1,0:T(8,128)(2,1)S(1)} %get-tuple-element.58), channel_id=1, source_target_pairs={{0,4},{4,8},{8,12},{12,14},{14,10},{10,6},{6,2},{2,0},{1,5},{5,9},... | collective-permute-start | bytes 393224 | tf_op jit(solution)/shard_map/ppermute | solution.py:53
  44.9 8.6 %collective-permute-start.27 = (bf16[64,1024]{1,0:T(8,128)(2,1)S(1)}, bf16[64,1024]{1,0:T(8,128)(2,1)S(1)}, u32[]{:S(2)}, u32[]{:S(2)}) collective-permute-start(bf16[64,1024]{1,0:T(8,128)(2,1)S(1)} %get-tuple-element.69), channel_id=1, source_target_pairs={{0,2},{4,0},{8,4},{12,8},{14,12},{10,14},{6,10},{2,6},{1,3},{5,1},... | collective-permute-start | bytes 393224 | tf_op jit(solution)/shard_map/ppermute | solution.py:53
  53.1 7.1 %collective-permute-start.24 = (bf16[64,1024]{1,0:T(8,128)(2,1)S(1)}, bf16[64,1024]{1,0:T(8,128)(2,1)S(1)}, u32[]{:S(2)}, u32[]{:S(2)}) collective-permute-start(bf16[64,1024]{1,0:T(8,128)(2,1)S(1)} %get-tuple-element.65), channel_id=1, source_target_pairs={{0,4},{4,8},{8,12},{12,14},{14,10},{10,6},{6,2},{2,0},{1,5},{5,9},... | collective-permute-start | bytes 393224 | tf_op jit(solution)/shard_map/ppermute | solution.py:53
  53.5 7.1 %collective-permute-start.28 = (bf16[64,1024]{1,0:T(8,128)(2,1)S(1)}, bf16[64,1024]{1,0:T(8,128)(2,1)S(1)}, u32[]{:S(2)}, u32[]{:S(2)}) collective-permute-start(bf16[64,1024]{1,0:T(8,128)(2,1)S(1)} %shard_map.119), channel_id=1, source_target_pairs={{0,2},{4,0},{8,4},{12,8},{14,12},{10,14},{6,10},{2,6},{1,3},{5,1},... | collective-permute-start | bytes 393224 | tf_op jit(solution)/shard_map/ppermute | solution.py:53
  58.6 8.0 %collective-permute-start.19 = (bf16[64,1024]{1,0:T(8,128)(2,1)S(1)}, bf16[64,1024]{1,0:T(8,128)(2,1)S(1)}, u32[]{:S(2)}, u32[]{:S(2)}) collective-permute-start(bf16[64,1024]{1,0:T(8,128)(2,1)S(1)} %shard_map.112), channel_id=1, source_target_pairs={{0,4},{4,8},{8,12},{12,14},{14,10},{10,6},{6,2},{2,0},{1,5},{5,9},... | collective-permute-start | bytes 393224 | tf_op jit(solution)/shard_map/ppermute | solution.py:53
  111.1 6.9 %collective-permute-start.48 = (bf16[64,1024]{1,0:T(8,128)(2,1)S(1)}, bf16[64,1024]{1,0:T(8,128)(2,1)S(1)}, u32[]{:S(2)}, u32[]{:S(2)}) collective-permute-start(bf16[64,1024]{1,0:T(8,128)(2,1)S(1)} %get-tuple-element.84), channel_id=1, source_target_pairs={{0,4},{4,8},{8,12},{12,14},{14,10},{10,6},{6,2},{2,0},{1,5},{5,9},... | collective-permute-start | bytes 393224 | tf_op jit(solution)/shard_map/ppermute | solution.py:53
  115.8 6.9 %collective-permute-start.52 = (bf16[64,1024]{1,0:T(8,128)(2,1)S(1)}, bf16[64,1024]{1,0:T(8,128)(2,1)S(1)}, u32[]{:S(2)}, u32[]{:S(2)}) collective-permute-start(bf16[64,1024]{1,0:T(8,128)(2,1)S(1)} %get-tuple-element.87), channel_id=1, source_target_pairs={{0,2},{4,0},{8,4},{12,8},{14,12},{10,14},{6,10},{2,6},{1,3},{5,1},... | collective-permute-start | bytes 393224 | tf_op jit(solution)/shard_map/ppermute | solution.py:53
  117.8 6.9 %collective-permute-start.55 = (bf16[64,1024]{1,0:T(8,128)(2,1)S(1)}, bf16[64,1024]{1,0:T(8,128)(2,1)S(1)}, u32[]{:S(2)}, u32[]{:S(2)}) collective-permute-start(bf16[64,1024]{1,0:T(8,128)(2,1)S(1)} %get-tuple-element.91), channel_id=1, source_target_pairs={{0,4},{4,8},{8,12},{12,14},{14,10},{10,6},{6,2},{2,0},{1,5},{5,9},... | collective-permute-start | bytes 393224 | tf_op jit(solution)/shard_map/ppermute | solution.py:53
  118.0 7.0 %collective-permute-start.49 = (bf16[64,1024]{1,0:T(8,128)(2,1)S(1)}, bf16[64,1024]{1,0:T(8,128)(2,1)S(1)}, u32[]{:S(2)}, u32[]{:S(2)}) collective-permute-start(bf16[64,1024]{1,0:T(8,128)(2,1)S(1)} %shard_map.133), channel_id=1, source_target_pairs={{0,4},{4,8},{8,12},{12,14},{14,10},{10,6},{6,2},{2,0},{1,5},{5,9},... | collective-permute-start | bytes 393224 | tf_op jit(solution)/shard_map/ppermute | solution.py:53
  120.0 6.9 %collective-permute-start.59 = (bf16[64,1024]{1,0:T(8,128)(2,1)S(1)}, bf16[64,1024]{1,0:T(8,128)(2,1)S(1)}, u32[]{:S(2)}, u32[]{:S(2)}) collective-permute-start(bf16[64,1024]{1,0:T(8,128)(2,1)S(1)} %shard_map.140), channel_id=1, source_target_pairs={{0,2},{4,0},{8,4},{12,8},{14,12},{10,14},{6,10},{2,6},{1,3},{5,1},... | collective-permute-start | bytes 393224 | tf_op jit(solution)/shard_map/ppermute | solution.py:53
  120.1 7.0 %collective-permute-start.62 = (bf16[8,1274]{1,0:T(8,128)(2,1)S(1)}, bf16[8,1274]{1,0:T(8,128)(2,1)S(1)}, u32[]{:S(2)}, u32[]{:S(2)}) collective-permute-start(bf16[8,1274]{1,0:T(8,128)(2,1)S(1)} %pad_maximum_fusion.1), channel_id=1, source_target_pairs={{0,1},{1,0},{2,3},{3,2},{4,5},{5,4},{6,7},{7,6},{8,9},{9,8},{10,11... | collective-permute-start | bytes 61160 | tf_op jit(solution)/shard_map/ppermute | solution.py:348
  122.8 6.9 %collective-permute-start.53 = (bf16[64,1024]{1,0:T(8,128)(2,1)S(1)}, bf16[64,1024]{1,0:T(8,128)(2,1)S(1)}, u32[]{:S(2)}, u32[]{:S(2)}) collective-permute-start(bf16[64,1024]{1,0:T(8,128)(2,1)S(1)} %shard_map.136), channel_id=1, source_target_pairs={{0,2},{4,0},{8,4},{12,8},{14,12},{10,14},{6,10},{2,6},{1,3},{5,1},... | collective-permute-start | bytes 393224 | tf_op jit(solution)/shard_map/ppermute | solution.py:53
  124.8 6.9 %collective-permute-start.56 = (bf16[64,1024]{1,0:T(8,128)(2,1)S(1)}, bf16[64,1024]{1,0:T(8,128)(2,1)S(1)}, u32[]{:S(2)}, u32[]{:S(2)}) collective-permute-start(bf16[64,1024]{1,0:T(8,128)(2,1)S(1)} %shard_map.138), channel_id=1, source_target_pairs={{0,4},{4,8},{8,12},{12,14},{14,10},{10,6},{6,2},{2,0},{1,5},{5,9},... | collective-permute-start | bytes 393224 | tf_op jit(solution)/shard_map/ppermute | solution.py:53
  125.0 8.5 %collective-permute-start.50 = (bf16[64,1024]{1,0:T(8,128)(2,1)S(1)}, bf16[64,1024]{1,0:T(8,128)(2,1)S(1)}, u32[]{:S(2)}, u32[]{:S(2)}) collective-permute-start(bf16[64,1024]{1,0:T(8,128)(2,1)S(1)} %shard_map.134), channel_id=1, source_target_pairs={{0,4},{4,8},{8,12},{12,14},{14,10},{10,6},{6,2},{2,0},{1,5},{5,9},... | collective-permute-start | bytes 393224 | tf_op jit(solution)/shard_map/ppermute | solution.py:53
  127.0 6.9 %collective-permute-start.60 = (bf16[64,1024]{1,0:T(8,128)(2,1)S(1)}, bf16[64,1024]{1,0:T(8,128)(2,1)S(1)}, u32[]{:S(2)}, u32[]{:S(2)}) collective-permute-start(bf16[64,1024]{1,0:T(8,128)(2,1)S(1)} %shard_map.141), channel_id=1, source_target_pairs={{0,2},{4,0},{8,4},{12,8},{14,12},{10,14},{6,10},{2,6},{1,3},{5,1},... | collective-permute-start | bytes 393224 | tf_op jit(solution)/shard_map/ppermute | solution.py:53
  129.7 9.3 %collective-permute-start.54 = (bf16[64,1024]{1,0:T(8,128)(2,1)S(1)}, bf16[64,1024]{1,0:T(8,128)(2,1)S(1)}, u32[]{:S(2)}, u32[]{:S(2)}) collective-permute-start(bf16[64,1024]{1,0:T(8,128)(2,1)S(1)} %shard_map.137), channel_id=1, source_target_pairs={{0,2},{4,0},{8,4},{12,8},{14,12},{10,14},{6,10},{2,6},{1,3},{5,1},... | collective-permute-start | bytes 393224 | tf_op jit(solution)/shard_map/ppermute | solution.py:53
  131.8 7.3 %collective-permute-start.57 = (bf16[64,1024]{1,0:T(8,128)(2,1)S(1)}, bf16[64,1024]{1,0:T(8,128)(2,1)S(1)}, u32[]{:S(2)}, u32[]{:S(2)}) collective-permute-start(bf16[64,1024]{1,0:T(8,128)(2,1)S(1)} %shard_map.139), channel_id=1, source_target_pairs={{0,4},{4,8},{8,12},{12,14},{14,10},{10,6},{6,2},{2,0},{1,5},{5,9},... | collective-permute-start | bytes 393224 | tf_op jit(solution)/shard_map/ppermute | solution.py:53
  (48 other events, 376.8 us)

commit v4 on v3

v4 whole, which is shorter than its diff:
```python
import functools

import jax
import jax.numpy as jnp
from jax import lax
from jax.experimental import pallas as pl
from jax.experimental.pallas import tpu as pltpu
from jax.sharding import PartitionSpec as P

LOSS_SCALE = 8.0
NORM_EPS = 1e-06
F32 = jnp.float32
BF16 = jnp.bfloat16
LANES = 128
VMEM_LIMIT = 32 * 1024 * 1024


def dot(left, right):
    return jnp.dot(left, right, preferred_element_type=F32)


def dot_t(left, right):
    return lax.dot_general(left, right, (((1,), (1,)), ((), ())), preferred_element_type=F32)


def call(kernel, outs, *args, flops=0):
    args = [pltpu.with_memory_space_constraint(a, pltpu.VMEM) for a in args]
    size = sum(a.size * a.dtype.itemsize for a in args)
    return pl.pallas_call(
        kernel,
        out_shape=[pltpu.VMEM(shape, dtype) for shape, dtype in outs],
        in_specs=[pl.BlockSpec(memory_space=pltpu.VMEM)] * len(args),
        out_specs=[pl.BlockSpec(memory_space=pltpu.VMEM)] * len(outs),
        compiler_params=pltpu.CompilerParams(vmem_limit_bytes=VMEM_LIMIT),
        cost_estimate=pl.CostEstimate(flops=flops, bytes_accessed=size, transcendentals=0),
    )(*args)


class Ring:
    def __init__(self, expert_count, group_count):
        self.count = expert_count
        self.half = expert_count // 2
        self.groups = group_count
        self.snake = group_count == 2
        if self.snake:
            self.order = list(range(0, expert_count, 2)) + list(range(expert_count - 1, 0, -2))
        else:
            self.order = list(range(expert_count))

    def send(self, value, away):
        pairs = []
        for i in range(self.count):
            for g in range(self.groups):
                there = self.order[(i + (1 if (g % 2 == 0) == away else -1)) % self.count]
                pairs.append((self.order[i] * self.groups + g, there * self.groups + g))
        return lax.ppermute(value, ("expert", "group"), pairs)

    def swap(self, value):
        return lax.ppermute(value, "group", [(g, g ^ 1) for g in range(self.groups)])

    def total(self, value):
        distance = 1
        while distance < self.count:
            other = lax.ppermute(
                value, "expert", [(e, e ^ distance) for e in range(self.count)]
            )
            value = (value.astype(F32) + other.astype(F32)).astype(BF16)
            distance *= 2
        return value

    def core(self):
        return lax.rem(lax.axis_index("group"), 2)

    def device_at(self, distance):
        here = lax.axis_index("expert")
        count = self.count
        if self.snake:
            here = jnp.where(here % 2 == 0, here // 2, count - 1 - here // 2)
        step = jnp.where(self.core() == 0, count - distance, distance)
        there = lax.rem(here + step, count)
        if self.snake:
            there = jnp.where(there < self.half, 2 * there, 2 * (count - 1 - there) + 1)
        return there

    def row_at(self, distance, other):
        core = self.core()
        return (1 - core if other else core) * self.count + self.device_at(distance)

    def gather(self, own, use, first=None):
        mid = own.shape[0] // 2
        mine, theirs = own, self.swap(own)
        use(0, (mine, theirs))
        for step in range(1, self.half):
            mine, theirs = self.send(mine, True), self.send(theirs, True)
            if first is not None and step == min(2, self.half - 1):
                theirs = first(theirs)
            use(step, (mine, theirs))

        def half_kernel(block_ref, out_ref):
            out_ref[...] = block_ref[pl.ds(pl.multiple_of(self.core() * mid, mid), mid), :]

        halves = [call(half_kernel, [((mid, own.shape[1]), own.dtype)], b)[0] for b in (mine, theirs)]
        use(self.half, tuple(self.send(h, True) for h in halves))

    def scatter(self, parts):
        mid = parts[self.half][0].shape[0]
        shape = parts[1][0].shape

        def half_kernel(block_ref, arrived_ref, out_ref):
            out_ref[...] = block_ref[...].astype(BF16)
            rows = pl.ds(pl.multiple_of(self.core() * mid, mid), mid)
            out_ref[rows, :] = (block_ref[rows, :] + arrived_ref[...].astype(F32)).astype(BF16)

        def add_kernel(block_ref, arrived_ref, out_ref):
            out_ref[...] = (block_ref[...] + arrived_ref[...].astype(F32)).astype(BF16)

        mine, theirs = parts[self.half]
        theirs, mine = self.send(theirs, False), self.send(mine, False)
        for step in range(self.half - 1, 0, -1):
            kernel = half_kernel if step == self.half - 1 else add_kernel
            theirs = self.send(call(kernel, [(shape, BF16)], parts[step][1], theirs)[0], False)
            mine = self.send(call(kernel, [(shape, BF16)], parts[step][0], mine)[0], False)
        return mine, self.swap(theirs)


def sum_kernel(own_ref, left_ref, right_ref, out_ref):
    arrived = left_ref[...].astype(F32) + right_ref[...].astype(F32)
    out_ref[...] = (own_ref[...] + arrived).astype(BF16)


def pack_kernel(ids_hbm, scores_hbm, tokens_hbm, out_ref, ids_ref, scores_ref, sems):
    rows, cols = tokens_hbm.shape
    token_copy = pltpu.make_async_copy(tokens_hbm, out_ref.at[:, pl.ds(0, cols)], sems.at[0])
    ids_copy = pltpu.make_async_copy(ids_hbm, ids_ref, sems.at[1])
    scores_copy = pltpu.make_async_copy(scores_hbm, scores_ref, sems.at[2])
    for copy in (ids_copy, scores_copy, token_copy):
        copy.start()
    ids_copy.wait()
    scores_copy.wait()
    scores = scores_ref[...]
    ids = ids_ref[...]
    route_weight = scores / jnp.sum(scores, axis=0, keepdims=True)
    expert = lax.broadcasted_iota(jnp.int32, (LANES // 2, rows), 0)
    weight_by = jnp.zeros((LANES // 2, rows), F32)
    for choice_k in range(scores.shape[0]):
        one = slice(choice_k, choice_k + 1)
        weight_by = weight_by + jnp.where(ids[one] == expert, route_weight[one], 0.0)
    high = weight_by.astype(BF16).astype(F32)
    out_ref[:, cols:] = jnp.concatenate([high, weight_by - high], axis=0).T.astype(BF16)
    token_copy.wait()


def pack(ids, scores, tokens):
    rows, cols = tokens.shape
    args = [pltpu.with_memory_space_constraint(a, pltpu.HBM) for a in (ids, scores, tokens)]
    return pl.pallas_call(
        pack_kernel,
        out_shape=pltpu.VMEM((rows, cols + LANES), BF16),
        in_specs=[pl.BlockSpec(memory_space=pl.ANY)] * 3,
        out_specs=pl.BlockSpec(memory_space=pltpu.VMEM),
        scratch_shapes=[
            pltpu.VMEM(ids.shape, ids.dtype),
            pltpu.VMEM(scores.shape, F32),
            pltpu.SemaphoreType.DMA((3,)),
        ],
        compiler_params=pltpu.CompilerParams(vmem_limit_bytes=VMEM_LIMIT),
    )(*args)


def assemble_kernel(shards, local_experts, *refs):
    gates, ups, downs = refs[:shards], refs[shards : 2 * shards], refs[2 * shards : 3 * shards]
    wide_ref, down_ref, _, sems = refs[3 * shards + 1 :]
    hidden_dim = gates[0].shape[2]
    copies = []

    def start(source, target):
        copies.append(pltpu.make_async_copy(source, target, sems.at[len(copies)]))
        copies[-1].start()

    for i in range(shards):
        place = 0
        if shards == 2:
            group = lax.axis_index("group")
            place = group if i == 0 else 1 - group
        depth, height = gates[i].shape[1], downs[i].shape[1]
        rows = pl.ds(pl.multiple_of(place * depth, 16), depth)
        for local in range(local_experts):
            begin = local * 2 * hidden_dim
            start(gates[i].at[local], wide_ref.at[rows, pl.ds(begin, hidden_dim)])
            start(ups[i].at[local], wide_ref.at[rows, pl.ds(begin + hidden_dim, hidden_dim)])
            top = pl.multiple_of(local * hidden_dim + place * height, 16)
            start(downs[i].at[local], down_ref.at[pl.ds(top, height), :])
    for copy in copies:
        copy.wait()


def exchange_shards(w_gate, w_up, w_down, group_count):
    shards = []
    for shard in (w_gate, w_up, w_down):
        if group_count == 2:
            shards += [shard, lax.ppermute(shard, "group", [(0, 1), (1, 0)])]
        else:
            shards += [lax.all_gather(shard, "group", axis=1, tiled=True)]
    return shards


def assemble(shards, local_experts, passed):
    count = len(shards) // 3
    hidden_dim = shards[0].shape[2]
    feature_dim = shards[-1].shape[2]
    if count == 2:
        shards = [
            pltpu.with_memory_space_constraint(w, pltpu.VMEM if i % 2 else pltpu.HBM)
            for i, w in enumerate(shards)
        ]
    return pl.pallas_call(
        functools.partial(assemble_kernel, count, local_experts),
        out_shape=[
            pltpu.VMEM((feature_dim, 2 * local_experts * hidden_dim), BF16),
            pltpu.VMEM((local_experts * hidden_dim, feature_dim), BF16),
            pltpu.VMEM(passed.shape, passed.dtype),
        ],
        in_specs=[
            pl.BlockSpec(memory_space=pltpu.VMEM if count == 2 and i % 2 else pl.ANY)
            for i in range(len(shards))
        ]
        + [pl.BlockSpec(memory_space=pltpu.VMEM)],
        out_specs=[pl.BlockSpec(memory_space=pltpu.VMEM)] * 3,
        scratch_shapes=[pltpu.SemaphoreType.DMA((3 * count * local_experts,))],
        input_output_aliases={len(shards): 2},
        compiler_params=pltpu.CompilerParams(vmem_limit_bytes=VMEM_LIMIT),
    )(*shards, pltpu.with_memory_space_constraint(passed, pltpu.VMEM))


def body(tokens, w_gate, w_up, w_down, route_ids, route_scores, norm_gain, class_head, targets):
    rows_here, feature_dim = tokens.shape
    expert_count = lax.axis_size("expert")
    group_count = lax.axis_size("group")
    local_experts, _, hidden_dim = w_gate.shape
    pair_dim = 2 * hidden_dim
    ring = Ring(expert_count, group_count)
    block = (rows_here, feature_dim)
    mid = rows_here // 2

    packed = pack(route_ids.T, route_scores.T, tokens)
    shards = exchange_shards(w_gate, w_up, w_down, group_count)
    weights_at = []

    def assemble_now(passed):
        wide, down, passed = assemble(shards, local_experts, passed)
        weights_at.extend([wide, down])
        return passed

    def rows_of(refs):
        return jnp.concatenate([ref[...] for ref in refs], axis=0) if len(refs) > 1 else refs[0][...]

    def forward_kernel(count, *refs):
        token_refs, (wide_ref, down_ref), outs = refs[:count], refs[count : count + 2], refs[count + 2 :]
        x = rows_of([ref.at[:, :feature_dim] for ref in token_refs])
        weights = rows_of([ref.at[:, feature_dim:] for ref in token_refs]).astype(F32)
        lane = lax.broadcasted_iota(jnp.int32, weights.shape, 1)
        total = None
        for local in range(local_experts):
            expert = lax.axis_index("expert") * local_experts + local
            mine = (lane == expert) | (lane == expert + LANES // 2)
            scale = jnp.sum(jnp.where(mine, weights, 0.0), axis=1, keepdims=True)
            act = dot(x, wide_ref[:, pl.ds(local * pair_dim, pair_dim)])
            gate_act, up_act = act[:, :hidden_dim], act[:, hidden_dim:]
            sigmoid_gate = jax.nn.sigmoid(gate_act)
            silu = gate_act * sigmoid_gate * scale
            slope = sigmoid_gate * (1.0 + gate_act * (1.0 - sigmoid_gate)) * scale
            cols = pl.ds(local * hidden_dim, hidden_dim)
            outs[0][:, cols] = (up_act * slope).astype(BF16)
            outs[1][:, cols] = silu.astype(BF16)
            hidden = (silu * up_act).astype(BF16)
            term = dot(hidden, down_ref[cols, :])
            total = term if total is None else total + term
        rows = total.shape[0] // len(outs[2:])
        for i, out in enumerate(outs[2:]):
            out[...] = total[i * rows : (i + 1) * rows].astype(out.dtype)

    tokens_at, part_at, saved_at = {}, {}, {}
    flops = 2 * feature_dim * hidden_dim * local_experts * 3

    def mine_at(blocks_at, k):
        return blocks_at[k][:1] if k == 0 else blocks_at[k]

    def part_outs(k):
        rows, dtype = (mid, BF16) if k == ring.half else (rows_here, F32)
        return [((rows, feature_dim), dtype)] * (1 if k == 0 else 2)

    def forward(k):
        blocks = mine_at(tokens_at, k)
        rows = sum(b.shape[0] for b in blocks)
        result = call(
            functools.partial(forward_kernel, len(blocks)),
            [((rows, local_experts * hidden_dim), BF16)] * 2 + part_outs(k),
            *blocks,
            *weights_at,
            flops=flops * rows,
        )
        saved_at[k] = result[:2]
        part_at[k] = result[2:]

    ring.gather(packed, tokens_at.__setitem__, assemble_now)
    wide, down = weights_at
    for k in tokens_at:
        forward(k)
    gain = norm_gain.reshape(1, feature_dim)
    moe_out = call(sum_kernel, [(block, BF16)], part_at[0][0], *ring.scatter(part_at))[0]
    moe_at = {}
    ring.gather(moe_out, moe_at.__setitem__)

    def residual_of(token_refs, moe_refs):
        token_rows = rows_of([ref.at[:, :feature_dim] for ref in token_refs]).astype(F32)
        return token_rows + rows_of(moe_refs).astype(F32)

    def inv_rms_of(residual):
        return lax.rsqrt(jnp.mean(residual * residual, axis=-1, keepdims=True) + NORM_EPS)

    def norm_kernel(*refs):
        residual = residual_of(refs[:2], refs[2:4])
        gain_ref, out_ref = refs[4:]
        normed = residual * inv_rms_of(residual) * gain_ref[...]
        row = lax.broadcasted_iota(jnp.int32, out_ref.shape, 0)
        pooled = jnp.zeros(out_ref.shape, F32)
        for i in range(2):
            part = normed[i * rows_here : (i + 1) * rows_here]
            mean = jnp.mean(part, axis=0, keepdims=True)
            pooled = jnp.where(row == ring.row_at(0, i), mean, pooled)
        out_ref[...] = pooled.astype(BF16)

    pooled_shape = (2 * expert_count, feature_dim)
    pooled = call(norm_kernel, [(pooled_shape, BF16)], *tokens_at[0], *moe_at[0], gain)[0]
    pooled = ring.total(pooled)
    target_own = targets.reshape(expert_count, -1).astype(F32)

    def target_kernel(own_ref, other_ref, out_ref):
        for i, ref in enumerate((own_ref, other_ref)):
            begin = (1 - ring.core() if i else ring.core()) * expert_count
            out_ref[pl.ds(pl.multiple_of(begin, expert_count), expert_count), :] = ref[...]

    target_shape = (2 * expert_count, target_own.shape[1])
    target_rows = call(target_kernel, [(target_shape, F32)], target_own, ring.swap(target_own))[0]
    logits = dot(pooled, class_head)
    logit_grad = (LOSS_SCALE * (jax.nn.sigmoid(logits) - target_rows)).astype(BF16)
    pooled_grad = ring.total(dot_t(logit_grad, class_head).astype(BF16)).astype(F32)

    if group_count > 2:
        both = jnp.concatenate([pooled, logit_grad], axis=1)
        both = lax.all_gather(both, "group", axis=0)[::2].reshape(-1, both.shape[1])
        pooled, logit_grad = both[:, :feature_dim], both[:, feature_dim:]
    head_grad = lax.dot_general(
        pooled, logit_grad, (((0,), (0,)), ((), ())), preferred_element_type=F32
    )

    def backward_kernel(k, count, *refs):
        residual = residual_of(refs[:count], refs[count : 2 * count])
        gate_save, up_save, grad_ref, gain_ref, wide_ref, down_ref = refs[2 * count : 2 * count + 6]
        outs = refs[2 * count + 6 :]
        inv_rms = inv_rms_of(residual)
        cube = inv_rms * inv_rms * inv_rms
        parts = []
        for i in range(count):
            some = residual.shape[0] // count
            rows = slice(i * some, (i + 1) * some)
            scaled = gain_ref[...] * grad_ref[pl.ds(ring.row_at(k, i), 1), :] / rows_here
            slope = cube[rows] * jnp.mean(residual[rows] * scaled, axis=-1, keepdims=True)
            parts.append(inv_rms[rows] * scaled - residual[rows] * slope)
        resid_grad = jnp.concatenate(parts, axis=0) if count > 1 else parts[0]
        down_back = dot_t(resid_grad.astype(BF16), down_ref[...])
        total = resid_grad if k == 0 else None
        for local in range(local_experts):
            cols = slice(local * hidden_dim, (local + 1) * hidden_dim)
            gate_grad = (down_back[:, cols] * gate_save[:, cols].astype(F32)).astype(BF16)
            up_grad = (down_back[:, cols] * up_save[:, cols].astype(F32)).astype(BF16)
            grads = jnp.concatenate([gate_grad, up_grad], axis=1)
            term = dot_t(grads, wide_ref[:, pl.ds(local * pair_dim, pair_dim)])
            total = term if total is None else total + term
        rows = total.shape[0] // len(outs)
        for i, out in enumerate(outs):
            out[...] = total[i * rows : (i + 1) * rows].astype(out.dtype)

    back_at = {}
    for k in reversed(list(tokens_at)):
        blocks = mine_at(tokens_at, k)
        back_at[k] = call(
            functools.partial(backward_kernel, k, len(blocks)),
            part_outs(k),
            *blocks,
            *mine_at(moe_at, k),
            *saved_at[k],
            pooled_grad,
            gain,
            wide,
            down,
            flops=flops * sum(b.shape[0] for b in blocks),
        )
    token_grad = pl.pallas_call(
        sum_kernel,
        out_shape=jax.ShapeDtypeStruct(block, BF16),
        in_specs=[pl.BlockSpec(memory_space=pltpu.VMEM)] * 3,
        out_specs=pl.BlockSpec(memory_space=pltpu.VMEM),
        compiler_params=pltpu.CompilerParams(vmem_limit_bytes=VMEM_LIMIT),
    )(back_at[0][0], *ring.scatter(back_at))
    return (token_grad, head_grad)


def solution(mesh):
    in_specs = (
        P(("rep", "expert", "group"), None),
        P("expert", "group", None),
        P("expert", "group", None),
        P("expert", "group", None),
        P(("rep", "expert", "group"), None),
        P(("rep", "expert", "group"), None),
        P(),
        P(None, "expert"),
        P("rep", "group", "expert"),
    )
    out_specs = (P(("rep", "expert", "group"), None), P("rep", "expert"))
    return jax.shard_map(body, mesh=mesh, in_specs=in_specs, out_specs=out_specs, check_vma=False)
```

time: 141 us -> 145 us (1.028)
  waiting for transfers between devices: 37.7 us -> 49 us
  local copies, waits for them, and re-layouts: 5.8 us -> 0.02 us
  starting transfers between devices: 70.7 us -> 69.2 us
    ppermute x60 -> x43, waiting for transfers between devices: 37.7 us -> 49 us  [the longest x32 42.4 us: send(): return lax.ppermute(value, ('expert', 'group'), pairs)]
    unnamed x18 -> x6, local copies, waits for them, and re-layouts: 5.79 us -> 0.02 us
    ppermute x60 -> x43, starting transfers between devices: 70.1 us -> 68.7 us  [the longest x32 58.4 us: send(): return lax.ppermute(value, ('expert', 'group'), pairs)]
    pallas_call x37 -> x29, Pallas kernels: 21.3 us -> 20.6 us  [call(): pl.pallas_call(kernel, out_shape=[pltpu.VMEM(shape, dtype) for shape, dty...]
  transfers between devices with their start and end apart: 63 -> 46, of which waited for: 24 -> 31; matrix products, arithmetic and copies ran while one was open for 1% -> 1% of each run, Pallas kernels for 14% -> 13%
where the time goes in v4:
time: 145 us
  starting transfers between devices  69.2 us (48%)
  waiting for transfers between devices  49 us (34%)
  Pallas kernels  24.1 us (17%)
  matrix products  1.72 us (1%)
    ppermute x32, starting transfers between devices, send(): return lax.ppermute(value, ('expert', 'group'), pairs)  58.4 us
    ppermute x32, waiting for transfers between devices, send(): return lax.ppermute(value, ('expert', 'group'), pairs)  42.4 us
    pallas_call x29, Pallas kernels, call(): pl.pallas_call(kernel, out_shape=[pltpu.VMEM(shape, dtype) for shape, dty...  20.6 us
    ppermute x6, starting transfers between devices, total(): lax.ppermute(value, 'expert', [(e, e ^ distance) for e in range(self.coun...  9.69 us
    ppermute x6, waiting for transfers between devices, total(): lax.ppermute(value, 'expert', [(e, e ^ distance) for e in range(self.coun...  3.9 us
  transfers between devices with their start and end apart: 46, of which 31 were waited for; matrix products, arithmetic and copies ran while one was open for 1% of the time, Pallas kernels for 13%

profile of v4, /device:TPU:0, one launch (start us, length us, event | category | flops | bytes accessed | tf_op | source)
XLA Modules:
  0.0 145.1 jit_solution(13841533402611040654)
XLA Ops:
  2.8 3.0 %collective-permute-start.6 = (bf16[128,1152]{1,0:T(8,128)(2,1)S(1)}, bf16[128,1152]{1,0:T(8,128)(2,1)S(1)}, u32[]{:S(2)}, u32[]{:S(2)}) collective-permute-start(bf16[128,1152]{1,0:T(8,128)(2,1)S(1)} %shard_map.104.refs_0_), channel_id=1, source_target_pairs={{0,4},{1,3},{4,8},{5,1},{8,12},{9,5},{12,14},{13,9},{14,10},{15,13... | collective-permute-start | bytes 884744 | tf_op jit(solution)/shard_map/ppermute | solution.py:56
  7.4 3.0 %collective-permute-done.6.refs_0_ = bf16[128,1152]{1,0:T(8,128)(2,1)S(1)} collective-permute-done((bf16[128,1152]{1,0:T(8,128)(2,1)S(1)}, bf16[128,1152]{1,0:T(8,128)(2,1)S(1)}, u32[]{:S(2)}, u32[]{:S(2)}) %collective-permute-start.6) | collective-permute-done | bytes 294944 | tf_op jit(solution)/shard_map/ppermute | solution.py:56
  10.4 2.1 %collective-permute-start.7 = (bf16[128,1152]{1,0:T(8,128)(2,1)S(1)}, bf16[128,1152]{1,0:T(8,128)(2,1)S(1)}, u32[]{:S(2)}, u32[]{:S(2)}) collective-permute-start(bf16[128,1152]{1,0:T(8,128)(2,1)S(1)} %collective-permute-done.6.refs_0_), channel_id=1, source_target_pairs={{0,4},{1,3},{4,8},{5,1},{8,12},{9,5},{12,14},{13,9},{14,10},{15,13... | collective-permute-start | bytes 884744 | tf_op jit(solution)/shard_map/ppermute | solution.py:56
  13.6 2.1 %collective-permute-start.5 = (bf16[128,1152]{1,0:T(8,128)(2,1)S(1)}, bf16[128,1152]{1,0:T(8,128)(2,1)S(1)}, u32[]{:S(2)}, u32[]{:S(2)}) collective-permute-start(bf16[128,1152]{1,0:T(8,128)(2,1)S(1)} %collective-permute-done.4.refs_1_), channel_id=1, source_target_pairs={{0,4},{1,3},{4,8},{5,1},{8,12},{9,5},{12,14},{13,9},{14,10},{15,13... | collective-permute-start | bytes 884744 | tf_op jit(solution)/shard_map/ppermute | solution.py:56
  17.2 2.1 %collective-permute-start.8 = (bf16[128,1152]{1,0:T(8,128)(2,1)S(1)}, bf16[128,1152]{1,0:T(8,128)(2,1)S(1)}, u32[]{:S(2)}, u32[]{:S(2)}) collective-permute-start(bf16[128,1152]{1,0:T(8,128)(2,1)S(1)} %collective-permute-done.7.refs_0_), channel_id=1, source_target_pairs={{0,4},{1,3},{4,8},{5,1},{8,12},{9,5},{12,14},{13,9},{14,10},{15,13... | collective-permute-start | bytes 884744 | tf_op jit(solution)/shard_map/ppermute | solution.py:56
  22.0 2.2 %collective-permute-start.9 = (bf16[128,1152]{1,0:T(8,128)(2,1)S(1)}, bf16[128,1152]{1,0:T(8,128)(2,1)S(1)}, u32[]{:S(2)}, u32[]{:S(2)}) collective-permute-start(bf16[128,1152]{1,0:T(8,128)(2,1)S(1)} %get-tuple-element.36.refs_1_), channel_id=1, source_target_pairs={{0,4},{1,3},{4,8},{5,1},{8,12},{9,5},{12,14},{13,9},{14,10},{15,13... | collective-permute-start | bytes 884744 | tf_op jit(solution)/shard_map/ppermute | solution.py:56
  26.1 2.7 %collective-permute-done.9.refs_1_.block_ref = bf16[128,1152]{1,0:T(8,128)(2,1)S(1)} collective-permute-done((bf16[128,1152]{1,0:T(8,128)(2,1)S(1)}, bf16[128,1152]{1,0:T(8,128)(2,1)S(1)}, u32[]{:S(2)}, u32[]{:S(2)}) %collective-permute-start.9) | collective-permute-done | bytes 294944 | tf_op jit(solution)/shard_map/ppermute | solution.py:56
  28.8 2.2 %collective-permute-start.11 = (bf16[64,1152]{1,0:T(8,128)(2,1)S(1)}, bf16[64,1152]{1,0:T(8,128)(2,1)S(1)}, u32[]{:S(2)}, u32[]{:S(2)}) collective-permute-start(bf16[64,1152]{1,0:T(8,128)(2,1)S(1)} %shard_map.111), channel_id=1, source_target_pairs={{0,4},{1,3},{4,8},{5,1},{8,12},{9,5},{12,14},{13,9},{14,10},{15,13... | collective-permute-start | bytes 442376 | tf_op jit(solution)/shard_map/ppermute | solution.py:56
  31.0 3.0 %collective-permute-done.11.refs_1_ = bf16[64,1152]{1,0:T(8,128)(2,1)S(1)} collective-permute-done((bf16[64,1152]{1,0:T(8,128)(2,1)S(1)}, bf16[64,1152]{1,0:T(8,128)(2,1)S(1)}, u32[]{:S(2)}, u32[]{:S(2)}) %collective-permute-start.11) | collective-permute-done | bytes 147488 | tf_op jit(solution)/shard_map/ppermute | solution.py:56
  35.1 2.1 %collective-permute-start.16 = (bf16[64,1024]{1,0:T(8,128)(2,1)S(1)}, bf16[64,1024]{1,0:T(8,128)(2,1)S(1)}, u32[]{:S(2)}, u32[]{:S(2)}) collective-permute-start(bf16[64,1024]{1,0:T(8,128)(2,1)S(1)} %get-tuple-element.43), channel_id=1, source_target_pairs={{0,2},{1,5},{4,0},{5,9},{8,4},{9,13},{12,8},{13,15},{14,12},{15,11... | collective-permute-start | bytes 393224 | tf_op jit(solution)/shard_map/ppermute | solution.py:56
  45.6 2.5 %collective-permute-done.12.arrived_ref = bf16[64,1024]{1,0:T(8,128)(2,1)S(1)} collective-permute-done((bf16[64,1024]{1,0:T(8,128)(2,1)S(1)}, bf16[64,1024]{1,0:T(8,128)(2,1)S(1)}, u32[]{:S(2)}, u32[]{:S(2)}) %collective-permute-start.12) | collective-permute-done | bytes 131104 | tf_op jit(solution)/shard_map/ppermute | solution.py:56
  65.0 2.6 %collective-permute-done.15.left_ref = bf16[128,1024]{1,0:T(8,128)(2,1)S(1)} collective-permute-done((bf16[128,1024]{1,0:T(8,128)(2,1)S(1)}, bf16[128,1024]{1,0:T(8,128)(2,1)S(1)}, u32[]{:S(2)}, u32[]{:S(2)}) %collective-permute-start.15) | collective-permute-done | bytes 262176 | tf_op jit(solution)/shard_map/ppermute | solution.py:56
  73.6 2.1 %collective-permute-start.23 = (bf16[16,1024]{1,0:T(8,128)(2,1)S(1)}, bf16[16,1024]{1,0:T(8,128)(2,1)S(1)}, u32[]{:S(2)}, u32[]{:S(2)}) collective-permute-start(bf16[16,1024]{1,0:T(8,128)(2,1)S(1)} %add_convert_fusion.5), channel_id=1, source_target_pairs={{0,4},{2,6},{4,0},{6,2},{8,12},{10,14},{12,8},{14,10},{1,5},{3,7},... | collective-permute-start | bytes 98312 | tf_op jit(solution)/shard_map/ppermute | solution.py:64
  77.6 3.1 %collective-permute-start.24 = (bf16[16,1024]{1,0:T(8,128)(2,1)S(1)}, bf16[16,1024]{1,0:T(8,128)(2,1)S(1)}, u32[]{:S(2)}, u32[]{:S(2)}) collective-permute-start(bf16[16,1024]{1,0:T(8,128)(2,1)S(1)} %add_convert_fusion.4), channel_id=1, source_target_pairs={{0,8},{2,10},{4,12},{6,14},{8,0},{10,2},{12,4},{14,6},{1,9},{3,11}... | collective-permute-start | bytes 98312 | tf_op jit(solution)/shard_map/ppermute | solution.py:64
  83.9 2.0 %collective-permute-start.26 = (bf16[16,1024]{1,0:T(8,128)(2,1)S(1)}, bf16[16,1024]{1,0:T(8,128)(2,1)S(1)}, u32[]{:S(2)}, u32[]{:S(2)}) collective-permute-start(bf16[16,1024]{1,0:T(8,128)(2,1)S(1)} %convolution_convert_fusion), channel_id=1, source_target_pairs={{0,2},{2,0},{4,6},{6,4},{8,10},{10,8},{12,14},{14,12},{1,3},{3,1},... | collective-permute-start | bytes 98312 | tf_op jit(solution)/shard_map/ppermute | solution.py:64
  85.9 2.7 %collective-permute-done.29.refs_2_ = bf16[128,1024]{1,0:T(8,128)(2,1)S(1)} collective-permute-done((bf16[128,1024]{1,0:T(8,128)(2,1)S(1)}, bf16[128,1024]{1,0:T(8,128)(2,1)S(1)}, u32[]{:S(2)}, u32[]{:S(2)}) %collective-permute-start.29) | collective-permute-done | bytes 262176 | tf_op jit(solution)/shard_map/ppermute | solution.py:56
  92.7 2.3 %collective-permute-done.31.refs_2_ = bf16[128,1024]{1,0:T(8,128)(2,1)S(1)} collective-permute-done((bf16[128,1024]{1,0:T(8,128)(2,1)S(1)}, bf16[128,1024]{1,0:T(8,128)(2,1)S(1)}, u32[]{:S(2)}, u32[]{:S(2)}) %collective-permute-start.31) | collective-permute-done | bytes 262176 | tf_op jit(solution)/shard_map/ppermute | solution.py:56
  106.4 2.8 %collective-permute-done.36.refs_3_ = bf16[64,1024]{1,0:T(8,128)(2,1)S(1)} collective-permute-done((bf16[64,1024]{1,0:T(8,128)(2,1)S(1)}, bf16[64,1024]{1,0:T(8,128)(2,1)S(1)}, u32[]{:S(2)}, u32[]{:S(2)}) %collective-permute-start.36) | collective-permute-done | bytes 131104 | tf_op jit(solution)/shard_map/ppermute | solution.py:56
  109.2 2.5 %shard_map.128 = (bf16[64,1024]{1,0:T(8,128)(2,1)S(1)}, bf16[64,1024]{1,0:T(8,128)(2,1)S(1)}) custom-call(bf16[64,1152]{1,0:T(8,128)(2,1)S(1)} %collective-permute-done.10.refs_0_, bf16[64,1152]{1,0:T(8,128)(2,1)S(1)} %collective-permute-done.11.refs_1_, bf16[64,1024]{1,0:T(8,128)(2,1)S(1)} %collective-permute-done.35.refs_2_, ...), custom_call_target="tpu_custom_call" | custom-call | flops 603979776 | bytes 5738496 | tf_op jit(solution)/shard_map/pallas_call | solution.py:29
  111.7 2.0 %collective-permute-start.41 = (bf16[64,1024]{1,0:T(8,128)(2,1)S(1)}, bf16[64,1024]{1,0:T(8,128)(2,1)S(1)}, u32[]{:S(2)}, u32[]{:S(2)}) collective-permute-start(bf16[64,1024]{1,0:T(8,128)(2,1)S(1)} %get-tuple-element.61), channel_id=1, source_target_pairs={{0,2},{1,5},{4,0},{5,9},{8,4},{9,13},{12,8},{13,15},{14,12},{15,11... | collective-permute-start | bytes 393224 | tf_op jit(solution)/shard_map/ppermute | solution.py:56
  113.7 2.5 %shard_map.125 = (f32[128,1024]{1,0:T(8,128)S(1)}, f32[128,1024]{1,0:T(8,128)S(1)}) custom-call(bf16[128,1152]{1,0:T(8,128)(2,1)S(1)} %collective-permute-done.8.refs_0_.block_ref, bf16[128,1152]{1,0:T(8,128)(2,1)S(1)} %collective-permute-done.9.refs_1_.block_ref, bf16[128,1024]{1,0:T(8,128)(2,1)S(1)} %collective-permute-done.33.refs_2_.block_ref, ...), custom_call_target="tpu_custom_call" | custom-call | flops 1207959552 | bytes 6688768 | tf_op jit(solution)/shard_map/pallas_call | solution.py:29
  120.7 2.5 %shard_map.124 = (f32[128,1024]{1,0:T(8,128)S(1)}, f32[128,1024]{1,0:T(8,128)S(1)}) custom-call(bf16[128,1152]{1,0:T(8,128)(2,1)S(1)} %collective-permute-done.7.refs_0_, bf16[128,1152]{1,0:T(8,128)(2,1)S(1)} %get-tuple-element.36.refs_1_, bf16[128,1024]{1,0:T(8,128)(2,1)S(1)} %collective-permute-done.31.refs_2_, ...), custom_call_target="tpu_custom_call" | custom-call | flops 1207959552 | bytes 6688768 | tf_op jit(solution)/shard_map/pallas_call | solution.py:29
  128.8 2.5 %shard_map.123 = (f32[128,1024]{1,0:T(8,128)S(1)}, f32[128,1024]{1,0:T(8,128)S(1)}) custom-call(bf16[128,1152]{1,0:T(8,128)(2,1)S(1)} %collective-permute-done.6.refs_0_, bf16[128,1152]{1,0:T(8,128)(2,1)S(1)} %collective-permute-done.4.refs_1_, bf16[128,1024]{1,0:T(8,128)(2,1)S(1)} %collective-permute-done.29.refs_2_, ...), custom_call_target="tpu_custom_call" | custom-call | flops 1207959552 | bytes 6688768 | tf_op jit(solution)/shard_map/pallas_call | solution.py:29
  141.9 2.0 %shard_map.122.own_ref = f32[128,1024]{1,0:T(8,128)S(1)} custom-call(bf16[128,1152]{1,0:T(8,128)(2,1)S(1)} %shard_map.104.refs_0_, bf16[128,1024]{1,0:T(8,128)(2,1)S(1)} %shard_map.119.refs_2_.refs_1_, bf16[128,768]{1,0:T(8,128)(2,1)S(1)} %get-tuple-element.44.refs_2_, bf16[128,768]{1,0:T(8,128)(2,1)S(1)} %get-tuple-element.45.refs_3_, ...), custom_call_target="tpu_custom_call" | custom-call | flops 603979776 | bytes 5738496 | tf_op jit(solution)/shard_map/pallas_call | solution.py:29
  (115 shorter events, 85.4 us)
Async XLA Ops:
  2.2 17.0 %collective-permute-start = (bf16[2,512,384]{2,1,0:T(8,128)(2,1)}, bf16[2,512,384]{2,1,0:T(8,128)(2,1)S(1)}, u32[]{:S(2)}, u32[]{:S(2)}) collective-permute-start(bf16[2,512,384]{2,1,0:T(8,128)(2,1)} %refs_0_.1), channel_id=1, source_target_pairs={{0,1},{1,0},{2,3},{3,2},{4,5},{5,4},{6,7},{7,6},{8,9},{9,8},{10,11... | collective-permute-start | bytes 2359304 | tf_op jit(solution)/shard_map/ppermute | solution.py:201
  2.3 17.0 %collective-permute-start.1 = (bf16[2,512,384]{2,1,0:T(8,128)(2,1)}, bf16[2,512,384]{2,1,0:T(8,128)(2,1)S(1)}, u32[]{:S(2)}, u32[]{:S(2)}) collective-permute-start(bf16[2,512,384]{2,1,0:T(8,128)(2,1)} %refs_2_.1), channel_id=1, source_target_pairs={{0,1},{1,0},{2,3},{3,2},{4,5},{5,4},{6,7},{7,6},{8,9},{9,8},{10,11... | collective-permute-start | bytes 2359304 | tf_op jit(solution)/shard_map/ppermute | solution.py:201
  2.7 16.5 %collective-permute-start.2 = (bf16[2,192,1024]{2,1,0:T(8,128)(2,1)}, bf16[2,192,1024]{2,1,0:T(8,128)(2,1)S(1)}, u32[]{:S(2)}, u32[]{:S(2)}) collective-permute-start(bf16[2,192,1024]{2,1,0:T(8,128)(2,1)} %refs_4_.1), channel_id=1, source_target_pairs={{0,1},{1,0},{2,3},{3,2},{4,5},{5,4},{6,7},{7,6},{8,9},{9,8},{10,11... | collective-permute-start | bytes 2359304 | tf_op jit(solution)/shard_map/ppermute | solution.py:201
  2.8 7.6 %collective-permute-start.6 = (bf16[128,1152]{1,0:T(8,128)(2,1)S(1)}, bf16[128,1152]{1,0:T(8,128)(2,1)S(1)}, u32[]{:S(2)}, u32[]{:S(2)}) collective-permute-start(bf16[128,1152]{1,0:T(8,128)(2,1)S(1)} %shard_map.104.refs_0_), channel_id=1, source_target_pairs={{0,4},{1,3},{4,8},{5,1},{8,12},{9,5},{12,14},{13,9},{14,10},{15,13... | collective-permute-start | bytes 884744 | tf_op jit(solution)/shard_map/ppermute | solution.py:56
  5.8 7.8 %collective-permute-start.4 = (bf16[128,1152]{1,0:T(8,128)(2,1)S(1)}, bf16[128,1152]{1,0:T(8,128)(2,1)S(1)}, u32[]{:S(2)}, u32[]{:S(2)}) collective-permute-start(bf16[128,1152]{1,0:T(8,128)(2,1)S(1)} %collective-permute-done.3.refs_1_), channel_id=1, source_target_pairs={{0,4},{1,3},{4,8},{5,1},{8,12},{9,5},{12,14},{13,9},{14,10},{15,13... | collective-permute-start | bytes 884744 | tf_op jit(solution)/shard_map/ppermute | solution.py:56
  10.4 6.7 %collective-permute-start.7 = (bf16[128,1152]{1,0:T(8,128)(2,1)S(1)}, bf16[128,1152]{1,0:T(8,128)(2,1)S(1)}, u32[]{:S(2)}, u32[]{:S(2)}) collective-permute-start(bf16[128,1152]{1,0:T(8,128)(2,1)S(1)} %collective-permute-done.6.refs_0_), channel_id=1, source_target_pairs={{0,4},{1,3},{4,8},{5,1},{8,12},{9,5},{12,14},{13,9},{14,10},{15,13... | collective-permute-start | bytes 884744 | tf_op jit(solution)/shard_map/ppermute | solution.py:56
  13.6 6.7 %collective-permute-start.5 = (bf16[128,1152]{1,0:T(8,128)(2,1)S(1)}, bf16[128,1152]{1,0:T(8,128)(2,1)S(1)}, u32[]{:S(2)}, u32[]{:S(2)}) collective-permute-start(bf16[128,1152]{1,0:T(8,128)(2,1)S(1)} %collective-permute-done.4.refs_1_), channel_id=1, source_target_pairs={{0,4},{1,3},{4,8},{5,1},{8,12},{9,5},{12,14},{13,9},{14,10},{15,13... | collective-permute-start | bytes 884744 | tf_op jit(solution)/shard_map/ppermute | solution.py:56
  17.2 7.0 %collective-permute-start.8 = (bf16[128,1152]{1,0:T(8,128)(2,1)S(1)}, bf16[128,1152]{1,0:T(8,128)(2,1)S(1)}, u32[]{:S(2)}, u32[]{:S(2)}) collective-permute-start(bf16[128,1152]{1,0:T(8,128)(2,1)S(1)} %collective-permute-done.7.refs_0_), channel_id=1, source_target_pairs={{0,4},{1,3},{4,8},{5,1},{8,12},{9,5},{12,14},{13,9},{14,10},{15,13... | collective-permute-start | bytes 884744 | tf_op jit(solution)/shard_map/ppermute | solution.py:56
  22.0 6.8 %collective-permute-start.9 = (bf16[128,1152]{1,0:T(8,128)(2,1)S(1)}, bf16[128,1152]{1,0:T(8,128)(2,1)S(1)}, u32[]{:S(2)}, u32[]{:S(2)}) collective-permute-start(bf16[128,1152]{1,0:T(8,128)(2,1)S(1)} %get-tuple-element.36.refs_1_), channel_id=1, source_target_pairs={{0,4},{1,3},{4,8},{5,1},{8,12},{9,5},{12,14},{13,9},{14,10},{15,13... | collective-permute-start | bytes 884744 | tf_op jit(solution)/shard_map/ppermute | solution.py:56
  24.2 6.8 %collective-permute-start.10 = (bf16[64,1152]{1,0:T(8,128)(2,1)S(1)}, bf16[64,1152]{1,0:T(8,128)(2,1)S(1)}, u32[]{:S(2)}, u32[]{:S(2)}) collective-permute-start(bf16[64,1152]{1,0:T(8,128)(2,1)S(1)} %shard_map.110), channel_id=1, source_target_pairs={{0,4},{1,3},{4,8},{5,1},{8,12},{9,5},{12,14},{13,9},{14,10},{15,13... | collective-permute-start | bytes 442376 | tf_op jit(solution)/shard_map/ppermute | solution.py:56
  40.3 9.9 %collective-permute-start.17 = (bf16[128,1024]{1,0:T(8,128)(2,1)S(1)}, bf16[128,1024]{1,0:T(8,128)(2,1)S(1)}, u32[]{:S(2)}, u32[]{:S(2)}) collective-permute-start(bf16[128,1024]{1,0:T(8,128)(2,1)S(1)} %shard_map.116), channel_id=1, source_target_pairs={{0,2},{1,5},{4,0},{5,9},{8,4},{9,13},{12,8},{13,15},{14,12},{15,11... | collective-permute-start | bytes 786440 | tf_op jit(solution)/shard_map/ppermute | solution.py:56
  48.2 6.4 %collective-permute-start.13 = (bf16[128,1024]{1,0:T(8,128)(2,1)S(1)}, bf16[128,1024]{1,0:T(8,128)(2,1)S(1)}, u32[]{:S(2)}, u32[]{:S(2)}) collective-permute-start(bf16[128,1024]{1,0:T(8,128)(2,1)S(1)} %shard_map.113), channel_id=1, source_target_pairs={{0,2},{1,5},{4,0},{5,9},{8,4},{9,13},{12,8},{13,15},{14,12},{15,11... | collective-permute-start | bytes 786440 | tf_op jit(solution)/shard_map/ppermute | solution.py:56
  50.2 7.2 %collective-permute-start.18 = (bf16[128,1024]{1,0:T(8,128)(2,1)S(1)}, bf16[128,1024]{1,0:T(8,128)(2,1)S(1)}, u32[]{:S(2)}, u32[]{:S(2)}) collective-permute-start(bf16[128,1024]{1,0:T(8,128)(2,1)S(1)} %shard_map.117), channel_id=1, source_target_pairs={{0,2},{1,5},{4,0},{5,9},{8,4},{9,13},{12,8},{13,15},{14,12},{15,11... | collective-permute-start | bytes 786440 | tf_op jit(solution)/shard_map/ppermute | solution.py:56
  57.4 6.4 %collective-permute-start.19 = (bf16[128,1024]{1,0:T(8,128)(2,1)S(1)}, bf16[128,1024]{1,0:T(8,128)(2,1)S(1)}, u32[]{:S(2)}, u32[]{:S(2)}) collective-permute-start(bf16[128,1024]{1,0:T(8,128)(2,1)S(1)} %shard_map.118), channel_id=1, source_target_pairs={{0,2},{1,5},{4,0},{5,9},{8,4},{9,13},{12,8},{13,15},{14,12},{15,11... | collective-permute-start | bytes 786440 | tf_op jit(solution)/shard_map/ppermute | solution.py:56
  81.9 6.7 %collective-permute-start.29 = (bf16[128,1024]{1,0:T(8,128)(2,1)S(1)}, bf16[128,1024]{1,0:T(8,128)(2,1)S(1)}, u32[]{:S(2)}, u32[]{:S(2)}) collective-permute-start(bf16[128,1024]{1,0:T(8,128)(2,1)S(1)} %shard_map.119.refs_2_.refs_1_), channel_id=1, source_target_pairs={{0,4},{1,3},{4,8},{5,1},{8,12},{9,5},{12,14},{13,9},{14,10},{15,13... | collective-permute-start | bytes 786440 | tf_op jit(solution)/shard_map/ppermute | solution.py:56
  83.4 8.0 %collective-permute-start.30 = (bf16[128,1024]{1,0:T(8,128)(2,1)S(1)}, bf16[128,1024]{1,0:T(8,128)(2,1)S(1)}, u32[]{:S(2)}, u32[]{:S(2)}) collective-permute-start(bf16[128,1024]{1,0:T(8,128)(2,1)S(1)} %collective-permute-done.21.refs_3_), channel_id=1, source_target_pairs={{0,4},{1,3},{4,8},{5,1},{8,12},{9,5},{12,14},{13,9},{14,10},{15,13... | collective-permute-start | bytes 786440 | tf_op jit(solution)/shard_map/ppermute | solution.py:56
  83.9 8.7 %collective-permute-start.26 = (bf16[16,1024]{1,0:T(8,128)(2,1)S(1)}, bf16[16,1024]{1,0:T(8,128)(2,1)S(1)}, u32[]{:S(2)}, u32[]{:S(2)}) collective-permute-start(bf16[16,1024]{1,0:T(8,128)(2,1)S(1)} %convolution_convert_fusion), channel_id=1, source_target_pairs={{0,2},{2,0},{4,6},{6,4},{8,10},{10,8},{12,14},{14,12},{1,3},{3,1},... | collective-permute-start | bytes 98312 | tf_op jit(solution)/shard_map/ppermute | solution.py:64
  92.6 6.7 %collective-permute-start.27 = (bf16[16,1024]{1,0:T(8,128)(2,1)S(1)}, bf16[16,1024]{1,0:T(8,128)(2,1)S(1)}, u32[]{:S(2)}, u32[]{:S(2)}) collective-permute-start(bf16[16,1024]{1,0:T(8,128)(2,1)S(1)} %add_convert_fusion.2), channel_id=1, source_target_pairs={{0,4},{2,6},{4,0},{6,2},{8,12},{10,14},{12,8},{14,10},{1,5},{3,7},... | collective-permute-start | bytes 98312 | tf_op jit(solution)/shard_map/ppermute | solution.py:64
  99.4 6.8 %collective-permute-start.28 = (bf16[16,1024]{1,0:T(8,128)(2,1)S(1)}, bf16[16,1024]{1,0:T(8,128)(2,1)S(1)}, u32[]{:S(2)}, u32[]{:S(2)}) collective-permute-start(bf16[16,1024]{1,0:T(8,128)(2,1)S(1)} %add_convert_fusion.1), channel_id=1, source_target_pairs={{0,8},{2,10},{4,12},{6,14},{8,0},{10,2},{12,4},{14,6},{1,9},{3,11}... | collective-permute-start | bytes 98312 | tf_op jit(solution)/shard_map/ppermute | solution.py:64
  116.9 9.7 %collective-permute-start.42 = (bf16[128,1024]{1,0:T(8,128)(2,1)S(1)}, bf16[128,1024]{1,0:T(8,128)(2,1)S(1)}, u32[]{:S(2)}, u32[]{:S(2)}) collective-permute-start(bf16[128,1024]{1,0:T(8,128)(2,1)S(1)} %shard_map.132), channel_id=1, source_target_pairs={{0,2},{1,5},{4,0},{5,9},{8,4},{9,13},{12,8},{13,15},{14,12},{15,11... | collective-permute-start | bytes 786440 | tf_op jit(solution)/shard_map/ppermute | solution.py:56
  124.8 6.5 %collective-permute-start.38 = (bf16[128,1024]{1,0:T(8,128)(2,1)S(1)}, bf16[128,1024]{1,0:T(8,128)(2,1)S(1)}, u32[]{:S(2)}, u32[]{:S(2)}) collective-permute-start(bf16[128,1024]{1,0:T(8,128)(2,1)S(1)} %shard_map.129), channel_id=1, source_target_pairs={{0,2},{1,5},{4,0},{5,9},{8,4},{9,13},{12,8},{13,15},{14,12},{15,11... | collective-permute-start | bytes 786440 | tf_op jit(solution)/shard_map/ppermute | solution.py:56
  126.8 7.3 %collective-permute-start.43 = (bf16[128,1024]{1,0:T(8,128)(2,1)S(1)}, bf16[128,1024]{1,0:T(8,128)(2,1)S(1)}, u32[]{:S(2)}, u32[]{:S(2)}) collective-permute-start(bf16[128,1024]{1,0:T(8,128)(2,1)S(1)} %shard_map.133), channel_id=1, source_target_pairs={{0,2},{1,5},{4,0},{5,9},{8,4},{9,13},{12,8},{13,15},{14,12},{15,11... | collective-permute-start | bytes 786440 | tf_op jit(solution)/shard_map/ppermute | solution.py:56
  131.4 6.4 %collective-permute-start.39 = (bf16[128,1024]{1,0:T(8,128)(2,1)S(1)}, bf16[128,1024]{1,0:T(8,128)(2,1)S(1)}, u32[]{:S(2)}, u32[]{:S(2)}) collective-permute-start(bf16[128,1024]{1,0:T(8,128)(2,1)S(1)} %shard_map.130), channel_id=1, source_target_pairs={{0,2},{1,5},{4,0},{5,9},{8,4},{9,13},{12,8},{13,15},{14,12},{15,11... | collective-permute-start | bytes 786440 | tf_op jit(solution)/shard_map/ppermute | solution.py:56
  134.1 6.5 %collective-permute-start.44 = (bf16[128,1024]{1,0:T(8,128)(2,1)S(1)}, bf16[128,1024]{1,0:T(8,128)(2,1)S(1)}, u32[]{:S(2)}, u32[]{:S(2)}) collective-permute-start(bf16[128,1024]{1,0:T(8,128)(2,1)S(1)} %shard_map.134), channel_id=1, source_target_pairs={{0,2},{1,5},{4,0},{5,9},{8,4},{9,13},{12,8},{13,15},{14,12},{15,11... | collective-permute-start | bytes 786440 | tf_op jit(solution)/shard_map/ppermute | solution.py:56
  (25 other events, 220.8 us)

commit v5 on v4

--- a/solution.py
+++ b/solution.py
@@ -47,24 +47,29 @@
         else:
             self.order = list(range(expert_count))
 
-    def send(self, value, away):
+    def send(self, value, away, cross=False):
         pairs = []
         for i in range(self.count):
             for g in range(self.groups):
-                there = self.order[(i + (1 if (g % 2 == 0) == away else -1)) % self.count]
-                pairs.append((self.order[i] * self.groups + g, there * self.groups + g))
+                right = (g % 2 == 0) == (away != (cross and away))
+                there = self.order[(i + (1 if right else -1)) % self.count]
+                pairs.append((self.order[i] * self.groups + g, there * self.groups + (g ^ cross)))
         return lax.ppermute(value, ("expert", "group"), pairs)
 
     def swap(self, value):
         return lax.ppermute(value, "group", [(g, g ^ 1) for g in range(self.groups)])
 
-    def total(self, value):
+    def total(self, value, guards):
+        def round_kernel(mine_ref, other_ref, guard_ref, out_ref):
+            out_ref[...] = (mine_ref[...].astype(F32) + other_ref[...].astype(F32)).astype(BF16)
+
         distance = 1
         while distance < self.count:
             other = lax.ppermute(
                 value, "expert", [(e, e ^ distance) for e in range(self.count)]
             )
-            value = (value.astype(F32) + other.astype(F32)).astype(BF16)
+            guard = guards.pop(0) if len(guards) > 1 else guards[0]
+            value = call(round_kernel, [(value.shape, BF16)], value, other, guard)[0]
             distance *= 2
         return value
 
@@ -82,18 +87,13 @@
             there = jnp.where(there < self.half, 2 * there, 2 * (count - 1 - there) + 1)
         return there
 
-    def row_at(self, distance, other):
-        core = self.core()
-        return (1 - core if other else core) * self.count + self.device_at(distance)
-
-    def gather(self, own, use, first=None):
+    def gather(self, own, use):
         mid = own.shape[0] // 2
-        mine, theirs = own, self.swap(own)
-        use(0, (mine, theirs))
-        for step in range(1, self.half):
+        use(0, (own,))
+        mine, theirs = self.send(own, True), self.send(own, True, True)
+        use(1, (mine, theirs))
+        for step in range(2, self.half):
             mine, theirs = self.send(mine, True), self.send(theirs, True)
-            if first is not None and step == min(2, self.half - 1):
-                theirs = first(theirs)
             use(step, (mine, theirs))
 
         def half_kernel(block_ref, out_ref):
@@ -103,24 +103,27 @@
         use(self.half, tuple(self.send(h, True) for h in halves))
 
     def scatter(self, parts):
-        mid = parts[self.half][0].shape[0]
-        shape = parts[1][0].shape
-
-        def half_kernel(block_ref, arrived_ref, out_ref):
+        rows, cols = parts[1][0].shape
+        mid = rows // 2
+
+        def half_kernel(place, block_ref, arrived_ref, out_ref):
             out_ref[...] = block_ref[...].astype(BF16)
-            rows = pl.ds(pl.multiple_of(self.core() * mid, mid), mid)
-            out_ref[rows, :] = (block_ref[rows, :] + arrived_ref[...].astype(F32)).astype(BF16)
-
-        def add_kernel(block_ref, arrived_ref, out_ref):
+            some = pl.ds(pl.multiple_of(self.core() * mid, mid), mid)
+            arrived = arrived_ref[pl.ds(place * mid, mid), :].astype(F32)
+            out_ref[some, :] = (block_ref[some, :] + arrived).astype(BF16)
+
+        def add_kernel(place, block_ref, arrived_ref, out_ref):
             out_ref[...] = (block_ref[...] + arrived_ref[...].astype(F32)).astype(BF16)
 
-        mine, theirs = parts[self.half]
-        theirs, mine = self.send(theirs, False), self.send(mine, False)
+        sums = [self.send(parts[self.half][0], False)] * 2
         for step in range(self.half - 1, 0, -1):
             kernel = half_kernel if step == self.half - 1 else add_kernel
-            theirs = self.send(call(kernel, [(shape, BF16)], parts[step][1], theirs)[0], False)
-            mine = self.send(call(kernel, [(shape, BF16)], parts[step][0], mine)[0], False)
-        return mine, self.swap(theirs)
+            for i in range(2):
+                added = call(
+                    functools.partial(kernel, i), [((rows, cols), BF16)], parts[step][i], sums[i]
+                )[0]
+                sums[i] = self.send(added, False, step == 1 and i == 1)
+        return sums
 
 
 def sum_kernel(own_ref, left_ref, right_ref, out_ref):
@@ -169,7 +172,7 @@
 
 def assemble_kernel(shards, local_experts, *refs):
     gates, ups, downs = refs[:shards], refs[shards : 2 * shards], refs[2 * shards : 3 * shards]
-    wide_ref, down_ref, _, sems = refs[3 * shards + 1 :]
+    wide_ref, down_ref, sems = refs[3 * shards :]
     hidden_dim = gates[0].shape[2]
     copies = []
 
@@ -204,7 +207,7 @@
     return shards
 
 
-def assemble(shards, local_experts, passed):
+def assemble(shards, local_experts):
     count = len(shards) // 3
     hidden_dim = shards[0].shape[2]
     feature_dim = shards[-1].shape[2]
@@ -218,18 +221,29 @@
         out_shape=[
             pltpu.VMEM((feature_dim, 2 * local_experts * hidden_dim), BF16),
             pltpu.VMEM((local_experts * hidden_dim, feature_dim), BF16),
-            pltpu.VMEM(passed.shape, passed.dtype),
         ],
         in_specs=[
             pl.BlockSpec(memory_space=pltpu.VMEM if count == 2 and i % 2 else pl.ANY)
             for i in range(len(shards))
-        ]
-        + [pl.BlockSpec(memory_space=pltpu.VMEM)],
-        out_specs=[pl.BlockSpec(memory_space=pltpu.VMEM)] * 3,
+        ],
+        out_specs=[pl.BlockSpec(memory_space=pltpu.VMEM)] * 2,
         scratch_shapes=[pltpu.SemaphoreType.DMA((3 * count * local_experts,))],
-        input_output_aliases={len(shards): 2},
         compiler_params=pltpu.CompilerParams(vmem_limit_bytes=VMEM_LIMIT),
-    )(*shards, pltpu.with_memory_space_constraint(passed, pltpu.VMEM))
+    )(*shards)
+
+
+def transpose_kernel(from_ref, to_ref):
+    strip = 2 * LANES
+
+    @pl.loop(0, to_ref.shape[0] // strip)
+    def _(i):
+        some = pl.ds(pl.multiple_of(i * strip, strip), strip)
+        to_ref[some, :] = from_ref[:, some].T
+
+
+def transposed(weights):
+    rows, cols = weights.shape
+    return call(transpose_kernel, [((cols, rows), BF16)], weights)[0]
 
 
 def body(tokens, w_gate, w_up, w_down, route_ids, route_scores, norm_gain, class_head, targets):
@@ -244,12 +258,7 @@
 
     packed = pack(route_ids.T, route_scores.T, tokens)
     shards = exchange_shards(w_gate, w_up, w_down, group_count)
-    weights_at = []
-
-    def assemble_now(passed):
-        wide, down, passed = assemble(shards, local_experts, passed)
-        weights_at.extend([wide, down])
-        return passed
+    wide, down = assemble(shards, local_experts)
 
     def rows_of(refs):
         return jnp.concatenate([ref[...] for ref in refs], axis=0) if len(refs) > 1 else refs[0][...]
@@ -279,36 +288,33 @@
         for i, out in enumerate(outs[2:]):
             out[...] = total[i * rows : (i + 1) * rows].astype(out.dtype)
 
-    tokens_at, part_at, saved_at = {}, {}, {}
+    tokens_at, part_at, saved_at, moe_at = {}, {}, {}, {}
     flops = 2 * feature_dim * hidden_dim * local_experts * 3
 
-    def mine_at(blocks_at, k):
-        return blocks_at[k][:1] if k == 0 else blocks_at[k]
-
     def part_outs(k):
-        rows, dtype = (mid, BF16) if k == ring.half else (rows_here, F32)
-        return [((rows, feature_dim), dtype)] * (1 if k == 0 else 2)
+        if k == ring.half:
+            return [(block, BF16)]
+        return [(block, F32)] * (1 if k == 0 else 2)
 
     def forward(k):
-        blocks = mine_at(tokens_at, k)
+        blocks = tokens_at[k]
         rows = sum(b.shape[0] for b in blocks)
         result = call(
             functools.partial(forward_kernel, len(blocks)),
             [((rows, local_experts * hidden_dim), BF16)] * 2 + part_outs(k),
             *blocks,
-            *weights_at,
+            wide,
+            down,
             flops=flops * rows,
         )
         saved_at[k] = result[:2]
         part_at[k] = result[2:]
 
-    ring.gather(packed, tokens_at.__setitem__, assemble_now)
-    wide, down = weights_at
+    ring.gather(packed, tokens_at.__setitem__)
     for k in tokens_at:
         forward(k)
     gain = norm_gain.reshape(1, feature_dim)
     moe_out = call(sum_kernel, [(block, BF16)], part_at[0][0], *ring.scatter(part_at))[0]
-    moe_at = {}
     ring.gather(moe_out, moe_at.__setitem__)
 
     def residual_of(token_refs, moe_refs):
@@ -318,82 +324,77 @@
     def inv_rms_of(residual):
         return lax.rsqrt(jnp.mean(residual * residual, axis=-1, keepdims=True) + NORM_EPS)
 
-    def norm_kernel(*refs):
-        residual = residual_of(refs[:2], refs[2:4])
-        gain_ref, out_ref = refs[4:]
+    def norm_kernel(tokens_ref, moe_ref, gain_ref, out_ref):
+        residual = residual_of([tokens_ref], [moe_ref])
         normed = residual * inv_rms_of(residual) * gain_ref[...]
         row = lax.broadcasted_iota(jnp.int32, out_ref.shape, 0)
-        pooled = jnp.zeros(out_ref.shape, F32)
-        for i in range(2):
-            part = normed[i * rows_here : (i + 1) * rows_here]
-            mean = jnp.mean(part, axis=0, keepdims=True)
-            pooled = jnp.where(row == ring.row_at(0, i), mean, pooled)
-        out_ref[...] = pooled.astype(BF16)
-
-    pooled_shape = (2 * expert_count, feature_dim)
-    pooled = call(norm_kernel, [(pooled_shape, BF16)], *tokens_at[0], *moe_at[0], gain)[0]
-    pooled = ring.total(pooled)
-    target_own = targets.reshape(expert_count, -1).astype(F32)
-
-    def target_kernel(own_ref, other_ref, out_ref):
-        for i, ref in enumerate((own_ref, other_ref)):
-            begin = (1 - ring.core() if i else ring.core()) * expert_count
-            out_ref[pl.ds(pl.multiple_of(begin, expert_count), expert_count), :] = ref[...]
-
-    target_shape = (2 * expert_count, target_own.shape[1])
-    target_rows = call(target_kernel, [(target_shape, F32)], target_own, ring.swap(target_own))[0]
+        mean = jnp.mean(normed, axis=0, keepdims=True)
+        out_ref[...] = jnp.where(row == ring.device_at(0), mean, 0.0).astype(BF16)
+
+    guards = [b for k in range(1, ring.half) for b in moe_at[k]]
+    pooled_shape = (expert_count, feature_dim)
+    pooled = call(norm_kernel, [(pooled_shape, BF16)], packed, moe_out, gain)[0]
+    pooled = ring.total(pooled, guards)
     logits = dot(pooled, class_head)
+    target_rows = targets.reshape(expert_count, -1).astype(F32)
     logit_grad = (LOSS_SCALE * (jax.nn.sigmoid(logits) - target_rows)).astype(BF16)
-    pooled_grad = ring.total(dot_t(logit_grad, class_head).astype(BF16)).astype(F32)
-
-    if group_count > 2:
-        both = jnp.concatenate([pooled, logit_grad], axis=1)
-        both = lax.all_gather(both, "group", axis=0)[::2].reshape(-1, both.shape[1])
-        pooled, logit_grad = both[:, :feature_dim], both[:, feature_dim:]
+    pooled_grad = ring.total(dot_t(logit_grad, class_head).astype(BF16), guards)
+    pooled_grads = [pooled_grad, ring.swap(pooled_grad)]
+
+    both = jnp.concatenate([pooled, logit_grad], axis=1)
+    if group_count == 2:
+        both = jnp.concatenate([both, ring.swap(both)], axis=0)
+    else:
+        both = lax.all_gather(both, "group", axis=0, tiled=True)
     head_grad = lax.dot_general(
-        pooled, logit_grad, (((0,), (0,)), ((), ())), preferred_element_type=F32
+        both[:, :feature_dim],
+        both[:, feature_dim:],
+        (((0,), (0,)), ((), ())),
+        preferred_element_type=F32,
     )
 
     def backward_kernel(k, count, *refs):
         residual = residual_of(refs[:count], refs[count : 2 * count])
-        gate_save, up_save, grad_ref, gain_ref, wide_ref, down_ref = refs[2 * count : 2 * count + 6]
-        outs = refs[2 * count + 6 :]
+        gate_save, up_save, *grad_refs = refs[2 * count : 2 * count + 4]
+        gain_ref, wide_ref, down_ref, *outs = refs[2 * count + 4 :]
         inv_rms = inv_rms_of(residual)
         cube = inv_rms * inv_rms * inv_rms
         parts = []
         for i in range(count):
             some = residual.shape[0] // count
             rows = slice(i * some, (i + 1) * some)
-            scaled = gain_ref[...] * grad_ref[pl.ds(ring.row_at(k, i), 1), :] / rows_here
+            scaled = gain_ref[...] * grad_refs[i][pl.ds(ring.device_at(k), 1), :] / rows_here
             slope = cube[rows] * jnp.mean(residual[rows] * scaled, axis=-1, keepdims=True)
             parts.append(inv_rms[rows] * scaled - residual[rows] * slope)
         resid_grad = jnp.concatenate(parts, axis=0) if count > 1 else parts[0]
-        down_back = dot_t(resid_grad.astype(BF16), down_ref[...])
+        down_back = dot(resid_grad.astype(BF16), down_ref[...])
         total = resid_grad if k == 0 else None
         for local in range(local_experts):
             cols = slice(local * hidden_dim, (local + 1) * hidden_dim)
             gate_grad = (down_back[:, cols] * gate_save[:, cols].astype(F32)).astype(BF16)
             up_grad = (down_back[:, cols] * up_save[:, cols].astype(F32)).astype(BF16)
             grads = jnp.concatenate([gate_grad, up_grad], axis=1)
-            term = dot_t(grads, wide_ref[:, pl.ds(local * pair_dim, pair_dim)])
+            term = dot(grads, wide_ref[pl.ds(local * pair_dim, pair_dim), :])
             total = term if total is None else total + term
         rows = total.shape[0] // len(outs)
         for i, out in enumerate(outs):
             out[...] = total[i * rows : (i + 1) * rows].astype(out.dtype)
 
+    wide_t, down_t = transposed(wide), transposed(down)
+    pooled_grads = [g.astype(F32) for g in pooled_grads]
     back_at = {}
     for k in reversed(list(tokens_at)):
-        blocks = mine_at(tokens_at, k)
+        blocks = tokens_at[k]
         back_at[k] = call(
             functools.partial(backward_kernel, k, len(blocks)),
             part_outs(k),
             *blocks,
-            *mine_at(moe_at, k),
+            *moe_at[k],
             *saved_at[k],
-            pooled_grad,
+            *pooled_grads,
             gain,
-            wide,
-            down,
+            wide_t,
+            down_t,
             flops=flops * sum(b.shape[0] for b in blocks),
         )
     token_grad = pl.pallas_call(

time: 145 us -> 142 us (0.979)
  starting transfers between devices: 69.2 us -> 46.7 us
  waiting for transfers between devices: 49 us -> 68 us
    ppermute x32 -> x30, starting transfers between devices: 58.4 us -> 40 us  [send(): return lax.ppermute(value, ('expert', 'group'), pairs)]
    ppermute x6, waiting for transfers between devices: 3.9 us -> 21.5 us  [total(): lax.ppermute(value, 'expert', [(e, e ^ distance) for e in range(self.coun...]
    ppermute x6, starting transfers between devices: 9.69 us -> 5.16 us  [total(): lax.ppermute(value, 'expert', [(e, e ^ distance) for e in range(self.coun...]
    ppermute x32 -> x30, waiting for transfers between devices: 42.4 us -> 46.5 us  [send(): return lax.ppermute(value, ('expert', 'group'), pairs)]
    ppermute x5 -> x2, waiting for transfers between devices: 2.7 us -> 0.01 us  [swap(): lax.ppermute(value, 'group', [(g, g ^ 1) for g in range(self.groups)])]
    pallas_call x29 -> x36, Pallas kernels: 20.6 us -> 20.4 us  [call(): pl.pallas_call(kernel, out_shape=[pltpu.VMEM(shape, dtype) for shape, dty...]
  transfers between devices with their start and end apart: 46 -> 41, of which waited for: 31 -> 27; matrix products, arithmetic and copies ran while one was open for 1% -> 1% of each run, Pallas kernels for 13% -> 14%
where the time goes in v5:
time: 142 us; the launch traced here: 141 us
  waiting for transfers between devices  68 us (48%)
  starting transfers between devices  46.7 us (33%)
  Pallas kernels  24 us (17%)
  matrix products  1.7 us (1%)
    ppermute x30, waiting for transfers between devices, send(): return lax.ppermute(value, ('expert', 'group'), pairs)  46.5 us
    ppermute x30, starting transfers between devices, send(): return lax.ppermute(value, ('expert', 'group'), pairs)  40 us
    ppermute x6, waiting for transfers between devices, total(): lax.ppermute(value, 'expert', [(e, e ^ distance) for e in range(self.coun...  21.5 us
    pallas_call x36, Pallas kernels, call(): pl.pallas_call(kernel, out_shape=[pltpu.VMEM(shape, dtype) for shape, dty...  20.4 us
    ppermute x6, starting transfers between devices, total(): lax.ppermute(value, 'expert', [(e, e ^ distance) for e in range(self.coun...  5.16 us
  transfers between devices with their start and end apart: 41, of which 27 were waited for; matrix products, arithmetic and copies ran while one was open for 1% of the time, Pallas kernels for 14%

profile of v5, /device:TPU:0, one launch (start us, length us, event | category | flops | bytes accessed | tf_op | source)
XLA Modules:
  0.0 141.4 jit_solution(14541941673081854555)
XLA Ops:
  1.7 3.1 %collective-permute-start.3 = (bf16[128,1152]{1,0:T(8,128)(2,1)S(1)}, bf16[128,1152]{1,0:T(8,128)(2,1)S(1)}, u32[]{:S(2)}, u32[]{:S(2)}) collective-permute-start(bf16[128,1152]{1,0:T(8,128)(2,1)S(1)} %shard_map.104.refs_0_.tokens_ref), channel_id=1, source_target_pairs={{0,4},{1,3},{4,8},{5,1},{8,12},{9,5},{12,14},{13,9},{14,10},{15,13... | collective-permute-start | bytes 884744 | tf_op jit(solution)/shard_map/ppermute | solution.py:57
  7.0 4.2 %collective-permute-done.3.refs_0_ = bf16[128,1152]{1,0:T(8,128)(2,1)S(1)} collective-permute-done((bf16[128,1152]{1,0:T(8,128)(2,1)S(1)}, bf16[128,1152]{1,0:T(8,128)(2,1)S(1)}, u32[]{:S(2)}, u32[]{:S(2)}) %collective-permute-start.3) | collective-permute-done | bytes 294944 | tf_op jit(solution)/shard_map/ppermute | solution.py:57
  11.2 2.5 %collective-permute-start.5 = (bf16[128,1152]{1,0:T(8,128)(2,1)S(1)}, bf16[128,1152]{1,0:T(8,128)(2,1)S(1)}, u32[]{:S(2)}, u32[]{:S(2)}) collective-permute-start(bf16[128,1152]{1,0:T(8,128)(2,1)S(1)} %collective-permute-done.3.refs_0_), channel_id=1, source_target_pairs={{0,4},{1,3},{4,8},{5,1},{8,12},{9,5},{12,14},{13,9},{14,10},{15,13... | collective-permute-start | bytes 884744 | tf_op jit(solution)/shard_map/ppermute | solution.py:57
  15.3 4.0 %collective-permute-done.5.refs_0_ = bf16[128,1152]{1,0:T(8,128)(2,1)S(1)} collective-permute-done((bf16[128,1152]{1,0:T(8,128)(2,1)S(1)}, bf16[128,1152]{1,0:T(8,128)(2,1)S(1)}, u32[]{:S(2)}, u32[]{:S(2)}) %collective-permute-start.5) | collective-permute-done | bytes 294944 | tf_op jit(solution)/shard_map/ppermute | solution.py:57
  23.6 2.5 %collective-permute-done.7.refs_0_.block_ref = bf16[128,1152]{1,0:T(8,128)(2,1)S(1)} collective-permute-done((bf16[128,1152]{1,0:T(8,128)(2,1)S(1)}, bf16[128,1152]{1,0:T(8,128)(2,1)S(1)}, u32[]{:S(2)}, u32[]{:S(2)}) %collective-permute-start.7) | collective-permute-done | bytes 294944 | tf_op jit(solution)/shard_map/ppermute | solution.py:57
  32.1 3.2 %collective-permute-done.10.refs_1_ = bf16[64,1152]{1,0:T(8,128)(2,1)S(1)} collective-permute-done((bf16[64,1152]{1,0:T(8,128)(2,1)S(1)}, bf16[64,1152]{1,0:T(8,128)(2,1)S(1)}, u32[]{:S(2)}, u32[]{:S(2)}) %collective-permute-start.10) | collective-permute-done | bytes 147488 | tf_op jit(solution)/shard_map/ppermute | solution.py:57
  36.4 2.5 %collective-permute-start.11 = (bf16[128,1024]{1,0:T(8,128)(2,1)S(1)}, bf16[128,1024]{1,0:T(8,128)(2,1)S(1)}, u32[]{:S(2)}, u32[]{:S(2)}) collective-permute-start(bf16[128,1024]{1,0:T(8,128)(2,1)S(1)} %get-tuple-element.34), channel_id=1, source_target_pairs={{0,2},{1,5},{4,0},{5,9},{8,4},{9,13},{12,8},{13,15},{14,12},{15,11... | collective-permute-start | bytes 786440 | tf_op jit(solution)/shard_map/ppermute | solution.py:57
  42.9 2.5 %collective-permute-start.12 = (bf16[128,1024]{1,0:T(8,128)(2,1)S(1)}, bf16[128,1024]{1,0:T(8,128)(2,1)S(1)}, u32[]{:S(2)}, u32[]{:S(2)}) collective-permute-start(bf16[128,1024]{1,0:T(8,128)(2,1)S(1)} %shard_map.113), channel_id=1, source_target_pairs={{0,2},{1,5},{4,0},{5,9},{8,4},{9,13},{12,8},{13,15},{14,12},{15,11... | collective-permute-start | bytes 786440 | tf_op jit(solution)/shard_map/ppermute | solution.py:57
  49.4 2.5 %collective-permute-start.13 = (bf16[128,1024]{1,0:T(8,128)(2,1)S(1)}, bf16[128,1024]{1,0:T(8,128)(2,1)S(1)}, u32[]{:S(2)}, u32[]{:S(2)}) collective-permute-start(bf16[128,1024]{1,0:T(8,128)(2,1)S(1)} %shard_map.114), channel_id=1, source_target_pairs={{0,2},{1,5},{4,0},{5,9},{8,4},{9,13},{12,8},{13,15},{14,12},{15,11... | collective-permute-start | bytes 786440 | tf_op jit(solution)/shard_map/ppermute | solution.py:57
  52.2 2.5 %collective-permute-start.16 = (bf16[128,1024]{1,0:T(8,128)(2,1)S(1)}, bf16[128,1024]{1,0:T(8,128)(2,1)S(1)}, u32[]{:S(2)}, u32[]{:S(2)}) collective-permute-start(bf16[128,1024]{1,0:T(8,128)(2,1)S(1)} %shard_map.117), channel_id=1, source_target_pairs={{0,2},{1,5},{4,0},{5,9},{8,4},{9,13},{12,8},{13,15},{14,12},{15,11... | collective-permute-start | bytes 786440 | tf_op jit(solution)/shard_map/ppermute | solution.py:57
  59.8 3.0 %collective-permute-done.14.left_ref = bf16[128,1024]{1,0:T(8,128)(2,1)S(1)} collective-permute-done((bf16[128,1024]{1,0:T(8,128)(2,1)S(1)}, bf16[128,1024]{1,0:T(8,128)(2,1)S(1)}, u32[]{:S(2)}, u32[]{:S(2)}) %collective-permute-start.14) | collective-permute-done | bytes 262176 | tf_op jit(solution)/shard_map/ppermute | solution.py:57
  65.4 2.9 %collective-permute-start.21 = (bf16[128,1024]{1,0:T(8,128)(2,1)S(1)}, bf16[128,1024]{1,0:T(8,128)(2,1)S(1)}, u32[]{:S(2)}, u32[]{:S(2)}) collective-permute-start(bf16[128,1024]{1,0:T(8,128)(2,1)S(1)} %shard_map.119.moe_ref.refs_1_), channel_id=1, source_target_pairs={{0,3},{1,4},{4,1},{5,8},{8,5},{9,12},{12,9},{13,14},{14,13},{15,10... | collective-permute-start | bytes 786440 | tf_op jit(solution)/shard_map/ppermute | solution.py:57
  68.3 5.3 %collective-permute-done.19.guard_ref.refs_2_ = bf16[128,1024]{1,0:T(8,128)(2,1)S(1)} collective-permute-done((bf16[128,1024]{1,0:T(8,128)(2,1)S(1)}, bf16[128,1024]{1,0:T(8,128)(2,1)S(1)}, u32[]{:S(2)}, u32[]{:S(2)}) %collective-permute-start.19) | collective-permute-done | bytes 262176 | tf_op jit(solution)/shard_map/ppermute | solution.py:57
  76.7 6.7 %collective-permute-done.18.other_ref = bf16[8,1024]{1,0:T(8,128)(2,1)S(1)} collective-permute-done((bf16[8,1024]{1,0:T(8,128)(2,1)S(1)}, bf16[8,1024]{1,0:T(8,128)(2,1)S(1)}, u32[]{:S(2)}, u32[]{:S(2)}) %collective-permute-start.18) | collective-permute-done | bytes 16416 | tf_op jit(solution)/shard_map/ppermute | solution.py:68
  88.5 3.8 %collective-permute-done.22.other_ref = bf16[8,1024]{1,0:T(8,128)(2,1)S(1)} collective-permute-done((bf16[8,1024]{1,0:T(8,128)(2,1)S(1)}, bf16[8,1024]{1,0:T(8,128)(2,1)S(1)}, u32[]{:S(2)}, u32[]{:S(2)}) %collective-permute-start.22) | collective-permute-done | bytes 16416 | tf_op jit(solution)/shard_map/ppermute | solution.py:68
  93.7 2.9 %collective-permute-start.32 = (bf16[64,1024]{1,0:T(8,128)(2,1)S(1)}, bf16[64,1024]{1,0:T(8,128)(2,1)S(1)}, u32[]{:S(2)}, u32[]{:S(2)}) collective-permute-start(bf16[64,1024]{1,0:T(8,128)(2,1)S(1)} %shard_map.134), channel_id=1, source_target_pairs={{0,4},{1,3},{4,8},{5,1},{8,12},{9,5},{12,14},{13,9},{14,10},{15,13... | collective-permute-start | bytes 393224 | tf_op jit(solution)/shard_map/ppermute | solution.py:57
  96.8 3.8 %collective-permute-done.24.other_ref = bf16[8,1024]{1,0:T(8,128)(2,1)S(1)} collective-permute-done((bf16[8,1024]{1,0:T(8,128)(2,1)S(1)}, bf16[8,1024]{1,0:T(8,128)(2,1)S(1)}, u32[]{:S(2)}, u32[]{:S(2)}) %collective-permute-start.24) | collective-permute-done | bytes 16416 | tf_op jit(solution)/shard_map/ppermute | solution.py:68
  101.7 2.6 %collective-permute-done.26.other_ref = bf16[8,1024]{1,0:T(8,128)(2,1)S(1)} collective-permute-done((bf16[8,1024]{1,0:T(8,128)(2,1)S(1)}, bf16[8,1024]{1,0:T(8,128)(2,1)S(1)}, u32[]{:S(2)}, u32[]{:S(2)}) %collective-permute-start.26) | collective-permute-done | bytes 16416 | tf_op jit(solution)/shard_map/ppermute | solution.py:68
  105.3 3.6 %collective-permute-done.28.other_ref = bf16[8,1024]{1,0:T(8,128)(2,1)S(1)} collective-permute-done((bf16[8,1024]{1,0:T(8,128)(2,1)S(1)}, bf16[8,1024]{1,0:T(8,128)(2,1)S(1)}, u32[]{:S(2)}, u32[]{:S(2)}) %collective-permute-start.28) | collective-permute-done | bytes 16416 | tf_op jit(solution)/shard_map/ppermute | solution.py:68
  112.6 2.5 %shard_map.132 = (f32[128,1024]{1,0:T(8,128)S(1)}, f32[128,1024]{1,0:T(8,128)S(1)}) custom-call(bf16[128,1152]{1,0:T(8,128)(2,1)S(1)} %collective-permute-done.7.refs_0_.block_ref, bf16[128,1152]{1,0:T(8,128)(2,1)S(1)} %collective-permute-done.8.refs_1_.block_ref, bf16[128,1024]{1,0:T(8,128)(2,1)S(1)} %collective-permute-done.27.guard_ref.refs_2_.block_ref, ...), custom_call_target="tpu_custom_call" | custom-call | flops 1207959552 | bytes 6688768 | tf_op jit(solution)/shard_map/pallas_call | solution.py:29
  115.2 3.8 %collective-permute-done.33.arrived_ref = bf16[128,1024]{1,0:T(8,128)(2,1)S(1)} collective-permute-done((bf16[128,1024]{1,0:T(8,128)(2,1)S(1)}, bf16[128,1024]{1,0:T(8,128)(2,1)S(1)}, u32[]{:S(2)}, u32[]{:S(2)}) %collective-permute-start.33) | collective-permute-done | bytes 262176 | tf_op jit(solution)/shard_map/ppermute | solution.py:57
  121.2 2.5 %shard_map.131 = (f32[128,1024]{1,0:T(8,128)S(1)}, f32[128,1024]{1,0:T(8,128)S(1)}) custom-call(bf16[128,1152]{1,0:T(8,128)(2,1)S(1)} %collective-permute-done.5.refs_0_, bf16[128,1152]{1,0:T(8,128)(2,1)S(1)} %collective-permute-done.6.refs_1_, bf16[128,1024]{1,0:T(8,128)(2,1)S(1)} %collective-permute-done.23.guard_ref.refs_2_, ...), custom_call_target="tpu_custom_call" | custom-call | flops 1207959552 | bytes 6688768 | tf_op jit(solution)/shard_map/pallas_call | solution.py:29
  125.6 2.6 %collective-permute-done.37.arrived_ref = bf16[128,1024]{1,0:T(8,128)(2,1)S(1)} collective-permute-done((bf16[128,1024]{1,0:T(8,128)(2,1)S(1)}, bf16[128,1024]{1,0:T(8,128)(2,1)S(1)}, u32[]{:S(2)}, u32[]{:S(2)}) %collective-permute-start.37) | collective-permute-done | bytes 262176 | tf_op jit(solution)/shard_map/ppermute | solution.py:57
  128.4 2.6 %shard_map.130 = (f32[128,1024]{1,0:T(8,128)S(1)}, f32[128,1024]{1,0:T(8,128)S(1)}) custom-call(bf16[128,1152]{1,0:T(8,128)(2,1)S(1)} %collective-permute-done.3.refs_0_, bf16[128,1152]{1,0:T(8,128)(2,1)S(1)} %collective-permute-done.4.refs_1_, bf16[128,1024]{1,0:T(8,128)(2,1)S(1)} %collective-permute-done.19.guard_ref.refs_2_, ...), custom_call_target="tpu_custom_call" | custom-call | flops 1207959552 | bytes 6688768 | tf_op jit(solution)/shard_map/pallas_call | solution.py:29
  (110 shorter events, 62.1 us)
Async XLA Ops:
  1.7 9.5 %collective-permute-start.3 = (bf16[128,1152]{1,0:T(8,128)(2,1)S(1)}, bf16[128,1152]{1,0:T(8,128)(2,1)S(1)}, u32[]{:S(2)}, u32[]{:S(2)}) collective-permute-start(bf16[128,1152]{1,0:T(8,128)(2,1)S(1)} %shard_map.104.refs_0_.tokens_ref), channel_id=1, source_target_pairs={{0,4},{1,3},{4,8},{5,1},{8,12},{9,5},{12,14},{13,9},{14,10},{15,13... | collective-permute-start | bytes 884744 | tf_op jit(solution)/shard_map/ppermute | solution.py:57
  4.8 8.9 %collective-permute-start.4 = (bf16[128,1152]{1,0:T(8,128)(2,1)S(1)}, bf16[128,1152]{1,0:T(8,128)(2,1)S(1)}, u32[]{:S(2)}, u32[]{:S(2)}) collective-permute-start(bf16[128,1152]{1,0:T(8,128)(2,1)S(1)} %shard_map.104.refs_0_.tokens_ref), channel_id=1, source_target_pairs={{0,3},{1,4},{4,1},{5,8},{8,5},{9,12},{12,9},{13,14},{14,13},{15,10... | collective-permute-start | bytes 884744 | tf_op jit(solution)/shard_map/ppermute | solution.py:57
  5.4 24.9 %collective-permute-start = (bf16[2,512,384]{2,1,0:T(8,128)(2,1)}, bf16[2,512,384]{2,1,0:T(8,128)(2,1)S(1)}, u32[]{:S(2)}, u32[]{:S(2)}) collective-permute-start(bf16[2,512,384]{2,1,0:T(8,128)(2,1)} %refs_0_.1), channel_id=1, source_target_pairs={{0,1},{1,0},{2,3},{3,2},{4,5},{5,4},{6,7},{7,6},{8,9},{9,8},{10,11... | collective-permute-start | bytes 2359304 | tf_op jit(solution)/shard_map/ppermute | solution.py:204
  6.5 23.9 %collective-permute-start.1 = (bf16[2,512,384]{2,1,0:T(8,128)(2,1)}, bf16[2,512,384]{2,1,0:T(8,128)(2,1)S(1)}, u32[]{:S(2)}, u32[]{:S(2)}) collective-permute-start(bf16[2,512,384]{2,1,0:T(8,128)(2,1)} %refs_2_.1), channel_id=1, source_target_pairs={{0,1},{1,0},{2,3},{3,2},{4,5},{5,4},{6,7},{7,6},{8,9},{9,8},{10,11... | collective-permute-start | bytes 2359304 | tf_op jit(solution)/shard_map/ppermute | solution.py:204
  6.5 23.9 %collective-permute-start.2 = (bf16[2,192,1024]{2,1,0:T(8,128)(2,1)}, bf16[2,192,1024]{2,1,0:T(8,128)(2,1)S(1)}, u32[]{:S(2)}, u32[]{:S(2)}) collective-permute-start(bf16[2,192,1024]{2,1,0:T(8,128)(2,1)} %refs_4_.1), channel_id=1, source_target_pairs={{0,1},{1,0},{2,3},{3,2},{4,5},{5,4},{6,7},{7,6},{8,9},{9,8},{10,11... | collective-permute-start | bytes 2359304 | tf_op jit(solution)/shard_map/ppermute | solution.py:204
  11.2 8.1 %collective-permute-start.5 = (bf16[128,1152]{1,0:T(8,128)(2,1)S(1)}, bf16[128,1152]{1,0:T(8,128)(2,1)S(1)}, u32[]{:S(2)}, u32[]{:S(2)}) collective-permute-start(bf16[128,1152]{1,0:T(8,128)(2,1)S(1)} %collective-permute-done.3.refs_0_), channel_id=1, source_target_pairs={{0,4},{1,3},{4,8},{5,1},{8,12},{9,5},{12,14},{13,9},{14,10},{15,13... | collective-permute-start | bytes 884744 | tf_op jit(solution)/shard_map/ppermute | solution.py:57
  13.7 8.8 %collective-permute-start.6 = (bf16[128,1152]{1,0:T(8,128)(2,1)S(1)}, bf16[128,1152]{1,0:T(8,128)(2,1)S(1)}, u32[]{:S(2)}, u32[]{:S(2)}) collective-permute-start(bf16[128,1152]{1,0:T(8,128)(2,1)S(1)} %collective-permute-done.4.refs_1_), channel_id=1, source_target_pairs={{0,4},{1,3},{4,8},{5,1},{8,12},{9,5},{12,14},{13,9},{14,10},{15,13... | collective-permute-start | bytes 884744 | tf_op jit(solution)/shard_map/ppermute | solution.py:57
  19.3 6.7 %collective-permute-start.7 = (bf16[128,1152]{1,0:T(8,128)(2,1)S(1)}, bf16[128,1152]{1,0:T(8,128)(2,1)S(1)}, u32[]{:S(2)}, u32[]{:S(2)}) collective-permute-start(bf16[128,1152]{1,0:T(8,128)(2,1)S(1)} %collective-permute-done.5.refs_0_), channel_id=1, source_target_pairs={{0,4},{1,3},{4,8},{5,1},{8,12},{9,5},{12,14},{13,9},{14,10},{15,13... | collective-permute-start | bytes 884744 | tf_op jit(solution)/shard_map/ppermute | solution.py:57
  22.4 6.7 %collective-permute-start.8 = (bf16[128,1152]{1,0:T(8,128)(2,1)S(1)}, bf16[128,1152]{1,0:T(8,128)(2,1)S(1)}, u32[]{:S(2)}, u32[]{:S(2)}) collective-permute-start(bf16[128,1152]{1,0:T(8,128)(2,1)S(1)} %collective-permute-done.6.refs_1_), channel_id=1, source_target_pairs={{0,4},{1,3},{4,8},{5,1},{8,12},{9,5},{12,14},{13,9},{14,10},{15,13... | collective-permute-start | bytes 884744 | tf_op jit(solution)/shard_map/ppermute | solution.py:57
  45.4 6.7 %collective-permute-start.15 = (bf16[128,1024]{1,0:T(8,128)(2,1)S(1)}, bf16[128,1024]{1,0:T(8,128)(2,1)S(1)}, u32[]{:S(2)}, u32[]{:S(2)}) collective-permute-start(bf16[128,1024]{1,0:T(8,128)(2,1)S(1)} %shard_map.116), channel_id=1, source_target_pairs={{0,2},{1,5},{4,0},{5,9},{8,4},{9,13},{12,8},{13,15},{14,12},{15,11... | collective-permute-start | bytes 786440 | tf_op jit(solution)/shard_map/ppermute | solution.py:57
  49.4 7.0 %collective-permute-start.13 = (bf16[128,1024]{1,0:T(8,128)(2,1)S(1)}, bf16[128,1024]{1,0:T(8,128)(2,1)S(1)}, u32[]{:S(2)}, u32[]{:S(2)}) collective-permute-start(bf16[128,1024]{1,0:T(8,128)(2,1)S(1)} %shard_map.114), channel_id=1, source_target_pairs={{0,2},{1,5},{4,0},{5,9},{8,4},{9,13},{12,8},{13,15},{14,12},{15,11... | collective-permute-start | bytes 786440 | tf_op jit(solution)/shard_map/ppermute | solution.py:57
  65.2 8.5 %collective-permute-start.19 = (bf16[128,1024]{1,0:T(8,128)(2,1)S(1)}, bf16[128,1024]{1,0:T(8,128)(2,1)S(1)}, u32[]{:S(2)}, u32[]{:S(2)}) collective-permute-start(bf16[128,1024]{1,0:T(8,128)(2,1)S(1)} %shard_map.119.moe_ref.refs_1_), channel_id=1, source_target_pairs={{0,4},{1,3},{4,8},{5,1},{8,12},{9,5},{12,14},{13,9},{14,10},{15,13... | collective-permute-start | bytes 786440 | tf_op jit(solution)/shard_map/ppermute | solution.py:57
  65.4 9.0 %collective-permute-start.21 = (bf16[128,1024]{1,0:T(8,128)(2,1)S(1)}, bf16[128,1024]{1,0:T(8,128)(2,1)S(1)}, u32[]{:S(2)}, u32[]{:S(2)}) collective-permute-start(bf16[128,1024]{1,0:T(8,128)(2,1)S(1)} %shard_map.119.moe_ref.refs_1_), channel_id=1, source_target_pairs={{0,3},{1,4},{4,1},{5,8},{8,5},{9,12},{12,9},{13,14},{14,13},{15,10... | collective-permute-start | bytes 786440 | tf_op jit(solution)/shard_map/ppermute | solution.py:57
  73.6 9.7 %collective-permute-start.23 = (bf16[128,1024]{1,0:T(8,128)(2,1)S(1)}, bf16[128,1024]{1,0:T(8,128)(2,1)S(1)}, u32[]{:S(2)}, u32[]{:S(2)}) collective-permute-start(bf16[128,1024]{1,0:T(8,128)(2,1)S(1)} %collective-permute-done.19.guard_ref.refs_2_), channel_id=1, source_target_pairs={{0,4},{1,3},{4,8},{5,1},{8,12},{9,5},{12,14},{13,9},{14,10},{15,13... | collective-permute-start | bytes 786440 | tf_op jit(solution)/shard_map/ppermute | solution.py:57
  74.4 11.0 %collective-permute-start.25 = (bf16[128,1024]{1,0:T(8,128)(2,1)S(1)}, bf16[128,1024]{1,0:T(8,128)(2,1)S(1)}, u32[]{:S(2)}, u32[]{:S(2)}) collective-permute-start(bf16[128,1024]{1,0:T(8,128)(2,1)S(1)} %collective-permute-done.21.guard_ref.refs_3_), channel_id=1, source_target_pairs={{0,4},{1,3},{4,8},{5,1},{8,12},{9,5},{12,14},{13,9},{14,10},{15,13... | collective-permute-start | bytes 786440 | tf_op jit(solution)/shard_map/ppermute | solution.py:57
  74.7 8.6 %collective-permute-start.18 = (bf16[8,1024]{1,0:T(8,128)(2,1)S(1)}, bf16[8,1024]{1,0:T(8,128)(2,1)S(1)}, u32[]{:S(2)}, u32[]{:S(2)}) collective-permute-start(bf16[8,1024]{1,0:T(8,128)(2,1)S(1)} %shard_map.120.mine_ref), channel_id=1, source_target_pairs={{0,2},{2,0},{4,6},{6,4},{8,10},{10,8},{12,14},{14,12},{1,3},{3,1},... | collective-permute-start | bytes 49160 | tf_op jit(solution)/shard_map/ppermute | solution.py:68
  83.4 9.1 %collective-permute-start.27 = (bf16[128,1024]{1,0:T(8,128)(2,1)S(1)}, bf16[128,1024]{1,0:T(8,128)(2,1)S(1)}, u32[]{:S(2)}, u32[]{:S(2)}) collective-permute-start(bf16[128,1024]{1,0:T(8,128)(2,1)S(1)} %collective-permute-done.23.guard_ref.refs_2_), channel_id=1, source_target_pairs={{0,4},{1,3},{4,8},{5,1},{8,12},{9,5},{12,14},{13,9},{14,10},{15,13... | collective-permute-start | bytes 786440 | tf_op jit(solution)/shard_map/ppermute | solution.py:57
  85.4 8.3 %collective-permute-start.29 = (bf16[128,1024]{1,0:T(8,128)(2,1)S(1)}, bf16[128,1024]{1,0:T(8,128)(2,1)S(1)}, u32[]{:S(2)}, u32[]{:S(2)}) collective-permute-start(bf16[128,1024]{1,0:T(8,128)(2,1)S(1)} %collective-permute-done.25.guard_ref.refs_3_), channel_id=1, source_target_pairs={{0,4},{1,3},{4,8},{5,1},{8,12},{9,5},{12,14},{13,9},{14,10},{15,13... | collective-permute-start | bytes 786440 | tf_op jit(solution)/shard_map/ppermute | solution.py:57
  92.5 18.3 %collective-permute-start.31 = (bf16[64,1024]{1,0:T(8,128)(2,1)S(1)}, bf16[64,1024]{1,0:T(8,128)(2,1)S(1)}, u32[]{:S(2)}, u32[]{:S(2)}) collective-permute-start(bf16[64,1024]{1,0:T(8,128)(2,1)S(1)} %shard_map.133), channel_id=1, source_target_pairs={{0,4},{1,3},{4,8},{5,1},{8,12},{9,5},{12,14},{13,9},{14,10},{15,13... | collective-permute-start | bytes 393224 | tf_op jit(solution)/shard_map/ppermute | solution.py:57
  93.7 17.2 %collective-permute-start.32 = (bf16[64,1024]{1,0:T(8,128)(2,1)S(1)}, bf16[64,1024]{1,0:T(8,128)(2,1)S(1)}, u32[]{:S(2)}, u32[]{:S(2)}) collective-permute-start(bf16[64,1024]{1,0:T(8,128)(2,1)S(1)} %shard_map.134), channel_id=1, source_target_pairs={{0,4},{1,3},{4,8},{5,1},{8,12},{9,5},{12,14},{13,9},{14,10},{15,13... | collective-permute-start | bytes 393224 | tf_op jit(solution)/shard_map/ppermute | solution.py:57
  112.3 6.6 %collective-permute-start.33 = (bf16[128,1024]{1,0:T(8,128)(2,1)S(1)}, bf16[128,1024]{1,0:T(8,128)(2,1)S(1)}, u32[]{:S(2)}, u32[]{:S(2)}) collective-permute-start(bf16[128,1024]{1,0:T(8,128)(2,1)S(1)} %shard_map.135), channel_id=1, source_target_pairs={{0,2},{1,5},{4,0},{5,9},{8,4},{9,13},{12,8},{13,15},{14,12},{15,11... | collective-permute-start | bytes 786440 | tf_op jit(solution)/shard_map/ppermute | solution.py:57
  119.1 9.1 %collective-permute-start.37 = (bf16[128,1024]{1,0:T(8,128)(2,1)S(1)}, bf16[128,1024]{1,0:T(8,128)(2,1)S(1)}, u32[]{:S(2)}, u32[]{:S(2)}) collective-permute-start(bf16[128,1024]{1,0:T(8,128)(2,1)S(1)} %shard_map.139), channel_id=1, source_target_pairs={{0,2},{1,5},{4,0},{5,9},{8,4},{9,13},{12,8},{13,15},{14,12},{15,11... | collective-permute-start | bytes 786440 | tf_op jit(solution)/shard_map/ppermute | solution.py:57
  121.2 7.2 %collective-permute-start.40 = (bf16[8,1274]{1,0:T(8,128)(2,1)S(1)}, bf16[8,1274]{1,0:T(8,128)(2,1)S(1)}, u32[]{:S(2)}, u32[]{:S(2)}) collective-permute-start(bf16[8,1274]{1,0:T(8,128)(2,1)S(1)} %pad_maximum_fusion.1), channel_id=1, source_target_pairs={{0,1},{1,0},{2,3},{3,2},{4,5},{5,4},{6,7},{7,6},{8,9},{9,8},{10,11... | collective-permute-start | bytes 61160 | tf_op jit(solution)/shard_map/ppermute | solution.py:60
  128.3 6.4 %collective-permute-start.38 = (bf16[128,1024]{1,0:T(8,128)(2,1)S(1)}, bf16[128,1024]{1,0:T(8,128)(2,1)S(1)}, u32[]{:S(2)}, u32[]{:S(2)}) collective-permute-start(bf16[128,1024]{1,0:T(8,128)(2,1)S(1)} %shard_map.140), channel_id=1, source_target_pairs={{0,2},{1,5},{4,0},{5,9},{8,4},{9,13},{12,8},{13,15},{14,12},{15,11... | collective-permute-start | bytes 786440 | tf_op jit(solution)/shard_map/ppermute | solution.py:57
  (20 other events, 233.5 us)

commit v6 on v3

--- a/solution.py
+++ b/solution.py
@@ -62,7 +62,7 @@
             there = jnp.where(there < self.half, 2 * there, 2 * (count - 1 - there) + 1)
         return there
 
-    def gather(self, top, bottom, use, first=None):
+    def gather(self, top, bottom, use):
         top_left = top_right = top
         bottom_left = bottom_right = bottom
         use((0,), (top, bottom))
@@ -71,8 +71,6 @@
             top_right = self.send(top_right, -1)
             bottom_left = self.send(bottom_left, 1)
             bottom_right = self.send(bottom_right, -1)
-            if first is not None and step == min(2, self.half - 1):
-                bottom_left = first(bottom_left)
             use((-step, step), (top_left, bottom_left, top_right, bottom_right))
         use((self.half,), (self.send(top_left, 1), self.send(bottom_right, -1)))
 
@@ -116,93 +114,190 @@
         out_ref[pl.ds(i * rows, rows), :] = (own[...] + arrived).astype(BF16)
 
 
-def pack_kernel(ids_ref, scores_ref, tokens_ref, top_ref, bottom_ref, sems):
-    rows, cols = tokens_ref.shape
+def pack_kernel(ids_hbm, scores_hbm, tokens_hbm, top_ref, bottom_ref, ids_ref, scores_ref, sems):
+    rows, cols = tokens_hbm.shape
     mid = rows // 2
-    copies = []
-    for i, ref in enumerate((top_ref, bottom_ref)):
-        source = tokens_ref.at[pl.ds(i * mid, mid), :]
-        copies.append(pltpu.make_async_copy(source, ref.at[:, pl.ds(0, cols)], sems.at[i]))
-        copies[-1].start()
+    quarter = LANES // 4
+    copies = [
+        pltpu.make_async_copy(ids_hbm, ids_ref, sems.at[0]),
+        pltpu.make_async_copy(scores_hbm, scores_ref, sems.at[1]),
+        pltpu.make_async_copy(
+            tokens_hbm.at[pl.ds(0, mid), :], top_ref.at[:, pl.ds(0, cols)], sems.at[2]
+        ),
+        pltpu.make_async_copy(tokens_hbm.at[pl.ds(mid, mid), :], bottom_ref, sems.at[3]),
+    ]
+    for copy in copies:
+        copy.start()
+    copies[0].wait()
+    copies[1].wait()
     scores = scores_ref[...]
     ids = ids_ref[...]
     route_weight = scores / jnp.sum(scores, axis=0, keepdims=True)
-    expert = lax.broadcasted_iota(jnp.int32, (LANES // 2, rows), 0)
-    weight_by = jnp.zeros((LANES // 2, rows), F32)
+    expert = lax.broadcasted_iota(jnp.int32, (quarter, rows), 0)
+    weight_by = jnp.zeros((quarter, rows), F32)
     for choice_k in range(scores.shape[0]):
         one = slice(choice_k, choice_k + 1)
         weight_by = weight_by + jnp.where(ids[one] == expert, route_weight[one], 0.0)
     high = weight_by.astype(BF16).astype(F32)
-    weights = jnp.concatenate([high, weight_by - high], axis=0).T.astype(BF16)
-    top_ref[:, cols:] = weights[:mid]
-    bottom_ref[:, cols:] = weights[mid:]
-    for copy in copies:
-        copy.wait()
-
-
-def assemble_kernel(shards, local_experts, *refs):
-    gates, ups, downs = refs[:shards], refs[shards : 2 * shards], refs[2 * shards : 3 * shards]
-    wide_ref, down_ref, _, sems = refs[3 * shards + 1 :]
-    hidden_dim = gates[0].shape[2]
-    copies = []
-
-    def start(source, target):
-        copies.append(pltpu.make_async_copy(source, target, sems.at[len(copies)]))
-        copies[-1].start()
-
-    for i in range(shards):
-        place = 0
-        if shards == 2:
-            group = lax.axis_index("group")
-            place = group if i == 0 else 1 - group
-        depth, height = gates[i].shape[1], downs[i].shape[1]
-        rows = pl.ds(pl.multiple_of(place * depth, 16), depth)
+    weights = jnp.concatenate([high, weight_by - high] * 2, axis=0).T
+    lane = lax.broadcasted_iota(jnp.int32, (mid, LANES), 1)
+    both = jnp.where(lane < 2 * quarter, weights[:mid], weights[mid:])
+    top_ref[:, cols:] = both.astype(BF16)
+    copies[2].wait()
+    copies[3].wait()
+
+
+def pack(ids, scores, tokens):
+    rows, cols = tokens.shape
+    args = [pltpu.with_memory_space_constraint(a, pltpu.HBM) for a in (ids, scores, tokens)]
+    return pl.pallas_call(
+        pack_kernel,
+        out_shape=[
+            pltpu.VMEM((rows // 2, cols + LANES), BF16),
+            pltpu.VMEM((rows // 2, cols), BF16),
+        ],
+        in_specs=[pl.BlockSpec(memory_space=pl.ANY)] * 3,
+        out_specs=[pl.BlockSpec(memory_space=pltpu.VMEM)] * 2,
+        scratch_shapes=[
+            pltpu.VMEM(ids.shape, ids.dtype),
+            pltpu.VMEM(scores.shape, F32),
+            pltpu.SemaphoreType.DMA((4,)),
+        ],
+        compiler_params=pltpu.CompilerParams(vmem_limit_bytes=VMEM_LIMIT),
+    )(*args)
+
+
+class Copies:
+    def __init__(self, sems):
+        self.sems, self.started = sems, []
+
+    def start(self, source, target):
+        copy = pltpu.make_async_copy(source, target, self.sems.at[len(self.started)])
+        copy.start()
+        self.started.append(copy)
+
+    def wait(self):
+        for copy in self.started:
+            copy.wait()
+
+
+def strips(gate_shape, down_shape):
+    local_experts, depth, hidden_dim = gate_shape
+    _, height, feature_dim = down_shape
+    row, places = 0, []
+    for _ in range(local_experts):
+        pair = [(row, depth), (row + depth, depth)]
+        row += 2 * depth
+        downs = []
+        for begin in range(0, feature_dim, hidden_dim):
+            downs.append((row, height, begin, min(hidden_dim, feature_dim - begin)))
+            row += height
+        places.append((pair, downs))
+    return row, places
+
+
+def pack_weights(w_gate, w_up, w_down):
+    rows, places = strips(w_gate.shape, w_down.shape)
+    hidden_dim = w_gate.shape[2]
+
+    def kernel(gate_hbm, up_hbm, down_hbm, out_ref, sems):
+        copies = Copies(sems)
+        for local, (pair, downs) in enumerate(places):
+            for source, (row, some) in zip((gate_hbm, up_hbm), pair):
+                copies.start(source.at[local], out_ref.at[pl.ds(row, some), :])
+            for row, some, begin, cols in downs:
+                source = down_hbm.at[local, :, pl.ds(begin, cols)]
+                copies.start(source, out_ref.at[pl.ds(row, some), pl.ds(0, cols)])
+                if cols < hidden_dim:
+                    out_ref[pl.ds(row, some), pl.ds(cols, hidden_dim - cols)] = jnp.zeros(
+                        (some, hidden_dim - cols), BF16
+                    )
+        copies.wait()
+
+    shards = [pltpu.with_memory_space_constraint(w, pltpu.HBM) for w in (w_gate, w_up, w_down)]
+    count = sum(len(pair) + len(downs) for pair, downs in places)
+    return pl.pallas_call(
+        kernel,
+        out_shape=pltpu.VMEM((rows, hidden_dim), BF16),
+        in_specs=[pl.BlockSpec(memory_space=pl.ANY)] * 3,
+        out_specs=pl.BlockSpec(memory_space=pltpu.VMEM),
+        scratch_shapes=[pltpu.SemaphoreType.DMA((count,))],
+        compiler_params=pltpu.CompilerParams(vmem_limit_bytes=VMEM_LIMIT),
+    )(*shards)
+
+
+def full_weights(w_gate, w_up, w_down, group_count):
+    local_experts, _, hidden_dim = w_gate.shape
+    feature_dim = w_down.shape[2]
+    paired = group_count == 2
+    if paired:
+        other = lax.ppermute(pack_weights(w_gate, w_up, w_down), "group", [(0, 1), (1, 0)])
+        other = pltpu.with_memory_space_constraint(other, pltpu.VMEM)
+        shards = [w_gate, w_up, w_down]
+    else:
+        shards = [lax.all_gather(w, "group", axis=1, tiled=True) for w in (w_gate, w_up, w_down)]
+    _, places = strips(shards[0].shape, shards[2].shape)
+    depth, height = shards[0].shape[1], shards[2].shape[1]
+
+    def kernel(*refs):
+        gate_hbm, up_hbm, down_hbm, *rest = refs
+        wide_ref, down_ref, sems = rest[-3:]
+        copies = Copies(sems)
+        mine = lax.axis_index("group") if paired else 0
+
+        def wide_at(place, local, is_up):
+            rows = pl.ds(pl.multiple_of(place * depth, 16), depth)
+            return wide_ref.at[rows, pl.ds((2 * local + is_up) * hidden_dim, hidden_dim)]
+
+        def down_at(place, local, begin, cols):
+            top = pl.multiple_of(local * hidden_dim + place * height, 16)
+            return down_ref.at[pl.ds(top, height), pl.ds(begin, cols)]
+
         for local in range(local_experts):
-            begin = local * 2 * hidden_dim
-            start(gates[i].at[local], wide_ref.at[rows, pl.ds(begin, hidden_dim)])
-            start(ups[i].at[local], wide_ref.at[rows, pl.ds(begin + hidden_dim, hidden_dim)])
-            top = pl.multiple_of(local * hidden_dim + place * height, 16)
-            start(downs[i].at[local], down_ref.at[pl.ds(top, height), :])
-    for copy in copies:
-        copy.wait()
-
-
-def exchange_shards(w_gate, w_up, w_down, group_count):
-    shards = []
-    for shard in (w_gate, w_up, w_down):
-        if group_count == 2:
-            shards += [shard, lax.ppermute(shard, "group", [(0, 1), (1, 0)])]
-        else:
-            shards += [lax.all_gather(shard, "group", axis=1, tiled=True)]
-    return shards
-
-
-def assemble(shards, local_experts, passed):
-    count = len(shards) // 3
-    hidden_dim = shards[0].shape[2]
-    feature_dim = shards[-1].shape[2]
-    if count == 2:
-        shards = [
-            pltpu.with_memory_space_constraint(w, pltpu.VMEM) if i % 2 else w
-            for i, w in enumerate(shards)
-        ]
+            for is_up, source in enumerate((gate_hbm, up_hbm)):
+                copies.start(source.at[local], wide_at(mine, local, is_up))
+            copies.start(down_hbm.at[local], down_at(mine, local, 0, feature_dim))
+        if paired:
+            for local, (pair, downs) in enumerate(places):
+                for is_up, (row, some) in enumerate(pair):
+                    copies.start(rest[0].at[pl.ds(row, some), :], wide_at(1 - mine, local, is_up))
+                for row, some, begin, cols in downs:
+                    source = rest[0].at[pl.ds(row, some), pl.ds(0, cols)]
+                    copies.start(source, down_at(1 - mine, local, begin, cols))
+        copies.wait()
+
+    shards = [pltpu.with_memory_space_constraint(w, pltpu.HBM) for w in shards]
+    count = 3 * local_experts
+    specs = [pl.BlockSpec(memory_space=pl.ANY)] * 3
+    if paired:
+        count += sum(len(pair) + len(downs) for pair, downs in places)
+        specs.append(pl.BlockSpec(memory_space=pltpu.VMEM))
+        shards.append(other)
     return pl.pallas_call(
-        functools.partial(assemble_kernel, count, local_experts),
+        kernel,
         out_shape=[
             pltpu.VMEM((feature_dim, 2 * local_experts * hidden_dim), BF16),
             pltpu.VMEM((local_experts * hidden_dim, feature_dim), BF16),
-            pltpu.VMEM(passed.shape, passed.dtype),
         ],
-        in_specs=[
-            pl.BlockSpec(memory_space=pltpu.VMEM if count == 2 and i % 2 else pl.ANY)
-            for i in range(len(shards))
-        ]
-        + [pl.BlockSpec(memory_space=pltpu.VMEM)],
-        out_specs=[pl.BlockSpec(memory_space=pltpu.VMEM)] * 3,
-        scratch_shapes=[pltpu.SemaphoreType.DMA((3 * count * local_experts,))],
-        input_output_aliases={len(shards): 2},
+        in_specs=specs,
+        out_specs=[pl.BlockSpec(memory_space=pltpu.VMEM)] * 2,
+        scratch_shapes=[pltpu.SemaphoreType.DMA((count,))],
         compiler_params=pltpu.CompilerParams(vmem_limit_bytes=VMEM_LIMIT),
-    )(*shards, pltpu.with_memory_space_constraint(passed, pltpu.VMEM))
+    )(*shards)
+
+
+def transpose_kernel(from_ref, to_ref):
+    strip = 2 * LANES
+
+    @pl.loop(0, to_ref.shape[0] // strip)
+    def _(i):
+        some = pl.ds(pl.multiple_of(i * strip, strip), strip)
+        to_ref[some, :] = from_ref[:, some].T
+
+
+def transposed(weights):
+    rows, cols = weights.shape
+    return call(transpose_kernel, [((cols, rows), BF16)], weights)[0]
 
 
 def body(tokens, w_gate, w_up, w_down, route_ids, route_scores, norm_gain, class_head, targets):
@@ -215,21 +310,8 @@
     block = (rows_here, feature_dim)
     mid = rows_here // 2
 
-    shards = exchange_shards(w_gate, w_up, w_down, group_count)
-    top, bottom = pl.pallas_call(
-        pack_kernel,
-        out_shape=[pltpu.VMEM((mid, feature_dim + LANES), BF16)] * 2,
-        in_specs=[pl.BlockSpec(memory_space=pltpu.VMEM)] * 2 + [pl.BlockSpec(memory_space=pl.ANY)],
-        out_specs=[pl.BlockSpec(memory_space=pltpu.VMEM)] * 2,
-        scratch_shapes=[pltpu.SemaphoreType.DMA((2,))],
-        compiler_params=pltpu.CompilerParams(vmem_limit_bytes=VMEM_LIMIT),
-    )(route_ids.T, route_scores.T, tokens)
-    weights_at = []
-
-    def assemble_now(passed):
-        wide, down, passed = assemble(shards, local_experts, passed)
-        weights_at.extend([wide, down])
-        return passed
+    top, bottom = pack(route_ids.T, route_scores.T, tokens)
+    wide, down = full_weights(w_gate, w_up, w_down, group_count)
 
     def rows_of(refs):
         return jnp.concatenate([ref[...] for ref in refs], axis=0) if len(refs) > 1 else refs[0][...]
@@ -237,13 +319,18 @@
     def forward_kernel(count, *refs):
         token_refs, (wide_ref, down_ref), outs = refs[:count], refs[count : count + 2], refs[count + 2 :]
         x = rows_of([ref.at[:, :feature_dim] for ref in token_refs])
-        weights = rows_of([ref.at[:, feature_dim:] for ref in token_refs]).astype(F32)
+        weights = jnp.concatenate([ref[:, feature_dim:] for ref in token_refs[::2]], axis=0).astype(F32)
         lane = lax.broadcasted_iota(jnp.int32, weights.shape, 1)
+        quarter = LANES // 4
         total = None
         for local in range(local_experts):
             expert = lax.axis_index("expert") * local_experts + local
-            mine = (lane == expert) | (lane == expert + LANES // 2)
-            scale = jnp.sum(jnp.where(mine, weights, 0.0), axis=1, keepdims=True)
+            scales = []
+            for begin in (expert, expert + 2 * quarter):
+                here = (lane == begin) | (lane == begin + quarter)
+                scales.append(jnp.sum(jnp.where(here, weights, 0.0), axis=1, keepdims=True))
+            pieces = [s[i : i + mid] for i in range(0, weights.shape[0], mid) for s in scales]
+            scale = jnp.concatenate(pieces, axis=0)
             act = dot(x, wide_ref[:, pl.ds(local * pair_dim, pair_dim)])
             gate_act, up_act = act[:, :hidden_dim], act[:, hidden_dim:]
             sigmoid_gate = jax.nn.sigmoid(gate_act)
@@ -277,14 +364,14 @@
             functools.partial(forward_kernel, len(blocks)),
             [((rows, local_experts * hidden_dim), BF16)] * 2 + part_outs(distances),
             *blocks,
-            *weights_at,
+            wide,
+            down,
             flops=flops * rows // rows_here,
         )
         saved_at[distances] = result[:2]
         keep_parts(part_at, distances, result[2:])
 
-    ring.gather(top, bottom, hold, assemble_now)
-    wide, down = weights_at
+    ring.gather(top, bottom, hold)
     for distances in tokens_at:
         forward(distances)
     gain = norm_gain.reshape(1, feature_dim)
@@ -368,18 +455,19 @@
             slope = cube[rows] * jnp.mean(residual[rows] * scaled, axis=-1, keepdims=True)
             parts.append(inv_rms[rows] * scaled - residual[rows] * slope)
         resid_grad = jnp.concatenate(parts, axis=0) if len(parts) > 1 else parts[0]
-        down_back = dot_t(resid_grad.astype(BF16), down_ref[...])
+        down_back = dot(resid_grad.astype(BF16), down_ref[...])
         total = resid_grad if distances == (0,) else None
         for local in range(local_experts):
             cols = slice(local * hidden_dim, (local + 1) * hidden_dim)
             gate_grad = (down_back[:, cols] * gate_save[:, cols].astype(F32)).astype(BF16)
             up_grad = (down_back[:, cols] * up_save[:, cols].astype(F32)).astype(BF16)
             grads = jnp.concatenate([gate_grad, up_grad], axis=1)
-            term = dot_t(grads, wide_ref[:, pl.ds(local * pair_dim, pair_dim)])
+            term = dot(grads, wide_ref[pl.ds(local * pair_dim, pair_dim), :])
             total = term if total is None else total + term
         for i, out in enumerate(outs):
             out[...] = total[i * mid : (i + 1) * mid].astype(out.dtype)
 
+    wide_t, down_t = transposed(wide), transposed(down)
     back_at = {}
 
     def backward(distances):
@@ -392,8 +480,8 @@
             *saved_at[distances],
             pooled_grad,
             gain,
-            wide,
-            down,
+            wide_t,
+            down_t,
             flops=flops * len(distances),
         )
         keep_parts(back_at, distances, result)

time: 141 us -> 129 us (0.915)
  starting transfers between devices: 70.7 us -> 64.8 us
  local copies, waits for them, and re-layouts: 5.8 us -> 0.03 us
  Pallas kernels: 23.5 us -> 26.6 us
  waiting for transfers between devices: 37.7 us -> 34.9 us
    unnamed x18 -> x6, local copies, waits for them, and re-layouts: 5.79 us -> 0.02 us
    ppermute x56, waiting for transfers between devices: 31.3 us -> 27.6 us  [send(): return lax.ppermute(value, 'expert', pairs)]
    ppermute x56, starting transfers between devices: 64.2 us -> 61 us  [send(): return lax.ppermute(value, 'expert', pairs)]
    pallas_call x2 -> x3, Pallas kernels: 1.4 us -> 4.51 us  [the longest x1 1.74 us: full_weights(): pl.pallas_call(kernel, out_shape=[pltpu.VMEM((feature_dim, 2 * local_expe...]
    ppermute x3, starting transfers between devices: 5.91 us -> 3.2 us  [body(): other = lax.ppermute(mine, 'expert', pairs)]
    pallas_call x37 -> x39, Pallas kernels: 21.3 us -> 21.3 us  [call(): pl.pallas_call(kernel, out_shape=[pltpu.VMEM(shape, dtype) for shape, dty...]
  transfers between devices with their start and end apart: 63 -> 61, of which waited for: 24 -> 23; matrix products, arithmetic and copies ran while one was open for 1% -> 1% of each run, Pallas kernels for 14% -> 17%
where the time goes in v6:
time: 129 us
  starting transfers between devices  64.8 us (50%)
  waiting for transfers between devices  34.9 us (27%)
  Pallas kernels  26.6 us (21%)
  matrix products  1.71 us (1%)
    ppermute x56, starting transfers between devices, send(): return lax.ppermute(value, 'expert', pairs)  61 us
    ppermute x56, waiting for transfers between devices, send(): return lax.ppermute(value, 'expert', pairs)  27.6 us
    pallas_call x39, Pallas kernels, call(): pl.pallas_call(kernel, out_shape=[pltpu.VMEM(shape, dtype) for shape, dty...  21.3 us
    ppermute x3, waiting for transfers between devices, body(): other = lax.ppermute(mine, 'expert', pairs)  7.24 us
    ppermute x3, starting transfers between devices, body(): other = lax.ppermute(mine, 'expert', pairs)  3.2 us
  transfers between devices with their start and end apart: 61, of which 23 were waited for; matrix products, arithmetic and copies ran while one was open for 1% of the time, Pallas kernels for 17%

profile of v6, /device:TPU:0, one launch (start us, length us, event | category | flops | bytes accessed | tf_op | source)
XLA Modules:
  0.0 129.1 jit_solution(16285288393981005123)
XLA Ops:
  3.9 2.6 %collective-permute-start.1 = (bf16[64,1152]{1,0:T(8,128)(2,1)S(1)}, bf16[64,1152]{1,0:T(8,128)(2,1)S(1)}, u32[]{:S(2)}, u32[]{:S(2)}) collective-permute-start(bf16[64,1152]{1,0:T(8,128)(2,1)S(1)} %get-tuple-element.48.refs_0_), channel_id=1, source_target_pairs={{0,4},{4,8},{8,12},{12,14},{14,10},{10,6},{6,2},{2,0},{1,5},{5,9},... | collective-permute-start | bytes 442376 | tf_op jit(solution)/shard_map/ppermute | solution.py:53
  6.6 4.4 %collective-permute-done.1.refs_0_ = bf16[64,1152]{1,0:T(8,128)(2,1)S(1)} collective-permute-done((bf16[64,1152]{1,0:T(8,128)(2,1)S(1)}, bf16[64,1152]{1,0:T(8,128)(2,1)S(1)}, u32[]{:S(2)}, u32[]{:S(2)}) %collective-permute-start.1) | collective-permute-done | bytes 147488 | tf_op jit(solution)/shard_map/ppermute | solution.py:53
  15.1 2.0 %collective-permute-done.5.refs_0_ = bf16[64,1152]{1,0:T(8,128)(2,1)S(1)} collective-permute-done((bf16[64,1152]{1,0:T(8,128)(2,1)S(1)}, bf16[64,1152]{1,0:T(8,128)(2,1)S(1)}, u32[]{:S(2)}, u32[]{:S(2)}) %collective-permute-start.5) | collective-permute-done | bytes 147488 | tf_op jit(solution)/shard_map/ppermute | solution.py:53
  17.1 2.5 %collective-permute-start.9 = (bf16[64,1152]{1,0:T(8,128)(2,1)S(1)}, bf16[64,1152]{1,0:T(8,128)(2,1)S(1)}, u32[]{:S(2)}, u32[]{:S(2)}) collective-permute-start(bf16[64,1152]{1,0:T(8,128)(2,1)S(1)} %collective-permute-done.5.refs_0_), channel_id=1, source_target_pairs={{0,4},{4,8},{8,12},{12,14},{14,10},{10,6},{6,2},{2,0},{1,5},{5,9},... | collective-permute-start | bytes 442376 | tf_op jit(solution)/shard_map/ppermute | solution.py:53
  19.6 2.6 %collective-permute-done.3.refs_2_ = bf16[64,1152]{1,0:T(8,128)(2,1)S(1)} collective-permute-done((bf16[64,1152]{1,0:T(8,128)(2,1)S(1)}, bf16[64,1152]{1,0:T(8,128)(2,1)S(1)}, u32[]{:S(2)}, u32[]{:S(2)}) %collective-permute-start.3) | collective-permute-done | bytes 147488 | tf_op jit(solution)/shard_map/ppermute | solution.py:53
  26.2 2.6 %collective-permute-done.7.refs_2_ = bf16[64,1152]{1,0:T(8,128)(2,1)S(1)} collective-permute-done((bf16[64,1152]{1,0:T(8,128)(2,1)S(1)}, bf16[64,1152]{1,0:T(8,128)(2,1)S(1)}, u32[]{:S(2)}, u32[]{:S(2)}) %collective-permute-start.7) | collective-permute-done | bytes 147488 | tf_op jit(solution)/shard_map/ppermute | solution.py:53
  44.2 2.0 %collective-permute-start.23 = (bf16[64,1024]{1,0:T(8,128)(2,1)S(1)}, bf16[64,1024]{1,0:T(8,128)(2,1)S(1)}, u32[]{:S(2)}, u32[]{:S(2)}) collective-permute-start(bf16[64,1024]{1,0:T(8,128)(2,1)S(1)} %shard_map.118), channel_id=1, source_target_pairs={{0,4},{4,8},{8,12},{12,14},{14,10},{10,6},{6,2},{2,0},{1,5},{5,9},... | collective-permute-start | bytes 393224 | tf_op jit(solution)/shard_map/ppermute | solution.py:53
  53.2 2.1 %collective-permute-start.18 = (bf16[64,1024]{1,0:T(8,128)(2,1)S(1)}, bf16[64,1024]{1,0:T(8,128)(2,1)S(1)}, u32[]{:S(2)}, u32[]{:S(2)}) collective-permute-start(bf16[64,1024]{1,0:T(8,128)(2,1)S(1)} %shard_map.114), channel_id=1, source_target_pairs={{0,4},{4,8},{8,12},{12,14},{14,10},{10,6},{6,2},{2,0},{1,5},{5,9},... | collective-permute-start | bytes 393224 | tf_op jit(solution)/shard_map/ppermute | solution.py:53
  58.6 2.5 %collective-permute-start.29 = (bf16[64,1024]{1,0:T(8,128)(2,1)S(1)}, bf16[64,1024]{1,0:T(8,128)(2,1)S(1)}, u32[]{:S(2)}, u32[]{:S(2)}) collective-permute-start(bf16[64,1024]{1,0:T(8,128)(2,1)S(1)} %shard_map.117.refs_2_), channel_id=1, source_target_pairs={{0,4},{4,8},{8,12},{12,14},{14,10},{10,6},{6,2},{2,0},{1,5},{5,9},... | collective-permute-start | bytes 393224 | tf_op jit(solution)/shard_map/ppermute | solution.py:53
  65.4 2.0 %collective-permute-start.30 = (bf16[64,1024]{1,0:T(8,128)(2,1)S(1)}, bf16[64,1024]{1,0:T(8,128)(2,1)S(1)}, u32[]{:S(2)}, u32[]{:S(2)}) collective-permute-start(bf16[64,1024]{1,0:T(8,128)(2,1)S(1)} %collective-permute-done.29.refs_4_), channel_id=1, source_target_pairs={{0,4},{4,8},{8,12},{12,14},{14,10},{10,6},{6,2},{2,0},{1,5},{5,9},... | collective-permute-start | bytes 393224 | tf_op jit(solution)/shard_map/ppermute | solution.py:53
  67.3 2.1 %collective-permute-done.33.refs_7_ = bf16[64,1024]{1,0:T(8,128)(2,1)S(1)} collective-permute-done((bf16[64,1024]{1,0:T(8,128)(2,1)S(1)}, bf16[64,1024]{1,0:T(8,128)(2,1)S(1)}, u32[]{:S(2)}, u32[]{:S(2)}) %collective-permute-start.33) | collective-permute-done | bytes 131104 | tf_op jit(solution)/shard_map/ppermute | solution.py:53
  69.5 2.8 %collective-permute-done.40.refs_6_ = bf16[64,1024]{1,0:T(8,128)(2,1)S(1)} collective-permute-done((bf16[64,1024]{1,0:T(8,128)(2,1)S(1)}, bf16[64,1024]{1,0:T(8,128)(2,1)S(1)}, u32[]{:S(2)}, u32[]{:S(2)}) %collective-permute-start.40) | collective-permute-done | bytes 131104 | tf_op jit(solution)/shard_map/ppermute | solution.py:53
  72.3 2.1 %collective-permute-start.38 = (bf16[64,1024]{1,0:T(8,128)(2,1)S(1)}, bf16[64,1024]{1,0:T(8,128)(2,1)S(1)}, u32[]{:S(2)}, u32[]{:S(2)}) collective-permute-start(bf16[64,1024]{1,0:T(8,128)(2,1)S(1)} %collective-permute-done.37.refs_5_), channel_id=1, source_target_pairs={{0,4},{4,8},{8,12},{12,14},{14,10},{10,6},{6,2},{2,0},{1,5},{5,9},... | collective-permute-start | bytes 393224 | tf_op jit(solution)/shard_map/ppermute | solution.py:53
  74.4 2.0 %collective-permute-start.31 = (bf16[64,1024]{1,0:T(8,128)(2,1)S(1)}, bf16[64,1024]{1,0:T(8,128)(2,1)S(1)}, u32[]{:S(2)}, u32[]{:S(2)}) collective-permute-start(bf16[64,1024]{1,0:T(8,128)(2,1)S(1)} %collective-permute-done.30.refs_4_), channel_id=1, source_target_pairs={{0,4},{4,8},{8,12},{12,14},{14,10},{10,6},{6,2},{2,0},{1,5},{5,9},... | collective-permute-start | bytes 393224 | tf_op jit(solution)/shard_map/ppermute | solution.py:53
  79.5 1.9 %collective-permute-start.32 = (bf16[64,1024]{1,0:T(8,128)(2,1)S(1)}, bf16[64,1024]{1,0:T(8,128)(2,1)S(1)}, u32[]{:S(2)}, u32[]{:S(2)}) collective-permute-start(bf16[64,1024]{1,0:T(8,128)(2,1)S(1)} %collective-permute-done.31.refs_4_), channel_id=1, source_target_pairs={{0,4},{4,8},{8,12},{12,14},{14,10},{10,6},{6,2},{2,0},{1,5},{5,9},... | collective-permute-start | bytes 393224 | tf_op jit(solution)/shard_map/ppermute | solution.py:53
  84.5 2.2 %collective-permute-done.36.refs_3_ = bf16[64,1024]{1,0:T(8,128)(2,1)S(1)} collective-permute-done((bf16[64,1024]{1,0:T(8,128)(2,1)S(1)}, bf16[64,1024]{1,0:T(8,128)(2,1)S(1)}, u32[]{:S(2)}, u32[]{:S(2)}) %collective-permute-start.36) | collective-permute-done | bytes 131104 | tf_op jit(solution)/shard_map/ppermute | solution.py:53
  87.3 3.8 %collective-permute-done.43 = bf16[8,1024]{1,0:T(8,128)(2,1)S(1)} collective-permute-done((bf16[8,1024]{1,0:T(8,128)(2,1)S(1)}, bf16[8,1024]{1,0:T(8,128)(2,1)S(1)}, u32[]{:S(2)}, u32[]{:S(2)}) %collective-permute-start.43) | collective-permute-done | bytes 16416 | tf_op jit(solution)/shard_map/ppermute | solution.py:429
  92.3 2.6 %collective-permute-done.44 = bf16[8,1024]{1,0:T(8,128)(2,1)S(1)} collective-permute-done((bf16[8,1024]{1,0:T(8,128)(2,1)S(1)}, bf16[8,1024]{1,0:T(8,128)(2,1)S(1)}, u32[]{:S(2)}, u32[]{:S(2)}) %collective-permute-start.44) | collective-permute-done | bytes 16416 | tf_op jit(solution)/shard_map/ppermute | solution.py:429
  94.9 2.0 %collective-permute-start.45 = (bf16[8,1024]{1,0:T(8,128)(2,1)S(1)}, bf16[8,1024]{1,0:T(8,128)(2,1)S(1)}, u32[]{:S(2)}, u32[]{:S(2)}) collective-permute-start(bf16[8,1024]{1,0:T(8,128)(2,1)S(1)} %add_convert_fusion), channel_id=1, source_target_pairs={{0,8},{2,10},{4,12},{6,14},{8,0},{10,2},{12,4},{14,6},{1,9},{3,11}... | collective-permute-start | bytes 49160 | tf_op jit(solution)/shard_map/ppermute | solution.py:429
  103.1 2.5 %shard_map.134 = (bf16[64,1024]{1,0:T(8,128)(2,1)S(1)}, f32[64,1024]{1,0:T(8,128)S(1)}, f32[64,1024]{1,0:T(8,128)S(1)}, bf16[64,1024]{1,0:T(8,128)(2,1)S(1)}) custom-call(bf16[64,1152]{1,0:T(8,128)(2,1)S(1)} %collective-permute-done.9.refs_0_, bf16[64,1024]{1,0:T(8,128)(2,1)S(1)} %collective-permute-done.10.refs_1_, ...), custom_call_target="tpu_custom_call" | custom-call | flops 1207959552 | bytes 6623232 | tf_op jit(solution)/shard_map/pallas_call | solution.py:29
  110.0 2.5 %shard_map.133 = (f32[64,1024]{1,0:T(8,128)S(1)}, f32[64,1024]{1,0:T(8,128)S(1)}, f32[64,1024]{1,0:T(8,128)S(1)}, f32[64,1024]{1,0:T(8,128)S(1)}) custom-call(bf16[64,1152]{1,0:T(8,128)(2,1)S(1)} %collective-permute-done.5.refs_0_, bf16[64,1024]{1,0:T(8,128)(2,1)S(1)} %collective-permute-done.6.refs_1_, bf16[64,1152]{1,0:T(8,128)(2,1)S(1)} %collective-permute-done.7.refs_2_, ...), custom_call_target="tpu_custom_call" | custom-call | flops 1207959552 | bytes 6623232 | tf_op jit(solution)/shard_map/pallas_call | solution.py:29
  112.8 1.9 %collective-permute-start.54 = (bf16[64,1024]{1,0:T(8,128)(2,1)S(1)}, bf16[64,1024]{1,0:T(8,128)(2,1)S(1)}, u32[]{:S(2)}, u32[]{:S(2)}) collective-permute-start(bf16[64,1024]{1,0:T(8,128)(2,1)S(1)} %shard_map.141), channel_id=1, source_target_pairs={{0,4},{4,8},{8,12},{12,14},{14,10},{10,6},{6,2},{2,0},{1,5},{5,9},... | collective-permute-start | bytes 393224 | tf_op jit(solution)/shard_map/ppermute | solution.py:53
  116.9 2.6 %shard_map.132 = (f32[64,1024]{1,0:T(8,128)S(1)}, f32[64,1024]{1,0:T(8,128)S(1)}, f32[64,1024]{1,0:T(8,128)S(1)}, f32[64,1024]{1,0:T(8,128)S(1)}) custom-call(bf16[64,1152]{1,0:T(8,128)(2,1)S(1)} %collective-permute-done.1.refs_0_, bf16[64,1024]{1,0:T(8,128)(2,1)S(1)} %collective-permute-done.2.refs_1_, bf16[64,1152]{1,0:T(8,128)(2,1)S(1)} %collective-permute-done.3.refs_2_, ...), custom_call_target="tpu_custom_call" | custom-call | flops 1207959552 | bytes 6623232 | tf_op jit(solution)/shard_map/pallas_call | solution.py:29
  119.8 1.9 %collective-permute-start.55 = (bf16[64,1024]{1,0:T(8,128)(2,1)S(1)}, bf16[64,1024]{1,0:T(8,128)(2,1)S(1)}, u32[]{:S(2)}, u32[]{:S(2)}) collective-permute-start(bf16[64,1024]{1,0:T(8,128)(2,1)S(1)} %shard_map.142), channel_id=1, source_target_pairs={{0,4},{4,8},{8,12},{12,14},{14,10},{10,6},{6,2},{2,0},{1,5},{5,9},... | collective-permute-start | bytes 393224 | tf_op jit(solution)/shard_map/ppermute | solution.py:53
  (157 shorter events, 69.7 us)
Async XLA Ops:
  2.4 28.5 %collective-permute-start = (bf16[3200,384]{1,0:T(8,128)(2,1)S(1)}, bf16[3200,384]{1,0:T(8,128)(2,1)S(1)}, u32[]{:S(2)}, u32[]{:S(2)}) collective-permute-start(bf16[3200,384]{1,0:T(8,128)(2,1)S(1)} %shard_map.105), channel_id=1, source_target_pairs={{0,1},{1,0},{2,3},{3,2},{4,5},{5,4},{6,7},{7,6},{8,9},{9,8},{10,11... | collective-permute-start | bytes 7372808 | tf_op jit(solution)/shard_map/ppermute | solution.py:234
  3.9 7.1 %collective-permute-start.1 = (bf16[64,1152]{1,0:T(8,128)(2,1)S(1)}, bf16[64,1152]{1,0:T(8,128)(2,1)S(1)}, u32[]{:S(2)}, u32[]{:S(2)}) collective-permute-start(bf16[64,1152]{1,0:T(8,128)(2,1)S(1)} %get-tuple-element.48.refs_0_), channel_id=1, source_target_pairs={{0,4},{4,8},{8,12},{12,14},{14,10},{10,6},{6,2},{2,0},{1,5},{5,9},... | collective-permute-start | bytes 442376 | tf_op jit(solution)/shard_map/ppermute | solution.py:53
  13.0 9.1 %collective-permute-start.3 = (bf16[64,1152]{1,0:T(8,128)(2,1)S(1)}, bf16[64,1152]{1,0:T(8,128)(2,1)S(1)}, u32[]{:S(2)}, u32[]{:S(2)}) collective-permute-start(bf16[64,1152]{1,0:T(8,128)(2,1)S(1)} %get-tuple-element.48.refs_0_), channel_id=1, source_target_pairs={{0,2},{4,0},{8,4},{12,8},{14,12},{10,14},{6,10},{2,6},{1,3},{5,1},... | collective-permute-start | bytes 442376 | tf_op jit(solution)/shard_map/ppermute | solution.py:53
  14.8 7.6 %collective-permute-start.2 = (bf16[64,1024]{1,0:T(8,128)(2,1)S(1)}, bf16[64,1024]{1,0:T(8,128)(2,1)S(1)}, u32[]{:S(2)}, u32[]{:S(2)}) collective-permute-start(bf16[64,1024]{1,0:T(8,128)(2,1)S(1)} %get-tuple-element.49.refs_1_), channel_id=1, source_target_pairs={{0,4},{4,8},{8,12},{12,14},{14,10},{10,6},{6,2},{2,0},{1,5},{5,9},... | collective-permute-start | bytes 393224 | tf_op jit(solution)/shard_map/ppermute | solution.py:53
  17.1 7.1 %collective-permute-start.9 = (bf16[64,1152]{1,0:T(8,128)(2,1)S(1)}, bf16[64,1152]{1,0:T(8,128)(2,1)S(1)}, u32[]{:S(2)}, u32[]{:S(2)}) collective-permute-start(bf16[64,1152]{1,0:T(8,128)(2,1)S(1)} %collective-permute-done.5.refs_0_), channel_id=1, source_target_pairs={{0,4},{4,8},{8,12},{12,14},{14,10},{10,6},{6,2},{2,0},{1,5},{5,9},... | collective-permute-start | bytes 442376 | tf_op jit(solution)/shard_map/ppermute | solution.py:53
  24.2 8.4 %collective-permute-start.13 = (bf16[64,1152]{1,0:T(8,128)(2,1)S(1)}, bf16[64,1152]{1,0:T(8,128)(2,1)S(1)}, u32[]{:S(2)}, u32[]{:S(2)}) collective-permute-start(bf16[64,1152]{1,0:T(8,128)(2,1)S(1)} %collective-permute-done.9.refs_0_), channel_id=1, source_target_pairs={{0,4},{4,8},{8,12},{12,14},{14,10},{10,6},{6,2},{2,0},{1,5},{5,9},... | collective-permute-start | bytes 442376 | tf_op jit(solution)/shard_map/ppermute | solution.py:53
  28.8 7.0 %collective-permute-start.11 = (bf16[64,1152]{1,0:T(8,128)(2,1)S(1)}, bf16[64,1152]{1,0:T(8,128)(2,1)S(1)}, u32[]{:S(2)}, u32[]{:S(2)}) collective-permute-start(bf16[64,1152]{1,0:T(8,128)(2,1)S(1)} %collective-permute-done.7.refs_2_), channel_id=1, source_target_pairs={{0,2},{4,0},{8,4},{12,8},{14,12},{10,14},{6,10},{2,6},{1,3},{5,1},... | collective-permute-start | bytes 442376 | tf_op jit(solution)/shard_map/ppermute | solution.py:53
  44.2 8.3 %collective-permute-start.23 = (bf16[64,1024]{1,0:T(8,128)(2,1)S(1)}, bf16[64,1024]{1,0:T(8,128)(2,1)S(1)}, u32[]{:S(2)}, u32[]{:S(2)}) collective-permute-start(bf16[64,1024]{1,0:T(8,128)(2,1)S(1)} %shard_map.118), channel_id=1, source_target_pairs={{0,4},{4,8},{8,12},{12,14},{14,10},{10,6},{6,2},{2,0},{1,5},{5,9},... | collective-permute-start | bytes 393224 | tf_op jit(solution)/shard_map/ppermute | solution.py:53
  48.1 8.1 %collective-permute-start.27 = (bf16[64,1024]{1,0:T(8,128)(2,1)S(1)}, bf16[64,1024]{1,0:T(8,128)(2,1)S(1)}, u32[]{:S(2)}, u32[]{:S(2)}) collective-permute-start(bf16[64,1024]{1,0:T(8,128)(2,1)S(1)} %shard_map.121), channel_id=1, source_target_pairs={{0,2},{4,0},{8,4},{12,8},{14,12},{10,14},{6,10},{2,6},{1,3},{5,1},... | collective-permute-start | bytes 393224 | tf_op jit(solution)/shard_map/ppermute | solution.py:53
  50.7 7.8 %collective-permute-start.21 = (bf16[64,1024]{1,0:T(8,128)(2,1)S(1)}, bf16[64,1024]{1,0:T(8,128)(2,1)S(1)}, u32[]{:S(2)}, u32[]{:S(2)}) collective-permute-start(bf16[64,1024]{1,0:T(8,128)(2,1)S(1)} %shard_map.116), channel_id=1, source_target_pairs={{0,2},{4,0},{8,4},{12,8},{14,12},{10,14},{6,10},{2,6},{1,3},{5,1},... | collective-permute-start | bytes 393224 | tf_op jit(solution)/shard_map/ppermute | solution.py:53
  63.0 9.3 %collective-permute-start.40 = (bf16[64,1024]{1,0:T(8,128)(2,1)S(1)}, bf16[64,1024]{1,0:T(8,128)(2,1)S(1)}, u32[]{:S(2)}, u32[]{:S(2)}) collective-permute-start(bf16[64,1024]{1,0:T(8,128)(2,1)S(1)} %shard_map.117.refs_2_), channel_id=1, source_target_pairs={{0,2},{4,0},{8,4},{12,8},{14,12},{10,14},{6,10},{2,6},{1,3},{5,1},... | collective-permute-start | bytes 393224 | tf_op jit(solution)/shard_map/ppermute | solution.py:53
  64.5 7.8 %collective-permute-start.37 = (bf16[64,1024]{1,0:T(8,128)(2,1)S(1)}, bf16[64,1024]{1,0:T(8,128)(2,1)S(1)}, u32[]{:S(2)}, u32[]{:S(2)}) collective-permute-start(bf16[64,1024]{1,0:T(8,128)(2,1)S(1)} %shard_map.123.refs_3_), channel_id=1, source_target_pairs={{0,4},{4,8},{8,12},{12,14},{14,10},{10,6},{6,2},{2,0},{1,5},{5,9},... | collective-permute-start | bytes 393224 | tf_op jit(solution)/shard_map/ppermute | solution.py:53
  65.4 9.1 %collective-permute-start.30 = (bf16[64,1024]{1,0:T(8,128)(2,1)S(1)}, bf16[64,1024]{1,0:T(8,128)(2,1)S(1)}, u32[]{:S(2)}, u32[]{:S(2)}) collective-permute-start(bf16[64,1024]{1,0:T(8,128)(2,1)S(1)} %collective-permute-done.29.refs_4_), channel_id=1, source_target_pairs={{0,4},{4,8},{8,12},{12,14},{14,10},{10,6},{6,2},{2,0},{1,5},{5,9},... | collective-permute-start | bytes 393224 | tf_op jit(solution)/shard_map/ppermute | solution.py:53
  69.5 7.0 %collective-permute-start.34 = (bf16[64,1024]{1,0:T(8,128)(2,1)S(1)}, bf16[64,1024]{1,0:T(8,128)(2,1)S(1)}, u32[]{:S(2)}, u32[]{:S(2)}) collective-permute-start(bf16[64,1024]{1,0:T(8,128)(2,1)S(1)} %collective-permute-done.33.refs_7_), channel_id=1, source_target_pairs={{0,2},{4,0},{8,4},{12,8},{14,12},{10,14},{6,10},{2,6},{1,3},{5,1},... | collective-permute-start | bytes 393224 | tf_op jit(solution)/shard_map/ppermute | solution.py:53
  105.7 6.8 %collective-permute-start.50 = (bf16[64,1024]{1,0:T(8,128)(2,1)S(1)}, bf16[64,1024]{1,0:T(8,128)(2,1)S(1)}, u32[]{:S(2)}, u32[]{:S(2)}) collective-permute-start(bf16[64,1024]{1,0:T(8,128)(2,1)S(1)} %get-tuple-element.85), channel_id=1, source_target_pairs={{0,2},{4,0},{8,4},{12,8},{14,12},{10,14},{6,10},{2,6},{1,3},{5,1},... | collective-permute-start | bytes 393224 | tf_op jit(solution)/shard_map/ppermute | solution.py:53
  105.9 6.9 %collective-permute-start.53 = (bf16[64,1024]{1,0:T(8,128)(2,1)S(1)}, bf16[64,1024]{1,0:T(8,128)(2,1)S(1)}, u32[]{:S(2)}, u32[]{:S(2)}) collective-permute-start(bf16[64,1024]{1,0:T(8,128)(2,1)S(1)} %get-tuple-element.89), channel_id=1, source_target_pairs={{0,4},{4,8},{8,12},{12,14},{14,10},{10,6},{6,2},{2,0},{1,5},{5,9},... | collective-permute-start | bytes 393224 | tf_op jit(solution)/shard_map/ppermute | solution.py:53
  107.8 6.9 %collective-permute-start.47 = (bf16[64,1024]{1,0:T(8,128)(2,1)S(1)}, bf16[64,1024]{1,0:T(8,128)(2,1)S(1)}, u32[]{:S(2)}, u32[]{:S(2)}) collective-permute-start(bf16[64,1024]{1,0:T(8,128)(2,1)S(1)} %shard_map.136), channel_id=1, source_target_pairs={{0,4},{4,8},{8,12},{12,14},{14,10},{10,6},{6,2},{2,0},{1,5},{5,9},... | collective-permute-start | bytes 393224 | tf_op jit(solution)/shard_map/ppermute | solution.py:53
  109.2 6.9 %collective-permute-start.57 = (bf16[64,1024]{1,0:T(8,128)(2,1)S(1)}, bf16[64,1024]{1,0:T(8,128)(2,1)S(1)}, u32[]{:S(2)}, u32[]{:S(2)}) collective-permute-start(bf16[64,1024]{1,0:T(8,128)(2,1)S(1)} %shard_map.143), channel_id=1, source_target_pairs={{0,2},{4,0},{8,4},{12,8},{14,12},{10,14},{6,10},{2,6},{1,3},{5,1},... | collective-permute-start | bytes 393224 | tf_op jit(solution)/shard_map/ppermute | solution.py:53
  110.0 7.0 %collective-permute-start.60 = (bf16[8,1274]{1,0:T(8,128)(2,1)S(1)}, bf16[8,1274]{1,0:T(8,128)(2,1)S(1)}, u32[]{:S(2)}, u32[]{:S(2)}) collective-permute-start(bf16[8,1274]{1,0:T(8,128)(2,1)S(1)} %pad_maximum_fusion.1), channel_id=1, source_target_pairs={{0,1},{1,0},{2,3},{3,2},{4,5},{5,4},{6,7},{7,6},{8,9},{9,8},{10,11... | collective-permute-start | bytes 61160 | tf_op jit(solution)/shard_map/ppermute | solution.py:435
  112.6 7.0 %collective-permute-start.51 = (bf16[64,1024]{1,0:T(8,128)(2,1)S(1)}, bf16[64,1024]{1,0:T(8,128)(2,1)S(1)}, u32[]{:S(2)}, u32[]{:S(2)}) collective-permute-start(bf16[64,1024]{1,0:T(8,128)(2,1)S(1)} %shard_map.139), channel_id=1, source_target_pairs={{0,2},{4,0},{8,4},{12,8},{14,12},{10,14},{6,10},{2,6},{1,3},{5,1},... | collective-permute-start | bytes 393224 | tf_op jit(solution)/shard_map/ppermute | solution.py:53
  112.8 7.0 %collective-permute-start.54 = (bf16[64,1024]{1,0:T(8,128)(2,1)S(1)}, bf16[64,1024]{1,0:T(8,128)(2,1)S(1)}, u32[]{:S(2)}, u32[]{:S(2)}) collective-permute-start(bf16[64,1024]{1,0:T(8,128)(2,1)S(1)} %shard_map.141), channel_id=1, source_target_pairs={{0,4},{4,8},{8,12},{12,14},{14,10},{10,6},{6,2},{2,0},{1,5},{5,9},... | collective-permute-start | bytes 393224 | tf_op jit(solution)/shard_map/ppermute | solution.py:53
  114.8 7.0 %collective-permute-start.48 = (bf16[64,1024]{1,0:T(8,128)(2,1)S(1)}, bf16[64,1024]{1,0:T(8,128)(2,1)S(1)}, u32[]{:S(2)}, u32[]{:S(2)}) collective-permute-start(bf16[64,1024]{1,0:T(8,128)(2,1)S(1)} %shard_map.137), channel_id=1, source_target_pairs={{0,4},{4,8},{8,12},{12,14},{14,10},{10,6},{6,2},{2,0},{1,5},{5,9},... | collective-permute-start | bytes 393224 | tf_op jit(solution)/shard_map/ppermute | solution.py:53
  116.2 7.1 %collective-permute-start.58 = (bf16[64,1024]{1,0:T(8,128)(2,1)S(1)}, bf16[64,1024]{1,0:T(8,128)(2,1)S(1)}, u32[]{:S(2)}, u32[]{:S(2)}) collective-permute-start(bf16[64,1024]{1,0:T(8,128)(2,1)S(1)} %shard_map.144), channel_id=1, source_target_pairs={{0,2},{4,0},{8,4},{12,8},{14,12},{10,14},{6,10},{2,6},{1,3},{5,1},... | collective-permute-start | bytes 393224 | tf_op jit(solution)/shard_map/ppermute | solution.py:53
  119.5 6.9 %collective-permute-start.52 = (bf16[64,1024]{1,0:T(8,128)(2,1)S(1)}, bf16[64,1024]{1,0:T(8,128)(2,1)S(1)}, u32[]{:S(2)}, u32[]{:S(2)}) collective-permute-start(bf16[64,1024]{1,0:T(8,128)(2,1)S(1)} %shard_map.140), channel_id=1, source_target_pairs={{0,2},{4,0},{8,4},{12,8},{14,12},{10,14},{6,10},{2,6},{1,3},{5,1},... | collective-permute-start | bytes 393224 | tf_op jit(solution)/shard_map/ppermute | solution.py:53
  (40 other events, 355.9 us)

commit v7 on v6

--- a/solution.py
+++ b/solution.py
@@ -114,59 +114,6 @@
         out_ref[pl.ds(i * rows, rows), :] = (own[...] + arrived).astype(BF16)
 
 
-def pack_kernel(ids_hbm, scores_hbm, tokens_hbm, top_ref, bottom_ref, ids_ref, scores_ref, sems):
-    rows, cols = tokens_hbm.shape
-    mid = rows // 2
-    quarter = LANES // 4
-    copies = [
-        pltpu.make_async_copy(ids_hbm, ids_ref, sems.at[0]),
-        pltpu.make_async_copy(scores_hbm, scores_ref, sems.at[1]),
-        pltpu.make_async_copy(
-            tokens_hbm.at[pl.ds(0, mid), :], top_ref.at[:, pl.ds(0, cols)], sems.at[2]
-        ),
-        pltpu.make_async_copy(tokens_hbm.at[pl.ds(mid, mid), :], bottom_ref, sems.at[3]),
-    ]
-    for copy in copies:
-        copy.start()
-    copies[0].wait()
-    copies[1].wait()
-    scores = scores_ref[...]
-    ids = ids_ref[...]
-    route_weight = scores / jnp.sum(scores, axis=0, keepdims=True)
-    expert = lax.broadcasted_iota(jnp.int32, (quarter, rows), 0)
-    weight_by = jnp.zeros((quarter, rows), F32)
-    for choice_k in range(scores.shape[0]):
-        one = slice(choice_k, choice_k + 1)
-        weight_by = weight_by + jnp.where(ids[one] == expert, route_weight[one], 0.0)
-    high = weight_by.astype(BF16).astype(F32)
-    weights = jnp.concatenate([high, weight_by - high] * 2, axis=0).T
-    lane = lax.broadcasted_iota(jnp.int32, (mid, LANES), 1)
-    both = jnp.where(lane < 2 * quarter, weights[:mid], weights[mid:])
-    top_ref[:, cols:] = both.astype(BF16)
-    copies[2].wait()
-    copies[3].wait()
-
-
-def pack(ids, scores, tokens):
-    rows, cols = tokens.shape
-    args = [pltpu.with_memory_space_constraint(a, pltpu.HBM) for a in (ids, scores, tokens)]
-    return pl.pallas_call(
-        pack_kernel,
-        out_shape=[
-            pltpu.VMEM((rows // 2, cols + LANES), BF16),
-            pltpu.VMEM((rows // 2, cols), BF16),
-        ],
-        in_specs=[pl.BlockSpec(memory_space=pl.ANY)] * 3,
-        out_specs=[pl.BlockSpec(memory_space=pltpu.VMEM)] * 2,
-        scratch_shapes=[
-            pltpu.VMEM(ids.shape, ids.dtype),
-            pltpu.VMEM(scores.shape, F32),
-            pltpu.SemaphoreType.DMA((4,)),
-        ],
-        compiler_params=pltpu.CompilerParams(vmem_limit_bytes=VMEM_LIMIT),
-    )(*args)
-
-
 class Copies:
     def __init__(self, sems):
         self.sems, self.started = sems, []
@@ -196,46 +143,76 @@
     return row, places
 
 
-def pack_weights(w_gate, w_up, w_down):
-    rows, places = strips(w_gate.shape, w_down.shape)
-    hidden_dim = w_gate.shape[2]
-
-    def kernel(gate_hbm, up_hbm, down_hbm, out_ref, sems):
+def pack(ids, scores, tokens, shards):
+    rows, cols = tokens.shape
+    mid = rows // 2
+    quarter = LANES // 4
+    inputs = [ids, scores, tokens, *shards]
+    packed_shape, places, count = None, [], 0
+    if shards:
+        hidden_dim = shards[0].shape[2]
+        packed_rows, places = strips(shards[0].shape, shards[2].shape)
+        packed_shape = (packed_rows, hidden_dim)
+        count = sum(len(pair) + len(downs) for pair, downs in places)
+
+    def kernel(*refs):
+        ids_hbm, scores_hbm, tokens_hbm, *shards_hbm = refs[: len(inputs)]
+        top_ref, bottom_ref, *packed_refs = refs[len(inputs) : -3]
+        ids_ref, scores_ref, sems = refs[-3:]
         copies = Copies(sems)
+        copies.start(ids_hbm, ids_ref)
+        copies.start(scores_hbm, scores_ref)
+        copies.start(tokens_hbm.at[pl.ds(0, mid), :], top_ref.at[:, pl.ds(0, cols)])
+        copies.start(tokens_hbm.at[pl.ds(mid, mid), :], bottom_ref)
         for local, (pair, downs) in enumerate(places):
-            for source, (row, some) in zip((gate_hbm, up_hbm), pair):
+            out_ref = packed_refs[0]
+            for source, (row, some) in zip(shards_hbm, pair):
                 copies.start(source.at[local], out_ref.at[pl.ds(row, some), :])
-            for row, some, begin, cols in downs:
-                source = down_hbm.at[local, :, pl.ds(begin, cols)]
-                copies.start(source, out_ref.at[pl.ds(row, some), pl.ds(0, cols)])
-                if cols < hidden_dim:
-                    out_ref[pl.ds(row, some), pl.ds(cols, hidden_dim - cols)] = jnp.zeros(
-                        (some, hidden_dim - cols), BF16
-                    )
-        copies.wait()
-
-    shards = [pltpu.with_memory_space_constraint(w, pltpu.HBM) for w in (w_gate, w_up, w_down)]
-    count = sum(len(pair) + len(downs) for pair, downs in places)
+            for row, some, begin, width in downs:
+                source = shards_hbm[2].at[local, :, pl.ds(begin, width)]
+                copies.start(source, out_ref.at[pl.ds(row, some), pl.ds(0, width)])
+                if width < hidden_dim:
+                    rest = hidden_dim - width
+                    out_ref[pl.ds(row, some), pl.ds(width, rest)] = jnp.zeros((some, rest), BF16)
+        copies.started[0].wait()
+        copies.started[1].wait()
+        scores = scores_ref[...]
+        ids = ids_ref[...]
+        route_weight = scores / jnp.sum(scores, axis=0, keepdims=True)
+        expert = lax.broadcasted_iota(jnp.int32, (quarter, rows), 0)
+        weight_by = jnp.zeros((quarter, rows), F32)
+        for choice_k in range(scores.shape[0]):
+            one = slice(choice_k, choice_k + 1)
+            weight_by = weight_by + jnp.where(ids[one] == expert, route_weight[one], 0.0)
+        high = weight_by.astype(BF16).astype(F32)
+        weights = jnp.concatenate([high, weight_by - high] * 2, axis=0).T
+        lane = lax.broadcasted_iota(jnp.int32, (mid, LANES), 1)
+        both = jnp.where(lane < 2 * quarter, weights[:mid], weights[mid:])
+        top_ref[:, cols:] = both.astype(BF16)
+        for copy in copies.started[2:]:
+            copy.wait()
+
+    outs = [pltpu.VMEM((mid, cols + LANES), BF16), pltpu.VMEM((mid, cols), BF16)]
+    if shards:
+        outs.append(pltpu.VMEM(packed_shape, BF16))
     return pl.pallas_call(
         kernel,
-        out_shape=pltpu.VMEM((rows, hidden_dim), BF16),
-        in_specs=[pl.BlockSpec(memory_space=pl.ANY)] * 3,
-        out_specs=pl.BlockSpec(memory_space=pltpu.VMEM),
-        scratch_shapes=[pltpu.SemaphoreType.DMA((count,))],
+        out_shape=outs,
+        in_specs=[pl.BlockSpec(memory_space=pl.ANY)] * len(inputs),
+        out_specs=[pl.BlockSpec(memory_space=pltpu.VMEM)] * len(outs),
+        scratch_shapes=[
+            pltpu.VMEM(ids.shape, ids.dtype),
+            pltpu.VMEM(scores.shape, F32),
+            pltpu.SemaphoreType.DMA((4 + count,)),
+        ],
         compiler_params=pltpu.CompilerParams(vmem_limit_bytes=VMEM_LIMIT),
-    )(*shards)
-
-
-def full_weights(w_gate, w_up, w_down, group_count):
-    local_experts, _, hidden_dim = w_gate.shape
-    feature_dim = w_down.shape[2]
-    paired = group_count == 2
-    if paired:
-        other = lax.ppermute(pack_weights(w_gate, w_up, w_down), "group", [(0, 1), (1, 0)])
-        other = pltpu.with_memory_space_constraint(other, pltpu.VMEM)
-        shards = [w_gate, w_up, w_down]
-    else:
-        shards = [lax.all_gather(w, "group", axis=1, tiled=True) for w in (w_gate, w_up, w_down)]
+    )(*[pltpu.with_memory_space_constraint(a, pltpu.HBM) for a in inputs])
+
+
+def full_weights(shards, packed):
+    local_experts, _, hidden_dim = shards[0].shape
+    feature_dim = shards[2].shape[2]
+    paired = packed is not None
     _, places = strips(shards[0].shape, shards[2].shape)
     depth, height = shards[0].shape[1], shards[2].shape[1]
 
@@ -272,7 +249,7 @@
     if paired:
         count += sum(len(pair) + len(downs) for pair, downs in places)
         specs.append(pl.BlockSpec(memory_space=pltpu.VMEM))
-        shards.append(other)
+        shards.append(pltpu.with_memory_space_constraint(packed, pltpu.VMEM))
     return pl.pallas_call(
         kernel,
         out_shape=[
@@ -310,14 +287,22 @@
     block = (rows_here, feature_dim)
     mid = rows_here // 2
 
-    top, bottom = pack(route_ids.T, route_scores.T, tokens)
-    wide, down = full_weights(w_gate, w_up, w_down, group_count)
+    shards = [w_gate, w_up, w_down]
+    if group_count == 2:
+        top, bottom, packed = pack(route_ids.T, route_scores.T, tokens, shards)
+        packed = lax.ppermute(packed, "group", [(0, 1), (1, 0)])
+    else:
+        top, bottom = pack(route_ids.T, route_scores.T, tokens, [])
+        shards = [lax.all_gather(w, "group", axis=1, tiled=True) for w in shards]
+        packed = None
+    wide, down = full_weights(shards, packed)
 
     def rows_of(refs):
         return jnp.concatenate([ref[...] for ref in refs], axis=0) if len(refs) > 1 else refs[0][...]
 
-    def forward_kernel(count, *refs):
-        token_refs, (wide_ref, down_ref), outs = refs[:count], refs[count : count + 2], refs[count + 2 :]
+    def forward_kernel(count, guards, *refs):
+        token_refs, (wide_ref, down_ref) = refs[:count], refs[count : count + 2]
+        outs = refs[count + 2 + guards :]
         x = rows_of([ref.at[:, :feature_dim] for ref in token_refs])
         weights = jnp.concatenate([ref[:, feature_dim:] for ref in token_refs[::2]], axis=0).astype(F32)
         lane = lax.broadcasted_iota(jnp.int32, weights.shape, 1)
@@ -360,12 +345,14 @@
     def forward(distances):
         blocks = tokens_at[distances]
         rows = mid * len(blocks)
+        guards = [saved_at[d][0] for d in ((0,), (-1, 1))] if distances == (ring.half,) else []
         result = call(
-            functools.partial(forward_kernel, len(blocks)),
+            functools.partial(forward_kernel, len(blocks), len(guards)),
             [((rows, local_experts * hidden_dim), BF16)] * 2 + part_outs(distances),
             *blocks,
             wide,
             down,
+            *guards,
             flops=flops * rows // rows_here,
         )
         saved_at[distances] = result[:2]
@@ -381,7 +368,7 @@
         for own, arrived in zip(part_at[0], ring.scatter(part_at))
     ]
 
-    moe_at, mean_at = {}, {}
+    norm_at, mean_at = {}, {}
 
     def residual_of(token_refs, moe_refs):
         token_rows = rows_of([ref.at[:, :feature_dim] for ref in token_refs]).astype(F32)
@@ -392,8 +379,11 @@
 
     def norm_kernel(distances, count, *refs):
         residual = residual_of(refs[:count], refs[count : 2 * count])
-        gain_ref, so_far, out_ref = refs[2 * count :]
-        normed = residual * inv_rms_of(residual) * gain_ref[...]
+        gain_ref, so_far, out_ref, residual_ref, inv_ref = refs[2 * count :]
+        inv_rms = inv_rms_of(residual)
+        residual_ref[...] = residual
+        inv_ref[...] = jnp.broadcast_to(inv_rms, inv_ref.shape)
+        normed = residual * inv_rms * gain_ref[...]
         pooled = so_far[...]
         row = lax.broadcasted_iota(jnp.int32, pooled.shape, 0)
         for i, k in enumerate(distances):
@@ -406,15 +396,15 @@
     mean_at["pooled"] = jnp.zeros(pooled_shape, F32)
 
     def norm(distances, blocks):
-        moe_at[distances] = blocks
-        mean_at["pooled"] = call(
+        rows = mid * len(blocks)
+        mean_at["pooled"], *norm_at[distances] = call(
             functools.partial(norm_kernel, distances, len(blocks)),
-            [(pooled_shape, F32)],
+            [(pooled_shape, F32), ((rows, feature_dim), F32), ((rows, LANES), F32)],
             *tokens_at[distances],
             *blocks,
             gain,
             mean_at["pooled"],
-        )[0]
+        )
 
     ring.gather(moe_top, moe_bottom, norm)
     pooled = mean_at["pooled"].astype(BF16)
@@ -442,11 +432,9 @@
         preferred_element_type=F32,
     )
 
-    def backward_kernel(distances, count, *refs):
-        residual = residual_of(refs[:count], refs[count : 2 * count])
-        gate_save, up_save, grad_ref, gain_ref, wide_ref, down_ref = refs[2 * count : 2 * count + 6]
-        outs = refs[2 * count + 6 :]
-        inv_rms = inv_rms_of(residual)
+    def backward_kernel(distances, residual_ref, inv_ref, gate_save, up_save, *refs):
+        grad_ref, gain_ref, wide_ref, down_ref, *outs = refs
+        residual, inv_rms = residual_ref[...], inv_ref[:, :1]
         cube = inv_rms * inv_rms * inv_rms
         parts = []
         for i, k in enumerate(distances):
@@ -471,12 +459,10 @@
     back_at = {}
 
     def backward(distances):
-        blocks = tokens_at[distances]
         result = call(
-            functools.partial(backward_kernel, distances, len(blocks)),
+            functools.partial(backward_kernel, distances),
             part_outs(distances),
-            *blocks,
-            *moe_at[distances],
+            *norm_at[distances],
             *saved_at[distances],
             pooled_grad,
             gain,

time: 129 us -> 129 us (level)
  starting transfers between devices: 64.8 us -> 68.8 us
  waiting for transfers between devices: 34.9 us -> 31.7 us
    ppermute x3, starting transfers between devices: 3.2 us -> 7.49 us  [body(): other = lax.ppermute(mine, 'expert', pairs)]
    ppermute x3, waiting for transfers between devices: 7.24 us -> 3.51 us  [body(): other = lax.ppermute(mine, 'expert', pairs)]
    pallas_call x2 -> x1, Pallas kernels: 2.76 us -> 1.92 us  [pack(): pl.pallas_call(kernel, out_shape=outs, in_specs=[pl.BlockSpec(memory_spac...]
  transfers between devices with their start and end apart: 61 -> 61, of which waited for: 23 -> 25; matrix products, arithmetic and copies ran while one was open for 1% -> 1% of each run, Pallas kernels for 17% -> 17%
where the time goes in v7:
time: 129 us
  starting transfers between devices  68.8 us (53%)
  waiting for transfers between devices  31.7 us (25%)
  Pallas kernels  25.7 us (20%)
  matrix products  1.71 us (1%)
    ppermute x56, starting transfers between devices, send(): return lax.ppermute(value, 'expert', pairs)  60.7 us
    ppermute x56, waiting for transfers between devices, send(): return lax.ppermute(value, 'expert', pairs)  28.2 us
    pallas_call x39, Pallas kernels, call(): pl.pallas_call(kernel, out_shape=[pltpu.VMEM(shape, dtype) for shape, dty...  21.2 us
    ppermute x3, starting transfers between devices, body(): other = lax.ppermute(mine, 'expert', pairs)  7.49 us
    ppermute x3, waiting for transfers between devices, body(): other = lax.ppermute(mine, 'expert', pairs)  3.51 us
  transfers between devices with their start and end apart: 61, of which 25 were waited for; matrix products, arithmetic and copies ran while one was open for 1% of the time, Pallas kernels for 17%

profile of v7, /device:TPU:0, one launch (start us, length us, event | category | flops | bytes accessed | tf_op | source)
XLA Modules:
  0.0 129.0 jit_solution(14365886958148421813)
XLA Ops:
  0.6 1.9 %shard_map.104 = (bf16[64,1152]{1,0:T(8,128)(2,1)S(1)}, bf16[64,1024]{1,0:T(8,128)(2,1)S(1)}, bf16[3200,384]{1,0:T(8,128)(2,1)S(1)}) custom-call(s32[8,128]{1,0:T(8,128)} %bitcast.19, f32[8,128]{1,0:T(8,128)} %bitcast.20, bf16[128,1024]{1,0:T(8,128)(2,1)} %refs_2_.2, bf16[2,512,384]{2,1,0:T(8,128)(2,1)} %refs_0_.1, bf16[2,512,384]{2,1,0:T(8,128)(2,1)} %refs_1_.1, ...), custom_call_target="tpu_custom_call" | custom-call | tf_op jit(solution)/shard_map/pallas_call | solution.py:198
  3.1 2.6 %collective-permute-start.1 = (bf16[64,1152]{1,0:T(8,128)(2,1)S(1)}, bf16[64,1152]{1,0:T(8,128)(2,1)S(1)}, u32[]{:S(2)}, u32[]{:S(2)}) collective-permute-start(bf16[64,1152]{1,0:T(8,128)(2,1)S(1)} %get-tuple-element.64.refs_0_), channel_id=1, source_target_pairs={{0,4},{4,8},{8,12},{12,14},{14,10},{10,6},{6,2},{2,0},{1,5},{5,9},... | collective-permute-start | bytes 442376 | tf_op jit(solution)/shard_map/ppermute | solution.py:53
  5.7 1.9 %collective-permute-start.3 = (bf16[64,1152]{1,0:T(8,128)(2,1)S(1)}, bf16[64,1152]{1,0:T(8,128)(2,1)S(1)}, u32[]{:S(2)}, u32[]{:S(2)}) collective-permute-start(bf16[64,1152]{1,0:T(8,128)(2,1)S(1)} %get-tuple-element.64.refs_0_), channel_id=1, source_target_pairs={{0,2},{4,0},{8,4},{12,8},{14,12},{10,14},{6,10},{2,6},{1,3},{5,1},... | collective-permute-start | bytes 442376 | tf_op jit(solution)/shard_map/ppermute | solution.py:53
  7.7 2.4 %collective-permute-done.1.refs_0_ = bf16[64,1152]{1,0:T(8,128)(2,1)S(1)} collective-permute-done((bf16[64,1152]{1,0:T(8,128)(2,1)S(1)}, bf16[64,1152]{1,0:T(8,128)(2,1)S(1)}, u32[]{:S(2)}, u32[]{:S(2)}) %collective-permute-start.1) | collective-permute-done | bytes 147488 | tf_op jit(solution)/shard_map/ppermute | solution.py:53
  14.7 2.1 %collective-permute-done.5.refs_0_ = bf16[64,1152]{1,0:T(8,128)(2,1)S(1)} collective-permute-done((bf16[64,1152]{1,0:T(8,128)(2,1)S(1)}, bf16[64,1152]{1,0:T(8,128)(2,1)S(1)}, u32[]{:S(2)}, u32[]{:S(2)}) %collective-permute-start.5) | collective-permute-done | bytes 147488 | tf_op jit(solution)/shard_map/ppermute | solution.py:53
  16.8 1.9 %collective-permute-start.9 = (bf16[64,1152]{1,0:T(8,128)(2,1)S(1)}, bf16[64,1152]{1,0:T(8,128)(2,1)S(1)}, u32[]{:S(2)}, u32[]{:S(2)}) collective-permute-start(bf16[64,1152]{1,0:T(8,128)(2,1)S(1)} %collective-permute-done.5.refs_0_), channel_id=1, source_target_pairs={{0,4},{4,8},{8,12},{12,14},{14,10},{10,6},{6,2},{2,0},{1,5},{5,9},... | collective-permute-start | bytes 442376 | tf_op jit(solution)/shard_map/ppermute | solution.py:53
  21.7 2.9 %collective-permute-done.6.refs_1_ = bf16[64,1024]{1,0:T(8,128)(2,1)S(1)} collective-permute-done((bf16[64,1024]{1,0:T(8,128)(2,1)S(1)}, bf16[64,1024]{1,0:T(8,128)(2,1)S(1)}, u32[]{:S(2)}, u32[]{:S(2)}) %collective-permute-start.6) | collective-permute-done | bytes 131104 | tf_op jit(solution)/shard_map/ppermute | solution.py:53
  40.7 1.9 %collective-permute-start.16 = (bf16[64,1024]{1,0:T(8,128)(2,1)S(1)}, bf16[64,1024]{1,0:T(8,128)(2,1)S(1)}, u32[]{:S(2)}, u32[]{:S(2)}) collective-permute-start(bf16[64,1024]{1,0:T(8,128)(2,1)S(1)} %shard_map.111), channel_id=1, source_target_pairs={{0,4},{4,8},{8,12},{12,14},{14,10},{10,6},{6,2},{2,0},{1,5},{5,9},... | collective-permute-start | bytes 393224 | tf_op jit(solution)/shard_map/ppermute | solution.py:53
  49.2 2.0 %collective-permute-start.27 = (bf16[64,1024]{1,0:T(8,128)(2,1)S(1)}, bf16[64,1024]{1,0:T(8,128)(2,1)S(1)}, u32[]{:S(2)}, u32[]{:S(2)}) collective-permute-start(bf16[64,1024]{1,0:T(8,128)(2,1)S(1)} %shard_map.120), channel_id=1, source_target_pairs={{0,2},{4,0},{8,4},{12,8},{14,12},{10,14},{6,10},{2,6},{1,3},{5,1},... | collective-permute-start | bytes 393224 | tf_op jit(solution)/shard_map/ppermute | solution.py:53
  53.0 2.5 %collective-permute-done.17.arrived_ref = bf16[64,1024]{1,0:T(8,128)(2,1)S(1)} collective-permute-done((bf16[64,1024]{1,0:T(8,128)(2,1)S(1)}, bf16[64,1024]{1,0:T(8,128)(2,1)S(1)}, u32[]{:S(2)}, u32[]{:S(2)}) %collective-permute-start.17) | collective-permute-done | bytes 131104 | tf_op jit(solution)/shard_map/ppermute | solution.py:53
  55.6 2.0 %collective-permute-start.24 = (bf16[64,1024]{1,0:T(8,128)(2,1)S(1)}, bf16[64,1024]{1,0:T(8,128)(2,1)S(1)}, u32[]{:S(2)}, u32[]{:S(2)}) collective-permute-start(bf16[64,1024]{1,0:T(8,128)(2,1)S(1)} %shard_map.118), channel_id=1, source_target_pairs={{0,4},{4,8},{8,12},{12,14},{14,10},{10,6},{6,2},{2,0},{1,5},{5,9},... | collective-permute-start | bytes 393224 | tf_op jit(solution)/shard_map/ppermute | solution.py:53
  57.8 2.8 %collective-permute-done.18.refs_1_ = bf16[64,1024]{1,0:T(8,128)(2,1)S(1)} collective-permute-done((bf16[64,1024]{1,0:T(8,128)(2,1)S(1)}, bf16[64,1024]{1,0:T(8,128)(2,1)S(1)}, u32[]{:S(2)}, u32[]{:S(2)}) %collective-permute-start.18) | collective-permute-done | bytes 131104 | tf_op jit(solution)/shard_map/ppermute | solution.py:53
  60.8 2.5 %collective-permute-done.24.refs_1_ = bf16[64,1024]{1,0:T(8,128)(2,1)S(1)} collective-permute-done((bf16[64,1024]{1,0:T(8,128)(2,1)S(1)}, bf16[64,1024]{1,0:T(8,128)(2,1)S(1)}, u32[]{:S(2)}, u32[]{:S(2)}) %collective-permute-start.24) | collective-permute-done | bytes 131104 | tf_op jit(solution)/shard_map/ppermute | solution.py:53
  69.4 1.9 %collective-permute-start.34 = (bf16[64,1024]{1,0:T(8,128)(2,1)S(1)}, bf16[64,1024]{1,0:T(8,128)(2,1)S(1)}, u32[]{:S(2)}, u32[]{:S(2)}) collective-permute-start(bf16[64,1024]{1,0:T(8,128)(2,1)S(1)} %collective-permute-done.33.refs_7_), channel_id=1, source_target_pairs={{0,2},{4,0},{8,4},{12,8},{14,12},{10,14},{6,10},{2,6},{1,3},{5,1},... | collective-permute-start | bytes 393224 | tf_op jit(solution)/shard_map/ppermute | solution.py:53
  72.3 1.9 %collective-permute-start.41 = (bf16[64,1024]{1,0:T(8,128)(2,1)S(1)}, bf16[64,1024]{1,0:T(8,128)(2,1)S(1)}, u32[]{:S(2)}, u32[]{:S(2)}) collective-permute-start(bf16[64,1024]{1,0:T(8,128)(2,1)S(1)} %collective-permute-done.40.refs_6_), channel_id=1, source_target_pairs={{0,2},{4,0},{8,4},{12,8},{14,12},{10,14},{6,10},{2,6},{1,3},{5,1},... | collective-permute-start | bytes 393224 | tf_op jit(solution)/shard_map/ppermute | solution.py:53
  75.3 2.1 %collective-permute-start.35 = (bf16[64,1024]{1,0:T(8,128)(2,1)S(1)}, bf16[64,1024]{1,0:T(8,128)(2,1)S(1)}, u32[]{:S(2)}, u32[]{:S(2)}) collective-permute-start(bf16[64,1024]{1,0:T(8,128)(2,1)S(1)} %collective-permute-done.34.refs_7_), channel_id=1, source_target_pairs={{0,2},{4,0},{8,4},{12,8},{14,12},{10,14},{6,10},{2,6},{1,3},{5,1},... | collective-permute-start | bytes 393224 | tf_op jit(solution)/shard_map/ppermute | solution.py:53
  77.5 1.9 %collective-permute-start.42 = (bf16[64,1024]{1,0:T(8,128)(2,1)S(1)}, bf16[64,1024]{1,0:T(8,128)(2,1)S(1)}, u32[]{:S(2)}, u32[]{:S(2)}) collective-permute-start(bf16[64,1024]{1,0:T(8,128)(2,1)S(1)} %collective-permute-done.41.refs_6_), channel_id=1, source_target_pairs={{0,2},{4,0},{8,4},{12,8},{14,12},{10,14},{6,10},{2,6},{1,3},{5,1},... | collective-permute-start | bytes 393224 | tf_op jit(solution)/shard_map/ppermute | solution.py:53
  80.5 2.1 %collective-permute-start.36 = (bf16[64,1024]{1,0:T(8,128)(2,1)S(1)}, bf16[64,1024]{1,0:T(8,128)(2,1)S(1)}, u32[]{:S(2)}, u32[]{:S(2)}) collective-permute-start(bf16[64,1024]{1,0:T(8,128)(2,1)S(1)} %collective-permute-done.35.refs_7_), channel_id=1, source_target_pairs={{0,2},{4,0},{8,4},{12,8},{14,12},{10,14},{6,10},{2,6},{1,3},{5,1},... | collective-permute-start | bytes 393224 | tf_op jit(solution)/shard_map/ppermute | solution.py:53
  86.1 2.1 %collective-permute-start.43 = (bf16[8,1024]{1,0:T(8,128)(2,1)S(1)}, bf16[8,1024]{1,0:T(8,128)(2,1)S(1)}, u32[]{:S(2)}, u32[]{:S(2)}) collective-permute-start(bf16[8,1024]{1,0:T(8,128)(2,1)S(1)} %convolution_convert_fusion), channel_id=1, source_target_pairs={{0,2},{2,0},{4,6},{6,4},{8,10},{10,8},{12,14},{14,12},{1,3},{3,1},... | collective-permute-start | bytes 49160 | tf_op jit(solution)/shard_map/ppermute | solution.py:419
  89.9 2.2 %collective-permute-start.44 = (bf16[8,1024]{1,0:T(8,128)(2,1)S(1)}, bf16[8,1024]{1,0:T(8,128)(2,1)S(1)}, u32[]{:S(2)}, u32[]{:S(2)}) collective-permute-start(bf16[8,1024]{1,0:T(8,128)(2,1)S(1)} %add_convert_fusion.1), channel_id=1, source_target_pairs={{0,4},{2,6},{4,0},{6,2},{8,12},{10,14},{12,8},{14,10},{1,5},{3,7},... | collective-permute-start | bytes 49160 | tf_op jit(solution)/shard_map/ppermute | solution.py:419
  93.9 3.2 %collective-permute-start.45 = (bf16[8,1024]{1,0:T(8,128)(2,1)S(1)}, bf16[8,1024]{1,0:T(8,128)(2,1)S(1)}, u32[]{:S(2)}, u32[]{:S(2)}) collective-permute-start(bf16[8,1024]{1,0:T(8,128)(2,1)S(1)} %add_convert_fusion), channel_id=1, source_target_pairs={{0,8},{2,10},{4,12},{6,14},{8,0},{10,2},{12,4},{14,6},{1,9},{3,11}... | collective-permute-start | bytes 49160 | tf_op jit(solution)/shard_map/ppermute | solution.py:419
  102.5 2.4 %shard_map.133 = (bf16[64,1024]{1,0:T(8,128)(2,1)S(1)}, f32[64,1024]{1,0:T(8,128)S(1)}, f32[64,1024]{1,0:T(8,128)S(1)}, bf16[64,1024]{1,0:T(8,128)(2,1)S(1)}) custom-call(f32[256,1024]{1,0:T(8,128)S(1)} %get-tuple-element.105.residual_ref, f32[256,128]{1,0:T(8,128)S(1)} %get-tuple-element.106.inv_ref, bf16[256,768]{1,0:T(8,128)(2,1)S(1)} %get-tuple-element.107.gate_save, ...), custom_call_target="tpu_custom_call" | custom-call | flops 1207959552 | bytes 6721536 | tf_op jit(solution)/shard_map/pallas_call | solution.py:29
  109.3 2.5 %shard_map.132 = (f32[64,1024]{1,0:T(8,128)S(1)}, f32[64,1024]{1,0:T(8,128)S(1)}, f32[64,1024]{1,0:T(8,128)S(1)}, f32[64,1024]{1,0:T(8,128)S(1)}) custom-call(f32[256,1024]{1,0:T(8,128)S(1)} %get-tuple-element.100.residual_ref, f32[256,128]{1,0:T(8,128)S(1)} %get-tuple-element.101.inv_ref, bf16[256,768]{1,0:T(8,128)(2,1)S(1)} %get-tuple-element.102.gate_save, ...), custom_call_target="tpu_custom_call" | custom-call | flops 1207959552 | bytes 6721536 | tf_op jit(solution)/shard_map/pallas_call | solution.py:29
  116.2 2.5 %shard_map.131 = (f32[64,1024]{1,0:T(8,128)S(1)}, f32[64,1024]{1,0:T(8,128)S(1)}, f32[64,1024]{1,0:T(8,128)S(1)}, f32[64,1024]{1,0:T(8,128)S(1)}) custom-call(f32[256,1024]{1,0:T(8,128)S(1)} %get-tuple-element.96.residual_ref, f32[256,128]{1,0:T(8,128)S(1)} %get-tuple-element.97.inv_ref, bf16[256,768]{1,0:T(8,128)(2,1)S(1)} %get-tuple-element.74.refs_5_.gate_save, ...), custom_call_target="tpu_custom_call" | custom-call | flops 1207959552 | bytes 6721536 | tf_op jit(solution)/shard_map/pallas_call | solution.py:29
  (156 shorter events, 73.7 us)
Async XLA Ops:
  2.6 26.1 %collective-permute-start = (bf16[3200,384]{1,0:T(8,128)(2,1)S(1)}, bf16[3200,384]{1,0:T(8,128)(2,1)S(1)}, u32[]{:S(2)}, u32[]{:S(2)}) collective-permute-start(bf16[3200,384]{1,0:T(8,128)(2,1)S(1)} %get-tuple-element.66), channel_id=1, source_target_pairs={{0,1},{1,0},{2,3},{3,2},{4,5},{5,4},{6,7},{7,6},{8,9},{9,8},{10,11... | collective-permute-start | bytes 7372808 | tf_op jit(solution)/shard_map/ppermute | solution.py:293
  3.1 7.0 %collective-permute-start.1 = (bf16[64,1152]{1,0:T(8,128)(2,1)S(1)}, bf16[64,1152]{1,0:T(8,128)(2,1)S(1)}, u32[]{:S(2)}, u32[]{:S(2)}) collective-permute-start(bf16[64,1152]{1,0:T(8,128)(2,1)S(1)} %get-tuple-element.64.refs_0_), channel_id=1, source_target_pairs={{0,4},{4,8},{8,12},{12,14},{14,10},{10,6},{6,2},{2,0},{1,5},{5,9},... | collective-permute-start | bytes 442376 | tf_op jit(solution)/shard_map/ppermute | solution.py:53
  5.7 7.8 %collective-permute-start.4 = (bf16[64,1024]{1,0:T(8,128)(2,1)S(1)}, bf16[64,1024]{1,0:T(8,128)(2,1)S(1)}, u32[]{:S(2)}, u32[]{:S(2)}) collective-permute-start(bf16[64,1024]{1,0:T(8,128)(2,1)S(1)} %get-tuple-element.65.refs_1_), channel_id=1, source_target_pairs={{0,2},{4,0},{8,4},{12,8},{14,12},{10,14},{6,10},{2,6},{1,3},{5,1},... | collective-permute-start | bytes 393224 | tf_op jit(solution)/shard_map/ppermute | solution.py:53
  5.7 8.7 %collective-permute-start.3 = (bf16[64,1152]{1,0:T(8,128)(2,1)S(1)}, bf16[64,1152]{1,0:T(8,128)(2,1)S(1)}, u32[]{:S(2)}, u32[]{:S(2)}) collective-permute-start(bf16[64,1152]{1,0:T(8,128)(2,1)S(1)} %get-tuple-element.64.refs_0_), channel_id=1, source_target_pairs={{0,2},{4,0},{8,4},{12,8},{14,12},{10,14},{6,10},{2,6},{1,3},{5,1},... | collective-permute-start | bytes 442376 | tf_op jit(solution)/shard_map/ppermute | solution.py:53
  11.9 7.7 %collective-permute-start.2 = (bf16[64,1024]{1,0:T(8,128)(2,1)S(1)}, bf16[64,1024]{1,0:T(8,128)(2,1)S(1)}, u32[]{:S(2)}, u32[]{:S(2)}) collective-permute-start(bf16[64,1024]{1,0:T(8,128)(2,1)S(1)} %get-tuple-element.65.refs_1_), channel_id=1, source_target_pairs={{0,4},{4,8},{8,12},{12,14},{14,10},{10,6},{6,2},{2,0},{1,5},{5,9},... | collective-permute-start | bytes 393224 | tf_op jit(solution)/shard_map/ppermute | solution.py:53
  13.5 8.0 %collective-permute-start.8 = (bf16[64,1024]{1,0:T(8,128)(2,1)S(1)}, bf16[64,1024]{1,0:T(8,128)(2,1)S(1)}, u32[]{:S(2)}, u32[]{:S(2)}) collective-permute-start(bf16[64,1024]{1,0:T(8,128)(2,1)S(1)} %collective-permute-done.4.refs_3_), channel_id=1, source_target_pairs={{0,2},{4,0},{8,4},{12,8},{14,12},{10,14},{6,10},{2,6},{1,3},{5,1},... | collective-permute-start | bytes 393224 | tf_op jit(solution)/shard_map/ppermute | solution.py:53
  14.5 12.0 %collective-permute-start.7 = (bf16[64,1152]{1,0:T(8,128)(2,1)S(1)}, bf16[64,1152]{1,0:T(8,128)(2,1)S(1)}, u32[]{:S(2)}, u32[]{:S(2)}) collective-permute-start(bf16[64,1152]{1,0:T(8,128)(2,1)S(1)} %collective-permute-done.3.refs_2_), channel_id=1, source_target_pairs={{0,2},{4,0},{8,4},{12,8},{14,12},{10,14},{6,10},{2,6},{1,3},{5,1},... | collective-permute-start | bytes 442376 | tf_op jit(solution)/shard_map/ppermute | solution.py:53
  16.8 11.6 %collective-permute-start.9 = (bf16[64,1152]{1,0:T(8,128)(2,1)S(1)}, bf16[64,1152]{1,0:T(8,128)(2,1)S(1)}, u32[]{:S(2)}, u32[]{:S(2)}) collective-permute-start(bf16[64,1152]{1,0:T(8,128)(2,1)S(1)} %collective-permute-done.5.refs_0_), channel_id=1, source_target_pairs={{0,4},{4,8},{8,12},{12,14},{14,10},{10,6},{6,2},{2,0},{1,5},{5,9},... | collective-permute-start | bytes 442376 | tf_op jit(solution)/shard_map/ppermute | solution.py:53
  24.6 12.1 %collective-permute-start.10 = (bf16[64,1024]{1,0:T(8,128)(2,1)S(1)}, bf16[64,1024]{1,0:T(8,128)(2,1)S(1)}, u32[]{:S(2)}, u32[]{:S(2)}) collective-permute-start(bf16[64,1024]{1,0:T(8,128)(2,1)S(1)} %collective-permute-done.6.refs_1_), channel_id=1, source_target_pairs={{0,4},{4,8},{8,12},{12,14},{14,10},{10,6},{6,2},{2,0},{1,5},{5,9},... | collective-permute-start | bytes 393224 | tf_op jit(solution)/shard_map/ppermute | solution.py:53
  26.5 10.3 %collective-permute-start.11 = (bf16[64,1152]{1,0:T(8,128)(2,1)S(1)}, bf16[64,1152]{1,0:T(8,128)(2,1)S(1)}, u32[]{:S(2)}, u32[]{:S(2)}) collective-permute-start(bf16[64,1152]{1,0:T(8,128)(2,1)S(1)} %collective-permute-done.7.refs_2_), channel_id=1, source_target_pairs={{0,2},{4,0},{8,4},{12,8},{14,12},{10,14},{6,10},{2,6},{1,3},{5,1},... | collective-permute-start | bytes 442376 | tf_op jit(solution)/shard_map/ppermute | solution.py:53
  38.5 6.9 %collective-permute-start.19 = (bf16[64,1024]{1,0:T(8,128)(2,1)S(1)}, bf16[64,1024]{1,0:T(8,128)(2,1)S(1)}, u32[]{:S(2)}, u32[]{:S(2)}) collective-permute-start(bf16[64,1024]{1,0:T(8,128)(2,1)S(1)} %get-tuple-element.78), channel_id=1, source_target_pairs={{0,2},{4,0},{8,4},{12,8},{14,12},{10,14},{6,10},{2,6},{1,3},{5,1},... | collective-permute-start | bytes 393224 | tf_op jit(solution)/shard_map/ppermute | solution.py:53
  40.7 8.3 %collective-permute-start.16 = (bf16[64,1024]{1,0:T(8,128)(2,1)S(1)}, bf16[64,1024]{1,0:T(8,128)(2,1)S(1)}, u32[]{:S(2)}, u32[]{:S(2)}) collective-permute-start(bf16[64,1024]{1,0:T(8,128)(2,1)S(1)} %shard_map.111), channel_id=1, source_target_pairs={{0,4},{4,8},{8,12},{12,14},{14,10},{10,6},{6,2},{2,0},{1,5},{5,9},... | collective-permute-start | bytes 393224 | tf_op jit(solution)/shard_map/ppermute | solution.py:53
  49.2 8.5 %collective-permute-start.27 = (bf16[64,1024]{1,0:T(8,128)(2,1)S(1)}, bf16[64,1024]{1,0:T(8,128)(2,1)S(1)}, u32[]{:S(2)}, u32[]{:S(2)}) collective-permute-start(bf16[64,1024]{1,0:T(8,128)(2,1)S(1)} %shard_map.120), channel_id=1, source_target_pairs={{0,2},{4,0},{8,4},{12,8},{14,12},{10,14},{6,10},{2,6},{1,3},{5,1},... | collective-permute-start | bytes 393224 | tf_op jit(solution)/shard_map/ppermute | solution.py:53
  55.6 7.7 %collective-permute-start.24 = (bf16[64,1024]{1,0:T(8,128)(2,1)S(1)}, bf16[64,1024]{1,0:T(8,128)(2,1)S(1)}, u32[]{:S(2)}, u32[]{:S(2)}) collective-permute-start(bf16[64,1024]{1,0:T(8,128)(2,1)S(1)} %shard_map.118), channel_id=1, source_target_pairs={{0,4},{4,8},{8,12},{12,14},{14,10},{10,6},{6,2},{2,0},{1,5},{5,9},... | collective-permute-start | bytes 393224 | tf_op jit(solution)/shard_map/ppermute | solution.py:53
  67.1 7.0 %collective-permute-start.30 = (bf16[64,1024]{1,0:T(8,128)(2,1)S(1)}, bf16[64,1024]{1,0:T(8,128)(2,1)S(1)}, u32[]{:S(2)}, u32[]{:S(2)}) collective-permute-start(bf16[64,1024]{1,0:T(8,128)(2,1)S(1)} %collective-permute-done.29.refs_4_), channel_id=1, source_target_pairs={{0,4},{4,8},{8,12},{12,14},{14,10},{10,6},{6,2},{2,0},{1,5},{5,9},... | collective-permute-start | bytes 393224 | tf_op jit(solution)/shard_map/ppermute | solution.py:53
  106.6 6.8 %collective-permute-start.53 = (bf16[64,1024]{1,0:T(8,128)(2,1)S(1)}, bf16[64,1024]{1,0:T(8,128)(2,1)S(1)}, u32[]{:S(2)}, u32[]{:S(2)}) collective-permute-start(bf16[64,1024]{1,0:T(8,128)(2,1)S(1)} %get-tuple-element.121), channel_id=1, source_target_pairs={{0,4},{4,8},{8,12},{12,14},{14,10},{10,6},{6,2},{2,0},{1,5},{5,9},... | collective-permute-start | bytes 393224 | tf_op jit(solution)/shard_map/ppermute | solution.py:53
  107.1 6.9 %collective-permute-start.47 = (bf16[64,1024]{1,0:T(8,128)(2,1)S(1)}, bf16[64,1024]{1,0:T(8,128)(2,1)S(1)}, u32[]{:S(2)}, u32[]{:S(2)}) collective-permute-start(bf16[64,1024]{1,0:T(8,128)(2,1)S(1)} %shard_map.135), channel_id=1, source_target_pairs={{0,4},{4,8},{8,12},{12,14},{14,10},{10,6},{6,2},{2,0},{1,5},{5,9},... | collective-permute-start | bytes 393224 | tf_op jit(solution)/shard_map/ppermute | solution.py:53
  108.9 6.9 %collective-permute-start.57 = (bf16[64,1024]{1,0:T(8,128)(2,1)S(1)}, bf16[64,1024]{1,0:T(8,128)(2,1)S(1)}, u32[]{:S(2)}, u32[]{:S(2)}) collective-permute-start(bf16[64,1024]{1,0:T(8,128)(2,1)S(1)} %shard_map.142), channel_id=1, source_target_pairs={{0,2},{4,0},{8,4},{12,8},{14,12},{10,14},{6,10},{2,6},{1,3},{5,1},... | collective-permute-start | bytes 393224 | tf_op jit(solution)/shard_map/ppermute | solution.py:53
  109.3 6.9 %collective-permute-start.60 = (bf16[8,1274]{1,0:T(8,128)(2,1)S(1)}, bf16[8,1274]{1,0:T(8,128)(2,1)S(1)}, u32[]{:S(2)}, u32[]{:S(2)}) collective-permute-start(bf16[8,1274]{1,0:T(8,128)(2,1)S(1)} %pad_maximum_fusion.1), channel_id=1, source_target_pairs={{0,1},{1,0},{2,3},{3,2},{4,5},{5,4},{6,7},{7,6},{8,9},{9,8},{10,11... | collective-permute-start | bytes 61160 | tf_op jit(solution)/shard_map/ppermute | solution.py:425
  111.8 6.9 %collective-permute-start.51 = (bf16[64,1024]{1,0:T(8,128)(2,1)S(1)}, bf16[64,1024]{1,0:T(8,128)(2,1)S(1)}, u32[]{:S(2)}, u32[]{:S(2)}) collective-permute-start(bf16[64,1024]{1,0:T(8,128)(2,1)S(1)} %shard_map.138), channel_id=1, source_target_pairs={{0,2},{4,0},{8,4},{12,8},{14,12},{10,14},{6,10},{2,6},{1,3},{5,1},... | collective-permute-start | bytes 393224 | tf_op jit(solution)/shard_map/ppermute | solution.py:53
  113.4 6.9 %collective-permute-start.54 = (bf16[64,1024]{1,0:T(8,128)(2,1)S(1)}, bf16[64,1024]{1,0:T(8,128)(2,1)S(1)}, u32[]{:S(2)}, u32[]{:S(2)}) collective-permute-start(bf16[64,1024]{1,0:T(8,128)(2,1)S(1)} %shard_map.140), channel_id=1, source_target_pairs={{0,4},{4,8},{8,12},{12,14},{14,10},{10,6},{6,2},{2,0},{1,5},{5,9},... | collective-permute-start | bytes 393224 | tf_op jit(solution)/shard_map/ppermute | solution.py:53
  114.0 8.0 %collective-permute-start.48 = (bf16[64,1024]{1,0:T(8,128)(2,1)S(1)}, bf16[64,1024]{1,0:T(8,128)(2,1)S(1)}, u32[]{:S(2)}, u32[]{:S(2)}) collective-permute-start(bf16[64,1024]{1,0:T(8,128)(2,1)S(1)} %shard_map.136), channel_id=1, source_target_pairs={{0,4},{4,8},{8,12},{12,14},{14,10},{10,6},{6,2},{2,0},{1,5},{5,9},... | collective-permute-start | bytes 393224 | tf_op jit(solution)/shard_map/ppermute | solution.py:53
  115.8 6.9 %collective-permute-start.58 = (bf16[64,1024]{1,0:T(8,128)(2,1)S(1)}, bf16[64,1024]{1,0:T(8,128)(2,1)S(1)}, u32[]{:S(2)}, u32[]{:S(2)}) collective-permute-start(bf16[64,1024]{1,0:T(8,128)(2,1)S(1)} %shard_map.143), channel_id=1, source_target_pairs={{0,2},{4,0},{8,4},{12,8},{14,12},{10,14},{6,10},{2,6},{1,3},{5,1},... | collective-permute-start | bytes 393224 | tf_op jit(solution)/shard_map/ppermute | solution.py:53
  118.7 8.1 %collective-permute-start.52 = (bf16[64,1024]{1,0:T(8,128)(2,1)S(1)}, bf16[64,1024]{1,0:T(8,128)(2,1)S(1)}, u32[]{:S(2)}, u32[]{:S(2)}) collective-permute-start(bf16[64,1024]{1,0:T(8,128)(2,1)S(1)} %shard_map.139), channel_id=1, source_target_pairs={{0,2},{4,0},{8,4},{12,8},{14,12},{10,14},{6,10},{2,6},{1,3},{5,1},... | collective-permute-start | bytes 393224 | tf_op jit(solution)/shard_map/ppermute | solution.py:53
  (40 other events, 359.0 us)

commit v8 on v7

--- a/solution.py
+++ b/solution.py
@@ -23,7 +23,7 @@
     return lax.dot_general(left, right, (((1,), (1,)), ((), ())), preferred_element_type=F32)
 
 
-def call(kernel, outs, *args, flops=0):
+def call(kernel, outs, *args, flops=0, scratch=()):
     args = [pltpu.with_memory_space_constraint(a, pltpu.VMEM) for a in args]
     size = sum(a.size * a.dtype.itemsize for a in args)
     return pl.pallas_call(
@@ -31,8 +31,24 @@
         out_shape=[pltpu.VMEM(shape, dtype) for shape, dtype in outs],
         in_specs=[pl.BlockSpec(memory_space=pltpu.VMEM)] * len(args),
         out_specs=[pl.BlockSpec(memory_space=pltpu.VMEM)] * len(outs),
+        scratch_shapes=list(scratch),
         compiler_params=pltpu.CompilerParams(vmem_limit_bytes=VMEM_LIMIT),
         cost_estimate=pl.CostEstimate(flops=flops, bytes_accessed=size, transcendentals=0),
+    )(*args)
+
+
+def after(value, guard):
+    def kernel(value_ref, guard_ref, out_ref):
+        pass
+
+    args = [pltpu.with_memory_space_constraint(a, pltpu.VMEM) for a in (value, guard)]
+    return pl.pallas_call(
+        kernel,
+        out_shape=pltpu.VMEM(value.shape, value.dtype),
+        in_specs=[pl.BlockSpec(memory_space=pltpu.VMEM)] * 2,
+        out_specs=pl.BlockSpec(memory_space=pltpu.VMEM),
+        input_output_aliases={0: 0},
+        compiler_params=pltpu.CompilerParams(vmem_limit_bytes=VMEM_LIMIT),
     )(*args)
 
 
@@ -62,11 +78,15 @@
             there = jnp.where(there < self.half, 2 * there, 2 * (count - 1 - there) + 1)
         return there
 
-    def gather(self, top, bottom, use):
+    def gather(self, top, bottom, use, waits=None):
         top_left = top_right = top
         bottom_left = bottom_right = bottom
         use((0,), (top, bottom))
         for step in range(1, self.half):
+            if waits and step in waits:
+                *others, last = waits[step]()
+                top_right = after(top_right, others[0]) if others else top_right
+                bottom_left = after(bottom_left, last)
             top_left = self.send(top_left, 1)
             top_right = self.send(top_right, -1)
             bottom_left = self.send(bottom_left, 1)
@@ -345,7 +365,7 @@
     def forward(distances):
         blocks = tokens_at[distances]
         rows = mid * len(blocks)
-        guards = [saved_at[d][0] for d in ((0,), (-1, 1))] if distances == (ring.half,) else []
+        guards = [saved_at[1 - ring.half, ring.half - 1][0]] if distances == (ring.half,) else []
         result = call(
             functools.partial(forward_kernel, len(blocks), len(guards)),
             [((rows, local_experts * hidden_dim), BF16)] * 2 + part_outs(distances),
@@ -358,9 +378,18 @@
         saved_at[distances] = result[:2]
         keep_parts(part_at, distances, result[2:])
 
-    ring.gather(top, bottom, hold)
+    def early(*done):
+        for distances in done:
+            forward(distances)
+        return [saved_at[d][0] for d in done]
+
+    waits = {}
+    if packed is not None and ring.half > 3:
+        waits = {2: lambda: [packed], 3: lambda: early((0,), (-1, 1))}
+    ring.gather(top, bottom, hold, waits)
     for distances in tokens_at:
-        forward(distances)
+        if distances not in saved_at:
+            forward(distances)
     gain = norm_gain.reshape(1, feature_dim)
     half_shape = (mid, feature_dim)
     moe_top, moe_bottom = [
@@ -412,13 +441,13 @@
     target_rows = targets.reshape(expert_count, -1).astype(F32)
     logit_grad = (LOSS_SCALE * (jax.nn.sigmoid(logits) - target_rows)).astype(BF16)
     pooled_grad = dot_t(logit_grad, class_head)
-    distance = 1
-    while distance < expert_count:
-        pairs = [(e, e ^ distance) for e in range(expert_count)]
+    span = 2
+    for masks in ([1], list(range(span, expert_count, span))):
         mine = pooled_grad.astype(BF16)
-        other = lax.ppermute(mine, "expert", pairs)
-        pooled_grad = mine.astype(F32) + other.astype(F32)
-        distance *= 2
+        pooled_grad = mine.astype(F32)
+        for mask in masks:
+            pairs = [(e, e ^ mask) for e in range(expert_count)]
+            pooled_grad = pooled_grad + lax.ppermute(mine, "expert", pairs).astype(F32)
 
     both = jnp.concatenate([pooled, logit_grad], axis=1)
     if group_count == 2:
@@ -433,18 +462,22 @@
     )
 
     def backward_kernel(distances, residual_ref, inv_ref, gate_save, up_save, *refs):
-        grad_ref, gain_ref, wide_ref, down_ref, *outs = refs
-        residual, inv_rms = residual_ref[...], inv_ref[:, :1]
-        cube = inv_rms * inv_rms * inv_rms
-        parts = []
+        grad_ref, gain_ref, wide_ref, down_ref, *outs = refs[:-1]
+        rows_ref = refs[-1]
+        piece = 32
         for i, k in enumerate(distances):
-            rows = slice(i * rows_here, (i + 1) * rows_here)
             scaled = gain_ref[...] * grad_ref[pl.ds(ring.device_at(k), 1), :] / rows_here
-            slope = cube[rows] * jnp.mean(residual[rows] * scaled, axis=-1, keepdims=True)
-            parts.append(inv_rms[rows] * scaled - residual[rows] * slope)
-        resid_grad = jnp.concatenate(parts, axis=0) if len(parts) > 1 else parts[0]
-        down_back = dot(resid_grad.astype(BF16), down_ref[...])
-        total = resid_grad if distances == (0,) else None
+            for begin in range(0, rows_here, piece):
+                rows = pl.ds(i * rows_here + begin, piece)
+                residual, inv_rms = residual_ref[rows, :], inv_ref[rows, :1]
+                cube = inv_rms * inv_rms * inv_rms
+                slope = cube * jnp.mean(residual * scaled, axis=-1, keepdims=True)
+                resid_grad = inv_rms * scaled - residual * slope
+                rows_ref[rows, :] = resid_grad.astype(BF16)
+                if distances == (0,):
+                    outs[begin // mid][pl.ds(begin % mid, piece), :] = resid_grad
+        down_back = dot(rows_ref[...], down_ref[...])
+        total = None
         for local in range(local_experts):
             cols = slice(local * hidden_dim, (local + 1) * hidden_dim)
             gate_grad = (down_back[:, cols] * gate_save[:, cols].astype(F32)).astype(BF16)
@@ -453,7 +486,8 @@
             term = dot(grads, wide_ref[pl.ds(local * pair_dim, pair_dim), :])
             total = term if total is None else total + term
         for i, out in enumerate(outs):
-            out[...] = total[i * mid : (i + 1) * mid].astype(out.dtype)
+            part = total[i * mid : (i + 1) * mid]
+            out[...] = out[...] + part if distances == (0,) else part.astype(out.dtype)
 
     wide_t, down_t = transposed(wide), transposed(down)
     back_at = {}
@@ -469,6 +503,7 @@
             wide_t,
             down_t,
             flops=flops * len(distances),
+            scratch=[pltpu.VMEM((rows_here * len(distances), feature_dim), BF16)],
         )
         keep_parts(back_at, distances, result)
 

time: 129 us -> 131 us (1.016)
  waiting for transfers between devices: 31.7 us -> 36.5 us
  starting transfers between devices: 68.8 us -> 65.2 us
    ppermute x56, waiting for transfers between devices: 28.2 us -> 31.9 us  [send(): return lax.ppermute(value, 'expert', pairs)]
    ppermute x3 -> x4, starting transfers between devices: 7.49 us -> 4.96 us  [body(): pooled_grad = pooled_grad + lax.ppermute(mine, 'expert', pairs).astype(F32)]
    ppermute x3 -> x4, waiting for transfers between devices: 3.51 us -> 4.52 us  [body(): pooled_grad = pooled_grad + lax.ppermute(mine, 'expert', pairs).astype(F32)]
  transfers between devices with their start and end apart: 61 -> 62, of which waited for: 25 -> 30; matrix products, arithmetic and copies ran while one was open for 1% -> 1% of each run, Pallas kernels for 17% -> 16%
where the time goes in v8:
time: 131 us; the launch traced here: 130 us
  starting transfers between devices  65.2 us (50%)
  waiting for transfers between devices  36.5 us (28%)
  Pallas kernels  25.9 us (20%)
  matrix products  1.71 us (1%)
    ppermute x56, starting transfers between devices, send(): return lax.ppermute(value, 'expert', pairs)  59.7 us
    ppermute x56, waiting for transfers between devices, send(): return lax.ppermute(value, 'expert', pairs)  31.9 us
    pallas_call x39, Pallas kernels, call(): pl.pallas_call(kernel, out_shape=[pltpu.VMEM(shape, dtype) for shape, dty...  21.5 us
    ppermute x4, starting transfers between devices, body(): pooled_grad = pooled_grad + lax.ppermute(mine, 'expert', pairs).astype(F32)  4.96 us
    ppermute x4, waiting for transfers between devices, body(): pooled_grad = pooled_grad + lax.ppermute(mine, 'expert', pairs).astype(F32)  4.52 us
  transfers between devices with their start and end apart: 62, of which 30 were waited for; matrix products, arithmetic and copies ran while one was open for 1% of the time, Pallas kernels for 16%

profile of v8, /device:TPU:0, one launch (start us, length us, event | category | flops | bytes accessed | tf_op | source)
XLA Modules:
  0.0 130.5 jit_solution(17168974413860986507)
XLA Ops:
  0.6 1.9 %shard_map.104 = (bf16[64,1152]{1,0:T(8,128)(2,1)S(1)}, bf16[64,1024]{1,0:T(8,128)(2,1)S(1)}, bf16[3200,384]{1,0:T(8,128)(2,1)S(1)}) custom-call(s32[8,128]{1,0:T(8,128)} %bitcast.19, f32[8,128]{1,0:T(8,128)} %bitcast.20, bf16[128,1024]{1,0:T(8,128)(2,1)} %refs_2_.2, bf16[2,512,384]{2,1,0:T(8,128)(2,1)} %refs_0_.1, bf16[2,512,384]{2,1,0:T(8,128)(2,1)} %refs_1_.1, ...), custom_call_target="tpu_custom_call" | custom-call | tf_op jit(solution)/shard_map/pallas_call | solution.py:218
  3.1 2.6 %collective-permute-start.1 = (bf16[64,1152]{1,0:T(8,128)(2,1)S(1)}, bf16[64,1152]{1,0:T(8,128)(2,1)S(1)}, u32[]{:S(2)}, u32[]{:S(2)}) collective-permute-start(bf16[64,1152]{1,0:T(8,128)(2,1)S(1)} %get-tuple-element.64.refs_0_), channel_id=1, source_target_pairs={{0,4},{4,8},{8,12},{12,14},{14,10},{10,6},{6,2},{2,0},{1,5},{5,9},... | collective-permute-start | bytes 442376 | tf_op jit(solution)/shard_map/ppermute | solution.py:69
  5.7 1.9 %collective-permute-start.4 = (bf16[64,1024]{1,0:T(8,128)(2,1)S(1)}, bf16[64,1024]{1,0:T(8,128)(2,1)S(1)}, u32[]{:S(2)}, u32[]{:S(2)}) collective-permute-start(bf16[64,1024]{1,0:T(8,128)(2,1)S(1)} %get-tuple-element.65.refs_1_), channel_id=1, source_target_pairs={{0,2},{4,0},{8,4},{12,8},{14,12},{10,14},{6,10},{2,6},{1,3},{5,1},... | collective-permute-start | bytes 393224 | tf_op jit(solution)/shard_map/ppermute | solution.py:69
  7.7 2.4 %collective-permute-done.1.refs_0_ = bf16[64,1152]{1,0:T(8,128)(2,1)S(1)} collective-permute-done((bf16[64,1152]{1,0:T(8,128)(2,1)S(1)}, bf16[64,1152]{1,0:T(8,128)(2,1)S(1)}, u32[]{:S(2)}, u32[]{:S(2)}) %collective-permute-start.1) | collective-permute-done | bytes 147488 | tf_op jit(solution)/shard_map/ppermute | solution.py:69
  10.1 1.8 %collective-permute-start.5 = (bf16[64,1152]{1,0:T(8,128)(2,1)S(1)}, bf16[64,1152]{1,0:T(8,128)(2,1)S(1)}, u32[]{:S(2)}, u32[]{:S(2)}) collective-permute-start(bf16[64,1152]{1,0:T(8,128)(2,1)S(1)} %collective-permute-done.1.refs_0_), channel_id=1, source_target_pairs={{0,4},{4,8},{8,12},{12,14},{14,10},{10,6},{6,2},{2,0},{1,5},{5,9},... | collective-permute-start | bytes 442376 | tf_op jit(solution)/shard_map/ppermute | solution.py:69
  12.4 2.0 %collective-permute-start.2 = (bf16[64,1024]{1,0:T(8,128)(2,1)S(1)}, bf16[64,1024]{1,0:T(8,128)(2,1)S(1)}, u32[]{:S(2)}, u32[]{:S(2)}) collective-permute-start(bf16[64,1024]{1,0:T(8,128)(2,1)S(1)} %get-tuple-element.65.refs_1_), channel_id=1, source_target_pairs={{0,4},{4,8},{8,12},{12,14},{14,10},{10,6},{6,2},{2,0},{1,5},{5,9},... | collective-permute-start | bytes 393224 | tf_op jit(solution)/shard_map/ppermute | solution.py:69
  15.1 3.4 %collective-permute-done.2.refs_1_ = bf16[64,1024]{1,0:T(8,128)(2,1)S(1)} collective-permute-done((bf16[64,1024]{1,0:T(8,128)(2,1)S(1)}, bf16[64,1024]{1,0:T(8,128)(2,1)S(1)}, u32[]{:S(2)}, u32[]{:S(2)}) %collective-permute-start.2) | collective-permute-done | bytes 131104 | tf_op jit(solution)/shard_map/ppermute | solution.py:69
  18.5 1.9 %collective-permute-done.8.refs_3_ = bf16[64,1024]{1,0:T(8,128)(2,1)S(1)} collective-permute-done((bf16[64,1024]{1,0:T(8,128)(2,1)S(1)}, bf16[64,1024]{1,0:T(8,128)(2,1)S(1)}, u32[]{:S(2)}, u32[]{:S(2)}) %collective-permute-start.8) | collective-permute-done | bytes 131104 | tf_op jit(solution)/shard_map/ppermute | solution.py:69
  20.7 1.7 %collective-permute-start.9 = (bf16[64,1152]{1,0:T(8,128)(2,1)S(1)}, bf16[64,1152]{1,0:T(8,128)(2,1)S(1)}, u32[]{:S(2)}, u32[]{:S(2)}) collective-permute-start(bf16[64,1152]{1,0:T(8,128)(2,1)S(1)} %collective-permute-done.5.refs_0_), channel_id=1, source_target_pairs={{0,4},{4,8},{8,12},{12,14},{14,10},{10,6},{6,2},{2,0},{1,5},{5,9},... | collective-permute-start | bytes 442376 | tf_op jit(solution)/shard_map/ppermute | solution.py:69
  24.1 1.7 %shard_map.105 = (bf16[1024,1536]{1,0:T(8,128)(2,1)S(1)}, bf16[768,1024]{1,0:T(8,128)(2,1)S(1)}) custom-call(bf16[2,512,384]{2,1,0:T(8,128)(2,1)} %refs_0_.1, bf16[2,512,384]{2,1,0:T(8,128)(2,1)} %refs_1_.1, bf16[2,192,1024]{2,1,0:T(8,128)(2,1)} %refs_2_.3, bf16[3200,384]{1,0:T(8,128)(2,1)S(1)} %collective-permute-done.refs_3_.guard_ref), custom_call_target="tpu_custom_call" | custom-call | tf_op jit(solution)/shard_map/pallas_call | solution.py:273
  27.5 1.7 %shard_map.107 = (bf16[256,768]{1,0:T(8,128)(2,1)S(1)}, bf16[256,768]{1,0:T(8,128)(2,1)S(1)}, f32[64,1024]{1,0:T(8,128)S(1)}, f32[64,1024]{1,0:T(8,128)S(1)}, f3...) custom-call(bf16[64,1152]{1,0:T(8,128)(2,1)S(1)} %collective-permute-done.1.refs_0_, ...), custom_call_target="tpu_custom_call" | custom-call | flops 1207959552 | bytes 5275648 | tf_op jit(solution)/shard_map/pallas_call | solution.py:29
  34.2 1.7 %shard_map.112 = (bf16[256,768]{1,0:T(8,128)(2,1)S(1)}, bf16[256,768]{1,0:T(8,128)(2,1)S(1)}, bf16[64,1024]{1,0:T(8,128)(2,1)S(1)}, f32[64,1024]{1,0:T(8,128)S(1...) custom-call(bf16[64,1152]{1,0:T(8,128)(2,1)S(1)} %collective-permute-done.9.refs_0_, ...), custom_call_target="tpu_custom_call" | custom-call | flops 1207959552 | bytes 5275648 | tf_op jit(solution)/shard_map/pallas_call | solution.py:29
  46.9 1.7 %shard_map.109 = (bf16[256,768]{1,0:T(8,128)(2,1)S(1)}, bf16[256,768]{1,0:T(8,128)(2,1)S(1)}, f32[64,1024]{1,0:T(8,128)S(1)}, f32[64,1024]{1,0:T(8,128)S(1)}, f3...) custom-call(bf16[64,1152]{1,0:T(8,128)(2,1)S(1)} %collective-permute-done.5.refs_0_, ...), custom_call_target="tpu_custom_call" | custom-call | flops 1207959552 | bytes 5275648 | tf_op jit(solution)/shard_map/pallas_call | solution.py:29
  55.8 2.7 %collective-permute-done.17.arrived_ref = bf16[64,1024]{1,0:T(8,128)(2,1)S(1)} collective-permute-done((bf16[64,1024]{1,0:T(8,128)(2,1)S(1)}, bf16[64,1024]{1,0:T(8,128)(2,1)S(1)}, u32[]{:S(2)}, u32[]{:S(2)}) %collective-permute-start.17) | collective-permute-done | bytes 131104 | tf_op jit(solution)/shard_map/ppermute | solution.py:69
  62.1 2.9 %collective-permute-done.18.refs_1_ = bf16[64,1024]{1,0:T(8,128)(2,1)S(1)} collective-permute-done((bf16[64,1024]{1,0:T(8,128)(2,1)S(1)}, bf16[64,1024]{1,0:T(8,128)(2,1)S(1)}, u32[]{:S(2)}, u32[]{:S(2)}) %collective-permute-start.18) | collective-permute-done | bytes 131104 | tf_op jit(solution)/shard_map/ppermute | solution.py:69
  68.3 1.8 %collective-permute-start.37 = (bf16[64,1024]{1,0:T(8,128)(2,1)S(1)}, bf16[64,1024]{1,0:T(8,128)(2,1)S(1)}, u32[]{:S(2)}, u32[]{:S(2)}) collective-permute-start(bf16[64,1024]{1,0:T(8,128)(2,1)S(1)} %shard_map.125.refs_3_), channel_id=1, source_target_pairs={{0,4},{4,8},{8,12},{12,14},{14,10},{10,6},{6,2},{2,0},{1,5},{5,9},... | collective-permute-start | bytes 393224 | tf_op jit(solution)/shard_map/ppermute | solution.py:69
  71.2 1.7 %collective-permute-start.30 = (bf16[64,1024]{1,0:T(8,128)(2,1)S(1)}, bf16[64,1024]{1,0:T(8,128)(2,1)S(1)}, u32[]{:S(2)}, u32[]{:S(2)}) collective-permute-start(bf16[64,1024]{1,0:T(8,128)(2,1)S(1)} %collective-permute-done.29.refs_4_), channel_id=1, source_target_pairs={{0,4},{4,8},{8,12},{12,14},{14,10},{10,6},{6,2},{2,0},{1,5},{5,9},... | collective-permute-start | bytes 393224 | tf_op jit(solution)/shard_map/ppermute | solution.py:69
  87.3 1.7 %collective-permute-done.36.refs_3_ = bf16[64,1024]{1,0:T(8,128)(2,1)S(1)} collective-permute-done((bf16[64,1024]{1,0:T(8,128)(2,1)S(1)}, bf16[64,1024]{1,0:T(8,128)(2,1)S(1)}, u32[]{:S(2)}, u32[]{:S(2)}) %collective-permute-start.36) | collective-permute-done | bytes 131104 | tf_op jit(solution)/shard_map/ppermute | solution.py:69
  90.2 3.5 %collective-permute-done.43 = bf16[8,1024]{1,0:T(8,128)(2,1)S(1)} collective-permute-done((bf16[8,1024]{1,0:T(8,128)(2,1)S(1)}, bf16[8,1024]{1,0:T(8,128)(2,1)S(1)}, u32[]{:S(2)}, u32[]{:S(2)}) %collective-permute-start.43) | collective-permute-done | bytes 16416 | tf_op jit(solution)/shard_map/ppermute | solution.py:450
  93.7 2.4 %collective-permute-start.46 = (bf16[8,1024]{1,0:T(8,128)(2,1)S(1)}, bf16[8,1024]{1,0:T(8,128)(2,1)S(1)}, u32[]{:S(2)}, u32[]{:S(2)}) collective-permute-start(bf16[8,1024]{1,0:T(8,128)(2,1)S(1)} %add_convert_fusion), channel_id=1, source_target_pairs={{0,12},{2,14},{4,8},{6,10},{8,4},{10,6},{12,0},{14,2},{1,13},{3,15... | collective-permute-start | bytes 49160 | tf_op jit(solution)/shard_map/ppermute | solution.py:450
  96.2 1.9 %collective-permute-start.44 = (bf16[8,1024]{1,0:T(8,128)(2,1)S(1)}, bf16[8,1024]{1,0:T(8,128)(2,1)S(1)}, u32[]{:S(2)}, u32[]{:S(2)}) collective-permute-start(bf16[8,1024]{1,0:T(8,128)(2,1)S(1)} %add_convert_fusion), channel_id=1, source_target_pairs={{0,4},{2,6},{4,0},{6,2},{8,12},{10,14},{12,8},{14,10},{1,5},{3,7},... | collective-permute-start | bytes 49160 | tf_op jit(solution)/shard_map/ppermute | solution.py:450
  104.6 2.4 %shard_map.136 = (bf16[64,1024]{1,0:T(8,128)(2,1)S(1)}, f32[64,1024]{1,0:T(8,128)S(1)}, f32[64,1024]{1,0:T(8,128)S(1)}, bf16[64,1024]{1,0:T(8,128)(2,1)S(1)}) custom-call(f32[256,1024]{1,0:T(8,128)S(1)} %get-tuple-element.106.residual_ref, f32[256,128]{1,0:T(8,128)S(1)} %get-tuple-element.107.inv_ref, ...), custom_call_target="tpu_custom_call" | custom-call | flops 1207959552 | bytes 6721536 | tf_op jit(solution)/shard_map/pallas_call | solution.py:29
  111.3 2.5 %shard_map.135 = (f32[64,1024]{1,0:T(8,128)S(1)}, f32[64,1024]{1,0:T(8,128)S(1)}, f32[64,1024]{1,0:T(8,128)S(1)}, f32[64,1024]{1,0:T(8,128)S(1)}) custom-call(f32[256,1024]{1,0:T(8,128)S(1)} %get-tuple-element.101.residual_ref, f32[256,128]{1,0:T(8,128)S(1)} %get-tuple-element.102.inv_ref, bf16[256,768]{1,0:T(8,128)(2,1)S(1)} %get-tuple-element.103.gate_save, ...), custom_call_target="tpu_custom_call" | custom-call | flops 1207959552 | bytes 6721536 | tf_op jit(solution)/shard_map/pallas_call | solution.py:29
  118.2 2.5 %shard_map.134 = (f32[64,1024]{1,0:T(8,128)S(1)}, f32[64,1024]{1,0:T(8,128)S(1)}, f32[64,1024]{1,0:T(8,128)S(1)}, f32[64,1024]{1,0:T(8,128)S(1)}) custom-call(f32[256,1024]{1,0:T(8,128)S(1)} %get-tuple-element.97.residual_ref, f32[256,128]{1,0:T(8,128)S(1)} %get-tuple-element.98.inv_ref, bf16[256,768]{1,0:T(8,128)(2,1)S(1)} %get-tuple-element.72.guard_ref.gate_save, ...), custom_call_target="tpu_custom_call" | custom-call | flops 1207959552 | bytes 6721536 | tf_op jit(solution)/shard_map/pallas_call | solution.py:29
  (163 shorter events, 76.8 us)
Async XLA Ops:
  2.6 19.9 %collective-permute-start = (bf16[3200,384]{1,0:T(8,128)(2,1)S(1)}, bf16[3200,384]{1,0:T(8,128)(2,1)S(1)}, u32[]{:S(2)}, u32[]{:S(2)}) collective-permute-start(bf16[3200,384]{1,0:T(8,128)(2,1)S(1)} %get-tuple-element.66), channel_id=1, source_target_pairs={{0,1},{1,0},{2,3},{3,2},{4,5},{5,4},{6,7},{7,6},{8,9},{9,8},{10,11... | collective-permute-start | bytes 7372808 | tf_op jit(solution)/shard_map/ppermute | solution.py:313
  3.1 7.0 %collective-permute-start.1 = (bf16[64,1152]{1,0:T(8,128)(2,1)S(1)}, bf16[64,1152]{1,0:T(8,128)(2,1)S(1)}, u32[]{:S(2)}, u32[]{:S(2)}) collective-permute-start(bf16[64,1152]{1,0:T(8,128)(2,1)S(1)} %get-tuple-element.64.refs_0_), channel_id=1, source_target_pairs={{0,4},{4,8},{8,12},{12,14},{14,10},{10,6},{6,2},{2,0},{1,5},{5,9},... | collective-permute-start | bytes 442376 | tf_op jit(solution)/shard_map/ppermute | solution.py:69
  5.7 6.7 %collective-permute-start.3 = (bf16[64,1152]{1,0:T(8,128)(2,1)S(1)}, bf16[64,1152]{1,0:T(8,128)(2,1)S(1)}, u32[]{:S(2)}, u32[]{:S(2)}) collective-permute-start(bf16[64,1152]{1,0:T(8,128)(2,1)S(1)} %get-tuple-element.64.refs_0_), channel_id=1, source_target_pairs={{0,2},{4,0},{8,4},{12,8},{14,12},{10,14},{6,10},{2,6},{1,3},{5,1},... | collective-permute-start | bytes 442376 | tf_op jit(solution)/shard_map/ppermute | solution.py:69
  5.7 9.2 %collective-permute-start.4 = (bf16[64,1024]{1,0:T(8,128)(2,1)S(1)}, bf16[64,1024]{1,0:T(8,128)(2,1)S(1)}, u32[]{:S(2)}, u32[]{:S(2)}) collective-permute-start(bf16[64,1024]{1,0:T(8,128)(2,1)S(1)} %get-tuple-element.65.refs_1_), channel_id=1, source_target_pairs={{0,2},{4,0},{8,4},{12,8},{14,12},{10,14},{6,10},{2,6},{1,3},{5,1},... | collective-permute-start | bytes 393224 | tf_op jit(solution)/shard_map/ppermute | solution.py:69
  10.1 10.6 %collective-permute-start.5 = (bf16[64,1152]{1,0:T(8,128)(2,1)S(1)}, bf16[64,1152]{1,0:T(8,128)(2,1)S(1)}, u32[]{:S(2)}, u32[]{:S(2)}) collective-permute-start(bf16[64,1152]{1,0:T(8,128)(2,1)S(1)} %collective-permute-done.1.refs_0_), channel_id=1, source_target_pairs={{0,4},{4,8},{8,12},{12,14},{14,10},{10,6},{6,2},{2,0},{1,5},{5,9},... | collective-permute-start | bytes 442376 | tf_op jit(solution)/shard_map/ppermute | solution.py:69
  12.4 10.0 %collective-permute-start.7 = (bf16[64,1152]{1,0:T(8,128)(2,1)S(1)}, bf16[64,1152]{1,0:T(8,128)(2,1)S(1)}, u32[]{:S(2)}, u32[]{:S(2)}) collective-permute-start(bf16[64,1152]{1,0:T(8,128)(2,1)S(1)} %collective-permute-done.3.refs_2_), channel_id=1, source_target_pairs={{0,2},{4,0},{8,4},{12,8},{14,12},{10,14},{6,10},{2,6},{1,3},{5,1},... | collective-permute-start | bytes 442376 | tf_op jit(solution)/shard_map/ppermute | solution.py:69
  20.4 12.0 %collective-permute-start.12 = (bf16[64,1024]{1,0:T(8,128)(2,1)S(1)}, bf16[64,1024]{1,0:T(8,128)(2,1)S(1)}, u32[]{:S(2)}, u32[]{:S(2)}) collective-permute-start(bf16[64,1024]{1,0:T(8,128)(2,1)S(1)} %collective-permute-done.8.refs_3_), channel_id=1, source_target_pairs={{0,2},{4,0},{8,4},{12,8},{14,12},{10,14},{6,10},{2,6},{1,3},{5,1},... | collective-permute-start | bytes 393224 | tf_op jit(solution)/shard_map/ppermute | solution.py:69
  20.7 10.1 %collective-permute-start.9 = (bf16[64,1152]{1,0:T(8,128)(2,1)S(1)}, bf16[64,1152]{1,0:T(8,128)(2,1)S(1)}, u32[]{:S(2)}, u32[]{:S(2)}) collective-permute-start(bf16[64,1152]{1,0:T(8,128)(2,1)S(1)} %collective-permute-done.5.refs_0_), channel_id=1, source_target_pairs={{0,4},{4,8},{8,12},{12,14},{14,10},{10,6},{6,2},{2,0},{1,5},{5,9},... | collective-permute-start | bytes 442376 | tf_op jit(solution)/shard_map/ppermute | solution.py:69
  22.5 6.7 %collective-permute-start.6 = (bf16[64,1024]{1,0:T(8,128)(2,1)S(1)}, bf16[64,1024]{1,0:T(8,128)(2,1)S(1)}, u32[]{:S(2)}, u32[]{:S(2)}) collective-permute-start(bf16[64,1024]{1,0:T(8,128)(2,1)S(1)} %shard_map.108), channel_id=1, source_target_pairs={{0,4},{4,8},{8,12},{12,14},{14,10},{10,6},{6,2},{2,0},{1,5},{5,9},... | collective-permute-start | bytes 393224 | tf_op jit(solution)/shard_map/ppermute | solution.py:69
  40.6 8.0 %collective-permute-start.19 = (bf16[64,1024]{1,0:T(8,128)(2,1)S(1)}, bf16[64,1024]{1,0:T(8,128)(2,1)S(1)}, u32[]{:S(2)}, u32[]{:S(2)}) collective-permute-start(bf16[64,1024]{1,0:T(8,128)(2,1)S(1)} %get-tuple-element.79), channel_id=1, source_target_pairs={{0,2},{4,0},{8,4},{12,8},{14,12},{10,14},{6,10},{2,6},{1,3},{5,1},... | collective-permute-start | bytes 393224 | tf_op jit(solution)/shard_map/ppermute | solution.py:69
  41.0 8.4 %collective-permute-start.22 = (bf16[64,1024]{1,0:T(8,128)(2,1)S(1)}, bf16[64,1024]{1,0:T(8,128)(2,1)S(1)}, u32[]{:S(2)}, u32[]{:S(2)}) collective-permute-start(bf16[64,1024]{1,0:T(8,128)(2,1)S(1)} %get-tuple-element.83), channel_id=1, source_target_pairs={{0,4},{4,8},{8,12},{12,14},{14,10},{10,6},{6,2},{2,0},{1,5},{5,9},... | collective-permute-start | bytes 393224 | tf_op jit(solution)/shard_map/ppermute | solution.py:69
  50.8 7.7 %collective-permute-start.17 = (bf16[64,1024]{1,0:T(8,128)(2,1)S(1)}, bf16[64,1024]{1,0:T(8,128)(2,1)S(1)}, u32[]{:S(2)}, u32[]{:S(2)}) collective-permute-start(bf16[64,1024]{1,0:T(8,128)(2,1)S(1)} %shard_map.115), channel_id=1, source_target_pairs={{0,4},{4,8},{8,12},{12,14},{14,10},{10,6},{6,2},{2,0},{1,5},{5,9},... | collective-permute-start | bytes 393224 | tf_op jit(solution)/shard_map/ppermute | solution.py:69
  52.5 9.0 %collective-permute-start.27 = (bf16[64,1024]{1,0:T(8,128)(2,1)S(1)}, bf16[64,1024]{1,0:T(8,128)(2,1)S(1)}, u32[]{:S(2)}, u32[]{:S(2)}) collective-permute-start(bf16[64,1024]{1,0:T(8,128)(2,1)S(1)} %shard_map.123), channel_id=1, source_target_pairs={{0,2},{4,0},{8,4},{12,8},{14,12},{10,14},{6,10},{2,6},{1,3},{5,1},... | collective-permute-start | bytes 393224 | tf_op jit(solution)/shard_map/ppermute | solution.py:69
  54.2 7.9 %collective-permute-start.21 = (bf16[64,1024]{1,0:T(8,128)(2,1)S(1)}, bf16[64,1024]{1,0:T(8,128)(2,1)S(1)}, u32[]{:S(2)}, u32[]{:S(2)}) collective-permute-start(bf16[64,1024]{1,0:T(8,128)(2,1)S(1)} %shard_map.118), channel_id=1, source_target_pairs={{0,2},{4,0},{8,4},{12,8},{14,12},{10,14},{6,10},{2,6},{1,3},{5,1},... | collective-permute-start | bytes 393224 | tf_op jit(solution)/shard_map/ppermute | solution.py:69
  107.0 6.8 %collective-permute-start.51 = (bf16[64,1024]{1,0:T(8,128)(2,1)S(1)}, bf16[64,1024]{1,0:T(8,128)(2,1)S(1)}, u32[]{:S(2)}, u32[]{:S(2)}) collective-permute-start(bf16[64,1024]{1,0:T(8,128)(2,1)S(1)} %get-tuple-element.117), channel_id=1, source_target_pairs={{0,2},{4,0},{8,4},{12,8},{14,12},{10,14},{6,10},{2,6},{1,3},{5,1},... | collective-permute-start | bytes 393224 | tf_op jit(solution)/shard_map/ppermute | solution.py:69
  108.1 6.8 %collective-permute-start.54 = (bf16[64,1024]{1,0:T(8,128)(2,1)S(1)}, bf16[64,1024]{1,0:T(8,128)(2,1)S(1)}, u32[]{:S(2)}, u32[]{:S(2)}) collective-permute-start(bf16[64,1024]{1,0:T(8,128)(2,1)S(1)} %get-tuple-element.121), channel_id=1, source_target_pairs={{0,4},{4,8},{8,12},{12,14},{14,10},{10,6},{6,2},{2,0},{1,5},{5,9},... | collective-permute-start | bytes 393224 | tf_op jit(solution)/shard_map/ppermute | solution.py:69
  109.1 6.9 %collective-permute-start.48 = (bf16[64,1024]{1,0:T(8,128)(2,1)S(1)}, bf16[64,1024]{1,0:T(8,128)(2,1)S(1)}, u32[]{:S(2)}, u32[]{:S(2)}) collective-permute-start(bf16[64,1024]{1,0:T(8,128)(2,1)S(1)} %shard_map.138), channel_id=1, source_target_pairs={{0,4},{4,8},{8,12},{12,14},{14,10},{10,6},{6,2},{2,0},{1,5},{5,9},... | collective-permute-start | bytes 393224 | tf_op jit(solution)/shard_map/ppermute | solution.py:69
  110.1 6.9 %collective-permute-start.58 = (bf16[64,1024]{1,0:T(8,128)(2,1)S(1)}, bf16[64,1024]{1,0:T(8,128)(2,1)S(1)}, u32[]{:S(2)}, u32[]{:S(2)}) collective-permute-start(bf16[64,1024]{1,0:T(8,128)(2,1)S(1)} %shard_map.145), channel_id=1, source_target_pairs={{0,2},{4,0},{8,4},{12,8},{14,12},{10,14},{6,10},{2,6},{1,3},{5,1},... | collective-permute-start | bytes 393224 | tf_op jit(solution)/shard_map/ppermute | solution.py:69
  111.3 6.9 %collective-permute-start.61 = (bf16[8,1274]{1,0:T(8,128)(2,1)S(1)}, bf16[8,1274]{1,0:T(8,128)(2,1)S(1)}, u32[]{:S(2)}, u32[]{:S(2)}) collective-permute-start(bf16[8,1274]{1,0:T(8,128)(2,1)S(1)} %pad_maximum_fusion.1), channel_id=1, source_target_pairs={{0,1},{1,0},{2,3},{3,2},{4,5},{5,4},{6,7},{7,6},{8,9},{9,8},{10,11... | collective-permute-start | bytes 61160 | tf_op jit(solution)/shard_map/ppermute | solution.py:454
  113.8 6.9 %collective-permute-start.52 = (bf16[64,1024]{1,0:T(8,128)(2,1)S(1)}, bf16[64,1024]{1,0:T(8,128)(2,1)S(1)}, u32[]{:S(2)}, u32[]{:S(2)}) collective-permute-start(bf16[64,1024]{1,0:T(8,128)(2,1)S(1)} %shard_map.141), channel_id=1, source_target_pairs={{0,2},{4,0},{8,4},{12,8},{14,12},{10,14},{6,10},{2,6},{1,3},{5,1},... | collective-permute-start | bytes 393224 | tf_op jit(solution)/shard_map/ppermute | solution.py:69
  114.9 6.9 %collective-permute-start.55 = (bf16[64,1024]{1,0:T(8,128)(2,1)S(1)}, bf16[64,1024]{1,0:T(8,128)(2,1)S(1)}, u32[]{:S(2)}, u32[]{:S(2)}) collective-permute-start(bf16[64,1024]{1,0:T(8,128)(2,1)S(1)} %shard_map.143), channel_id=1, source_target_pairs={{0,4},{4,8},{8,12},{12,14},{14,10},{10,6},{6,2},{2,0},{1,5},{5,9},... | collective-permute-start | bytes 393224 | tf_op jit(solution)/shard_map/ppermute | solution.py:69
  116.0 7.4 %collective-permute-start.49 = (bf16[64,1024]{1,0:T(8,128)(2,1)S(1)}, bf16[64,1024]{1,0:T(8,128)(2,1)S(1)}, u32[]{:S(2)}, u32[]{:S(2)}) collective-permute-start(bf16[64,1024]{1,0:T(8,128)(2,1)S(1)} %shard_map.139), channel_id=1, source_target_pairs={{0,4},{4,8},{8,12},{12,14},{14,10},{10,6},{6,2},{2,0},{1,5},{5,9},... | collective-permute-start | bytes 393224 | tf_op jit(solution)/shard_map/ppermute | solution.py:69
  117.0 7.5 %collective-permute-start.59 = (bf16[64,1024]{1,0:T(8,128)(2,1)S(1)}, bf16[64,1024]{1,0:T(8,128)(2,1)S(1)}, u32[]{:S(2)}, u32[]{:S(2)}) collective-permute-start(bf16[64,1024]{1,0:T(8,128)(2,1)S(1)} %shard_map.146), channel_id=1, source_target_pairs={{0,2},{4,0},{8,4},{12,8},{14,12},{10,14},{6,10},{2,6},{1,3},{5,1},... | collective-permute-start | bytes 393224 | tf_op jit(solution)/shard_map/ppermute | solution.py:69
  120.7 7.6 %collective-permute-start.53 = (bf16[64,1024]{1,0:T(8,128)(2,1)S(1)}, bf16[64,1024]{1,0:T(8,128)(2,1)S(1)}, u32[]{:S(2)}, u32[]{:S(2)}) collective-permute-start(bf16[64,1024]{1,0:T(8,128)(2,1)S(1)} %shard_map.142), channel_id=1, source_target_pairs={{0,2},{4,0},{8,4},{12,8},{14,12},{10,14},{6,10},{2,6},{1,3},{5,1},... | collective-permute-start | bytes 393224 | tf_op jit(solution)/shard_map/ppermute | solution.py:69
  (41 other events, 363.3 us)

commit v9 on v7

--- a/solution.py
+++ b/solution.py
@@ -87,6 +87,29 @@
                 bottom_left = self.send(add(parts[step - 1][1], bottom_left), 1)
                 top_right = self.send(add(parts[1 - step][0], top_right), -1)
         return (top_left, top_right), (bottom_left, bottom_right)
+
+    def scatter_whole(self, ends, parts):
+        mid = ends[0].shape[0]
+
+        def half_kernel(first, block_ref, arrived_ref, out_ref):
+            added, kept = pl.ds(first, mid), pl.ds(mid - first, mid)
+            out_ref[added, :] = (block_ref[added, :] + arrived_ref[...].astype(F32)).astype(BF16)
+            out_ref[kept, :] = block_ref[kept, :].astype(BF16)
+
+        left, right = self.send(ends[0], 1), self.send(ends[1], -1)
+        for step in range(self.half - 1, 0, -1):
+            blocks = parts[step], parts[-step]
+            if step == self.half - 1:
+                halves = [functools.partial(half_kernel, first) for first in (0, mid)]
+                shape = blocks[0].shape
+                left, right = [
+                    call(kernel, [(shape, BF16)], block, arrived)[0]
+                    for kernel, block, arrived in zip(halves, blocks, (left, right))
+                ]
+            else:
+                left, right = add(blocks[0], left), add(blocks[1], right)
+            left, right = self.send(left, 1), self.send(right, -1)
+        return left, right
 
     def part_types(self, distances):
         types = []
@@ -300,14 +323,14 @@
     def rows_of(refs):
         return jnp.concatenate([ref[...] for ref in refs], axis=0) if len(refs) > 1 else refs[0][...]
 
-    def forward_kernel(count, guards, *refs):
+    def forward_kernel(count, *refs):
         token_refs, (wide_ref, down_ref) = refs[:count], refs[count : count + 2]
-        outs = refs[count + 2 + guards :]
+        outs = refs[count + 2 :]
         x = rows_of([ref.at[:, :feature_dim] for ref in token_refs])
         weights = jnp.concatenate([ref[:, feature_dim:] for ref in token_refs[::2]], axis=0).astype(F32)
         lane = lax.broadcasted_iota(jnp.int32, weights.shape, 1)
         quarter = LANES // 4
-        total = None
+        hidden = []
         for local in range(local_experts):
             expert = lax.axis_index("expert") * local_experts + local
             scales = []
@@ -324,9 +347,8 @@
             cols = pl.ds(local * hidden_dim, hidden_dim)
             outs[0][:, cols] = (up_act * slope).astype(BF16)
             outs[1][:, cols] = silu.astype(BF16)
-            hidden = (silu * up_act).astype(BF16)
-            term = dot(hidden, down_ref[cols, :])
-            total = term if total is None else total + term
+            hidden.append((silu * up_act).astype(BF16))
+        total = dot(jnp.concatenate(hidden, axis=1), down_ref[...])
         for i, out in enumerate(outs[2:]):
             out[...] = total[i * mid : (i + 1) * mid].astype(out.dtype)
 
@@ -345,14 +367,12 @@
     def forward(distances):
         blocks = tokens_at[distances]
         rows = mid * len(blocks)
-        guards = [saved_at[d][0] for d in ((0,), (-1, 1))] if distances == (ring.half,) else []
         result = call(
-            functools.partial(forward_kernel, len(blocks), len(guards)),
+            functools.partial(forward_kernel, len(blocks)),
             [((rows, local_experts * hidden_dim), BF16)] * 2 + part_outs(distances),
             *blocks,
             wide,
             down,
-            *guards,
             flops=flops * rows // rows_here,
         )
         saved_at[distances] = result[:2]
@@ -412,13 +432,13 @@
     target_rows = targets.reshape(expert_count, -1).astype(F32)
     logit_grad = (LOSS_SCALE * (jax.nn.sigmoid(logits) - target_rows)).astype(BF16)
     pooled_grad = dot_t(logit_grad, class_head)
-    distance = 1
-    while distance < expert_count:
-        pairs = [(e, e ^ distance) for e in range(expert_count)]
+    span = 2
+    for masks in ([1], list(range(span, expert_count, span))):
         mine = pooled_grad.astype(BF16)
-        other = lax.ppermute(mine, "expert", pairs)
-        pooled_grad = mine.astype(F32) + other.astype(F32)
-        distance *= 2
+        pooled_grad = mine.astype(F32)
+        for mask in masks:
+            pairs = [(e, e ^ mask) for e in range(expert_count)]
+            pooled_grad = pooled_grad + lax.ppermute(mine, "expert", pairs).astype(F32)
 
     both = jnp.concatenate([pooled, logit_grad], axis=1)
     if group_count == 2:
@@ -444,24 +464,29 @@
             parts.append(inv_rms[rows] * scaled - residual[rows] * slope)
         resid_grad = jnp.concatenate(parts, axis=0) if len(parts) > 1 else parts[0]
         down_back = dot(resid_grad.astype(BF16), down_ref[...])
-        total = resid_grad if distances == (0,) else None
+        grads = []
         for local in range(local_experts):
             cols = slice(local * hidden_dim, (local + 1) * hidden_dim)
-            gate_grad = (down_back[:, cols] * gate_save[:, cols].astype(F32)).astype(BF16)
-            up_grad = (down_back[:, cols] * up_save[:, cols].astype(F32)).astype(BF16)
-            grads = jnp.concatenate([gate_grad, up_grad], axis=1)
-            term = dot(grads, wide_ref[pl.ds(local * pair_dim, pair_dim), :])
-            total = term if total is None else total + term
+            for save in (gate_save, up_save):
+                grads.append((down_back[:, cols] * save[:, cols].astype(F32)).astype(BF16))
+        total = dot(jnp.concatenate(grads, axis=1), wide_ref[...])
+        if distances == (0,):
+            total = total + resid_grad
+        rows = total.shape[0] // len(outs)
         for i, out in enumerate(outs):
-            out[...] = total[i * mid : (i + 1) * mid].astype(out.dtype)
+            out[...] = total[i * rows : (i + 1) * rows].astype(out.dtype)
 
     wide_t, down_t = transposed(wide), transposed(down)
     back_at = {}
 
     def backward(distances):
+        if distances == (ring.half,):
+            outs = [((mid, feature_dim), BF16)] * 2
+        else:
+            outs = [(block, F32)] * len(distances)
         result = call(
             functools.partial(backward_kernel, distances),
-            part_outs(distances),
+            outs,
             *norm_at[distances],
             *saved_at[distances],
             pooled_grad,
@@ -470,18 +495,20 @@
             down_t,
             flops=flops * len(distances),
         )
-        keep_parts(back_at, distances, result)
+        if distances == (ring.half,):
+            back_at["ends"] = result
+        else:
+            back_at.update(zip(distances, result))
 
     for distances in reversed(list(tokens_at)):
         backward(distances)
-    (top_left, top_right), (bottom_left, bottom_right) = ring.scatter(back_at)
     token_grad = pl.pallas_call(
         sum_kernel,
         out_shape=jax.ShapeDtypeStruct(block, BF16),
-        in_specs=[pl.BlockSpec(memory_space=pltpu.VMEM)] * 6,
+        in_specs=[pl.BlockSpec(memory_space=pltpu.VMEM)] * 3,
         out_specs=pl.BlockSpec(memory_space=pltpu.VMEM),
         compiler_params=pltpu.CompilerParams(vmem_limit_bytes=VMEM_LIMIT),
-    )(back_at[0][0], top_left, top_right, back_at[0][1], bottom_left, bottom_right)
+    )(back_at[0], *ring.scatter_whole(back_at["ends"], back_at))
     return (token_grad, head_grad)
 
 

time: 129 us -> 125 us (0.969)
  starting transfers between devices: 68.8 us -> 61.2 us
  waiting for transfers between devices: 31.7 us -> 39.1 us
  Pallas kernels: 25.7 us -> 21.8 us
    ppermute x56 -> x50, waiting for transfers between devices: 28.2 us -> 35 us  [send(): return lax.ppermute(value, 'expert', pairs)]
    ppermute x56 -> x50, starting transfers between devices: 60.7 us -> 56.1 us  [send(): return lax.ppermute(value, 'expert', pairs)]
    pallas_call x39 -> x35, Pallas kernels: 21.2 us -> 17.3 us  [call(): pl.pallas_call(kernel, out_shape=[pltpu.VMEM(shape, dtype) for shape, dty...]
    ppermute x3 -> x4, starting transfers between devices: 7.49 us -> 4.66 us  [body(): pooled_grad = pooled_grad + lax.ppermute(mine, 'expert', pairs).astype(F32)]
    ppermute x3 -> x4, waiting for transfers between devices: 3.51 us -> 4.13 us  [body(): pooled_grad = pooled_grad + lax.ppermute(mine, 'expert', pairs).astype(F32)]
  transfers between devices with their start and end apart: 61 -> 56, of which waited for: 25 -> 27; matrix products, arithmetic and copies ran while one was open for 1% -> 1% of each run, Pallas kernels for 17% -> 14%
where the time goes in v9:
time: 125 us
  starting transfers between devices  61.2 us (49%)
  waiting for transfers between devices  39.1 us (31%)
  Pallas kernels  21.8 us (17%)
  matrix products  1.71 us (1%)
    ppermute x50, starting transfers between devices, send(): return lax.ppermute(value, 'expert', pairs)  56.1 us
    ppermute x50, waiting for transfers between devices, send(): return lax.ppermute(value, 'expert', pairs)  35 us
    pallas_call x35, Pallas kernels, call(): pl.pallas_call(kernel, out_shape=[pltpu.VMEM(shape, dtype) for shape, dty...  17.3 us
    ppermute x4, starting transfers between devices, body(): pooled_grad = pooled_grad + lax.ppermute(mine, 'expert', pairs).astype(F32)  4.66 us
    ppermute x4, waiting for transfers between devices, body(): pooled_grad = pooled_grad + lax.ppermute(mine, 'expert', pairs).astype(F32)  4.13 us
  transfers between devices with their start and end apart: 56, of which 27 were waited for; matrix products, arithmetic and copies ran while one was open for 1% of the time, Pallas kernels for 14%

profile of v9, /device:TPU:0, one launch (start us, length us, event | category | flops | bytes accessed | tf_op | source)
XLA Modules:
  0.0 124.9 jit_solution(977836747149060538)
XLA Ops:
  0.6 1.9 %shard_map.104 = (bf16[64,1152]{1,0:T(8,128)(2,1)S(1)}, bf16[64,1024]{1,0:T(8,128)(2,1)S(1)}, bf16[3200,384]{1,0:T(8,128)(2,1)S(1)}) custom-call(s32[8,128]{1,0:T(8,128)} %bitcast.19, f32[8,128]{1,0:T(8,128)} %bitcast.20, bf16[128,1024]{1,0:T(8,128)(2,1)} %refs_2_.2, bf16[2,512,384]{2,1,0:T(8,128)(2,1)} %refs_0_.1, bf16[2,512,384]{2,1,0:T(8,128)(2,1)} %refs_1_.1, ...), custom_call_target="tpu_custom_call" | custom-call | tf_op jit(solution)/shard_map/pallas_call | solution.py:221
  3.1 2.6 %collective-permute-start.1 = (bf16[64,1152]{1,0:T(8,128)(2,1)S(1)}, bf16[64,1152]{1,0:T(8,128)(2,1)S(1)}, u32[]{:S(2)}, u32[]{:S(2)}) collective-permute-start(bf16[64,1152]{1,0:T(8,128)(2,1)S(1)} %get-tuple-element.56.refs_0_), channel_id=1, source_target_pairs={{0,4},{4,8},{8,12},{12,14},{14,10},{10,6},{6,2},{2,0},{1,5},{5,9},... | collective-permute-start | bytes 442376 | tf_op jit(solution)/shard_map/ppermute | solution.py:53
  5.7 4.4 %collective-permute-done.1.refs_0_ = bf16[64,1152]{1,0:T(8,128)(2,1)S(1)} collective-permute-done((bf16[64,1152]{1,0:T(8,128)(2,1)S(1)}, bf16[64,1152]{1,0:T(8,128)(2,1)S(1)}, u32[]{:S(2)}, u32[]{:S(2)}) %collective-permute-start.1) | collective-permute-done | bytes 147488 | tf_op jit(solution)/shard_map/ppermute | solution.py:53
  10.1 1.8 %collective-permute-start.5 = (bf16[64,1152]{1,0:T(8,128)(2,1)S(1)}, bf16[64,1152]{1,0:T(8,128)(2,1)S(1)}, u32[]{:S(2)}, u32[]{:S(2)}) collective-permute-start(bf16[64,1152]{1,0:T(8,128)(2,1)S(1)} %collective-permute-done.1.refs_0_), channel_id=1, source_target_pairs={{0,4},{4,8},{8,12},{12,14},{14,10},{10,6},{6,2},{2,0},{1,5},{5,9},... | collective-permute-start | bytes 442376 | tf_op jit(solution)/shard_map/ppermute | solution.py:53
  14.2 2.0 %collective-permute-done.5.refs_0_ = bf16[64,1152]{1,0:T(8,128)(2,1)S(1)} collective-permute-done((bf16[64,1152]{1,0:T(8,128)(2,1)S(1)}, bf16[64,1152]{1,0:T(8,128)(2,1)S(1)}, u32[]{:S(2)}, u32[]{:S(2)}) %collective-permute-start.5) | collective-permute-done | bytes 147488 | tf_op jit(solution)/shard_map/ppermute | solution.py:53
  16.2 2.5 %collective-permute-start.9 = (bf16[64,1152]{1,0:T(8,128)(2,1)S(1)}, bf16[64,1152]{1,0:T(8,128)(2,1)S(1)}, u32[]{:S(2)}, u32[]{:S(2)}) collective-permute-start(bf16[64,1152]{1,0:T(8,128)(2,1)S(1)} %collective-permute-done.5.refs_0_), channel_id=1, source_target_pairs={{0,4},{4,8},{8,12},{12,14},{14,10},{10,6},{6,2},{2,0},{1,5},{5,9},... | collective-permute-start | bytes 442376 | tf_op jit(solution)/shard_map/ppermute | solution.py:53
  18.7 2.6 %collective-permute-done.3.refs_2_ = bf16[64,1152]{1,0:T(8,128)(2,1)S(1)} collective-permute-done((bf16[64,1152]{1,0:T(8,128)(2,1)S(1)}, bf16[64,1152]{1,0:T(8,128)(2,1)S(1)}, u32[]{:S(2)}, u32[]{:S(2)}) %collective-permute-start.3) | collective-permute-done | bytes 147488 | tf_op jit(solution)/shard_map/ppermute | solution.py:53
  21.4 1.9 %collective-permute-start.6 = (bf16[64,1024]{1,0:T(8,128)(2,1)S(1)}, bf16[64,1024]{1,0:T(8,128)(2,1)S(1)}, u32[]{:S(2)}, u32[]{:S(2)}) collective-permute-start(bf16[64,1024]{1,0:T(8,128)(2,1)S(1)} %collective-permute-done.2.refs_1_), channel_id=1, source_target_pairs={{0,4},{4,8},{8,12},{12,14},{14,10},{10,6},{6,2},{2,0},{1,5},{5,9},... | collective-permute-start | bytes 393224 | tf_op jit(solution)/shard_map/ppermute | solution.py:53
  25.3 2.6 %collective-permute-done.7.refs_2_ = bf16[64,1152]{1,0:T(8,128)(2,1)S(1)} collective-permute-done((bf16[64,1152]{1,0:T(8,128)(2,1)S(1)}, bf16[64,1152]{1,0:T(8,128)(2,1)S(1)}, u32[]{:S(2)}, u32[]{:S(2)}) %collective-permute-start.7) | collective-permute-done | bytes 147488 | tf_op jit(solution)/shard_map/ppermute | solution.py:53
  28.1 1.8 %collective-permute-start.10 = (bf16[64,1024]{1,0:T(8,128)(2,1)S(1)}, bf16[64,1024]{1,0:T(8,128)(2,1)S(1)}, u32[]{:S(2)}, u32[]{:S(2)}) collective-permute-start(bf16[64,1024]{1,0:T(8,128)(2,1)S(1)} %collective-permute-done.6.refs_1_), channel_id=1, source_target_pairs={{0,4},{4,8},{8,12},{12,14},{14,10},{10,6},{6,2},{2,0},{1,5},{5,9},... | collective-permute-start | bytes 393224 | tf_op jit(solution)/shard_map/ppermute | solution.py:53
  43.5 2.1 %collective-permute-start.23 = (bf16[64,1024]{1,0:T(8,128)(2,1)S(1)}, bf16[64,1024]{1,0:T(8,128)(2,1)S(1)}, u32[]{:S(2)}, u32[]{:S(2)}) collective-permute-start(bf16[64,1024]{1,0:T(8,128)(2,1)S(1)} %shard_map.117), channel_id=1, source_target_pairs={{0,4},{4,8},{8,12},{12,14},{14,10},{10,6},{6,2},{2,0},{1,5},{5,9},... | collective-permute-start | bytes 393224 | tf_op jit(solution)/shard_map/ppermute | solution.py:53
  52.2 2.5 %collective-permute-start.18 = (bf16[64,1024]{1,0:T(8,128)(2,1)S(1)}, bf16[64,1024]{1,0:T(8,128)(2,1)S(1)}, u32[]{:S(2)}, u32[]{:S(2)}) collective-permute-start(bf16[64,1024]{1,0:T(8,128)(2,1)S(1)} %shard_map.113), channel_id=1, source_target_pairs={{0,4},{4,8},{8,12},{12,14},{14,10},{10,6},{6,2},{2,0},{1,5},{5,9},... | collective-permute-start | bytes 393224 | tf_op jit(solution)/shard_map/ppermute | solution.py:53
  58.5 2.5 %collective-permute-start.29 = (bf16[64,1024]{1,0:T(8,128)(2,1)S(1)}, bf16[64,1024]{1,0:T(8,128)(2,1)S(1)}, u32[]{:S(2)}, u32[]{:S(2)}) collective-permute-start(bf16[64,1024]{1,0:T(8,128)(2,1)S(1)} %shard_map.116.refs_2_), channel_id=1, source_target_pairs={{0,4},{4,8},{8,12},{12,14},{14,10},{10,6},{6,2},{2,0},{1,5},{5,9},... | collective-permute-start | bytes 393224 | tf_op jit(solution)/shard_map/ppermute | solution.py:53
  64.7 2.3 %collective-permute-start.30 = (bf16[64,1024]{1,0:T(8,128)(2,1)S(1)}, bf16[64,1024]{1,0:T(8,128)(2,1)S(1)}, u32[]{:S(2)}, u32[]{:S(2)}) collective-permute-start(bf16[64,1024]{1,0:T(8,128)(2,1)S(1)} %collective-permute-done.29.refs_4_), channel_id=1, source_target_pairs={{0,4},{4,8},{8,12},{12,14},{14,10},{10,6},{6,2},{2,0},{1,5},{5,9},... | collective-permute-start | bytes 393224 | tf_op jit(solution)/shard_map/ppermute | solution.py:53
  68.4 2.5 %collective-permute-done.40.refs_6_ = bf16[64,1024]{1,0:T(8,128)(2,1)S(1)} collective-permute-done((bf16[64,1024]{1,0:T(8,128)(2,1)S(1)}, bf16[64,1024]{1,0:T(8,128)(2,1)S(1)}, u32[]{:S(2)}, u32[]{:S(2)}) %collective-permute-start.40) | collective-permute-done | bytes 131104 | tf_op jit(solution)/shard_map/ppermute | solution.py:53
  71.2 2.1 %collective-permute-start.38 = (bf16[64,1024]{1,0:T(8,128)(2,1)S(1)}, bf16[64,1024]{1,0:T(8,128)(2,1)S(1)}, u32[]{:S(2)}, u32[]{:S(2)}) collective-permute-start(bf16[64,1024]{1,0:T(8,128)(2,1)S(1)} %collective-permute-done.37.refs_5_), channel_id=1, source_target_pairs={{0,4},{4,8},{8,12},{12,14},{14,10},{10,6},{6,2},{2,0},{1,5},{5,9},... | collective-permute-start | bytes 393224 | tf_op jit(solution)/shard_map/ppermute | solution.py:53
  73.2 2.0 %collective-permute-start.31 = (bf16[64,1024]{1,0:T(8,128)(2,1)S(1)}, bf16[64,1024]{1,0:T(8,128)(2,1)S(1)}, u32[]{:S(2)}, u32[]{:S(2)}) collective-permute-start(bf16[64,1024]{1,0:T(8,128)(2,1)S(1)} %collective-permute-done.30.refs_4_), channel_id=1, source_target_pairs={{0,4},{4,8},{8,12},{12,14},{14,10},{10,6},{6,2},{2,0},{1,5},{5,9},... | collective-permute-start | bytes 393224 | tf_op jit(solution)/shard_map/ppermute | solution.py:53
  78.4 1.8 %collective-permute-start.32 = (bf16[64,1024]{1,0:T(8,128)(2,1)S(1)}, bf16[64,1024]{1,0:T(8,128)(2,1)S(1)}, u32[]{:S(2)}, u32[]{:S(2)}) collective-permute-start(bf16[64,1024]{1,0:T(8,128)(2,1)S(1)} %collective-permute-done.31.refs_4_), channel_id=1, source_target_pairs={{0,4},{4,8},{8,12},{12,14},{14,10},{10,6},{6,2},{2,0},{1,5},{5,9},... | collective-permute-start | bytes 393224 | tf_op jit(solution)/shard_map/ppermute | solution.py:53
  83.4 1.9 %collective-permute-done.36.refs_3_ = bf16[64,1024]{1,0:T(8,128)(2,1)S(1)} collective-permute-done((bf16[64,1024]{1,0:T(8,128)(2,1)S(1)}, bf16[64,1024]{1,0:T(8,128)(2,1)S(1)}, u32[]{:S(2)}, u32[]{:S(2)}) %collective-permute-start.36) | collective-permute-done | bytes 131104 | tf_op jit(solution)/shard_map/ppermute | solution.py:53
  86.1 3.6 %collective-permute-done.43 = bf16[8,1024]{1,0:T(8,128)(2,1)S(1)} collective-permute-done((bf16[8,1024]{1,0:T(8,128)(2,1)S(1)}, bf16[8,1024]{1,0:T(8,128)(2,1)S(1)}, u32[]{:S(2)}, u32[]{:S(2)}) %collective-permute-start.43) | collective-permute-done | bytes 16416 | tf_op jit(solution)/shard_map/ppermute | solution.py:441
  89.7 2.0 %collective-permute-start.46 = (bf16[8,1024]{1,0:T(8,128)(2,1)S(1)}, bf16[8,1024]{1,0:T(8,128)(2,1)S(1)}, u32[]{:S(2)}, u32[]{:S(2)}) collective-permute-start(bf16[8,1024]{1,0:T(8,128)(2,1)S(1)} %add_convert_fusion), channel_id=1, source_target_pairs={{0,12},{2,14},{4,8},{6,10},{8,4},{10,6},{12,0},{14,2},{1,13},{3,15... | collective-permute-start | bytes 49160 | tf_op jit(solution)/shard_map/ppermute | solution.py:441
  106.5 2.6 %collective-permute-done.52.arrived_ref = bf16[128,1024]{1,0:T(8,128)(2,1)S(1)} collective-permute-done((bf16[128,1024]{1,0:T(8,128)(2,1)S(1)}, bf16[128,1024]{1,0:T(8,128)(2,1)S(1)}, u32[]{:S(2)}, u32[]{:S(2)}) %collective-permute-start.52) | collective-permute-done | bytes 262176 | tf_op jit(solution)/shard_map/ppermute | solution.py:53
  113.0 3.1 %collective-permute-done.53.arrived_ref = bf16[128,1024]{1,0:T(8,128)(2,1)S(1)} collective-permute-done((bf16[128,1024]{1,0:T(8,128)(2,1)S(1)}, bf16[128,1024]{1,0:T(8,128)(2,1)S(1)}, u32[]{:S(2)}, u32[]{:S(2)}) %collective-permute-start.53) | collective-permute-done | bytes 262176 | tf_op jit(solution)/shard_map/ppermute | solution.py:53
  120.7 1.9 %collective-permute-done.54.refs_2_ = bf16[128,1024]{1,0:T(8,128)(2,1)S(1)} collective-permute-done((bf16[128,1024]{1,0:T(8,128)(2,1)S(1)}, bf16[128,1024]{1,0:T(8,128)(2,1)S(1)}, u32[]{:S(2)}, u32[]{:S(2)}) %collective-permute-start.54) | collective-permute-done | bytes 262176 | tf_op jit(solution)/shard_map/ppermute | solution.py:53
  (141 shorter events, 66.9 us)
Async XLA Ops:
  2.6 27.4 %collective-permute-start = (bf16[3200,384]{1,0:T(8,128)(2,1)S(1)}, bf16[3200,384]{1,0:T(8,128)(2,1)S(1)}, u32[]{:S(2)}, u32[]{:S(2)}) collective-permute-start(bf16[3200,384]{1,0:T(8,128)(2,1)S(1)} %get-tuple-element.58), channel_id=1, source_target_pairs={{0,1},{1,0},{2,3},{3,2},{4,5},{5,4},{6,7},{7,6},{8,9},{9,8},{10,11... | collective-permute-start | bytes 7372808 | tf_op jit(solution)/shard_map/ppermute | solution.py:316
  3.1 7.0 %collective-permute-start.1 = (bf16[64,1152]{1,0:T(8,128)(2,1)S(1)}, bf16[64,1152]{1,0:T(8,128)(2,1)S(1)}, u32[]{:S(2)}, u32[]{:S(2)}) collective-permute-start(bf16[64,1152]{1,0:T(8,128)(2,1)S(1)} %get-tuple-element.56.refs_0_), channel_id=1, source_target_pairs={{0,4},{4,8},{8,12},{12,14},{14,10},{10,6},{6,2},{2,0},{1,5},{5,9},... | collective-permute-start | bytes 442376 | tf_op jit(solution)/shard_map/ppermute | solution.py:53
  11.9 6.8 %collective-permute-start.8 = (bf16[64,1024]{1,0:T(8,128)(2,1)S(1)}, bf16[64,1024]{1,0:T(8,128)(2,1)S(1)}, u32[]{:S(2)}, u32[]{:S(2)}) collective-permute-start(bf16[64,1024]{1,0:T(8,128)(2,1)S(1)} %collective-permute-done.4.refs_3_), channel_id=1, source_target_pairs={{0,2},{4,0},{8,4},{12,8},{14,12},{10,14},{6,10},{2,6},{1,3},{5,1},... | collective-permute-start | bytes 393224 | tf_op jit(solution)/shard_map/ppermute | solution.py:53
  12.1 9.1 %collective-permute-start.3 = (bf16[64,1152]{1,0:T(8,128)(2,1)S(1)}, bf16[64,1152]{1,0:T(8,128)(2,1)S(1)}, u32[]{:S(2)}, u32[]{:S(2)}) collective-permute-start(bf16[64,1152]{1,0:T(8,128)(2,1)S(1)} %get-tuple-element.56.refs_0_), channel_id=1, source_target_pairs={{0,2},{4,0},{8,4},{12,8},{14,12},{10,14},{6,10},{2,6},{1,3},{5,1},... | collective-permute-start | bytes 442376 | tf_op jit(solution)/shard_map/ppermute | solution.py:53
  13.9 7.6 %collective-permute-start.2 = (bf16[64,1024]{1,0:T(8,128)(2,1)S(1)}, bf16[64,1024]{1,0:T(8,128)(2,1)S(1)}, u32[]{:S(2)}, u32[]{:S(2)}) collective-permute-start(bf16[64,1024]{1,0:T(8,128)(2,1)S(1)} %get-tuple-element.57.refs_1_), channel_id=1, source_target_pairs={{0,4},{4,8},{8,12},{12,14},{14,10},{10,6},{6,2},{2,0},{1,5},{5,9},... | collective-permute-start | bytes 393224 | tf_op jit(solution)/shard_map/ppermute | solution.py:53
  16.2 7.1 %collective-permute-start.9 = (bf16[64,1152]{1,0:T(8,128)(2,1)S(1)}, bf16[64,1152]{1,0:T(8,128)(2,1)S(1)}, u32[]{:S(2)}, u32[]{:S(2)}) collective-permute-start(bf16[64,1152]{1,0:T(8,128)(2,1)S(1)} %collective-permute-done.5.refs_0_), channel_id=1, source_target_pairs={{0,4},{4,8},{8,12},{12,14},{14,10},{10,6},{6,2},{2,0},{1,5},{5,9},... | collective-permute-start | bytes 442376 | tf_op jit(solution)/shard_map/ppermute | solution.py:53
  21.3 6.7 %collective-permute-start.7 = (bf16[64,1152]{1,0:T(8,128)(2,1)S(1)}, bf16[64,1152]{1,0:T(8,128)(2,1)S(1)}, u32[]{:S(2)}, u32[]{:S(2)}) collective-permute-start(bf16[64,1152]{1,0:T(8,128)(2,1)S(1)} %collective-permute-done.3.refs_2_), channel_id=1, source_target_pairs={{0,2},{4,0},{8,4},{12,8},{14,12},{10,14},{6,10},{2,6},{1,3},{5,1},... | collective-permute-start | bytes 442376 | tf_op jit(solution)/shard_map/ppermute | solution.py:53
  21.4 6.7 %collective-permute-start.6 = (bf16[64,1024]{1,0:T(8,128)(2,1)S(1)}, bf16[64,1024]{1,0:T(8,128)(2,1)S(1)}, u32[]{:S(2)}, u32[]{:S(2)}) collective-permute-start(bf16[64,1024]{1,0:T(8,128)(2,1)S(1)} %collective-permute-done.2.refs_1_), channel_id=1, source_target_pairs={{0,4},{4,8},{8,12},{12,14},{14,10},{10,6},{6,2},{2,0},{1,5},{5,9},... | collective-permute-start | bytes 393224 | tf_op jit(solution)/shard_map/ppermute | solution.py:53
  23.3 8.4 %collective-permute-start.13 = (bf16[64,1152]{1,0:T(8,128)(2,1)S(1)}, bf16[64,1152]{1,0:T(8,128)(2,1)S(1)}, u32[]{:S(2)}, u32[]{:S(2)}) collective-permute-start(bf16[64,1152]{1,0:T(8,128)(2,1)S(1)} %collective-permute-done.9.refs_0_), channel_id=1, source_target_pairs={{0,4},{4,8},{8,12},{12,14},{14,10},{10,6},{6,2},{2,0},{1,5},{5,9},... | collective-permute-start | bytes 442376 | tf_op jit(solution)/shard_map/ppermute | solution.py:53
  25.1 6.6 %collective-permute-start.14 = (bf16[64,1024]{1,0:T(8,128)(2,1)S(1)}, bf16[64,1024]{1,0:T(8,128)(2,1)S(1)}, u32[]{:S(2)}, u32[]{:S(2)}) collective-permute-start(bf16[64,1024]{1,0:T(8,128)(2,1)S(1)} %collective-permute-done.12.refs_3_), channel_id=1, source_target_pairs={{0,2},{4,0},{8,4},{12,8},{14,12},{10,14},{6,10},{2,6},{1,3},{5,1},... | collective-permute-start | bytes 393224 | tf_op jit(solution)/shard_map/ppermute | solution.py:53
  27.9 6.9 %collective-permute-start.11 = (bf16[64,1152]{1,0:T(8,128)(2,1)S(1)}, bf16[64,1152]{1,0:T(8,128)(2,1)S(1)}, u32[]{:S(2)}, u32[]{:S(2)}) collective-permute-start(bf16[64,1152]{1,0:T(8,128)(2,1)S(1)} %collective-permute-done.7.refs_2_), channel_id=1, source_target_pairs={{0,2},{4,0},{8,4},{12,8},{14,12},{10,14},{6,10},{2,6},{1,3},{5,1},... | collective-permute-start | bytes 442376 | tf_op jit(solution)/shard_map/ppermute | solution.py:53
  28.1 6.7 %collective-permute-start.10 = (bf16[64,1024]{1,0:T(8,128)(2,1)S(1)}, bf16[64,1024]{1,0:T(8,128)(2,1)S(1)}, u32[]{:S(2)}, u32[]{:S(2)}) collective-permute-start(bf16[64,1024]{1,0:T(8,128)(2,1)S(1)} %collective-permute-done.6.refs_1_), channel_id=1, source_target_pairs={{0,4},{4,8},{8,12},{12,14},{14,10},{10,6},{6,2},{2,0},{1,5},{5,9},... | collective-permute-start | bytes 393224 | tf_op jit(solution)/shard_map/ppermute | solution.py:53
  36.3 7.0 %collective-permute-start.19 = (bf16[64,1024]{1,0:T(8,128)(2,1)S(1)}, bf16[64,1024]{1,0:T(8,128)(2,1)S(1)}, u32[]{:S(2)}, u32[]{:S(2)}) collective-permute-start(bf16[64,1024]{1,0:T(8,128)(2,1)S(1)} %get-tuple-element.68), channel_id=1, source_target_pairs={{0,2},{4,0},{8,4},{12,8},{14,12},{10,14},{6,10},{2,6},{1,3},{5,1},... | collective-permute-start | bytes 393224 | tf_op jit(solution)/shard_map/ppermute | solution.py:53
  36.6 6.8 %collective-permute-start.22 = (bf16[64,1024]{1,0:T(8,128)(2,1)S(1)}, bf16[64,1024]{1,0:T(8,128)(2,1)S(1)}, u32[]{:S(2)}, u32[]{:S(2)}) collective-permute-start(bf16[64,1024]{1,0:T(8,128)(2,1)S(1)} %get-tuple-element.72), channel_id=1, source_target_pairs={{0,4},{4,8},{8,12},{12,14},{14,10},{10,6},{6,2},{2,0},{1,5},{5,9},... | collective-permute-start | bytes 393224 | tf_op jit(solution)/shard_map/ppermute | solution.py:53
  40.7 6.5 %collective-permute-start.26 = (bf16[64,1024]{1,0:T(8,128)(2,1)S(1)}, bf16[64,1024]{1,0:T(8,128)(2,1)S(1)}, u32[]{:S(2)}, u32[]{:S(2)}) collective-permute-start(bf16[64,1024]{1,0:T(8,128)(2,1)S(1)} %shard_map.119), channel_id=1, source_target_pairs={{0,2},{4,0},{8,4},{12,8},{14,12},{10,14},{6,10},{2,6},{1,3},{5,1},... | collective-permute-start | bytes 393224 | tf_op jit(solution)/shard_map/ppermute | solution.py:53
  43.5 7.7 %collective-permute-start.23 = (bf16[64,1024]{1,0:T(8,128)(2,1)S(1)}, bf16[64,1024]{1,0:T(8,128)(2,1)S(1)}, u32[]{:S(2)}, u32[]{:S(2)}) collective-permute-start(bf16[64,1024]{1,0:T(8,128)(2,1)S(1)} %shard_map.117), channel_id=1, source_target_pairs={{0,4},{4,8},{8,12},{12,14},{14,10},{10,6},{6,2},{2,0},{1,5},{5,9},... | collective-permute-start | bytes 393224 | tf_op jit(solution)/shard_map/ppermute | solution.py:53
  47.3 8.4 %collective-permute-start.27 = (bf16[64,1024]{1,0:T(8,128)(2,1)S(1)}, bf16[64,1024]{1,0:T(8,128)(2,1)S(1)}, u32[]{:S(2)}, u32[]{:S(2)}) collective-permute-start(bf16[64,1024]{1,0:T(8,128)(2,1)S(1)} %shard_map.120), channel_id=1, source_target_pairs={{0,2},{4,0},{8,4},{12,8},{14,12},{10,14},{6,10},{2,6},{1,3},{5,1},... | collective-permute-start | bytes 393224 | tf_op jit(solution)/shard_map/ppermute | solution.py:53
  49.5 8.4 %collective-permute-start.21 = (bf16[64,1024]{1,0:T(8,128)(2,1)S(1)}, bf16[64,1024]{1,0:T(8,128)(2,1)S(1)}, u32[]{:S(2)}, u32[]{:S(2)}) collective-permute-start(bf16[64,1024]{1,0:T(8,128)(2,1)S(1)} %shard_map.115), channel_id=1, source_target_pairs={{0,2},{4,0},{8,4},{12,8},{14,12},{10,14},{6,10},{2,6},{1,3},{5,1},... | collective-permute-start | bytes 393224 | tf_op jit(solution)/shard_map/ppermute | solution.py:53
  62.7 8.2 %collective-permute-start.40 = (bf16[64,1024]{1,0:T(8,128)(2,1)S(1)}, bf16[64,1024]{1,0:T(8,128)(2,1)S(1)}, u32[]{:S(2)}, u32[]{:S(2)}) collective-permute-start(bf16[64,1024]{1,0:T(8,128)(2,1)S(1)} %shard_map.116.refs_2_), channel_id=1, source_target_pairs={{0,2},{4,0},{8,4},{12,8},{14,12},{10,14},{6,10},{2,6},{1,3},{5,1},... | collective-permute-start | bytes 393224 | tf_op jit(solution)/shard_map/ppermute | solution.py:53
  63.3 7.9 %collective-permute-start.37 = (bf16[64,1024]{1,0:T(8,128)(2,1)S(1)}, bf16[64,1024]{1,0:T(8,128)(2,1)S(1)}, u32[]{:S(2)}, u32[]{:S(2)}) collective-permute-start(bf16[64,1024]{1,0:T(8,128)(2,1)S(1)} %shard_map.122.refs_3_), channel_id=1, source_target_pairs={{0,4},{4,8},{8,12},{12,14},{14,10},{10,6},{6,2},{2,0},{1,5},{5,9},... | collective-permute-start | bytes 393224 | tf_op jit(solution)/shard_map/ppermute | solution.py:53
  64.7 8.5 %collective-permute-start.30 = (bf16[64,1024]{1,0:T(8,128)(2,1)S(1)}, bf16[64,1024]{1,0:T(8,128)(2,1)S(1)}, u32[]{:S(2)}, u32[]{:S(2)}) collective-permute-start(bf16[64,1024]{1,0:T(8,128)(2,1)S(1)} %collective-permute-done.29.refs_4_), channel_id=1, source_target_pairs={{0,4},{4,8},{8,12},{12,14},{14,10},{10,6},{6,2},{2,0},{1,5},{5,9},... | collective-permute-start | bytes 393224 | tf_op jit(solution)/shard_map/ppermute | solution.py:53
  68.1 7.2 %collective-permute-start.34 = (bf16[64,1024]{1,0:T(8,128)(2,1)S(1)}, bf16[64,1024]{1,0:T(8,128)(2,1)S(1)}, u32[]{:S(2)}, u32[]{:S(2)}) collective-permute-start(bf16[64,1024]{1,0:T(8,128)(2,1)S(1)} %collective-permute-done.33.refs_7_), channel_id=1, source_target_pairs={{0,2},{4,0},{8,4},{12,8},{14,12},{10,14},{6,10},{2,6},{1,3},{5,1},... | collective-permute-start | bytes 393224 | tf_op jit(solution)/shard_map/ppermute | solution.py:53
  109.1 6.9 %collective-permute-start.53 = (bf16[128,1024]{1,0:T(8,128)(2,1)S(1)}, bf16[128,1024]{1,0:T(8,128)(2,1)S(1)}, u32[]{:S(2)}, u32[]{:S(2)}) collective-permute-start(bf16[128,1024]{1,0:T(8,128)(2,1)S(1)} %shard_map.139), channel_id=1, source_target_pairs={{0,2},{4,0},{8,4},{12,8},{14,12},{10,14},{6,10},{2,6},{1,3},{5,1},... | collective-permute-start | bytes 786440 | tf_op jit(solution)/shard_map/ppermute | solution.py:53
  110.8 6.9 %collective-permute-start.49 = (bf16[128,1024]{1,0:T(8,128)(2,1)S(1)}, bf16[128,1024]{1,0:T(8,128)(2,1)S(1)}, u32[]{:S(2)}, u32[]{:S(2)}) collective-permute-start(bf16[128,1024]{1,0:T(8,128)(2,1)S(1)} %shard_map.136), channel_id=1, source_target_pairs={{0,4},{4,8},{8,12},{12,14},{14,10},{10,6},{6,2},{2,0},{1,5},{5,9},... | collective-permute-start | bytes 786440 | tf_op jit(solution)/shard_map/ppermute | solution.py:53
  (35 other events, 316.5 us)

commit v10 on v9

--- a/solution.py
+++ b/solution.py
@@ -33,6 +33,21 @@
         out_specs=[pl.BlockSpec(memory_space=pltpu.VMEM)] * len(outs),
         compiler_params=pltpu.CompilerParams(vmem_limit_bytes=VMEM_LIMIT),
         cost_estimate=pl.CostEstimate(flops=flops, bytes_accessed=size, transcendentals=0),
+    )(*args)
+
+
+def after(value, guard):
+    def kernel(value_ref, guard_ref, out_ref):
+        pass
+
+    args = [pltpu.with_memory_space_constraint(a, pltpu.VMEM) for a in (value, guard)]
+    return pl.pallas_call(
+        kernel,
+        out_shape=pltpu.VMEM(value.shape, value.dtype),
+        in_specs=[pl.BlockSpec(memory_space=pltpu.VMEM)] * 2,
+        out_specs=pl.BlockSpec(memory_space=pltpu.VMEM),
+        input_output_aliases={0: 0},
+        compiler_params=pltpu.CompilerParams(vmem_limit_bytes=VMEM_LIMIT),
     )(*args)
 
 
@@ -108,8 +123,9 @@
                 ]
             else:
                 left, right = add(blocks[0], left), add(blocks[1], right)
+            last = left
             left, right = self.send(left, 1), self.send(right, -1)
-        return left, right
+        return left, right, last
 
     def part_types(self, distances):
         types = []
@@ -440,18 +456,6 @@
             pairs = [(e, e ^ mask) for e in range(expert_count)]
             pooled_grad = pooled_grad + lax.ppermute(mine, "expert", pairs).astype(F32)
 
-    both = jnp.concatenate([pooled, logit_grad], axis=1)
-    if group_count == 2:
-        both = jnp.concatenate([both, lax.ppermute(both, "group", [(0, 1), (1, 0)])], axis=0)
-    else:
-        both = lax.all_gather(both, "group", axis=0, tiled=True)
-    head_grad = lax.dot_general(
-        both[:, :feature_dim],
-        both[:, feature_dim:],
-        (((0,), (0,)), ((), ())),
-        preferred_element_type=F32,
-    )
-
     def backward_kernel(distances, residual_ref, inv_ref, gate_save, up_save, *refs):
         grad_ref, gain_ref, wide_ref, down_ref, *outs = refs
         residual, inv_rms = residual_ref[...], inv_ref[:, :1]
@@ -502,13 +506,26 @@
 
     for distances in reversed(list(tokens_at)):
         backward(distances)
+    left, right, last = ring.scatter_whole(back_at["ends"], back_at)
     token_grad = pl.pallas_call(
         sum_kernel,
         out_shape=jax.ShapeDtypeStruct(block, BF16),
         in_specs=[pl.BlockSpec(memory_space=pltpu.VMEM)] * 3,
         out_specs=pl.BlockSpec(memory_space=pltpu.VMEM),
         compiler_params=pltpu.CompilerParams(vmem_limit_bytes=VMEM_LIMIT),
-    )(back_at[0], *ring.scatter_whole(back_at["ends"], back_at))
+    )(back_at[0], left, right)
+
+    both = after(jnp.concatenate([pooled, logit_grad], axis=1), last)
+    if group_count == 2:
+        both = jnp.concatenate([both, lax.ppermute(both, "group", [(0, 1), (1, 0)])], axis=0)
+    else:
+        both = lax.all_gather(both, "group", axis=0, tiled=True)
+    head_grad = lax.dot_general(
+        both[:, :feature_dim],
+        both[:, feature_dim:],
+        (((0,), (0,)), ((), ())),
+        preferred_element_type=F32,
+    )
     return (token_grad, head_grad)
 
 

time: 125 us -> 126 us (level)
  transfers between devices with their start and end apart: 56 -> 56, of which waited for: 27 -> 28; matrix products, arithmetic and copies ran while one was open for 1% -> 1% of each run, Pallas kernels for 14% -> 14%
where the time goes in v10:
time: 126 us
  starting transfers between devices  62.4 us (50%)
  waiting for transfers between devices  38.8 us (31%)
  Pallas kernels  21.8 us (17%)
  matrix products  1.71 us (1%)
    ppermute x50, starting transfers between devices, send(): return lax.ppermute(value, 'expert', pairs)  57.2 us
    ppermute x50, waiting for transfers between devices, send(): return lax.ppermute(value, 'expert', pairs)  34.5 us
    pallas_call x35, Pallas kernels, call(): pl.pallas_call(kernel, out_shape=[pltpu.VMEM(shape, dtype) for shape, dty...  17.3 us
    ppermute x4, starting transfers between devices, body(): pooled_grad = pooled_grad + lax.ppermute(mine, 'expert', pairs).astype(F32)  4.66 us
    ppermute x4, waiting for transfers between devices, body(): pooled_grad = pooled_grad + lax.ppermute(mine, 'expert', pairs).astype(F32)  4.24 us
  transfers between devices with their start and end apart: 56, of which 28 were waited for; matrix products, arithmetic and copies ran while one was open for 1% of the time, Pallas kernels for 14%

profile of v10, /device:TPU:0, one launch (start us, length us, event | category | flops | bytes accessed | tf_op | source)
XLA Modules:
  0.0 125.8 jit_solution(16945221977702572454)
XLA Ops:
  0.6 1.9 %shard_map.104 = (bf16[64,1152]{1,0:T(8,128)(2,1)S(1)}, bf16[64,1024]{1,0:T(8,128)(2,1)S(1)}, bf16[3200,384]{1,0:T(8,128)(2,1)S(1)}) custom-call(s32[8,128]{1,0:T(8,128)} %bitcast.19, f32[8,128]{1,0:T(8,128)} %bitcast.20, bf16[128,1024]{1,0:T(8,128)(2,1)} %refs_2_.2, bf16[2,512,384]{2,1,0:T(8,128)(2,1)} %refs_0_.1, bf16[2,512,384]{2,1,0:T(8,128)(2,1)} %refs_1_.1, ...), custom_call_target="tpu_custom_call" | custom-call | tf_op jit(solution)/shard_map/pallas_call | solution.py:237
  3.1 2.6 %collective-permute-start.1 = (bf16[64,1152]{1,0:T(8,128)(2,1)S(1)}, bf16[64,1152]{1,0:T(8,128)(2,1)S(1)}, u32[]{:S(2)}, u32[]{:S(2)}) collective-permute-start(bf16[64,1152]{1,0:T(8,128)(2,1)S(1)} %get-tuple-element.56.refs_0_), channel_id=1, source_target_pairs={{0,4},{4,8},{8,12},{12,14},{14,10},{10,6},{6,2},{2,0},{1,5},{5,9},... | collective-permute-start | bytes 442376 | tf_op jit(solution)/shard_map/ppermute | solution.py:68
  5.7 4.4 %collective-permute-done.1.refs_0_ = bf16[64,1152]{1,0:T(8,128)(2,1)S(1)} collective-permute-done((bf16[64,1152]{1,0:T(8,128)(2,1)S(1)}, bf16[64,1152]{1,0:T(8,128)(2,1)S(1)}, u32[]{:S(2)}, u32[]{:S(2)}) %collective-permute-start.1) | collective-permute-done | bytes 147488 | tf_op jit(solution)/shard_map/ppermute | solution.py:68
  14.2 2.0 %collective-permute-done.5.refs_0_ = bf16[64,1152]{1,0:T(8,128)(2,1)S(1)} collective-permute-done((bf16[64,1152]{1,0:T(8,128)(2,1)S(1)}, bf16[64,1152]{1,0:T(8,128)(2,1)S(1)}, u32[]{:S(2)}, u32[]{:S(2)}) %collective-permute-start.5) | collective-permute-done | bytes 147488 | tf_op jit(solution)/shard_map/ppermute | solution.py:68
  16.2 2.5 %collective-permute-start.9 = (bf16[64,1152]{1,0:T(8,128)(2,1)S(1)}, bf16[64,1152]{1,0:T(8,128)(2,1)S(1)}, u32[]{:S(2)}, u32[]{:S(2)}) collective-permute-start(bf16[64,1152]{1,0:T(8,128)(2,1)S(1)} %collective-permute-done.5.refs_0_), channel_id=1, source_target_pairs={{0,4},{4,8},{8,12},{12,14},{14,10},{10,6},{6,2},{2,0},{1,5},{5,9},... | collective-permute-start | bytes 442376 | tf_op jit(solution)/shard_map/ppermute | solution.py:68
  18.7 2.6 %collective-permute-done.3.refs_2_ = bf16[64,1152]{1,0:T(8,128)(2,1)S(1)} collective-permute-done((bf16[64,1152]{1,0:T(8,128)(2,1)S(1)}, bf16[64,1152]{1,0:T(8,128)(2,1)S(1)}, u32[]{:S(2)}, u32[]{:S(2)}) %collective-permute-start.3) | collective-permute-done | bytes 147488 | tf_op jit(solution)/shard_map/ppermute | solution.py:68
  21.4 1.9 %collective-permute-start.6 = (bf16[64,1024]{1,0:T(8,128)(2,1)S(1)}, bf16[64,1024]{1,0:T(8,128)(2,1)S(1)}, u32[]{:S(2)}, u32[]{:S(2)}) collective-permute-start(bf16[64,1024]{1,0:T(8,128)(2,1)S(1)} %collective-permute-done.2.refs_1_), channel_id=1, source_target_pairs={{0,4},{4,8},{8,12},{12,14},{14,10},{10,6},{6,2},{2,0},{1,5},{5,9},... | collective-permute-start | bytes 393224 | tf_op jit(solution)/shard_map/ppermute | solution.py:68
  25.3 2.6 %collective-permute-done.7.refs_2_ = bf16[64,1152]{1,0:T(8,128)(2,1)S(1)} collective-permute-done((bf16[64,1152]{1,0:T(8,128)(2,1)S(1)}, bf16[64,1152]{1,0:T(8,128)(2,1)S(1)}, u32[]{:S(2)}, u32[]{:S(2)}) %collective-permute-start.7) | collective-permute-done | bytes 147488 | tf_op jit(solution)/shard_map/ppermute | solution.py:68
  43.5 2.1 %collective-permute-start.23 = (bf16[64,1024]{1,0:T(8,128)(2,1)S(1)}, bf16[64,1024]{1,0:T(8,128)(2,1)S(1)}, u32[]{:S(2)}, u32[]{:S(2)}) collective-permute-start(bf16[64,1024]{1,0:T(8,128)(2,1)S(1)} %shard_map.117), channel_id=1, source_target_pairs={{0,4},{4,8},{8,12},{12,14},{14,10},{10,6},{6,2},{2,0},{1,5},{5,9},... | collective-permute-start | bytes 393224 | tf_op jit(solution)/shard_map/ppermute | solution.py:68
  52.2 2.5 %collective-permute-start.18 = (bf16[64,1024]{1,0:T(8,128)(2,1)S(1)}, bf16[64,1024]{1,0:T(8,128)(2,1)S(1)}, u32[]{:S(2)}, u32[]{:S(2)}) collective-permute-start(bf16[64,1024]{1,0:T(8,128)(2,1)S(1)} %shard_map.113), channel_id=1, source_target_pairs={{0,4},{4,8},{8,12},{12,14},{14,10},{10,6},{6,2},{2,0},{1,5},{5,9},... | collective-permute-start | bytes 393224 | tf_op jit(solution)/shard_map/ppermute | solution.py:68
  58.5 2.5 %collective-permute-start.29 = (bf16[64,1024]{1,0:T(8,128)(2,1)S(1)}, bf16[64,1024]{1,0:T(8,128)(2,1)S(1)}, u32[]{:S(2)}, u32[]{:S(2)}) collective-permute-start(bf16[64,1024]{1,0:T(8,128)(2,1)S(1)} %shard_map.116.refs_2_), channel_id=1, source_target_pairs={{0,4},{4,8},{8,12},{12,14},{14,10},{10,6},{6,2},{2,0},{1,5},{5,9},... | collective-permute-start | bytes 393224 | tf_op jit(solution)/shard_map/ppermute | solution.py:68
  64.7 2.3 %collective-permute-start.30 = (bf16[64,1024]{1,0:T(8,128)(2,1)S(1)}, bf16[64,1024]{1,0:T(8,128)(2,1)S(1)}, u32[]{:S(2)}, u32[]{:S(2)}) collective-permute-start(bf16[64,1024]{1,0:T(8,128)(2,1)S(1)} %collective-permute-done.29.refs_4_), channel_id=1, source_target_pairs={{0,4},{4,8},{8,12},{12,14},{14,10},{10,6},{6,2},{2,0},{1,5},{5,9},... | collective-permute-start | bytes 393224 | tf_op jit(solution)/shard_map/ppermute | solution.py:68
  68.5 2.3 %collective-permute-done.40.refs_6_ = bf16[64,1024]{1,0:T(8,128)(2,1)S(1)} collective-permute-done((bf16[64,1024]{1,0:T(8,128)(2,1)S(1)}, bf16[64,1024]{1,0:T(8,128)(2,1)S(1)}, u32[]{:S(2)}, u32[]{:S(2)}) %collective-permute-start.40) | collective-permute-done | bytes 131104 | tf_op jit(solution)/shard_map/ppermute | solution.py:68
  73.1 2.0 %collective-permute-start.31 = (bf16[64,1024]{1,0:T(8,128)(2,1)S(1)}, bf16[64,1024]{1,0:T(8,128)(2,1)S(1)}, u32[]{:S(2)}, u32[]{:S(2)}) collective-permute-start(bf16[64,1024]{1,0:T(8,128)(2,1)S(1)} %collective-permute-done.30.refs_4_), channel_id=1, source_target_pairs={{0,4},{4,8},{8,12},{12,14},{14,10},{10,6},{6,2},{2,0},{1,5},{5,9},... | collective-permute-start | bytes 393224 | tf_op jit(solution)/shard_map/ppermute | solution.py:68
  83.2 1.9 %collective-permute-done.36.refs_3_ = bf16[64,1024]{1,0:T(8,128)(2,1)S(1)} collective-permute-done((bf16[64,1024]{1,0:T(8,128)(2,1)S(1)}, bf16[64,1024]{1,0:T(8,128)(2,1)S(1)}, u32[]{:S(2)}, u32[]{:S(2)}) %collective-permute-start.36) | collective-permute-done | bytes 131104 | tf_op jit(solution)/shard_map/ppermute | solution.py:68
  86.0 3.6 %collective-permute-done.43 = bf16[8,1024]{1,0:T(8,128)(2,1)S(1)} collective-permute-done((bf16[8,1024]{1,0:T(8,128)(2,1)S(1)}, bf16[8,1024]{1,0:T(8,128)(2,1)S(1)}, u32[]{:S(2)}, u32[]{:S(2)}) %collective-permute-start.43) | collective-permute-done | bytes 16416 | tf_op jit(solution)/shard_map/ppermute | solution.py:457
  89.5 2.1 %collective-permute-start.46 = (bf16[8,1024]{1,0:T(8,128)(2,1)S(1)}, bf16[8,1024]{1,0:T(8,128)(2,1)S(1)}, u32[]{:S(2)}, u32[]{:S(2)}) collective-permute-start(bf16[8,1024]{1,0:T(8,128)(2,1)S(1)} %add_convert_fusion), channel_id=1, source_target_pairs={{0,12},{2,14},{4,8},{6,10},{8,4},{10,6},{12,0},{14,2},{1,13},{3,15... | collective-permute-start | bytes 49160 | tf_op jit(solution)/shard_map/ppermute | solution.py:457
  101.3 1.9 %collective-permute-done.51.arrived_ref = bf16[64,1024]{1,0:T(8,128)(2,1)S(1)} collective-permute-done((bf16[64,1024]{1,0:T(8,128)(2,1)S(1)}, bf16[64,1024]{1,0:T(8,128)(2,1)S(1)}, u32[]{:S(2)}, u32[]{:S(2)}) %collective-permute-start.51) | collective-permute-done | bytes 131104 | tf_op jit(solution)/shard_map/ppermute | solution.py:68
  103.2 2.4 %collective-permute-start.52 = (bf16[128,1024]{1,0:T(8,128)(2,1)S(1)}, bf16[128,1024]{1,0:T(8,128)(2,1)S(1)}, u32[]{:S(2)}, u32[]{:S(2)}) collective-permute-start(bf16[128,1024]{1,0:T(8,128)(2,1)S(1)} %shard_map.138), channel_id=1, source_target_pairs={{0,2},{4,0},{8,4},{12,8},{14,12},{10,14},{6,10},{2,6},{1,3},{5,1},... | collective-permute-start | bytes 786440 | tf_op jit(solution)/shard_map/ppermute | solution.py:68
  107.4 2.3 %collective-permute-done.52.arrived_ref = bf16[128,1024]{1,0:T(8,128)(2,1)S(1)} collective-permute-done((bf16[128,1024]{1,0:T(8,128)(2,1)S(1)}, bf16[128,1024]{1,0:T(8,128)(2,1)S(1)}, u32[]{:S(2)}, u32[]{:S(2)}) %collective-permute-start.52) | collective-permute-done | bytes 262176 | tf_op jit(solution)/shard_map/ppermute | solution.py:68
  109.7 2.4 %collective-permute-start.53 = (bf16[128,1024]{1,0:T(8,128)(2,1)S(1)}, bf16[128,1024]{1,0:T(8,128)(2,1)S(1)}, u32[]{:S(2)}, u32[]{:S(2)}) collective-permute-start(bf16[128,1024]{1,0:T(8,128)(2,1)S(1)} %shard_map.139), channel_id=1, source_target_pairs={{0,2},{4,0},{8,4},{12,8},{14,12},{10,14},{6,10},{2,6},{1,3},{5,1},... | collective-permute-start | bytes 786440 | tf_op jit(solution)/shard_map/ppermute | solution.py:68
  113.8 2.3 %collective-permute-done.53.arrived_ref = bf16[128,1024]{1,0:T(8,128)(2,1)S(1)} collective-permute-done((bf16[128,1024]{1,0:T(8,128)(2,1)S(1)}, bf16[128,1024]{1,0:T(8,128)(2,1)S(1)}, u32[]{:S(2)}, u32[]{:S(2)}) %collective-permute-start.53) | collective-permute-done | bytes 262176 | tf_op jit(solution)/shard_map/ppermute | solution.py:68
  116.2 2.4 %collective-permute-start.54 = (bf16[128,1024]{1,0:T(8,128)(2,1)S(1)}, bf16[128,1024]{1,0:T(8,128)(2,1)S(1)}, u32[]{:S(2)}, u32[]{:S(2)}) collective-permute-start(bf16[128,1024]{1,0:T(8,128)(2,1)S(1)} %shard_map.140), channel_id=1, source_target_pairs={{0,2},{4,0},{8,4},{12,8},{14,12},{10,14},{6,10},{2,6},{1,3},{5,1},... | collective-permute-start | bytes 786440 | tf_op jit(solution)/shard_map/ppermute | solution.py:68
  122.6 2.4 %collective-permute-done.50.refs_1_ = bf16[128,1024]{1,0:T(8,128)(2,1)S(1)} collective-permute-done((bf16[128,1024]{1,0:T(8,128)(2,1)S(1)}, bf16[128,1024]{1,0:T(8,128)(2,1)S(1)}, u32[]{:S(2)}, u32[]{:S(2)}) %collective-permute-start.50) | collective-permute-done | bytes 262176 | tf_op jit(solution)/shard_map/ppermute | solution.py:68
  (141 shorter events, 66.9 us)
Async XLA Ops:
  2.6 27.4 %collective-permute-start = (bf16[3200,384]{1,0:T(8,128)(2,1)S(1)}, bf16[3200,384]{1,0:T(8,128)(2,1)S(1)}, u32[]{:S(2)}, u32[]{:S(2)}) collective-permute-start(bf16[3200,384]{1,0:T(8,128)(2,1)S(1)} %get-tuple-element.58), channel_id=1, source_target_pairs={{0,1},{1,0},{2,3},{3,2},{4,5},{5,4},{6,7},{7,6},{8,9},{9,8},{10,11... | collective-permute-start | bytes 7372808 | tf_op jit(solution)/shard_map/ppermute | solution.py:332
  3.1 7.0 %collective-permute-start.1 = (bf16[64,1152]{1,0:T(8,128)(2,1)S(1)}, bf16[64,1152]{1,0:T(8,128)(2,1)S(1)}, u32[]{:S(2)}, u32[]{:S(2)}) collective-permute-start(bf16[64,1152]{1,0:T(8,128)(2,1)S(1)} %get-tuple-element.56.refs_0_), channel_id=1, source_target_pairs={{0,4},{4,8},{8,12},{12,14},{14,10},{10,6},{6,2},{2,0},{1,5},{5,9},... | collective-permute-start | bytes 442376 | tf_op jit(solution)/shard_map/ppermute | solution.py:68
  11.9 6.8 %collective-permute-start.8 = (bf16[64,1024]{1,0:T(8,128)(2,1)S(1)}, bf16[64,1024]{1,0:T(8,128)(2,1)S(1)}, u32[]{:S(2)}, u32[]{:S(2)}) collective-permute-start(bf16[64,1024]{1,0:T(8,128)(2,1)S(1)} %collective-permute-done.4.refs_3_), channel_id=1, source_target_pairs={{0,2},{4,0},{8,4},{12,8},{14,12},{10,14},{6,10},{2,6},{1,3},{5,1},... | collective-permute-start | bytes 393224 | tf_op jit(solution)/shard_map/ppermute | solution.py:68
  12.1 9.1 %collective-permute-start.3 = (bf16[64,1152]{1,0:T(8,128)(2,1)S(1)}, bf16[64,1152]{1,0:T(8,128)(2,1)S(1)}, u32[]{:S(2)}, u32[]{:S(2)}) collective-permute-start(bf16[64,1152]{1,0:T(8,128)(2,1)S(1)} %get-tuple-element.56.refs_0_), channel_id=1, source_target_pairs={{0,2},{4,0},{8,4},{12,8},{14,12},{10,14},{6,10},{2,6},{1,3},{5,1},... | collective-permute-start | bytes 442376 | tf_op jit(solution)/shard_map/ppermute | solution.py:68
  13.9 7.6 %collective-permute-start.2 = (bf16[64,1024]{1,0:T(8,128)(2,1)S(1)}, bf16[64,1024]{1,0:T(8,128)(2,1)S(1)}, u32[]{:S(2)}, u32[]{:S(2)}) collective-permute-start(bf16[64,1024]{1,0:T(8,128)(2,1)S(1)} %get-tuple-element.57.refs_1_), channel_id=1, source_target_pairs={{0,4},{4,8},{8,12},{12,14},{14,10},{10,6},{6,2},{2,0},{1,5},{5,9},... | collective-permute-start | bytes 393224 | tf_op jit(solution)/shard_map/ppermute | solution.py:68
  16.2 7.1 %collective-permute-start.9 = (bf16[64,1152]{1,0:T(8,128)(2,1)S(1)}, bf16[64,1152]{1,0:T(8,128)(2,1)S(1)}, u32[]{:S(2)}, u32[]{:S(2)}) collective-permute-start(bf16[64,1152]{1,0:T(8,128)(2,1)S(1)} %collective-permute-done.5.refs_0_), channel_id=1, source_target_pairs={{0,4},{4,8},{8,12},{12,14},{14,10},{10,6},{6,2},{2,0},{1,5},{5,9},... | collective-permute-start | bytes 442376 | tf_op jit(solution)/shard_map/ppermute | solution.py:68
  21.3 6.7 %collective-permute-start.7 = (bf16[64,1152]{1,0:T(8,128)(2,1)S(1)}, bf16[64,1152]{1,0:T(8,128)(2,1)S(1)}, u32[]{:S(2)}, u32[]{:S(2)}) collective-permute-start(bf16[64,1152]{1,0:T(8,128)(2,1)S(1)} %collective-permute-done.3.refs_2_), channel_id=1, source_target_pairs={{0,2},{4,0},{8,4},{12,8},{14,12},{10,14},{6,10},{2,6},{1,3},{5,1},... | collective-permute-start | bytes 442376 | tf_op jit(solution)/shard_map/ppermute | solution.py:68
  21.4 6.7 %collective-permute-start.6 = (bf16[64,1024]{1,0:T(8,128)(2,1)S(1)}, bf16[64,1024]{1,0:T(8,128)(2,1)S(1)}, u32[]{:S(2)}, u32[]{:S(2)}) collective-permute-start(bf16[64,1024]{1,0:T(8,128)(2,1)S(1)} %collective-permute-done.2.refs_1_), channel_id=1, source_target_pairs={{0,4},{4,8},{8,12},{12,14},{14,10},{10,6},{6,2},{2,0},{1,5},{5,9},... | collective-permute-start | bytes 393224 | tf_op jit(solution)/shard_map/ppermute | solution.py:68
  23.3 8.4 %collective-permute-start.13 = (bf16[64,1152]{1,0:T(8,128)(2,1)S(1)}, bf16[64,1152]{1,0:T(8,128)(2,1)S(1)}, u32[]{:S(2)}, u32[]{:S(2)}) collective-permute-start(bf16[64,1152]{1,0:T(8,128)(2,1)S(1)} %collective-permute-done.9.refs_0_), channel_id=1, source_target_pairs={{0,4},{4,8},{8,12},{12,14},{14,10},{10,6},{6,2},{2,0},{1,5},{5,9},... | collective-permute-start | bytes 442376 | tf_op jit(solution)/shard_map/ppermute | solution.py:68
  25.1 6.6 %collective-permute-start.14 = (bf16[64,1024]{1,0:T(8,128)(2,1)S(1)}, bf16[64,1024]{1,0:T(8,128)(2,1)S(1)}, u32[]{:S(2)}, u32[]{:S(2)}) collective-permute-start(bf16[64,1024]{1,0:T(8,128)(2,1)S(1)} %collective-permute-done.12.refs_3_), channel_id=1, source_target_pairs={{0,2},{4,0},{8,4},{12,8},{14,12},{10,14},{6,10},{2,6},{1,3},{5,1},... | collective-permute-start | bytes 393224 | tf_op jit(solution)/shard_map/ppermute | solution.py:68
  27.9 6.9 %collective-permute-start.11 = (bf16[64,1152]{1,0:T(8,128)(2,1)S(1)}, bf16[64,1152]{1,0:T(8,128)(2,1)S(1)}, u32[]{:S(2)}, u32[]{:S(2)}) collective-permute-start(bf16[64,1152]{1,0:T(8,128)(2,1)S(1)} %collective-permute-done.7.refs_2_), channel_id=1, source_target_pairs={{0,2},{4,0},{8,4},{12,8},{14,12},{10,14},{6,10},{2,6},{1,3},{5,1},... | collective-permute-start | bytes 442376 | tf_op jit(solution)/shard_map/ppermute | solution.py:68
  28.1 6.7 %collective-permute-start.10 = (bf16[64,1024]{1,0:T(8,128)(2,1)S(1)}, bf16[64,1024]{1,0:T(8,128)(2,1)S(1)}, u32[]{:S(2)}, u32[]{:S(2)}) collective-permute-start(bf16[64,1024]{1,0:T(8,128)(2,1)S(1)} %collective-permute-done.6.refs_1_), channel_id=1, source_target_pairs={{0,4},{4,8},{8,12},{12,14},{14,10},{10,6},{6,2},{2,0},{1,5},{5,9},... | collective-permute-start | bytes 393224 | tf_op jit(solution)/shard_map/ppermute | solution.py:68
  36.3 7.0 %collective-permute-start.19 = (bf16[64,1024]{1,0:T(8,128)(2,1)S(1)}, bf16[64,1024]{1,0:T(8,128)(2,1)S(1)}, u32[]{:S(2)}, u32[]{:S(2)}) collective-permute-start(bf16[64,1024]{1,0:T(8,128)(2,1)S(1)} %get-tuple-element.68), channel_id=1, source_target_pairs={{0,2},{4,0},{8,4},{12,8},{14,12},{10,14},{6,10},{2,6},{1,3},{5,1},... | collective-permute-start | bytes 393224 | tf_op jit(solution)/shard_map/ppermute | solution.py:68
  36.6 6.8 %collective-permute-start.22 = (bf16[64,1024]{1,0:T(8,128)(2,1)S(1)}, bf16[64,1024]{1,0:T(8,128)(2,1)S(1)}, u32[]{:S(2)}, u32[]{:S(2)}) collective-permute-start(bf16[64,1024]{1,0:T(8,128)(2,1)S(1)} %get-tuple-element.72), channel_id=1, source_target_pairs={{0,4},{4,8},{8,12},{12,14},{14,10},{10,6},{6,2},{2,0},{1,5},{5,9},... | collective-permute-start | bytes 393224 | tf_op jit(solution)/shard_map/ppermute | solution.py:68
  39.2 6.5 %collective-permute-start.16 = (bf16[64,1024]{1,0:T(8,128)(2,1)S(1)}, bf16[64,1024]{1,0:T(8,128)(2,1)S(1)}, u32[]{:S(2)}, u32[]{:S(2)}) collective-permute-start(bf16[64,1024]{1,0:T(8,128)(2,1)S(1)} %shard_map.111), channel_id=1, source_target_pairs={{0,4},{4,8},{8,12},{12,14},{14,10},{10,6},{6,2},{2,0},{1,5},{5,9},... | collective-permute-start | bytes 393224 | tf_op jit(solution)/shard_map/ppermute | solution.py:68
  40.7 6.5 %collective-permute-start.26 = (bf16[64,1024]{1,0:T(8,128)(2,1)S(1)}, bf16[64,1024]{1,0:T(8,128)(2,1)S(1)}, u32[]{:S(2)}, u32[]{:S(2)}) collective-permute-start(bf16[64,1024]{1,0:T(8,128)(2,1)S(1)} %shard_map.119), channel_id=1, source_target_pairs={{0,2},{4,0},{8,4},{12,8},{14,12},{10,14},{6,10},{2,6},{1,3},{5,1},... | collective-permute-start | bytes 393224 | tf_op jit(solution)/shard_map/ppermute | solution.py:68
  43.5 7.7 %collective-permute-start.23 = (bf16[64,1024]{1,0:T(8,128)(2,1)S(1)}, bf16[64,1024]{1,0:T(8,128)(2,1)S(1)}, u32[]{:S(2)}, u32[]{:S(2)}) collective-permute-start(bf16[64,1024]{1,0:T(8,128)(2,1)S(1)} %shard_map.117), channel_id=1, source_target_pairs={{0,4},{4,8},{8,12},{12,14},{14,10},{10,6},{6,2},{2,0},{1,5},{5,9},... | collective-permute-start | bytes 393224 | tf_op jit(solution)/shard_map/ppermute | solution.py:68
  47.3 8.4 %collective-permute-start.27 = (bf16[64,1024]{1,0:T(8,128)(2,1)S(1)}, bf16[64,1024]{1,0:T(8,128)(2,1)S(1)}, u32[]{:S(2)}, u32[]{:S(2)}) collective-permute-start(bf16[64,1024]{1,0:T(8,128)(2,1)S(1)} %shard_map.120), channel_id=1, source_target_pairs={{0,2},{4,0},{8,4},{12,8},{14,12},{10,14},{6,10},{2,6},{1,3},{5,1},... | collective-permute-start | bytes 393224 | tf_op jit(solution)/shard_map/ppermute | solution.py:68
  49.5 8.4 %collective-permute-start.21 = (bf16[64,1024]{1,0:T(8,128)(2,1)S(1)}, bf16[64,1024]{1,0:T(8,128)(2,1)S(1)}, u32[]{:S(2)}, u32[]{:S(2)}) collective-permute-start(bf16[64,1024]{1,0:T(8,128)(2,1)S(1)} %shard_map.115), channel_id=1, source_target_pairs={{0,2},{4,0},{8,4},{12,8},{14,12},{10,14},{6,10},{2,6},{1,3},{5,1},... | collective-permute-start | bytes 393224 | tf_op jit(solution)/shard_map/ppermute | solution.py:68
  54.8 6.5 %collective-permute-start.24 = (bf16[64,1024]{1,0:T(8,128)(2,1)S(1)}, bf16[64,1024]{1,0:T(8,128)(2,1)S(1)}, u32[]{:S(2)}, u32[]{:S(2)}) collective-permute-start(bf16[64,1024]{1,0:T(8,128)(2,1)S(1)} %shard_map.118), channel_id=1, source_target_pairs={{0,4},{4,8},{8,12},{12,14},{14,10},{10,6},{6,2},{2,0},{1,5},{5,9},... | collective-permute-start | bytes 393224 | tf_op jit(solution)/shard_map/ppermute | solution.py:68
  62.7 8.2 %collective-permute-start.40 = (bf16[64,1024]{1,0:T(8,128)(2,1)S(1)}, bf16[64,1024]{1,0:T(8,128)(2,1)S(1)}, u32[]{:S(2)}, u32[]{:S(2)}) collective-permute-start(bf16[64,1024]{1,0:T(8,128)(2,1)S(1)} %shard_map.116.refs_2_), channel_id=1, source_target_pairs={{0,2},{4,0},{8,4},{12,8},{14,12},{10,14},{6,10},{2,6},{1,3},{5,1},... | collective-permute-start | bytes 393224 | tf_op jit(solution)/shard_map/ppermute | solution.py:68
  63.1 8.2 %collective-permute-start.37 = (bf16[64,1024]{1,0:T(8,128)(2,1)S(1)}, bf16[64,1024]{1,0:T(8,128)(2,1)S(1)}, u32[]{:S(2)}, u32[]{:S(2)}) collective-permute-start(bf16[64,1024]{1,0:T(8,128)(2,1)S(1)} %shard_map.122.refs_3_), channel_id=1, source_target_pairs={{0,4},{4,8},{8,12},{12,14},{14,10},{10,6},{6,2},{2,0},{1,5},{5,9},... | collective-permute-start | bytes 393224 | tf_op jit(solution)/shard_map/ppermute | solution.py:68
  64.7 8.4 %collective-permute-start.30 = (bf16[64,1024]{1,0:T(8,128)(2,1)S(1)}, bf16[64,1024]{1,0:T(8,128)(2,1)S(1)}, u32[]{:S(2)}, u32[]{:S(2)}) collective-permute-start(bf16[64,1024]{1,0:T(8,128)(2,1)S(1)} %collective-permute-done.29.refs_4_), channel_id=1, source_target_pairs={{0,4},{4,8},{8,12},{12,14},{14,10},{10,6},{6,2},{2,0},{1,5},{5,9},... | collective-permute-start | bytes 393224 | tf_op jit(solution)/shard_map/ppermute | solution.py:68
  68.0 7.1 %collective-permute-start.34 = (bf16[64,1024]{1,0:T(8,128)(2,1)S(1)}, bf16[64,1024]{1,0:T(8,128)(2,1)S(1)}, u32[]{:S(2)}, u32[]{:S(2)}) collective-permute-start(bf16[64,1024]{1,0:T(8,128)(2,1)S(1)} %collective-permute-done.33.refs_7_), channel_id=1, source_target_pairs={{0,2},{4,0},{8,4},{12,8},{14,12},{10,14},{6,10},{2,6},{1,3},{5,1},... | collective-permute-start | bytes 393224 | tf_op jit(solution)/shard_map/ppermute | solution.py:68
  (35 other events, 312.8 us)

commit v11 on v10

--- a/solution.py
+++ b/solution.py
@@ -89,21 +89,7 @@
             use((-step, step), (top_left, bottom_left, top_right, bottom_right))
         use((self.half,), (self.send(top_left, 1), self.send(bottom_right, -1)))
 
-    def scatter(self, parts):
-        most = self.half - 1
-        top_left = self.send(parts[self.half][0], 1)
-        bottom_right = self.send(parts[self.half][1], -1)
-        bottom_left = self.send(parts[most][1], 1)
-        top_right = self.send(parts[-most][0], -1)
-        for step in range(most, 0, -1):
-            top_left = self.send(add(parts[step][0], top_left), 1)
-            bottom_right = self.send(add(parts[-step][1], bottom_right), -1)
-            if step > 1:
-                bottom_left = self.send(add(parts[step - 1][1], bottom_left), 1)
-                top_right = self.send(add(parts[1 - step][0], top_right), -1)
-        return (top_left, top_right), (bottom_left, bottom_right)
-
-    def scatter_whole(self, ends, parts):
+    def scatter(self, ends, parts):
         mid = ends[0].shape[0]
 
         def half_kernel(first, block_ref, arrived_ref, out_ref):
@@ -111,29 +97,24 @@
             out_ref[added, :] = (block_ref[added, :] + arrived_ref[...].astype(F32)).astype(BF16)
             out_ref[kept, :] = block_ref[kept, :].astype(BF16)
 
-        left, right = self.send(ends[0], 1), self.send(ends[1], -1)
-        for step in range(self.half - 1, 0, -1):
-            blocks = parts[step], parts[-step]
-            if step == self.half - 1:
-                halves = [functools.partial(half_kernel, first) for first in (0, mid)]
-                shape = blocks[0].shape
-                left, right = [
-                    call(kernel, [(shape, BF16)], block, arrived)[0]
-                    for kernel, block, arrived in zip(halves, blocks, (left, right))
-                ]
+        def right_kernel(first, block_ref, arrived_ref, guard_ref, out_ref):
+            if arrived_ref.shape[0] == mid:
+                half_kernel(first, block_ref, arrived_ref, out_ref)
             else:
-                left, right = add(blocks[0], left), add(blocks[1], right)
-            last = left
-            left, right = self.send(left, 1), self.send(right, -1)
-        return left, right, last
-
-    def part_types(self, distances):
-        types = []
-        for k in distances:
-            first = BF16 if k == self.half or k == 1 - self.half else F32
-            second = BF16 if k == self.half or k == self.half - 1 else F32
-            types += [first, second]
-        return types
+                add_kernel(block_ref, arrived_ref, out_ref)
+
+        most = self.half - 1
+        from_right = self.send(ends[1], -1)
+        from_left = self.send(after(ends[0], parts[max(most - 1, 0)]), 1)
+        for step in range(most, 0, -1):
+            shape = [(parts[step].shape, BF16)]
+            kernel = functools.partial(half_kernel, mid) if step == most else add_kernel
+            leftward = call(kernel, shape, parts[-step], from_right)[0]
+            from_right = self.send(leftward, -1)
+            kernel = functools.partial(right_kernel, 0)
+            rightward = call(kernel, shape, parts[step], from_left, parts[max(step - 2, 0)])[0]
+            from_left = self.send(rightward, 1)
+        return from_left, from_right, rightward
 
 
 def add_kernel(block_ref, arrived_ref, out_ref):
@@ -144,13 +125,12 @@
     return call(add_kernel, [(block.shape, BF16)], block, arrived)[0]
 
 
-def sum_kernel(*refs):
-    out_ref = refs[-1]
-    rows = refs[0].shape[0]
-    for i in range(len(refs) // 3):
-        own, left, right = refs[3 * i : 3 * i + 3]
-        arrived = left[...].astype(F32) + right[...].astype(F32)
-        out_ref[pl.ds(i * rows, rows), :] = (own[...] + arrived).astype(BF16)
+def sum_kernel(own_ref, left_ref, right_ref, *outs):
+    arrived = left_ref[...].astype(F32) + right_ref[...].astype(F32)
+    total = (own_ref[...] + arrived).astype(BF16)
+    rows = total.shape[0] // len(outs)
+    for i, out in enumerate(outs):
+        out[...] = total[i * rows : (i + 1) * rows]
 
 
 class Copies:
@@ -365,8 +345,9 @@
             outs[1][:, cols] = silu.astype(BF16)
             hidden.append((silu * up_act).astype(BF16))
         total = dot(jnp.concatenate(hidden, axis=1), down_ref[...])
+        rows = total.shape[0] // len(outs[2:])
         for i, out in enumerate(outs[2:]):
-            out[...] = total[i * mid : (i + 1) * mid].astype(out.dtype)
+            out[...] = total[i * rows : (i + 1) * rows].astype(out.dtype)
 
     tokens_at, saved_at, part_at = {}, {}, {}
     flops = 2 * rows_here * feature_dim * hidden_dim * local_experts * 3
@@ -374,11 +355,16 @@
     def hold(distances, blocks):
         tokens_at[distances] = blocks
 
-    def keep_parts(parts, distances, halves):
-        parts.update({k: halves[2 * i : 2 * i + 2] for i, k in enumerate(distances)})
-
     def part_outs(distances):
-        return [((mid, feature_dim), dtype) for dtype in ring.part_types(distances)]
+        if distances == (ring.half,):
+            return [((mid, feature_dim), BF16)] * 2
+        return [(block, F32)] * len(distances)
+
+    def keep_parts(parts, distances, results):
+        if distances == (ring.half,):
+            parts["ends"] = results
+        else:
+            parts.update(zip(distances, results))
 
     def forward(distances):
         blocks = tokens_at[distances]
@@ -398,11 +384,9 @@
     for distances in tokens_at:
         forward(distances)
     gain = norm_gain.reshape(1, feature_dim)
-    half_shape = (mid, feature_dim)
-    moe_top, moe_bottom = [
-        call(sum_kernel, [(half_shape, BF16)], own, *arrived)[0]
-        for own, arrived in zip(part_at[0], ring.scatter(part_at))
-    ]
+    from_left, from_right, _ = ring.scatter(part_at["ends"], part_at)
+    halves = [((mid, feature_dim), BF16)] * 2
+    moe_top, moe_bottom = call(sum_kernel, halves, part_at[0], from_left, from_right)
 
     norm_at, mean_at = {}, {}
 
@@ -484,13 +468,9 @@
     back_at = {}
 
     def backward(distances):
-        if distances == (ring.half,):
-            outs = [((mid, feature_dim), BF16)] * 2
-        else:
-            outs = [(block, F32)] * len(distances)
         result = call(
             functools.partial(backward_kernel, distances),
-            outs,
+            part_outs(distances),
             *norm_at[distances],
             *saved_at[distances],
             pooled_grad,
@@ -499,21 +479,18 @@
             down_t,
             flops=flops * len(distances),
         )
-        if distances == (ring.half,):
-            back_at["ends"] = result
-        else:
-            back_at.update(zip(distances, result))
+        keep_parts(back_at, distances, result)
 
     for distances in reversed(list(tokens_at)):
         backward(distances)
-    left, right, last = ring.scatter_whole(back_at["ends"], back_at)
+    from_left, from_right, last = ring.scatter(back_at["ends"], back_at)
     token_grad = pl.pallas_call(
         sum_kernel,
         out_shape=jax.ShapeDtypeStruct(block, BF16),
         in_specs=[pl.BlockSpec(memory_space=pltpu.VMEM)] * 3,
         out_specs=pl.BlockSpec(memory_space=pltpu.VMEM),
         compiler_params=pltpu.CompilerParams(vmem_limit_bytes=VMEM_LIMIT),
-    )(back_at[0], left, right)
+    )(back_at[0], from_left, from_right)
 
     both = after(jnp.concatenate([pooled, logit_grad], axis=1), last)
     if group_count == 2:

time: 126 us -> 135 us (1.071)
  waiting for transfers between devices: 38.8 us -> 57.2 us
  starting transfers between devices: 62.4 us -> 53 us
    ppermute x50 -> x44, waiting for transfers between devices: 34.5 us -> 49.8 us  [send(): return lax.ppermute(value, 'expert', pairs)]
    ppermute x50 -> x44, starting transfers between devices: 57.2 us -> 47.8 us  [send(): return lax.ppermute(value, 'expert', pairs)]
    ppermute x4, waiting for transfers between devices: 4.24 us -> 6.15 us  [body(): pooled_grad = pooled_grad + lax.ppermute(mine, 'expert', pairs).astype(F32)]
    pallas_call x35 -> x30, Pallas kernels: 17.3 us -> 17.2 us  [call(): pl.pallas_call(kernel, out_shape=[pltpu.VMEM(shape, dtype) for shape, dty...]
  transfers between devices with their start and end apart: 56 -> 50, of which waited for: 28 -> 30; matrix products, arithmetic and copies ran while one was open for 1% -> 1% of each run, Pallas kernels for 14% -> 13%
where the time goes in v11:
time: 135 us
  waiting for transfers between devices  57.2 us (42%)
  starting transfers between devices  53 us (39%)
  Pallas kernels  21.6 us (16%)
  matrix products  1.71 us (1%)
    ppermute x44, waiting for transfers between devices, send(): return lax.ppermute(value, 'expert', pairs)  49.8 us
    ppermute x44, starting transfers between devices, send(): return lax.ppermute(value, 'expert', pairs)  47.8 us
    pallas_call x30, Pallas kernels, call(): pl.pallas_call(kernel, out_shape=[pltpu.VMEM(shape, dtype) for shape, dty...  17.2 us
    ppermute x4, waiting for transfers between devices, body(): pooled_grad = pooled_grad + lax.ppermute(mine, 'expert', pairs).astype(F32)  6.15 us
    ppermute x4, starting transfers between devices, body(): pooled_grad = pooled_grad + lax.ppermute(mine, 'expert', pairs).astype(F32)  4.64 us
  transfers between devices with their start and end apart: 50, of which 30 were waited for; matrix products, arithmetic and copies ran while one was open for 1% of the time, Pallas kernels for 13%

profile of v11, /device:TPU:0, one launch (start us, length us, event | category | flops | bytes accessed | tf_op | source)
XLA Modules:
  0.0 134.6 jit_solution(15187300644925648844)
XLA Ops:
  0.6 1.9 %shard_map.104 = (bf16[64,1152]{1,0:T(8,128)(2,1)S(1)}, bf16[64,1024]{1,0:T(8,128)(2,1)S(1)}, bf16[3200,384]{1,0:T(8,128)(2,1)S(1)}) custom-call(s32[8,128]{1,0:T(8,128)} %bitcast.19, f32[8,128]{1,0:T(8,128)} %bitcast.20, bf16[128,1024]{1,0:T(8,128)(2,1)} %refs_2_.2, bf16[2,512,384]{2,1,0:T(8,128)(2,1)} %refs_0_.1, bf16[2,512,384]{2,1,0:T(8,128)(2,1)} %refs_1_.1, ...), custom_call_target="tpu_custom_call" | custom-call | tf_op jit(solution)/shard_map/pallas_call | solution.py:217
  3.1 2.6 %collective-permute-start.1 = (bf16[64,1152]{1,0:T(8,128)(2,1)S(1)}, bf16[64,1152]{1,0:T(8,128)(2,1)S(1)}, u32[]{:S(2)}, u32[]{:S(2)}) collective-permute-start(bf16[64,1152]{1,0:T(8,128)(2,1)S(1)} %get-tuple-element.51.refs_0_), channel_id=1, source_target_pairs={{0,4},{4,8},{8,12},{12,14},{14,10},{10,6},{6,2},{2,0},{1,5},{5,9},... | collective-permute-start | bytes 442376 | tf_op jit(solution)/shard_map/ppermute | solution.py:68
  5.7 4.4 %collective-permute-done.1.refs_0_ = bf16[64,1152]{1,0:T(8,128)(2,1)S(1)} collective-permute-done((bf16[64,1152]{1,0:T(8,128)(2,1)S(1)}, bf16[64,1152]{1,0:T(8,128)(2,1)S(1)}, u32[]{:S(2)}, u32[]{:S(2)}) %collective-permute-start.1) | collective-permute-done | bytes 147488 | tf_op jit(solution)/shard_map/ppermute | solution.py:68
  10.1 1.8 %collective-permute-start.5 = (bf16[64,1152]{1,0:T(8,128)(2,1)S(1)}, bf16[64,1152]{1,0:T(8,128)(2,1)S(1)}, u32[]{:S(2)}, u32[]{:S(2)}) collective-permute-start(bf16[64,1152]{1,0:T(8,128)(2,1)S(1)} %collective-permute-done.1.refs_0_), channel_id=1, source_target_pairs={{0,4},{4,8},{8,12},{12,14},{14,10},{10,6},{6,2},{2,0},{1,5},{5,9},... | collective-permute-start | bytes 442376 | tf_op jit(solution)/shard_map/ppermute | solution.py:68
  12.1 1.7 %collective-permute-start.8 = (bf16[64,1024]{1,0:T(8,128)(2,1)S(1)}, bf16[64,1024]{1,0:T(8,128)(2,1)S(1)}, u32[]{:S(2)}, u32[]{:S(2)}) collective-permute-start(bf16[64,1024]{1,0:T(8,128)(2,1)S(1)} %collective-permute-done.4.refs_3_), channel_id=1, source_target_pairs={{0,2},{4,0},{8,4},{12,8},{14,12},{10,14},{6,10},{2,6},{1,3},{5,1},... | collective-permute-start | bytes 393224 | tf_op jit(solution)/shard_map/ppermute | solution.py:68
  14.2 2.0 %collective-permute-done.5.refs_0_ = bf16[64,1152]{1,0:T(8,128)(2,1)S(1)} collective-permute-done((bf16[64,1152]{1,0:T(8,128)(2,1)S(1)}, bf16[64,1152]{1,0:T(8,128)(2,1)S(1)}, u32[]{:S(2)}, u32[]{:S(2)}) %collective-permute-start.5) | collective-permute-done | bytes 147488 | tf_op jit(solution)/shard_map/ppermute | solution.py:68
  16.2 2.5 %collective-permute-start.9 = (bf16[64,1152]{1,0:T(8,128)(2,1)S(1)}, bf16[64,1152]{1,0:T(8,128)(2,1)S(1)}, u32[]{:S(2)}, u32[]{:S(2)}) collective-permute-start(bf16[64,1152]{1,0:T(8,128)(2,1)S(1)} %collective-permute-done.5.refs_0_), channel_id=1, source_target_pairs={{0,4},{4,8},{8,12},{12,14},{14,10},{10,6},{6,2},{2,0},{1,5},{5,9},... | collective-permute-start | bytes 442376 | tf_op jit(solution)/shard_map/ppermute | solution.py:68
  22.3 2.4 %collective-permute-start.13 = (bf16[64,1152]{1,0:T(8,128)(2,1)S(1)}, bf16[64,1152]{1,0:T(8,128)(2,1)S(1)}, u32[]{:S(2)}, u32[]{:S(2)}) collective-permute-start(bf16[64,1152]{1,0:T(8,128)(2,1)S(1)} %collective-permute-done.9.refs_0_), channel_id=1, source_target_pairs={{0,4},{4,8},{8,12},{12,14},{14,10},{10,6},{6,2},{2,0},{1,5},{5,9},... | collective-permute-start | bytes 442376 | tf_op jit(solution)/shard_map/ppermute | solution.py:68
  29.3 1.7 %shard_map.105 = (bf16[1024,1536]{1,0:T(8,128)(2,1)S(1)}, bf16[768,1024]{1,0:T(8,128)(2,1)S(1)}) custom-call(bf16[2,512,384]{2,1,0:T(8,128)(2,1)} %refs_0_.1, bf16[2,512,384]{2,1,0:T(8,128)(2,1)} %refs_1_.1, bf16[2,192,1024]{2,1,0:T(8,128)(2,1)} %refs_2_.3, bf16[3200,384]{1,0:T(8,128)(2,1)S(1)} %collective-permute-done.refs_3_), custom_call_target="tpu_custom_call" | custom-call | tf_op jit(solution)/shard_map/pallas_call | solution.py:272
  33.6 1.6 %collective-permute-start.15 = (bf16[64,1024]{1,0:T(8,128)(2,1)S(1)}, bf16[64,1024]{1,0:T(8,128)(2,1)S(1)}, u32[]{:S(2)}, u32[]{:S(2)}) collective-permute-start(bf16[64,1024]{1,0:T(8,128)(2,1)S(1)} %shard_map.111), channel_id=1, source_target_pairs={{0,4},{4,8},{8,12},{12,14},{14,10},{10,6},{6,2},{2,0},{1,5},{5,9},... | collective-permute-start | bytes 393224 | tf_op jit(solution)/shard_map/ppermute | solution.py:68
  40.0 1.6 %collective-permute-start.16 = (bf16[128,1024]{1,0:T(8,128)(2,1)S(1)}, bf16[128,1024]{1,0:T(8,128)(2,1)S(1)}, u32[]{:S(2)}, u32[]{:S(2)}) collective-permute-start(bf16[128,1024]{1,0:T(8,128)(2,1)S(1)} %shard_map.112), channel_id=1, source_target_pairs={{0,4},{4,8},{8,12},{12,14},{14,10},{10,6},{6,2},{2,0},{1,5},{5,9},... | collective-permute-start | bytes 786440 | tf_op jit(solution)/shard_map/ppermute | solution.py:68
  43.1 5.8 %collective-permute-done.16.arrived_ref = bf16[128,1024]{1,0:T(8,128)(2,1)S(1)} collective-permute-done((bf16[128,1024]{1,0:T(8,128)(2,1)S(1)}, bf16[128,1024]{1,0:T(8,128)(2,1)S(1)}, u32[]{:S(2)}, u32[]{:S(2)}) %collective-permute-start.16) | collective-permute-done | bytes 262176 | tf_op jit(solution)/shard_map/ppermute | solution.py:68
  49.0 1.7 %collective-permute-start.17 = (bf16[128,1024]{1,0:T(8,128)(2,1)S(1)}, bf16[128,1024]{1,0:T(8,128)(2,1)S(1)}, u32[]{:S(2)}, u32[]{:S(2)}) collective-permute-start(bf16[128,1024]{1,0:T(8,128)(2,1)S(1)} %shard_map.113), channel_id=1, source_target_pairs={{0,4},{4,8},{8,12},{12,14},{14,10},{10,6},{6,2},{2,0},{1,5},{5,9},... | collective-permute-start | bytes 786440 | tf_op jit(solution)/shard_map/ppermute | solution.py:68
  51.4 6.2 %collective-permute-done.17.arrived_ref = bf16[128,1024]{1,0:T(8,128)(2,1)S(1)} collective-permute-done((bf16[128,1024]{1,0:T(8,128)(2,1)S(1)}, bf16[128,1024]{1,0:T(8,128)(2,1)S(1)}, u32[]{:S(2)}, u32[]{:S(2)}) %collective-permute-start.17) | collective-permute-done | bytes 262176 | tf_op jit(solution)/shard_map/ppermute | solution.py:68
  57.7 1.6 %collective-permute-start.18 = (bf16[128,1024]{1,0:T(8,128)(2,1)S(1)}, bf16[128,1024]{1,0:T(8,128)(2,1)S(1)}, u32[]{:S(2)}, u32[]{:S(2)}) collective-permute-start(bf16[128,1024]{1,0:T(8,128)(2,1)S(1)} %shard_map.114), channel_id=1, source_target_pairs={{0,4},{4,8},{8,12},{12,14},{14,10},{10,6},{6,2},{2,0},{1,5},{5,9},... | collective-permute-start | bytes 786440 | tf_op jit(solution)/shard_map/ppermute | solution.py:68
  59.8 7.0 %collective-permute-done.18.left_ref = bf16[128,1024]{1,0:T(8,128)(2,1)S(1)} collective-permute-done((bf16[128,1024]{1,0:T(8,128)(2,1)S(1)}, bf16[128,1024]{1,0:T(8,128)(2,1)S(1)}, u32[]{:S(2)}, u32[]{:S(2)}) %collective-permute-start.18) | collective-permute-done | bytes 262176 | tf_op jit(solution)/shard_map/ppermute | solution.py:68
  72.4 1.8 %collective-permute-done.23.refs_4_ = bf16[64,1024]{1,0:T(8,128)(2,1)S(1)} collective-permute-done((bf16[64,1024]{1,0:T(8,128)(2,1)S(1)}, bf16[64,1024]{1,0:T(8,128)(2,1)S(1)}, u32[]{:S(2)}, u32[]{:S(2)}) %collective-permute-start.23) | collective-permute-done | bytes 131104 | tf_op jit(solution)/shard_map/ppermute | solution.py:68
  89.2 1.9 %collective-permute-done.30.refs_3_ = bf16[64,1024]{1,0:T(8,128)(2,1)S(1)} collective-permute-done((bf16[64,1024]{1,0:T(8,128)(2,1)S(1)}, bf16[64,1024]{1,0:T(8,128)(2,1)S(1)}, u32[]{:S(2)}, u32[]{:S(2)}) %collective-permute-start.30) | collective-permute-done | bytes 131104 | tf_op jit(solution)/shard_map/ppermute | solution.py:68
  91.9 3.8 %collective-permute-done.37 = bf16[8,1024]{1,0:T(8,128)(2,1)S(1)} collective-permute-done((bf16[8,1024]{1,0:T(8,128)(2,1)S(1)}, bf16[8,1024]{1,0:T(8,128)(2,1)S(1)}, u32[]{:S(2)}, u32[]{:S(2)}) %collective-permute-start.37) | collective-permute-done | bytes 16416 | tf_op jit(solution)/shard_map/ppermute | solution.py:441
  96.9 1.8 %collective-permute-start.39 = (bf16[8,1024]{1,0:T(8,128)(2,1)S(1)}, bf16[8,1024]{1,0:T(8,128)(2,1)S(1)}, u32[]{:S(2)}, u32[]{:S(2)}) collective-permute-start(bf16[8,1024]{1,0:T(8,128)(2,1)S(1)} %add_convert_fusion), channel_id=1, source_target_pairs={{0,8},{2,10},{4,12},{6,14},{8,0},{10,2},{12,4},{14,6},{1,9},{3,11}... | collective-permute-start | bytes 49160 | tf_op jit(solution)/shard_map/ppermute | solution.py:441
  102.0 2.4 %collective-permute-done.40 = bf16[8,1024]{1,0:T(8,128)(2,1)S(1)} collective-permute-done((bf16[8,1024]{1,0:T(8,128)(2,1)S(1)}, bf16[8,1024]{1,0:T(8,128)(2,1)S(1)}, u32[]{:S(2)}, u32[]{:S(2)}) %collective-permute-start.40) | collective-permute-done | bytes 16416 | tf_op jit(solution)/shard_map/ppermute | solution.py:441
  115.6 2.5 %collective-permute-done.46.arrived_ref = bf16[128,1024]{1,0:T(8,128)(2,1)S(1)} collective-permute-done((bf16[128,1024]{1,0:T(8,128)(2,1)S(1)}, bf16[128,1024]{1,0:T(8,128)(2,1)S(1)}, u32[]{:S(2)}, u32[]{:S(2)}) %collective-permute-start.46) | collective-permute-done | bytes 262176 | tf_op jit(solution)/shard_map/ppermute | solution.py:68
  122.1 2.5 %collective-permute-done.47.arrived_ref = bf16[128,1024]{1,0:T(8,128)(2,1)S(1)} collective-permute-done((bf16[128,1024]{1,0:T(8,128)(2,1)S(1)}, bf16[128,1024]{1,0:T(8,128)(2,1)S(1)}, u32[]{:S(2)}, u32[]{:S(2)}) %collective-permute-start.47) | collective-permute-done | bytes 262176 | tf_op jit(solution)/shard_map/ppermute | solution.py:68
  131.1 2.7 %collective-permute-done.44.left_ref = bf16[128,1024]{1,0:T(8,128)(2,1)S(1)} collective-permute-done((bf16[128,1024]{1,0:T(8,128)(2,1)S(1)}, bf16[128,1024]{1,0:T(8,128)(2,1)S(1)}, u32[]{:S(2)}, u32[]{:S(2)}) %collective-permute-start.44) | collective-permute-done | bytes 262176 | tf_op jit(solution)/shard_map/ppermute | solution.py:68
  (126 shorter events, 67.4 us)
Async XLA Ops:
  2.6 26.7 %collective-permute-start = (bf16[3200,384]{1,0:T(8,128)(2,1)S(1)}, bf16[3200,384]{1,0:T(8,128)(2,1)S(1)}, u32[]{:S(2)}, u32[]{:S(2)}) collective-permute-start(bf16[3200,384]{1,0:T(8,128)(2,1)S(1)} %get-tuple-element.53), channel_id=1, source_target_pairs={{0,1},{1,0},{2,3},{3,2},{4,5},{5,4},{6,7},{7,6},{8,9},{9,8},{10,11... | collective-permute-start | bytes 7372808 | tf_op jit(solution)/shard_map/ppermute | solution.py:312
  3.1 7.0 %collective-permute-start.1 = (bf16[64,1152]{1,0:T(8,128)(2,1)S(1)}, bf16[64,1152]{1,0:T(8,128)(2,1)S(1)}, u32[]{:S(2)}, u32[]{:S(2)}) collective-permute-start(bf16[64,1152]{1,0:T(8,128)(2,1)S(1)} %get-tuple-element.51.refs_0_), channel_id=1, source_target_pairs={{0,4},{4,8},{8,12},{12,14},{14,10},{10,6},{6,2},{2,0},{1,5},{5,9},... | collective-permute-start | bytes 442376 | tf_op jit(solution)/shard_map/ppermute | solution.py:68
  11.9 8.3 %collective-permute-start.3 = (bf16[64,1152]{1,0:T(8,128)(2,1)S(1)}, bf16[64,1152]{1,0:T(8,128)(2,1)S(1)}, u32[]{:S(2)}, u32[]{:S(2)}) collective-permute-start(bf16[64,1152]{1,0:T(8,128)(2,1)S(1)} %get-tuple-element.51.refs_0_), channel_id=1, source_target_pairs={{0,2},{4,0},{8,4},{12,8},{14,12},{10,14},{6,10},{2,6},{1,3},{5,1},... | collective-permute-start | bytes 442376 | tf_op jit(solution)/shard_map/ppermute | solution.py:68
  12.1 7.7 %collective-permute-start.8 = (bf16[64,1024]{1,0:T(8,128)(2,1)S(1)}, bf16[64,1024]{1,0:T(8,128)(2,1)S(1)}, u32[]{:S(2)}, u32[]{:S(2)}) collective-permute-start(bf16[64,1024]{1,0:T(8,128)(2,1)S(1)} %collective-permute-done.4.refs_3_), channel_id=1, source_target_pairs={{0,2},{4,0},{8,4},{12,8},{14,12},{10,14},{6,10},{2,6},{1,3},{5,1},... | collective-permute-start | bytes 393224 | tf_op jit(solution)/shard_map/ppermute | solution.py:68
  13.9 7.9 %collective-permute-start.2 = (bf16[64,1024]{1,0:T(8,128)(2,1)S(1)}, bf16[64,1024]{1,0:T(8,128)(2,1)S(1)}, u32[]{:S(2)}, u32[]{:S(2)}) collective-permute-start(bf16[64,1024]{1,0:T(8,128)(2,1)S(1)} %get-tuple-element.52.refs_1_), channel_id=1, source_target_pairs={{0,4},{4,8},{8,12},{12,14},{14,10},{10,6},{6,2},{2,0},{1,5},{5,9},... | collective-permute-start | bytes 393224 | tf_op jit(solution)/shard_map/ppermute | solution.py:68
  20.3 8.6 %collective-permute-start.7 = (bf16[64,1152]{1,0:T(8,128)(2,1)S(1)}, bf16[64,1152]{1,0:T(8,128)(2,1)S(1)}, u32[]{:S(2)}, u32[]{:S(2)}) collective-permute-start(bf16[64,1152]{1,0:T(8,128)(2,1)S(1)} %collective-permute-done.3.refs_2_), channel_id=1, source_target_pairs={{0,2},{4,0},{8,4},{12,8},{14,12},{10,14},{6,10},{2,6},{1,3},{5,1},... | collective-permute-start | bytes 442376 | tf_op jit(solution)/shard_map/ppermute | solution.py:68
  22.3 10.3 %collective-permute-start.13 = (bf16[64,1152]{1,0:T(8,128)(2,1)S(1)}, bf16[64,1152]{1,0:T(8,128)(2,1)S(1)}, u32[]{:S(2)}, u32[]{:S(2)}) collective-permute-start(bf16[64,1152]{1,0:T(8,128)(2,1)S(1)} %collective-permute-done.9.refs_0_), channel_id=1, source_target_pairs={{0,4},{4,8},{8,12},{12,14},{14,10},{10,6},{6,2},{2,0},{1,5},{5,9},... | collective-permute-start | bytes 442376 | tf_op jit(solution)/shard_map/ppermute | solution.py:68
  25.7 6.9 %collective-permute-start.14 = (bf16[64,1024]{1,0:T(8,128)(2,1)S(1)}, bf16[64,1024]{1,0:T(8,128)(2,1)S(1)}, u32[]{:S(2)}, u32[]{:S(2)}) collective-permute-start(bf16[64,1024]{1,0:T(8,128)(2,1)S(1)} %collective-permute-done.12.refs_3_), channel_id=1, source_target_pairs={{0,2},{4,0},{8,4},{12,8},{14,12},{10,14},{6,10},{2,6},{1,3},{5,1},... | collective-permute-start | bytes 393224 | tf_op jit(solution)/shard_map/ppermute | solution.py:68
  27.1 10.0 %collective-permute-start.10 = (bf16[64,1024]{1,0:T(8,128)(2,1)S(1)}, bf16[64,1024]{1,0:T(8,128)(2,1)S(1)}, u32[]{:S(2)}, u32[]{:S(2)}) collective-permute-start(bf16[64,1024]{1,0:T(8,128)(2,1)S(1)} %collective-permute-done.6.refs_1_), channel_id=1, source_target_pairs={{0,4},{4,8},{8,12},{12,14},{14,10},{10,6},{6,2},{2,0},{1,5},{5,9},... | collective-permute-start | bytes 393224 | tf_op jit(solution)/shard_map/ppermute | solution.py:68
  28.8 8.3 %collective-permute-start.11 = (bf16[64,1152]{1,0:T(8,128)(2,1)S(1)}, bf16[64,1152]{1,0:T(8,128)(2,1)S(1)}, u32[]{:S(2)}, u32[]{:S(2)}) collective-permute-start(bf16[64,1152]{1,0:T(8,128)(2,1)S(1)} %collective-permute-done.7.refs_2_), channel_id=1, source_target_pairs={{0,2},{4,0},{8,4},{12,8},{14,12},{10,14},{6,10},{2,6},{1,3},{5,1},... | collective-permute-start | bytes 442376 | tf_op jit(solution)/shard_map/ppermute | solution.py:68
  40.0 9.0 %collective-permute-start.16 = (bf16[128,1024]{1,0:T(8,128)(2,1)S(1)}, bf16[128,1024]{1,0:T(8,128)(2,1)S(1)}, u32[]{:S(2)}, u32[]{:S(2)}) collective-permute-start(bf16[128,1024]{1,0:T(8,128)(2,1)S(1)} %shard_map.112), channel_id=1, source_target_pairs={{0,4},{4,8},{8,12},{12,14},{14,10},{10,6},{6,2},{2,0},{1,5},{5,9},... | collective-permute-start | bytes 786440 | tf_op jit(solution)/shard_map/ppermute | solution.py:68
  41.6 9.2 %collective-permute-start.20 = (bf16[128,1024]{1,0:T(8,128)(2,1)S(1)}, bf16[128,1024]{1,0:T(8,128)(2,1)S(1)}, u32[]{:S(2)}, u32[]{:S(2)}) collective-permute-start(bf16[128,1024]{1,0:T(8,128)(2,1)S(1)} %shard_map.115), channel_id=1, source_target_pairs={{0,2},{4,0},{8,4},{12,8},{14,12},{10,14},{6,10},{2,6},{1,3},{5,1},... | collective-permute-start | bytes 786440 | tf_op jit(solution)/shard_map/ppermute | solution.py:68
  49.0 8.6 %collective-permute-start.17 = (bf16[128,1024]{1,0:T(8,128)(2,1)S(1)}, bf16[128,1024]{1,0:T(8,128)(2,1)S(1)}, u32[]{:S(2)}, u32[]{:S(2)}) collective-permute-start(bf16[128,1024]{1,0:T(8,128)(2,1)S(1)} %shard_map.113), channel_id=1, source_target_pairs={{0,4},{4,8},{8,12},{12,14},{14,10},{10,6},{6,2},{2,0},{1,5},{5,9},... | collective-permute-start | bytes 786440 | tf_op jit(solution)/shard_map/ppermute | solution.py:68
  50.9 8.5 %collective-permute-start.21 = (bf16[128,1024]{1,0:T(8,128)(2,1)S(1)}, bf16[128,1024]{1,0:T(8,128)(2,1)S(1)}, u32[]{:S(2)}, u32[]{:S(2)}) collective-permute-start(bf16[128,1024]{1,0:T(8,128)(2,1)S(1)} %shard_map.116), channel_id=1, source_target_pairs={{0,2},{4,0},{8,4},{12,8},{14,12},{10,14},{6,10},{2,6},{1,3},{5,1},... | collective-permute-start | bytes 786440 | tf_op jit(solution)/shard_map/ppermute | solution.py:68
  57.7 9.2 %collective-permute-start.18 = (bf16[128,1024]{1,0:T(8,128)(2,1)S(1)}, bf16[128,1024]{1,0:T(8,128)(2,1)S(1)}, u32[]{:S(2)}, u32[]{:S(2)}) collective-permute-start(bf16[128,1024]{1,0:T(8,128)(2,1)S(1)} %shard_map.114), channel_id=1, source_target_pairs={{0,4},{4,8},{8,12},{12,14},{14,10},{10,6},{6,2},{2,0},{1,5},{5,9},... | collective-permute-start | bytes 786440 | tf_op jit(solution)/shard_map/ppermute | solution.py:68
  59.4 8.9 %collective-permute-start.22 = (bf16[128,1024]{1,0:T(8,128)(2,1)S(1)}, bf16[128,1024]{1,0:T(8,128)(2,1)S(1)}, u32[]{:S(2)}, u32[]{:S(2)}) collective-permute-start(bf16[128,1024]{1,0:T(8,128)(2,1)S(1)} %shard_map.117), channel_id=1, source_target_pairs={{0,2},{4,0},{8,4},{12,8},{14,12},{10,14},{6,10},{2,6},{1,3},{5,1},... | collective-permute-start | bytes 786440 | tf_op jit(solution)/shard_map/ppermute | solution.py:68
  70.4 6.6 %collective-permute-start.31 = (bf16[64,1024]{1,0:T(8,128)(2,1)S(1)}, bf16[64,1024]{1,0:T(8,128)(2,1)S(1)}, u32[]{:S(2)}, u32[]{:S(2)}) collective-permute-start(bf16[64,1024]{1,0:T(8,128)(2,1)S(1)} %get-tuple-element.66.refs_3_), channel_id=1, source_target_pairs={{0,4},{4,8},{8,12},{12,14},{14,10},{10,6},{6,2},{2,0},{1,5},{5,9},... | collective-permute-start | bytes 393224 | tf_op jit(solution)/shard_map/ppermute | solution.py:68
  71.9 6.6 %collective-permute-start.34 = (bf16[64,1024]{1,0:T(8,128)(2,1)S(1)}, bf16[64,1024]{1,0:T(8,128)(2,1)S(1)}, u32[]{:S(2)}, u32[]{:S(2)}) collective-permute-start(bf16[64,1024]{1,0:T(8,128)(2,1)S(1)} %get-tuple-element.65.refs_2_), channel_id=1, source_target_pairs={{0,2},{4,0},{8,4},{12,8},{14,12},{10,14},{6,10},{2,6},{1,3},{5,1},... | collective-permute-start | bytes 393224 | tf_op jit(solution)/shard_map/ppermute | solution.py:68
  107.9 6.5 %collective-permute-start.41 = (bf16[64,1024]{1,0:T(8,128)(2,1)S(1)}, bf16[64,1024]{1,0:T(8,128)(2,1)S(1)}, u32[]{:S(2)}, u32[]{:S(2)}) collective-permute-start(bf16[64,1024]{1,0:T(8,128)(2,1)S(1)} %shard_map.131), channel_id=1, source_target_pairs={{0,4},{4,8},{8,12},{12,14},{14,10},{10,6},{6,2},{2,0},{1,5},{5,9},... | collective-permute-start | bytes 393224 | tf_op jit(solution)/shard_map/ppermute | solution.py:68
  111.7 6.4 %collective-permute-start.46 = (bf16[128,1024]{1,0:T(8,128)(2,1)S(1)}, bf16[128,1024]{1,0:T(8,128)(2,1)S(1)}, u32[]{:S(2)}, u32[]{:S(2)}) collective-permute-start(bf16[128,1024]{1,0:T(8,128)(2,1)S(1)} %shard_map.135), channel_id=1, source_target_pairs={{0,2},{4,0},{8,4},{12,8},{14,12},{10,14},{6,10},{2,6},{1,3},{5,1},... | collective-permute-start | bytes 786440 | tf_op jit(solution)/shard_map/ppermute | solution.py:68
  114.4 6.4 %collective-permute-start.42 = (bf16[128,1024]{1,0:T(8,128)(2,1)S(1)}, bf16[128,1024]{1,0:T(8,128)(2,1)S(1)}, u32[]{:S(2)}, u32[]{:S(2)}) collective-permute-start(bf16[128,1024]{1,0:T(8,128)(2,1)S(1)} %shard_map.132), channel_id=1, source_target_pairs={{0,4},{4,8},{8,12},{12,14},{14,10},{10,6},{6,2},{2,0},{1,5},{5,9},... | collective-permute-start | bytes 786440 | tf_op jit(solution)/shard_map/ppermute | solution.py:68
  118.2 6.4 %collective-permute-start.47 = (bf16[128,1024]{1,0:T(8,128)(2,1)S(1)}, bf16[128,1024]{1,0:T(8,128)(2,1)S(1)}, u32[]{:S(2)}, u32[]{:S(2)}) collective-permute-start(bf16[128,1024]{1,0:T(8,128)(2,1)S(1)} %shard_map.136), channel_id=1, source_target_pairs={{0,2},{4,0},{8,4},{12,8},{14,12},{10,14},{6,10},{2,6},{1,3},{5,1},... | collective-permute-start | bytes 786440 | tf_op jit(solution)/shard_map/ppermute | solution.py:68
  120.9 6.4 %collective-permute-start.43 = (bf16[128,1024]{1,0:T(8,128)(2,1)S(1)}, bf16[128,1024]{1,0:T(8,128)(2,1)S(1)}, u32[]{:S(2)}, u32[]{:S(2)}) collective-permute-start(bf16[128,1024]{1,0:T(8,128)(2,1)S(1)} %shard_map.133), channel_id=1, source_target_pairs={{0,4},{4,8},{8,12},{12,14},{14,10},{10,6},{6,2},{2,0},{1,5},{5,9},... | collective-permute-start | bytes 786440 | tf_op jit(solution)/shard_map/ppermute | solution.py:68
  124.7 6.4 %collective-permute-start.48 = (bf16[128,1024]{1,0:T(8,128)(2,1)S(1)}, bf16[128,1024]{1,0:T(8,128)(2,1)S(1)}, u32[]{:S(2)}, u32[]{:S(2)}) collective-permute-start(bf16[128,1024]{1,0:T(8,128)(2,1)S(1)} %shard_map.137), channel_id=1, source_target_pairs={{0,2},{4,0},{8,4},{12,8},{14,12},{10,14},{6,10},{2,6},{1,3},{5,1},... | collective-permute-start | bytes 786440 | tf_op jit(solution)/shard_map/ppermute | solution.py:68
  (29 other events, 290.5 us)

commit v12 on v11

--- a/solution.py
+++ b/solution.py
@@ -36,21 +36,6 @@
     )(*args)
 
 
-def after(value, guard):
-    def kernel(value_ref, guard_ref, out_ref):
-        pass
-
-    args = [pltpu.with_memory_space_constraint(a, pltpu.VMEM) for a in (value, guard)]
-    return pl.pallas_call(
-        kernel,
-        out_shape=pltpu.VMEM(value.shape, value.dtype),
-        in_specs=[pl.BlockSpec(memory_space=pltpu.VMEM)] * 2,
-        out_specs=pl.BlockSpec(memory_space=pltpu.VMEM),
-        input_output_aliases={0: 0},
-        compiler_params=pltpu.CompilerParams(vmem_limit_bytes=VMEM_LIMIT),
-    )(*args)
-
-
 class Ring:
     def __init__(self, expert_count, group_count):
         self.count = expert_count
@@ -97,32 +82,21 @@
             out_ref[added, :] = (block_ref[added, :] + arrived_ref[...].astype(F32)).astype(BF16)
             out_ref[kept, :] = block_ref[kept, :].astype(BF16)
 
-        def right_kernel(first, block_ref, arrived_ref, guard_ref, out_ref):
-            if arrived_ref.shape[0] == mid:
-                half_kernel(first, block_ref, arrived_ref, out_ref)
-            else:
-                add_kernel(block_ref, arrived_ref, out_ref)
-
-        most = self.half - 1
-        from_right = self.send(ends[1], -1)
-        from_left = self.send(after(ends[0], parts[max(most - 1, 0)]), 1)
-        for step in range(most, 0, -1):
+        from_right, from_left = self.send(ends[1], -1), self.send(ends[0], 1)
+        for step in range(self.half - 1, 0, -1):
+            kernels = [add_kernel, add_kernel]
+            if step == self.half - 1:
+                kernels = [functools.partial(half_kernel, first) for first in (mid, 0)]
             shape = [(parts[step].shape, BF16)]
-            kernel = functools.partial(half_kernel, mid) if step == most else add_kernel
-            leftward = call(kernel, shape, parts[-step], from_right)[0]
+            leftward = call(kernels[0], shape, parts[-step], from_right)[0]
             from_right = self.send(leftward, -1)
-            kernel = functools.partial(right_kernel, 0)
-            rightward = call(kernel, shape, parts[step], from_left, parts[max(step - 2, 0)])[0]
+            rightward = call(kernels[1], shape, parts[step], from_left)[0]
             from_left = self.send(rightward, 1)
-        return from_left, from_right, rightward
+        return from_left, from_right
 
 
 def add_kernel(block_ref, arrived_ref, out_ref):
     out_ref[...] = (block_ref[...] + arrived_ref[...].astype(F32)).astype(BF16)
-
-
-def add(block, arrived):
-    return call(add_kernel, [(block.shape, BF16)], block, arrived)[0]
 
 
 def sum_kernel(own_ref, left_ref, right_ref, *outs):
@@ -316,91 +290,95 @@
         packed = None
     wide, down = full_weights(shards, packed)
 
-    def rows_of(refs):
-        return jnp.concatenate([ref[...] for ref in refs], axis=0) if len(refs) > 1 else refs[0][...]
-
-    def forward_kernel(count, *refs):
-        token_refs, (wide_ref, down_ref) = refs[:count], refs[count : count + 2]
-        outs = refs[count + 2 :]
-        x = rows_of([ref.at[:, :feature_dim] for ref in token_refs])
-        weights = jnp.concatenate([ref[:, feature_dim:] for ref in token_refs[::2]], axis=0).astype(F32)
-        lane = lax.broadcasted_iota(jnp.int32, weights.shape, 1)
+    far, bottom_half, top_half = ring.half, "bottom", "top"
+    units = [(bottom_half,), (top_half, 1 - far, far - 1)]
+    units += [(-k, k) for k in range(far - 2, 0, -1)] + [(0,)]
+
+    def half_rows(item):
+        return {top_half: (0,), bottom_half: (1,)}.get(item, (0, 1))
+
+    def distance_of(item):
+        return far if item in (top_half, bottom_half) else item
+
+    def rows_of(unit):
+        return sum(mid * len(half_rows(item)) for item in unit)
+
+    def part_outs(unit):
+        return [
+            ((mid * len(half_rows(item)), feature_dim), F32 if item == distance_of(item) else BF16)
+            for item in unit
+        ]
+
+    def store_parts(total, unit, outs):
+        begin = 0
+        for out in outs:
+            out[...] = total[begin : begin + out.shape[0]].astype(out.dtype)
+            begin += out.shape[0]
+
+    def forward_kernel(unit, *refs):
+        wide_ref, down_ref, gate_save, up_save, *outs = refs[2 * len(unit) :]
+        rows, scales = [], [[] for _ in range(local_experts)]
         quarter = LANES // 4
+        lane = lax.broadcasted_iota(jnp.int32, (mid, LANES), 1)
+        for i, item in enumerate(unit):
+            top_ref, bottom_ref = refs[2 * i : 2 * i + 2]
+            weights = top_ref[:, feature_dim:].astype(F32)
+            for half in half_rows(item):
+                rows.append(bottom_ref[...] if half else top_ref[:, :feature_dim])
+                for local in range(local_experts):
+                    begin = lax.axis_index("expert") * local_experts + local + 2 * quarter * half
+                    here = (lane == begin) | (lane == begin + quarter)
+                    scale = jnp.sum(jnp.where(here, weights, 0.0), axis=1, keepdims=True)
+                    scales[local].append(scale)
+        x = jnp.concatenate(rows, axis=0) if len(rows) > 1 else rows[0]
         hidden = []
         for local in range(local_experts):
-            expert = lax.axis_index("expert") * local_experts + local
-            scales = []
-            for begin in (expert, expert + 2 * quarter):
-                here = (lane == begin) | (lane == begin + quarter)
-                scales.append(jnp.sum(jnp.where(here, weights, 0.0), axis=1, keepdims=True))
-            pieces = [s[i : i + mid] for i in range(0, weights.shape[0], mid) for s in scales]
-            scale = jnp.concatenate(pieces, axis=0)
+            scale = jnp.concatenate(scales[local], axis=0) if len(rows) > 1 else scales[local][0]
             act = dot(x, wide_ref[:, pl.ds(local * pair_dim, pair_dim)])
             gate_act, up_act = act[:, :hidden_dim], act[:, hidden_dim:]
             sigmoid_gate = jax.nn.sigmoid(gate_act)
             silu = gate_act * sigmoid_gate * scale
             slope = sigmoid_gate * (1.0 + gate_act * (1.0 - sigmoid_gate)) * scale
             cols = pl.ds(local * hidden_dim, hidden_dim)
-            outs[0][:, cols] = (up_act * slope).astype(BF16)
-            outs[1][:, cols] = silu.astype(BF16)
+            gate_save[:, cols] = (up_act * slope).astype(BF16)
+            up_save[:, cols] = silu.astype(BF16)
             hidden.append((silu * up_act).astype(BF16))
-        total = dot(jnp.concatenate(hidden, axis=1), down_ref[...])
-        rows = total.shape[0] // len(outs[2:])
-        for i, out in enumerate(outs[2:]):
-            out[...] = total[i * rows : (i + 1) * rows].astype(out.dtype)
+        store_parts(dot(jnp.concatenate(hidden, axis=1), down_ref[...]), unit, outs)
 
     tokens_at, saved_at, part_at = {}, {}, {}
-    flops = 2 * rows_here * feature_dim * hidden_dim * local_experts * 3
+    flops = 2 * feature_dim * hidden_dim * local_experts * 3
 
     def hold(distances, blocks):
-        tokens_at[distances] = blocks
-
-    def part_outs(distances):
-        if distances == (ring.half,):
-            return [((mid, feature_dim), BF16)] * 2
-        return [(block, F32)] * len(distances)
-
-    def keep_parts(parts, distances, results):
-        if distances == (ring.half,):
-            parts["ends"] = results
-        else:
-            parts.update(zip(distances, results))
-
-    def forward(distances):
-        blocks = tokens_at[distances]
-        rows = mid * len(blocks)
-        result = call(
-            functools.partial(forward_kernel, len(blocks)),
-            [((rows, local_experts * hidden_dim), BF16)] * 2 + part_outs(distances),
-            *blocks,
+        tokens_at.update({k: blocks[2 * i : 2 * i + 2] for i, k in enumerate(distances)})
+
+    ring.gather(top, bottom, hold)
+    for unit in units:
+        rows = rows_of(unit)
+        results = call(
+            functools.partial(forward_kernel, unit),
+            [((rows, local_experts * hidden_dim), BF16)] * 2 + part_outs(unit),
+            *[half for item in unit for half in tokens_at[distance_of(item)]],
             wide,
             down,
-            flops=flops * rows // rows_here,
+            flops=flops * rows,
         )
-        saved_at[distances] = result[:2]
-        keep_parts(part_at, distances, result[2:])
-
-    ring.gather(top, bottom, hold)
-    for distances in tokens_at:
-        forward(distances)
+        saved_at[unit] = results[:2]
+        part_at.update(zip(unit, results[2:]))
     gain = norm_gain.reshape(1, feature_dim)
-    from_left, from_right, _ = ring.scatter(part_at["ends"], part_at)
+    from_left, from_right = ring.scatter((part_at[top_half], part_at[bottom_half]), part_at)
     halves = [((mid, feature_dim), BF16)] * 2
     moe_top, moe_bottom = call(sum_kernel, halves, part_at[0], from_left, from_right)
 
     norm_at, mean_at = {}, {}
 
-    def residual_of(token_refs, moe_refs):
-        token_rows = rows_of([ref.at[:, :feature_dim] for ref in token_refs]).astype(F32)
-        return token_rows + rows_of(moe_refs).astype(F32)
-
-    def inv_rms_of(residual):
-        return lax.rsqrt(jnp.mean(residual * residual, axis=-1, keepdims=True) + NORM_EPS)
-
-    def norm_kernel(distances, count, *refs):
-        residual = residual_of(refs[:count], refs[count : 2 * count])
+    def norm_kernel(distances, *refs):
+        count = 2 * len(distances)
+        tokens_here = [ref[:, :feature_dim].astype(F32) for ref in refs[:count]]
+        residual = jnp.concatenate(
+            [rows + ref[...].astype(F32) for rows, ref in zip(tokens_here, refs[count : 2 * count])], axis=0
+        )
         gain_ref, so_far, out_ref, residual_ref, inv_ref = refs[2 * count :]
-        inv_rms = inv_rms_of(residual)
+        inv_rms = lax.rsqrt(jnp.mean(residual * residual, axis=-1, keepdims=True) + NORM_EPS)
         residual_ref[...] = residual
         inv_ref[...] = jnp.broadcast_to(inv_rms, inv_ref.shape)
         normed = residual * inv_rms * gain_ref[...]
@@ -417,14 +395,15 @@
 
     def norm(distances, blocks):
         rows = mid * len(blocks)
-        mean_at["pooled"], *norm_at[distances] = call(
-            functools.partial(norm_kernel, distances, len(blocks)),
+        mean_at["pooled"], *kept = call(
+            functools.partial(norm_kernel, distances),
             [(pooled_shape, F32), ((rows, feature_dim), F32), ((rows, LANES), F32)],
-            *tokens_at[distances],
+            *[half for k in distances for half in tokens_at[k]],
             *blocks,
             gain,
             mean_at["pooled"],
         )
+        norm_at.update({k: (i * rows_here, kept) for i, k in enumerate(distances)})
 
     ring.gather(moe_top, moe_bottom, norm)
     pooled = mean_at["pooled"].astype(BF16)
@@ -440,16 +419,17 @@
             pairs = [(e, e ^ mask) for e in range(expert_count)]
             pooled_grad = pooled_grad + lax.ppermute(mine, "expert", pairs).astype(F32)
 
-    def backward_kernel(distances, residual_ref, inv_ref, gate_save, up_save, *refs):
-        grad_ref, gain_ref, wide_ref, down_ref, *outs = refs
-        residual, inv_rms = residual_ref[...], inv_ref[:, :1]
-        cube = inv_rms * inv_rms * inv_rms
+    def backward_kernel(unit, *refs):
+        gate_save, up_save, grad_ref, gain_ref, wide_ref, down_ref, *outs = refs[2 * len(unit) :]
         parts = []
-        for i, k in enumerate(distances):
-            rows = slice(i * rows_here, (i + 1) * rows_here)
+        for i, item in enumerate(unit):
+            k, some = distance_of(item), half_rows(item)
+            rows = pl.ds(norm_at[k][0] + some[0] * mid, len(some) * mid)
+            residual, inv_rms = refs[2 * i][rows, :], refs[2 * i + 1][rows, :1]
             scaled = gain_ref[...] * grad_ref[pl.ds(ring.device_at(k), 1), :] / rows_here
-            slope = cube[rows] * jnp.mean(residual[rows] * scaled, axis=-1, keepdims=True)
-            parts.append(inv_rms[rows] * scaled - residual[rows] * slope)
+            cube = inv_rms * inv_rms * inv_rms
+            slope = cube * jnp.mean(residual * scaled, axis=-1, keepdims=True)
+            parts.append(inv_rms * scaled - residual * slope)
         resid_grad = jnp.concatenate(parts, axis=0) if len(parts) > 1 else parts[0]
         down_back = dot(resid_grad.astype(BF16), down_ref[...])
         grads = []
@@ -458,41 +438,32 @@
             for save in (gate_save, up_save):
                 grads.append((down_back[:, cols] * save[:, cols].astype(F32)).astype(BF16))
         total = dot(jnp.concatenate(grads, axis=1), wide_ref[...])
-        if distances == (0,):
-            total = total + resid_grad
-        rows = total.shape[0] // len(outs)
-        for i, out in enumerate(outs):
-            out[...] = total[i * rows : (i + 1) * rows].astype(out.dtype)
+        store_parts(total + resid_grad if unit == (0,) else total, unit, outs)
 
     wide_t, down_t = transposed(wide), transposed(down)
     back_at = {}
-
-    def backward(distances):
-        result = call(
-            functools.partial(backward_kernel, distances),
-            part_outs(distances),
-            *norm_at[distances],
-            *saved_at[distances],
+    for unit in units:
+        results = call(
+            functools.partial(backward_kernel, unit),
+            part_outs(unit),
+            *[kept for item in unit for kept in norm_at[distance_of(item)][1]],
+            *saved_at[unit],
             pooled_grad,
             gain,
             wide_t,
             down_t,
-            flops=flops * len(distances),
+            flops=flops * rows_of(unit),
         )
-        keep_parts(back_at, distances, result)
-
-    for distances in reversed(list(tokens_at)):
-        backward(distances)
-    from_left, from_right, last = ring.scatter(back_at["ends"], back_at)
+        back_at.update(zip(unit, results))
     token_grad = pl.pallas_call(
         sum_kernel,
         out_shape=jax.ShapeDtypeStruct(block, BF16),
         in_specs=[pl.BlockSpec(memory_space=pltpu.VMEM)] * 3,
         out_specs=pl.BlockSpec(memory_space=pltpu.VMEM),
         compiler_params=pltpu.CompilerParams(vmem_limit_bytes=VMEM_LIMIT),
-    )(back_at[0], from_left, from_right)
-
-    both = after(jnp.concatenate([pooled, logit_grad], axis=1), last)
+    )(back_at[0], *ring.scatter((back_at[top_half], back_at[bottom_half]), back_at))
+
+    both = jnp.concatenate([pooled, logit_grad], axis=1)
     if group_count == 2:
         both = jnp.concatenate([both, lax.ppermute(both, "group", [(0, 1), (1, 0)])], axis=0)
     else:

time: 135 us -> 133 us (0.985)
  waiting for transfers between devices: 57.2 us -> 53.1 us
  starting transfers between devices: 53 us -> 54.5 us
    ppermute x4, waiting for transfers between devices: 6.15 us -> 4.09 us  [body(): pooled_grad = pooled_grad + lax.ppermute(mine, 'expert', pairs).astype(F32)]
  transfers between devices with their start and end apart: 50 -> 50, of which waited for: 30 -> 35; matrix products, arithmetic and copies ran while one was open for 1% -> 1% of each run, Pallas kernels for 13% -> 12%
where the time goes in v12:
time: 133 us
  starting transfers between devices  54.5 us (41%)
  waiting for transfers between devices  53.1 us (40%)
  Pallas kernels  22.7 us (17%)
  matrix products  1.71 us (1%)
    ppermute x44, starting transfers between devices, send(): return lax.ppermute(value, 'expert', pairs)  49.1 us
    ppermute x44, waiting for transfers between devices, send(): return lax.ppermute(value, 'expert', pairs)  49 us
    pallas_call x30, Pallas kernels, call(): pl.pallas_call(kernel, out_shape=[pltpu.VMEM(shape, dtype) for shape, dty...  18.3 us
    ppermute x4, starting transfers between devices, body(): pooled_grad = pooled_grad + lax.ppermute(mine, 'expert', pairs).astype(F32)  4.91 us
    ppermute x4, waiting for transfers between devices, body(): pooled_grad = pooled_grad + lax.ppermute(mine, 'expert', pairs).astype(F32)  4.09 us
  transfers between devices with their start and end apart: 50, of which 35 were waited for; matrix products, arithmetic and copies ran while one was open for 1% of the time, Pallas kernels for 12%

profile of v12, /device:TPU:0, one launch (start us, length us, event | category | flops | bytes accessed | tf_op | source)
XLA Modules:
  0.0 133.1 jit_solution(12714254552865433427)
XLA Ops:
  0.6 1.9 %shard_map.104 = (bf16[64,1152]{1,0:T(8,128)(2,1)S(1)}, bf16[64,1024]{1,0:T(8,128)(2,1)S(1)}, bf16[3200,384]{1,0:T(8,128)(2,1)S(1)}) custom-call(s32[8,128]{1,0:T(8,128)} %bitcast.19, f32[8,128]{1,0:T(8,128)} %bitcast.20, bf16[128,1024]{1,0:T(8,128)(2,1)} %refs_2_.2, bf16[2,512,384]{2,1,0:T(8,128)(2,1)} %refs_0_.1, bf16[2,512,384]{2,1,0:T(8,128)(2,1)} %refs_1_.1, ...), custom_call_target="tpu_custom_call" | custom-call | tf_op jit(solution)/shard_map/pallas_call | solution.py:191
  3.1 2.6 %collective-permute-start.1 = (bf16[64,1152]{1,0:T(8,128)(2,1)S(1)}, bf16[64,1152]{1,0:T(8,128)(2,1)S(1)}, u32[]{:S(2)}, u32[]{:S(2)}) collective-permute-start(bf16[64,1152]{1,0:T(8,128)(2,1)S(1)} %get-tuple-element.50.refs_0_), channel_id=1, source_target_pairs={{0,4},{4,8},{8,12},{12,14},{14,10},{10,6},{6,2},{2,0},{1,5},{5,9},... | collective-permute-start | bytes 442376 | tf_op jit(solution)/shard_map/ppermute | solution.py:53
  5.7 1.9 %collective-permute-start.3 = (bf16[64,1152]{1,0:T(8,128)(2,1)S(1)}, bf16[64,1152]{1,0:T(8,128)(2,1)S(1)}, u32[]{:S(2)}, u32[]{:S(2)}) collective-permute-start(bf16[64,1152]{1,0:T(8,128)(2,1)S(1)} %get-tuple-element.50.refs_0_), channel_id=1, source_target_pairs={{0,2},{4,0},{8,4},{12,8},{14,12},{10,14},{6,10},{2,6},{1,3},{5,1},... | collective-permute-start | bytes 442376 | tf_op jit(solution)/shard_map/ppermute | solution.py:53
  7.7 2.4 %collective-permute-done.1.refs_0_ = bf16[64,1152]{1,0:T(8,128)(2,1)S(1)} collective-permute-done((bf16[64,1152]{1,0:T(8,128)(2,1)S(1)}, bf16[64,1152]{1,0:T(8,128)(2,1)S(1)}, u32[]{:S(2)}, u32[]{:S(2)}) %collective-permute-start.1) | collective-permute-done | bytes 147488 | tf_op jit(solution)/shard_map/ppermute | solution.py:53
  10.1 1.8 %collective-permute-start.5 = (bf16[64,1152]{1,0:T(8,128)(2,1)S(1)}, bf16[64,1152]{1,0:T(8,128)(2,1)S(1)}, u32[]{:S(2)}, u32[]{:S(2)}) collective-permute-start(bf16[64,1152]{1,0:T(8,128)(2,1)S(1)} %collective-permute-done.1.refs_0_), channel_id=1, source_target_pairs={{0,4},{4,8},{8,12},{12,14},{14,10},{10,6},{6,2},{2,0},{1,5},{5,9},... | collective-permute-start | bytes 442376 | tf_op jit(solution)/shard_map/ppermute | solution.py:53
  14.7 2.1 %collective-permute-done.5.refs_0_ = bf16[64,1152]{1,0:T(8,128)(2,1)S(1)} collective-permute-done((bf16[64,1152]{1,0:T(8,128)(2,1)S(1)}, bf16[64,1152]{1,0:T(8,128)(2,1)S(1)}, u32[]{:S(2)}, u32[]{:S(2)}) %collective-permute-start.5) | collective-permute-done | bytes 147488 | tf_op jit(solution)/shard_map/ppermute | solution.py:53
  16.8 1.9 %collective-permute-start.9 = (bf16[64,1152]{1,0:T(8,128)(2,1)S(1)}, bf16[64,1152]{1,0:T(8,128)(2,1)S(1)}, u32[]{:S(2)}, u32[]{:S(2)}) collective-permute-start(bf16[64,1152]{1,0:T(8,128)(2,1)S(1)} %collective-permute-done.5.refs_0_), channel_id=1, source_target_pairs={{0,4},{4,8},{8,12},{12,14},{14,10},{10,6},{6,2},{2,0},{1,5},{5,9},... | collective-permute-start | bytes 442376 | tf_op jit(solution)/shard_map/ppermute | solution.py:53
  19.6 1.9 %collective-permute-start.6 = (bf16[64,1024]{1,0:T(8,128)(2,1)S(1)}, bf16[64,1024]{1,0:T(8,128)(2,1)S(1)}, u32[]{:S(2)}, u32[]{:S(2)}) collective-permute-start(bf16[64,1024]{1,0:T(8,128)(2,1)S(1)} %collective-permute-done.2.refs_1_), channel_id=1, source_target_pairs={{0,4},{4,8},{8,12},{12,14},{14,10},{10,6},{6,2},{2,0},{1,5},{5,9},... | collective-permute-start | bytes 393224 | tf_op jit(solution)/shard_map/ppermute | solution.py:53
  21.7 1.8 %collective-permute-start.14 = (bf16[64,1152]{1,0:T(8,128)(2,1)S(1)}, bf16[64,1152]{1,0:T(8,128)(2,1)S(1)}, u32[]{:S(2)}, u32[]{:S(2)}) collective-permute-start(bf16[64,1152]{1,0:T(8,128)(2,1)S(1)} %collective-permute-done.7.refs_2_), channel_id=1, source_target_pairs={{0,2},{4,0},{8,4},{12,8},{14,12},{10,14},{6,10},{2,6},{1,3},{5,1},... | collective-permute-start | bytes 442376 | tf_op jit(solution)/shard_map/ppermute | solution.py:53
  26.1 1.7 %collective-permute-start.13 = (bf16[64,1024]{1,0:T(8,128)(2,1)S(1)}, bf16[64,1024]{1,0:T(8,128)(2,1)S(1)}, u32[]{:S(2)}, u32[]{:S(2)}) collective-permute-start(bf16[64,1024]{1,0:T(8,128)(2,1)S(1)} %collective-permute-done.6.refs_1_), channel_id=1, source_target_pairs={{0,4},{4,8},{8,12},{12,14},{14,10},{10,6},{6,2},{2,0},{1,5},{5,9},... | collective-permute-start | bytes 393224 | tf_op jit(solution)/shard_map/ppermute | solution.py:53
  28.2 1.7 %shard_map.105 = (bf16[1024,1536]{1,0:T(8,128)(2,1)S(1)}, bf16[768,1024]{1,0:T(8,128)(2,1)S(1)}) custom-call(bf16[2,512,384]{2,1,0:T(8,128)(2,1)} %refs_0_.1, bf16[2,512,384]{2,1,0:T(8,128)(2,1)} %refs_1_.1, bf16[2,192,1024]{2,1,0:T(8,128)(2,1)} %refs_2_.3, bf16[3200,384]{1,0:T(8,128)(2,1)S(1)} %collective-permute-done.refs_3_), custom_call_target="tpu_custom_call" | custom-call | tf_op jit(solution)/shard_map/pallas_call | solution.py:246
  31.1 1.7 %collective-permute-done.12.refs_1_ = bf16[64,1024]{1,0:T(8,128)(2,1)S(1)} collective-permute-done((bf16[64,1024]{1,0:T(8,128)(2,1)S(1)}, bf16[64,1024]{1,0:T(8,128)(2,1)S(1)}, u32[]{:S(2)}, u32[]{:S(2)}) %collective-permute-start.12) | collective-permute-done | bytes 131104 | tf_op jit(solution)/shard_map/ppermute | solution.py:53
  32.8 1.9 %shard_map.109 = (bf16[320,768]{1,0:T(8,128)(2,1)S(1)}, bf16[320,768]{1,0:T(8,128)(2,1)S(1)}, bf16[64,1024]{1,0:T(8,128)(2,1)S(1)}, f32[128,1024]{1,0:T(8,128)S(1)}, f32[128,1024]{1,0:T(8,128)S(1)}) custom-call(bf16[64,1152]{1,0:T(8,128)(2,1)S(1)} %collective-permute-done.10.refs_0_, bf16[64,1024]{1,0:T(8,128)(2,1)S(1)} %collective-permute-done.12.refs_1_, ...), custom_call_target="tpu_custom_call" | custom-call | flops 1509949440 | bytes 5554176 | tf_op jit(solution)/shard_map/pallas_call | solution.py:29
  37.9 3.2 %collective-permute-done.15.arrived_ref = bf16[64,1024]{1,0:T(8,128)(2,1)S(1)} collective-permute-done((bf16[64,1024]{1,0:T(8,128)(2,1)S(1)}, bf16[64,1024]{1,0:T(8,128)(2,1)S(1)}, u32[]{:S(2)}, u32[]{:S(2)}) %collective-permute-start.15) | collective-permute-done | bytes 131104 | tf_op jit(solution)/shard_map/ppermute | solution.py:53
  45.9 4.4 %collective-permute-done.16.arrived_ref = bf16[128,1024]{1,0:T(8,128)(2,1)S(1)} collective-permute-done((bf16[128,1024]{1,0:T(8,128)(2,1)S(1)}, bf16[128,1024]{1,0:T(8,128)(2,1)S(1)}, u32[]{:S(2)}, u32[]{:S(2)}) %collective-permute-start.16) | collective-permute-done | bytes 262176 | tf_op jit(solution)/shard_map/ppermute | solution.py:53
  54.7 4.1 %collective-permute-done.17.arrived_ref = bf16[128,1024]{1,0:T(8,128)(2,1)S(1)} collective-permute-done((bf16[128,1024]{1,0:T(8,128)(2,1)S(1)}, bf16[128,1024]{1,0:T(8,128)(2,1)S(1)}, u32[]{:S(2)}, u32[]{:S(2)}) %collective-permute-start.17) | collective-permute-done | bytes 262176 | tf_op jit(solution)/shard_map/ppermute | solution.py:53
  62.1 5.9 %collective-permute-done.18.left_ref = bf16[128,1024]{1,0:T(8,128)(2,1)S(1)} collective-permute-done((bf16[128,1024]{1,0:T(8,128)(2,1)S(1)}, bf16[128,1024]{1,0:T(8,128)(2,1)S(1)}, u32[]{:S(2)}, u32[]{:S(2)}) %collective-permute-start.18) | collective-permute-done | bytes 262176 | tf_op jit(solution)/shard_map/ppermute | solution.py:53
  73.6 1.8 %collective-permute-done.23.refs_4_ = bf16[64,1024]{1,0:T(8,128)(2,1)S(1)} collective-permute-done((bf16[64,1024]{1,0:T(8,128)(2,1)S(1)}, bf16[64,1024]{1,0:T(8,128)(2,1)S(1)}, u32[]{:S(2)}, u32[]{:S(2)}) %collective-permute-start.23) | collective-permute-done | bytes 131104 | tf_op jit(solution)/shard_map/ppermute | solution.py:53
  88.4 1.8 %collective-permute-done.36.refs_6_ = bf16[64,1024]{1,0:T(8,128)(2,1)S(1)} collective-permute-done((bf16[64,1024]{1,0:T(8,128)(2,1)S(1)}, bf16[64,1024]{1,0:T(8,128)(2,1)S(1)}, u32[]{:S(2)}, u32[]{:S(2)}) %collective-permute-start.36) | collective-permute-done | bytes 131104 | tf_op jit(solution)/shard_map/ppermute | solution.py:53
  93.2 3.3 %collective-permute-done.37 = bf16[8,1024]{1,0:T(8,128)(2,1)S(1)} collective-permute-done((bf16[8,1024]{1,0:T(8,128)(2,1)S(1)}, bf16[8,1024]{1,0:T(8,128)(2,1)S(1)}, u32[]{:S(2)}, u32[]{:S(2)}) %collective-permute-start.37) | collective-permute-done | bytes 16416 | tf_op jit(solution)/shard_map/ppermute | solution.py:420
  98.0 1.7 %collective-permute-start.39 = (bf16[8,1024]{1,0:T(8,128)(2,1)S(1)}, bf16[8,1024]{1,0:T(8,128)(2,1)S(1)}, u32[]{:S(2)}, u32[]{:S(2)}) collective-permute-start(bf16[8,1024]{1,0:T(8,128)(2,1)S(1)} %add_convert_fusion), channel_id=1, source_target_pairs={{0,8},{2,10},{4,12},{6,14},{8,0},{10,2},{12,4},{14,6},{1,9},{3,11}... | collective-permute-start | bytes 49160 | tf_op jit(solution)/shard_map/ppermute | solution.py:420
  103.6 1.9 %shard_map.128 = (bf16[64,1024]{1,0:T(8,128)(2,1)S(1)}, f32[128,1024]{1,0:T(8,128)S(1)}, f32[128,1024]{1,0:T(8,128)S(1)}) custom-call(f32[128,1024]{1,0:T(8,128)S(1)} %get-tuple-element.85.refs_0_, f32[128,128]{1,0:T(8,128)S(1)} %get-tuple-element.86.refs_1_, f32[256,1024]{1,0:T(8,128)S(1)} %get-tuple-element.87.refs_2_.refs_4_, ...), custom_call_target="tpu_custom_call" | custom-call | flops 1509949440 | bytes 8687616 | tf_op jit(solution)/shard_map/pallas_call | solution.py:29
  108.8 1.8 %collective-permute-done.41.arrived_ref = bf16[64,1024]{1,0:T(8,128)(2,1)S(1)} collective-permute-done((bf16[64,1024]{1,0:T(8,128)(2,1)S(1)}, bf16[64,1024]{1,0:T(8,128)(2,1)S(1)}, u32[]{:S(2)}, u32[]{:S(2)}) %collective-permute-start.41) | collective-permute-done | bytes 131104 | tf_op jit(solution)/shard_map/ppermute | solution.py:53
  122.0 2.3 %collective-permute-done.43.arrived_ref = bf16[128,1024]{1,0:T(8,128)(2,1)S(1)} collective-permute-done((bf16[128,1024]{1,0:T(8,128)(2,1)S(1)}, bf16[128,1024]{1,0:T(8,128)(2,1)S(1)}, u32[]{:S(2)}, u32[]{:S(2)}) %collective-permute-start.43) | collective-permute-done | bytes 262176 | tf_op jit(solution)/shard_map/ppermute | solution.py:53
  (124 shorter events, 74.4 us)
Async XLA Ops:
  2.6 25.6 %collective-permute-start = (bf16[3200,384]{1,0:T(8,128)(2,1)S(1)}, bf16[3200,384]{1,0:T(8,128)(2,1)S(1)}, u32[]{:S(2)}, u32[]{:S(2)}) collective-permute-start(bf16[3200,384]{1,0:T(8,128)(2,1)S(1)} %get-tuple-element.52), channel_id=1, source_target_pairs={{0,1},{1,0},{2,3},{3,2},{4,5},{5,4},{6,7},{7,6},{8,9},{9,8},{10,11... | collective-permute-start | bytes 7372808 | tf_op jit(solution)/shard_map/ppermute | solution.py:286
  3.1 7.0 %collective-permute-start.1 = (bf16[64,1152]{1,0:T(8,128)(2,1)S(1)}, bf16[64,1152]{1,0:T(8,128)(2,1)S(1)}, u32[]{:S(2)}, u32[]{:S(2)}) collective-permute-start(bf16[64,1152]{1,0:T(8,128)(2,1)S(1)} %get-tuple-element.50.refs_0_), channel_id=1, source_target_pairs={{0,4},{4,8},{8,12},{12,14},{14,10},{10,6},{6,2},{2,0},{1,5},{5,9},... | collective-permute-start | bytes 442376 | tf_op jit(solution)/shard_map/ppermute | solution.py:53
  5.7 7.8 %collective-permute-start.4 = (bf16[64,1024]{1,0:T(8,128)(2,1)S(1)}, bf16[64,1024]{1,0:T(8,128)(2,1)S(1)}, u32[]{:S(2)}, u32[]{:S(2)}) collective-permute-start(bf16[64,1024]{1,0:T(8,128)(2,1)S(1)} %get-tuple-element.51.refs_1_), channel_id=1, source_target_pairs={{0,2},{4,0},{8,4},{12,8},{14,12},{10,14},{6,10},{2,6},{1,3},{5,1},... | collective-permute-start | bytes 393224 | tf_op jit(solution)/shard_map/ppermute | solution.py:53
  5.7 8.7 %collective-permute-start.3 = (bf16[64,1152]{1,0:T(8,128)(2,1)S(1)}, bf16[64,1152]{1,0:T(8,128)(2,1)S(1)}, u32[]{:S(2)}, u32[]{:S(2)}) collective-permute-start(bf16[64,1152]{1,0:T(8,128)(2,1)S(1)} %get-tuple-element.50.refs_0_), channel_id=1, source_target_pairs={{0,2},{4,0},{8,4},{12,8},{14,12},{10,14},{6,10},{2,6},{1,3},{5,1},... | collective-permute-start | bytes 442376 | tf_op jit(solution)/shard_map/ppermute | solution.py:53
  10.1 6.7 %collective-permute-start.5 = (bf16[64,1152]{1,0:T(8,128)(2,1)S(1)}, bf16[64,1152]{1,0:T(8,128)(2,1)S(1)}, u32[]{:S(2)}, u32[]{:S(2)}) collective-permute-start(bf16[64,1152]{1,0:T(8,128)(2,1)S(1)} %collective-permute-done.1.refs_0_), channel_id=1, source_target_pairs={{0,4},{4,8},{8,12},{12,14},{14,10},{10,6},{6,2},{2,0},{1,5},{5,9},... | collective-permute-start | bytes 442376 | tf_op jit(solution)/shard_map/ppermute | solution.py:53
  11.9 7.7 %collective-permute-start.2 = (bf16[64,1024]{1,0:T(8,128)(2,1)S(1)}, bf16[64,1024]{1,0:T(8,128)(2,1)S(1)}, u32[]{:S(2)}, u32[]{:S(2)}) collective-permute-start(bf16[64,1024]{1,0:T(8,128)(2,1)S(1)} %get-tuple-element.51.refs_1_), channel_id=1, source_target_pairs={{0,4},{4,8},{8,12},{12,14},{14,10},{10,6},{6,2},{2,0},{1,5},{5,9},... | collective-permute-start | bytes 393224 | tf_op jit(solution)/shard_map/ppermute | solution.py:53
  13.5 8.0 %collective-permute-start.8 = (bf16[64,1024]{1,0:T(8,128)(2,1)S(1)}, bf16[64,1024]{1,0:T(8,128)(2,1)S(1)}, u32[]{:S(2)}, u32[]{:S(2)}) collective-permute-start(bf16[64,1024]{1,0:T(8,128)(2,1)S(1)} %collective-permute-done.4.refs_3_), channel_id=1, source_target_pairs={{0,2},{4,0},{8,4},{12,8},{14,12},{10,14},{6,10},{2,6},{1,3},{5,1},... | collective-permute-start | bytes 393224 | tf_op jit(solution)/shard_map/ppermute | solution.py:53
  14.5 7.2 %collective-permute-start.7 = (bf16[64,1152]{1,0:T(8,128)(2,1)S(1)}, bf16[64,1152]{1,0:T(8,128)(2,1)S(1)}, u32[]{:S(2)}, u32[]{:S(2)}) collective-permute-start(bf16[64,1152]{1,0:T(8,128)(2,1)S(1)} %collective-permute-done.3.refs_2_), channel_id=1, source_target_pairs={{0,2},{4,0},{8,4},{12,8},{14,12},{10,14},{6,10},{2,6},{1,3},{5,1},... | collective-permute-start | bytes 442376 | tf_op jit(solution)/shard_map/ppermute | solution.py:53
  16.8 6.6 %collective-permute-start.9 = (bf16[64,1152]{1,0:T(8,128)(2,1)S(1)}, bf16[64,1152]{1,0:T(8,128)(2,1)S(1)}, u32[]{:S(2)}, u32[]{:S(2)}) collective-permute-start(bf16[64,1152]{1,0:T(8,128)(2,1)S(1)} %collective-permute-done.5.refs_0_), channel_id=1, source_target_pairs={{0,4},{4,8},{8,12},{12,14},{14,10},{10,6},{6,2},{2,0},{1,5},{5,9},... | collective-permute-start | bytes 442376 | tf_op jit(solution)/shard_map/ppermute | solution.py:53
  19.6 6.5 %collective-permute-start.6 = (bf16[64,1024]{1,0:T(8,128)(2,1)S(1)}, bf16[64,1024]{1,0:T(8,128)(2,1)S(1)}, u32[]{:S(2)}, u32[]{:S(2)}) collective-permute-start(bf16[64,1024]{1,0:T(8,128)(2,1)S(1)} %collective-permute-done.2.refs_1_), channel_id=1, source_target_pairs={{0,4},{4,8},{8,12},{12,14},{14,10},{10,6},{6,2},{2,0},{1,5},{5,9},... | collective-permute-start | bytes 393224 | tf_op jit(solution)/shard_map/ppermute | solution.py:53
  21.7 9.4 %collective-permute-start.14 = (bf16[64,1152]{1,0:T(8,128)(2,1)S(1)}, bf16[64,1152]{1,0:T(8,128)(2,1)S(1)}, u32[]{:S(2)}, u32[]{:S(2)}) collective-permute-start(bf16[64,1152]{1,0:T(8,128)(2,1)S(1)} %collective-permute-done.7.refs_2_), channel_id=1, source_target_pairs={{0,2},{4,0},{8,4},{12,8},{14,12},{10,14},{6,10},{2,6},{1,3},{5,1},... | collective-permute-start | bytes 442376 | tf_op jit(solution)/shard_map/ppermute | solution.py:53
  23.4 9.4 %collective-permute-start.10 = (bf16[64,1152]{1,0:T(8,128)(2,1)S(1)}, bf16[64,1152]{1,0:T(8,128)(2,1)S(1)}, u32[]{:S(2)}, u32[]{:S(2)}) collective-permute-start(bf16[64,1152]{1,0:T(8,128)(2,1)S(1)} %collective-permute-done.9.refs_2_.refs_0_), channel_id=1, source_target_pairs={{0,4},{4,8},{8,12},{12,14},{14,10},{10,6},{6,2},{2,0},{1,5},{5,9},... | collective-permute-start | bytes 442376 | tf_op jit(solution)/shard_map/ppermute | solution.py:53
  41.1 9.1 %collective-permute-start.16 = (bf16[128,1024]{1,0:T(8,128)(2,1)S(1)}, bf16[128,1024]{1,0:T(8,128)(2,1)S(1)}, u32[]{:S(2)}, u32[]{:S(2)}) collective-permute-start(bf16[128,1024]{1,0:T(8,128)(2,1)S(1)} %shard_map.110), channel_id=1, source_target_pairs={{0,4},{4,8},{8,12},{12,14},{14,10},{10,6},{6,2},{2,0},{1,5},{5,9},... | collective-permute-start | bytes 786440 | tf_op jit(solution)/shard_map/ppermute | solution.py:53
  43.8 8.7 %collective-permute-start.20 = (bf16[128,1024]{1,0:T(8,128)(2,1)S(1)}, bf16[128,1024]{1,0:T(8,128)(2,1)S(1)}, u32[]{:S(2)}, u32[]{:S(2)}) collective-permute-start(bf16[128,1024]{1,0:T(8,128)(2,1)S(1)} %shard_map.114), channel_id=1, source_target_pairs={{0,2},{4,0},{8,4},{12,8},{14,12},{10,14},{6,10},{2,6},{1,3},{5,1},... | collective-permute-start | bytes 786440 | tf_op jit(solution)/shard_map/ppermute | solution.py:53
  50.3 8.5 %collective-permute-start.17 = (bf16[128,1024]{1,0:T(8,128)(2,1)S(1)}, bf16[128,1024]{1,0:T(8,128)(2,1)S(1)}, u32[]{:S(2)}, u32[]{:S(2)}) collective-permute-start(bf16[128,1024]{1,0:T(8,128)(2,1)S(1)} %shard_map.111), channel_id=1, source_target_pairs={{0,4},{4,8},{8,12},{12,14},{14,10},{10,6},{6,2},{2,0},{1,5},{5,9},... | collective-permute-start | bytes 786440 | tf_op jit(solution)/shard_map/ppermute | solution.py:53
  52.6 7.9 %collective-permute-start.21 = (bf16[128,1024]{1,0:T(8,128)(2,1)S(1)}, bf16[128,1024]{1,0:T(8,128)(2,1)S(1)}, u32[]{:S(2)}, u32[]{:S(2)}) collective-permute-start(bf16[128,1024]{1,0:T(8,128)(2,1)S(1)} %shard_map.115), channel_id=1, source_target_pairs={{0,2},{4,0},{8,4},{12,8},{14,12},{10,14},{6,10},{2,6},{1,3},{5,1},... | collective-permute-start | bytes 786440 | tf_op jit(solution)/shard_map/ppermute | solution.py:53
  58.8 9.2 %collective-permute-start.18 = (bf16[128,1024]{1,0:T(8,128)(2,1)S(1)}, bf16[128,1024]{1,0:T(8,128)(2,1)S(1)}, u32[]{:S(2)}, u32[]{:S(2)}) collective-permute-start(bf16[128,1024]{1,0:T(8,128)(2,1)S(1)} %shard_map.112), channel_id=1, source_target_pairs={{0,4},{4,8},{8,12},{12,14},{14,10},{10,6},{6,2},{2,0},{1,5},{5,9},... | collective-permute-start | bytes 786440 | tf_op jit(solution)/shard_map/ppermute | solution.py:53
  60.6 8.8 %collective-permute-start.22 = (bf16[128,1024]{1,0:T(8,128)(2,1)S(1)}, bf16[128,1024]{1,0:T(8,128)(2,1)S(1)}, u32[]{:S(2)}, u32[]{:S(2)}) collective-permute-start(bf16[128,1024]{1,0:T(8,128)(2,1)S(1)} %shard_map.116), channel_id=1, source_target_pairs={{0,2},{4,0},{8,4},{12,8},{14,12},{10,14},{6,10},{2,6},{1,3},{5,1},... | collective-permute-start | bytes 786440 | tf_op jit(solution)/shard_map/ppermute | solution.py:53
  71.5 6.7 %collective-permute-start.31 = (bf16[64,1024]{1,0:T(8,128)(2,1)S(1)}, bf16[64,1024]{1,0:T(8,128)(2,1)S(1)}, u32[]{:S(2)}, u32[]{:S(2)}) collective-permute-start(bf16[64,1024]{1,0:T(8,128)(2,1)S(1)} %get-tuple-element.65.refs_3_), channel_id=1, source_target_pairs={{0,4},{4,8},{8,12},{12,14},{14,10},{10,6},{6,2},{2,0},{1,5},{5,9},... | collective-permute-start | bytes 393224 | tf_op jit(solution)/shard_map/ppermute | solution.py:53
  73.1 6.9 %collective-permute-start.34 = (bf16[64,1024]{1,0:T(8,128)(2,1)S(1)}, bf16[64,1024]{1,0:T(8,128)(2,1)S(1)}, u32[]{:S(2)}, u32[]{:S(2)}) collective-permute-start(bf16[64,1024]{1,0:T(8,128)(2,1)S(1)} %get-tuple-element.64.refs_2_), channel_id=1, source_target_pairs={{0,2},{4,0},{8,4},{12,8},{14,12},{10,14},{6,10},{2,6},{1,3},{5,1},... | collective-permute-start | bytes 393224 | tf_op jit(solution)/shard_map/ppermute | solution.py:53
  110.6 6.4 %collective-permute-start.42 = (bf16[128,1024]{1,0:T(8,128)(2,1)S(1)}, bf16[128,1024]{1,0:T(8,128)(2,1)S(1)}, u32[]{:S(2)}, u32[]{:S(2)}) collective-permute-start(bf16[128,1024]{1,0:T(8,128)(2,1)S(1)} %shard_map.129), channel_id=1, source_target_pairs={{0,4},{4,8},{8,12},{12,14},{14,10},{10,6},{6,2},{2,0},{1,5},{5,9},... | collective-permute-start | bytes 786440 | tf_op jit(solution)/shard_map/ppermute | solution.py:53
  112.9 6.4 %collective-permute-start.46 = (bf16[128,1024]{1,0:T(8,128)(2,1)S(1)}, bf16[128,1024]{1,0:T(8,128)(2,1)S(1)}, u32[]{:S(2)}, u32[]{:S(2)}) collective-permute-start(bf16[128,1024]{1,0:T(8,128)(2,1)S(1)} %shard_map.133), channel_id=1, source_target_pairs={{0,2},{4,0},{8,4},{12,8},{14,12},{10,14},{6,10},{2,6},{1,3},{5,1},... | collective-permute-start | bytes 786440 | tf_op jit(solution)/shard_map/ppermute | solution.py:53
  113.9 6.5 %collective-permute-start.49 = (bf16[8,1274]{1,0:T(8,128)(2,1)S(1)}, bf16[8,1274]{1,0:T(8,128)(2,1)S(1)}, u32[]{:S(2)}, u32[]{:S(2)}) collective-permute-start(bf16[8,1274]{1,0:T(8,128)(2,1)S(1)} %pad_maximum_fusion.1), channel_id=1, source_target_pairs={{0,1},{1,0},{2,3},{3,2},{4,5},{5,4},{6,7},{7,6},{8,9},{9,8},{10,11... | collective-permute-start | bytes 61160 | tf_op jit(solution)/shard_map/ppermute | solution.py:468
  117.1 7.2 %collective-permute-start.43 = (bf16[128,1024]{1,0:T(8,128)(2,1)S(1)}, bf16[128,1024]{1,0:T(8,128)(2,1)S(1)}, u32[]{:S(2)}, u32[]{:S(2)}) collective-permute-start(bf16[128,1024]{1,0:T(8,128)(2,1)S(1)} %shard_map.130), channel_id=1, source_target_pairs={{0,4},{4,8},{8,12},{12,14},{14,10},{10,6},{6,2},{2,0},{1,5},{5,9},... | collective-permute-start | bytes 786440 | tf_op jit(solution)/shard_map/ppermute | solution.py:53
  (29 other events, 281.3 us)

commit v13 on v9

--- a/solution.py
+++ b/solution.py
@@ -40,6 +40,7 @@
     def __init__(self, expert_count, group_count):
         self.count = expert_count
         self.half = expert_count // 2
+        self.groups = group_count
         self.snake = group_count == 2
         if self.snake:
             self.order = list(range(0, expert_count, 2)) + list(range(expert_count - 1, 0, -2))
@@ -47,20 +48,40 @@
             self.order = list(range(expert_count))
 
     def send(self, value, distance):
-        pairs = [
-            (self.order[i], self.order[(i + distance) % self.count]) for i in range(self.count)
-        ]
-        return lax.ppermute(value, "expert", pairs)
+        pairs = []
+        for i in range(self.count):
+            for g in range(self.groups):
+                there = self.order[(i + (-distance if g % 2 else distance)) % self.count]
+                pairs.append((self.order[i] * self.groups + g, there * self.groups + g))
+        return lax.ppermute(value, ("expert", "group"), pairs)
 
     def device_at(self, distance):
         here = lax.axis_index("expert")
         count = self.count
         if self.snake:
             here = jnp.where(here % 2 == 0, here // 2, count - 1 - here // 2)
-        there = lax.rem(here + distance % count, count)
+        ahead = distance % count
+        step = jnp.where(lax.rem(lax.axis_index("group"), 2) == 0, ahead, count - ahead)
+        there = lax.rem(here + step, count)
         if self.snake:
             there = jnp.where(there < self.half, 2 * there, 2 * (count - 1 - there) + 1)
         return there
+
+    def signed(self, behind):
+        return -behind if behind < self.half else self.count - behind
+
+    def gather_round(self, own):
+        blocks = {0: own}
+        for behind in range(1, self.count):
+            own = self.send(own, 1)
+            blocks[self.signed(behind)] = own
+        return blocks
+
+    def scatter_round(self, parts):
+        total = parts[self.signed(1)]
+        for behind in range(2, self.count):
+            total = add(parts[self.signed(behind)], self.send(total, 1))
+        return self.send(total, 1)
 
     def gather(self, top, bottom, use):
         top_left = top_right = top
@@ -73,20 +94,6 @@
             bottom_right = self.send(bottom_right, -1)
             use((-step, step), (top_left, bottom_left, top_right, bottom_right))
         use((self.half,), (self.send(top_left, 1), self.send(bottom_right, -1)))
-
-    def scatter(self, parts):
-        most = self.half - 1
-        top_left = self.send(parts[self.half][0], 1)
-        bottom_right = self.send(parts[self.half][1], -1)
-        bottom_left = self.send(parts[most][1], 1)
-        top_right = self.send(parts[-most][0], -1)
-        for step in range(most, 0, -1):
-            top_left = self.send(add(parts[step][0], top_left), 1)
-            bottom_right = self.send(add(parts[-step][1], bottom_right), -1)
-            if step > 1:
-                bottom_left = self.send(add(parts[step - 1][1], bottom_left), 1)
-                top_right = self.send(add(parts[1 - step][0], top_right), -1)
-        return (top_left, top_right), (bottom_left, bottom_right)
 
     def scatter_whole(self, ends, parts):
         mid = ends[0].shape[0]
@@ -111,14 +118,6 @@
             left, right = self.send(left, 1), self.send(right, -1)
         return left, right
 
-    def part_types(self, distances):
-        types = []
-        for k in distances:
-            first = BF16 if k == self.half or k == 1 - self.half else F32
-            second = BF16 if k == self.half or k == self.half - 1 else F32
-            types += [first, second]
-        return types
-
 
 def add_kernel(block_ref, arrived_ref, out_ref):
     out_ref[...] = (block_ref[...] + arrived_ref[...].astype(F32)).astype(BF16)
@@ -128,13 +127,14 @@
     return call(add_kernel, [(block.shape, BF16)], block, arrived)[0]
 
 
-def sum_kernel(*refs):
-    out_ref = refs[-1]
-    rows = refs[0].shape[0]
-    for i in range(len(refs) // 3):
-        own, left, right = refs[3 * i : 3 * i + 3]
-        arrived = left[...].astype(F32) + right[...].astype(F32)
-        out_ref[pl.ds(i * rows, rows), :] = (own[...] + arrived).astype(BF16)
+def sum_kernel(count, *refs):
+    total = refs[0][...]
+    for ref in refs[1:count]:
+        total = total + ref[...].astype(F32)
+    outs = refs[count:]
+    rows = total.shape[0] // len(outs)
+    for i, out in enumerate(outs):
+        out[...] = total[i * rows : (i + 1) * rows].astype(BF16)
 
 
 class Copies:
@@ -168,8 +168,6 @@
 
 def pack(ids, scores, tokens, shards):
     rows, cols = tokens.shape
-    mid = rows // 2
-    quarter = LANES // 4
     inputs = [ids, scores, tokens, *shards]
     packed_shape, places, count = None, [], 0
     if shards:
@@ -180,13 +178,12 @@
 
     def kernel(*refs):
         ids_hbm, scores_hbm, tokens_hbm, *shards_hbm = refs[: len(inputs)]
-        top_ref, bottom_ref, *packed_refs = refs[len(inputs) : -3]
+        block_ref, *packed_refs = refs[len(inputs) : -3]
         ids_ref, scores_ref, sems = refs[-3:]
         copies = Copies(sems)
         copies.start(ids_hbm, ids_ref)
         copies.start(scores_hbm, scores_ref)
-        copies.start(tokens_hbm.at[pl.ds(0, mid), :], top_ref.at[:, pl.ds(0, cols)])
-        copies.start(tokens_hbm.at[pl.ds(mid, mid), :], bottom_ref)
+        copies.start(tokens_hbm, block_ref.at[:, pl.ds(0, cols)])
         for local, (pair, downs) in enumerate(places):
             out_ref = packed_refs[0]
             for source, (row, some) in zip(shards_hbm, pair):
@@ -202,20 +199,17 @@
         scores = scores_ref[...]
         ids = ids_ref[...]
         route_weight = scores / jnp.sum(scores, axis=0, keepdims=True)
-        expert = lax.broadcasted_iota(jnp.int32, (quarter, rows), 0)
-        weight_by = jnp.zeros((quarter, rows), F32)
+        expert = lax.broadcasted_iota(jnp.int32, (LANES // 2, rows), 0)
+        weight_by = jnp.zeros((LANES // 2, rows), F32)
         for choice_k in range(scores.shape[0]):
             one = slice(choice_k, choice_k + 1)
             weight_by = weight_by + jnp.where(ids[one] == expert, route_weight[one], 0.0)
         high = weight_by.astype(BF16).astype(F32)
-        weights = jnp.concatenate([high, weight_by - high] * 2, axis=0).T
-        lane = lax.broadcasted_iota(jnp.int32, (mid, LANES), 1)
-        both = jnp.where(lane < 2 * quarter, weights[:mid], weights[mid:])
-        top_ref[:, cols:] = both.astype(BF16)
+        block_ref[:, cols:] = jnp.concatenate([high, weight_by - high], axis=0).T.astype(BF16)
         for copy in copies.started[2:]:
             copy.wait()
 
-    outs = [pltpu.VMEM((mid, cols + LANES), BF16), pltpu.VMEM((mid, cols), BF16)]
+    outs = [pltpu.VMEM((rows, cols + LANES), BF16)]
     if shards:
         outs.append(pltpu.VMEM(packed_shape, BF16))
     return pl.pallas_call(
@@ -226,7 +220,7 @@
         scratch_shapes=[
             pltpu.VMEM(ids.shape, ids.dtype),
             pltpu.VMEM(scores.shape, F32),
-            pltpu.SemaphoreType.DMA((4 + count,)),
+            pltpu.SemaphoreType.DMA((3 + count,)),
         ],
         compiler_params=pltpu.CompilerParams(vmem_limit_bytes=VMEM_LIMIT),
     )(*[pltpu.with_memory_space_constraint(a, pltpu.HBM) for a in inputs])
@@ -312,94 +306,66 @@
 
     shards = [w_gate, w_up, w_down]
     if group_count == 2:
-        top, bottom, packed = pack(route_ids.T, route_scores.T, tokens, shards)
+        own, packed = pack(route_ids.T, route_scores.T, tokens, shards)
         packed = lax.ppermute(packed, "group", [(0, 1), (1, 0)])
     else:
-        top, bottom = pack(route_ids.T, route_scores.T, tokens, [])
+        (own,) = pack(route_ids.T, route_scores.T, tokens, [])
         shards = [lax.all_gather(w, "group", axis=1, tiled=True) for w in shards]
         packed = None
     wide, down = full_weights(shards, packed)
 
-    def rows_of(refs):
-        return jnp.concatenate([ref[...] for ref in refs], axis=0) if len(refs) > 1 else refs[0][...]
-
-    def forward_kernel(count, *refs):
-        token_refs, (wide_ref, down_ref) = refs[:count], refs[count : count + 2]
-        outs = refs[count + 2 :]
-        x = rows_of([ref.at[:, :feature_dim] for ref in token_refs])
-        weights = jnp.concatenate([ref[:, feature_dim:] for ref in token_refs[::2]], axis=0).astype(F32)
+    def forward_kernel(block_ref, wide_ref, down_ref, gate_save, up_save, out_ref):
+        x = block_ref[:, :feature_dim]
+        weights = block_ref[:, feature_dim:].astype(F32)
         lane = lax.broadcasted_iota(jnp.int32, weights.shape, 1)
-        quarter = LANES // 4
         hidden = []
         for local in range(local_experts):
             expert = lax.axis_index("expert") * local_experts + local
-            scales = []
-            for begin in (expert, expert + 2 * quarter):
-                here = (lane == begin) | (lane == begin + quarter)
-                scales.append(jnp.sum(jnp.where(here, weights, 0.0), axis=1, keepdims=True))
-            pieces = [s[i : i + mid] for i in range(0, weights.shape[0], mid) for s in scales]
-            scale = jnp.concatenate(pieces, axis=0)
+            mine = (lane == expert) | (lane == expert + LANES // 2)
+            scale = jnp.sum(jnp.where(mine, weights, 0.0), axis=1, keepdims=True)
             act = dot(x, wide_ref[:, pl.ds(local * pair_dim, pair_dim)])
             gate_act, up_act = act[:, :hidden_dim], act[:, hidden_dim:]
             sigmoid_gate = jax.nn.sigmoid(gate_act)
             silu = gate_act * sigmoid_gate * scale
             slope = sigmoid_gate * (1.0 + gate_act * (1.0 - sigmoid_gate)) * scale
             cols = pl.ds(local * hidden_dim, hidden_dim)
-            outs[0][:, cols] = (up_act * slope).astype(BF16)
-            outs[1][:, cols] = silu.astype(BF16)
+            gate_save[:, cols] = (up_act * slope).astype(BF16)
+            up_save[:, cols] = silu.astype(BF16)
             hidden.append((silu * up_act).astype(BF16))
-        total = dot(jnp.concatenate(hidden, axis=1), down_ref[...])
-        for i, out in enumerate(outs[2:]):
-            out[...] = total[i * mid : (i + 1) * mid].astype(out.dtype)
-
-    tokens_at, saved_at, part_at = {}, {}, {}
+        out_ref[...] = dot(jnp.concatenate(hidden, axis=1), down_ref[...]).astype(out_ref.dtype)
+
+    tokens_at = ring.gather_round(own)
+    part_at, saved_at = {}, {}
     flops = 2 * rows_here * feature_dim * hidden_dim * local_experts * 3
-
-    def hold(distances, blocks):
-        tokens_at[distances] = blocks
-
-    def keep_parts(parts, distances, halves):
-        parts.update({k: halves[2 * i : 2 * i + 2] for i, k in enumerate(distances)})
-
-    def part_outs(distances):
-        return [((mid, feature_dim), dtype) for dtype in ring.part_types(distances)]
-
-    def forward(distances):
-        blocks = tokens_at[distances]
-        rows = mid * len(blocks)
-        result = call(
-            functools.partial(forward_kernel, len(blocks)),
-            [((rows, local_experts * hidden_dim), BF16)] * 2 + part_outs(distances),
-            *blocks,
+    for k, rows in tokens_at.items():
+        *saved_at[k], part_at[k] = call(
+            forward_kernel,
+            [((rows_here, local_experts * hidden_dim), BF16)] * 2
+            + [(block, BF16 if k == ring.signed(1) else F32)],
+            rows,
             wide,
             down,
-            flops=flops * rows // rows_here,
+            flops=flops,
         )
-        saved_at[distances] = result[:2]
-        keep_parts(part_at, distances, result[2:])
-
-    ring.gather(top, bottom, hold)
-    for distances in tokens_at:
-        forward(distances)
     gain = norm_gain.reshape(1, feature_dim)
-    half_shape = (mid, feature_dim)
-    moe_top, moe_bottom = [
-        call(sum_kernel, [(half_shape, BF16)], own, *arrived)[0]
-        for own, arrived in zip(part_at[0], ring.scatter(part_at))
-    ]
+    moe_top, moe_bottom = call(
+        functools.partial(sum_kernel, 2),
+        [((mid, feature_dim), BF16)] * 2,
+        part_at[0],
+        ring.scatter_round(part_at),
+    )
 
     norm_at, mean_at = {}, {}
-
-    def residual_of(token_refs, moe_refs):
-        token_rows = rows_of([ref.at[:, :feature_dim] for ref in token_refs]).astype(F32)
-        return token_rows + rows_of(moe_refs).astype(F32)
 
     def inv_rms_of(residual):
         return lax.rsqrt(jnp.mean(residual * residual, axis=-1, keepdims=True) + NORM_EPS)
 
-    def norm_kernel(distances, count, *refs):
-        residual = residual_of(refs[:count], refs[count : 2 * count])
-        gain_ref, so_far, out_ref, residual_ref, inv_ref = refs[2 * count :]
+    def norm_kernel(distances, *refs):
+        count = len(distances)
+        residual = jnp.concatenate([ref[:, :feature_dim].astype(F32) for ref in refs[:count]], axis=0)
+        moe_rows = [ref[...].astype(F32) for ref in refs[count : 3 * count]]
+        residual = residual + jnp.concatenate(moe_rows, axis=0)
+        gain_ref, so_far, out_ref, residual_ref, inv_ref = refs[3 * count :]
         inv_rms = inv_rms_of(residual)
         residual_ref[...] = residual
         inv_ref[...] = jnp.broadcast_to(inv_rms, inv_ref.shape)
@@ -418,9 +384,9 @@
     def norm(distances, blocks):
         rows = mid * len(blocks)
         mean_at["pooled"], *norm_at[distances] = call(
-            functools.partial(norm_kernel, distances, len(blocks)),
+            functools.partial(norm_kernel, distances),
             [(pooled_shape, F32), ((rows, feature_dim), F32), ((rows, LANES), F32)],
-            *tokens_at[distances],
+            *[tokens_at[k] for k in distances],
             *blocks,
             gain,
             mean_at["pooled"],
@@ -452,8 +418,8 @@
         preferred_element_type=F32,
     )
 
-    def backward_kernel(distances, residual_ref, inv_ref, gate_save, up_save, *refs):
-        grad_ref, gain_ref, wide_ref, down_ref, *outs = refs
+    def backward_kernel(distances, residual_ref, inv_ref, *refs):
+        saved, (grad_ref, gain_ref, wide_ref, down_ref, *outs) = refs[: 2 * len(distances)], refs[2 * len(distances) :]
         residual, inv_rms = residual_ref[...], inv_ref[:, :1]
         cube = inv_rms * inv_rms * inv_rms
         parts = []
@@ -467,8 +433,9 @@
         grads = []
         for local in range(local_experts):
             cols = slice(local * hidden_dim, (local + 1) * hidden_dim)
-            for save in (gate_save, up_save):
-                grads.append((down_back[:, cols] * save[:, cols].astype(F32)).astype(BF16))
+            for saves in (saved[::2], saved[1::2]):
+                save = jnp.concatenate([ref[:, cols] for ref in saves], axis=0).astype(F32)
+                grads.append((down_back[:, cols] * save).astype(BF16))
         total = dot(jnp.concatenate(grads, axis=1), wide_ref[...])
         if distances == (0,):
             total = total + resid_grad
@@ -488,7 +455,7 @@
             functools.partial(backward_kernel, distances),
             outs,
             *norm_at[distances],
-            *saved_at[distances],
+            *[save for k in distances for save in saved_at[k]],
             pooled_grad,
             gain,
             wide_t,
@@ -500,10 +467,10 @@
         else:
             back_at.update(zip(distances, result))
 
-    for distances in reversed(list(tokens_at)):
+    for distances in reversed(list(norm_at)):
         backward(distances)
     token_grad = pl.pallas_call(
-        sum_kernel,
+        functools.partial(sum_kernel, 3),
         out_shape=jax.ShapeDtypeStruct(block, BF16),
         in_specs=[pl.BlockSpec(memory_space=pltpu.VMEM)] * 3,
         out_specs=pl.BlockSpec(memory_space=pltpu.VMEM),

time: 125 us -> 129 us (1.032)
  waiting for transfers between devices: 39.1 us -> 47.1 us
  starting transfers between devices: 61.2 us -> 56.5 us
    ppermute x50 -> x36, waiting for transfers between devices: 35 us -> 42.3 us  [send(): return lax.ppermute(value, ('expert', 'group'), pairs)]
    ppermute x50 -> x36, starting transfers between devices: 56.1 us -> 50.7 us  [send(): return lax.ppermute(value, ('expert', 'group'), pairs)]
    pallas_call x35 -> x33, Pallas kernels: 17.3 us -> 18.2 us  [call(): pl.pallas_call(kernel, out_shape=[pltpu.VMEM(shape, dtype) for shape, dty...]
  transfers between devices with their start and end apart: 56 -> 42, of which waited for: 27 -> 29; matrix products, arithmetic and copies ran while one was open for 1% -> 1% of each run, Pallas kernels for 14% -> 14%
where the time goes in v13:
time: 129 us
  starting transfers between devices  56.5 us (44%)
  waiting for transfers between devices  47.1 us (37%)
  Pallas kernels  22.6 us (18%)
  matrix products  1.71 us (1%)
    ppermute x36, starting transfers between devices, send(): return lax.ppermute(value, ('expert', 'group'), pairs)  50.7 us
    ppermute x36, waiting for transfers between devices, send(): return lax.ppermute(value, ('expert', 'group'), pairs)  42.3 us
    pallas_call x33, Pallas kernels, call(): pl.pallas_call(kernel, out_shape=[pltpu.VMEM(shape, dtype) for shape, dty...  18.2 us
    ppermute x4, starting transfers between devices, body(): pooled_grad = pooled_grad + lax.ppermute(mine, 'expert', pairs).astype(F32)  5.28 us
    ppermute x4, waiting for transfers between devices, body(): pooled_grad = pooled_grad + lax.ppermute(mine, 'expert', pairs).astype(F32)  4.8 us
  transfers between devices with their start and end apart: 42, of which 29 were waited for; matrix products, arithmetic and copies ran while one was open for 1% of the time, Pallas kernels for 14%

profile of v13, /device:TPU:0, one launch (start us, length us, event | category | flops | bytes accessed | tf_op | source)
XLA Modules:
  0.0 128.8 jit_solution(18019955796301693956)
XLA Ops:
  0.6 1.9 %shard_map.104 = (bf16[128,1152]{1,0:T(8,128)(2,1)S(1)}, bf16[3200,384]{1,0:T(8,128)(2,1)S(1)}) custom-call(s32[8,128]{1,0:T(8,128)} %bitcast.19, f32[8,128]{1,0:T(8,128)} %bitcast.20, bf16[128,1024]{1,0:T(8,128)(2,1)} %refs_2_.2, bf16[2,512,384]{2,1,0:T(8,128)(2,1)} %refs_0_.1, bf16[2,512,384]{2,1,0:T(8,128)(2,1)} %refs_1_.1, bf16[2,192,1024]{2,1,0:T(8,128)(2,1)} %refs_2_.3), custom_call_target="tpu_custom_call" | custom-call | tf_op jit(solution)/shard_map/pallas_call | solution.py:215
  3.0 2.6 %collective-permute-start.1 = (bf16[128,1152]{1,0:T(8,128)(2,1)S(1)}, bf16[128,1152]{1,0:T(8,128)(2,1)S(1)}, u32[]{:S(2)}, u32[]{:S(2)}) collective-permute-start(bf16[128,1152]{1,0:T(8,128)(2,1)S(1)} %get-tuple-element.55.block_ref.refs_0_), channel_id=1, source_target_pairs={{0,4},{1,3},{4,8},{5,1},{8,12},{9,5},{12,14},{13,9},{14,10},{15,13... | collective-permute-start | bytes 884744 | tf_op jit(solution)/shard_map/ppermute | solution.py:56
  5.7 4.6 %collective-permute-done.1.block_ref.refs_0_ = bf16[128,1152]{1,0:T(8,128)(2,1)S(1)} collective-permute-done((bf16[128,1152]{1,0:T(8,128)(2,1)S(1)}, bf16[128,1152]{1,0:T(8,128)(2,1)S(1)}, u32[]{:S(2)}, u32[]{:S(2)}) %collective-permute-start.1) | collective-permute-done | bytes 294944 | tf_op jit(solution)/shard_map/ppermute | solution.py:56
  10.3 2.1 %collective-permute-start.2 = (bf16[128,1152]{1,0:T(8,128)(2,1)S(1)}, bf16[128,1152]{1,0:T(8,128)(2,1)S(1)}, u32[]{:S(2)}, u32[]{:S(2)}) collective-permute-start(bf16[128,1152]{1,0:T(8,128)(2,1)S(1)} %collective-permute-done.1.block_ref.refs_0_), channel_id=1, source_target_pairs={{0,4},{1,3},{4,8},{5,1},{8,12},{9,5},{12,14},{13,9},{14,10},{15,13... | collective-permute-start | bytes 884744 | tf_op jit(solution)/shard_map/ppermute | solution.py:56
  17.0 2.1 %collective-permute-start.3 = (bf16[128,1152]{1,0:T(8,128)(2,1)S(1)}, bf16[128,1152]{1,0:T(8,128)(2,1)S(1)}, u32[]{:S(2)}, u32[]{:S(2)}) collective-permute-start(bf16[128,1152]{1,0:T(8,128)(2,1)S(1)} %collective-permute-done.2.block_ref.refs_0_), channel_id=1, source_target_pairs={{0,4},{1,3},{4,8},{5,1},{8,12},{9,5},{12,14},{13,9},{14,10},{15,13... | collective-permute-start | bytes 884744 | tf_op jit(solution)/shard_map/ppermute | solution.py:56
  36.1 2.0 %collective-permute-done.5.block_ref.refs_1_ = bf16[128,1152]{1,0:T(8,128)(2,1)S(1)} collective-permute-done((bf16[128,1152]{1,0:T(8,128)(2,1)S(1)}, bf16[128,1152]{1,0:T(8,128)(2,1)S(1)}, u32[]{:S(2)}, u32[]{:S(2)}) %collective-permute-start.5) | collective-permute-done | bytes 294944 | tf_op jit(solution)/shard_map/ppermute | solution.py:56
  42.6 2.2 %collective-permute-done.6.block_ref.refs_1_ = bf16[128,1152]{1,0:T(8,128)(2,1)S(1)} collective-permute-done((bf16[128,1152]{1,0:T(8,128)(2,1)S(1)}, bf16[128,1152]{1,0:T(8,128)(2,1)S(1)}, u32[]{:S(2)}, u32[]{:S(2)}) %collective-permute-start.6) | collective-permute-done | bytes 294944 | tf_op jit(solution)/shard_map/ppermute | solution.py:56
  49.3 2.2 %collective-permute-done.7.block_ref.refs_1_ = bf16[128,1152]{1,0:T(8,128)(2,1)S(1)} collective-permute-done((bf16[128,1152]{1,0:T(8,128)(2,1)S(1)}, bf16[128,1152]{1,0:T(8,128)(2,1)S(1)}, u32[]{:S(2)}, u32[]{:S(2)}) %collective-permute-start.7) | collective-permute-done | bytes 294944 | tf_op jit(solution)/shard_map/ppermute | solution.py:56
  52.5 1.9 %collective-permute-done.13.arrived_ref = bf16[128,1024]{1,0:T(8,128)(2,1)S(1)} collective-permute-done((bf16[128,1024]{1,0:T(8,128)(2,1)S(1)}, bf16[128,1024]{1,0:T(8,128)(2,1)S(1)}, u32[]{:S(2)}, u32[]{:S(2)}) %collective-permute-start.13) | collective-permute-done | bytes 262176 | tf_op jit(solution)/shard_map/ppermute | solution.py:56
  57.0 5.8 %collective-permute-done.14.refs_1_ = bf16[128,1024]{1,0:T(8,128)(2,1)S(1)} collective-permute-done((bf16[128,1024]{1,0:T(8,128)(2,1)S(1)}, bf16[128,1024]{1,0:T(8,128)(2,1)S(1)}, u32[]{:S(2)}, u32[]{:S(2)}) %collective-permute-start.14) | collective-permute-done | bytes 262176 | tf_op jit(solution)/shard_map/ppermute | solution.py:56
  62.8 2.5 %collective-permute-start.15 = (bf16[64,1024]{1,0:T(8,128)(2,1)S(1)}, bf16[64,1024]{1,0:T(8,128)(2,1)S(1)}, u32[]{:S(2)}, u32[]{:S(2)}) collective-permute-start(bf16[64,1024]{1,0:T(8,128)(2,1)S(1)} %get-tuple-element.67.refs_1_), channel_id=1, source_target_pairs={{0,4},{1,3},{4,8},{5,1},{8,12},{9,5},{12,14},{13,9},{14,10},{15,13... | collective-permute-start | bytes 393224 | tf_op jit(solution)/shard_map/ppermute | solution.py:56
  65.4 2.1 %collective-permute-start.23 = (bf16[64,1024]{1,0:T(8,128)(2,1)S(1)}, bf16[64,1024]{1,0:T(8,128)(2,1)S(1)}, u32[]{:S(2)}, u32[]{:S(2)}) collective-permute-start(bf16[64,1024]{1,0:T(8,128)(2,1)S(1)} %get-tuple-element.68.refs_2_), channel_id=1, source_target_pairs={{0,4},{1,3},{4,8},{5,1},{8,12},{9,5},{12,14},{13,9},{14,10},{15,13... | collective-permute-start | bytes 393224 | tf_op jit(solution)/shard_map/ppermute | solution.py:56
  67.4 1.8 %collective-permute-done.15.refs_2_ = bf16[64,1024]{1,0:T(8,128)(2,1)S(1)} collective-permute-done((bf16[64,1024]{1,0:T(8,128)(2,1)S(1)}, bf16[64,1024]{1,0:T(8,128)(2,1)S(1)}, u32[]{:S(2)}, u32[]{:S(2)}) %collective-permute-start.15) | collective-permute-done | bytes 131104 | tf_op jit(solution)/shard_map/ppermute | solution.py:56
  69.3 2.5 %collective-permute-start.16 = (bf16[64,1024]{1,0:T(8,128)(2,1)S(1)}, bf16[64,1024]{1,0:T(8,128)(2,1)S(1)}, u32[]{:S(2)}, u32[]{:S(2)}) collective-permute-start(bf16[64,1024]{1,0:T(8,128)(2,1)S(1)} %collective-permute-done.15.refs_2_), channel_id=1, source_target_pairs={{0,4},{1,3},{4,8},{5,1},{8,12},{9,5},{12,14},{13,9},{14,10},{15,13... | collective-permute-start | bytes 393224 | tf_op jit(solution)/shard_map/ppermute | solution.py:56
  71.8 2.6 %collective-permute-done.26.refs_4_ = bf16[64,1024]{1,0:T(8,128)(2,1)S(1)} collective-permute-done((bf16[64,1024]{1,0:T(8,128)(2,1)S(1)}, bf16[64,1024]{1,0:T(8,128)(2,1)S(1)}, u32[]{:S(2)}, u32[]{:S(2)}) %collective-permute-start.26) | collective-permute-done | bytes 131104 | tf_op jit(solution)/shard_map/ppermute | solution.py:56
  74.3 2.0 %collective-permute-start.24 = (bf16[64,1024]{1,0:T(8,128)(2,1)S(1)}, bf16[64,1024]{1,0:T(8,128)(2,1)S(1)}, u32[]{:S(2)}, u32[]{:S(2)}) collective-permute-start(bf16[64,1024]{1,0:T(8,128)(2,1)S(1)} %collective-permute-done.23.refs_3_), channel_id=1, source_target_pairs={{0,4},{1,3},{4,8},{5,1},{8,12},{9,5},{12,14},{13,9},{14,10},{15,13... | collective-permute-start | bytes 393224 | tf_op jit(solution)/shard_map/ppermute | solution.py:56
  79.3 2.0 %collective-permute-start.25 = (bf16[64,1024]{1,0:T(8,128)(2,1)S(1)}, bf16[64,1024]{1,0:T(8,128)(2,1)S(1)}, u32[]{:S(2)}, u32[]{:S(2)}) collective-permute-start(bf16[64,1024]{1,0:T(8,128)(2,1)S(1)} %collective-permute-done.24.refs_3_), channel_id=1, source_target_pairs={{0,4},{1,3},{4,8},{5,1},{8,12},{9,5},{12,14},{13,9},{14,10},{15,13... | collective-permute-start | bytes 393224 | tf_op jit(solution)/shard_map/ppermute | solution.py:56
  89.2 2.9 %collective-permute-done.29 = bf16[8,1024]{1,0:T(8,128)(2,1)S(1)} collective-permute-done((bf16[8,1024]{1,0:T(8,128)(2,1)S(1)}, bf16[8,1024]{1,0:T(8,128)(2,1)S(1)}, u32[]{:S(2)}, u32[]{:S(2)}) %collective-permute-start.29) | collective-permute-done | bytes 16416 | tf_op jit(solution)/shard_map/ppermute | solution.py:407
  92.2 3.5 %collective-permute-start.32 = (bf16[8,1024]{1,0:T(8,128)(2,1)S(1)}, bf16[8,1024]{1,0:T(8,128)(2,1)S(1)}, u32[]{:S(2)}, u32[]{:S(2)}) collective-permute-start(bf16[8,1024]{1,0:T(8,128)(2,1)S(1)} %add_convert_fusion), channel_id=1, source_target_pairs={{0,12},{2,14},{4,8},{6,10},{8,4},{10,6},{12,0},{14,2},{1,13},{3,15... | collective-permute-start | bytes 49160 | tf_op jit(solution)/shard_map/ppermute | solution.py:407
  98.4 1.9 %collective-permute-done.31 = bf16[8,1024]{1,0:T(8,128)(2,1)S(1)} collective-permute-done((bf16[8,1024]{1,0:T(8,128)(2,1)S(1)}, bf16[8,1024]{1,0:T(8,128)(2,1)S(1)}, u32[]{:S(2)}, u32[]{:S(2)}) %collective-permute-start.31) | collective-permute-done | bytes 16416 | tf_op jit(solution)/shard_map/ppermute | solution.py:407
  110.3 2.6 %collective-permute-done.38.arrived_ref = bf16[128,1024]{1,0:T(8,128)(2,1)S(1)} collective-permute-done((bf16[128,1024]{1,0:T(8,128)(2,1)S(1)}, bf16[128,1024]{1,0:T(8,128)(2,1)S(1)}, u32[]{:S(2)}, u32[]{:S(2)}) %collective-permute-start.38) | collective-permute-done | bytes 262176 | tf_op jit(solution)/shard_map/ppermute | solution.py:56
  113.5 2.5 %collective-permute-start.35 = (bf16[128,1024]{1,0:T(8,128)(2,1)S(1)}, bf16[128,1024]{1,0:T(8,128)(2,1)S(1)}, u32[]{:S(2)}, u32[]{:S(2)}) collective-permute-start(bf16[128,1024]{1,0:T(8,128)(2,1)S(1)} %shard_map.134), channel_id=1, source_target_pairs={{0,4},{1,3},{4,8},{5,1},{8,12},{9,5},{12,14},{13,9},{14,10},{15,13... | collective-permute-start | bytes 786440 | tf_op jit(solution)/shard_map/ppermute | solution.py:56
  117.6 2.1 %collective-permute-done.39.arrived_ref = bf16[128,1024]{1,0:T(8,128)(2,1)S(1)} collective-permute-done((bf16[128,1024]{1,0:T(8,128)(2,1)S(1)}, bf16[128,1024]{1,0:T(8,128)(2,1)S(1)}, u32[]{:S(2)}, u32[]{:S(2)}) %collective-permute-start.39) | collective-permute-done | bytes 262176 | tf_op jit(solution)/shard_map/ppermute | solution.py:56
  121.6 2.5 %collective-permute-start.36 = (bf16[128,1024]{1,0:T(8,128)(2,1)S(1)}, bf16[128,1024]{1,0:T(8,128)(2,1)S(1)}, u32[]{:S(2)}, u32[]{:S(2)}) collective-permute-start(bf16[128,1024]{1,0:T(8,128)(2,1)S(1)} %shard_map.135), channel_id=1, source_target_pairs={{0,4},{1,3},{4,8},{5,1},{8,12},{9,5},{12,14},{13,9},{14,10},{15,13... | collective-permute-start | bytes 786440 | tf_op jit(solution)/shard_map/ppermute | solution.py:56
  (111 shorter events, 66.9 us)
Async XLA Ops:
  2.5 9.9 %collective-permute-start = (bf16[3200,384]{1,0:T(8,128)(2,1)S(1)}, bf16[3200,384]{1,0:T(8,128)(2,1)S(1)}, u32[]{:S(2)}, u32[]{:S(2)}) collective-permute-start(bf16[3200,384]{1,0:T(8,128)(2,1)S(1)} %get-tuple-element.56), channel_id=1, source_target_pairs={{0,1},{1,0},{2,3},{3,2},{4,5},{5,4},{6,7},{7,6},{8,9},{9,8},{10,11... | collective-permute-start | bytes 7372808 | tf_op jit(solution)/shard_map/ppermute | solution.py:310
  3.0 7.3 %collective-permute-start.1 = (bf16[128,1152]{1,0:T(8,128)(2,1)S(1)}, bf16[128,1152]{1,0:T(8,128)(2,1)S(1)}, u32[]{:S(2)}, u32[]{:S(2)}) collective-permute-start(bf16[128,1152]{1,0:T(8,128)(2,1)S(1)} %get-tuple-element.55.block_ref.refs_0_), channel_id=1, source_target_pairs={{0,4},{1,3},{4,8},{5,1},{8,12},{9,5},{12,14},{13,9},{14,10},{15,13... | collective-permute-start | bytes 884744 | tf_op jit(solution)/shard_map/ppermute | solution.py:56
  10.3 6.7 %collective-permute-start.2 = (bf16[128,1152]{1,0:T(8,128)(2,1)S(1)}, bf16[128,1152]{1,0:T(8,128)(2,1)S(1)}, u32[]{:S(2)}, u32[]{:S(2)}) collective-permute-start(bf16[128,1152]{1,0:T(8,128)(2,1)S(1)} %collective-permute-done.1.block_ref.refs_0_), channel_id=1, source_target_pairs={{0,4},{1,3},{4,8},{5,1},{8,12},{9,5},{12,14},{13,9},{14,10},{15,13... | collective-permute-start | bytes 884744 | tf_op jit(solution)/shard_map/ppermute | solution.py:56
  15.1 6.4 %collective-permute-start.8 = (bf16[128,1024]{1,0:T(8,128)(2,1)S(1)}, bf16[128,1024]{1,0:T(8,128)(2,1)S(1)}, u32[]{:S(2)}, u32[]{:S(2)}) collective-permute-start(bf16[128,1024]{1,0:T(8,128)(2,1)S(1)} %get-tuple-element.66), channel_id=1, source_target_pairs={{0,4},{1,3},{4,8},{5,1},{8,12},{9,5},{12,14},{13,9},{14,10},{15,13... | collective-permute-start | bytes 786440 | tf_op jit(solution)/shard_map/ppermute | solution.py:56
  17.0 7.7 %collective-permute-start.3 = (bf16[128,1152]{1,0:T(8,128)(2,1)S(1)}, bf16[128,1152]{1,0:T(8,128)(2,1)S(1)}, u32[]{:S(2)}, u32[]{:S(2)}) collective-permute-start(bf16[128,1152]{1,0:T(8,128)(2,1)S(1)} %collective-permute-done.2.block_ref.refs_0_), channel_id=1, source_target_pairs={{0,4},{1,3},{4,8},{5,1},{8,12},{9,5},{12,14},{13,9},{14,10},{15,13... | collective-permute-start | bytes 884744 | tf_op jit(solution)/shard_map/ppermute | solution.py:56
  24.7 6.7 %collective-permute-start.4 = (bf16[128,1152]{1,0:T(8,128)(2,1)S(1)}, bf16[128,1152]{1,0:T(8,128)(2,1)S(1)}, u32[]{:S(2)}, u32[]{:S(2)}) collective-permute-start(bf16[128,1152]{1,0:T(8,128)(2,1)S(1)} %collective-permute-done.3.block_ref.refs_0_), channel_id=1, source_target_pairs={{0,4},{1,3},{4,8},{5,1},{8,12},{9,5},{12,14},{13,9},{14,10},{15,13... | collective-permute-start | bytes 884744 | tf_op jit(solution)/shard_map/ppermute | solution.py:56
  31.4 6.7 %collective-permute-start.5 = (bf16[128,1152]{1,0:T(8,128)(2,1)S(1)}, bf16[128,1152]{1,0:T(8,128)(2,1)S(1)}, u32[]{:S(2)}, u32[]{:S(2)}) collective-permute-start(bf16[128,1152]{1,0:T(8,128)(2,1)S(1)} %collective-permute-done.4.block_ref.refs_0_), channel_id=1, source_target_pairs={{0,4},{1,3},{4,8},{5,1},{8,12},{9,5},{12,14},{13,9},{14,10},{15,13... | collective-permute-start | bytes 884744 | tf_op jit(solution)/shard_map/ppermute | solution.py:56
  34.5 6.4 %collective-permute-start.11 = (bf16[128,1024]{1,0:T(8,128)(2,1)S(1)}, bf16[128,1024]{1,0:T(8,128)(2,1)S(1)}, u32[]{:S(2)}, u32[]{:S(2)}) collective-permute-start(bf16[128,1024]{1,0:T(8,128)(2,1)S(1)} %shard_map.116), channel_id=1, source_target_pairs={{0,4},{1,3},{4,8},{5,1},{8,12},{9,5},{12,14},{13,9},{14,10},{15,13... | collective-permute-start | bytes 786440 | tf_op jit(solution)/shard_map/ppermute | solution.py:56
  38.1 6.7 %collective-permute-start.6 = (bf16[128,1152]{1,0:T(8,128)(2,1)S(1)}, bf16[128,1152]{1,0:T(8,128)(2,1)S(1)}, u32[]{:S(2)}, u32[]{:S(2)}) collective-permute-start(bf16[128,1152]{1,0:T(8,128)(2,1)S(1)} %collective-permute-done.5.block_ref.refs_1_), channel_id=1, source_target_pairs={{0,4},{1,3},{4,8},{5,1},{8,12},{9,5},{12,14},{13,9},{14,10},{15,13... | collective-permute-start | bytes 884744 | tf_op jit(solution)/shard_map/ppermute | solution.py:56
  41.0 6.7 %collective-permute-start.12 = (bf16[128,1024]{1,0:T(8,128)(2,1)S(1)}, bf16[128,1024]{1,0:T(8,128)(2,1)S(1)}, u32[]{:S(2)}, u32[]{:S(2)}) collective-permute-start(bf16[128,1024]{1,0:T(8,128)(2,1)S(1)} %shard_map.117), channel_id=1, source_target_pairs={{0,4},{1,3},{4,8},{5,1},{8,12},{9,5},{12,14},{13,9},{14,10},{15,13... | collective-permute-start | bytes 786440 | tf_op jit(solution)/shard_map/ppermute | solution.py:56
  44.8 6.7 %collective-permute-start.7 = (bf16[128,1152]{1,0:T(8,128)(2,1)S(1)}, bf16[128,1152]{1,0:T(8,128)(2,1)S(1)}, u32[]{:S(2)}, u32[]{:S(2)}) collective-permute-start(bf16[128,1152]{1,0:T(8,128)(2,1)S(1)} %collective-permute-done.6.block_ref.refs_1_), channel_id=1, source_target_pairs={{0,4},{1,3},{4,8},{5,1},{8,12},{9,5},{12,14},{13,9},{14,10},{15,13... | collective-permute-start | bytes 884744 | tf_op jit(solution)/shard_map/ppermute | solution.py:56
  47.7 6.7 %collective-permute-start.13 = (bf16[128,1024]{1,0:T(8,128)(2,1)S(1)}, bf16[128,1024]{1,0:T(8,128)(2,1)S(1)}, u32[]{:S(2)}, u32[]{:S(2)}) collective-permute-start(bf16[128,1024]{1,0:T(8,128)(2,1)S(1)} %shard_map.118), channel_id=1, source_target_pairs={{0,4},{1,3},{4,8},{5,1},{8,12},{9,5},{12,14},{13,9},{14,10},{15,13... | collective-permute-start | bytes 786440 | tf_op jit(solution)/shard_map/ppermute | solution.py:56
  54.4 8.3 %collective-permute-start.14 = (bf16[128,1024]{1,0:T(8,128)(2,1)S(1)}, bf16[128,1024]{1,0:T(8,128)(2,1)S(1)}, u32[]{:S(2)}, u32[]{:S(2)}) collective-permute-start(bf16[128,1024]{1,0:T(8,128)(2,1)S(1)} %shard_map.119), channel_id=1, source_target_pairs={{0,4},{1,3},{4,8},{5,1},{8,12},{9,5},{12,14},{13,9},{14,10},{15,13... | collective-permute-start | bytes 786440 | tf_op jit(solution)/shard_map/ppermute | solution.py:56
  62.8 6.4 %collective-permute-start.15 = (bf16[64,1024]{1,0:T(8,128)(2,1)S(1)}, bf16[64,1024]{1,0:T(8,128)(2,1)S(1)}, u32[]{:S(2)}, u32[]{:S(2)}) collective-permute-start(bf16[64,1024]{1,0:T(8,128)(2,1)S(1)} %get-tuple-element.67.refs_1_), channel_id=1, source_target_pairs={{0,4},{1,3},{4,8},{5,1},{8,12},{9,5},{12,14},{13,9},{14,10},{15,13... | collective-permute-start | bytes 393224 | tf_op jit(solution)/shard_map/ppermute | solution.py:56
  65.4 9.0 %collective-permute-start.26 = (bf16[64,1024]{1,0:T(8,128)(2,1)S(1)}, bf16[64,1024]{1,0:T(8,128)(2,1)S(1)}, u32[]{:S(2)}, u32[]{:S(2)}) collective-permute-start(bf16[64,1024]{1,0:T(8,128)(2,1)S(1)} %get-tuple-element.67.refs_1_), channel_id=1, source_target_pairs={{0,2},{1,5},{4,0},{5,9},{8,4},{9,13},{12,8},{13,15},{14,12},{15,11... | collective-permute-start | bytes 393224 | tf_op jit(solution)/shard_map/ppermute | solution.py:56
  65.4 9.0 %collective-permute-start.23 = (bf16[64,1024]{1,0:T(8,128)(2,1)S(1)}, bf16[64,1024]{1,0:T(8,128)(2,1)S(1)}, u32[]{:S(2)}, u32[]{:S(2)}) collective-permute-start(bf16[64,1024]{1,0:T(8,128)(2,1)S(1)} %get-tuple-element.68.refs_2_), channel_id=1, source_target_pairs={{0,4},{1,3},{4,8},{5,1},{8,12},{9,5},{12,14},{13,9},{14,10},{15,13... | collective-permute-start | bytes 393224 | tf_op jit(solution)/shard_map/ppermute | solution.py:56
  69.3 7.1 %collective-permute-start.16 = (bf16[64,1024]{1,0:T(8,128)(2,1)S(1)}, bf16[64,1024]{1,0:T(8,128)(2,1)S(1)}, u32[]{:S(2)}, u32[]{:S(2)}) collective-permute-start(bf16[64,1024]{1,0:T(8,128)(2,1)S(1)} %collective-permute-done.15.refs_2_), channel_id=1, source_target_pairs={{0,4},{1,3},{4,8},{5,1},{8,12},{9,5},{12,14},{13,9},{14,10},{15,13... | collective-permute-start | bytes 393224 | tf_op jit(solution)/shard_map/ppermute | solution.py:56
  106.5 6.4 %collective-permute-start.38 = (bf16[128,1024]{1,0:T(8,128)(2,1)S(1)}, bf16[128,1024]{1,0:T(8,128)(2,1)S(1)}, u32[]{:S(2)}, u32[]{:S(2)}) collective-permute-start(bf16[128,1024]{1,0:T(8,128)(2,1)S(1)} %shard_map.136), channel_id=1, source_target_pairs={{0,2},{1,5},{4,0},{5,9},{8,4},{9,13},{12,8},{13,15},{14,12},{15,11... | collective-permute-start | bytes 786440 | tf_op jit(solution)/shard_map/ppermute | solution.py:56
  106.9 6.6 %collective-permute-start.34 = (bf16[128,1024]{1,0:T(8,128)(2,1)S(1)}, bf16[128,1024]{1,0:T(8,128)(2,1)S(1)}, u32[]{:S(2)}, u32[]{:S(2)}) collective-permute-start(bf16[128,1024]{1,0:T(8,128)(2,1)S(1)} %shard_map.133), channel_id=1, source_target_pairs={{0,4},{1,3},{4,8},{5,1},{8,12},{9,5},{12,14},{13,9},{14,10},{15,13... | collective-permute-start | bytes 786440 | tf_op jit(solution)/shard_map/ppermute | solution.py:56
  108.6 7.4 %collective-permute-start.41 = (bf16[8,1274]{1,0:T(8,128)(2,1)S(1)}, bf16[8,1274]{1,0:T(8,128)(2,1)S(1)}, u32[]{:S(2)}, u32[]{:S(2)}) collective-permute-start(bf16[8,1274]{1,0:T(8,128)(2,1)S(1)} %pad_maximum_fusion.1), channel_id=1, source_target_pairs={{0,1},{1,0},{2,3},{3,2},{4,5},{5,4},{6,7},{7,6},{8,9},{9,8},{10,11... | collective-permute-start | bytes 61160 | tf_op jit(solution)/shard_map/ppermute | solution.py:411
  112.9 6.8 %collective-permute-start.39 = (bf16[128,1024]{1,0:T(8,128)(2,1)S(1)}, bf16[128,1024]{1,0:T(8,128)(2,1)S(1)}, u32[]{:S(2)}, u32[]{:S(2)}) collective-permute-start(bf16[128,1024]{1,0:T(8,128)(2,1)S(1)} %shard_map.137), channel_id=1, source_target_pairs={{0,2},{1,5},{4,0},{5,9},{8,4},{9,13},{12,8},{13,15},{14,12},{15,11... | collective-permute-start | bytes 786440 | tf_op jit(solution)/shard_map/ppermute | solution.py:56
  113.5 8.1 %collective-permute-start.35 = (bf16[128,1024]{1,0:T(8,128)(2,1)S(1)}, bf16[128,1024]{1,0:T(8,128)(2,1)S(1)}, u32[]{:S(2)}, u32[]{:S(2)}) collective-permute-start(bf16[128,1024]{1,0:T(8,128)(2,1)S(1)} %shard_map.134), channel_id=1, source_target_pairs={{0,4},{1,3},{4,8},{5,1},{8,12},{9,5},{12,14},{13,9},{14,10},{15,13... | collective-permute-start | bytes 786440 | tf_op jit(solution)/shard_map/ppermute | solution.py:56
  119.8 7.1 %collective-permute-start.40 = (bf16[128,1024]{1,0:T(8,128)(2,1)S(1)}, bf16[128,1024]{1,0:T(8,128)(2,1)S(1)}, u32[]{:S(2)}, u32[]{:S(2)}) collective-permute-start(bf16[128,1024]{1,0:T(8,128)(2,1)S(1)} %shard_map.138), channel_id=1, source_target_pairs={{0,2},{1,5},{4,0},{5,9},{8,4},{9,13},{12,8},{13,15},{14,12},{15,11... | collective-permute-start | bytes 786440 | tf_op jit(solution)/shard_map/ppermute | solution.py:56
  121.6 6.4 %collective-permute-start.36 = (bf16[128,1024]{1,0:T(8,128)(2,1)S(1)}, bf16[128,1024]{1,0:T(8,128)(2,1)S(1)}, u32[]{:S(2)}, u32[]{:S(2)}) collective-permute-start(bf16[128,1024]{1,0:T(8,128)(2,1)S(1)} %shard_map.135), channel_id=1, source_target_pairs={{0,4},{1,3},{4,8},{5,1},{8,12},{9,5},{12,14},{13,9},{14,10},{15,13... | collective-permute-start | bytes 786440 | tf_op jit(solution)/shard_map/ppermute | solution.py:56
  (21 other events, 236.3 us)

commit v14 on v13

--- a/solution.py
+++ b/solution.py
@@ -36,6 +36,21 @@
     )(*args)
 
 
+def after(value, guards):
+    def kernel(*refs):
+        pass
+
+    args = [pltpu.with_memory_space_constraint(a, pltpu.VMEM) for a in (value, *guards)]
+    return pl.pallas_call(
+        kernel,
+        out_shape=pltpu.VMEM(value.shape, value.dtype),
+        in_specs=[pl.BlockSpec(memory_space=pltpu.VMEM)] * len(args),
+        out_specs=pl.BlockSpec(memory_space=pltpu.VMEM),
+        input_output_aliases={0: 0},
+        compiler_params=pltpu.CompilerParams(vmem_limit_bytes=VMEM_LIMIT),
+    )(*args)
+
+
 class Ring:
     def __init__(self, expert_count, group_count):
         self.count = expert_count
@@ -67,21 +82,30 @@
             there = jnp.where(there < self.half, 2 * there, 2 * (count - 1 - there) + 1)
         return there
 
-    def signed(self, behind):
-        return -behind if behind < self.half else self.count - behind
-
-    def gather_round(self, own):
+    def signed(self, distance):
+        distance %= self.count
+        return distance if distance <= self.half else distance - self.count
+
+    def gather_whole(self, own, meanwhile):
         blocks = {0: own}
-        for behind in range(1, self.count):
-            own = self.send(own, 1)
-            blocks[self.signed(behind)] = own
+        from_left = from_right = own
+        for step in range(1, self.half + 1):
+            if step > 2:
+                guards = meanwhile(step - 2, blocks)
+                from_left = after(from_left, guards)
+                from_right = after(from_right, guards) if step < self.half else from_right
+            from_left = self.send(from_left, 1)
+            blocks[self.signed(-step)] = from_left
+            if step < self.half:
+                from_right = self.send(from_right, -1)
+                blocks[step] = from_right
         return blocks
 
-    def scatter_round(self, parts):
-        total = parts[self.signed(1)]
-        for behind in range(2, self.count):
-            total = add(parts[self.signed(behind)], self.send(total, 1))
-        return self.send(total, 1)
+    def scatter_hop(self, step, parts, arrived):
+        top, bottom = parts[self.signed(-step)][0], parts[self.signed(step)][1]
+        if arrived:
+            top, bottom = add(top, arrived[0]), add(bottom, arrived[1])
+        return self.send(top, 1), self.send(bottom, -1)
 
     def gather(self, top, bottom, use):
         top_left = top_right = top
@@ -314,9 +338,11 @@
         packed = None
     wide, down = full_weights(shards, packed)
 
-    def forward_kernel(block_ref, wide_ref, down_ref, gate_save, up_save, out_ref):
-        x = block_ref[:, :feature_dim]
-        weights = block_ref[:, feature_dim:].astype(F32)
+    def forward_kernel(count, *refs):
+        wide_ref, down_ref, gate_save, up_save, *outs = refs[count:]
+        blocks = [ref[...] for ref in refs[:count]]
+        rows = jnp.concatenate(blocks, axis=0) if count > 1 else blocks[0]
+        x, weights = rows[:, :feature_dim], rows[:, feature_dim:].astype(F32)
         lane = lax.broadcasted_iota(jnp.int32, weights.shape, 1)
         hidden = []
         for local in range(local_experts):
@@ -332,28 +358,50 @@
             gate_save[:, cols] = (up_act * slope).astype(BF16)
             up_save[:, cols] = silu.astype(BF16)
             hidden.append((silu * up_act).astype(BF16))
-        out_ref[...] = dot(jnp.concatenate(hidden, axis=1), down_ref[...]).astype(out_ref.dtype)
-
-    tokens_at = ring.gather_round(own)
+        total = dot(jnp.concatenate(hidden, axis=1), down_ref[...])
+        for i, out in enumerate(outs):
+            out[...] = total[i * mid : (i + 1) * mid].astype(out.dtype)
+
     part_at, saved_at = {}, {}
     flops = 2 * rows_here * feature_dim * hidden_dim * local_experts * 3
-    for k, rows in tokens_at.items():
-        *saved_at[k], part_at[k] = call(
-            forward_kernel,
-            [((rows_here, local_experts * hidden_dim), BF16)] * 2
-            + [(block, BF16 if k == ring.signed(1) else F32)],
-            rows,
+
+    def forward(distances, blocks):
+        count = len(distances)
+        first_sends = ((ring.signed(-1), 0), (ring.signed(1), 1))
+        results = call(
+            functools.partial(forward_kernel, count),
+            [((rows_here * count, local_experts * hidden_dim), BF16)] * 2
+            + [
+                ((mid, feature_dim), BF16 if (k, half) in first_sends else F32)
+                for k in distances
+                for half in (0, 1)
+            ],
+            *[blocks[k] for k in distances],
             wide,
             down,
-            flops=flops,
+            flops=flops * count,
         )
+        saved_at[distances] = results[:2]
+        part_at.update({k: results[2 + 2 * i : 4 + 2 * i] for i, k in enumerate(distances)})
+
+    arrived = []
+
+    def scatter_on(step, blocks):
+        forward((-step, step), blocks)
+        arrived[:] = ring.scatter_hop(step, part_at, arrived)
+        return arrived
+
+    tokens_at = ring.gather_whole(own, scatter_on)
+    for distances in [(0,)] + [(-k, k) for k in range(1, ring.half)] + [(ring.half,)]:
+        if distances not in saved_at:
+            forward(distances, tokens_at)
+    for step in range(max(1, ring.half - 1), expert_count):
+        arrived[:] = ring.scatter_hop(step, part_at, arrived)
     gain = norm_gain.reshape(1, feature_dim)
-    moe_top, moe_bottom = call(
-        functools.partial(sum_kernel, 2),
-        [((mid, feature_dim), BF16)] * 2,
-        part_at[0],
-        ring.scatter_round(part_at),
-    )
+    moe_top, moe_bottom = [
+        call(functools.partial(sum_kernel, 2), [((mid, feature_dim), BF16)], part, others)[0]
+        for part, others in zip(part_at[0], arrived)
+    ]
 
     norm_at, mean_at = {}, {}
 
@@ -418,8 +466,8 @@
         preferred_element_type=F32,
     )
 
-    def backward_kernel(distances, residual_ref, inv_ref, *refs):
-        saved, (grad_ref, gain_ref, wide_ref, down_ref, *outs) = refs[: 2 * len(distances)], refs[2 * len(distances) :]
+    def backward_kernel(distances, residual_ref, inv_ref, gate_save, up_save, *refs):
+        grad_ref, gain_ref, wide_ref, down_ref, *outs = refs
         residual, inv_rms = residual_ref[...], inv_ref[:, :1]
         cube = inv_rms * inv_rms * inv_rms
         parts = []
@@ -433,9 +481,8 @@
         grads = []
         for local in range(local_experts):
             cols = slice(local * hidden_dim, (local + 1) * hidden_dim)
-            for saves in (saved[::2], saved[1::2]):
-                save = jnp.concatenate([ref[:, cols] for ref in saves], axis=0).astype(F32)
-                grads.append((down_back[:, cols] * save).astype(BF16))
+            for save in (gate_save, up_save):
+                grads.append((down_back[:, cols] * save[:, cols].astype(F32)).astype(BF16))
         total = dot(jnp.concatenate(grads, axis=1), wide_ref[...])
         if distances == (0,):
             total = total + resid_grad
@@ -455,7 +502,7 @@
             functools.partial(backward_kernel, distances),
             outs,
             *norm_at[distances],
-            *[save for k in distances for save in saved_at[k]],
+            *saved_at[distances],
             pooled_grad,
             gain,
             wide_t,

time: 129 us -> 136 us (1.054)
  waiting for transfers between devices: 47.1 us -> 64.3 us
  starting transfers between devices: 56.5 us -> 47.2 us
    ppermute x36 -> x43, waiting for transfers between devices: 42.3 us -> 59.8 us  [send(): return lax.ppermute(value, ('expert', 'group'), pairs)]
    ppermute x36 -> x43, starting transfers between devices: 50.7 us -> 41.3 us  [send(): return lax.ppermute(value, ('expert', 'group'), pairs)]
    pallas_call x33 -> x37, Pallas kernels: 18.2 us -> 17.3 us  [call(): pl.pallas_call(kernel, out_shape=[pltpu.VMEM(shape, dtype) for shape, dty...]
  transfers between devices with their start and end apart: 42 -> 49, of which waited for: 29 -> 35; matrix products, arithmetic and copies ran while one was open for 1% -> 1% of each run, Pallas kernels for 14% -> 13%
where the time goes in v14:
time: 136 us
  waiting for transfers between devices  64.3 us (47%)
  starting transfers between devices  47.2 us (35%)
  Pallas kernels  21.7 us (16%)
  matrix products  1.71 us (1%)
    ppermute x43, waiting for transfers between devices, send(): return lax.ppermute(value, ('expert', 'group'), pairs)  59.8 us
    ppermute x43, starting transfers between devices, send(): return lax.ppermute(value, ('expert', 'group'), pairs)  41.3 us
    pallas_call x37, Pallas kernels, call(): pl.pallas_call(kernel, out_shape=[pltpu.VMEM(shape, dtype) for shape, dty...  17.3 us
    ppermute x4, starting transfers between devices, body(): pooled_grad = pooled_grad + lax.ppermute(mine, 'expert', pairs).astype(F32)  5.36 us
    ppermute x4, waiting for transfers between devices, body(): pooled_grad = pooled_grad + lax.ppermute(mine, 'expert', pairs).astype(F32)  4.47 us
  transfers between devices with their start and end apart: 49, of which 35 were waited for; matrix products, arithmetic and copies ran while one was open for 1% of the time, Pallas kernels for 13%

profile of v14, /device:TPU:0, one launch (start us, length us, event | category | flops | bytes accessed | tf_op | source)
XLA Modules:
  0.0 136.0 jit_solution(6631956278937766772)
XLA Ops:
  0.6 1.9 %shard_map.104 = (bf16[128,1152]{1,0:T(8,128)(2,1)S(1)}, bf16[3200,384]{1,0:T(8,128)(2,1)S(1)}) custom-call(s32[8,128]{1,0:T(8,128)} %bitcast.19, f32[8,128]{1,0:T(8,128)} %bitcast.20, bf16[128,1024]{1,0:T(8,128)(2,1)} %refs_2_.2, bf16[2,512,384]{2,1,0:T(8,128)(2,1)} %refs_0_.1, bf16[2,512,384]{2,1,0:T(8,128)(2,1)} %refs_1_.1, bf16[2,192,1024]{2,1,0:T(8,128)(2,1)} %refs_2_.3), custom_call_target="tpu_custom_call" | custom-call | tf_op jit(solution)/shard_map/pallas_call | solution.py:239
  3.0 2.6 %collective-permute-start.1 = (bf16[128,1152]{1,0:T(8,128)(2,1)S(1)}, bf16[128,1152]{1,0:T(8,128)(2,1)S(1)}, u32[]{:S(2)}, u32[]{:S(2)}) collective-permute-start(bf16[128,1152]{1,0:T(8,128)(2,1)S(1)} %get-tuple-element.55.refs_0_), channel_id=1, source_target_pairs={{0,4},{1,3},{4,8},{5,1},{8,12},{9,5},{12,14},{13,9},{14,10},{15,13... | collective-permute-start | bytes 884744 | tf_op jit(solution)/shard_map/ppermute | solution.py:71
  5.7 6.9 %collective-permute-done.1.refs_0_ = bf16[128,1152]{1,0:T(8,128)(2,1)S(1)} collective-permute-done((bf16[128,1152]{1,0:T(8,128)(2,1)S(1)}, bf16[128,1152]{1,0:T(8,128)(2,1)S(1)}, u32[]{:S(2)}, u32[]{:S(2)}) %collective-permute-start.1) | collective-permute-done | bytes 294944 | tf_op jit(solution)/shard_map/ppermute | solution.py:71
  12.6 2.5 %collective-permute-start.3 = (bf16[128,1152]{1,0:T(8,128)(2,1)S(1)}, bf16[128,1152]{1,0:T(8,128)(2,1)S(1)}, u32[]{:S(2)}, u32[]{:S(2)}) collective-permute-start(bf16[128,1152]{1,0:T(8,128)(2,1)S(1)} %collective-permute-done.1.refs_0_), channel_id=1, source_target_pairs={{0,4},{1,3},{4,8},{5,1},{8,12},{9,5},{12,14},{13,9},{14,10},{15,13... | collective-permute-start | bytes 884744 | tf_op jit(solution)/shard_map/ppermute | solution.py:71
  18.3 2.1 %collective-permute-start.5 = (bf16[64,1024]{1,0:T(8,128)(2,1)S(1)}, bf16[64,1024]{1,0:T(8,128)(2,1)S(1)}, u32[]{:S(2)}, u32[]{:S(2)}) collective-permute-start(bf16[64,1024]{1,0:T(8,128)(2,1)S(1)} %get-tuple-element.62), channel_id=1, source_target_pairs={{0,4},{1,3},{4,8},{5,1},{8,12},{9,5},{12,14},{13,9},{14,10},{15,13... | collective-permute-start | bytes 393224 | tf_op jit(solution)/shard_map/ppermute | solution.py:71
  20.4 1.9 %collective-permute-done.3.refs_0_ = bf16[128,1152]{1,0:T(8,128)(2,1)S(1)} collective-permute-done((bf16[128,1152]{1,0:T(8,128)(2,1)S(1)}, bf16[128,1152]{1,0:T(8,128)(2,1)S(1)}, u32[]{:S(2)}, u32[]{:S(2)}) %collective-permute-start.3) | collective-permute-done | bytes 294944 | tf_op jit(solution)/shard_map/ppermute | solution.py:71
  22.3 2.6 %collective-permute-done.5.refs_1_.arrived_ref = bf16[64,1024]{1,0:T(8,128)(2,1)S(1)} collective-permute-done((bf16[64,1024]{1,0:T(8,128)(2,1)S(1)}, bf16[64,1024]{1,0:T(8,128)(2,1)S(1)}, u32[]{:S(2)}, u32[]{:S(2)}) %collective-permute-start.5) | collective-permute-done | bytes 131104 | tf_op jit(solution)/shard_map/ppermute | solution.py:71
  29.1 1.8 %collective-permute-start.9 = (bf16[64,1024]{1,0:T(8,128)(2,1)S(1)}, bf16[64,1024]{1,0:T(8,128)(2,1)S(1)}, u32[]{:S(2)}, u32[]{:S(2)}) collective-permute-start(bf16[64,1024]{1,0:T(8,128)(2,1)S(1)} %shard_map.112), channel_id=1, source_target_pairs={{0,4},{1,3},{4,8},{5,1},{8,12},{9,5},{12,14},{13,9},{14,10},{15,13... | collective-permute-start | bytes 393224 | tf_op jit(solution)/shard_map/ppermute | solution.py:71
  31.2 3.7 %collective-permute-done.7.refs_0_ = bf16[128,1152]{1,0:T(8,128)(2,1)S(1)} collective-permute-done((bf16[128,1152]{1,0:T(8,128)(2,1)S(1)}, bf16[128,1152]{1,0:T(8,128)(2,1)S(1)}, u32[]{:S(2)}, u32[]{:S(2)}) %collective-permute-start.7) | collective-permute-done | bytes 294944 | tf_op jit(solution)/shard_map/ppermute | solution.py:71
  35.0 2.8 %collective-permute-done.9.refs_1_.arrived_ref = bf16[64,1024]{1,0:T(8,128)(2,1)S(1)} collective-permute-done((bf16[64,1024]{1,0:T(8,128)(2,1)S(1)}, bf16[64,1024]{1,0:T(8,128)(2,1)S(1)}, u32[]{:S(2)}, u32[]{:S(2)}) %collective-permute-start.9) | collective-permute-done | bytes 131104 | tf_op jit(solution)/shard_map/ppermute | solution.py:71
  41.0 1.8 %collective-permute-start.17 = (bf16[64,1024]{1,0:T(8,128)(2,1)S(1)}, bf16[64,1024]{1,0:T(8,128)(2,1)S(1)}, u32[]{:S(2)}, u32[]{:S(2)}) collective-permute-start(bf16[64,1024]{1,0:T(8,128)(2,1)S(1)} %shard_map.122), channel_id=1, source_target_pairs={{0,2},{1,5},{4,0},{5,9},{8,4},{9,13},{12,8},{13,15},{14,12},{15,11... | collective-permute-start | bytes 393224 | tf_op jit(solution)/shard_map/ppermute | solution.py:71
  46.7 2.0 %collective-permute-start.13 = (bf16[64,1024]{1,0:T(8,128)(2,1)S(1)}, bf16[64,1024]{1,0:T(8,128)(2,1)S(1)}, u32[]{:S(2)}, u32[]{:S(2)}) collective-permute-start(bf16[64,1024]{1,0:T(8,128)(2,1)S(1)} %shard_map.117), channel_id=1, source_target_pairs={{0,4},{1,3},{4,8},{5,1},{8,12},{9,5},{12,14},{13,9},{14,10},{15,13... | collective-permute-start | bytes 393224 | tf_op jit(solution)/shard_map/ppermute | solution.py:71
  49.3 4.1 %collective-permute-done.13.arrived_ref = bf16[64,1024]{1,0:T(8,128)(2,1)S(1)} collective-permute-done((bf16[64,1024]{1,0:T(8,128)(2,1)S(1)}, bf16[64,1024]{1,0:T(8,128)(2,1)S(1)}, u32[]{:S(2)}, u32[]{:S(2)}) %collective-permute-start.13) | collective-permute-done | bytes 131104 | tf_op jit(solution)/shard_map/ppermute | solution.py:71
  55.6 3.3 %collective-permute-done.14.arrived_ref = bf16[64,1024]{1,0:T(8,128)(2,1)S(1)} collective-permute-done((bf16[64,1024]{1,0:T(8,128)(2,1)S(1)}, bf16[64,1024]{1,0:T(8,128)(2,1)S(1)}, u32[]{:S(2)}, u32[]{:S(2)}) %collective-permute-start.14) | collective-permute-done | bytes 131104 | tf_op jit(solution)/shard_map/ppermute | solution.py:71
  61.1 2.9 %collective-permute-done.15.arrived_ref = bf16[64,1024]{1,0:T(8,128)(2,1)S(1)} collective-permute-done((bf16[64,1024]{1,0:T(8,128)(2,1)S(1)}, bf16[64,1024]{1,0:T(8,128)(2,1)S(1)}, u32[]{:S(2)}, u32[]{:S(2)}) %collective-permute-start.15) | collective-permute-done | bytes 131104 | tf_op jit(solution)/shard_map/ppermute | solution.py:71
  67.1 2.3 %collective-permute-done.16.refs_1_ = bf16[64,1024]{1,0:T(8,128)(2,1)S(1)} collective-permute-done((bf16[64,1024]{1,0:T(8,128)(2,1)S(1)}, bf16[64,1024]{1,0:T(8,128)(2,1)S(1)}, u32[]{:S(2)}, u32[]{:S(2)}) %collective-permute-start.16) | collective-permute-done | bytes 131104 | tf_op jit(solution)/shard_map/ppermute | solution.py:71
  69.8 1.9 %collective-permute-done.21.refs_1_ = bf16[64,1024]{1,0:T(8,128)(2,1)S(1)} collective-permute-done((bf16[64,1024]{1,0:T(8,128)(2,1)S(1)}, bf16[64,1024]{1,0:T(8,128)(2,1)S(1)}, u32[]{:S(2)}, u32[]{:S(2)}) %collective-permute-start.21) | collective-permute-done | bytes 131104 | tf_op jit(solution)/shard_map/ppermute | solution.py:71
  76.2 1.9 %collective-permute-done.26.refs_5_ = bf16[64,1024]{1,0:T(8,128)(2,1)S(1)} collective-permute-done((bf16[64,1024]{1,0:T(8,128)(2,1)S(1)}, bf16[64,1024]{1,0:T(8,128)(2,1)S(1)}, u32[]{:S(2)}, u32[]{:S(2)}) %collective-permute-start.26) | collective-permute-done | bytes 131104 | tf_op jit(solution)/shard_map/ppermute | solution.py:71
  95.3 2.9 %collective-permute-done.36 = bf16[8,1024]{1,0:T(8,128)(2,1)S(1)} collective-permute-done((bf16[8,1024]{1,0:T(8,128)(2,1)S(1)}, bf16[8,1024]{1,0:T(8,128)(2,1)S(1)}, u32[]{:S(2)}, u32[]{:S(2)}) %collective-permute-start.36) | collective-permute-done | bytes 16416 | tf_op jit(solution)/shard_map/ppermute | solution.py:455
  98.1 3.0 %collective-permute-start.39 = (bf16[8,1024]{1,0:T(8,128)(2,1)S(1)}, bf16[8,1024]{1,0:T(8,128)(2,1)S(1)}, u32[]{:S(2)}, u32[]{:S(2)}) collective-permute-start(bf16[8,1024]{1,0:T(8,128)(2,1)S(1)} %add_convert_fusion), channel_id=1, source_target_pairs={{0,12},{2,14},{4,8},{6,10},{8,4},{10,6},{12,0},{14,2},{1,13},{3,15... | collective-permute-start | bytes 49160 | tf_op jit(solution)/shard_map/ppermute | solution.py:455
  116.0 2.6 %collective-permute-done.41.arrived_ref = bf16[128,1024]{1,0:T(8,128)(2,1)S(1)} collective-permute-done((bf16[128,1024]{1,0:T(8,128)(2,1)S(1)}, bf16[128,1024]{1,0:T(8,128)(2,1)S(1)}, u32[]{:S(2)}, u32[]{:S(2)}) %collective-permute-start.41) | collective-permute-done | bytes 262176 | tf_op jit(solution)/shard_map/ppermute | solution.py:71
  119.3 2.1 %collective-permute-start.46 = (bf16[128,1024]{1,0:T(8,128)(2,1)S(1)}, bf16[128,1024]{1,0:T(8,128)(2,1)S(1)}, u32[]{:S(2)}, u32[]{:S(2)}) collective-permute-start(bf16[128,1024]{1,0:T(8,128)(2,1)S(1)} %shard_map.144), channel_id=1, source_target_pairs={{0,2},{1,5},{4,0},{5,9},{8,4},{9,13},{12,8},{13,15},{14,12},{15,11... | collective-permute-start | bytes 786440 | tf_op jit(solution)/shard_map/ppermute | solution.py:71
  123.1 2.5 %collective-permute-done.42.arrived_ref = bf16[128,1024]{1,0:T(8,128)(2,1)S(1)} collective-permute-done((bf16[128,1024]{1,0:T(8,128)(2,1)S(1)}, bf16[128,1024]{1,0:T(8,128)(2,1)S(1)}, u32[]{:S(2)}, u32[]{:S(2)}) %collective-permute-start.42) | collective-permute-done | bytes 262176 | tf_op jit(solution)/shard_map/ppermute | solution.py:71
  132.0 3.2 %collective-permute-done.47.refs_2_ = bf16[128,1024]{1,0:T(8,128)(2,1)S(1)} collective-permute-done((bf16[128,1024]{1,0:T(8,128)(2,1)S(1)}, bf16[128,1024]{1,0:T(8,128)(2,1)S(1)}, u32[]{:S(2)}, u32[]{:S(2)}) %collective-permute-start.47) | collective-permute-done | bytes 262176 | tf_op jit(solution)/shard_map/ppermute | solution.py:71
  (135 shorter events, 70.0 us)
Async XLA Ops:
  2.5 12.5 %collective-permute-start = (bf16[3200,384]{1,0:T(8,128)(2,1)S(1)}, bf16[3200,384]{1,0:T(8,128)(2,1)S(1)}, u32[]{:S(2)}, u32[]{:S(2)}) collective-permute-start(bf16[3200,384]{1,0:T(8,128)(2,1)S(1)} %get-tuple-element.56), channel_id=1, source_target_pairs={{0,1},{1,0},{2,3},{3,2},{4,5},{5,4},{6,7},{7,6},{8,9},{9,8},{10,11... | collective-permute-start | bytes 7372808 | tf_op jit(solution)/shard_map/ppermute | solution.py:334
  3.0 9.5 %collective-permute-start.1 = (bf16[128,1152]{1,0:T(8,128)(2,1)S(1)}, bf16[128,1152]{1,0:T(8,128)(2,1)S(1)}, u32[]{:S(2)}, u32[]{:S(2)}) collective-permute-start(bf16[128,1152]{1,0:T(8,128)(2,1)S(1)} %get-tuple-element.55.refs_0_), channel_id=1, source_target_pairs={{0,4},{1,3},{4,8},{5,1},{8,12},{9,5},{12,14},{13,9},{14,10},{15,13... | collective-permute-start | bytes 884744 | tf_op jit(solution)/shard_map/ppermute | solution.py:71
  5.7 9.4 %collective-permute-start.2 = (bf16[128,1152]{1,0:T(8,128)(2,1)S(1)}, bf16[128,1152]{1,0:T(8,128)(2,1)S(1)}, u32[]{:S(2)}, u32[]{:S(2)}) collective-permute-start(bf16[128,1152]{1,0:T(8,128)(2,1)S(1)} %get-tuple-element.55.refs_0_), channel_id=1, source_target_pairs={{0,2},{1,5},{4,0},{5,9},{8,4},{9,13},{12,8},{13,15},{14,12},{15,11... | collective-permute-start | bytes 884744 | tf_op jit(solution)/shard_map/ppermute | solution.py:71
  12.6 9.8 %collective-permute-start.3 = (bf16[128,1152]{1,0:T(8,128)(2,1)S(1)}, bf16[128,1152]{1,0:T(8,128)(2,1)S(1)}, u32[]{:S(2)}, u32[]{:S(2)}) collective-permute-start(bf16[128,1152]{1,0:T(8,128)(2,1)S(1)} %collective-permute-done.1.refs_0_), channel_id=1, source_target_pairs={{0,4},{1,3},{4,8},{5,1},{8,12},{9,5},{12,14},{13,9},{14,10},{15,13... | collective-permute-start | bytes 884744 | tf_op jit(solution)/shard_map/ppermute | solution.py:71
  15.0 12.1 %collective-permute-start.4 = (bf16[128,1152]{1,0:T(8,128)(2,1)S(1)}, bf16[128,1152]{1,0:T(8,128)(2,1)S(1)}, u32[]{:S(2)}, u32[]{:S(2)}) collective-permute-start(bf16[128,1152]{1,0:T(8,128)(2,1)S(1)} %collective-permute-done.2.refs_1_), channel_id=1, source_target_pairs={{0,2},{1,5},{4,0},{5,9},{8,4},{9,13},{12,8},{13,15},{14,12},{15,11... | collective-permute-start | bytes 884744 | tf_op jit(solution)/shard_map/ppermute | solution.py:71
  18.3 6.6 %collective-permute-start.5 = (bf16[64,1024]{1,0:T(8,128)(2,1)S(1)}, bf16[64,1024]{1,0:T(8,128)(2,1)S(1)}, u32[]{:S(2)}, u32[]{:S(2)}) collective-permute-start(bf16[64,1024]{1,0:T(8,128)(2,1)S(1)} %get-tuple-element.62), channel_id=1, source_target_pairs={{0,4},{1,3},{4,8},{5,1},{8,12},{9,5},{12,14},{13,9},{14,10},{15,13... | collective-permute-start | bytes 393224 | tf_op jit(solution)/shard_map/ppermute | solution.py:71
  25.4 9.6 %collective-permute-start.7 = (bf16[128,1152]{1,0:T(8,128)(2,1)S(1)}, bf16[128,1152]{1,0:T(8,128)(2,1)S(1)}, u32[]{:S(2)}, u32[]{:S(2)}) collective-permute-start(bf16[128,1152]{1,0:T(8,128)(2,1)S(1)} %shard_map.109), channel_id=1, source_target_pairs={{0,4},{1,3},{4,8},{5,1},{8,12},{9,5},{12,14},{13,9},{14,10},{15,13... | collective-permute-start | bytes 884744 | tf_op jit(solution)/shard_map/ppermute | solution.py:71
  27.2 11.9 %collective-permute-start.8 = (bf16[128,1152]{1,0:T(8,128)(2,1)S(1)}, bf16[128,1152]{1,0:T(8,128)(2,1)S(1)}, u32[]{:S(2)}, u32[]{:S(2)}) collective-permute-start(bf16[128,1152]{1,0:T(8,128)(2,1)S(1)} %shard_map.110), channel_id=1, source_target_pairs={{0,2},{1,5},{4,0},{5,9},{8,4},{9,13},{12,8},{13,15},{14,12},{15,11... | collective-permute-start | bytes 884744 | tf_op jit(solution)/shard_map/ppermute | solution.py:71
  29.1 8.7 %collective-permute-start.9 = (bf16[64,1024]{1,0:T(8,128)(2,1)S(1)}, bf16[64,1024]{1,0:T(8,128)(2,1)S(1)}, u32[]{:S(2)}, u32[]{:S(2)}) collective-permute-start(bf16[64,1024]{1,0:T(8,128)(2,1)S(1)} %shard_map.112), channel_id=1, source_target_pairs={{0,4},{1,3},{4,8},{5,1},{8,12},{9,5},{12,14},{13,9},{14,10},{15,13... | collective-permute-start | bytes 393224 | tf_op jit(solution)/shard_map/ppermute | solution.py:71
  30.9 6.9 %collective-permute-start.10 = (bf16[64,1024]{1,0:T(8,128)(2,1)S(1)}, bf16[64,1024]{1,0:T(8,128)(2,1)S(1)}, u32[]{:S(2)}, u32[]{:S(2)}) collective-permute-start(bf16[64,1024]{1,0:T(8,128)(2,1)S(1)} %shard_map.113), channel_id=1, source_target_pairs={{0,2},{1,5},{4,0},{5,9},{8,4},{9,13},{12,8},{13,15},{14,12},{15,11... | collective-permute-start | bytes 393224 | tf_op jit(solution)/shard_map/ppermute | solution.py:71
  37.8 6.7 %collective-permute-start.11 = (bf16[128,1152]{1,0:T(8,128)(2,1)S(1)}, bf16[128,1152]{1,0:T(8,128)(2,1)S(1)}, u32[]{:S(2)}, u32[]{:S(2)}) collective-permute-start(bf16[128,1152]{1,0:T(8,128)(2,1)S(1)} %shard_map.114), channel_id=1, source_target_pairs={{0,4},{1,3},{4,8},{5,1},{8,12},{9,5},{12,14},{13,9},{14,10},{15,13... | collective-permute-start | bytes 884744 | tf_op jit(solution)/shard_map/ppermute | solution.py:71
  41.0 7.7 %collective-permute-start.17 = (bf16[64,1024]{1,0:T(8,128)(2,1)S(1)}, bf16[64,1024]{1,0:T(8,128)(2,1)S(1)}, u32[]{:S(2)}, u32[]{:S(2)}) collective-permute-start(bf16[64,1024]{1,0:T(8,128)(2,1)S(1)} %shard_map.122), channel_id=1, source_target_pairs={{0,2},{1,5},{4,0},{5,9},{8,4},{9,13},{12,8},{13,15},{14,12},{15,11... | collective-permute-start | bytes 393224 | tf_op jit(solution)/shard_map/ppermute | solution.py:71
  46.7 6.7 %collective-permute-start.13 = (bf16[64,1024]{1,0:T(8,128)(2,1)S(1)}, bf16[64,1024]{1,0:T(8,128)(2,1)S(1)}, u32[]{:S(2)}, u32[]{:S(2)}) collective-permute-start(bf16[64,1024]{1,0:T(8,128)(2,1)S(1)} %shard_map.117), channel_id=1, source_target_pairs={{0,4},{1,3},{4,8},{5,1},{8,12},{9,5},{12,14},{13,9},{14,10},{15,13... | collective-permute-start | bytes 393224 | tf_op jit(solution)/shard_map/ppermute | solution.py:71
  69.5 6.4 %collective-permute-start.22 = (bf16[64,1024]{1,0:T(8,128)(2,1)S(1)}, bf16[64,1024]{1,0:T(8,128)(2,1)S(1)}, u32[]{:S(2)}, u32[]{:S(2)}) collective-permute-start(bf16[64,1024]{1,0:T(8,128)(2,1)S(1)} %shard_map.121.refs_1_), channel_id=1, source_target_pairs={{0,4},{1,3},{4,8},{5,1},{8,12},{9,5},{12,14},{13,9},{14,10},{15,13... | collective-permute-start | bytes 393224 | tf_op jit(solution)/shard_map/ppermute | solution.py:71
  72.3 6.4 %collective-permute-start.30 = (bf16[64,1024]{1,0:T(8,128)(2,1)S(1)}, bf16[64,1024]{1,0:T(8,128)(2,1)S(1)}, u32[]{:S(2)}, u32[]{:S(2)}) collective-permute-start(bf16[64,1024]{1,0:T(8,128)(2,1)S(1)} %shard_map.127.refs_2_), channel_id=1, source_target_pairs={{0,4},{1,3},{4,8},{5,1},{8,12},{9,5},{12,14},{13,9},{14,10},{15,13... | collective-permute-start | bytes 393224 | tf_op jit(solution)/shard_map/ppermute | solution.py:71
  73.9 6.4 %collective-permute-start.33 = (bf16[64,1024]{1,0:T(8,128)(2,1)S(1)}, bf16[64,1024]{1,0:T(8,128)(2,1)S(1)}, u32[]{:S(2)}, u32[]{:S(2)}) collective-permute-start(bf16[64,1024]{1,0:T(8,128)(2,1)S(1)} %shard_map.121.refs_1_), channel_id=1, source_target_pairs={{0,2},{1,5},{4,0},{5,9},{8,4},{9,13},{12,8},{13,15},{14,12},{15,11... | collective-permute-start | bytes 393224 | tf_op jit(solution)/shard_map/ppermute | solution.py:71
  78.8 6.4 %collective-permute-start.31 = (bf16[64,1024]{1,0:T(8,128)(2,1)S(1)}, bf16[64,1024]{1,0:T(8,128)(2,1)S(1)}, u32[]{:S(2)}, u32[]{:S(2)}) collective-permute-start(bf16[64,1024]{1,0:T(8,128)(2,1)S(1)} %collective-permute-done.30.refs_3_), channel_id=1, source_target_pairs={{0,4},{1,3},{4,8},{5,1},{8,12},{9,5},{12,14},{13,9},{14,10},{15,13... | collective-permute-start | bytes 393224 | tf_op jit(solution)/shard_map/ppermute | solution.py:71
  112.2 6.4 %collective-permute-start.41 = (bf16[128,1024]{1,0:T(8,128)(2,1)S(1)}, bf16[128,1024]{1,0:T(8,128)(2,1)S(1)}, u32[]{:S(2)}, u32[]{:S(2)}) collective-permute-start(bf16[128,1024]{1,0:T(8,128)(2,1)S(1)} %shard_map.140), channel_id=1, source_target_pairs={{0,4},{1,3},{4,8},{5,1},{8,12},{9,5},{12,14},{13,9},{14,10},{15,13... | collective-permute-start | bytes 786440 | tf_op jit(solution)/shard_map/ppermute | solution.py:71
  112.8 6.4 %collective-permute-start.45 = (bf16[128,1024]{1,0:T(8,128)(2,1)S(1)}, bf16[128,1024]{1,0:T(8,128)(2,1)S(1)}, u32[]{:S(2)}, u32[]{:S(2)}) collective-permute-start(bf16[128,1024]{1,0:T(8,128)(2,1)S(1)} %shard_map.143), channel_id=1, source_target_pairs={{0,2},{1,5},{4,0},{5,9},{8,4},{9,13},{12,8},{13,15},{14,12},{15,11... | collective-permute-start | bytes 786440 | tf_op jit(solution)/shard_map/ppermute | solution.py:71
  114.4 7.0 %collective-permute-start.48 = (bf16[8,1274]{1,0:T(8,128)(2,1)S(1)}, bf16[8,1274]{1,0:T(8,128)(2,1)S(1)}, u32[]{:S(2)}, u32[]{:S(2)}) collective-permute-start(bf16[8,1274]{1,0:T(8,128)(2,1)S(1)} %pad_maximum_fusion.1), channel_id=1, source_target_pairs={{0,1},{1,0},{2,3},{3,2},{4,5},{5,4},{6,7},{7,6},{8,9},{9,8},{10,11... | collective-permute-start | bytes 61160 | tf_op jit(solution)/shard_map/ppermute | solution.py:459
  118.7 6.9 %collective-permute-start.42 = (bf16[128,1024]{1,0:T(8,128)(2,1)S(1)}, bf16[128,1024]{1,0:T(8,128)(2,1)S(1)}, u32[]{:S(2)}, u32[]{:S(2)}) collective-permute-start(bf16[128,1024]{1,0:T(8,128)(2,1)S(1)} %shard_map.141), channel_id=1, source_target_pairs={{0,4},{1,3},{4,8},{5,1},{8,12},{9,5},{12,14},{13,9},{14,10},{15,13... | collective-permute-start | bytes 786440 | tf_op jit(solution)/shard_map/ppermute | solution.py:71
  119.3 9.1 %collective-permute-start.46 = (bf16[128,1024]{1,0:T(8,128)(2,1)S(1)}, bf16[128,1024]{1,0:T(8,128)(2,1)S(1)}, u32[]{:S(2)}, u32[]{:S(2)}) collective-permute-start(bf16[128,1024]{1,0:T(8,128)(2,1)S(1)} %shard_map.144), channel_id=1, source_target_pairs={{0,2},{1,5},{4,0},{5,9},{8,4},{9,13},{12,8},{13,15},{14,12},{15,11... | collective-permute-start | bytes 786440 | tf_op jit(solution)/shard_map/ppermute | solution.py:71
  125.6 6.4 %collective-permute-start.43 = (bf16[128,1024]{1,0:T(8,128)(2,1)S(1)}, bf16[128,1024]{1,0:T(8,128)(2,1)S(1)}, u32[]{:S(2)}, u32[]{:S(2)}) collective-permute-start(bf16[128,1024]{1,0:T(8,128)(2,1)S(1)} %shard_map.142), channel_id=1, source_target_pairs={{0,4},{1,3},{4,8},{5,1},{8,12},{9,5},{12,14},{13,9},{14,10},{15,13... | collective-permute-start | bytes 786440 | tf_op jit(solution)/shard_map/ppermute | solution.py:71
  128.5 6.7 %collective-permute-start.47 = (bf16[128,1024]{1,0:T(8,128)(2,1)S(1)}, bf16[128,1024]{1,0:T(8,128)(2,1)S(1)}, u32[]{:S(2)}, u32[]{:S(2)}) collective-permute-start(bf16[128,1024]{1,0:T(8,128)(2,1)S(1)} %shard_map.145), channel_id=1, source_target_pairs={{0,2},{1,5},{4,0},{5,9},{8,4},{9,13},{12,8},{13,15},{14,12},{15,11... | collective-permute-start | bytes 786440 | tf_op jit(solution)/shard_map/ppermute | solution.py:71
  (28 other events, 274.0 us)

commit v15 on v9

--- a/solution.py
+++ b/solution.py
@@ -36,6 +36,21 @@
     )(*args)
 
 
+def after(value, guards):
+    def kernel(*refs):
+        pass
+
+    args = [pltpu.with_memory_space_constraint(a, pltpu.VMEM) for a in (value, *guards)]
+    return pl.pallas_call(
+        kernel,
+        out_shape=pltpu.VMEM(value.shape, value.dtype),
+        in_specs=[pl.BlockSpec(memory_space=pltpu.VMEM)] * len(args),
+        out_specs=pl.BlockSpec(memory_space=pltpu.VMEM),
+        input_output_aliases={0: 0},
+        compiler_params=pltpu.CompilerParams(vmem_limit_bytes=VMEM_LIMIT),
+    )(*args)
+
+
 class Ring:
     def __init__(self, expert_count, group_count):
         self.count = expert_count
@@ -62,11 +77,14 @@
             there = jnp.where(there < self.half, 2 * there, 2 * (count - 1 - there) + 1)
         return there
 
-    def gather(self, top, bottom, use):
+    def gather(self, top, bottom, use, paced=False):
         top_left = top_right = top
         bottom_left = bottom_right = bottom
         use((0,), (top, bottom))
         for step in range(1, self.half):
+            if paced and step > 1:
+                top_left = after(top_left, [top_right])
+                bottom_right = after(bottom_right, [bottom_left])
             top_left = self.send(top_left, 1)
             top_right = self.send(top_right, -1)
             bottom_left = self.send(bottom_left, 1)
@@ -87,29 +105,6 @@
                 bottom_left = self.send(add(parts[step - 1][1], bottom_left), 1)
                 top_right = self.send(add(parts[1 - step][0], top_right), -1)
         return (top_left, top_right), (bottom_left, bottom_right)
-
-    def scatter_whole(self, ends, parts):
-        mid = ends[0].shape[0]
-
-        def half_kernel(first, block_ref, arrived_ref, out_ref):
-            added, kept = pl.ds(first, mid), pl.ds(mid - first, mid)
-            out_ref[added, :] = (block_ref[added, :] + arrived_ref[...].astype(F32)).astype(BF16)
-            out_ref[kept, :] = block_ref[kept, :].astype(BF16)
-
-        left, right = self.send(ends[0], 1), self.send(ends[1], -1)
-        for step in range(self.half - 1, 0, -1):
-            blocks = parts[step], parts[-step]
-            if step == self.half - 1:
-                halves = [functools.partial(half_kernel, first) for first in (0, mid)]
-                shape = blocks[0].shape
-                left, right = [
-                    call(kernel, [(shape, BF16)], block, arrived)[0]
-                    for kernel, block, arrived in zip(halves, blocks, (left, right))
-                ]
-            else:
-                left, right = add(blocks[0], left), add(blocks[1], right)
-            left, right = self.send(left, 1), self.send(right, -1)
-        return left, right
 
     def part_types(self, distances):
         types = []
@@ -378,7 +373,7 @@
         saved_at[distances] = result[:2]
         keep_parts(part_at, distances, result[2:])
 
-    ring.gather(top, bottom, hold)
+    ring.gather(top, bottom, hold, paced=True)
     for distances in tokens_at:
         forward(distances)
     gain = norm_gain.reshape(1, feature_dim)
@@ -480,13 +475,9 @@
     back_at = {}
 
     def backward(distances):
-        if distances == (ring.half,):
-            outs = [((mid, feature_dim), BF16)] * 2
-        else:
-            outs = [(block, F32)] * len(distances)
         result = call(
             functools.partial(backward_kernel, distances),
-            outs,
+            part_outs(distances),
             *norm_at[distances],
             *saved_at[distances],
             pooled_grad,
@@ -495,20 +486,18 @@
             down_t,
             flops=flops * len(distances),
         )
-        if distances == (ring.half,):
-            back_at["ends"] = result
-        else:
-            back_at.update(zip(distances, result))
+        keep_parts(back_at, distances, result)
 
     for distances in reversed(list(tokens_at)):
         backward(distances)
+    (top_left, top_right), (bottom_left, bottom_right) = ring.scatter(back_at)
     token_grad = pl.pallas_call(
         sum_kernel,
         out_shape=jax.ShapeDtypeStruct(block, BF16),
-        in_specs=[pl.BlockSpec(memory_space=pltpu.VMEM)] * 3,
+        in_specs=[pl.BlockSpec(memory_space=pltpu.VMEM)] * 6,
         out_specs=pl.BlockSpec(memory_space=pltpu.VMEM),
         compiler_params=pltpu.CompilerParams(vmem_limit_bytes=VMEM_LIMIT),
-    )(back_at[0], *ring.scatter_whole(back_at["ends"], back_at))
+    )(back_at[0][0], top_left, top_right, back_at[0][1], bottom_left, bottom_right)
     return (token_grad, head_grad)
 
 

time: 125 us -> 126 us (level)
  starting transfers between devices: 61.2 us -> 67.4 us
  waiting for transfers between devices: 39.1 us -> 33.4 us
    ppermute x50 -> x56, waiting for transfers between devices: 35 us -> 29.6 us  [send(): return lax.ppermute(value, 'expert', pairs)]
    ppermute x50 -> x56, starting transfers between devices: 56.1 us -> 61.3 us  [send(): return lax.ppermute(value, 'expert', pairs)]
    pallas_call x35 -> x39, Pallas kernels: 17.3 us -> 17.3 us  [call(): pl.pallas_call(kernel, out_shape=[pltpu.VMEM(shape, dtype) for shape, dty...]
  transfers between devices with their start and end apart: 56 -> 62, of which waited for: 27 -> 28; matrix products, arithmetic and copies ran while one was open for 1% -> 1% of each run, Pallas kernels for 14% -> 14%
where the time goes in v15:
time: 126 us; the launch traced here: 125 us
  starting transfers between devices  67.4 us (53%)
  waiting for transfers between devices  33.4 us (27%)
  Pallas kernels  21.8 us (17%)
  matrix products  1.71 us (1%)
    ppermute x56, starting transfers between devices, send(): return lax.ppermute(value, 'expert', pairs)  61.3 us
    ppermute x56, waiting for transfers between devices, send(): return lax.ppermute(value, 'expert', pairs)  29.6 us
    pallas_call x39, Pallas kernels, call(): pl.pallas_call(kernel, out_shape=[pltpu.VMEM(shape, dtype) for shape, dty...  17.3 us
    ppermute x4, starting transfers between devices, body(): pooled_grad = pooled_grad + lax.ppermute(mine, 'expert', pairs).astype(F32)  5.63 us
    ppermute x4, waiting for transfers between devices, body(): pooled_grad = pooled_grad + lax.ppermute(mine, 'expert', pairs).astype(F32)  3.8 us
  transfers between devices with their start and end apart: 62, of which 28 were waited for; matrix products, arithmetic and copies ran while one was open for 1% of the time, Pallas kernels for 14%

profile of v15, /device:TPU:0, one launch (start us, length us, event | category | flops | bytes accessed | tf_op | source)
XLA Modules:
  0.0 125.5 jit_solution(7870301025970338902)
XLA Ops:
  0.6 1.9 %shard_map.104 = (bf16[64,1152]{1,0:T(8,128)(2,1)S(1)}, bf16[64,1024]{1,0:T(8,128)(2,1)S(1)}, bf16[3200,384]{1,0:T(8,128)(2,1)S(1)}) custom-call(s32[8,128]{1,0:T(8,128)} %bitcast.19, f32[8,128]{1,0:T(8,128)} %bitcast.20, bf16[128,1024]{1,0:T(8,128)(2,1)} %refs_2_.2, bf16[2,512,384]{2,1,0:T(8,128)(2,1)} %refs_0_.1, bf16[2,512,384]{2,1,0:T(8,128)(2,1)} %refs_1_.1, ...), custom_call_target="tpu_custom_call" | custom-call | tf_op jit(solution)/shard_map/pallas_call | solution.py:216
  3.1 2.6 %collective-permute-start.1 = (bf16[64,1152]{1,0:T(8,128)(2,1)S(1)}, bf16[64,1152]{1,0:T(8,128)(2,1)S(1)}, u32[]{:S(2)}, u32[]{:S(2)}) collective-permute-start(bf16[64,1152]{1,0:T(8,128)(2,1)S(1)} %get-tuple-element.64.refs_0_), channel_id=1, source_target_pairs={{0,4},{4,8},{8,12},{12,14},{14,10},{10,6},{6,2},{2,0},{1,5},{5,9},... | collective-permute-start | bytes 442376 | tf_op jit(solution)/shard_map/ppermute | solution.py:68
  5.7 1.9 %collective-permute-start.4 = (bf16[64,1024]{1,0:T(8,128)(2,1)S(1)}, bf16[64,1024]{1,0:T(8,128)(2,1)S(1)}, u32[]{:S(2)}, u32[]{:S(2)}) collective-permute-start(bf16[64,1024]{1,0:T(8,128)(2,1)S(1)} %get-tuple-element.65.refs_1_), channel_id=1, source_target_pairs={{0,2},{4,0},{8,4},{12,8},{14,12},{10,14},{6,10},{2,6},{1,3},{5,1},... | collective-permute-start | bytes 393224 | tf_op jit(solution)/shard_map/ppermute | solution.py:68
  7.8 2.5 %collective-permute-done.1.refs_0_ = bf16[64,1152]{1,0:T(8,128)(2,1)S(1)} collective-permute-done((bf16[64,1152]{1,0:T(8,128)(2,1)S(1)}, bf16[64,1152]{1,0:T(8,128)(2,1)S(1)}, u32[]{:S(2)}, u32[]{:S(2)}) %collective-permute-start.1) | collective-permute-done | bytes 147488 | tf_op jit(solution)/shard_map/ppermute | solution.py:68
  10.3 2.1 %collective-permute-done.3.refs_2_.refs_1_ = bf16[64,1152]{1,0:T(8,128)(2,1)S(1)} collective-permute-done((bf16[64,1152]{1,0:T(8,128)(2,1)S(1)}, bf16[64,1152]{1,0:T(8,128)(2,1)S(1)}, u32[]{:S(2)}, u32[]{:S(2)}) %collective-permute-start.3) | collective-permute-done | bytes 147488 | tf_op jit(solution)/shard_map/ppermute | solution.py:68
  12.4 1.6 %collective-permute-start.5 = (bf16[64,1152]{1,0:T(8,128)(2,1)S(1)}, bf16[64,1152]{1,0:T(8,128)(2,1)S(1)}, u32[]{:S(2)}, u32[]{:S(2)}) collective-permute-start(bf16[64,1152]{1,0:T(8,128)(2,1)S(1)} %shard_map.108), channel_id=1, source_target_pairs={{0,4},{4,8},{8,12},{12,14},{14,10},{10,6},{6,2},{2,0},{1,5},{5,9},... | collective-permute-start | bytes 442376 | tf_op jit(solution)/shard_map/ppermute | solution.py:68
  16.6 1.8 %collective-permute-done.5.refs_0_ = bf16[64,1152]{1,0:T(8,128)(2,1)S(1)} collective-permute-done((bf16[64,1152]{1,0:T(8,128)(2,1)S(1)}, bf16[64,1152]{1,0:T(8,128)(2,1)S(1)}, u32[]{:S(2)}, u32[]{:S(2)}) %collective-permute-start.5) | collective-permute-done | bytes 147488 | tf_op jit(solution)/shard_map/ppermute | solution.py:68
  19.5 1.6 %collective-permute-start.9 = (bf16[64,1152]{1,0:T(8,128)(2,1)S(1)}, bf16[64,1152]{1,0:T(8,128)(2,1)S(1)}, u32[]{:S(2)}, u32[]{:S(2)}) collective-permute-start(bf16[64,1152]{1,0:T(8,128)(2,1)S(1)} %shard_map.111), channel_id=1, source_target_pairs={{0,4},{4,8},{8,12},{12,14},{14,10},{10,6},{6,2},{2,0},{1,5},{5,9},... | collective-permute-start | bytes 442376 | tf_op jit(solution)/shard_map/ppermute | solution.py:68
  22.6 2.2 %collective-permute-done.9.refs_0_ = bf16[64,1152]{1,0:T(8,128)(2,1)S(1)} collective-permute-done((bf16[64,1152]{1,0:T(8,128)(2,1)S(1)}, bf16[64,1152]{1,0:T(8,128)(2,1)S(1)}, u32[]{:S(2)}, u32[]{:S(2)}) %collective-permute-start.9) | collective-permute-done | bytes 147488 | tf_op jit(solution)/shard_map/ppermute | solution.py:68
  24.8 1.6 %collective-permute-start.13 = (bf16[64,1152]{1,0:T(8,128)(2,1)S(1)}, bf16[64,1152]{1,0:T(8,128)(2,1)S(1)}, u32[]{:S(2)}, u32[]{:S(2)}) collective-permute-start(bf16[64,1152]{1,0:T(8,128)(2,1)S(1)} %collective-permute-done.9.refs_0_), channel_id=1, source_target_pairs={{0,4},{4,8},{8,12},{12,14},{14,10},{10,6},{6,2},{2,0},{1,5},{5,9},... | collective-permute-start | bytes 442376 | tf_op jit(solution)/shard_map/ppermute | solution.py:68
  26.9 1.9 %collective-permute-start.14 = (bf16[64,1024]{1,0:T(8,128)(2,1)S(1)}, bf16[64,1024]{1,0:T(8,128)(2,1)S(1)}, u32[]{:S(2)}, u32[]{:S(2)}) collective-permute-start(bf16[64,1024]{1,0:T(8,128)(2,1)S(1)} %collective-permute-done.12.refs_3_), channel_id=1, source_target_pairs={{0,2},{4,0},{8,4},{12,8},{14,12},{10,14},{6,10},{2,6},{1,3},{5,1},... | collective-permute-start | bytes 393224 | tf_op jit(solution)/shard_map/ppermute | solution.py:68
  30.8 1.7 %shard_map.105 = (bf16[1024,1536]{1,0:T(8,128)(2,1)S(1)}, bf16[768,1024]{1,0:T(8,128)(2,1)S(1)}) custom-call(bf16[2,512,384]{2,1,0:T(8,128)(2,1)} %refs_0_.1, bf16[2,512,384]{2,1,0:T(8,128)(2,1)} %refs_1_.1, bf16[2,192,1024]{2,1,0:T(8,128)(2,1)} %refs_2_.3, bf16[3200,384]{1,0:T(8,128)(2,1)S(1)} %collective-permute-done.refs_3_), custom_call_target="tpu_custom_call" | custom-call | tf_op jit(solution)/shard_map/pallas_call | solution.py:271
  37.2 1.9 %collective-permute-start.19 = (bf16[64,1024]{1,0:T(8,128)(2,1)S(1)}, bf16[64,1024]{1,0:T(8,128)(2,1)S(1)}, u32[]{:S(2)}, u32[]{:S(2)}) collective-permute-start(bf16[64,1024]{1,0:T(8,128)(2,1)S(1)} %get-tuple-element.76), channel_id=1, source_target_pairs={{0,2},{4,0},{8,4},{12,8},{14,12},{10,14},{6,10},{2,6},{1,3},{5,1},... | collective-permute-start | bytes 393224 | tf_op jit(solution)/shard_map/ppermute | solution.py:68
  40.5 1.7 %collective-permute-start.26 = (bf16[64,1024]{1,0:T(8,128)(2,1)S(1)}, bf16[64,1024]{1,0:T(8,128)(2,1)S(1)}, u32[]{:S(2)}, u32[]{:S(2)}) collective-permute-start(bf16[64,1024]{1,0:T(8,128)(2,1)S(1)} %shard_map.123), channel_id=1, source_target_pairs={{0,2},{4,0},{8,4},{12,8},{14,12},{10,14},{6,10},{2,6},{1,3},{5,1},... | collective-permute-start | bytes 393224 | tf_op jit(solution)/shard_map/ppermute | solution.py:68
  52.1 2.4 %collective-permute-done.17.arrived_ref = bf16[64,1024]{1,0:T(8,128)(2,1)S(1)} collective-permute-done((bf16[64,1024]{1,0:T(8,128)(2,1)S(1)}, bf16[64,1024]{1,0:T(8,128)(2,1)S(1)}, u32[]{:S(2)}, u32[]{:S(2)}) %collective-permute-start.17) | collective-permute-done | bytes 131104 | tf_op jit(solution)/shard_map/ppermute | solution.py:68
  55.6 1.6 %collective-permute-start.28 = (bf16[64,1024]{1,0:T(8,128)(2,1)S(1)}, bf16[64,1024]{1,0:T(8,128)(2,1)S(1)}, u32[]{:S(2)}, u32[]{:S(2)}) collective-permute-start(bf16[64,1024]{1,0:T(8,128)(2,1)S(1)} %shard_map.125), channel_id=1, source_target_pairs={{0,2},{4,0},{8,4},{12,8},{14,12},{10,14},{6,10},{2,6},{1,3},{5,1},... | collective-permute-start | bytes 393224 | tf_op jit(solution)/shard_map/ppermute | solution.py:68
  63.3 2.1 %collective-permute-start.40 = (bf16[64,1024]{1,0:T(8,128)(2,1)S(1)}, bf16[64,1024]{1,0:T(8,128)(2,1)S(1)}, u32[]{:S(2)}, u32[]{:S(2)}) collective-permute-start(bf16[64,1024]{1,0:T(8,128)(2,1)S(1)} %shard_map.120.refs_2_), channel_id=1, source_target_pairs={{0,2},{4,0},{8,4},{12,8},{14,12},{10,14},{6,10},{2,6},{1,3},{5,1},... | collective-permute-start | bytes 393224 | tf_op jit(solution)/shard_map/ppermute | solution.py:68
  68.8 2.0 %collective-permute-done.40.refs_6_ = bf16[64,1024]{1,0:T(8,128)(2,1)S(1)} collective-permute-done((bf16[64,1024]{1,0:T(8,128)(2,1)S(1)}, bf16[64,1024]{1,0:T(8,128)(2,1)S(1)}, u32[]{:S(2)}, u32[]{:S(2)}) %collective-permute-start.40) | collective-permute-done | bytes 131104 | tf_op jit(solution)/shard_map/ppermute | solution.py:68
  87.8 2.7 %collective-permute-done.43 = bf16[8,1024]{1,0:T(8,128)(2,1)S(1)} collective-permute-done((bf16[8,1024]{1,0:T(8,128)(2,1)S(1)}, bf16[8,1024]{1,0:T(8,128)(2,1)S(1)}, u32[]{:S(2)}, u32[]{:S(2)}) %collective-permute-start.43) | collective-permute-done | bytes 16416 | tf_op jit(solution)/shard_map/ppermute | solution.py:436
  90.5 2.7 %collective-permute-start.46 = (bf16[8,1024]{1,0:T(8,128)(2,1)S(1)}, bf16[8,1024]{1,0:T(8,128)(2,1)S(1)}, u32[]{:S(2)}, u32[]{:S(2)}) collective-permute-start(bf16[8,1024]{1,0:T(8,128)(2,1)S(1)} %add_convert_fusion), channel_id=1, source_target_pairs={{0,12},{2,14},{4,8},{6,10},{8,4},{10,6},{12,0},{14,2},{1,13},{3,15... | collective-permute-start | bytes 49160 | tf_op jit(solution)/shard_map/ppermute | solution.py:436
  93.2 1.7 %collective-permute-start.44 = (bf16[8,1024]{1,0:T(8,128)(2,1)S(1)}, bf16[8,1024]{1,0:T(8,128)(2,1)S(1)}, u32[]{:S(2)}, u32[]{:S(2)}) collective-permute-start(bf16[8,1024]{1,0:T(8,128)(2,1)S(1)} %add_convert_fusion), channel_id=1, source_target_pairs={{0,4},{2,6},{4,0},{6,2},{8,12},{10,14},{12,8},{14,10},{1,5},{3,7},... | collective-permute-start | bytes 49160 | tf_op jit(solution)/shard_map/ppermute | solution.py:436
  101.0 1.6 %shard_map.137 = (bf16[64,1024]{1,0:T(8,128)(2,1)S(1)}, f32[64,1024]{1,0:T(8,128)S(1)}, f32[64,1024]{1,0:T(8,128)S(1)}, bf16[64,1024]{1,0:T(8,128)(2,1)S(1)}) custom-call(f32[256,1024]{1,0:T(8,128)S(1)} %get-tuple-element.105.residual_ref, f32[256,128]{1,0:T(8,128)S(1)} %get-tuple-element.106.inv_ref, bf16[256,768]{1,0:T(8,128)(2,1)S(1)} %get-tuple-element.107.gate_save, ...), custom_call_target="tpu_custom_call" | custom-call | flops 1207959552 | bytes 6721536 | tf_op jit(solution)/shard_map/pallas_call | solution.py:29
  106.9 1.6 %shard_map.136 = (f32[64,1024]{1,0:T(8,128)S(1)}, f32[64,1024]{1,0:T(8,128)S(1)}, f32[64,1024]{1,0:T(8,128)S(1)}, f32[64,1024]{1,0:T(8,128)S(1)}) custom-call(f32[256,1024]{1,0:T(8,128)S(1)} %get-tuple-element.100.residual_ref, f32[256,128]{1,0:T(8,128)S(1)} %get-tuple-element.101.inv_ref, bf16[256,768]{1,0:T(8,128)(2,1)S(1)} %get-tuple-element.102.gate_save, ...), custom_call_target="tpu_custom_call" | custom-call | flops 1207959552 | bytes 6721536 | tf_op jit(solution)/shard_map/pallas_call | solution.py:29
  113.0 1.6 %shard_map.135 = (f32[64,1024]{1,0:T(8,128)S(1)}, f32[64,1024]{1,0:T(8,128)S(1)}, f32[64,1024]{1,0:T(8,128)S(1)}, f32[64,1024]{1,0:T(8,128)S(1)}) custom-call(f32[256,1024]{1,0:T(8,128)S(1)} %get-tuple-element.95.residual_ref, f32[256,128]{1,0:T(8,128)S(1)} %get-tuple-element.96.inv_ref, bf16[256,768]{1,0:T(8,128)(2,1)S(1)} %get-tuple-element.97.gate_save, ...), custom_call_target="tpu_custom_call" | custom-call | flops 1207959552 | bytes 6721536 | tf_op jit(solution)/shard_map/pallas_call | solution.py:29
  (165 shorter events, 77.2 us)
Async XLA Ops:
  2.6 28.2 %collective-permute-start = (bf16[3200,384]{1,0:T(8,128)(2,1)S(1)}, bf16[3200,384]{1,0:T(8,128)(2,1)S(1)}, u32[]{:S(2)}, u32[]{:S(2)}) collective-permute-start(bf16[3200,384]{1,0:T(8,128)(2,1)S(1)} %get-tuple-element.66), channel_id=1, source_target_pairs={{0,1},{1,0},{2,3},{3,2},{4,5},{5,4},{6,7},{7,6},{8,9},{9,8},{10,11... | collective-permute-start | bytes 7372808 | tf_op jit(solution)/shard_map/ppermute | solution.py:311
  3.1 7.2 %collective-permute-start.1 = (bf16[64,1152]{1,0:T(8,128)(2,1)S(1)}, bf16[64,1152]{1,0:T(8,128)(2,1)S(1)}, u32[]{:S(2)}, u32[]{:S(2)}) collective-permute-start(bf16[64,1152]{1,0:T(8,128)(2,1)S(1)} %get-tuple-element.64.refs_0_), channel_id=1, source_target_pairs={{0,4},{4,8},{8,12},{12,14},{14,10},{10,6},{6,2},{2,0},{1,5},{5,9},... | collective-permute-start | bytes 442376 | tf_op jit(solution)/shard_map/ppermute | solution.py:68
  5.7 6.7 %collective-permute-start.3 = (bf16[64,1152]{1,0:T(8,128)(2,1)S(1)}, bf16[64,1152]{1,0:T(8,128)(2,1)S(1)}, u32[]{:S(2)}, u32[]{:S(2)}) collective-permute-start(bf16[64,1152]{1,0:T(8,128)(2,1)S(1)} %get-tuple-element.64.refs_0_), channel_id=1, source_target_pairs={{0,2},{4,0},{8,4},{12,8},{14,12},{10,14},{6,10},{2,6},{1,3},{5,1},... | collective-permute-start | bytes 442376 | tf_op jit(solution)/shard_map/ppermute | solution.py:68
  5.7 8.7 %collective-permute-start.4 = (bf16[64,1024]{1,0:T(8,128)(2,1)S(1)}, bf16[64,1024]{1,0:T(8,128)(2,1)S(1)}, u32[]{:S(2)}, u32[]{:S(2)}) collective-permute-start(bf16[64,1024]{1,0:T(8,128)(2,1)S(1)} %get-tuple-element.65.refs_1_), channel_id=1, source_target_pairs={{0,2},{4,0},{8,4},{12,8},{14,12},{10,14},{6,10},{2,6},{1,3},{5,1},... | collective-permute-start | bytes 393224 | tf_op jit(solution)/shard_map/ppermute | solution.py:68
  7.7 6.8 %collective-permute-start.2 = (bf16[64,1024]{1,0:T(8,128)(2,1)S(1)}, bf16[64,1024]{1,0:T(8,128)(2,1)S(1)}, u32[]{:S(2)}, u32[]{:S(2)}) collective-permute-start(bf16[64,1024]{1,0:T(8,128)(2,1)S(1)} %get-tuple-element.65.refs_1_), channel_id=1, source_target_pairs={{0,4},{4,8},{8,12},{12,14},{14,10},{10,6},{6,2},{2,0},{1,5},{5,9},... | collective-permute-start | bytes 393224 | tf_op jit(solution)/shard_map/ppermute | solution.py:68
  24.8 7.8 %collective-permute-start.13 = (bf16[64,1152]{1,0:T(8,128)(2,1)S(1)}, bf16[64,1152]{1,0:T(8,128)(2,1)S(1)}, u32[]{:S(2)}, u32[]{:S(2)}) collective-permute-start(bf16[64,1152]{1,0:T(8,128)(2,1)S(1)} %collective-permute-done.9.refs_0_), channel_id=1, source_target_pairs={{0,4},{4,8},{8,12},{12,14},{14,10},{10,6},{6,2},{2,0},{1,5},{5,9},... | collective-permute-start | bytes 442376 | tf_op jit(solution)/shard_map/ppermute | solution.py:68
  28.8 6.9 %collective-permute-start.11 = (bf16[64,1152]{1,0:T(8,128)(2,1)S(1)}, bf16[64,1152]{1,0:T(8,128)(2,1)S(1)}, u32[]{:S(2)}, u32[]{:S(2)}) collective-permute-start(bf16[64,1152]{1,0:T(8,128)(2,1)S(1)} %collective-permute-done.7.refs_2_.refs_1_), channel_id=1, source_target_pairs={{0,2},{4,0},{8,4},{12,8},{14,12},{10,14},{6,10},{2,6},{1,3},{5,1},... | collective-permute-start | bytes 442376 | tf_op jit(solution)/shard_map/ppermute | solution.py:68
  40.0 6.8 %collective-permute-start.16 = (bf16[64,1024]{1,0:T(8,128)(2,1)S(1)}, bf16[64,1024]{1,0:T(8,128)(2,1)S(1)}, u32[]{:S(2)}, u32[]{:S(2)}) collective-permute-start(bf16[64,1024]{1,0:T(8,128)(2,1)S(1)} %shard_map.115), channel_id=1, source_target_pairs={{0,4},{4,8},{8,12},{12,14},{14,10},{10,6},{6,2},{2,0},{1,5},{5,9},... | collective-permute-start | bytes 393224 | tf_op jit(solution)/shard_map/ppermute | solution.py:68
  40.5 7.1 %collective-permute-start.26 = (bf16[64,1024]{1,0:T(8,128)(2,1)S(1)}, bf16[64,1024]{1,0:T(8,128)(2,1)S(1)}, u32[]{:S(2)}, u32[]{:S(2)}) collective-permute-start(bf16[64,1024]{1,0:T(8,128)(2,1)S(1)} %shard_map.123), channel_id=1, source_target_pairs={{0,2},{4,0},{8,4},{12,8},{14,12},{10,14},{6,10},{2,6},{1,3},{5,1},... | collective-permute-start | bytes 393224 | tf_op jit(solution)/shard_map/ppermute | solution.py:68
  43.7 6.8 %collective-permute-start.20 = (bf16[64,1024]{1,0:T(8,128)(2,1)S(1)}, bf16[64,1024]{1,0:T(8,128)(2,1)S(1)}, u32[]{:S(2)}, u32[]{:S(2)}) collective-permute-start(bf16[64,1024]{1,0:T(8,128)(2,1)S(1)} %shard_map.118), channel_id=1, source_target_pairs={{0,2},{4,0},{8,4},{12,8},{14,12},{10,14},{6,10},{2,6},{1,3},{5,1},... | collective-permute-start | bytes 393224 | tf_op jit(solution)/shard_map/ppermute | solution.py:68
  45.4 6.7 %collective-permute-start.23 = (bf16[64,1024]{1,0:T(8,128)(2,1)S(1)}, bf16[64,1024]{1,0:T(8,128)(2,1)S(1)}, u32[]{:S(2)}, u32[]{:S(2)}) collective-permute-start(bf16[64,1024]{1,0:T(8,128)(2,1)S(1)} %shard_map.121), channel_id=1, source_target_pairs={{0,4},{4,8},{8,12},{12,14},{14,10},{10,6},{6,2},{2,0},{1,5},{5,9},... | collective-permute-start | bytes 393224 | tf_op jit(solution)/shard_map/ppermute | solution.py:68
  46.9 7.6 %collective-permute-start.17 = (bf16[64,1024]{1,0:T(8,128)(2,1)S(1)}, bf16[64,1024]{1,0:T(8,128)(2,1)S(1)}, u32[]{:S(2)}, u32[]{:S(2)}) collective-permute-start(bf16[64,1024]{1,0:T(8,128)(2,1)S(1)} %shard_map.116), channel_id=1, source_target_pairs={{0,4},{4,8},{8,12},{12,14},{14,10},{10,6},{6,2},{2,0},{1,5},{5,9},... | collective-permute-start | bytes 393224 | tf_op jit(solution)/shard_map/ppermute | solution.py:68
  47.6 8.0 %collective-permute-start.27 = (bf16[64,1024]{1,0:T(8,128)(2,1)S(1)}, bf16[64,1024]{1,0:T(8,128)(2,1)S(1)}, u32[]{:S(2)}, u32[]{:S(2)}) collective-permute-start(bf16[64,1024]{1,0:T(8,128)(2,1)S(1)} %shard_map.124), channel_id=1, source_target_pairs={{0,2},{4,0},{8,4},{12,8},{14,12},{10,14},{6,10},{2,6},{1,3},{5,1},... | collective-permute-start | bytes 393224 | tf_op jit(solution)/shard_map/ppermute | solution.py:68
  50.6 7.6 %collective-permute-start.21 = (bf16[64,1024]{1,0:T(8,128)(2,1)S(1)}, bf16[64,1024]{1,0:T(8,128)(2,1)S(1)}, u32[]{:S(2)}, u32[]{:S(2)}) collective-permute-start(bf16[64,1024]{1,0:T(8,128)(2,1)S(1)} %shard_map.119), channel_id=1, source_target_pairs={{0,2},{4,0},{8,4},{12,8},{14,12},{10,14},{6,10},{2,6},{1,3},{5,1},... | collective-permute-start | bytes 393224 | tf_op jit(solution)/shard_map/ppermute | solution.py:68
  55.1 7.3 %collective-permute-start.24 = (bf16[64,1024]{1,0:T(8,128)(2,1)S(1)}, bf16[64,1024]{1,0:T(8,128)(2,1)S(1)}, u32[]{:S(2)}, u32[]{:S(2)}) collective-permute-start(bf16[64,1024]{1,0:T(8,128)(2,1)S(1)} %shard_map.122), channel_id=1, source_target_pairs={{0,4},{4,8},{8,12},{12,14},{14,10},{10,6},{6,2},{2,0},{1,5},{5,9},... | collective-permute-start | bytes 393224 | tf_op jit(solution)/shard_map/ppermute | solution.py:68
  55.6 6.8 %collective-permute-start.28 = (bf16[64,1024]{1,0:T(8,128)(2,1)S(1)}, bf16[64,1024]{1,0:T(8,128)(2,1)S(1)}, u32[]{:S(2)}, u32[]{:S(2)}) collective-permute-start(bf16[64,1024]{1,0:T(8,128)(2,1)S(1)} %shard_map.125), channel_id=1, source_target_pairs={{0,2},{4,0},{8,4},{12,8},{14,12},{10,14},{6,10},{2,6},{1,3},{5,1},... | collective-permute-start | bytes 393224 | tf_op jit(solution)/shard_map/ppermute | solution.py:68
  63.3 7.6 %collective-permute-start.40 = (bf16[64,1024]{1,0:T(8,128)(2,1)S(1)}, bf16[64,1024]{1,0:T(8,128)(2,1)S(1)}, u32[]{:S(2)}, u32[]{:S(2)}) collective-permute-start(bf16[64,1024]{1,0:T(8,128)(2,1)S(1)} %shard_map.120.refs_2_), channel_id=1, source_target_pairs={{0,2},{4,0},{8,4},{12,8},{14,12},{10,14},{6,10},{2,6},{1,3},{5,1},... | collective-permute-start | bytes 393224 | tf_op jit(solution)/shard_map/ppermute | solution.py:68
  65.3 7.1 %collective-permute-start.37 = (bf16[64,1024]{1,0:T(8,128)(2,1)S(1)}, bf16[64,1024]{1,0:T(8,128)(2,1)S(1)}, u32[]{:S(2)}, u32[]{:S(2)}) collective-permute-start(bf16[64,1024]{1,0:T(8,128)(2,1)S(1)} %shard_map.126.refs_3_), channel_id=1, source_target_pairs={{0,4},{4,8},{8,12},{12,14},{14,10},{10,6},{6,2},{2,0},{1,5},{5,9},... | collective-permute-start | bytes 393224 | tf_op jit(solution)/shard_map/ppermute | solution.py:68
  65.4 9.5 %collective-permute-start.30 = (bf16[64,1024]{1,0:T(8,128)(2,1)S(1)}, bf16[64,1024]{1,0:T(8,128)(2,1)S(1)}, u32[]{:S(2)}, u32[]{:S(2)}) collective-permute-start(bf16[64,1024]{1,0:T(8,128)(2,1)S(1)} %collective-permute-done.29.refs_4_), channel_id=1, source_target_pairs={{0,4},{4,8},{8,12},{12,14},{14,10},{10,6},{6,2},{2,0},{1,5},{5,9},... | collective-permute-start | bytes 393224 | tf_op jit(solution)/shard_map/ppermute | solution.py:68
  68.0 7.8 %collective-permute-start.34 = (bf16[64,1024]{1,0:T(8,128)(2,1)S(1)}, bf16[64,1024]{1,0:T(8,128)(2,1)S(1)}, u32[]{:S(2)}, u32[]{:S(2)}) collective-permute-start(bf16[64,1024]{1,0:T(8,128)(2,1)S(1)} %collective-permute-done.33.refs_7_), channel_id=1, source_target_pairs={{0,2},{4,0},{8,4},{12,8},{14,12},{10,14},{6,10},{2,6},{1,3},{5,1},... | collective-permute-start | bytes 393224 | tf_op jit(solution)/shard_map/ppermute | solution.py:68
  110.8 7.9 %collective-permute-start.49 = (bf16[64,1024]{1,0:T(8,128)(2,1)S(1)}, bf16[64,1024]{1,0:T(8,128)(2,1)S(1)}, u32[]{:S(2)}, u32[]{:S(2)}) collective-permute-start(bf16[64,1024]{1,0:T(8,128)(2,1)S(1)} %shard_map.140), channel_id=1, source_target_pairs={{0,4},{4,8},{8,12},{12,14},{14,10},{10,6},{6,2},{2,0},{1,5},{5,9},... | collective-permute-start | bytes 393224 | tf_op jit(solution)/shard_map/ppermute | solution.py:68
  111.7 7.9 %collective-permute-start.59 = (bf16[64,1024]{1,0:T(8,128)(2,1)S(1)}, bf16[64,1024]{1,0:T(8,128)(2,1)S(1)}, u32[]{:S(2)}, u32[]{:S(2)}) collective-permute-start(bf16[64,1024]{1,0:T(8,128)(2,1)S(1)} %shard_map.147), channel_id=1, source_target_pairs={{0,2},{4,0},{8,4},{12,8},{14,12},{10,14},{6,10},{2,6},{1,3},{5,1},... | collective-permute-start | bytes 393224 | tf_op jit(solution)/shard_map/ppermute | solution.py:68
  115.0 8.3 %collective-permute-start.53 = (bf16[64,1024]{1,0:T(8,128)(2,1)S(1)}, bf16[64,1024]{1,0:T(8,128)(2,1)S(1)}, u32[]{:S(2)}, u32[]{:S(2)}) collective-permute-start(bf16[64,1024]{1,0:T(8,128)(2,1)S(1)} %shard_map.143), channel_id=1, source_target_pairs={{0,2},{4,0},{8,4},{12,8},{14,12},{10,14},{6,10},{2,6},{1,3},{5,1},... | collective-permute-start | bytes 393224 | tf_op jit(solution)/shard_map/ppermute | solution.py:68
  116.3 7.0 %collective-permute-start.56 = (bf16[64,1024]{1,0:T(8,128)(2,1)S(1)}, bf16[64,1024]{1,0:T(8,128)(2,1)S(1)}, u32[]{:S(2)}, u32[]{:S(2)}) collective-permute-start(bf16[64,1024]{1,0:T(8,128)(2,1)S(1)} %shard_map.145), channel_id=1, source_target_pairs={{0,4},{4,8},{8,12},{12,14},{14,10},{10,6},{6,2},{2,0},{1,5},{5,9},... | collective-permute-start | bytes 393224 | tf_op jit(solution)/shard_map/ppermute | solution.py:68
  (41 other events, 351.2 us)

commit v16 on v15

--- a/solution.py
+++ b/solution.py
@@ -77,14 +77,13 @@
             there = jnp.where(there < self.half, 2 * there, 2 * (count - 1 - there) + 1)
         return there
 
-    def gather(self, top, bottom, use, paced=False):
+    def gather(self, top, bottom, use, guard=None):
         top_left = top_right = top
         bottom_left = bottom_right = bottom
         use((0,), (top, bottom))
         for step in range(1, self.half):
-            if paced and step > 1:
-                top_left = after(top_left, [top_right])
-                bottom_right = after(bottom_right, [bottom_left])
+            if guard is not None and step == self.half - 1:
+                top_right = after(top_right, [guard])
             top_left = self.send(top_left, 1)
             top_right = self.send(top_right, -1)
             bottom_left = self.send(bottom_left, 1)
@@ -373,7 +372,7 @@
         saved_at[distances] = result[:2]
         keep_parts(part_at, distances, result[2:])
 
-    ring.gather(top, bottom, hold, paced=True)
+    ring.gather(top, bottom, hold, wide)
     for distances in tokens_at:
         forward(distances)
     gain = norm_gain.reshape(1, feature_dim)

time: 126 us -> 123 us (0.976)
  waiting for transfers between devices: 33.4 us -> 29.2 us
  starting transfers between devices: 67.4 us -> 69.1 us
    ppermute x56, waiting for transfers between devices: 29.6 us -> 25.8 us  [send(): return lax.ppermute(value, 'expert', pairs)]
    ppermute x56, starting transfers between devices: 61.3 us -> 62.6 us  [send(): return lax.ppermute(value, 'expert', pairs)]
where the time goes in v16:
time: 123 us
  starting transfers between devices  69.1 us (56%)
  waiting for transfers between devices  29.2 us (24%)
  Pallas kernels  21.8 us (18%)
  matrix products  1.71 us (1%)
    ppermute x56, starting transfers between devices, send(): return lax.ppermute(value, 'expert', pairs)  62.6 us
    ppermute x56, waiting for transfers between devices, send(): return lax.ppermute(value, 'expert', pairs)  25.8 us
    pallas_call x39, Pallas kernels, call(): pl.pallas_call(kernel, out_shape=[pltpu.VMEM(shape, dtype) for shape, dty...  17.4 us
    ppermute x4, starting transfers between devices, body(): pooled_grad = pooled_grad + lax.ppermute(mine, 'expert', pairs).astype(F32)  5.95 us
    ppermute x4, waiting for transfers between devices, body(): pooled_grad = pooled_grad + lax.ppermute(mine, 'expert', pairs).astype(F32)  3.43 us
  transfers between devices with their start and end apart: 62, of which 28 were waited for; matrix products, arithmetic and copies ran while one was open for 1% of the time, Pallas kernels for 14%

profile of v16, /device:TPU:0, one launch (start us, length us, event | category | flops | bytes accessed | tf_op | source)
XLA Modules:
  0.0 123.0 jit_solution(10292182289018732559)
XLA Ops:
  0.6 1.9 %shard_map.104 = (bf16[64,1152]{1,0:T(8,128)(2,1)S(1)}, bf16[64,1024]{1,0:T(8,128)(2,1)S(1)}, bf16[3200,384]{1,0:T(8,128)(2,1)S(1)}) custom-call(s32[8,128]{1,0:T(8,128)} %bitcast.19, f32[8,128]{1,0:T(8,128)} %bitcast.20, bf16[128,1024]{1,0:T(8,128)(2,1)} %refs_2_.2, bf16[2,512,384]{2,1,0:T(8,128)(2,1)} %refs_0_.1, bf16[2,512,384]{2,1,0:T(8,128)(2,1)} %refs_1_.1, ...), custom_call_target="tpu_custom_call" | custom-call | tf_op jit(solution)/shard_map/pallas_call | solution.py:215
  3.1 2.6 %collective-permute-start.1 = (bf16[64,1152]{1,0:T(8,128)(2,1)S(1)}, bf16[64,1152]{1,0:T(8,128)(2,1)S(1)}, u32[]{:S(2)}, u32[]{:S(2)}) collective-permute-start(bf16[64,1152]{1,0:T(8,128)(2,1)S(1)} %get-tuple-element.64.refs_0_), channel_id=1, source_target_pairs={{0,4},{4,8},{8,12},{12,14},{14,10},{10,6},{6,2},{2,0},{1,5},{5,9},... | collective-permute-start | bytes 442376 | tf_op jit(solution)/shard_map/ppermute | solution.py:68
  5.7 4.4 %collective-permute-done.1.refs_0_ = bf16[64,1152]{1,0:T(8,128)(2,1)S(1)} collective-permute-done((bf16[64,1152]{1,0:T(8,128)(2,1)S(1)}, bf16[64,1152]{1,0:T(8,128)(2,1)S(1)}, u32[]{:S(2)}, u32[]{:S(2)}) %collective-permute-start.1) | collective-permute-done | bytes 147488 | tf_op jit(solution)/shard_map/ppermute | solution.py:68
  10.1 1.8 %collective-permute-start.5 = (bf16[64,1152]{1,0:T(8,128)(2,1)S(1)}, bf16[64,1152]{1,0:T(8,128)(2,1)S(1)}, u32[]{:S(2)}, u32[]{:S(2)}) collective-permute-start(bf16[64,1152]{1,0:T(8,128)(2,1)S(1)} %collective-permute-done.1.refs_0_), channel_id=1, source_target_pairs={{0,4},{4,8},{8,12},{12,14},{14,10},{10,6},{6,2},{2,0},{1,5},{5,9},... | collective-permute-start | bytes 442376 | tf_op jit(solution)/shard_map/ppermute | solution.py:68
  12.1 1.7 %collective-permute-start.3 = (bf16[64,1152]{1,0:T(8,128)(2,1)S(1)}, bf16[64,1152]{1,0:T(8,128)(2,1)S(1)}, u32[]{:S(2)}, u32[]{:S(2)}) collective-permute-start(bf16[64,1152]{1,0:T(8,128)(2,1)S(1)} %get-tuple-element.64.refs_0_), channel_id=1, source_target_pairs={{0,2},{4,0},{8,4},{12,8},{14,12},{10,14},{6,10},{2,6},{1,3},{5,1},... | collective-permute-start | bytes 442376 | tf_op jit(solution)/shard_map/ppermute | solution.py:68
  14.2 2.0 %collective-permute-done.5.refs_0_ = bf16[64,1152]{1,0:T(8,128)(2,1)S(1)} collective-permute-done((bf16[64,1152]{1,0:T(8,128)(2,1)S(1)}, bf16[64,1152]{1,0:T(8,128)(2,1)S(1)}, u32[]{:S(2)}, u32[]{:S(2)}) %collective-permute-start.5) | collective-permute-done | bytes 147488 | tf_op jit(solution)/shard_map/ppermute | solution.py:68
  16.2 2.5 %collective-permute-start.9 = (bf16[64,1152]{1,0:T(8,128)(2,1)S(1)}, bf16[64,1152]{1,0:T(8,128)(2,1)S(1)}, u32[]{:S(2)}, u32[]{:S(2)}) collective-permute-start(bf16[64,1152]{1,0:T(8,128)(2,1)S(1)} %collective-permute-done.5.refs_0_), channel_id=1, source_target_pairs={{0,4},{4,8},{8,12},{12,14},{14,10},{10,6},{6,2},{2,0},{1,5},{5,9},... | collective-permute-start | bytes 442376 | tf_op jit(solution)/shard_map/ppermute | solution.py:68
  18.7 2.6 %collective-permute-done.3.refs_2_ = bf16[64,1152]{1,0:T(8,128)(2,1)S(1)} collective-permute-done((bf16[64,1152]{1,0:T(8,128)(2,1)S(1)}, bf16[64,1152]{1,0:T(8,128)(2,1)S(1)}, u32[]{:S(2)}, u32[]{:S(2)}) %collective-permute-start.3) | collective-permute-done | bytes 147488 | tf_op jit(solution)/shard_map/ppermute | solution.py:68
  21.4 1.9 %collective-permute-start.6 = (bf16[64,1024]{1,0:T(8,128)(2,1)S(1)}, bf16[64,1024]{1,0:T(8,128)(2,1)S(1)}, u32[]{:S(2)}, u32[]{:S(2)}) collective-permute-start(bf16[64,1024]{1,0:T(8,128)(2,1)S(1)} %collective-permute-done.2.refs_1_), channel_id=1, source_target_pairs={{0,4},{4,8},{8,12},{12,14},{14,10},{10,6},{6,2},{2,0},{1,5},{5,9},... | collective-permute-start | bytes 393224 | tf_op jit(solution)/shard_map/ppermute | solution.py:68
  23.3 1.8 %collective-permute-start.13 = (bf16[64,1152]{1,0:T(8,128)(2,1)S(1)}, bf16[64,1152]{1,0:T(8,128)(2,1)S(1)}, u32[]{:S(2)}, u32[]{:S(2)}) collective-permute-start(bf16[64,1152]{1,0:T(8,128)(2,1)S(1)} %collective-permute-done.9.refs_0_), channel_id=1, source_target_pairs={{0,4},{4,8},{8,12},{12,14},{14,10},{10,6},{6,2},{2,0},{1,5},{5,9},... | collective-permute-start | bytes 442376 | tf_op jit(solution)/shard_map/ppermute | solution.py:68
  25.3 1.9 %collective-permute-done.7.refs_2_ = bf16[64,1152]{1,0:T(8,128)(2,1)S(1)} collective-permute-done((bf16[64,1152]{1,0:T(8,128)(2,1)S(1)}, bf16[64,1152]{1,0:T(8,128)(2,1)S(1)}, u32[]{:S(2)}, u32[]{:S(2)}) %collective-permute-start.7) | collective-permute-done | bytes 147488 | tf_op jit(solution)/shard_map/ppermute | solution.py:68
  27.3 1.8 %shard_map.105 = (bf16[1024,1536]{1,0:T(8,128)(2,1)S(1)}, bf16[768,1024]{1,0:T(8,128)(2,1)S(1)}) custom-call(bf16[2,512,384]{2,1,0:T(8,128)(2,1)} %refs_0_.1, bf16[2,512,384]{2,1,0:T(8,128)(2,1)} %refs_1_.1, bf16[2,192,1024]{2,1,0:T(8,128)(2,1)} %refs_2_.3, bf16[3200,384]{1,0:T(8,128)(2,1)S(1)} %collective-permute-done.refs_3_), custom_call_target="tpu_custom_call" | custom-call | tf_op jit(solution)/shard_map/pallas_call | solution.py:270
  32.2 1.6 %collective-permute-start.15 = (bf16[64,1024]{1,0:T(8,128)(2,1)S(1)}, bf16[64,1024]{1,0:T(8,128)(2,1)S(1)}, u32[]{:S(2)}, u32[]{:S(2)}) collective-permute-start(bf16[64,1024]{1,0:T(8,128)(2,1)S(1)} %get-tuple-element.73), channel_id=1, source_target_pairs={{0,4},{4,8},{8,12},{12,14},{14,10},{10,6},{6,2},{2,0},{1,5},{5,9},... | collective-permute-start | bytes 393224 | tf_op jit(solution)/shard_map/ppermute | solution.py:68
  48.2 1.7 %collective-permute-start.27 = (bf16[64,1024]{1,0:T(8,128)(2,1)S(1)}, bf16[64,1024]{1,0:T(8,128)(2,1)S(1)}, u32[]{:S(2)}, u32[]{:S(2)}) collective-permute-start(bf16[64,1024]{1,0:T(8,128)(2,1)S(1)} %shard_map.121), channel_id=1, source_target_pairs={{0,2},{4,0},{8,4},{12,8},{14,12},{10,14},{6,10},{2,6},{1,3},{5,1},... | collective-permute-start | bytes 393224 | tf_op jit(solution)/shard_map/ppermute | solution.py:68
  51.6 2.1 %collective-permute-start.18 = (bf16[64,1024]{1,0:T(8,128)(2,1)S(1)}, bf16[64,1024]{1,0:T(8,128)(2,1)S(1)}, u32[]{:S(2)}, u32[]{:S(2)}) collective-permute-start(bf16[64,1024]{1,0:T(8,128)(2,1)S(1)} %shard_map.114), channel_id=1, source_target_pairs={{0,4},{4,8},{8,12},{12,14},{14,10},{10,6},{6,2},{2,0},{1,5},{5,9},... | collective-permute-start | bytes 393224 | tf_op jit(solution)/shard_map/ppermute | solution.py:68
  54.3 2.1 %collective-permute-start.28 = (bf16[64,1024]{1,0:T(8,128)(2,1)S(1)}, bf16[64,1024]{1,0:T(8,128)(2,1)S(1)}, u32[]{:S(2)}, u32[]{:S(2)}) collective-permute-start(bf16[64,1024]{1,0:T(8,128)(2,1)S(1)} %shard_map.122), channel_id=1, source_target_pairs={{0,2},{4,0},{8,4},{12,8},{14,12},{10,14},{6,10},{2,6},{1,3},{5,1},... | collective-permute-start | bytes 393224 | tf_op jit(solution)/shard_map/ppermute | solution.py:68
  57.9 2.1 %collective-permute-start.29 = (bf16[64,1024]{1,0:T(8,128)(2,1)S(1)}, bf16[64,1024]{1,0:T(8,128)(2,1)S(1)}, u32[]{:S(2)}, u32[]{:S(2)}) collective-permute-start(bf16[64,1024]{1,0:T(8,128)(2,1)S(1)} %shard_map.117.refs_2_), channel_id=1, source_target_pairs={{0,4},{4,8},{8,12},{12,14},{14,10},{10,6},{6,2},{2,0},{1,5},{5,9},... | collective-permute-start | bytes 393224 | tf_op jit(solution)/shard_map/ppermute | solution.py:68
  64.3 2.2 %collective-permute-start.30 = (bf16[64,1024]{1,0:T(8,128)(2,1)S(1)}, bf16[64,1024]{1,0:T(8,128)(2,1)S(1)}, u32[]{:S(2)}, u32[]{:S(2)}) collective-permute-start(bf16[64,1024]{1,0:T(8,128)(2,1)S(1)} %collective-permute-done.29.refs_4_), channel_id=1, source_target_pairs={{0,4},{4,8},{8,12},{12,14},{14,10},{10,6},{6,2},{2,0},{1,5},{5,9},... | collective-permute-start | bytes 393224 | tf_op jit(solution)/shard_map/ppermute | solution.py:68
  69.7 1.7 %collective-permute-start.41 = (bf16[64,1024]{1,0:T(8,128)(2,1)S(1)}, bf16[64,1024]{1,0:T(8,128)(2,1)S(1)}, u32[]{:S(2)}, u32[]{:S(2)}) collective-permute-start(bf16[64,1024]{1,0:T(8,128)(2,1)S(1)} %collective-permute-done.40.refs_6_), channel_id=1, source_target_pairs={{0,2},{4,0},{8,4},{12,8},{14,12},{10,14},{6,10},{2,6},{1,3},{5,1},... | collective-permute-start | bytes 393224 | tf_op jit(solution)/shard_map/ppermute | solution.py:68
  74.6 1.8 %collective-permute-start.42 = (bf16[64,1024]{1,0:T(8,128)(2,1)S(1)}, bf16[64,1024]{1,0:T(8,128)(2,1)S(1)}, u32[]{:S(2)}, u32[]{:S(2)}) collective-permute-start(bf16[64,1024]{1,0:T(8,128)(2,1)S(1)} %collective-permute-done.41.refs_6_), channel_id=1, source_target_pairs={{0,2},{4,0},{8,4},{12,8},{14,12},{10,14},{6,10},{2,6},{1,3},{5,1},... | collective-permute-start | bytes 393224 | tf_op jit(solution)/shard_map/ppermute | solution.py:68
  78.4 1.6 %collective-permute-start.36 = (bf16[64,1024]{1,0:T(8,128)(2,1)S(1)}, bf16[64,1024]{1,0:T(8,128)(2,1)S(1)}, u32[]{:S(2)}, u32[]{:S(2)}) collective-permute-start(bf16[64,1024]{1,0:T(8,128)(2,1)S(1)} %collective-permute-done.35.refs_7_), channel_id=1, source_target_pairs={{0,2},{4,0},{8,4},{12,8},{14,12},{10,14},{6,10},{2,6},{1,3},{5,1},... | collective-permute-start | bytes 393224 | tf_op jit(solution)/shard_map/ppermute | solution.py:68
  85.7 2.3 %collective-permute-done.43 = bf16[8,1024]{1,0:T(8,128)(2,1)S(1)} collective-permute-done((bf16[8,1024]{1,0:T(8,128)(2,1)S(1)}, bf16[8,1024]{1,0:T(8,128)(2,1)S(1)}, u32[]{:S(2)}, u32[]{:S(2)}) %collective-permute-start.43) | collective-permute-done | bytes 16416 | tf_op jit(solution)/shard_map/ppermute | solution.py:435
  87.9 2.8 %collective-permute-start.46 = (bf16[8,1024]{1,0:T(8,128)(2,1)S(1)}, bf16[8,1024]{1,0:T(8,128)(2,1)S(1)}, u32[]{:S(2)}, u32[]{:S(2)}) collective-permute-start(bf16[8,1024]{1,0:T(8,128)(2,1)S(1)} %add_convert_fusion), channel_id=1, source_target_pairs={{0,12},{2,14},{4,8},{6,10},{8,4},{10,6},{12,0},{14,2},{1,13},{3,15... | collective-permute-start | bytes 49160 | tf_op jit(solution)/shard_map/ppermute | solution.py:435
  90.7 1.6 %collective-permute-start.44 = (bf16[8,1024]{1,0:T(8,128)(2,1)S(1)}, bf16[8,1024]{1,0:T(8,128)(2,1)S(1)}, u32[]{:S(2)}, u32[]{:S(2)}) collective-permute-start(bf16[8,1024]{1,0:T(8,128)(2,1)S(1)} %add_convert_fusion), channel_id=1, source_target_pairs={{0,4},{2,6},{4,0},{6,2},{8,12},{10,14},{12,8},{14,10},{1,5},{3,7},... | collective-permute-start | bytes 49160 | tf_op jit(solution)/shard_map/ppermute | solution.py:435
  (159 shorter events, 71.4 us)
Async XLA Ops:
  2.6 24.7 %collective-permute-start = (bf16[3200,384]{1,0:T(8,128)(2,1)S(1)}, bf16[3200,384]{1,0:T(8,128)(2,1)S(1)}, u32[]{:S(2)}, u32[]{:S(2)}) collective-permute-start(bf16[3200,384]{1,0:T(8,128)(2,1)S(1)} %get-tuple-element.66), channel_id=1, source_target_pairs={{0,1},{1,0},{2,3},{3,2},{4,5},{5,4},{6,7},{7,6},{8,9},{9,8},{10,11... | collective-permute-start | bytes 7372808 | tf_op jit(solution)/shard_map/ppermute | solution.py:310
  3.1 7.0 %collective-permute-start.1 = (bf16[64,1152]{1,0:T(8,128)(2,1)S(1)}, bf16[64,1152]{1,0:T(8,128)(2,1)S(1)}, u32[]{:S(2)}, u32[]{:S(2)}) collective-permute-start(bf16[64,1152]{1,0:T(8,128)(2,1)S(1)} %get-tuple-element.64.refs_0_), channel_id=1, source_target_pairs={{0,4},{4,8},{8,12},{12,14},{14,10},{10,6},{6,2},{2,0},{1,5},{5,9},... | collective-permute-start | bytes 442376 | tf_op jit(solution)/shard_map/ppermute | solution.py:68
  11.9 6.8 %collective-permute-start.8 = (bf16[64,1024]{1,0:T(8,128)(2,1)S(1)}, bf16[64,1024]{1,0:T(8,128)(2,1)S(1)}, u32[]{:S(2)}, u32[]{:S(2)}) collective-permute-start(bf16[64,1024]{1,0:T(8,128)(2,1)S(1)} %collective-permute-done.4.refs_3_), channel_id=1, source_target_pairs={{0,2},{4,0},{8,4},{12,8},{14,12},{10,14},{6,10},{2,6},{1,3},{5,1},... | collective-permute-start | bytes 393224 | tf_op jit(solution)/shard_map/ppermute | solution.py:68
  12.1 9.1 %collective-permute-start.3 = (bf16[64,1152]{1,0:T(8,128)(2,1)S(1)}, bf16[64,1152]{1,0:T(8,128)(2,1)S(1)}, u32[]{:S(2)}, u32[]{:S(2)}) collective-permute-start(bf16[64,1152]{1,0:T(8,128)(2,1)S(1)} %get-tuple-element.64.refs_0_), channel_id=1, source_target_pairs={{0,2},{4,0},{8,4},{12,8},{14,12},{10,14},{6,10},{2,6},{1,3},{5,1},... | collective-permute-start | bytes 442376 | tf_op jit(solution)/shard_map/ppermute | solution.py:68
  13.9 7.6 %collective-permute-start.2 = (bf16[64,1024]{1,0:T(8,128)(2,1)S(1)}, bf16[64,1024]{1,0:T(8,128)(2,1)S(1)}, u32[]{:S(2)}, u32[]{:S(2)}) collective-permute-start(bf16[64,1024]{1,0:T(8,128)(2,1)S(1)} %get-tuple-element.65.refs_1_), channel_id=1, source_target_pairs={{0,4},{4,8},{8,12},{12,14},{14,10},{10,6},{6,2},{2,0},{1,5},{5,9},... | collective-permute-start | bytes 393224 | tf_op jit(solution)/shard_map/ppermute | solution.py:68
  16.2 7.1 %collective-permute-start.9 = (bf16[64,1152]{1,0:T(8,128)(2,1)S(1)}, bf16[64,1152]{1,0:T(8,128)(2,1)S(1)}, u32[]{:S(2)}, u32[]{:S(2)}) collective-permute-start(bf16[64,1152]{1,0:T(8,128)(2,1)S(1)} %collective-permute-done.5.refs_0_), channel_id=1, source_target_pairs={{0,4},{4,8},{8,12},{12,14},{14,10},{10,6},{6,2},{2,0},{1,5},{5,9},... | collective-permute-start | bytes 442376 | tf_op jit(solution)/shard_map/ppermute | solution.py:68
  21.4 8.2 %collective-permute-start.6 = (bf16[64,1024]{1,0:T(8,128)(2,1)S(1)}, bf16[64,1024]{1,0:T(8,128)(2,1)S(1)}, u32[]{:S(2)}, u32[]{:S(2)}) collective-permute-start(bf16[64,1024]{1,0:T(8,128)(2,1)S(1)} %collective-permute-done.2.refs_1_), channel_id=1, source_target_pairs={{0,4},{4,8},{8,12},{12,14},{14,10},{10,6},{6,2},{2,0},{1,5},{5,9},... | collective-permute-start | bytes 393224 | tf_op jit(solution)/shard_map/ppermute | solution.py:68
  23.3 7.8 %collective-permute-start.13 = (bf16[64,1152]{1,0:T(8,128)(2,1)S(1)}, bf16[64,1152]{1,0:T(8,128)(2,1)S(1)}, u32[]{:S(2)}, u32[]{:S(2)}) collective-permute-start(bf16[64,1152]{1,0:T(8,128)(2,1)S(1)} %collective-permute-done.9.refs_0_), channel_id=1, source_target_pairs={{0,4},{4,8},{8,12},{12,14},{14,10},{10,6},{6,2},{2,0},{1,5},{5,9},... | collective-permute-start | bytes 442376 | tf_op jit(solution)/shard_map/ppermute | solution.py:68
  32.2 6.4 %collective-permute-start.15 = (bf16[64,1024]{1,0:T(8,128)(2,1)S(1)}, bf16[64,1024]{1,0:T(8,128)(2,1)S(1)}, u32[]{:S(2)}, u32[]{:S(2)}) collective-permute-start(bf16[64,1024]{1,0:T(8,128)(2,1)S(1)} %get-tuple-element.73), channel_id=1, source_target_pairs={{0,4},{4,8},{8,12},{12,14},{14,10},{10,6},{6,2},{2,0},{1,5},{5,9},... | collective-permute-start | bytes 393224 | tf_op jit(solution)/shard_map/ppermute | solution.py:68
  33.8 8.0 %collective-permute-start.25 = (bf16[64,1024]{1,0:T(8,128)(2,1)S(1)}, bf16[64,1024]{1,0:T(8,128)(2,1)S(1)}, u32[]{:S(2)}, u32[]{:S(2)}) collective-permute-start(bf16[64,1024]{1,0:T(8,128)(2,1)S(1)} %get-tuple-element.84), channel_id=1, source_target_pairs={{0,2},{4,0},{8,4},{12,8},{14,12},{10,14},{6,10},{2,6},{1,3},{5,1},... | collective-permute-start | bytes 393224 | tf_op jit(solution)/shard_map/ppermute | solution.py:68
  36.3 7.5 %collective-permute-start.19 = (bf16[64,1024]{1,0:T(8,128)(2,1)S(1)}, bf16[64,1024]{1,0:T(8,128)(2,1)S(1)}, u32[]{:S(2)}, u32[]{:S(2)}) collective-permute-start(bf16[64,1024]{1,0:T(8,128)(2,1)S(1)} %get-tuple-element.76), channel_id=1, source_target_pairs={{0,2},{4,0},{8,4},{12,8},{14,12},{10,14},{6,10},{2,6},{1,3},{5,1},... | collective-permute-start | bytes 393224 | tf_op jit(solution)/shard_map/ppermute | solution.py:68
  40.2 7.5 %collective-permute-start.22 = (bf16[64,1024]{1,0:T(8,128)(2,1)S(1)}, bf16[64,1024]{1,0:T(8,128)(2,1)S(1)}, u32[]{:S(2)}, u32[]{:S(2)}) collective-permute-start(bf16[64,1024]{1,0:T(8,128)(2,1)S(1)} %get-tuple-element.80), channel_id=1, source_target_pairs={{0,4},{4,8},{8,12},{12,14},{14,10},{10,6},{6,2},{2,0},{1,5},{5,9},... | collective-permute-start | bytes 393224 | tf_op jit(solution)/shard_map/ppermute | solution.py:68
  43.9 7.6 %collective-permute-start.20 = (bf16[64,1024]{1,0:T(8,128)(2,1)S(1)}, bf16[64,1024]{1,0:T(8,128)(2,1)S(1)}, u32[]{:S(2)}, u32[]{:S(2)}) collective-permute-start(bf16[64,1024]{1,0:T(8,128)(2,1)S(1)} %shard_map.115), channel_id=1, source_target_pairs={{0,2},{4,0},{8,4},{12,8},{14,12},{10,14},{6,10},{2,6},{1,3},{5,1},... | collective-permute-start | bytes 393224 | tf_op jit(solution)/shard_map/ppermute | solution.py:68
  45.0 6.5 %collective-permute-start.17 = (bf16[64,1024]{1,0:T(8,128)(2,1)S(1)}, bf16[64,1024]{1,0:T(8,128)(2,1)S(1)}, u32[]{:S(2)}, u32[]{:S(2)}) collective-permute-start(bf16[64,1024]{1,0:T(8,128)(2,1)S(1)} %shard_map.113), channel_id=1, source_target_pairs={{0,4},{4,8},{8,12},{12,14},{14,10},{10,6},{6,2},{2,0},{1,5},{5,9},... | collective-permute-start | bytes 393224 | tf_op jit(solution)/shard_map/ppermute | solution.py:68
  47.8 6.4 %collective-permute-start.23 = (bf16[64,1024]{1,0:T(8,128)(2,1)S(1)}, bf16[64,1024]{1,0:T(8,128)(2,1)S(1)}, u32[]{:S(2)}, u32[]{:S(2)}) collective-permute-start(bf16[64,1024]{1,0:T(8,128)(2,1)S(1)} %shard_map.118), channel_id=1, source_target_pairs={{0,4},{4,8},{8,12},{12,14},{14,10},{10,6},{6,2},{2,0},{1,5},{5,9},... | collective-permute-start | bytes 393224 | tf_op jit(solution)/shard_map/ppermute | solution.py:68
  54.2 6.5 %collective-permute-start.24 = (bf16[64,1024]{1,0:T(8,128)(2,1)S(1)}, bf16[64,1024]{1,0:T(8,128)(2,1)S(1)}, u32[]{:S(2)}, u32[]{:S(2)}) collective-permute-start(bf16[64,1024]{1,0:T(8,128)(2,1)S(1)} %shard_map.119), channel_id=1, source_target_pairs={{0,4},{4,8},{8,12},{12,14},{14,10},{10,6},{6,2},{2,0},{1,5},{5,9},... | collective-permute-start | bytes 393224 | tf_op jit(solution)/shard_map/ppermute | solution.py:68
  54.3 6.4 %collective-permute-start.28 = (bf16[64,1024]{1,0:T(8,128)(2,1)S(1)}, bf16[64,1024]{1,0:T(8,128)(2,1)S(1)}, u32[]{:S(2)}, u32[]{:S(2)}) collective-permute-start(bf16[64,1024]{1,0:T(8,128)(2,1)S(1)} %shard_map.122), channel_id=1, source_target_pairs={{0,2},{4,0},{8,4},{12,8},{14,12},{10,14},{6,10},{2,6},{1,3},{5,1},... | collective-permute-start | bytes 393224 | tf_op jit(solution)/shard_map/ppermute | solution.py:68
  62.2 7.4 %collective-permute-start.40 = (bf16[64,1024]{1,0:T(8,128)(2,1)S(1)}, bf16[64,1024]{1,0:T(8,128)(2,1)S(1)}, u32[]{:S(2)}, u32[]{:S(2)}) collective-permute-start(bf16[64,1024]{1,0:T(8,128)(2,1)S(1)} %shard_map.117.refs_2_), channel_id=1, source_target_pairs={{0,2},{4,0},{8,4},{12,8},{14,12},{10,14},{6,10},{2,6},{1,3},{5,1},... | collective-permute-start | bytes 393224 | tf_op jit(solution)/shard_map/ppermute | solution.py:68
  63.3 8.2 %collective-permute-start.37 = (bf16[64,1024]{1,0:T(8,128)(2,1)S(1)}, bf16[64,1024]{1,0:T(8,128)(2,1)S(1)}, u32[]{:S(2)}, u32[]{:S(2)}) collective-permute-start(bf16[64,1024]{1,0:T(8,128)(2,1)S(1)} %shard_map.123.refs_3_), channel_id=1, source_target_pairs={{0,4},{4,8},{8,12},{12,14},{14,10},{10,6},{6,2},{2,0},{1,5},{5,9},... | collective-permute-start | bytes 393224 | tf_op jit(solution)/shard_map/ppermute | solution.py:68
  64.3 8.2 %collective-permute-start.30 = (bf16[64,1024]{1,0:T(8,128)(2,1)S(1)}, bf16[64,1024]{1,0:T(8,128)(2,1)S(1)}, u32[]{:S(2)}, u32[]{:S(2)}) collective-permute-start(bf16[64,1024]{1,0:T(8,128)(2,1)S(1)} %collective-permute-done.29.refs_4_), channel_id=1, source_target_pairs={{0,4},{4,8},{8,12},{12,14},{14,10},{10,6},{6,2},{2,0},{1,5},{5,9},... | collective-permute-start | bytes 393224 | tf_op jit(solution)/shard_map/ppermute | solution.py:68
  108.3 7.8 %collective-permute-start.49 = (bf16[64,1024]{1,0:T(8,128)(2,1)S(1)}, bf16[64,1024]{1,0:T(8,128)(2,1)S(1)}, u32[]{:S(2)}, u32[]{:S(2)}) collective-permute-start(bf16[64,1024]{1,0:T(8,128)(2,1)S(1)} %shard_map.137), channel_id=1, source_target_pairs={{0,4},{4,8},{8,12},{12,14},{14,10},{10,6},{6,2},{2,0},{1,5},{5,9},... | collective-permute-start | bytes 393224 | tf_op jit(solution)/shard_map/ppermute | solution.py:68
  109.2 8.0 %collective-permute-start.59 = (bf16[64,1024]{1,0:T(8,128)(2,1)S(1)}, bf16[64,1024]{1,0:T(8,128)(2,1)S(1)}, u32[]{:S(2)}, u32[]{:S(2)}) collective-permute-start(bf16[64,1024]{1,0:T(8,128)(2,1)S(1)} %shard_map.144), channel_id=1, source_target_pairs={{0,2},{4,0},{8,4},{12,8},{14,12},{10,14},{6,10},{2,6},{1,3},{5,1},... | collective-permute-start | bytes 393224 | tf_op jit(solution)/shard_map/ppermute | solution.py:68
  112.5 8.3 %collective-permute-start.53 = (bf16[64,1024]{1,0:T(8,128)(2,1)S(1)}, bf16[64,1024]{1,0:T(8,128)(2,1)S(1)}, u32[]{:S(2)}, u32[]{:S(2)}) collective-permute-start(bf16[64,1024]{1,0:T(8,128)(2,1)S(1)} %shard_map.140), channel_id=1, source_target_pairs={{0,2},{4,0},{8,4},{12,8},{14,12},{10,14},{6,10},{2,6},{1,3},{5,1},... | collective-permute-start | bytes 393224 | tf_op jit(solution)/shard_map/ppermute | solution.py:68
  113.8 7.0 %collective-permute-start.56 = (bf16[64,1024]{1,0:T(8,128)(2,1)S(1)}, bf16[64,1024]{1,0:T(8,128)(2,1)S(1)}, u32[]{:S(2)}, u32[]{:S(2)}) collective-permute-start(bf16[64,1024]{1,0:T(8,128)(2,1)S(1)} %shard_map.142), channel_id=1, source_target_pairs={{0,4},{4,8},{8,12},{12,14},{14,10},{10,6},{6,2},{2,0},{1,5},{5,9},... | collective-permute-start | bytes 393224 | tf_op jit(solution)/shard_map/ppermute | solution.py:68
  (41 other events, 349.5 us)

commit v17 on v16

--- a/solution.py
+++ b/solution.py
@@ -277,6 +277,11 @@
         out_specs=[pl.BlockSpec(memory_space=pltpu.VMEM)] * 2,
         scratch_shapes=[pltpu.SemaphoreType.DMA((count,))],
         compiler_params=pltpu.CompilerParams(vmem_limit_bytes=VMEM_LIMIT),
+        cost_estimate=pl.CostEstimate(
+            flops=0,
+            bytes_accessed=12 * local_experts * hidden_dim * feature_dim,
+            transcendentals=0,
+        ),
     )(*shards)
 
 
@@ -425,14 +430,31 @@
     logits = dot(pooled, class_head)
     target_rows = targets.reshape(expert_count, -1).astype(F32)
     logit_grad = (LOSS_SCALE * (jax.nn.sigmoid(logits) - target_rows)).astype(BF16)
-    pooled_grad = dot_t(logit_grad, class_head)
+    wide_t, down_t = transposed(wide), transposed(down)
+
+    def grad_sum_kernel(count, *refs):
+        total = refs[0][...].astype(F32)
+        for ref in refs[1:count]:
+            total = total + ref[...].astype(F32)
+        refs[-1][...] = total.astype(refs[-1].dtype)
+
+    grad_rows = dot_t(logit_grad, class_head).astype(BF16)
     span = 2
-    for masks in ([1], list(range(span, expert_count, span))):
-        mine = pooled_grad.astype(BF16)
-        pooled_grad = mine.astype(F32)
+    for masks, others, dtype in (
+        ([1], [wide_t, down_t], BF16),
+        (list(range(span, expert_count, span)), [], F32),
+    ):
+        terms = [grad_rows]
         for mask in masks:
             pairs = [(e, e ^ mask) for e in range(expert_count)]
-            pooled_grad = pooled_grad + lax.ppermute(mine, "expert", pairs).astype(F32)
+            terms.append(lax.ppermute(grad_rows, "expert", pairs))
+        grad_rows = call(
+            functools.partial(grad_sum_kernel, len(terms)),
+            [(pooled_shape, dtype)],
+            *terms,
+            *others,
+        )[0]
+    pooled_grad = grad_rows
 
     both = jnp.concatenate([pooled, logit_grad], axis=1)
     if group_count == 2:
@@ -470,7 +492,6 @@
         for i, out in enumerate(outs):
             out[...] = total[i * rows : (i + 1) * rows].astype(out.dtype)
 
-    wide_t, down_t = transposed(wide), transposed(down)
     back_at = {}
 
     def backward(distances):

time: 123 us -> 123 us (level)
    pallas_call x39 -> x41, Pallas kernels: 17.4 us -> 17.4 us  [call(): pl.pallas_call(kernel, out_shape=[pltpu.VMEM(shape, dtype) for shape, dty...]
  transfers between devices with their start and end apart: 62 -> 62, of which waited for: 28 -> 30; matrix products, arithmetic and copies ran while one was open for 1% -> 1% of each run, Pallas kernels for 14% -> 15%
where the time goes in v17:
time: 123 us
  starting transfers between devices  68.4 us (56%)
  waiting for transfers between devices  30 us (24%)
  Pallas kernels  21.9 us (18%)
  matrix products  1.71 us (1%)
    ppermute x56, starting transfers between devices, send(): return lax.ppermute(value, 'expert', pairs)  62.2 us
    ppermute x56, waiting for transfers between devices, send(): return lax.ppermute(value, 'expert', pairs)  26.3 us
    pallas_call x41, Pallas kernels, call(): pl.pallas_call(kernel, out_shape=[pltpu.VMEM(shape, dtype) for shape, dty...  17.4 us
    ppermute x4, starting transfers between devices, body(): terms.append(lax.ppermute(grad_rows, 'expert', pairs))  5.62 us
    ppermute x4, waiting for transfers between devices, body(): terms.append(lax.ppermute(grad_rows, 'expert', pairs))  3.71 us
  transfers between devices with their start and end apart: 62, of which 30 were waited for; matrix products, arithmetic and copies ran while one was open for 1% of the time, Pallas kernels for 15%

profile of v17, /device:TPU:0, one launch (start us, length us, event | category | flops | bytes accessed | tf_op | source)
XLA Modules:
  0.0 123.1 jit_solution(11615198651944996297)
XLA Ops:
  0.6 1.9 %shard_map.104 = (bf16[64,1152]{1,0:T(8,128)(2,1)S(1)}, bf16[64,1024]{1,0:T(8,128)(2,1)S(1)}, bf16[3200,384]{1,0:T(8,128)(2,1)S(1)}) custom-call(s32[8,128]{1,0:T(8,128)} %bitcast.19, f32[8,128]{1,0:T(8,128)} %bitcast.20, bf16[128,1024]{1,0:T(8,128)(2,1)} %refs_2_.2, bf16[2,512,384]{2,1,0:T(8,128)(2,1)} %refs_0_.1, bf16[2,512,384]{2,1,0:T(8,128)(2,1)} %refs_1_.1, ...), custom_call_target="tpu_custom_call" | custom-call | tf_op jit(solution)/shard_map/pallas_call | solution.py:215
  3.1 2.6 %collective-permute-start.1 = (bf16[64,1152]{1,0:T(8,128)(2,1)S(1)}, bf16[64,1152]{1,0:T(8,128)(2,1)S(1)}, u32[]{:S(2)}, u32[]{:S(2)}) collective-permute-start(bf16[64,1152]{1,0:T(8,128)(2,1)S(1)} %get-tuple-element.64.refs_0_), channel_id=1, source_target_pairs={{0,4},{4,8},{8,12},{12,14},{14,10},{10,6},{6,2},{2,0},{1,5},{5,9},... | collective-permute-start | bytes 442376 | tf_op jit(solution)/shard_map/ppermute | solution.py:68
  5.7 4.4 %collective-permute-done.1.refs_0_ = bf16[64,1152]{1,0:T(8,128)(2,1)S(1)} collective-permute-done((bf16[64,1152]{1,0:T(8,128)(2,1)S(1)}, bf16[64,1152]{1,0:T(8,128)(2,1)S(1)}, u32[]{:S(2)}, u32[]{:S(2)}) %collective-permute-start.1) | collective-permute-done | bytes 147488 | tf_op jit(solution)/shard_map/ppermute | solution.py:68
  10.1 1.8 %collective-permute-start.5 = (bf16[64,1152]{1,0:T(8,128)(2,1)S(1)}, bf16[64,1152]{1,0:T(8,128)(2,1)S(1)}, u32[]{:S(2)}, u32[]{:S(2)}) collective-permute-start(bf16[64,1152]{1,0:T(8,128)(2,1)S(1)} %collective-permute-done.1.refs_0_), channel_id=1, source_target_pairs={{0,4},{4,8},{8,12},{12,14},{14,10},{10,6},{6,2},{2,0},{1,5},{5,9},... | collective-permute-start | bytes 442376 | tf_op jit(solution)/shard_map/ppermute | solution.py:68
  12.1 1.7 %collective-permute-start.3 = (bf16[64,1152]{1,0:T(8,128)(2,1)S(1)}, bf16[64,1152]{1,0:T(8,128)(2,1)S(1)}, u32[]{:S(2)}, u32[]{:S(2)}) collective-permute-start(bf16[64,1152]{1,0:T(8,128)(2,1)S(1)} %get-tuple-element.64.refs_0_), channel_id=1, source_target_pairs={{0,2},{4,0},{8,4},{12,8},{14,12},{10,14},{6,10},{2,6},{1,3},{5,1},... | collective-permute-start | bytes 442376 | tf_op jit(solution)/shard_map/ppermute | solution.py:68
  14.2 2.0 %collective-permute-done.5.refs_0_ = bf16[64,1152]{1,0:T(8,128)(2,1)S(1)} collective-permute-done((bf16[64,1152]{1,0:T(8,128)(2,1)S(1)}, bf16[64,1152]{1,0:T(8,128)(2,1)S(1)}, u32[]{:S(2)}, u32[]{:S(2)}) %collective-permute-start.5) | collective-permute-done | bytes 147488 | tf_op jit(solution)/shard_map/ppermute | solution.py:68
  16.2 2.5 %collective-permute-start.9 = (bf16[64,1152]{1,0:T(8,128)(2,1)S(1)}, bf16[64,1152]{1,0:T(8,128)(2,1)S(1)}, u32[]{:S(2)}, u32[]{:S(2)}) collective-permute-start(bf16[64,1152]{1,0:T(8,128)(2,1)S(1)} %collective-permute-done.5.refs_0_), channel_id=1, source_target_pairs={{0,4},{4,8},{8,12},{12,14},{14,10},{10,6},{6,2},{2,0},{1,5},{5,9},... | collective-permute-start | bytes 442376 | tf_op jit(solution)/shard_map/ppermute | solution.py:68
  18.7 2.6 %collective-permute-done.3.refs_2_ = bf16[64,1152]{1,0:T(8,128)(2,1)S(1)} collective-permute-done((bf16[64,1152]{1,0:T(8,128)(2,1)S(1)}, bf16[64,1152]{1,0:T(8,128)(2,1)S(1)}, u32[]{:S(2)}, u32[]{:S(2)}) %collective-permute-start.3) | collective-permute-done | bytes 147488 | tf_op jit(solution)/shard_map/ppermute | solution.py:68
  21.4 1.9 %collective-permute-start.6 = (bf16[64,1024]{1,0:T(8,128)(2,1)S(1)}, bf16[64,1024]{1,0:T(8,128)(2,1)S(1)}, u32[]{:S(2)}, u32[]{:S(2)}) collective-permute-start(bf16[64,1024]{1,0:T(8,128)(2,1)S(1)} %collective-permute-done.2.refs_1_), channel_id=1, source_target_pairs={{0,4},{4,8},{8,12},{12,14},{14,10},{10,6},{6,2},{2,0},{1,5},{5,9},... | collective-permute-start | bytes 393224 | tf_op jit(solution)/shard_map/ppermute | solution.py:68
  23.3 1.8 %collective-permute-start.13 = (bf16[64,1152]{1,0:T(8,128)(2,1)S(1)}, bf16[64,1152]{1,0:T(8,128)(2,1)S(1)}, u32[]{:S(2)}, u32[]{:S(2)}) collective-permute-start(bf16[64,1152]{1,0:T(8,128)(2,1)S(1)} %collective-permute-done.9.refs_0_), channel_id=1, source_target_pairs={{0,4},{4,8},{8,12},{12,14},{14,10},{10,6},{6,2},{2,0},{1,5},{5,9},... | collective-permute-start | bytes 442376 | tf_op jit(solution)/shard_map/ppermute | solution.py:68
  25.3 1.9 %collective-permute-done.7.refs_2_ = bf16[64,1152]{1,0:T(8,128)(2,1)S(1)} collective-permute-done((bf16[64,1152]{1,0:T(8,128)(2,1)S(1)}, bf16[64,1152]{1,0:T(8,128)(2,1)S(1)}, u32[]{:S(2)}, u32[]{:S(2)}) %collective-permute-start.7) | collective-permute-done | bytes 147488 | tf_op jit(solution)/shard_map/ppermute | solution.py:68
  27.3 1.8 %shard_map.105 = (bf16[1024,1536]{1,0:T(8,128)(2,1)S(1)}, bf16[768,1024]{1,0:T(8,128)(2,1)S(1)}) custom-call(bf16[2,512,384]{2,1,0:T(8,128)(2,1)} %refs_0_.1, bf16[2,512,384]{2,1,0:T(8,128)(2,1)} %refs_1_.1, bf16[2,192,1024]{2,1,0:T(8,128)(2,1)} %refs_2_.3, bf16[3200,384]{1,0:T(8,128)(2,1)S(1)} %collective-permute-done.refs_3_), custom_call_target="tpu_custom_call" | custom-call | bytes 9437184 | tf_op jit(solution)/shard_map/pallas_call | solution.py:270
  32.2 1.6 %collective-permute-start.15 = (bf16[64,1024]{1,0:T(8,128)(2,1)S(1)}, bf16[64,1024]{1,0:T(8,128)(2,1)S(1)}, u32[]{:S(2)}, u32[]{:S(2)}) collective-permute-start(bf16[64,1024]{1,0:T(8,128)(2,1)S(1)} %get-tuple-element.73), channel_id=1, source_target_pairs={{0,4},{4,8},{8,12},{12,14},{14,10},{10,6},{6,2},{2,0},{1,5},{5,9},... | collective-permute-start | bytes 393224 | tf_op jit(solution)/shard_map/ppermute | solution.py:68
  48.2 1.7 %collective-permute-start.27 = (bf16[64,1024]{1,0:T(8,128)(2,1)S(1)}, bf16[64,1024]{1,0:T(8,128)(2,1)S(1)}, u32[]{:S(2)}, u32[]{:S(2)}) collective-permute-start(bf16[64,1024]{1,0:T(8,128)(2,1)S(1)} %shard_map.121), channel_id=1, source_target_pairs={{0,2},{4,0},{8,4},{12,8},{14,12},{10,14},{6,10},{2,6},{1,3},{5,1},... | collective-permute-start | bytes 393224 | tf_op jit(solution)/shard_map/ppermute | solution.py:68
  51.6 2.1 %collective-permute-start.18 = (bf16[64,1024]{1,0:T(8,128)(2,1)S(1)}, bf16[64,1024]{1,0:T(8,128)(2,1)S(1)}, u32[]{:S(2)}, u32[]{:S(2)}) collective-permute-start(bf16[64,1024]{1,0:T(8,128)(2,1)S(1)} %shard_map.114), channel_id=1, source_target_pairs={{0,4},{4,8},{8,12},{12,14},{14,10},{10,6},{6,2},{2,0},{1,5},{5,9},... | collective-permute-start | bytes 393224 | tf_op jit(solution)/shard_map/ppermute | solution.py:68
  54.3 2.1 %collective-permute-start.28 = (bf16[64,1024]{1,0:T(8,128)(2,1)S(1)}, bf16[64,1024]{1,0:T(8,128)(2,1)S(1)}, u32[]{:S(2)}, u32[]{:S(2)}) collective-permute-start(bf16[64,1024]{1,0:T(8,128)(2,1)S(1)} %shard_map.122), channel_id=1, source_target_pairs={{0,2},{4,0},{8,4},{12,8},{14,12},{10,14},{6,10},{2,6},{1,3},{5,1},... | collective-permute-start | bytes 393224 | tf_op jit(solution)/shard_map/ppermute | solution.py:68
  57.9 2.1 %collective-permute-start.29 = (bf16[64,1024]{1,0:T(8,128)(2,1)S(1)}, bf16[64,1024]{1,0:T(8,128)(2,1)S(1)}, u32[]{:S(2)}, u32[]{:S(2)}) collective-permute-start(bf16[64,1024]{1,0:T(8,128)(2,1)S(1)} %shard_map.117.refs_2_), channel_id=1, source_target_pairs={{0,4},{4,8},{8,12},{12,14},{14,10},{10,6},{6,2},{2,0},{1,5},{5,9},... | collective-permute-start | bytes 393224 | tf_op jit(solution)/shard_map/ppermute | solution.py:68
  64.1 2.3 %collective-permute-start.30 = (bf16[64,1024]{1,0:T(8,128)(2,1)S(1)}, bf16[64,1024]{1,0:T(8,128)(2,1)S(1)}, u32[]{:S(2)}, u32[]{:S(2)}) collective-permute-start(bf16[64,1024]{1,0:T(8,128)(2,1)S(1)} %collective-permute-done.29.refs_4_), channel_id=1, source_target_pairs={{0,4},{4,8},{8,12},{12,14},{14,10},{10,6},{6,2},{2,0},{1,5},{5,9},... | collective-permute-start | bytes 393224 | tf_op jit(solution)/shard_map/ppermute | solution.py:68
  69.6 1.6 %collective-permute-start.41 = (bf16[64,1024]{1,0:T(8,128)(2,1)S(1)}, bf16[64,1024]{1,0:T(8,128)(2,1)S(1)}, u32[]{:S(2)}, u32[]{:S(2)}) collective-permute-start(bf16[64,1024]{1,0:T(8,128)(2,1)S(1)} %collective-permute-done.40.refs_6_), channel_id=1, source_target_pairs={{0,2},{4,0},{8,4},{12,8},{14,12},{10,14},{6,10},{2,6},{1,3},{5,1},... | collective-permute-start | bytes 393224 | tf_op jit(solution)/shard_map/ppermute | solution.py:68
  88.1 2.7 %collective-permute-start.46 = (bf16[8,1024]{1,0:T(8,128)(2,1)S(1)}, bf16[8,1024]{1,0:T(8,128)(2,1)S(1)}, u32[]{:S(2)}, u32[]{:S(2)}) collective-permute-start(bf16[8,1024]{1,0:T(8,128)(2,1)S(1)} %shard_map.131.refs_0_), channel_id=1, source_target_pairs={{0,12},{2,14},{4,8},{6,10},{8,4},{10,6},{12,0},{14,2},{1,13},{3,15... | collective-permute-start | bytes 49160 | tf_op jit(solution)/shard_map/ppermute | solution.py:450
  90.8 1.6 %collective-permute-start.44 = (bf16[8,1024]{1,0:T(8,128)(2,1)S(1)}, bf16[8,1024]{1,0:T(8,128)(2,1)S(1)}, u32[]{:S(2)}, u32[]{:S(2)}) collective-permute-start(bf16[8,1024]{1,0:T(8,128)(2,1)S(1)} %shard_map.131.refs_0_), channel_id=1, source_target_pairs={{0,4},{2,6},{4,0},{6,2},{8,12},{10,14},{12,8},{14,10},{1,5},{3,7},... | collective-permute-start | bytes 49160 | tf_op jit(solution)/shard_map/ppermute | solution.py:450
  93.8 1.7 %collective-permute-done.45.refs_2_ = bf16[8,1024]{1,0:T(8,128)(2,1)S(1)} collective-permute-done((bf16[8,1024]{1,0:T(8,128)(2,1)S(1)}, bf16[8,1024]{1,0:T(8,128)(2,1)S(1)}, u32[]{:S(2)}, u32[]{:S(2)}) %collective-permute-start.45) | collective-permute-done | bytes 16416 | tf_op jit(solution)/shard_map/ppermute | solution.py:450
  104.5 1.6 %shard_map.135 = (f32[64,1024]{1,0:T(8,128)S(1)}, f32[64,1024]{1,0:T(8,128)S(1)}, f32[64,1024]{1,0:T(8,128)S(1)}, f32[64,1024]{1,0:T(8,128)S(1)}) custom-call(f32[256,1024]{1,0:T(8,128)S(1)} %get-tuple-element.100.residual_ref, f32[256,128]{1,0:T(8,128)S(1)} %get-tuple-element.101.inv_ref, bf16[256,768]{1,0:T(8,128)(2,1)S(1)} %get-tuple-element.102.gate_save, ...), custom_call_target="tpu_custom_call" | custom-call | flops 1207959552 | bytes 6721536 | tf_op jit(solution)/shard_map/pallas_call | solution.py:29
  110.6 1.6 %shard_map.134 = (f32[64,1024]{1,0:T(8,128)S(1)}, f32[64,1024]{1,0:T(8,128)S(1)}, f32[64,1024]{1,0:T(8,128)S(1)}, f32[64,1024]{1,0:T(8,128)S(1)}) custom-call(f32[256,1024]{1,0:T(8,128)S(1)} %get-tuple-element.95.residual_ref, f32[256,128]{1,0:T(8,128)S(1)} %get-tuple-element.96.inv_ref, bf16[256,768]{1,0:T(8,128)(2,1)S(1)} %get-tuple-element.97.gate_save, ...), custom_call_target="tpu_custom_call" | custom-call | flops 1207959552 | bytes 6721536 | tf_op jit(solution)/shard_map/pallas_call | solution.py:29
  (159 shorter events, 72.3 us)
Async XLA Ops:
  2.6 24.7 %collective-permute-start = (bf16[3200,384]{1,0:T(8,128)(2,1)S(1)}, bf16[3200,384]{1,0:T(8,128)(2,1)S(1)}, u32[]{:S(2)}, u32[]{:S(2)}) collective-permute-start(bf16[3200,384]{1,0:T(8,128)(2,1)S(1)} %get-tuple-element.66), channel_id=1, source_target_pairs={{0,1},{1,0},{2,3},{3,2},{4,5},{5,4},{6,7},{7,6},{8,9},{9,8},{10,11... | collective-permute-start | bytes 7372808 | tf_op jit(solution)/shard_map/ppermute | solution.py:315
  3.1 7.0 %collective-permute-start.1 = (bf16[64,1152]{1,0:T(8,128)(2,1)S(1)}, bf16[64,1152]{1,0:T(8,128)(2,1)S(1)}, u32[]{:S(2)}, u32[]{:S(2)}) collective-permute-start(bf16[64,1152]{1,0:T(8,128)(2,1)S(1)} %get-tuple-element.64.refs_0_), channel_id=1, source_target_pairs={{0,4},{4,8},{8,12},{12,14},{14,10},{10,6},{6,2},{2,0},{1,5},{5,9},... | collective-permute-start | bytes 442376 | tf_op jit(solution)/shard_map/ppermute | solution.py:68
  11.9 6.8 %collective-permute-start.8 = (bf16[64,1024]{1,0:T(8,128)(2,1)S(1)}, bf16[64,1024]{1,0:T(8,128)(2,1)S(1)}, u32[]{:S(2)}, u32[]{:S(2)}) collective-permute-start(bf16[64,1024]{1,0:T(8,128)(2,1)S(1)} %collective-permute-done.4.refs_3_), channel_id=1, source_target_pairs={{0,2},{4,0},{8,4},{12,8},{14,12},{10,14},{6,10},{2,6},{1,3},{5,1},... | collective-permute-start | bytes 393224 | tf_op jit(solution)/shard_map/ppermute | solution.py:68
  12.1 9.1 %collective-permute-start.3 = (bf16[64,1152]{1,0:T(8,128)(2,1)S(1)}, bf16[64,1152]{1,0:T(8,128)(2,1)S(1)}, u32[]{:S(2)}, u32[]{:S(2)}) collective-permute-start(bf16[64,1152]{1,0:T(8,128)(2,1)S(1)} %get-tuple-element.64.refs_0_), channel_id=1, source_target_pairs={{0,2},{4,0},{8,4},{12,8},{14,12},{10,14},{6,10},{2,6},{1,3},{5,1},... | collective-permute-start | bytes 442376 | tf_op jit(solution)/shard_map/ppermute | solution.py:68
  13.9 7.6 %collective-permute-start.2 = (bf16[64,1024]{1,0:T(8,128)(2,1)S(1)}, bf16[64,1024]{1,0:T(8,128)(2,1)S(1)}, u32[]{:S(2)}, u32[]{:S(2)}) collective-permute-start(bf16[64,1024]{1,0:T(8,128)(2,1)S(1)} %get-tuple-element.65.refs_1_), channel_id=1, source_target_pairs={{0,4},{4,8},{8,12},{12,14},{14,10},{10,6},{6,2},{2,0},{1,5},{5,9},... | collective-permute-start | bytes 393224 | tf_op jit(solution)/shard_map/ppermute | solution.py:68
  16.2 7.1 %collective-permute-start.9 = (bf16[64,1152]{1,0:T(8,128)(2,1)S(1)}, bf16[64,1152]{1,0:T(8,128)(2,1)S(1)}, u32[]{:S(2)}, u32[]{:S(2)}) collective-permute-start(bf16[64,1152]{1,0:T(8,128)(2,1)S(1)} %collective-permute-done.5.refs_0_), channel_id=1, source_target_pairs={{0,4},{4,8},{8,12},{12,14},{14,10},{10,6},{6,2},{2,0},{1,5},{5,9},... | collective-permute-start | bytes 442376 | tf_op jit(solution)/shard_map/ppermute | solution.py:68
  21.4 8.2 %collective-permute-start.6 = (bf16[64,1024]{1,0:T(8,128)(2,1)S(1)}, bf16[64,1024]{1,0:T(8,128)(2,1)S(1)}, u32[]{:S(2)}, u32[]{:S(2)}) collective-permute-start(bf16[64,1024]{1,0:T(8,128)(2,1)S(1)} %collective-permute-done.2.refs_1_), channel_id=1, source_target_pairs={{0,4},{4,8},{8,12},{12,14},{14,10},{10,6},{6,2},{2,0},{1,5},{5,9},... | collective-permute-start | bytes 393224 | tf_op jit(solution)/shard_map/ppermute | solution.py:68
  23.3 7.8 %collective-permute-start.13 = (bf16[64,1152]{1,0:T(8,128)(2,1)S(1)}, bf16[64,1152]{1,0:T(8,128)(2,1)S(1)}, u32[]{:S(2)}, u32[]{:S(2)}) collective-permute-start(bf16[64,1152]{1,0:T(8,128)(2,1)S(1)} %collective-permute-done.9.refs_0_), channel_id=1, source_target_pairs={{0,4},{4,8},{8,12},{12,14},{14,10},{10,6},{6,2},{2,0},{1,5},{5,9},... | collective-permute-start | bytes 442376 | tf_op jit(solution)/shard_map/ppermute | solution.py:68
  32.2 6.4 %collective-permute-start.15 = (bf16[64,1024]{1,0:T(8,128)(2,1)S(1)}, bf16[64,1024]{1,0:T(8,128)(2,1)S(1)}, u32[]{:S(2)}, u32[]{:S(2)}) collective-permute-start(bf16[64,1024]{1,0:T(8,128)(2,1)S(1)} %get-tuple-element.73), channel_id=1, source_target_pairs={{0,4},{4,8},{8,12},{12,14},{14,10},{10,6},{6,2},{2,0},{1,5},{5,9},... | collective-permute-start | bytes 393224 | tf_op jit(solution)/shard_map/ppermute | solution.py:68
  33.8 8.0 %collective-permute-start.25 = (bf16[64,1024]{1,0:T(8,128)(2,1)S(1)}, bf16[64,1024]{1,0:T(8,128)(2,1)S(1)}, u32[]{:S(2)}, u32[]{:S(2)}) collective-permute-start(bf16[64,1024]{1,0:T(8,128)(2,1)S(1)} %get-tuple-element.84), channel_id=1, source_target_pairs={{0,2},{4,0},{8,4},{12,8},{14,12},{10,14},{6,10},{2,6},{1,3},{5,1},... | collective-permute-start | bytes 393224 | tf_op jit(solution)/shard_map/ppermute | solution.py:68
  36.3 7.5 %collective-permute-start.19 = (bf16[64,1024]{1,0:T(8,128)(2,1)S(1)}, bf16[64,1024]{1,0:T(8,128)(2,1)S(1)}, u32[]{:S(2)}, u32[]{:S(2)}) collective-permute-start(bf16[64,1024]{1,0:T(8,128)(2,1)S(1)} %get-tuple-element.76), channel_id=1, source_target_pairs={{0,2},{4,0},{8,4},{12,8},{14,12},{10,14},{6,10},{2,6},{1,3},{5,1},... | collective-permute-start | bytes 393224 | tf_op jit(solution)/shard_map/ppermute | solution.py:68
  38.6 6.4 %collective-permute-start.16 = (bf16[64,1024]{1,0:T(8,128)(2,1)S(1)}, bf16[64,1024]{1,0:T(8,128)(2,1)S(1)}, u32[]{:S(2)}, u32[]{:S(2)}) collective-permute-start(bf16[64,1024]{1,0:T(8,128)(2,1)S(1)} %shard_map.112), channel_id=1, source_target_pairs={{0,4},{4,8},{8,12},{12,14},{14,10},{10,6},{6,2},{2,0},{1,5},{5,9},... | collective-permute-start | bytes 393224 | tf_op jit(solution)/shard_map/ppermute | solution.py:68
  40.2 7.5 %collective-permute-start.22 = (bf16[64,1024]{1,0:T(8,128)(2,1)S(1)}, bf16[64,1024]{1,0:T(8,128)(2,1)S(1)}, u32[]{:S(2)}, u32[]{:S(2)}) collective-permute-start(bf16[64,1024]{1,0:T(8,128)(2,1)S(1)} %get-tuple-element.80), channel_id=1, source_target_pairs={{0,4},{4,8},{8,12},{12,14},{14,10},{10,6},{6,2},{2,0},{1,5},{5,9},... | collective-permute-start | bytes 393224 | tf_op jit(solution)/shard_map/ppermute | solution.py:68
  43.9 7.6 %collective-permute-start.20 = (bf16[64,1024]{1,0:T(8,128)(2,1)S(1)}, bf16[64,1024]{1,0:T(8,128)(2,1)S(1)}, u32[]{:S(2)}, u32[]{:S(2)}) collective-permute-start(bf16[64,1024]{1,0:T(8,128)(2,1)S(1)} %shard_map.115), channel_id=1, source_target_pairs={{0,2},{4,0},{8,4},{12,8},{14,12},{10,14},{6,10},{2,6},{1,3},{5,1},... | collective-permute-start | bytes 393224 | tf_op jit(solution)/shard_map/ppermute | solution.py:68
  45.0 6.5 %collective-permute-start.17 = (bf16[64,1024]{1,0:T(8,128)(2,1)S(1)}, bf16[64,1024]{1,0:T(8,128)(2,1)S(1)}, u32[]{:S(2)}, u32[]{:S(2)}) collective-permute-start(bf16[64,1024]{1,0:T(8,128)(2,1)S(1)} %shard_map.113), channel_id=1, source_target_pairs={{0,4},{4,8},{8,12},{12,14},{14,10},{10,6},{6,2},{2,0},{1,5},{5,9},... | collective-permute-start | bytes 393224 | tf_op jit(solution)/shard_map/ppermute | solution.py:68
  54.1 6.5 %collective-permute-start.24 = (bf16[64,1024]{1,0:T(8,128)(2,1)S(1)}, bf16[64,1024]{1,0:T(8,128)(2,1)S(1)}, u32[]{:S(2)}, u32[]{:S(2)}) collective-permute-start(bf16[64,1024]{1,0:T(8,128)(2,1)S(1)} %shard_map.119), channel_id=1, source_target_pairs={{0,4},{4,8},{8,12},{12,14},{14,10},{10,6},{6,2},{2,0},{1,5},{5,9},... | collective-permute-start | bytes 393224 | tf_op jit(solution)/shard_map/ppermute | solution.py:68
  54.3 6.5 %collective-permute-start.28 = (bf16[64,1024]{1,0:T(8,128)(2,1)S(1)}, bf16[64,1024]{1,0:T(8,128)(2,1)S(1)}, u32[]{:S(2)}, u32[]{:S(2)}) collective-permute-start(bf16[64,1024]{1,0:T(8,128)(2,1)S(1)} %shard_map.122), channel_id=1, source_target_pairs={{0,2},{4,0},{8,4},{12,8},{14,12},{10,14},{6,10},{2,6},{1,3},{5,1},... | collective-permute-start | bytes 393224 | tf_op jit(solution)/shard_map/ppermute | solution.py:68
  62.1 7.6 %collective-permute-start.40 = (bf16[64,1024]{1,0:T(8,128)(2,1)S(1)}, bf16[64,1024]{1,0:T(8,128)(2,1)S(1)}, u32[]{:S(2)}, u32[]{:S(2)}) collective-permute-start(bf16[64,1024]{1,0:T(8,128)(2,1)S(1)} %shard_map.117.refs_2_), channel_id=1, source_target_pairs={{0,2},{4,0},{8,4},{12,8},{14,12},{10,14},{6,10},{2,6},{1,3},{5,1},... | collective-permute-start | bytes 393224 | tf_op jit(solution)/shard_map/ppermute | solution.py:68
  63.3 8.0 %collective-permute-start.37 = (bf16[64,1024]{1,0:T(8,128)(2,1)S(1)}, bf16[64,1024]{1,0:T(8,128)(2,1)S(1)}, u32[]{:S(2)}, u32[]{:S(2)}) collective-permute-start(bf16[64,1024]{1,0:T(8,128)(2,1)S(1)} %shard_map.123.refs_3_), channel_id=1, source_target_pairs={{0,4},{4,8},{8,12},{12,14},{14,10},{10,6},{6,2},{2,0},{1,5},{5,9},... | collective-permute-start | bytes 393224 | tf_op jit(solution)/shard_map/ppermute | solution.py:68
  64.1 8.3 %collective-permute-start.30 = (bf16[64,1024]{1,0:T(8,128)(2,1)S(1)}, bf16[64,1024]{1,0:T(8,128)(2,1)S(1)}, u32[]{:S(2)}, u32[]{:S(2)}) collective-permute-start(bf16[64,1024]{1,0:T(8,128)(2,1)S(1)} %collective-permute-done.29.refs_4_), channel_id=1, source_target_pairs={{0,4},{4,8},{8,12},{12,14},{14,10},{10,6},{6,2},{2,0},{1,5},{5,9},... | collective-permute-start | bytes 393224 | tf_op jit(solution)/shard_map/ppermute | solution.py:68
  108.4 7.8 %collective-permute-start.49 = (bf16[64,1024]{1,0:T(8,128)(2,1)S(1)}, bf16[64,1024]{1,0:T(8,128)(2,1)S(1)}, u32[]{:S(2)}, u32[]{:S(2)}) collective-permute-start(bf16[64,1024]{1,0:T(8,128)(2,1)S(1)} %shard_map.139), channel_id=1, source_target_pairs={{0,4},{4,8},{8,12},{12,14},{14,10},{10,6},{6,2},{2,0},{1,5},{5,9},... | collective-permute-start | bytes 393224 | tf_op jit(solution)/shard_map/ppermute | solution.py:68
  109.3 8.0 %collective-permute-start.59 = (bf16[64,1024]{1,0:T(8,128)(2,1)S(1)}, bf16[64,1024]{1,0:T(8,128)(2,1)S(1)}, u32[]{:S(2)}, u32[]{:S(2)}) collective-permute-start(bf16[64,1024]{1,0:T(8,128)(2,1)S(1)} %shard_map.146), channel_id=1, source_target_pairs={{0,2},{4,0},{8,4},{12,8},{14,12},{10,14},{6,10},{2,6},{1,3},{5,1},... | collective-permute-start | bytes 393224 | tf_op jit(solution)/shard_map/ppermute | solution.py:68
  112.6 8.2 %collective-permute-start.53 = (bf16[64,1024]{1,0:T(8,128)(2,1)S(1)}, bf16[64,1024]{1,0:T(8,128)(2,1)S(1)}, u32[]{:S(2)}, u32[]{:S(2)}) collective-permute-start(bf16[64,1024]{1,0:T(8,128)(2,1)S(1)} %shard_map.142), channel_id=1, source_target_pairs={{0,2},{4,0},{8,4},{12,8},{14,12},{10,14},{6,10},{2,6},{1,3},{5,1},... | collective-permute-start | bytes 393224 | tf_op jit(solution)/shard_map/ppermute | solution.py:68
  113.8 7.0 %collective-permute-start.56 = (bf16[64,1024]{1,0:T(8,128)(2,1)S(1)}, bf16[64,1024]{1,0:T(8,128)(2,1)S(1)}, u32[]{:S(2)}, u32[]{:S(2)}) collective-permute-start(bf16[64,1024]{1,0:T(8,128)(2,1)S(1)} %shard_map.144), channel_id=1, source_target_pairs={{0,4},{4,8},{8,12},{12,14},{14,10},{10,6},{6,2},{2,0},{1,5},{5,9},... | collective-permute-start | bytes 393224 | tf_op jit(solution)/shard_map/ppermute | solution.py:68
  (41 other events, 348.5 us)

commit v18 on v17

--- a/solution.py
+++ b/solution.py
@@ -95,14 +95,18 @@
         most = self.half - 1
         top_left = self.send(parts[self.half][0], 1)
         bottom_right = self.send(parts[self.half][1], -1)
-        bottom_left = self.send(parts[most][1], 1)
-        top_right = self.send(parts[-most][0], -1)
+        bottom_left = top_right = None
         for step in range(most, 0, -1):
-            top_left = self.send(add(parts[step][0], top_left), 1)
-            bottom_right = self.send(add(parts[-step][1], bottom_right), -1)
-            if step > 1:
-                bottom_left = self.send(add(parts[step - 1][1], bottom_left), 1)
-                top_right = self.send(add(parts[1 - step][0], top_right), -1)
+            top_sum = add(parts[step][0], top_left)
+            bottom_sum = add(parts[-step][1], bottom_right)
+            top_left, bottom_right = self.send(top_sum, 1), self.send(bottom_sum, -1)
+            if step == most:
+                bottom_left = after(parts[step][1], [top_sum])
+                top_right = after(parts[-step][0], [bottom_sum])
+            else:
+                bottom_left = add(parts[step][1], bottom_left)
+                top_right = add(parts[-step][0], top_right)
+            bottom_left, top_right = self.send(bottom_left, 1), self.send(top_right, -1)
         return (top_left, top_right), (bottom_left, bottom_right)
 
     def part_types(self, distances):
@@ -131,14 +135,22 @@
         out_ref[pl.ds(i * rows, rows), :] = (own[...] + arrived).astype(BF16)
 
 
+PIECES = 4
+
+
 class Copies:
     def __init__(self, sems):
         self.sems, self.started = sems, []
 
-    def start(self, source, target):
-        copy = pltpu.make_async_copy(source, target, self.sems.at[len(self.started)])
-        copy.start()
-        self.started.append(copy)
+    def start(self, source, target, pieces=1):
+        assert source.shape[0] % (16 * pieces) == 0 or pieces == 1
+        rows = source.shape[0] // pieces
+        for i in range(pieces):
+            some = pl.ds(i * rows, rows)
+            sem = self.sems.at[len(self.started)]
+            copy = pltpu.make_async_copy(source.at[some], target.at[some], sem)
+            copy.start()
+            self.started.append(copy)
 
     def wait(self):
         for copy in self.started:
@@ -170,7 +182,7 @@
         hidden_dim = shards[0].shape[2]
         packed_rows, places = strips(shards[0].shape, shards[2].shape)
         packed_shape = (packed_rows, hidden_dim)
-        count = sum(len(pair) + len(downs) for pair, downs in places)
+        count = sum(PIECES * len(pair) + len(downs) for pair, downs in places)
 
     def kernel(*refs):
         ids_hbm, scores_hbm, tokens_hbm, *shards_hbm = refs[: len(inputs)]
@@ -184,7 +196,7 @@
         for local, (pair, downs) in enumerate(places):
             out_ref = packed_refs[0]
             for source, (row, some) in zip(shards_hbm, pair):
-                copies.start(source.at[local], out_ref.at[pl.ds(row, some), :])
+                copies.start(source.at[local], out_ref.at[pl.ds(row, some), :], PIECES)
             for row, some, begin, width in downs:
                 source = shards_hbm[2].at[local, :, pl.ds(begin, width)]
                 copies.start(source, out_ref.at[pl.ds(row, some), pl.ds(0, width)])
@@ -249,22 +261,23 @@
 
         for local in range(local_experts):
             for is_up, source in enumerate((gate_hbm, up_hbm)):
-                copies.start(source.at[local], wide_at(mine, local, is_up))
-            copies.start(down_hbm.at[local], down_at(mine, local, 0, feature_dim))
+                copies.start(source.at[local], wide_at(mine, local, is_up), PIECES)
+            copies.start(down_hbm.at[local], down_at(mine, local, 0, feature_dim), PIECES)
         if paired:
             for local, (pair, downs) in enumerate(places):
                 for is_up, (row, some) in enumerate(pair):
-                    copies.start(rest[0].at[pl.ds(row, some), :], wide_at(1 - mine, local, is_up))
+                    source = rest[0].at[pl.ds(row, some), :]
+                    copies.start(source, wide_at(1 - mine, local, is_up), PIECES)
                 for row, some, begin, cols in downs:
                     source = rest[0].at[pl.ds(row, some), pl.ds(0, cols)]
                     copies.start(source, down_at(1 - mine, local, begin, cols))
         copies.wait()
 
     shards = [pltpu.with_memory_space_constraint(w, pltpu.HBM) for w in shards]
-    count = 3 * local_experts
+    count = 3 * PIECES * local_experts
     specs = [pl.BlockSpec(memory_space=pl.ANY)] * 3
     if paired:
-        count += sum(len(pair) + len(downs) for pair, downs in places)
+        count += sum(PIECES * len(pair) + len(downs) for pair, downs in places)
         specs.append(pl.BlockSpec(memory_space=pltpu.VMEM))
         shards.append(pltpu.with_memory_space_constraint(packed, pltpu.VMEM))
     return pl.pallas_call(

time: 123 us -> 126 us (1.024)
  waiting for transfers between devices: 30 us -> 37.4 us
  starting transfers between devices: 68.4 us -> 63.6 us
    ppermute x56, waiting for transfers between devices: 26.3 us -> 32.9 us  [send(): return lax.ppermute(value, 'expert', pairs)]
    ppermute x56, starting transfers between devices: 62.2 us -> 58.4 us  [send(): return lax.ppermute(value, 'expert', pairs)]
  transfers between devices with their start and end apart: 62 -> 62, of which waited for: 30 -> 33; matrix products, arithmetic and copies ran while one was open for 1% -> 1% of each run, Pallas kernels for 15% -> 14%
where the time goes in v18:
time: 126 us
  starting transfers between devices  63.6 us (50%)
  waiting for transfers between devices  37.4 us (30%)
  Pallas kernels  22.4 us (18%)
  matrix products  1.71 us (1%)
    ppermute x56, starting transfers between devices, send(): return lax.ppermute(value, 'expert', pairs)  58.4 us
    ppermute x56, waiting for transfers between devices, send(): return lax.ppermute(value, 'expert', pairs)  32.9 us
    pallas_call x41, Pallas kernels, call(): pl.pallas_call(kernel, out_shape=[pltpu.VMEM(shape, dtype) for shape, dty...  17.4 us
    ppermute x4, starting transfers between devices, body(): terms.append(lax.ppermute(grad_rows, 'expert', pairs))  4.76 us
    ppermute x4, waiting for transfers between devices, body(): terms.append(lax.ppermute(grad_rows, 'expert', pairs))  4.51 us
  transfers between devices with their start and end apart: 62, of which 33 were waited for; matrix products, arithmetic and copies ran while one was open for 1% of the time, Pallas kernels for 14%

profile of v18, /device:TPU:0, one launch (start us, length us, event | category | flops | bytes accessed | tf_op | source)
XLA Modules:
  0.0 126.3 jit_solution(8610235890842586331)
XLA Ops:
  0.6 2.1 %shard_map.104 = (bf16[64,1152]{1,0:T(8,128)(2,1)S(1)}, bf16[64,1024]{1,0:T(8,128)(2,1)S(1)}, bf16[3200,384]{1,0:T(8,128)(2,1)S(1)}) custom-call(s32[8,128]{1,0:T(8,128)} %bitcast.19, f32[8,128]{1,0:T(8,128)} %bitcast.20, bf16[128,1024]{1,0:T(8,128)(2,1)} %refs_2_.2, bf16[2,512,384]{2,1,0:T(8,128)(2,1)} %refs_0_.1, bf16[2,512,384]{2,1,0:T(8,128)(2,1)} %refs_1_.1, ...), custom_call_target="tpu_custom_call" | custom-call | tf_op jit(solution)/shard_map/pallas_call | solution.py:227
  3.3 2.6 %collective-permute-start.1 = (bf16[64,1152]{1,0:T(8,128)(2,1)S(1)}, bf16[64,1152]{1,0:T(8,128)(2,1)S(1)}, u32[]{:S(2)}, u32[]{:S(2)}) collective-permute-start(bf16[64,1152]{1,0:T(8,128)(2,1)S(1)} %get-tuple-element.64.refs_0_), channel_id=1, source_target_pairs={{0,4},{4,8},{8,12},{12,14},{14,10},{10,6},{6,2},{2,0},{1,5},{5,9},... | collective-permute-start | bytes 442376 | tf_op jit(solution)/shard_map/ppermute | solution.py:68
  5.9 4.4 %collective-permute-done.1.refs_0_ = bf16[64,1152]{1,0:T(8,128)(2,1)S(1)} collective-permute-done((bf16[64,1152]{1,0:T(8,128)(2,1)S(1)}, bf16[64,1152]{1,0:T(8,128)(2,1)S(1)}, u32[]{:S(2)}, u32[]{:S(2)}) %collective-permute-start.1) | collective-permute-done | bytes 147488 | tf_op jit(solution)/shard_map/ppermute | solution.py:68
  10.3 1.8 %collective-permute-start.5 = (bf16[64,1152]{1,0:T(8,128)(2,1)S(1)}, bf16[64,1152]{1,0:T(8,128)(2,1)S(1)}, u32[]{:S(2)}, u32[]{:S(2)}) collective-permute-start(bf16[64,1152]{1,0:T(8,128)(2,1)S(1)} %collective-permute-done.1.refs_0_), channel_id=1, source_target_pairs={{0,4},{4,8},{8,12},{12,14},{14,10},{10,6},{6,2},{2,0},{1,5},{5,9},... | collective-permute-start | bytes 442376 | tf_op jit(solution)/shard_map/ppermute | solution.py:68
  12.3 1.7 %collective-permute-start.3 = (bf16[64,1152]{1,0:T(8,128)(2,1)S(1)}, bf16[64,1152]{1,0:T(8,128)(2,1)S(1)}, u32[]{:S(2)}, u32[]{:S(2)}) collective-permute-start(bf16[64,1152]{1,0:T(8,128)(2,1)S(1)} %get-tuple-element.64.refs_0_), channel_id=1, source_target_pairs={{0,2},{4,0},{8,4},{12,8},{14,12},{10,14},{6,10},{2,6},{1,3},{5,1},... | collective-permute-start | bytes 442376 | tf_op jit(solution)/shard_map/ppermute | solution.py:68
  14.3 2.0 %collective-permute-done.5.refs_0_ = bf16[64,1152]{1,0:T(8,128)(2,1)S(1)} collective-permute-done((bf16[64,1152]{1,0:T(8,128)(2,1)S(1)}, bf16[64,1152]{1,0:T(8,128)(2,1)S(1)}, u32[]{:S(2)}, u32[]{:S(2)}) %collective-permute-start.5) | collective-permute-done | bytes 147488 | tf_op jit(solution)/shard_map/ppermute | solution.py:68
  16.4 2.5 %collective-permute-start.9 = (bf16[64,1152]{1,0:T(8,128)(2,1)S(1)}, bf16[64,1152]{1,0:T(8,128)(2,1)S(1)}, u32[]{:S(2)}, u32[]{:S(2)}) collective-permute-start(bf16[64,1152]{1,0:T(8,128)(2,1)S(1)} %collective-permute-done.5.refs_0_), channel_id=1, source_target_pairs={{0,4},{4,8},{8,12},{12,14},{14,10},{10,6},{6,2},{2,0},{1,5},{5,9},... | collective-permute-start | bytes 442376 | tf_op jit(solution)/shard_map/ppermute | solution.py:68
  18.9 2.6 %collective-permute-done.3.refs_2_ = bf16[64,1152]{1,0:T(8,128)(2,1)S(1)} collective-permute-done((bf16[64,1152]{1,0:T(8,128)(2,1)S(1)}, bf16[64,1152]{1,0:T(8,128)(2,1)S(1)}, u32[]{:S(2)}, u32[]{:S(2)}) %collective-permute-start.3) | collective-permute-done | bytes 147488 | tf_op jit(solution)/shard_map/ppermute | solution.py:68
  21.6 1.9 %collective-permute-start.6 = (bf16[64,1024]{1,0:T(8,128)(2,1)S(1)}, bf16[64,1024]{1,0:T(8,128)(2,1)S(1)}, u32[]{:S(2)}, u32[]{:S(2)}) collective-permute-start(bf16[64,1024]{1,0:T(8,128)(2,1)S(1)} %collective-permute-done.2.refs_1_), channel_id=1, source_target_pairs={{0,4},{4,8},{8,12},{12,14},{14,10},{10,6},{6,2},{2,0},{1,5},{5,9},... | collective-permute-start | bytes 393224 | tf_op jit(solution)/shard_map/ppermute | solution.py:68
  23.4 1.8 %collective-permute-start.13 = (bf16[64,1152]{1,0:T(8,128)(2,1)S(1)}, bf16[64,1152]{1,0:T(8,128)(2,1)S(1)}, u32[]{:S(2)}, u32[]{:S(2)}) collective-permute-start(bf16[64,1152]{1,0:T(8,128)(2,1)S(1)} %collective-permute-done.9.refs_0_), channel_id=1, source_target_pairs={{0,4},{4,8},{8,12},{12,14},{14,10},{10,6},{6,2},{2,0},{1,5},{5,9},... | collective-permute-start | bytes 442376 | tf_op jit(solution)/shard_map/ppermute | solution.py:68
  25.5 1.9 %collective-permute-done.7.refs_2_ = bf16[64,1152]{1,0:T(8,128)(2,1)S(1)} collective-permute-done((bf16[64,1152]{1,0:T(8,128)(2,1)S(1)}, bf16[64,1152]{1,0:T(8,128)(2,1)S(1)}, u32[]{:S(2)}, u32[]{:S(2)}) %collective-permute-start.7) | collective-permute-done | bytes 147488 | tf_op jit(solution)/shard_map/ppermute | solution.py:68
  27.4 2.1 %shard_map.105 = (bf16[1024,1536]{1,0:T(8,128)(2,1)S(1)}, bf16[768,1024]{1,0:T(8,128)(2,1)S(1)}) custom-call(bf16[2,512,384]{2,1,0:T(8,128)(2,1)} %refs_0_.1, bf16[2,512,384]{2,1,0:T(8,128)(2,1)} %refs_1_.1, bf16[2,192,1024]{2,1,0:T(8,128)(2,1)} %refs_2_.3, bf16[3200,384]{1,0:T(8,128)(2,1)S(1)} %collective-permute-done.refs_3_), custom_call_target="tpu_custom_call" | custom-call | bytes 9437184 | tf_op jit(solution)/shard_map/pallas_call | solution.py:283
  36.7 1.9 %collective-permute-done.19.arrived_ref = bf16[64,1024]{1,0:T(8,128)(2,1)S(1)} collective-permute-done((bf16[64,1024]{1,0:T(8,128)(2,1)S(1)}, bf16[64,1024]{1,0:T(8,128)(2,1)S(1)}, u32[]{:S(2)}, u32[]{:S(2)}) %collective-permute-start.19) | collective-permute-done | bytes 131104 | tf_op jit(solution)/shard_map/ppermute | solution.py:68
  45.4 1.7 %collective-permute-start.17 = (bf16[64,1024]{1,0:T(8,128)(2,1)S(1)}, bf16[64,1024]{1,0:T(8,128)(2,1)S(1)}, u32[]{:S(2)}, u32[]{:S(2)}) collective-permute-start(bf16[64,1024]{1,0:T(8,128)(2,1)S(1)} %shard_map.113), channel_id=1, source_target_pairs={{0,4},{4,8},{8,12},{12,14},{14,10},{10,6},{6,2},{2,0},{1,5},{5,9},... | collective-permute-start | bytes 393224 | tf_op jit(solution)/shard_map/ppermute | solution.py:68
  47.2 2.2 %collective-permute-start.24 = (bf16[64,1024]{1,0:T(8,128)(2,1)S(1)}, bf16[64,1024]{1,0:T(8,128)(2,1)S(1)}, u32[]{:S(2)}, u32[]{:S(2)}) collective-permute-start(bf16[64,1024]{1,0:T(8,128)(2,1)S(1)} %shard_map.121), channel_id=1, source_target_pairs={{0,4},{4,8},{8,12},{12,14},{14,10},{10,6},{6,2},{2,0},{1,5},{5,9},... | collective-permute-start | bytes 393224 | tf_op jit(solution)/shard_map/ppermute | solution.py:68
  62.6 1.9 %collective-permute-start.40 = (bf16[64,1024]{1,0:T(8,128)(2,1)S(1)}, bf16[64,1024]{1,0:T(8,128)(2,1)S(1)}, u32[]{:S(2)}, u32[]{:S(2)}) collective-permute-start(bf16[64,1024]{1,0:T(8,128)(2,1)S(1)} %shard_map.119.refs_2_), channel_id=1, source_target_pairs={{0,2},{4,0},{8,4},{12,8},{14,12},{10,14},{6,10},{2,6},{1,3},{5,1},... | collective-permute-start | bytes 393224 | tf_op jit(solution)/shard_map/ppermute | solution.py:68
  66.1 2.0 %collective-permute-done.33.refs_7_ = bf16[64,1024]{1,0:T(8,128)(2,1)S(1)} collective-permute-done((bf16[64,1024]{1,0:T(8,128)(2,1)S(1)}, bf16[64,1024]{1,0:T(8,128)(2,1)S(1)}, u32[]{:S(2)}, u32[]{:S(2)}) %collective-permute-start.33) | collective-permute-done | bytes 131104 | tf_op jit(solution)/shard_map/ppermute | solution.py:68
  69.0 1.9 %collective-permute-done.40.refs_6_ = bf16[64,1024]{1,0:T(8,128)(2,1)S(1)} collective-permute-done((bf16[64,1024]{1,0:T(8,128)(2,1)S(1)}, bf16[64,1024]{1,0:T(8,128)(2,1)S(1)}, u32[]{:S(2)}, u32[]{:S(2)}) %collective-permute-start.40) | collective-permute-done | bytes 131104 | tf_op jit(solution)/shard_map/ppermute | solution.py:68
  73.0 1.6 %collective-permute-start.31 = (bf16[64,1024]{1,0:T(8,128)(2,1)S(1)}, bf16[64,1024]{1,0:T(8,128)(2,1)S(1)}, u32[]{:S(2)}, u32[]{:S(2)}) collective-permute-start(bf16[64,1024]{1,0:T(8,128)(2,1)S(1)} %collective-permute-done.30.refs_4_), channel_id=1, source_target_pairs={{0,4},{4,8},{8,12},{12,14},{14,10},{10,6},{6,2},{2,0},{1,5},{5,9},... | collective-permute-start | bytes 393224 | tf_op jit(solution)/shard_map/ppermute | solution.py:68
  83.3 1.7 %collective-permute-done.36.refs_3_ = bf16[64,1024]{1,0:T(8,128)(2,1)S(1)} collective-permute-done((bf16[64,1024]{1,0:T(8,128)(2,1)S(1)}, bf16[64,1024]{1,0:T(8,128)(2,1)S(1)}, u32[]{:S(2)}, u32[]{:S(2)}) %collective-permute-start.36) | collective-permute-done | bytes 131104 | tf_op jit(solution)/shard_map/ppermute | solution.py:68
  89.4 2.4 %collective-permute-start.46 = (bf16[8,1024]{1,0:T(8,128)(2,1)S(1)}, bf16[8,1024]{1,0:T(8,128)(2,1)S(1)}, u32[]{:S(2)}, u32[]{:S(2)}) collective-permute-start(bf16[8,1024]{1,0:T(8,128)(2,1)S(1)} %shard_map.133.refs_0_), channel_id=1, source_target_pairs={{0,12},{2,14},{4,8},{6,10},{8,4},{10,6},{12,0},{14,2},{1,13},{3,15... | collective-permute-start | bytes 49160 | tf_op jit(solution)/shard_map/ppermute | solution.py:463
  99.9 1.6 %shard_map.138 = (bf16[64,1024]{1,0:T(8,128)(2,1)S(1)}, f32[64,1024]{1,0:T(8,128)S(1)}, f32[64,1024]{1,0:T(8,128)S(1)}, bf16[64,1024]{1,0:T(8,128)(2,1)S(1)}) custom-call(f32[256,1024]{1,0:T(8,128)S(1)} %get-tuple-element.105.residual_ref, f32[256,128]{1,0:T(8,128)S(1)} %get-tuple-element.106.inv_ref, bf16[256,768]{1,0:T(8,128)(2,1)S(1)} %get-tuple-element.107.gate_save, ...), custom_call_target="tpu_custom_call" | custom-call | flops 1207959552 | bytes 6721536 | tf_op jit(solution)/shard_map/pallas_call | solution.py:29
  107.1 1.6 %shard_map.137 = (f32[64,1024]{1,0:T(8,128)S(1)}, f32[64,1024]{1,0:T(8,128)S(1)}, f32[64,1024]{1,0:T(8,128)S(1)}, f32[64,1024]{1,0:T(8,128)S(1)}) custom-call(f32[256,1024]{1,0:T(8,128)S(1)} %get-tuple-element.100.residual_ref, f32[256,128]{1,0:T(8,128)S(1)} %get-tuple-element.101.inv_ref, bf16[256,768]{1,0:T(8,128)(2,1)S(1)} %get-tuple-element.102.gate_save, ...), custom_call_target="tpu_custom_call" | custom-call | flops 1207959552 | bytes 6721536 | tf_op jit(solution)/shard_map/pallas_call | solution.py:29
  113.8 1.6 %shard_map.136 = (f32[64,1024]{1,0:T(8,128)S(1)}, f32[64,1024]{1,0:T(8,128)S(1)}, f32[64,1024]{1,0:T(8,128)S(1)}, f32[64,1024]{1,0:T(8,128)S(1)}) custom-call(f32[256,1024]{1,0:T(8,128)S(1)} %get-tuple-element.95.residual_ref, f32[256,128]{1,0:T(8,128)S(1)} %get-tuple-element.96.inv_ref, bf16[256,768]{1,0:T(8,128)(2,1)S(1)} %get-tuple-element.97.gate_save, ...), custom_call_target="tpu_custom_call" | custom-call | flops 1207959552 | bytes 6721536 | tf_op jit(solution)/shard_map/pallas_call | solution.py:29
  (163 shorter events, 75.7 us)
Async XLA Ops:
  2.7 24.7 %collective-permute-start = (bf16[3200,384]{1,0:T(8,128)(2,1)S(1)}, bf16[3200,384]{1,0:T(8,128)(2,1)S(1)}, u32[]{:S(2)}, u32[]{:S(2)}) collective-permute-start(bf16[3200,384]{1,0:T(8,128)(2,1)S(1)} %get-tuple-element.66), channel_id=1, source_target_pairs={{0,1},{1,0},{2,3},{3,2},{4,5},{5,4},{6,7},{7,6},{8,9},{9,8},{10,11... | collective-permute-start | bytes 7372808 | tf_op jit(solution)/shard_map/ppermute | solution.py:328
  3.3 7.0 %collective-permute-start.1 = (bf16[64,1152]{1,0:T(8,128)(2,1)S(1)}, bf16[64,1152]{1,0:T(8,128)(2,1)S(1)}, u32[]{:S(2)}, u32[]{:S(2)}) collective-permute-start(bf16[64,1152]{1,0:T(8,128)(2,1)S(1)} %get-tuple-element.64.refs_0_), channel_id=1, source_target_pairs={{0,4},{4,8},{8,12},{12,14},{14,10},{10,6},{6,2},{2,0},{1,5},{5,9},... | collective-permute-start | bytes 442376 | tf_op jit(solution)/shard_map/ppermute | solution.py:68
  12.1 6.8 %collective-permute-start.8 = (bf16[64,1024]{1,0:T(8,128)(2,1)S(1)}, bf16[64,1024]{1,0:T(8,128)(2,1)S(1)}, u32[]{:S(2)}, u32[]{:S(2)}) collective-permute-start(bf16[64,1024]{1,0:T(8,128)(2,1)S(1)} %collective-permute-done.4.refs_3_), channel_id=1, source_target_pairs={{0,2},{4,0},{8,4},{12,8},{14,12},{10,14},{6,10},{2,6},{1,3},{5,1},... | collective-permute-start | bytes 393224 | tf_op jit(solution)/shard_map/ppermute | solution.py:68
  12.3 9.1 %collective-permute-start.3 = (bf16[64,1152]{1,0:T(8,128)(2,1)S(1)}, bf16[64,1152]{1,0:T(8,128)(2,1)S(1)}, u32[]{:S(2)}, u32[]{:S(2)}) collective-permute-start(bf16[64,1152]{1,0:T(8,128)(2,1)S(1)} %get-tuple-element.64.refs_0_), channel_id=1, source_target_pairs={{0,2},{4,0},{8,4},{12,8},{14,12},{10,14},{6,10},{2,6},{1,3},{5,1},... | collective-permute-start | bytes 442376 | tf_op jit(solution)/shard_map/ppermute | solution.py:68
  14.0 7.6 %collective-permute-start.2 = (bf16[64,1024]{1,0:T(8,128)(2,1)S(1)}, bf16[64,1024]{1,0:T(8,128)(2,1)S(1)}, u32[]{:S(2)}, u32[]{:S(2)}) collective-permute-start(bf16[64,1024]{1,0:T(8,128)(2,1)S(1)} %get-tuple-element.65.refs_1_), channel_id=1, source_target_pairs={{0,4},{4,8},{8,12},{12,14},{14,10},{10,6},{6,2},{2,0},{1,5},{5,9},... | collective-permute-start | bytes 393224 | tf_op jit(solution)/shard_map/ppermute | solution.py:68
  16.4 7.1 %collective-permute-start.9 = (bf16[64,1152]{1,0:T(8,128)(2,1)S(1)}, bf16[64,1152]{1,0:T(8,128)(2,1)S(1)}, u32[]{:S(2)}, u32[]{:S(2)}) collective-permute-start(bf16[64,1152]{1,0:T(8,128)(2,1)S(1)} %collective-permute-done.5.refs_0_), channel_id=1, source_target_pairs={{0,4},{4,8},{8,12},{12,14},{14,10},{10,6},{6,2},{2,0},{1,5},{5,9},... | collective-permute-start | bytes 442376 | tf_op jit(solution)/shard_map/ppermute | solution.py:68
  21.6 8.6 %collective-permute-start.6 = (bf16[64,1024]{1,0:T(8,128)(2,1)S(1)}, bf16[64,1024]{1,0:T(8,128)(2,1)S(1)}, u32[]{:S(2)}, u32[]{:S(2)}) collective-permute-start(bf16[64,1024]{1,0:T(8,128)(2,1)S(1)} %collective-permute-done.2.refs_1_), channel_id=1, source_target_pairs={{0,4},{4,8},{8,12},{12,14},{14,10},{10,6},{6,2},{2,0},{1,5},{5,9},... | collective-permute-start | bytes 393224 | tf_op jit(solution)/shard_map/ppermute | solution.py:68
  23.4 8.2 %collective-permute-start.13 = (bf16[64,1152]{1,0:T(8,128)(2,1)S(1)}, bf16[64,1152]{1,0:T(8,128)(2,1)S(1)}, u32[]{:S(2)}, u32[]{:S(2)}) collective-permute-start(bf16[64,1152]{1,0:T(8,128)(2,1)S(1)} %collective-permute-done.9.refs_0_), channel_id=1, source_target_pairs={{0,4},{4,8},{8,12},{12,14},{14,10},{10,6},{6,2},{2,0},{1,5},{5,9},... | collective-permute-start | bytes 442376 | tf_op jit(solution)/shard_map/ppermute | solution.py:68
  42.8 6.6 %collective-permute-start.26 = (bf16[64,1024]{1,0:T(8,128)(2,1)S(1)}, bf16[64,1024]{1,0:T(8,128)(2,1)S(1)}, u32[]{:S(2)}, u32[]{:S(2)}) collective-permute-start(bf16[64,1024]{1,0:T(8,128)(2,1)S(1)} %shard_map.115.refs_1_), channel_id=1, source_target_pairs={{0,2},{4,0},{8,4},{12,8},{14,12},{10,14},{6,10},{2,6},{1,3},{5,1},... | collective-permute-start | bytes 393224 | tf_op jit(solution)/shard_map/ppermute | solution.py:68
  45.4 6.7 %collective-permute-start.17 = (bf16[64,1024]{1,0:T(8,128)(2,1)S(1)}, bf16[64,1024]{1,0:T(8,128)(2,1)S(1)}, u32[]{:S(2)}, u32[]{:S(2)}) collective-permute-start(bf16[64,1024]{1,0:T(8,128)(2,1)S(1)} %shard_map.113), channel_id=1, source_target_pairs={{0,4},{4,8},{8,12},{12,14},{14,10},{10,6},{6,2},{2,0},{1,5},{5,9},... | collective-permute-start | bytes 393224 | tf_op jit(solution)/shard_map/ppermute | solution.py:68
  47.2 6.8 %collective-permute-start.24 = (bf16[64,1024]{1,0:T(8,128)(2,1)S(1)}, bf16[64,1024]{1,0:T(8,128)(2,1)S(1)}, u32[]{:S(2)}, u32[]{:S(2)}) collective-permute-start(bf16[64,1024]{1,0:T(8,128)(2,1)S(1)} %shard_map.121), channel_id=1, source_target_pairs={{0,4},{4,8},{8,12},{12,14},{14,10},{10,6},{6,2},{2,0},{1,5},{5,9},... | collective-permute-start | bytes 393224 | tf_op jit(solution)/shard_map/ppermute | solution.py:68
  54.1 7.0 %collective-permute-start.25 = (bf16[64,1024]{1,0:T(8,128)(2,1)S(1)}, bf16[64,1024]{1,0:T(8,128)(2,1)S(1)}, u32[]{:S(2)}, u32[]{:S(2)}) collective-permute-start(bf16[64,1024]{1,0:T(8,128)(2,1)S(1)} %shard_map.122), channel_id=1, source_target_pairs={{0,4},{4,8},{8,12},{12,14},{14,10},{10,6},{6,2},{2,0},{1,5},{5,9},... | collective-permute-start | bytes 393224 | tf_op jit(solution)/shard_map/ppermute | solution.py:68
  62.6 8.3 %collective-permute-start.40 = (bf16[64,1024]{1,0:T(8,128)(2,1)S(1)}, bf16[64,1024]{1,0:T(8,128)(2,1)S(1)}, u32[]{:S(2)}, u32[]{:S(2)}) collective-permute-start(bf16[64,1024]{1,0:T(8,128)(2,1)S(1)} %shard_map.119.refs_2_), channel_id=1, source_target_pairs={{0,2},{4,0},{8,4},{12,8},{14,12},{10,14},{6,10},{2,6},{1,3},{5,1},... | collective-permute-start | bytes 393224 | tf_op jit(solution)/shard_map/ppermute | solution.py:68
  64.5 7.3 %collective-permute-start.37 = (bf16[64,1024]{1,0:T(8,128)(2,1)S(1)}, bf16[64,1024]{1,0:T(8,128)(2,1)S(1)}, u32[]{:S(2)}, u32[]{:S(2)}) collective-permute-start(bf16[64,1024]{1,0:T(8,128)(2,1)S(1)} %shard_map.125.refs_3_), channel_id=1, source_target_pairs={{0,4},{4,8},{8,12},{12,14},{14,10},{10,6},{6,2},{2,0},{1,5},{5,9},... | collective-permute-start | bytes 393224 | tf_op jit(solution)/shard_map/ppermute | solution.py:68
  64.8 8.2 %collective-permute-start.30 = (bf16[64,1024]{1,0:T(8,128)(2,1)S(1)}, bf16[64,1024]{1,0:T(8,128)(2,1)S(1)}, u32[]{:S(2)}, u32[]{:S(2)}) collective-permute-start(bf16[64,1024]{1,0:T(8,128)(2,1)S(1)} %collective-permute-done.29.refs_4_), channel_id=1, source_target_pairs={{0,4},{4,8},{8,12},{12,14},{14,10},{10,6},{6,2},{2,0},{1,5},{5,9},... | collective-permute-start | bytes 393224 | tf_op jit(solution)/shard_map/ppermute | solution.py:68
  68.1 6.5 %collective-permute-start.34 = (bf16[64,1024]{1,0:T(8,128)(2,1)S(1)}, bf16[64,1024]{1,0:T(8,128)(2,1)S(1)}, u32[]{:S(2)}, u32[]{:S(2)}) collective-permute-start(bf16[64,1024]{1,0:T(8,128)(2,1)S(1)} %collective-permute-done.33.refs_7_), channel_id=1, source_target_pairs={{0,2},{4,0},{8,4},{12,8},{14,12},{10,14},{6,10},{2,6},{1,3},{5,1},... | collective-permute-start | bytes 393224 | tf_op jit(solution)/shard_map/ppermute | solution.py:68
  98.7 6.5 %collective-permute-start.51 = (bf16[64,1024]{1,0:T(8,128)(2,1)S(1)}, bf16[64,1024]{1,0:T(8,128)(2,1)S(1)}, u32[]{:S(2)}, u32[]{:S(2)}) collective-permute-start(bf16[64,1024]{1,0:T(8,128)(2,1)S(1)} %get-tuple-element.119), channel_id=1, source_target_pairs={{0,2},{4,0},{8,4},{12,8},{14,12},{10,14},{6,10},{2,6},{1,3},{5,1},... | collective-permute-start | bytes 393224 | tf_op jit(solution)/shard_map/ppermute | solution.py:68
  102.9 7.4 %collective-permute-start.48 = (bf16[64,1024]{1,0:T(8,128)(2,1)S(1)}, bf16[64,1024]{1,0:T(8,128)(2,1)S(1)}, u32[]{:S(2)}, u32[]{:S(2)}) collective-permute-start(bf16[64,1024]{1,0:T(8,128)(2,1)S(1)} %shard_map.140.refs_1_), channel_id=1, source_target_pairs={{0,4},{4,8},{8,12},{12,14},{14,10},{10,6},{6,2},{2,0},{1,5},{5,9},... | collective-permute-start | bytes 393224 | tf_op jit(solution)/shard_map/ppermute | solution.py:68
  105.3 7.2 %collective-permute-start.58 = (bf16[64,1024]{1,0:T(8,128)(2,1)S(1)}, bf16[64,1024]{1,0:T(8,128)(2,1)S(1)}, u32[]{:S(2)}, u32[]{:S(2)}) collective-permute-start(bf16[64,1024]{1,0:T(8,128)(2,1)S(1)} %shard_map.143.refs_1_), channel_id=1, source_target_pairs={{0,2},{4,0},{8,4},{12,8},{14,12},{10,14},{6,10},{2,6},{1,3},{5,1},... | collective-permute-start | bytes 393224 | tf_op jit(solution)/shard_map/ppermute | solution.py:68
  107.1 6.6 %collective-permute-start.61 = (bf16[8,1274]{1,0:T(8,128)(2,1)S(1)}, bf16[8,1274]{1,0:T(8,128)(2,1)S(1)}, u32[]{:S(2)}, u32[]{:S(2)}) collective-permute-start(bf16[8,1274]{1,0:T(8,128)(2,1)S(1)} %pad_maximum_fusion.1), channel_id=1, source_target_pairs={{0,1},{1,0},{2,3},{3,2},{4,5},{5,4},{6,7},{7,6},{8,9},{9,8},{10,11... | collective-permute-start | bytes 61160 | tf_op jit(solution)/shard_map/ppermute | solution.py:474
  110.3 7.8 %collective-permute-start.49 = (bf16[64,1024]{1,0:T(8,128)(2,1)S(1)}, bf16[64,1024]{1,0:T(8,128)(2,1)S(1)}, u32[]{:S(2)}, u32[]{:S(2)}) collective-permute-start(bf16[64,1024]{1,0:T(8,128)(2,1)S(1)} %shard_map.141), channel_id=1, source_target_pairs={{0,4},{4,8},{8,12},{12,14},{14,10},{10,6},{6,2},{2,0},{1,5},{5,9},... | collective-permute-start | bytes 393224 | tf_op jit(solution)/shard_map/ppermute | solution.py:68
  111.8 7.2 %collective-permute-start.53 = (bf16[64,1024]{1,0:T(8,128)(2,1)S(1)}, bf16[64,1024]{1,0:T(8,128)(2,1)S(1)}, u32[]{:S(2)}, u32[]{:S(2)}) collective-permute-start(bf16[64,1024]{1,0:T(8,128)(2,1)S(1)} %shard_map.145), channel_id=1, source_target_pairs={{0,2},{4,0},{8,4},{12,8},{14,12},{10,14},{6,10},{2,6},{1,3},{5,1},... | collective-permute-start | bytes 393224 | tf_op jit(solution)/shard_map/ppermute | solution.py:68
  112.5 7.8 %collective-permute-start.59 = (bf16[64,1024]{1,0:T(8,128)(2,1)S(1)}, bf16[64,1024]{1,0:T(8,128)(2,1)S(1)}, u32[]{:S(2)}, u32[]{:S(2)}) collective-permute-start(bf16[64,1024]{1,0:T(8,128)(2,1)S(1)} %shard_map.150), channel_id=1, source_target_pairs={{0,2},{4,0},{8,4},{12,8},{14,12},{10,14},{6,10},{2,6},{1,3},{5,1},... | collective-permute-start | bytes 393224 | tf_op jit(solution)/shard_map/ppermute | solution.py:68
  115.8 7.2 %collective-permute-start.57 = (bf16[64,1024]{1,0:T(8,128)(2,1)S(1)}, bf16[64,1024]{1,0:T(8,128)(2,1)S(1)}, u32[]{:S(2)}, u32[]{:S(2)}) collective-permute-start(bf16[64,1024]{1,0:T(8,128)(2,1)S(1)} %shard_map.149), channel_id=1, source_target_pairs={{0,4},{4,8},{8,12},{12,14},{14,10},{10,6},{6,2},{2,0},{1,5},{5,9},... | collective-permute-start | bytes 393224 | tf_op jit(solution)/shard_map/ppermute | solution.py:68
  (41 other events, 345.8 us)

commit v19 on v17

--- a/solution.py
+++ b/solution.py
@@ -56,6 +56,8 @@
         self.count = expert_count
         self.half = expert_count // 2
         self.snake = group_count == 2
+        self.groups = group_count
+        self.token = None
         if self.snake:
             self.order = list(range(0, expert_count, 2)) + list(range(expert_count - 1, 0, -2))
         else:
@@ -66,6 +68,13 @@
             (self.order[i], self.order[(i + distance) % self.count]) for i in range(self.count)
         ]
         return lax.ppermute(value, "expert", pairs)
+
+    def in_step(self, value, behind):
+        if self.groups != 2:
+            return value
+        token = after(self.token, [behind])
+        self.token = lax.ppermute(token, "group", [(0, 1), (1, 0)])
+        return after(value, [self.token])
 
     def device_at(self, distance):
         here = lax.axis_index("expert")
@@ -84,6 +93,8 @@
         for step in range(1, self.half):
             if guard is not None and step == self.half - 1:
                 top_right = after(top_right, [guard])
+            if step > 1:
+                top_right = self.in_step(top_right, top_left)
             top_left = self.send(top_left, 1)
             top_right = self.send(top_right, -1)
             bottom_left = self.send(bottom_left, 1)
@@ -91,18 +102,22 @@
             use((-step, step), (top_left, bottom_left, top_right, bottom_right))
         use((self.half,), (self.send(top_left, 1), self.send(bottom_right, -1)))
 
-    def scatter(self, parts):
+    def scatter(self, parts, paced=False):
         most = self.half - 1
         top_left = self.send(parts[self.half][0], 1)
         bottom_right = self.send(parts[self.half][1], -1)
         bottom_left = self.send(parts[most][1], 1)
         top_right = self.send(parts[-most][0], -1)
         for step in range(most, 0, -1):
-            top_left = self.send(add(parts[step][0], top_left), 1)
+            top_sum = add(parts[step][0], top_left)
+            top_left = self.send(top_sum, 1)
             bottom_right = self.send(add(parts[-step][1], bottom_right), -1)
             if step > 1:
                 bottom_left = self.send(add(parts[step - 1][1], bottom_left), 1)
-                top_right = self.send(add(parts[1 - step][0], top_right), -1)
+                top_right = add(parts[1 - step][0], top_right)
+                if paced:
+                    top_right = self.in_step(top_right, top_sum)
+                top_right = self.send(top_right, -1)
         return (top_left, top_right), (bottom_left, bottom_right)
 
     def part_types(self, distances):
@@ -377,6 +392,7 @@
         saved_at[distances] = result[:2]
         keep_parts(part_at, distances, result[2:])
 
+    ring.token = norm_gain[: 8 * LANES].reshape(8, LANES)
     ring.gather(top, bottom, hold, wide)
     for distances in tokens_at:
         forward(distances)
@@ -384,7 +400,7 @@
     half_shape = (mid, feature_dim)
     moe_top, moe_bottom = [
         call(sum_kernel, [(half_shape, BF16)], own, *arrived)[0]
-        for own, arrived in zip(part_at[0], ring.scatter(part_at))
+        for own, arrived in zip(part_at[0], ring.scatter(part_at, paced=True))
     ]
 
     norm_at, mean_at = {}, {}

time: 123 us -> 126 us (1.024)
  waiting for transfers between devices: 30 us -> 34.1 us
  starting transfers between devices: 68.4 us -> 66.8 us
    ppermute x56, waiting for transfers between devices: 26.3 us -> 29.7 us  [send(): return lax.ppermute(value, 'expert', pairs)]
    ppermute x56, starting transfers between devices: 62.2 us -> 60.4 us  [send(): return lax.ppermute(value, 'expert', pairs)]
  transfers between devices with their start and end apart: 62 -> 68, of which waited for: 30 -> 24; matrix products, arithmetic and copies ran while one was open for 1% -> 1% of each run, Pallas kernels for 15% -> 14%
where the time goes in v19:
time: 126 us
  starting transfers between devices  66.8 us (53%)
  waiting for transfers between devices  34.1 us (27%)
  Pallas kernels  21.9 us (17%)
  matrix products  1.71 us (1%)
    ppermute x56, starting transfers between devices, send(): return lax.ppermute(value, 'expert', pairs)  60.4 us
    ppermute x56, waiting for transfers between devices, send(): return lax.ppermute(value, 'expert', pairs)  29.7 us
    pallas_call x41, Pallas kernels, call(): pl.pallas_call(kernel, out_shape=[pltpu.VMEM(shape, dtype) for shape, dty...  17.4 us
    ppermute x4, starting transfers between devices, body(): terms.append(lax.ppermute(grad_rows, 'expert', pairs))  5.85 us
    ppermute x4, waiting for transfers between devices, body(): terms.append(lax.ppermute(grad_rows, 'expert', pairs))  3.27 us
  transfers between devices with their start and end apart: 68, of which 24 were waited for; matrix products, arithmetic and copies ran while one was open for 1% of the time, Pallas kernels for 14%

profile of v19, /device:TPU:0, one launch (start us, length us, event | category | flops | bytes accessed | tf_op | source)
XLA Modules:
  0.0 125.7 jit_solution(10494879686310960347)
XLA Ops:
  0.7 1.9 %shard_map.104 = (bf16[64,1152]{1,0:T(8,128)(2,1)S(1)}, bf16[64,1024]{1,0:T(8,128)(2,1)S(1)}, bf16[3200,384]{1,0:T(8,128)(2,1)S(1)}) custom-call(s32[8,128]{1,0:T(8,128)} %bitcast.21, f32[8,128]{1,0:T(8,128)} %bitcast.22, bf16[128,1024]{1,0:T(8,128)(2,1)} %refs_2_.2, bf16[2,512,384]{2,1,0:T(8,128)(2,1)} %refs_0_.1, bf16[2,512,384]{2,1,0:T(8,128)(2,1)} %refs_1_.1, ...), custom_call_target="tpu_custom_call" | custom-call | tf_op jit(solution)/shard_map/pallas_call | solution.py:230
  3.1 2.6 %collective-permute-start.1 = (bf16[64,1152]{1,0:T(8,128)(2,1)S(1)}, bf16[64,1152]{1,0:T(8,128)(2,1)S(1)}, u32[]{:S(2)}, u32[]{:S(2)}) collective-permute-start(bf16[64,1152]{1,0:T(8,128)(2,1)S(1)} %get-tuple-element.64.refs_0_), channel_id=1, source_target_pairs={{0,4},{4,8},{8,12},{12,14},{14,10},{10,6},{6,2},{2,0},{1,5},{5,9},... | collective-permute-start | bytes 442376 | tf_op jit(solution)/shard_map/ppermute | solution.py:70
  5.7 4.4 %collective-permute-done.1.refs_0_.refs_1_ = bf16[64,1152]{1,0:T(8,128)(2,1)S(1)} collective-permute-done((bf16[64,1152]{1,0:T(8,128)(2,1)S(1)}, bf16[64,1152]{1,0:T(8,128)(2,1)S(1)}, u32[]{:S(2)}, u32[]{:S(2)}) %collective-permute-start.1) | collective-permute-done | bytes 147488 | tf_op jit(solution)/shard_map/ppermute | solution.py:70
  10.1 1.8 %collective-permute-start.5 = (bf16[64,1152]{1,0:T(8,128)(2,1)S(1)}, bf16[64,1152]{1,0:T(8,128)(2,1)S(1)}, u32[]{:S(2)}, u32[]{:S(2)}) collective-permute-start(bf16[64,1152]{1,0:T(8,128)(2,1)S(1)} %collective-permute-done.1.refs_0_.refs_1_), channel_id=1, source_target_pairs={{0,4},{4,8},{8,12},{12,14},{14,10},{10,6},{6,2},{2,0},{1,5},{5,9},... | collective-permute-start | bytes 442376 | tf_op jit(solution)/shard_map/ppermute | solution.py:70
  14.2 2.0 %collective-permute-done.5.refs_0_.refs_1_ = bf16[64,1152]{1,0:T(8,128)(2,1)S(1)} collective-permute-done((bf16[64,1152]{1,0:T(8,128)(2,1)S(1)}, bf16[64,1152]{1,0:T(8,128)(2,1)S(1)}, u32[]{:S(2)}, u32[]{:S(2)}) %collective-permute-start.5) | collective-permute-done | bytes 147488 | tf_op jit(solution)/shard_map/ppermute | solution.py:70
  16.2 2.5 %collective-permute-start.10 = (bf16[64,1152]{1,0:T(8,128)(2,1)S(1)}, bf16[64,1152]{1,0:T(8,128)(2,1)S(1)}, u32[]{:S(2)}, u32[]{:S(2)}) collective-permute-start(bf16[64,1152]{1,0:T(8,128)(2,1)S(1)} %collective-permute-done.5.refs_0_.refs_1_), channel_id=1, source_target_pairs={{0,4},{4,8},{8,12},{12,14},{14,10},{10,6},{6,2},{2,0},{1,5},{5,9},... | collective-permute-start | bytes 442376 | tf_op jit(solution)/shard_map/ppermute | solution.py:70
  18.7 2.5 %collective-permute-done.3.refs_2_ = bf16[64,1152]{1,0:T(8,128)(2,1)S(1)} collective-permute-done((bf16[64,1152]{1,0:T(8,128)(2,1)S(1)}, bf16[64,1152]{1,0:T(8,128)(2,1)S(1)}, u32[]{:S(2)}, u32[]{:S(2)}) %collective-permute-start.3) | collective-permute-done | bytes 147488 | tf_op jit(solution)/shard_map/ppermute | solution.py:70
  22.6 1.9 %collective-permute-start.6 = (bf16[64,1024]{1,0:T(8,128)(2,1)S(1)}, bf16[64,1024]{1,0:T(8,128)(2,1)S(1)}, u32[]{:S(2)}, u32[]{:S(2)}) collective-permute-start(bf16[64,1024]{1,0:T(8,128)(2,1)S(1)} %collective-permute-done.2.refs_1_), channel_id=1, source_target_pairs={{0,4},{4,8},{8,12},{12,14},{14,10},{10,6},{6,2},{2,0},{1,5},{5,9},... | collective-permute-start | bytes 393224 | tf_op jit(solution)/shard_map/ppermute | solution.py:70
  26.5 2.2 %collective-permute-done.8.refs_2_ = bf16[64,1152]{1,0:T(8,128)(2,1)S(1)} collective-permute-done((bf16[64,1152]{1,0:T(8,128)(2,1)S(1)}, bf16[64,1152]{1,0:T(8,128)(2,1)S(1)}, u32[]{:S(2)}, u32[]{:S(2)}) %collective-permute-start.8) | collective-permute-done | bytes 147488 | tf_op jit(solution)/shard_map/ppermute | solution.py:70
  28.7 1.8 %shard_map.105 = (bf16[1024,1536]{1,0:T(8,128)(2,1)S(1)}, bf16[768,1024]{1,0:T(8,128)(2,1)S(1)}) custom-call(bf16[2,512,384]{2,1,0:T(8,128)(2,1)} %refs_0_.1, bf16[2,512,384]{2,1,0:T(8,128)(2,1)} %refs_1_.1, bf16[2,192,1024]{2,1,0:T(8,128)(2,1)} %refs_2_.3, bf16[3200,384]{1,0:T(8,128)(2,1)S(1)} %collective-permute-done.refs_3_), custom_call_target="tpu_custom_call" | custom-call | bytes 9437184 | tf_op jit(solution)/shard_map/pallas_call | solution.py:285
  30.7 1.9 %collective-permute-start.11 = (bf16[64,1024]{1,0:T(8,128)(2,1)S(1)}, bf16[64,1024]{1,0:T(8,128)(2,1)S(1)}, u32[]{:S(2)}, u32[]{:S(2)}) collective-permute-start(bf16[64,1024]{1,0:T(8,128)(2,1)S(1)} %collective-permute-done.6.refs_1_), channel_id=1, source_target_pairs={{0,4},{4,8},{8,12},{12,14},{14,10},{10,6},{6,2},{2,0},{1,5},{5,9},... | collective-permute-start | bytes 393224 | tf_op jit(solution)/shard_map/ppermute | solution.py:70
  38.7 2.1 %collective-permute-start.21 = (bf16[64,1024]{1,0:T(8,128)(2,1)S(1)}, bf16[64,1024]{1,0:T(8,128)(2,1)S(1)}, u32[]{:S(2)}, u32[]{:S(2)}) collective-permute-start(bf16[64,1024]{1,0:T(8,128)(2,1)S(1)} %get-tuple-element.76), channel_id=1, source_target_pairs={{0,2},{4,0},{8,4},{12,8},{14,12},{10,14},{6,10},{2,6},{1,3},{5,1},... | collective-permute-start | bytes 393224 | tf_op jit(solution)/shard_map/ppermute | solution.py:70
  44.8 2.2 %collective-permute-start.23 = (bf16[64,1024]{1,0:T(8,128)(2,1)S(1)}, bf16[64,1024]{1,0:T(8,128)(2,1)S(1)}, u32[]{:S(2)}, u32[]{:S(2)}) collective-permute-start(bf16[64,1024]{1,0:T(8,128)(2,1)S(1)} %shard_map.121), channel_id=1, source_target_pairs={{0,2},{4,0},{8,4},{12,8},{14,12},{10,14},{6,10},{2,6},{1,3},{5,1},... | collective-permute-start | bytes 393224 | tf_op jit(solution)/shard_map/ppermute | solution.py:70
  51.5 2.0 %collective-permute-start.25 = (bf16[64,1024]{1,0:T(8,128)(2,1)S(1)}, bf16[64,1024]{1,0:T(8,128)(2,1)S(1)}, u32[]{:S(2)}, u32[]{:S(2)}) collective-permute-start(bf16[64,1024]{1,0:T(8,128)(2,1)S(1)} %shard_map.124), channel_id=1, source_target_pairs={{0,2},{4,0},{8,4},{12,8},{14,12},{10,14},{6,10},{2,6},{1,3},{5,1},... | collective-permute-start | bytes 393224 | tf_op jit(solution)/shard_map/ppermute | solution.py:70
  55.7 1.8 %collective-permute-start.32 = (bf16[64,1024]{1,0:T(8,128)(2,1)S(1)}, bf16[64,1024]{1,0:T(8,128)(2,1)S(1)}, u32[]{:S(2)}, u32[]{:S(2)}) collective-permute-start(bf16[64,1024]{1,0:T(8,128)(2,1)S(1)} %shard_map.130), channel_id=1, source_target_pairs={{0,2},{4,0},{8,4},{12,8},{14,12},{10,14},{6,10},{2,6},{1,3},{5,1},... | collective-permute-start | bytes 393224 | tf_op jit(solution)/shard_map/ppermute | solution.py:70
  60.5 2.2 %collective-permute-done.28.refs_1_ = bf16[64,1024]{1,0:T(8,128)(2,1)S(1)} collective-permute-done((bf16[64,1024]{1,0:T(8,128)(2,1)S(1)}, bf16[64,1024]{1,0:T(8,128)(2,1)S(1)}, u32[]{:S(2)}, u32[]{:S(2)}) %collective-permute-start.28) | collective-permute-done | bytes 131104 | tf_op jit(solution)/shard_map/ppermute | solution.py:70
  82.2 2.0 %collective-permute-done.48.refs_6_ = bf16[64,1024]{1,0:T(8,128)(2,1)S(1)} collective-permute-done((bf16[64,1024]{1,0:T(8,128)(2,1)S(1)}, bf16[64,1024]{1,0:T(8,128)(2,1)S(1)}, u32[]{:S(2)}, u32[]{:S(2)}) %collective-permute-start.48) | collective-permute-done | bytes 131104 | tf_op jit(solution)/shard_map/ppermute | solution.py:70
  90.2 2.5 %collective-permute-start.52 = (bf16[8,1024]{1,0:T(8,128)(2,1)S(1)}, bf16[8,1024]{1,0:T(8,128)(2,1)S(1)}, u32[]{:S(2)}, u32[]{:S(2)}) collective-permute-start(bf16[8,1024]{1,0:T(8,128)(2,1)S(1)} %shard_map.143.refs_0_), channel_id=1, source_target_pairs={{0,12},{2,14},{4,8},{6,10},{8,4},{10,6},{12,0},{14,2},{1,13},{3,15... | collective-permute-start | bytes 49160 | tf_op jit(solution)/shard_map/ppermute | solution.py:466
  92.7 1.9 %collective-permute-start.50 = (bf16[8,1024]{1,0:T(8,128)(2,1)S(1)}, bf16[8,1024]{1,0:T(8,128)(2,1)S(1)}, u32[]{:S(2)}, u32[]{:S(2)}) collective-permute-start(bf16[8,1024]{1,0:T(8,128)(2,1)S(1)} %shard_map.143.refs_0_), channel_id=1, source_target_pairs={{0,4},{2,6},{4,0},{6,2},{8,12},{10,14},{12,8},{14,10},{1,5},{3,7},... | collective-permute-start | bytes 49160 | tf_op jit(solution)/shard_map/ppermute | solution.py:466
  102.1 1.9 %collective-permute-start.57 = (bf16[64,1024]{1,0:T(8,128)(2,1)S(1)}, bf16[64,1024]{1,0:T(8,128)(2,1)S(1)}, u32[]{:S(2)}, u32[]{:S(2)}) collective-permute-start(bf16[64,1024]{1,0:T(8,128)(2,1)S(1)} %get-tuple-element.117), channel_id=1, source_target_pairs={{0,2},{4,0},{8,4},{12,8},{14,12},{10,14},{6,10},{2,6},{1,3},{5,1},... | collective-permute-start | bytes 393224 | tf_op jit(solution)/shard_map/ppermute | solution.py:70
  108.7 1.9 %collective-permute-start.58 = (bf16[64,1024]{1,0:T(8,128)(2,1)S(1)}, bf16[64,1024]{1,0:T(8,128)(2,1)S(1)}, u32[]{:S(2)}, u32[]{:S(2)}) collective-permute-start(bf16[64,1024]{1,0:T(8,128)(2,1)S(1)} %shard_map.153), channel_id=1, source_target_pairs={{0,2},{4,0},{8,4},{12,8},{14,12},{10,14},{6,10},{2,6},{1,3},{5,1},... | collective-permute-start | bytes 393224 | tf_op jit(solution)/shard_map/ppermute | solution.py:70
  115.1 1.9 %collective-permute-start.59 = (bf16[64,1024]{1,0:T(8,128)(2,1)S(1)}, bf16[64,1024]{1,0:T(8,128)(2,1)S(1)}, u32[]{:S(2)}, u32[]{:S(2)}) collective-permute-start(bf16[64,1024]{1,0:T(8,128)(2,1)S(1)} %shard_map.154), channel_id=1, source_target_pairs={{0,2},{4,0},{8,4},{12,8},{14,12},{10,14},{6,10},{2,6},{1,3},{5,1},... | collective-permute-start | bytes 393224 | tf_op jit(solution)/shard_map/ppermute | solution.py:70
  117.3 2.2 %collective-permute-done.55.arrived_ref = bf16[64,1024]{1,0:T(8,128)(2,1)S(1)} collective-permute-done((bf16[64,1024]{1,0:T(8,128)(2,1)S(1)}, bf16[64,1024]{1,0:T(8,128)(2,1)S(1)}, u32[]{:S(2)}, u32[]{:S(2)}) %collective-permute-start.55) | collective-permute-done | bytes 131104 | tf_op jit(solution)/shard_map/ppermute | solution.py:70
  119.9 1.8 %collective-permute-start.66 = (bf16[64,1024]{1,0:T(8,128)(2,1)S(1)}, bf16[64,1024]{1,0:T(8,128)(2,1)S(1)}, u32[]{:S(2)}, u32[]{:S(2)}) collective-permute-start(bf16[64,1024]{1,0:T(8,128)(2,1)S(1)} %shard_map.159), channel_id=1, source_target_pairs={{0,2},{4,0},{8,4},{12,8},{14,12},{10,14},{6,10},{2,6},{1,3},{5,1},... | collective-permute-start | bytes 393224 | tf_op jit(solution)/shard_map/ppermute | solution.py:70
  (185 shorter events, 72.7 us)
Async XLA Ops:
  2.6 26.1 %collective-permute-start = (bf16[3200,384]{1,0:T(8,128)(2,1)S(1)}, bf16[3200,384]{1,0:T(8,128)(2,1)S(1)}, u32[]{:S(2)}, u32[]{:S(2)}) collective-permute-start(bf16[3200,384]{1,0:T(8,128)(2,1)S(1)} %get-tuple-element.66), channel_id=1, source_target_pairs={{0,1},{1,0},{2,3},{3,2},{4,5},{5,4},{6,7},{7,6},{8,9},{9,8},{10,11... | collective-permute-start | bytes 7372808 | tf_op jit(solution)/shard_map/ppermute | solution.py:330
  3.1 7.0 %collective-permute-start.1 = (bf16[64,1152]{1,0:T(8,128)(2,1)S(1)}, bf16[64,1152]{1,0:T(8,128)(2,1)S(1)}, u32[]{:S(2)}, u32[]{:S(2)}) collective-permute-start(bf16[64,1152]{1,0:T(8,128)(2,1)S(1)} %get-tuple-element.64.refs_0_), channel_id=1, source_target_pairs={{0,4},{4,8},{8,12},{12,14},{14,10},{10,6},{6,2},{2,0},{1,5},{5,9},... | collective-permute-start | bytes 442376 | tf_op jit(solution)/shard_map/ppermute | solution.py:70
  11.9 6.8 %collective-permute-start.9 = (bf16[64,1024]{1,0:T(8,128)(2,1)S(1)}, bf16[64,1024]{1,0:T(8,128)(2,1)S(1)}, u32[]{:S(2)}, u32[]{:S(2)}) collective-permute-start(bf16[64,1024]{1,0:T(8,128)(2,1)S(1)} %collective-permute-done.4.refs_3_), channel_id=1, source_target_pairs={{0,2},{4,0},{8,4},{12,8},{14,12},{10,14},{6,10},{2,6},{1,3},{5,1},... | collective-permute-start | bytes 393224 | tf_op jit(solution)/shard_map/ppermute | solution.py:70
  12.1 9.1 %collective-permute-start.3 = (bf16[64,1152]{1,0:T(8,128)(2,1)S(1)}, bf16[64,1152]{1,0:T(8,128)(2,1)S(1)}, u32[]{:S(2)}, u32[]{:S(2)}) collective-permute-start(bf16[64,1152]{1,0:T(8,128)(2,1)S(1)} %get-tuple-element.64.refs_0_), channel_id=1, source_target_pairs={{0,2},{4,0},{8,4},{12,8},{14,12},{10,14},{6,10},{2,6},{1,3},{5,1},... | collective-permute-start | bytes 442376 | tf_op jit(solution)/shard_map/ppermute | solution.py:70
  13.9 8.7 %collective-permute-start.2 = (bf16[64,1024]{1,0:T(8,128)(2,1)S(1)}, bf16[64,1024]{1,0:T(8,128)(2,1)S(1)}, u32[]{:S(2)}, u32[]{:S(2)}) collective-permute-start(bf16[64,1024]{1,0:T(8,128)(2,1)S(1)} %get-tuple-element.65.refs_1_), channel_id=1, source_target_pairs={{0,4},{4,8},{8,12},{12,14},{14,10},{10,6},{6,2},{2,0},{1,5},{5,9},... | collective-permute-start | bytes 393224 | tf_op jit(solution)/shard_map/ppermute | solution.py:70
  16.2 8.3 %collective-permute-start.10 = (bf16[64,1152]{1,0:T(8,128)(2,1)S(1)}, bf16[64,1152]{1,0:T(8,128)(2,1)S(1)}, u32[]{:S(2)}, u32[]{:S(2)}) collective-permute-start(bf16[64,1152]{1,0:T(8,128)(2,1)S(1)} %collective-permute-done.5.refs_0_.refs_1_), channel_id=1, source_target_pairs={{0,4},{4,8},{8,12},{12,14},{14,10},{10,6},{6,2},{2,0},{1,5},{5,9},... | collective-permute-start | bytes 442376 | tf_op jit(solution)/shard_map/ppermute | solution.py:70
  18.7 7.3 %collective-permute-start.14 = (bf16[64,1024]{1,0:T(8,128)(2,1)S(1)}, bf16[64,1024]{1,0:T(8,128)(2,1)S(1)}, u32[]{:S(2)}, u32[]{:S(2)}) collective-permute-start(bf16[64,1024]{1,0:T(8,128)(2,1)S(1)} %collective-permute-done.9.refs_3_), channel_id=1, source_target_pairs={{0,2},{4,0},{8,4},{12,8},{14,12},{10,14},{6,10},{2,6},{1,3},{5,1},... | collective-permute-start | bytes 393224 | tf_op jit(solution)/shard_map/ppermute | solution.py:70
  22.6 8.1 %collective-permute-start.6 = (bf16[64,1024]{1,0:T(8,128)(2,1)S(1)}, bf16[64,1024]{1,0:T(8,128)(2,1)S(1)}, u32[]{:S(2)}, u32[]{:S(2)}) collective-permute-start(bf16[64,1024]{1,0:T(8,128)(2,1)S(1)} %collective-permute-done.2.refs_1_), channel_id=1, source_target_pairs={{0,4},{4,8},{8,12},{12,14},{14,10},{10,6},{6,2},{2,0},{1,5},{5,9},... | collective-permute-start | bytes 393224 | tf_op jit(solution)/shard_map/ppermute | solution.py:70
  24.5 8.1 %collective-permute-start.15 = (bf16[64,1152]{1,0:T(8,128)(2,1)S(1)}, bf16[64,1152]{1,0:T(8,128)(2,1)S(1)}, u32[]{:S(2)}, u32[]{:S(2)}) collective-permute-start(bf16[64,1152]{1,0:T(8,128)(2,1)S(1)} %collective-permute-done.10.refs_0_), channel_id=1, source_target_pairs={{0,4},{4,8},{8,12},{12,14},{14,10},{10,6},{6,2},{2,0},{1,5},{5,9},... | collective-permute-start | bytes 442376 | tf_op jit(solution)/shard_map/ppermute | solution.py:70
  30.5 6.7 %collective-permute-start.13 = (bf16[64,1152]{1,0:T(8,128)(2,1)S(1)}, bf16[64,1152]{1,0:T(8,128)(2,1)S(1)}, u32[]{:S(2)}, u32[]{:S(2)}) collective-permute-start(bf16[64,1152]{1,0:T(8,128)(2,1)S(1)} %shard_map.113), channel_id=1, source_target_pairs={{0,2},{4,0},{8,4},{12,8},{14,12},{10,14},{6,10},{2,6},{1,3},{5,1},... | collective-permute-start | bytes 442376 | tf_op jit(solution)/shard_map/ppermute | solution.py:70
  33.6 7.3 %collective-permute-start.17 = (bf16[64,1024]{1,0:T(8,128)(2,1)S(1)}, bf16[64,1024]{1,0:T(8,128)(2,1)S(1)}, u32[]{:S(2)}, u32[]{:S(2)}) collective-permute-start(bf16[64,1024]{1,0:T(8,128)(2,1)S(1)} %get-tuple-element.73), channel_id=1, source_target_pairs={{0,4},{4,8},{8,12},{12,14},{14,10},{10,6},{6,2},{2,0},{1,5},{5,9},... | collective-permute-start | bytes 393224 | tf_op jit(solution)/shard_map/ppermute | solution.py:70
  35.2 7.5 %collective-permute-start.29 = (bf16[64,1024]{1,0:T(8,128)(2,1)S(1)}, bf16[64,1024]{1,0:T(8,128)(2,1)S(1)}, u32[]{:S(2)}, u32[]{:S(2)}) collective-permute-start(bf16[64,1024]{1,0:T(8,128)(2,1)S(1)} %get-tuple-element.84), channel_id=1, source_target_pairs={{0,2},{4,0},{8,4},{12,8},{14,12},{10,14},{6,10},{2,6},{1,3},{5,1},... | collective-permute-start | bytes 393224 | tf_op jit(solution)/shard_map/ppermute | solution.py:70
  44.8 6.6 %collective-permute-start.23 = (bf16[64,1024]{1,0:T(8,128)(2,1)S(1)}, bf16[64,1024]{1,0:T(8,128)(2,1)S(1)}, u32[]{:S(2)}, u32[]{:S(2)}) collective-permute-start(bf16[64,1024]{1,0:T(8,128)(2,1)S(1)} %shard_map.121), channel_id=1, source_target_pairs={{0,2},{4,0},{8,4},{12,8},{14,12},{10,14},{6,10},{2,6},{1,3},{5,1},... | collective-permute-start | bytes 393224 | tf_op jit(solution)/shard_map/ppermute | solution.py:70
  47.7 7.5 %collective-permute-start.27 = (bf16[64,1024]{1,0:T(8,128)(2,1)S(1)}, bf16[64,1024]{1,0:T(8,128)(2,1)S(1)}, u32[]{:S(2)}, u32[]{:S(2)}) collective-permute-start(bf16[64,1024]{1,0:T(8,128)(2,1)S(1)} %shard_map.126), channel_id=1, source_target_pairs={{0,4},{4,8},{8,12},{12,14},{14,10},{10,6},{6,2},{2,0},{1,5},{5,9},... | collective-permute-start | bytes 393224 | tf_op jit(solution)/shard_map/ppermute | solution.py:70
  51.5 7.0 %collective-permute-start.25 = (bf16[64,1024]{1,0:T(8,128)(2,1)S(1)}, bf16[64,1024]{1,0:T(8,128)(2,1)S(1)}, u32[]{:S(2)}, u32[]{:S(2)}) collective-permute-start(bf16[64,1024]{1,0:T(8,128)(2,1)S(1)} %shard_map.124), channel_id=1, source_target_pairs={{0,2},{4,0},{8,4},{12,8},{14,12},{10,14},{6,10},{2,6},{1,3},{5,1},... | collective-permute-start | bytes 393224 | tf_op jit(solution)/shard_map/ppermute | solution.py:70
  55.3 7.4 %collective-permute-start.28 = (bf16[64,1024]{1,0:T(8,128)(2,1)S(1)}, bf16[64,1024]{1,0:T(8,128)(2,1)S(1)}, u32[]{:S(2)}, u32[]{:S(2)}) collective-permute-start(bf16[64,1024]{1,0:T(8,128)(2,1)S(1)} %shard_map.127), channel_id=1, source_target_pairs={{0,4},{4,8},{8,12},{12,14},{14,10},{10,6},{6,2},{2,0},{1,5},{5,9},... | collective-permute-start | bytes 393224 | tf_op jit(solution)/shard_map/ppermute | solution.py:70
  55.7 7.0 %collective-permute-start.32 = (bf16[64,1024]{1,0:T(8,128)(2,1)S(1)}, bf16[64,1024]{1,0:T(8,128)(2,1)S(1)}, u32[]{:S(2)}, u32[]{:S(2)}) collective-permute-start(bf16[64,1024]{1,0:T(8,128)(2,1)S(1)} %shard_map.130), channel_id=1, source_target_pairs={{0,2},{4,0},{8,4},{12,8},{14,12},{10,14},{6,10},{2,6},{1,3},{5,1},... | collective-permute-start | bytes 393224 | tf_op jit(solution)/shard_map/ppermute | solution.py:70
  72.6 6.7 %collective-permute-start.35 = (bf16[64,1024]{1,0:T(8,128)(2,1)S(1)}, bf16[64,1024]{1,0:T(8,128)(2,1)S(1)}, u32[]{:S(2)}, u32[]{:S(2)}) collective-permute-start(bf16[64,1024]{1,0:T(8,128)(2,1)S(1)} %collective-permute-done.34.refs_1_.refs_4_), channel_id=1, source_target_pairs={{0,4},{4,8},{8,12},{12,14},{14,10},{10,6},{6,2},{2,0},{1,5},{5,9},... | collective-permute-start | bytes 393224 | tf_op jit(solution)/shard_map/ppermute | solution.py:70
  102.1 6.6 %collective-permute-start.57 = (bf16[64,1024]{1,0:T(8,128)(2,1)S(1)}, bf16[64,1024]{1,0:T(8,128)(2,1)S(1)}, u32[]{:S(2)}, u32[]{:S(2)}) collective-permute-start(bf16[64,1024]{1,0:T(8,128)(2,1)S(1)} %get-tuple-element.117), channel_id=1, source_target_pairs={{0,2},{4,0},{8,4},{12,8},{14,12},{10,14},{6,10},{2,6},{1,3},{5,1},... | collective-permute-start | bytes 393224 | tf_op jit(solution)/shard_map/ppermute | solution.py:70
  104.0 6.7 %collective-permute-start.60 = (bf16[64,1024]{1,0:T(8,128)(2,1)S(1)}, bf16[64,1024]{1,0:T(8,128)(2,1)S(1)}, u32[]{:S(2)}, u32[]{:S(2)}) collective-permute-start(bf16[64,1024]{1,0:T(8,128)(2,1)S(1)} %get-tuple-element.121), channel_id=1, source_target_pairs={{0,4},{4,8},{8,12},{12,14},{14,10},{10,6},{6,2},{2,0},{1,5},{5,9},... | collective-permute-start | bytes 393224 | tf_op jit(solution)/shard_map/ppermute | solution.py:70
  110.9 8.6 %collective-permute-start.55 = (bf16[64,1024]{1,0:T(8,128)(2,1)S(1)}, bf16[64,1024]{1,0:T(8,128)(2,1)S(1)}, u32[]{:S(2)}, u32[]{:S(2)}) collective-permute-start(bf16[64,1024]{1,0:T(8,128)(2,1)S(1)} %shard_map.151), channel_id=1, source_target_pairs={{0,4},{4,8},{8,12},{12,14},{14,10},{10,6},{6,2},{2,0},{1,5},{5,9},... | collective-permute-start | bytes 393224 | tf_op jit(solution)/shard_map/ppermute | solution.py:70
  111.9 8.0 %collective-permute-start.65 = (bf16[64,1024]{1,0:T(8,128)(2,1)S(1)}, bf16[64,1024]{1,0:T(8,128)(2,1)S(1)}, u32[]{:S(2)}, u32[]{:S(2)}) collective-permute-start(bf16[64,1024]{1,0:T(8,128)(2,1)S(1)} %shard_map.158), channel_id=1, source_target_pairs={{0,2},{4,0},{8,4},{12,8},{14,12},{10,14},{6,10},{2,6},{1,3},{5,1},... | collective-permute-start | bytes 393224 | tf_op jit(solution)/shard_map/ppermute | solution.py:70
  115.1 9.0 %collective-permute-start.59 = (bf16[64,1024]{1,0:T(8,128)(2,1)S(1)}, bf16[64,1024]{1,0:T(8,128)(2,1)S(1)}, u32[]{:S(2)}, u32[]{:S(2)}) collective-permute-start(bf16[64,1024]{1,0:T(8,128)(2,1)S(1)} %shard_map.154), channel_id=1, source_target_pairs={{0,2},{4,0},{8,4},{12,8},{14,12},{10,14},{6,10},{2,6},{1,3},{5,1},... | collective-permute-start | bytes 393224 | tf_op jit(solution)/shard_map/ppermute | solution.py:70
  117.1 7.0 %collective-permute-start.62 = (bf16[64,1024]{1,0:T(8,128)(2,1)S(1)}, bf16[64,1024]{1,0:T(8,128)(2,1)S(1)}, u32[]{:S(2)}, u32[]{:S(2)}) collective-permute-start(bf16[64,1024]{1,0:T(8,128)(2,1)S(1)} %shard_map.156), channel_id=1, source_target_pairs={{0,4},{4,8},{8,12},{12,14},{14,10},{10,6},{6,2},{2,0},{1,5},{5,9},... | collective-permute-start | bytes 393224 | tf_op jit(solution)/shard_map/ppermute | solution.py:70
  (47 other events, 355.3 us)

commit v20 on v17

--- a/solution.py
+++ b/solution.py
@@ -93,16 +93,44 @@
 
     def scatter(self, parts):
         most = self.half - 1
-        top_left = self.send(parts[self.half][0], 1)
-        bottom_right = self.send(parts[self.half][1], -1)
-        bottom_left = self.send(parts[most][1], 1)
-        top_right = self.send(parts[-most][0], -1)
-        for step in range(most, 0, -1):
-            top_left = self.send(add(parts[step][0], top_left), 1)
-            bottom_right = self.send(add(parts[-step][1], bottom_right), -1)
-            if step > 1:
-                bottom_left = self.send(add(parts[step - 1][1], bottom_left), 1)
-                top_right = self.send(add(parts[1 - step][0], top_right), -1)
+        mid, cols = parts[most][0].shape
+
+        def join_kernel(first, sum_ref, arrived_ref, other_ref, out_ref):
+            out_ref[pl.ds(first, mid), :] = (sum_ref[...] + arrived_ref[...].astype(F32)).astype(BF16)
+            out_ref[pl.ds(mid - first, mid), :] = other_ref[...]
+
+        def part_kernel(first, block_ref, arrived_ref, out_ref):
+            arrived = arrived_ref[pl.ds(first, mid), :].astype(F32)
+            out_ref[...] = (block_ref[...] + arrived).astype(BF16)
+
+        def joined(first, halves, arrived):
+            kernel = functools.partial(join_kernel, first)
+            own, other = (halves[1], halves[0]) if first else halves
+            return call(kernel, [((2 * mid, cols), BF16)], own, arrived, other)[0]
+
+        def parted(first, block, arrived):
+            return call(functools.partial(part_kernel, first), [((mid, cols), BF16)], block, arrived)[0]
+
+        from_left = self.send(parts[self.half][0], 1)
+        from_right = self.send(parts[self.half][1], -1)
+        from_left = self.send(joined(0, parts[most], from_left), 1)
+        from_right = self.send(joined(mid, parts[-most], from_right), -1)
+        top_left = bottom_left = from_left
+        top_right = bottom_right = from_right
+        for step in range(most - 1, 0, -1):
+            plus = add
+            if step == most - 1:
+                plus = None
+            sums = []
+            for first, block, arrived in (
+                (0, parts[step][0], top_left),
+                (mid, parts[-step][1], bottom_right),
+                (mid, parts[step][1], bottom_left),
+                (0, parts[-step][0], top_right),
+            ):
+                sums.append(plus(block, arrived) if plus else parted(first, block, arrived))
+            top_left, bottom_right = self.send(sums[0], 1), self.send(sums[1], -1)
+            bottom_left, top_right = self.send(sums[2], 1), self.send(sums[3], -1)
         return (top_left, top_right), (bottom_left, bottom_right)
 
     def part_types(self, distances):

time: 123 us -> 127 us (1.033)
  waiting for transfers between devices: 30 us -> 40.6 us
  starting transfers between devices: 68.4 us -> 62.1 us
    ppermute x56 -> x52, waiting for transfers between devices: 26.3 us -> 36.5 us  [send(): return lax.ppermute(value, 'expert', pairs)]
    ppermute x56 -> x52, starting transfers between devices: 62.2 us -> 55.7 us  [send(): return lax.ppermute(value, 'expert', pairs)]
  transfers between devices with their start and end apart: 62 -> 58, of which waited for: 30 -> 29; matrix products, arithmetic and copies ran while one was open for 1% -> 1% of each run, Pallas kernels for 15% -> 14%
where the time goes in v20:
time: 127 us
  starting transfers between devices  62.1 us (49%)
  waiting for transfers between devices  40.6 us (32%)
  Pallas kernels  21.8 us (17%)
  matrix products  1.71 us (1%)
    ppermute x52, starting transfers between devices, send(): return lax.ppermute(value, 'expert', pairs)  55.7 us
    ppermute x52, waiting for transfers between devices, send(): return lax.ppermute(value, 'expert', pairs)  36.5 us
    pallas_call x41, Pallas kernels, call(): pl.pallas_call(kernel, out_shape=[pltpu.VMEM(shape, dtype) for shape, dty...  17.3 us
    ppermute x4, starting transfers between devices, body(): terms.append(lax.ppermute(grad_rows, 'expert', pairs))  5.85 us
    ppermute x4, waiting for transfers between devices, body(): terms.append(lax.ppermute(grad_rows, 'expert', pairs))  4.05 us
  transfers between devices with their start and end apart: 58, of which 29 were waited for; matrix products, arithmetic and copies ran while one was open for 1% of the time, Pallas kernels for 14%

profile of v20, /device:TPU:0, one launch (start us, length us, event | category | flops | bytes accessed | tf_op | source)
XLA Modules:
  0.0 127.2 jit_solution(7971660437280412478)
XLA Ops:
  0.6 1.9 %shard_map.104 = (bf16[64,1152]{1,0:T(8,128)(2,1)S(1)}, bf16[64,1024]{1,0:T(8,128)(2,1)S(1)}, bf16[3200,384]{1,0:T(8,128)(2,1)S(1)}) custom-call(s32[8,128]{1,0:T(8,128)} %bitcast.19, f32[8,128]{1,0:T(8,128)} %bitcast.20, bf16[128,1024]{1,0:T(8,128)(2,1)} %refs_2_.2, bf16[2,512,384]{2,1,0:T(8,128)(2,1)} %refs_0_.1, bf16[2,512,384]{2,1,0:T(8,128)(2,1)} %refs_1_.1, ...), custom_call_target="tpu_custom_call" | custom-call | tf_op jit(solution)/shard_map/pallas_call | solution.py:243
  3.1 2.6 %collective-permute-start.1 = (bf16[64,1152]{1,0:T(8,128)(2,1)S(1)}, bf16[64,1152]{1,0:T(8,128)(2,1)S(1)}, u32[]{:S(2)}, u32[]{:S(2)}) collective-permute-start(bf16[64,1152]{1,0:T(8,128)(2,1)S(1)} %get-tuple-element.64.refs_0_), channel_id=1, source_target_pairs={{0,4},{4,8},{8,12},{12,14},{14,10},{10,6},{6,2},{2,0},{1,5},{5,9},... | collective-permute-start | bytes 442376 | tf_op jit(solution)/shard_map/ppermute | solution.py:68
  5.7 4.4 %collective-permute-done.1.refs_0_ = bf16[64,1152]{1,0:T(8,128)(2,1)S(1)} collective-permute-done((bf16[64,1152]{1,0:T(8,128)(2,1)S(1)}, bf16[64,1152]{1,0:T(8,128)(2,1)S(1)}, u32[]{:S(2)}, u32[]{:S(2)}) %collective-permute-start.1) | collective-permute-done | bytes 147488 | tf_op jit(solution)/shard_map/ppermute | solution.py:68
  10.1 1.8 %collective-permute-start.5 = (bf16[64,1152]{1,0:T(8,128)(2,1)S(1)}, bf16[64,1152]{1,0:T(8,128)(2,1)S(1)}, u32[]{:S(2)}, u32[]{:S(2)}) collective-permute-start(bf16[64,1152]{1,0:T(8,128)(2,1)S(1)} %collective-permute-done.1.refs_0_), channel_id=1, source_target_pairs={{0,4},{4,8},{8,12},{12,14},{14,10},{10,6},{6,2},{2,0},{1,5},{5,9},... | collective-permute-start | bytes 442376 | tf_op jit(solution)/shard_map/ppermute | solution.py:68
  12.1 1.7 %collective-permute-start.3 = (bf16[64,1152]{1,0:T(8,128)(2,1)S(1)}, bf16[64,1152]{1,0:T(8,128)(2,1)S(1)}, u32[]{:S(2)}, u32[]{:S(2)}) collective-permute-start(bf16[64,1152]{1,0:T(8,128)(2,1)S(1)} %get-tuple-element.64.refs_0_), channel_id=1, source_target_pairs={{0,2},{4,0},{8,4},{12,8},{14,12},{10,14},{6,10},{2,6},{1,3},{5,1},... | collective-permute-start | bytes 442376 | tf_op jit(solution)/shard_map/ppermute | solution.py:68
  14.2 2.0 %collective-permute-done.5.refs_0_ = bf16[64,1152]{1,0:T(8,128)(2,1)S(1)} collective-permute-done((bf16[64,1152]{1,0:T(8,128)(2,1)S(1)}, bf16[64,1152]{1,0:T(8,128)(2,1)S(1)}, u32[]{:S(2)}, u32[]{:S(2)}) %collective-permute-start.5) | collective-permute-done | bytes 147488 | tf_op jit(solution)/shard_map/ppermute | solution.py:68
  16.2 2.5 %collective-permute-start.9 = (bf16[64,1152]{1,0:T(8,128)(2,1)S(1)}, bf16[64,1152]{1,0:T(8,128)(2,1)S(1)}, u32[]{:S(2)}, u32[]{:S(2)}) collective-permute-start(bf16[64,1152]{1,0:T(8,128)(2,1)S(1)} %collective-permute-done.5.refs_0_), channel_id=1, source_target_pairs={{0,4},{4,8},{8,12},{12,14},{14,10},{10,6},{6,2},{2,0},{1,5},{5,9},... | collective-permute-start | bytes 442376 | tf_op jit(solution)/shard_map/ppermute | solution.py:68
  18.7 2.6 %collective-permute-done.3.refs_2_ = bf16[64,1152]{1,0:T(8,128)(2,1)S(1)} collective-permute-done((bf16[64,1152]{1,0:T(8,128)(2,1)S(1)}, bf16[64,1152]{1,0:T(8,128)(2,1)S(1)}, u32[]{:S(2)}, u32[]{:S(2)}) %collective-permute-start.3) | collective-permute-done | bytes 147488 | tf_op jit(solution)/shard_map/ppermute | solution.py:68
  21.4 1.9 %collective-permute-start.6 = (bf16[64,1024]{1,0:T(8,128)(2,1)S(1)}, bf16[64,1024]{1,0:T(8,128)(2,1)S(1)}, u32[]{:S(2)}, u32[]{:S(2)}) collective-permute-start(bf16[64,1024]{1,0:T(8,128)(2,1)S(1)} %collective-permute-done.2.refs_1_), channel_id=1, source_target_pairs={{0,4},{4,8},{8,12},{12,14},{14,10},{10,6},{6,2},{2,0},{1,5},{5,9},... | collective-permute-start | bytes 393224 | tf_op jit(solution)/shard_map/ppermute | solution.py:68
  23.3 1.8 %collective-permute-start.13 = (bf16[64,1152]{1,0:T(8,128)(2,1)S(1)}, bf16[64,1152]{1,0:T(8,128)(2,1)S(1)}, u32[]{:S(2)}, u32[]{:S(2)}) collective-permute-start(bf16[64,1152]{1,0:T(8,128)(2,1)S(1)} %collective-permute-done.9.refs_0_), channel_id=1, source_target_pairs={{0,4},{4,8},{8,12},{12,14},{14,10},{10,6},{6,2},{2,0},{1,5},{5,9},... | collective-permute-start | bytes 442376 | tf_op jit(solution)/shard_map/ppermute | solution.py:68
  25.3 1.9 %collective-permute-done.7.refs_2_ = bf16[64,1152]{1,0:T(8,128)(2,1)S(1)} collective-permute-done((bf16[64,1152]{1,0:T(8,128)(2,1)S(1)}, bf16[64,1152]{1,0:T(8,128)(2,1)S(1)}, u32[]{:S(2)}, u32[]{:S(2)}) %collective-permute-start.7) | collective-permute-done | bytes 147488 | tf_op jit(solution)/shard_map/ppermute | solution.py:68
  27.3 1.8 %shard_map.105 = (bf16[1024,1536]{1,0:T(8,128)(2,1)S(1)}, bf16[768,1024]{1,0:T(8,128)(2,1)S(1)}) custom-call(bf16[2,512,384]{2,1,0:T(8,128)(2,1)} %refs_0_.1, bf16[2,512,384]{2,1,0:T(8,128)(2,1)} %refs_1_.1, bf16[2,192,1024]{2,1,0:T(8,128)(2,1)} %refs_2_.3, bf16[3200,384]{1,0:T(8,128)(2,1)S(1)} %collective-permute-done.refs_3_), custom_call_target="tpu_custom_call" | custom-call | bytes 9437184 | tf_op jit(solution)/shard_map/pallas_call | solution.py:298
  32.7 1.7 %collective-permute-start.15 = (bf16[64,1024]{1,0:T(8,128)(2,1)S(1)}, bf16[64,1024]{1,0:T(8,128)(2,1)S(1)}, u32[]{:S(2)}, u32[]{:S(2)}) collective-permute-start(bf16[64,1024]{1,0:T(8,128)(2,1)S(1)} %get-tuple-element.73), channel_id=1, source_target_pairs={{0,4},{4,8},{8,12},{12,14},{14,10},{10,6},{6,2},{2,0},{1,5},{5,9},... | collective-permute-start | bytes 393224 | tf_op jit(solution)/shard_map/ppermute | solution.py:68
  36.1 2.7 %collective-permute-done.19.arrived_ref = bf16[64,1024]{1,0:T(8,128)(2,1)S(1)} collective-permute-done((bf16[64,1024]{1,0:T(8,128)(2,1)S(1)}, bf16[64,1024]{1,0:T(8,128)(2,1)S(1)}, u32[]{:S(2)}, u32[]{:S(2)}) %collective-permute-start.19) | collective-permute-done | bytes 131104 | tf_op jit(solution)/shard_map/ppermute | solution.py:68
  39.2 1.8 %collective-permute-start.16 = (bf16[128,1024]{1,0:T(8,128)(2,1)S(1)}, bf16[128,1024]{1,0:T(8,128)(2,1)S(1)}, u32[]{:S(2)}, u32[]{:S(2)}) collective-permute-start(bf16[128,1024]{1,0:T(8,128)(2,1)S(1)} %shard_map.112), channel_id=1, source_target_pairs={{0,4},{4,8},{8,12},{12,14},{14,10},{10,6},{6,2},{2,0},{1,5},{5,9},... | collective-permute-start | bytes 786440 | tf_op jit(solution)/shard_map/ppermute | solution.py:68
  42.5 4.6 %collective-permute-done.20.arrived_ref = bf16[128,1024]{1,0:T(8,128)(2,1)S(1)} collective-permute-done((bf16[128,1024]{1,0:T(8,128)(2,1)S(1)}, bf16[128,1024]{1,0:T(8,128)(2,1)S(1)}, u32[]{:S(2)}, u32[]{:S(2)}) %collective-permute-start.20) | collective-permute-done | bytes 262176 | tf_op jit(solution)/shard_map/ppermute | solution.py:68
  60.4 1.8 %collective-permute-start.27 = (bf16[64,1024]{1,0:T(8,128)(2,1)S(1)}, bf16[64,1024]{1,0:T(8,128)(2,1)S(1)}, u32[]{:S(2)}, u32[]{:S(2)}) collective-permute-start(bf16[64,1024]{1,0:T(8,128)(2,1)S(1)} %shard_map.118.refs_2_), channel_id=1, source_target_pairs={{0,4},{4,8},{8,12},{12,14},{14,10},{10,6},{6,2},{2,0},{1,5},{5,9},... | collective-permute-start | bytes 393224 | tf_op jit(solution)/shard_map/ppermute | solution.py:68
  68.5 2.1 %collective-permute-done.31.refs_7_ = bf16[64,1024]{1,0:T(8,128)(2,1)S(1)} collective-permute-done((bf16[64,1024]{1,0:T(8,128)(2,1)S(1)}, bf16[64,1024]{1,0:T(8,128)(2,1)S(1)}, u32[]{:S(2)}, u32[]{:S(2)}) %collective-permute-start.31) | collective-permute-done | bytes 131104 | tf_op jit(solution)/shard_map/ppermute | solution.py:68
  91.1 3.3 %collective-permute-start.44 = (bf16[8,1024]{1,0:T(8,128)(2,1)S(1)}, bf16[8,1024]{1,0:T(8,128)(2,1)S(1)}, u32[]{:S(2)}, u32[]{:S(2)}) collective-permute-start(bf16[8,1024]{1,0:T(8,128)(2,1)S(1)} %shard_map.131.refs_0_), channel_id=1, source_target_pairs={{0,12},{2,14},{4,8},{6,10},{8,4},{10,6},{12,0},{14,2},{1,13},{3,15... | collective-permute-start | bytes 49160 | tf_op jit(solution)/shard_map/ppermute | solution.py:478
  96.9 2.2 %collective-permute-done.43.refs_2_ = bf16[8,1024]{1,0:T(8,128)(2,1)S(1)} collective-permute-done((bf16[8,1024]{1,0:T(8,128)(2,1)S(1)}, bf16[8,1024]{1,0:T(8,128)(2,1)S(1)}, u32[]{:S(2)}, u32[]{:S(2)}) %collective-permute-start.43) | collective-permute-done | bytes 16416 | tf_op jit(solution)/shard_map/ppermute | solution.py:478
  105.7 1.7 %collective-permute-start.46 = (bf16[128,1024]{1,0:T(8,128)(2,1)S(1)}, bf16[128,1024]{1,0:T(8,128)(2,1)S(1)}, u32[]{:S(2)}, u32[]{:S(2)}) collective-permute-start(bf16[128,1024]{1,0:T(8,128)(2,1)S(1)} %shard_map.138), channel_id=1, source_target_pairs={{0,4},{4,8},{8,12},{12,14},{14,10},{10,6},{6,2},{2,0},{1,5},{5,9},... | collective-permute-start | bytes 786440 | tf_op jit(solution)/shard_map/ppermute | solution.py:68
  109.0 2.6 %collective-permute-done.50.arrived_ref = bf16[128,1024]{1,0:T(8,128)(2,1)S(1)} collective-permute-done((bf16[128,1024]{1,0:T(8,128)(2,1)S(1)}, bf16[128,1024]{1,0:T(8,128)(2,1)S(1)}, u32[]{:S(2)}, u32[]{:S(2)}) %collective-permute-start.50) | collective-permute-done | bytes 262176 | tf_op jit(solution)/shard_map/ppermute | solution.py:68
  114.4 1.7 %collective-permute-start.53 = (bf16[64,1024]{1,0:T(8,128)(2,1)S(1)}, bf16[64,1024]{1,0:T(8,128)(2,1)S(1)}, u32[]{:S(2)}, u32[]{:S(2)}) collective-permute-start(bf16[64,1024]{1,0:T(8,128)(2,1)S(1)} %shard_map.144), channel_id=1, source_target_pairs={{0,4},{4,8},{8,12},{12,14},{14,10},{10,6},{6,2},{2,0},{1,5},{5,9},... | collective-permute-start | bytes 393224 | tf_op jit(solution)/shard_map/ppermute | solution.py:68
  119.5 1.7 %collective-permute-start.48 = (bf16[64,1024]{1,0:T(8,128)(2,1)S(1)}, bf16[64,1024]{1,0:T(8,128)(2,1)S(1)}, u32[]{:S(2)}, u32[]{:S(2)}) collective-permute-start(bf16[64,1024]{1,0:T(8,128)(2,1)S(1)} %shard_map.140), channel_id=1, source_target_pairs={{0,4},{4,8},{8,12},{12,14},{14,10},{10,6},{6,2},{2,0},{1,5},{5,9},... | collective-permute-start | bytes 393224 | tf_op jit(solution)/shard_map/ppermute | solution.py:68
  (151 shorter events, 71.4 us)
Async XLA Ops:
  2.6 24.7 %collective-permute-start = (bf16[3200,384]{1,0:T(8,128)(2,1)S(1)}, bf16[3200,384]{1,0:T(8,128)(2,1)S(1)}, u32[]{:S(2)}, u32[]{:S(2)}) collective-permute-start(bf16[3200,384]{1,0:T(8,128)(2,1)S(1)} %get-tuple-element.66), channel_id=1, source_target_pairs={{0,1},{1,0},{2,3},{3,2},{4,5},{5,4},{6,7},{7,6},{8,9},{9,8},{10,11... | collective-permute-start | bytes 7372808 | tf_op jit(solution)/shard_map/ppermute | solution.py:343
  3.1 7.0 %collective-permute-start.1 = (bf16[64,1152]{1,0:T(8,128)(2,1)S(1)}, bf16[64,1152]{1,0:T(8,128)(2,1)S(1)}, u32[]{:S(2)}, u32[]{:S(2)}) collective-permute-start(bf16[64,1152]{1,0:T(8,128)(2,1)S(1)} %get-tuple-element.64.refs_0_), channel_id=1, source_target_pairs={{0,4},{4,8},{8,12},{12,14},{14,10},{10,6},{6,2},{2,0},{1,5},{5,9},... | collective-permute-start | bytes 442376 | tf_op jit(solution)/shard_map/ppermute | solution.py:68
  11.9 6.8 %collective-permute-start.8 = (bf16[64,1024]{1,0:T(8,128)(2,1)S(1)}, bf16[64,1024]{1,0:T(8,128)(2,1)S(1)}, u32[]{:S(2)}, u32[]{:S(2)}) collective-permute-start(bf16[64,1024]{1,0:T(8,128)(2,1)S(1)} %collective-permute-done.4.refs_3_), channel_id=1, source_target_pairs={{0,2},{4,0},{8,4},{12,8},{14,12},{10,14},{6,10},{2,6},{1,3},{5,1},... | collective-permute-start | bytes 393224 | tf_op jit(solution)/shard_map/ppermute | solution.py:68
  12.1 9.1 %collective-permute-start.3 = (bf16[64,1152]{1,0:T(8,128)(2,1)S(1)}, bf16[64,1152]{1,0:T(8,128)(2,1)S(1)}, u32[]{:S(2)}, u32[]{:S(2)}) collective-permute-start(bf16[64,1152]{1,0:T(8,128)(2,1)S(1)} %get-tuple-element.64.refs_0_), channel_id=1, source_target_pairs={{0,2},{4,0},{8,4},{12,8},{14,12},{10,14},{6,10},{2,6},{1,3},{5,1},... | collective-permute-start | bytes 442376 | tf_op jit(solution)/shard_map/ppermute | solution.py:68
  13.9 7.6 %collective-permute-start.2 = (bf16[64,1024]{1,0:T(8,128)(2,1)S(1)}, bf16[64,1024]{1,0:T(8,128)(2,1)S(1)}, u32[]{:S(2)}, u32[]{:S(2)}) collective-permute-start(bf16[64,1024]{1,0:T(8,128)(2,1)S(1)} %get-tuple-element.65.refs_1_), channel_id=1, source_target_pairs={{0,4},{4,8},{8,12},{12,14},{14,10},{10,6},{6,2},{2,0},{1,5},{5,9},... | collective-permute-start | bytes 393224 | tf_op jit(solution)/shard_map/ppermute | solution.py:68
  16.2 7.1 %collective-permute-start.9 = (bf16[64,1152]{1,0:T(8,128)(2,1)S(1)}, bf16[64,1152]{1,0:T(8,128)(2,1)S(1)}, u32[]{:S(2)}, u32[]{:S(2)}) collective-permute-start(bf16[64,1152]{1,0:T(8,128)(2,1)S(1)} %collective-permute-done.5.refs_0_), channel_id=1, source_target_pairs={{0,4},{4,8},{8,12},{12,14},{14,10},{10,6},{6,2},{2,0},{1,5},{5,9},... | collective-permute-start | bytes 442376 | tf_op jit(solution)/shard_map/ppermute | solution.py:68
  21.4 8.2 %collective-permute-start.6 = (bf16[64,1024]{1,0:T(8,128)(2,1)S(1)}, bf16[64,1024]{1,0:T(8,128)(2,1)S(1)}, u32[]{:S(2)}, u32[]{:S(2)}) collective-permute-start(bf16[64,1024]{1,0:T(8,128)(2,1)S(1)} %collective-permute-done.2.refs_1_), channel_id=1, source_target_pairs={{0,4},{4,8},{8,12},{12,14},{14,10},{10,6},{6,2},{2,0},{1,5},{5,9},... | collective-permute-start | bytes 393224 | tf_op jit(solution)/shard_map/ppermute | solution.py:68
  23.3 8.1 %collective-permute-start.13 = (bf16[64,1152]{1,0:T(8,128)(2,1)S(1)}, bf16[64,1152]{1,0:T(8,128)(2,1)S(1)}, u32[]{:S(2)}, u32[]{:S(2)}) collective-permute-start(bf16[64,1152]{1,0:T(8,128)(2,1)S(1)} %collective-permute-done.9.refs_0_), channel_id=1, source_target_pairs={{0,4},{4,8},{8,12},{12,14},{14,10},{10,6},{6,2},{2,0},{1,5},{5,9},... | collective-permute-start | bytes 442376 | tf_op jit(solution)/shard_map/ppermute | solution.py:68
  32.4 6.4 %collective-permute-start.19 = (bf16[64,1024]{1,0:T(8,128)(2,1)S(1)}, bf16[64,1024]{1,0:T(8,128)(2,1)S(1)}, u32[]{:S(2)}, u32[]{:S(2)}) collective-permute-start(bf16[64,1024]{1,0:T(8,128)(2,1)S(1)} %get-tuple-element.78), channel_id=1, source_target_pairs={{0,2},{4,0},{8,4},{12,8},{14,12},{10,14},{6,10},{2,6},{1,3},{5,1},... | collective-permute-start | bytes 393224 | tf_op jit(solution)/shard_map/ppermute | solution.py:68
  32.7 6.5 %collective-permute-start.15 = (bf16[64,1024]{1,0:T(8,128)(2,1)S(1)}, bf16[64,1024]{1,0:T(8,128)(2,1)S(1)}, u32[]{:S(2)}, u32[]{:S(2)}) collective-permute-start(bf16[64,1024]{1,0:T(8,128)(2,1)S(1)} %get-tuple-element.73), channel_id=1, source_target_pairs={{0,4},{4,8},{8,12},{12,14},{14,10},{10,6},{6,2},{2,0},{1,5},{5,9},... | collective-permute-start | bytes 393224 | tf_op jit(solution)/shard_map/ppermute | solution.py:68
  38.9 8.3 %collective-permute-start.20 = (bf16[128,1024]{1,0:T(8,128)(2,1)S(1)}, bf16[128,1024]{1,0:T(8,128)(2,1)S(1)}, u32[]{:S(2)}, u32[]{:S(2)}) collective-permute-start(bf16[128,1024]{1,0:T(8,128)(2,1)S(1)} %shard_map.115), channel_id=1, source_target_pairs={{0,2},{4,0},{8,4},{12,8},{14,12},{10,14},{6,10},{2,6},{1,3},{5,1},... | collective-permute-start | bytes 786440 | tf_op jit(solution)/shard_map/ppermute | solution.py:68
  39.2 9.2 %collective-permute-start.16 = (bf16[128,1024]{1,0:T(8,128)(2,1)S(1)}, bf16[128,1024]{1,0:T(8,128)(2,1)S(1)}, u32[]{:S(2)}, u32[]{:S(2)}) collective-permute-start(bf16[128,1024]{1,0:T(8,128)(2,1)S(1)} %shard_map.112), channel_id=1, source_target_pairs={{0,4},{4,8},{8,12},{12,14},{14,10},{10,6},{6,2},{2,0},{1,5},{5,9},... | collective-permute-start | bytes 786440 | tf_op jit(solution)/shard_map/ppermute | solution.py:68
  49.9 6.9 %collective-permute-start.23 = (bf16[64,1024]{1,0:T(8,128)(2,1)S(1)}, bf16[64,1024]{1,0:T(8,128)(2,1)S(1)}, u32[]{:S(2)}, u32[]{:S(2)}) collective-permute-start(bf16[64,1024]{1,0:T(8,128)(2,1)S(1)} %shard_map.119), channel_id=1, source_target_pairs={{0,4},{4,8},{8,12},{12,14},{14,10},{10,6},{6,2},{2,0},{1,5},{5,9},... | collective-permute-start | bytes 393224 | tf_op jit(solution)/shard_map/ppermute | solution.py:68
  56.8 6.5 %collective-permute-start.24 = (bf16[64,1024]{1,0:T(8,128)(2,1)S(1)}, bf16[64,1024]{1,0:T(8,128)(2,1)S(1)}, u32[]{:S(2)}, u32[]{:S(2)}) collective-permute-start(bf16[64,1024]{1,0:T(8,128)(2,1)S(1)} %shard_map.120), channel_id=1, source_target_pairs={{0,4},{4,8},{8,12},{12,14},{14,10},{10,6},{6,2},{2,0},{1,5},{5,9},... | collective-permute-start | bytes 393224 | tf_op jit(solution)/shard_map/ppermute | solution.py:68
  60.4 7.1 %collective-permute-start.27 = (bf16[64,1024]{1,0:T(8,128)(2,1)S(1)}, bf16[64,1024]{1,0:T(8,128)(2,1)S(1)}, u32[]{:S(2)}, u32[]{:S(2)}) collective-permute-start(bf16[64,1024]{1,0:T(8,128)(2,1)S(1)} %shard_map.118.refs_2_), channel_id=1, source_target_pairs={{0,4},{4,8},{8,12},{12,14},{14,10},{10,6},{6,2},{2,0},{1,5},{5,9},... | collective-permute-start | bytes 393224 | tf_op jit(solution)/shard_map/ppermute | solution.py:68
  65.5 7.6 %collective-permute-start.38 = (bf16[64,1024]{1,0:T(8,128)(2,1)S(1)}, bf16[64,1024]{1,0:T(8,128)(2,1)S(1)}, u32[]{:S(2)}, u32[]{:S(2)}) collective-permute-start(bf16[64,1024]{1,0:T(8,128)(2,1)S(1)} %shard_map.118.refs_2_), channel_id=1, source_target_pairs={{0,2},{4,0},{8,4},{12,8},{14,12},{10,14},{6,10},{2,6},{1,3},{5,1},... | collective-permute-start | bytes 393224 | tf_op jit(solution)/shard_map/ppermute | solution.py:68
  66.4 8.1 %collective-permute-start.35 = (bf16[64,1024]{1,0:T(8,128)(2,1)S(1)}, bf16[64,1024]{1,0:T(8,128)(2,1)S(1)}, u32[]{:S(2)}, u32[]{:S(2)}) collective-permute-start(bf16[64,1024]{1,0:T(8,128)(2,1)S(1)} %shard_map.123.refs_3_), channel_id=1, source_target_pairs={{0,4},{4,8},{8,12},{12,14},{14,10},{10,6},{6,2},{2,0},{1,5},{5,9},... | collective-permute-start | bytes 393224 | tf_op jit(solution)/shard_map/ppermute | solution.py:68
  67.5 7.6 %collective-permute-start.28 = (bf16[64,1024]{1,0:T(8,128)(2,1)S(1)}, bf16[64,1024]{1,0:T(8,128)(2,1)S(1)}, u32[]{:S(2)}, u32[]{:S(2)}) collective-permute-start(bf16[64,1024]{1,0:T(8,128)(2,1)S(1)} %collective-permute-done.27.refs_4_), channel_id=1, source_target_pairs={{0,4},{4,8},{8,12},{12,14},{14,10},{10,6},{6,2},{2,0},{1,5},{5,9},... | collective-permute-start | bytes 393224 | tf_op jit(solution)/shard_map/ppermute | solution.py:68
  105.2 6.4 %collective-permute-start.50 = (bf16[128,1024]{1,0:T(8,128)(2,1)S(1)}, bf16[128,1024]{1,0:T(8,128)(2,1)S(1)}, u32[]{:S(2)}, u32[]{:S(2)}) collective-permute-start(bf16[128,1024]{1,0:T(8,128)(2,1)S(1)} %shard_map.141), channel_id=1, source_target_pairs={{0,2},{4,0},{8,4},{12,8},{14,12},{10,14},{6,10},{2,6},{1,3},{5,1},... | collective-permute-start | bytes 786440 | tf_op jit(solution)/shard_map/ppermute | solution.py:68
  105.7 7.7 %collective-permute-start.46 = (bf16[128,1024]{1,0:T(8,128)(2,1)S(1)}, bf16[128,1024]{1,0:T(8,128)(2,1)S(1)}, u32[]{:S(2)}, u32[]{:S(2)}) collective-permute-start(bf16[128,1024]{1,0:T(8,128)(2,1)S(1)} %shard_map.138), channel_id=1, source_target_pairs={{0,4},{4,8},{8,12},{12,14},{14,10},{10,6},{6,2},{2,0},{1,5},{5,9},... | collective-permute-start | bytes 786440 | tf_op jit(solution)/shard_map/ppermute | solution.py:68
  107.4 8.7 %collective-permute-start.57 = (bf16[8,1274]{1,0:T(8,128)(2,1)S(1)}, bf16[8,1274]{1,0:T(8,128)(2,1)S(1)}, u32[]{:S(2)}, u32[]{:S(2)}) collective-permute-start(bf16[8,1274]{1,0:T(8,128)(2,1)S(1)} %pad_maximum_fusion.1), channel_id=1, source_target_pairs={{0,1},{1,0},{2,3},{3,2},{4,5},{5,4},{6,7},{7,6},{8,9},{9,8},{10,11... | collective-permute-start | bytes 61160 | tf_op jit(solution)/shard_map/ppermute | solution.py:489
  112.2 6.8 %collective-permute-start.55 = (bf16[64,1024]{1,0:T(8,128)(2,1)S(1)}, bf16[64,1024]{1,0:T(8,128)(2,1)S(1)}, u32[]{:S(2)}, u32[]{:S(2)}) collective-permute-start(bf16[64,1024]{1,0:T(8,128)(2,1)S(1)} %shard_map.146), channel_id=1, source_target_pairs={{0,2},{4,0},{8,4},{12,8},{14,12},{10,14},{6,10},{2,6},{1,3},{5,1},... | collective-permute-start | bytes 393224 | tf_op jit(solution)/shard_map/ppermute | solution.py:68
  114.4 7.0 %collective-permute-start.53 = (bf16[64,1024]{1,0:T(8,128)(2,1)S(1)}, bf16[64,1024]{1,0:T(8,128)(2,1)S(1)}, u32[]{:S(2)}, u32[]{:S(2)}) collective-permute-start(bf16[64,1024]{1,0:T(8,128)(2,1)S(1)} %shard_map.144), channel_id=1, source_target_pairs={{0,4},{4,8},{8,12},{12,14},{14,10},{10,6},{6,2},{2,0},{1,5},{5,9},... | collective-permute-start | bytes 393224 | tf_op jit(solution)/shard_map/ppermute | solution.py:68
  117.7 7.1 %collective-permute-start.52 = (bf16[64,1024]{1,0:T(8,128)(2,1)S(1)}, bf16[64,1024]{1,0:T(8,128)(2,1)S(1)}, u32[]{:S(2)}, u32[]{:S(2)}) collective-permute-start(bf16[64,1024]{1,0:T(8,128)(2,1)S(1)} %shard_map.143), channel_id=1, source_target_pairs={{0,2},{4,0},{8,4},{12,8},{14,12},{10,14},{6,10},{2,6},{1,3},{5,1},... | collective-permute-start | bytes 393224 | tf_op jit(solution)/shard_map/ppermute | solution.py:68
  (37 other events, 324.5 us)

commit v21 on v17

--- a/solution.py
+++ b/solution.py
@@ -387,7 +387,7 @@
         for own, arrived in zip(part_at[0], ring.scatter(part_at))
     ]
 
-    norm_at, mean_at = {}, {}
+    norm_at, mean_at, moe_at = {}, {}, {}
 
     def residual_of(token_refs, moe_refs):
         token_rows = rows_of([ref.at[:, :feature_dim] for ref in token_refs]).astype(F32)
@@ -415,6 +415,7 @@
     mean_at["pooled"] = jnp.zeros(pooled_shape, F32)
 
     def norm(distances, blocks):
+        moe_at[distances] = blocks
         rows = mid * len(blocks)
         mean_at["pooled"], *norm_at[distances] = call(
             functools.partial(norm_kernel, distances, len(blocks)),
@@ -438,24 +439,60 @@
             total = total + ref[...].astype(F32)
         refs[-1][...] = total.astype(refs[-1].dtype)
 
-    grad_rows = dot_t(logit_grad, class_head).astype(BF16)
+    def grad_kernel(count, *refs):
+        gain_ref, down_ref, *_, scaled_ref, back_ref = refs[count:]
+        total = refs[0][...].astype(F32)
+        for ref in refs[1:count]:
+            total = total + ref[...].astype(F32)
+        scaled = gain_ref[...] * total / rows_here
+        scaled_ref[...] = scaled
+        high = scaled.astype(BF16)
+        low = (scaled - high.astype(F32)).astype(BF16)
+        back_ref[...] = dot(high, down_ref[...]) + dot(low, down_ref[...])
+
+    def project_kernel(count, *refs):
+        down_ref, out_ref = refs[2 * count :]
+        tokens_here = [ref[:, :feature_dim] for ref in refs[:count]]
+        moe_here = [ref[...] for ref in refs[count : 2 * count]]
+        out = dot(jnp.concatenate(tokens_here, axis=0), down_ref[...])
+        out_ref[...] = out + dot(jnp.concatenate(moe_here, axis=0), down_ref[...])
+
+    def terms_of(rows, masks):
+        pairs = [[(e, e ^ mask) for e in range(expert_count)] for mask in masks]
+        return [rows] + [lax.ppermute(rows, "expert", p) for p in pairs]
+
+    project_at = {}
+    for distances, blocks in moe_at.items():
+        rows = mid * len(blocks)
+        project_at[distances] = call(
+            functools.partial(project_kernel, len(blocks)),
+            [((rows, local_experts * hidden_dim), F32)],
+            *tokens_at[distances],
+            *blocks,
+            down_t,
+            flops=4 * rows * feature_dim * hidden_dim * local_experts,
+        )[0]
+
+    near = [d for d in project_at if 0 < d[-1] < ring.half - 1]
+    last = [d for d in project_at if d not in near]
+    terms = terms_of(dot_t(logit_grad, class_head).astype(BF16), [1])
+    grad_rows = call(
+        functools.partial(grad_sum_kernel, 2),
+        [(pooled_shape, BF16)],
+        *terms,
+        wide_t,
+        *[project_at[d] for d in near],
+    )[0]
     span = 2
-    for masks, others, dtype in (
-        ([1], [wide_t, down_t], BF16),
-        (list(range(span, expert_count, span)), [], F32),
-    ):
-        terms = [grad_rows]
-        for mask in masks:
-            pairs = [(e, e ^ mask) for e in range(expert_count)]
-            terms.append(lax.ppermute(grad_rows, "expert", pairs))
-        grad_rows = call(
-            functools.partial(grad_sum_kernel, len(terms)),
-            [(pooled_shape, dtype)],
-            *terms,
-            *others,
-        )[0]
-    pooled_grad = grad_rows
-
+    terms = terms_of(grad_rows, range(span, expert_count, span))
+    scaled_rows, back_rows = call(
+        functools.partial(grad_kernel, len(terms)),
+        [(pooled_shape, F32), ((expert_count, local_experts * hidden_dim), F32)],
+        *terms,
+        gain,
+        down_t,
+        *[project_at[d] for d in last],
+    )
     both = jnp.concatenate([pooled, logit_grad], axis=1)
     if group_count == 2:
         both = jnp.concatenate([both, lax.ppermute(both, "group", [(0, 1), (1, 0)])], axis=0)
@@ -468,18 +505,20 @@
         preferred_element_type=F32,
     )
 
-    def backward_kernel(distances, residual_ref, inv_ref, gate_save, up_save, *refs):
-        grad_ref, gain_ref, wide_ref, down_ref, *outs = refs
+    def backward_kernel(distances, residual_ref, inv_ref, gate_save, up_save, project_ref, *refs):
+        scaled_ref, back_ref, wide_ref, *outs = refs
         residual, inv_rms = residual_ref[...], inv_ref[:, :1]
         cube = inv_rms * inv_rms * inv_rms
         parts = []
         for i, k in enumerate(distances):
             rows = slice(i * rows_here, (i + 1) * rows_here)
-            scaled = gain_ref[...] * grad_ref[pl.ds(ring.device_at(k), 1), :] / rows_here
+            device = pl.ds(ring.device_at(k), 1)
+            scaled = scaled_ref[device, :]
             slope = cube[rows] * jnp.mean(residual[rows] * scaled, axis=-1, keepdims=True)
-            parts.append(inv_rms[rows] * scaled - residual[rows] * slope)
-        resid_grad = jnp.concatenate(parts, axis=0) if len(parts) > 1 else parts[0]
-        down_back = dot(resid_grad.astype(BF16), down_ref[...])
+            parts.append(inv_rms[rows] * back_ref[device, :] - project_ref[rows, :] * slope)
+        down_back = jnp.concatenate(parts, axis=0) if len(parts) > 1 else parts[0]
+        if distances == (0,):
+            resid_grad = inv_rms * scaled - residual * slope
         grads = []
         for local in range(local_experts):
             cols = slice(local * hidden_dim, (local + 1) * hidden_dim)
@@ -500,10 +539,10 @@
             part_outs(distances),
             *norm_at[distances],
             *saved_at[distances],
-            pooled_grad,
-            gain,
+            project_at[distances],
+            scaled_rows,
+            back_rows,
             wide_t,
-            down_t,
             flops=flops * len(distances),
         )
         keep_parts(back_at, distances, result)

time: 123 us -> 125 us (1.016)
  waiting for transfers between devices: 30 us -> 25.5 us
  Pallas kernels: 21.9 us -> 25 us
  starting transfers between devices: 68.4 us -> 71.1 us
    ppermute x56, waiting for transfers between devices: 26.3 us -> 21.7 us  [send(): return lax.ppermute(value, 'expert', pairs)]
    pallas_call x41 -> x46, Pallas kernels: 17.4 us -> 20.5 us  [call(): pl.pallas_call(kernel, out_shape=[pltpu.VMEM(shape, dtype) for shape, dty...]
    ppermute x56, starting transfers between devices: 62.2 us -> 64.3 us  [send(): return lax.ppermute(value, 'expert', pairs)]
  transfers between devices with their start and end apart: 62 -> 62, of which waited for: 30 -> 24; matrix products, arithmetic and copies ran while one was open for 1% -> 1% of each run, Pallas kernels for 15% -> 17%
where the time goes in v21:
time: 125 us
  starting transfers between devices  71.1 us (57%)
  waiting for transfers between devices  25.5 us (20%)
  Pallas kernels  25 us (20%)
  matrix products  1.71 us (1%)
    ppermute x56, starting transfers between devices, send(): return lax.ppermute(value, 'expert', pairs)  64.3 us
    ppermute x56, waiting for transfers between devices, send(): return lax.ppermute(value, 'expert', pairs)  21.7 us
    pallas_call x46, Pallas kernels, call(): pl.pallas_call(kernel, out_shape=[pltpu.VMEM(shape, dtype) for shape, dty...  20.5 us
    ppermute x4, starting transfers between devices, terms_of(): return [rows] + [lax.ppermute(rows, 'expert', p) for p in pairs]  6.28 us
    ppermute x4, waiting for transfers between devices, terms_of(): return [rows] + [lax.ppermute(rows, 'expert', p) for p in pairs]  3.81 us
  transfers between devices with their start and end apart: 62, of which 24 were waited for; matrix products, arithmetic and copies ran while one was open for 1% of the time, Pallas kernels for 17%

profile of v21, /device:TPU:0, one launch (start us, length us, event | category | flops | bytes accessed | tf_op | source)
XLA Modules:
  0.0 124.5 jit_solution(16003529007619193516)
XLA Ops:
  0.6 1.9 %shard_map.104 = (bf16[64,1152]{1,0:T(8,128)(2,1)S(1)}, bf16[64,1024]{1,0:T(8,128)(2,1)S(1)}, bf16[3200,384]{1,0:T(8,128)(2,1)S(1)}) custom-call(s32[8,128]{1,0:T(8,128)} %bitcast.15, f32[8,128]{1,0:T(8,128)} %bitcast.16, bf16[128,1024]{1,0:T(8,128)(2,1)} %refs_2_.2, bf16[2,512,384]{2,1,0:T(8,128)(2,1)} %refs_0_.1, bf16[2,512,384]{2,1,0:T(8,128)(2,1)} %refs_1_.1, ...), custom_call_target="tpu_custom_call" | custom-call | tf_op jit(solution)/shard_map/pallas_call | solution.py:215
  3.1 2.6 %collective-permute-start.1 = (bf16[64,1152]{1,0:T(8,128)(2,1)S(1)}, bf16[64,1152]{1,0:T(8,128)(2,1)S(1)}, u32[]{:S(2)}, u32[]{:S(2)}) collective-permute-start(bf16[64,1152]{1,0:T(8,128)(2,1)S(1)} %get-tuple-element.66.refs_0_), channel_id=1, source_target_pairs={{0,4},{4,8},{8,12},{12,14},{14,10},{10,6},{6,2},{2,0},{1,5},{5,9},... | collective-permute-start | bytes 442376 | tf_op jit(solution)/shard_map/ppermute | solution.py:68
  5.7 4.4 %collective-permute-done.1.refs_0_ = bf16[64,1152]{1,0:T(8,128)(2,1)S(1)} collective-permute-done((bf16[64,1152]{1,0:T(8,128)(2,1)S(1)}, bf16[64,1152]{1,0:T(8,128)(2,1)S(1)}, u32[]{:S(2)}, u32[]{:S(2)}) %collective-permute-start.1) | collective-permute-done | bytes 147488 | tf_op jit(solution)/shard_map/ppermute | solution.py:68
  10.1 1.8 %collective-permute-start.5 = (bf16[64,1152]{1,0:T(8,128)(2,1)S(1)}, bf16[64,1152]{1,0:T(8,128)(2,1)S(1)}, u32[]{:S(2)}, u32[]{:S(2)}) collective-permute-start(bf16[64,1152]{1,0:T(8,128)(2,1)S(1)} %collective-permute-done.1.refs_0_), channel_id=1, source_target_pairs={{0,4},{4,8},{8,12},{12,14},{14,10},{10,6},{6,2},{2,0},{1,5},{5,9},... | collective-permute-start | bytes 442376 | tf_op jit(solution)/shard_map/ppermute | solution.py:68
  12.1 1.7 %collective-permute-start.3 = (bf16[64,1152]{1,0:T(8,128)(2,1)S(1)}, bf16[64,1152]{1,0:T(8,128)(2,1)S(1)}, u32[]{:S(2)}, u32[]{:S(2)}) collective-permute-start(bf16[64,1152]{1,0:T(8,128)(2,1)S(1)} %get-tuple-element.66.refs_0_), channel_id=1, source_target_pairs={{0,2},{4,0},{8,4},{12,8},{14,12},{10,14},{6,10},{2,6},{1,3},{5,1},... | collective-permute-start | bytes 442376 | tf_op jit(solution)/shard_map/ppermute | solution.py:68
  14.2 2.0 %collective-permute-done.5.refs_0_ = bf16[64,1152]{1,0:T(8,128)(2,1)S(1)} collective-permute-done((bf16[64,1152]{1,0:T(8,128)(2,1)S(1)}, bf16[64,1152]{1,0:T(8,128)(2,1)S(1)}, u32[]{:S(2)}, u32[]{:S(2)}) %collective-permute-start.5) | collective-permute-done | bytes 147488 | tf_op jit(solution)/shard_map/ppermute | solution.py:68
  16.2 2.5 %collective-permute-start.9 = (bf16[64,1152]{1,0:T(8,128)(2,1)S(1)}, bf16[64,1152]{1,0:T(8,128)(2,1)S(1)}, u32[]{:S(2)}, u32[]{:S(2)}) collective-permute-start(bf16[64,1152]{1,0:T(8,128)(2,1)S(1)} %collective-permute-done.5.refs_0_), channel_id=1, source_target_pairs={{0,4},{4,8},{8,12},{12,14},{14,10},{10,6},{6,2},{2,0},{1,5},{5,9},... | collective-permute-start | bytes 442376 | tf_op jit(solution)/shard_map/ppermute | solution.py:68
  18.7 2.6 %collective-permute-done.3.refs_2_ = bf16[64,1152]{1,0:T(8,128)(2,1)S(1)} collective-permute-done((bf16[64,1152]{1,0:T(8,128)(2,1)S(1)}, bf16[64,1152]{1,0:T(8,128)(2,1)S(1)}, u32[]{:S(2)}, u32[]{:S(2)}) %collective-permute-start.3) | collective-permute-done | bytes 147488 | tf_op jit(solution)/shard_map/ppermute | solution.py:68
  21.4 1.9 %collective-permute-start.6 = (bf16[64,1024]{1,0:T(8,128)(2,1)S(1)}, bf16[64,1024]{1,0:T(8,128)(2,1)S(1)}, u32[]{:S(2)}, u32[]{:S(2)}) collective-permute-start(bf16[64,1024]{1,0:T(8,128)(2,1)S(1)} %collective-permute-done.2.refs_1_), channel_id=1, source_target_pairs={{0,4},{4,8},{8,12},{12,14},{14,10},{10,6},{6,2},{2,0},{1,5},{5,9},... | collective-permute-start | bytes 393224 | tf_op jit(solution)/shard_map/ppermute | solution.py:68
  23.3 1.8 %collective-permute-start.13 = (bf16[64,1152]{1,0:T(8,128)(2,1)S(1)}, bf16[64,1152]{1,0:T(8,128)(2,1)S(1)}, u32[]{:S(2)}, u32[]{:S(2)}) collective-permute-start(bf16[64,1152]{1,0:T(8,128)(2,1)S(1)} %collective-permute-done.9.refs_0_), channel_id=1, source_target_pairs={{0,4},{4,8},{8,12},{12,14},{14,10},{10,6},{6,2},{2,0},{1,5},{5,9},... | collective-permute-start | bytes 442376 | tf_op jit(solution)/shard_map/ppermute | solution.py:68
  25.3 1.9 %collective-permute-done.7.refs_2_ = bf16[64,1152]{1,0:T(8,128)(2,1)S(1)} collective-permute-done((bf16[64,1152]{1,0:T(8,128)(2,1)S(1)}, bf16[64,1152]{1,0:T(8,128)(2,1)S(1)}, u32[]{:S(2)}, u32[]{:S(2)}) %collective-permute-start.7) | collective-permute-done | bytes 147488 | tf_op jit(solution)/shard_map/ppermute | solution.py:68
  27.3 1.8 %shard_map.105 = (bf16[1024,1536]{1,0:T(8,128)(2,1)S(1)}, bf16[768,1024]{1,0:T(8,128)(2,1)S(1)}) custom-call(bf16[2,512,384]{2,1,0:T(8,128)(2,1)} %refs_0_.1, bf16[2,512,384]{2,1,0:T(8,128)(2,1)} %refs_1_.1, bf16[2,192,1024]{2,1,0:T(8,128)(2,1)} %refs_2_.3, bf16[3200,384]{1,0:T(8,128)(2,1)S(1)} %collective-permute-done.refs_3_), custom_call_target="tpu_custom_call" | custom-call | bytes 9437184 | tf_op jit(solution)/shard_map/pallas_call | solution.py:270
  48.2 1.7 %collective-permute-start.27 = (bf16[64,1024]{1,0:T(8,128)(2,1)S(1)}, bf16[64,1024]{1,0:T(8,128)(2,1)S(1)}, u32[]{:S(2)}, u32[]{:S(2)}) collective-permute-start(bf16[64,1024]{1,0:T(8,128)(2,1)S(1)} %shard_map.121), channel_id=1, source_target_pairs={{0,2},{4,0},{8,4},{12,8},{14,12},{10,14},{6,10},{2,6},{1,3},{5,1},... | collective-permute-start | bytes 393224 | tf_op jit(solution)/shard_map/ppermute | solution.py:68
  51.6 2.1 %collective-permute-start.18 = (bf16[64,1024]{1,0:T(8,128)(2,1)S(1)}, bf16[64,1024]{1,0:T(8,128)(2,1)S(1)}, u32[]{:S(2)}, u32[]{:S(2)}) collective-permute-start(bf16[64,1024]{1,0:T(8,128)(2,1)S(1)} %shard_map.114), channel_id=1, source_target_pairs={{0,4},{4,8},{8,12},{12,14},{14,10},{10,6},{6,2},{2,0},{1,5},{5,9},... | collective-permute-start | bytes 393224 | tf_op jit(solution)/shard_map/ppermute | solution.py:68
  54.2 2.1 %collective-permute-start.28 = (bf16[64,1024]{1,0:T(8,128)(2,1)S(1)}, bf16[64,1024]{1,0:T(8,128)(2,1)S(1)}, u32[]{:S(2)}, u32[]{:S(2)}) collective-permute-start(bf16[64,1024]{1,0:T(8,128)(2,1)S(1)} %shard_map.122), channel_id=1, source_target_pairs={{0,2},{4,0},{8,4},{12,8},{14,12},{10,14},{6,10},{2,6},{1,3},{5,1},... | collective-permute-start | bytes 393224 | tf_op jit(solution)/shard_map/ppermute | solution.py:68
  58.0 2.1 %collective-permute-start.29 = (bf16[64,1024]{1,0:T(8,128)(2,1)S(1)}, bf16[64,1024]{1,0:T(8,128)(2,1)S(1)}, u32[]{:S(2)}, u32[]{:S(2)}) collective-permute-start(bf16[64,1024]{1,0:T(8,128)(2,1)S(1)} %shard_map.117.refs_2_), channel_id=1, source_target_pairs={{0,4},{4,8},{8,12},{12,14},{14,10},{10,6},{6,2},{2,0},{1,5},{5,9},... | collective-permute-start | bytes 393224 | tf_op jit(solution)/shard_map/ppermute | solution.py:68
  64.3 2.1 %collective-permute-start.30 = (bf16[64,1024]{1,0:T(8,128)(2,1)S(1)}, bf16[64,1024]{1,0:T(8,128)(2,1)S(1)}, u32[]{:S(2)}, u32[]{:S(2)}) collective-permute-start(bf16[64,1024]{1,0:T(8,128)(2,1)S(1)} %collective-permute-done.29.refs_4_), channel_id=1, source_target_pairs={{0,4},{4,8},{8,12},{12,14},{14,10},{10,6},{6,2},{2,0},{1,5},{5,9},... | collective-permute-start | bytes 393224 | tf_op jit(solution)/shard_map/ppermute | solution.py:68
  68.2 1.7 %collective-permute-start.41 = (bf16[64,1024]{1,0:T(8,128)(2,1)S(1)}, bf16[64,1024]{1,0:T(8,128)(2,1)S(1)}, u32[]{:S(2)}, u32[]{:S(2)}) collective-permute-start(bf16[64,1024]{1,0:T(8,128)(2,1)S(1)} %collective-permute-done.40.refs_6_), channel_id=1, source_target_pairs={{0,2},{4,0},{8,4},{12,8},{14,12},{10,14},{6,10},{2,6},{1,3},{5,1},... | collective-permute-start | bytes 393224 | tf_op jit(solution)/shard_map/ppermute | solution.py:68
  70.9 1.9 %collective-permute-start.31 = (bf16[64,1024]{1,0:T(8,128)(2,1)S(1)}, bf16[64,1024]{1,0:T(8,128)(2,1)S(1)}, u32[]{:S(2)}, u32[]{:S(2)}) collective-permute-start(bf16[64,1024]{1,0:T(8,128)(2,1)S(1)} %collective-permute-done.30.refs_4_), channel_id=1, source_target_pairs={{0,4},{4,8},{8,12},{12,14},{14,10},{10,6},{6,2},{2,0},{1,5},{5,9},... | collective-permute-start | bytes 393224 | tf_op jit(solution)/shard_map/ppermute | solution.py:68
  85.6 1.9 %collective-permute-start.43 = (bf16[8,1024]{1,0:T(8,128)(2,1)S(1)}, bf16[8,1024]{1,0:T(8,128)(2,1)S(1)}, u32[]{:S(2)}, u32[]{:S(2)}) collective-permute-start(bf16[8,1024]{1,0:T(8,128)(2,1)S(1)} %convolution_convert_fusion.refs_0_), channel_id=1, source_target_pairs={{0,2},{2,0},{4,6},{6,4},{8,10},{10,8},{12,14},{14,12},{1,3},{3,1},... | collective-permute-start | bytes 49160 | tf_op jit(solution)/shard_map/ppermute | solution.py:462
  89.4 3.3 %collective-permute-start.46 = (bf16[8,1024]{1,0:T(8,128)(2,1)S(1)}, bf16[8,1024]{1,0:T(8,128)(2,1)S(1)}, u32[]{:S(2)}, u32[]{:S(2)}) collective-permute-start(bf16[8,1024]{1,0:T(8,128)(2,1)S(1)} %shard_map.134.refs_0_), channel_id=1, source_target_pairs={{0,12},{2,14},{4,8},{6,10},{8,4},{10,6},{12,0},{14,2},{1,13},{3,15... | collective-permute-start | bytes 49160 | tf_op jit(solution)/shard_map/ppermute | solution.py:462
  94.9 2.4 %collective-permute-done.45.refs_2_ = bf16[8,1024]{1,0:T(8,128)(2,1)S(1)} collective-permute-done((bf16[8,1024]{1,0:T(8,128)(2,1)S(1)}, bf16[8,1024]{1,0:T(8,128)(2,1)S(1)}, u32[]{:S(2)}, u32[]{:S(2)}) %collective-permute-start.45) | collective-permute-done | bytes 16416 | tf_op jit(solution)/shard_map/ppermute | solution.py:462
  98.9 1.8 %collective-permute-start.57 = (bf16[64,1024]{1,0:T(8,128)(2,1)S(1)}, bf16[64,1024]{1,0:T(8,128)(2,1)S(1)}, u32[]{:S(2)}, u32[]{:S(2)}) collective-permute-start(bf16[64,1024]{1,0:T(8,128)(2,1)S(1)} %get-tuple-element.129), channel_id=1, source_target_pairs={{0,2},{4,0},{8,4},{12,8},{14,12},{10,14},{6,10},{2,6},{1,3},{5,1},... | collective-permute-start | bytes 393224 | tf_op jit(solution)/shard_map/ppermute | solution.py:68
  116.2 1.9 %collective-permute-done.49.arrived_ref = bf16[64,1024]{1,0:T(8,128)(2,1)S(1)} collective-permute-done((bf16[64,1024]{1,0:T(8,128)(2,1)S(1)}, bf16[64,1024]{1,0:T(8,128)(2,1)S(1)}, u32[]{:S(2)}, u32[]{:S(2)}) %collective-permute-start.49) | collective-permute-done | bytes 131104 | tf_op jit(solution)/shard_map/ppermute | solution.py:68
  (164 shorter events, 71.5 us)
Async XLA Ops:
  2.6 24.7 %collective-permute-start = (bf16[3200,384]{1,0:T(8,128)(2,1)S(1)}, bf16[3200,384]{1,0:T(8,128)(2,1)S(1)}, u32[]{:S(2)}, u32[]{:S(2)}) collective-permute-start(bf16[3200,384]{1,0:T(8,128)(2,1)S(1)} %get-tuple-element.68), channel_id=1, source_target_pairs={{0,1},{1,0},{2,3},{3,2},{4,5},{5,4},{6,7},{7,6},{8,9},{9,8},{10,11... | collective-permute-start | bytes 7372808 | tf_op jit(solution)/shard_map/ppermute | solution.py:315
  3.1 7.0 %collective-permute-start.1 = (bf16[64,1152]{1,0:T(8,128)(2,1)S(1)}, bf16[64,1152]{1,0:T(8,128)(2,1)S(1)}, u32[]{:S(2)}, u32[]{:S(2)}) collective-permute-start(bf16[64,1152]{1,0:T(8,128)(2,1)S(1)} %get-tuple-element.66.refs_0_), channel_id=1, source_target_pairs={{0,4},{4,8},{8,12},{12,14},{14,10},{10,6},{6,2},{2,0},{1,5},{5,9},... | collective-permute-start | bytes 442376 | tf_op jit(solution)/shard_map/ppermute | solution.py:68
  11.9 6.8 %collective-permute-start.8 = (bf16[64,1024]{1,0:T(8,128)(2,1)S(1)}, bf16[64,1024]{1,0:T(8,128)(2,1)S(1)}, u32[]{:S(2)}, u32[]{:S(2)}) collective-permute-start(bf16[64,1024]{1,0:T(8,128)(2,1)S(1)} %collective-permute-done.4.refs_3_), channel_id=1, source_target_pairs={{0,2},{4,0},{8,4},{12,8},{14,12},{10,14},{6,10},{2,6},{1,3},{5,1},... | collective-permute-start | bytes 393224 | tf_op jit(solution)/shard_map/ppermute | solution.py:68
  12.1 9.1 %collective-permute-start.3 = (bf16[64,1152]{1,0:T(8,128)(2,1)S(1)}, bf16[64,1152]{1,0:T(8,128)(2,1)S(1)}, u32[]{:S(2)}, u32[]{:S(2)}) collective-permute-start(bf16[64,1152]{1,0:T(8,128)(2,1)S(1)} %get-tuple-element.66.refs_0_), channel_id=1, source_target_pairs={{0,2},{4,0},{8,4},{12,8},{14,12},{10,14},{6,10},{2,6},{1,3},{5,1},... | collective-permute-start | bytes 442376 | tf_op jit(solution)/shard_map/ppermute | solution.py:68
  13.9 7.6 %collective-permute-start.2 = (bf16[64,1024]{1,0:T(8,128)(2,1)S(1)}, bf16[64,1024]{1,0:T(8,128)(2,1)S(1)}, u32[]{:S(2)}, u32[]{:S(2)}) collective-permute-start(bf16[64,1024]{1,0:T(8,128)(2,1)S(1)} %get-tuple-element.67.refs_1_), channel_id=1, source_target_pairs={{0,4},{4,8},{8,12},{12,14},{14,10},{10,6},{6,2},{2,0},{1,5},{5,9},... | collective-permute-start | bytes 393224 | tf_op jit(solution)/shard_map/ppermute | solution.py:68
  16.2 7.1 %collective-permute-start.9 = (bf16[64,1152]{1,0:T(8,128)(2,1)S(1)}, bf16[64,1152]{1,0:T(8,128)(2,1)S(1)}, u32[]{:S(2)}, u32[]{:S(2)}) collective-permute-start(bf16[64,1152]{1,0:T(8,128)(2,1)S(1)} %collective-permute-done.5.refs_0_), channel_id=1, source_target_pairs={{0,4},{4,8},{8,12},{12,14},{14,10},{10,6},{6,2},{2,0},{1,5},{5,9},... | collective-permute-start | bytes 442376 | tf_op jit(solution)/shard_map/ppermute | solution.py:68
  21.4 8.2 %collective-permute-start.6 = (bf16[64,1024]{1,0:T(8,128)(2,1)S(1)}, bf16[64,1024]{1,0:T(8,128)(2,1)S(1)}, u32[]{:S(2)}, u32[]{:S(2)}) collective-permute-start(bf16[64,1024]{1,0:T(8,128)(2,1)S(1)} %collective-permute-done.2.refs_1_), channel_id=1, source_target_pairs={{0,4},{4,8},{8,12},{12,14},{14,10},{10,6},{6,2},{2,0},{1,5},{5,9},... | collective-permute-start | bytes 393224 | tf_op jit(solution)/shard_map/ppermute | solution.py:68
  23.3 7.8 %collective-permute-start.13 = (bf16[64,1152]{1,0:T(8,128)(2,1)S(1)}, bf16[64,1152]{1,0:T(8,128)(2,1)S(1)}, u32[]{:S(2)}, u32[]{:S(2)}) collective-permute-start(bf16[64,1152]{1,0:T(8,128)(2,1)S(1)} %collective-permute-done.9.refs_0_), channel_id=1, source_target_pairs={{0,4},{4,8},{8,12},{12,14},{14,10},{10,6},{6,2},{2,0},{1,5},{5,9},... | collective-permute-start | bytes 442376 | tf_op jit(solution)/shard_map/ppermute | solution.py:68
  33.8 8.0 %collective-permute-start.25 = (bf16[64,1024]{1,0:T(8,128)(2,1)S(1)}, bf16[64,1024]{1,0:T(8,128)(2,1)S(1)}, u32[]{:S(2)}, u32[]{:S(2)}) collective-permute-start(bf16[64,1024]{1,0:T(8,128)(2,1)S(1)} %get-tuple-element.86), channel_id=1, source_target_pairs={{0,2},{4,0},{8,4},{12,8},{14,12},{10,14},{6,10},{2,6},{1,3},{5,1},... | collective-permute-start | bytes 393224 | tf_op jit(solution)/shard_map/ppermute | solution.py:68
  36.3 7.5 %collective-permute-start.19 = (bf16[64,1024]{1,0:T(8,128)(2,1)S(1)}, bf16[64,1024]{1,0:T(8,128)(2,1)S(1)}, u32[]{:S(2)}, u32[]{:S(2)}) collective-permute-start(bf16[64,1024]{1,0:T(8,128)(2,1)S(1)} %get-tuple-element.78), channel_id=1, source_target_pairs={{0,2},{4,0},{8,4},{12,8},{14,12},{10,14},{6,10},{2,6},{1,3},{5,1},... | collective-permute-start | bytes 393224 | tf_op jit(solution)/shard_map/ppermute | solution.py:68
  40.2 7.5 %collective-permute-start.22 = (bf16[64,1024]{1,0:T(8,128)(2,1)S(1)}, bf16[64,1024]{1,0:T(8,128)(2,1)S(1)}, u32[]{:S(2)}, u32[]{:S(2)}) collective-permute-start(bf16[64,1024]{1,0:T(8,128)(2,1)S(1)} %get-tuple-element.82), channel_id=1, source_target_pairs={{0,4},{4,8},{8,12},{12,14},{14,10},{10,6},{6,2},{2,0},{1,5},{5,9},... | collective-permute-start | bytes 393224 | tf_op jit(solution)/shard_map/ppermute | solution.py:68
  43.9 7.6 %collective-permute-start.20 = (bf16[64,1024]{1,0:T(8,128)(2,1)S(1)}, bf16[64,1024]{1,0:T(8,128)(2,1)S(1)}, u32[]{:S(2)}, u32[]{:S(2)}) collective-permute-start(bf16[64,1024]{1,0:T(8,128)(2,1)S(1)} %shard_map.115), channel_id=1, source_target_pairs={{0,2},{4,0},{8,4},{12,8},{14,12},{10,14},{6,10},{2,6},{1,3},{5,1},... | collective-permute-start | bytes 393224 | tf_op jit(solution)/shard_map/ppermute | solution.py:68
  45.0 6.5 %collective-permute-start.17 = (bf16[64,1024]{1,0:T(8,128)(2,1)S(1)}, bf16[64,1024]{1,0:T(8,128)(2,1)S(1)}, u32[]{:S(2)}, u32[]{:S(2)}) collective-permute-start(bf16[64,1024]{1,0:T(8,128)(2,1)S(1)} %shard_map.113), channel_id=1, source_target_pairs={{0,4},{4,8},{8,12},{12,14},{14,10},{10,6},{6,2},{2,0},{1,5},{5,9},... | collective-permute-start | bytes 393224 | tf_op jit(solution)/shard_map/ppermute | solution.py:68
  54.1 6.5 %collective-permute-start.24 = (bf16[64,1024]{1,0:T(8,128)(2,1)S(1)}, bf16[64,1024]{1,0:T(8,128)(2,1)S(1)}, u32[]{:S(2)}, u32[]{:S(2)}) collective-permute-start(bf16[64,1024]{1,0:T(8,128)(2,1)S(1)} %shard_map.119), channel_id=1, source_target_pairs={{0,4},{4,8},{8,12},{12,14},{14,10},{10,6},{6,2},{2,0},{1,5},{5,9},... | collective-permute-start | bytes 393224 | tf_op jit(solution)/shard_map/ppermute | solution.py:68
  63.2 6.7 %collective-permute-start.37 = (bf16[64,1024]{1,0:T(8,128)(2,1)S(1)}, bf16[64,1024]{1,0:T(8,128)(2,1)S(1)}, u32[]{:S(2)}, u32[]{:S(2)}) collective-permute-start(bf16[64,1024]{1,0:T(8,128)(2,1)S(1)} %shard_map.123.refs_3_), channel_id=1, source_target_pairs={{0,4},{4,8},{8,12},{12,14},{14,10},{10,6},{6,2},{2,0},{1,5},{5,9},... | collective-permute-start | bytes 393224 | tf_op jit(solution)/shard_map/ppermute | solution.py:68
  64.3 6.6 %collective-permute-start.30 = (bf16[64,1024]{1,0:T(8,128)(2,1)S(1)}, bf16[64,1024]{1,0:T(8,128)(2,1)S(1)}, u32[]{:S(2)}, u32[]{:S(2)}) collective-permute-start(bf16[64,1024]{1,0:T(8,128)(2,1)S(1)} %collective-permute-done.29.refs_4_), channel_id=1, source_target_pairs={{0,4},{4,8},{8,12},{12,14},{14,10},{10,6},{6,2},{2,0},{1,5},{5,9},... | collective-permute-start | bytes 393224 | tf_op jit(solution)/shard_map/ppermute | solution.py:68
  68.2 9.0 %collective-permute-start.41 = (bf16[64,1024]{1,0:T(8,128)(2,1)S(1)}, bf16[64,1024]{1,0:T(8,128)(2,1)S(1)}, u32[]{:S(2)}, u32[]{:S(2)}) collective-permute-start(bf16[64,1024]{1,0:T(8,128)(2,1)S(1)} %collective-permute-done.40.refs_6_), channel_id=1, source_target_pairs={{0,2},{4,0},{8,4},{12,8},{14,12},{10,14},{6,10},{2,6},{1,3},{5,1},... | collective-permute-start | bytes 393224 | tf_op jit(solution)/shard_map/ppermute | solution.py:68
  69.9 8.6 %collective-permute-start.38 = (bf16[64,1024]{1,0:T(8,128)(2,1)S(1)}, bf16[64,1024]{1,0:T(8,128)(2,1)S(1)}, u32[]{:S(2)}, u32[]{:S(2)}) collective-permute-start(bf16[64,1024]{1,0:T(8,128)(2,1)S(1)} %collective-permute-done.37.refs_5_), channel_id=1, source_target_pairs={{0,4},{4,8},{8,12},{12,14},{14,10},{10,6},{6,2},{2,0},{1,5},{5,9},... | collective-permute-start | bytes 393224 | tf_op jit(solution)/shard_map/ppermute | solution.py:68
  70.9 8.4 %collective-permute-start.31 = (bf16[64,1024]{1,0:T(8,128)(2,1)S(1)}, bf16[64,1024]{1,0:T(8,128)(2,1)S(1)}, u32[]{:S(2)}, u32[]{:S(2)}) collective-permute-start(bf16[64,1024]{1,0:T(8,128)(2,1)S(1)} %collective-permute-done.30.refs_4_), channel_id=1, source_target_pairs={{0,4},{4,8},{8,12},{12,14},{14,10},{10,6},{6,2},{2,0},{1,5},{5,9},... | collective-permute-start | bytes 393224 | tf_op jit(solution)/shard_map/ppermute | solution.py:68
  72.8 7.1 %collective-permute-start.35 = (bf16[64,1024]{1,0:T(8,128)(2,1)S(1)}, bf16[64,1024]{1,0:T(8,128)(2,1)S(1)}, u32[]{:S(2)}, u32[]{:S(2)}) collective-permute-start(bf16[64,1024]{1,0:T(8,128)(2,1)S(1)} %collective-permute-done.34.refs_7_), channel_id=1, source_target_pairs={{0,2},{4,0},{8,4},{12,8},{14,12},{10,14},{6,10},{2,6},{1,3},{5,1},... | collective-permute-start | bytes 393224 | tf_op jit(solution)/shard_map/ppermute | solution.py:68
  110.0 8.1 %collective-permute-start.49 = (bf16[64,1024]{1,0:T(8,128)(2,1)S(1)}, bf16[64,1024]{1,0:T(8,128)(2,1)S(1)}, u32[]{:S(2)}, u32[]{:S(2)}) collective-permute-start(bf16[64,1024]{1,0:T(8,128)(2,1)S(1)} %shard_map.144), channel_id=1, source_target_pairs={{0,4},{4,8},{8,12},{12,14},{14,10},{10,6},{6,2},{2,0},{1,5},{5,9},... | collective-permute-start | bytes 393224 | tf_op jit(solution)/shard_map/ppermute | solution.py:68
  110.6 8.1 %collective-permute-start.59 = (bf16[64,1024]{1,0:T(8,128)(2,1)S(1)}, bf16[64,1024]{1,0:T(8,128)(2,1)S(1)}, u32[]{:S(2)}, u32[]{:S(2)}) collective-permute-start(bf16[64,1024]{1,0:T(8,128)(2,1)S(1)} %shard_map.151), channel_id=1, source_target_pairs={{0,2},{4,0},{8,4},{12,8},{14,12},{10,14},{6,10},{2,6},{1,3},{5,1},... | collective-permute-start | bytes 393224 | tf_op jit(solution)/shard_map/ppermute | solution.py:68
  114.0 8.5 %collective-permute-start.53 = (bf16[64,1024]{1,0:T(8,128)(2,1)S(1)}, bf16[64,1024]{1,0:T(8,128)(2,1)S(1)}, u32[]{:S(2)}, u32[]{:S(2)}) collective-permute-start(bf16[64,1024]{1,0:T(8,128)(2,1)S(1)} %shard_map.147), channel_id=1, source_target_pairs={{0,2},{4,0},{8,4},{12,8},{14,12},{10,14},{6,10},{2,6},{1,3},{5,1},... | collective-permute-start | bytes 393224 | tf_op jit(solution)/shard_map/ppermute | solution.py:68
  115.7 6.8 %collective-permute-start.56 = (bf16[64,1024]{1,0:T(8,128)(2,1)S(1)}, bf16[64,1024]{1,0:T(8,128)(2,1)S(1)}, u32[]{:S(2)}, u32[]{:S(2)}) collective-permute-start(bf16[64,1024]{1,0:T(8,128)(2,1)S(1)} %shard_map.149), channel_id=1, source_target_pairs={{0,4},{4,8},{8,12},{12,14},{14,10},{10,6},{6,2},{2,0},{1,5},{5,9},... | collective-permute-start | bytes 393224 | tf_op jit(solution)/shard_map/ppermute | solution.py:68
  (41 other events, 308.9 us)

commit v22 on v16

--- a/solution.py
+++ b/solution.py
@@ -98,12 +98,13 @@
         bottom_left = self.send(parts[most][1], 1)
         top_right = self.send(parts[-most][0], -1)
         for step in range(most, 0, -1):
-            top_left = self.send(add(parts[step][0], top_left), 1)
+            last = add(parts[step][0], top_left)
+            top_left = self.send(last, 1)
             bottom_right = self.send(add(parts[-step][1], bottom_right), -1)
             if step > 1:
                 bottom_left = self.send(add(parts[step - 1][1], bottom_left), 1)
                 top_right = self.send(add(parts[1 - step][0], top_right), -1)
-        return (top_left, top_right), (bottom_left, bottom_right)
+        return (top_left, top_right), (bottom_left, bottom_right), last
 
     def part_types(self, distances):
         types = []
@@ -434,18 +435,6 @@
             pairs = [(e, e ^ mask) for e in range(expert_count)]
             pooled_grad = pooled_grad + lax.ppermute(mine, "expert", pairs).astype(F32)
 
-    both = jnp.concatenate([pooled, logit_grad], axis=1)
-    if group_count == 2:
-        both = jnp.concatenate([both, lax.ppermute(both, "group", [(0, 1), (1, 0)])], axis=0)
-    else:
-        both = lax.all_gather(both, "group", axis=0, tiled=True)
-    head_grad = lax.dot_general(
-        both[:, :feature_dim],
-        both[:, feature_dim:],
-        (((0,), (0,)), ((), ())),
-        preferred_element_type=F32,
-    )
-
     def backward_kernel(distances, residual_ref, inv_ref, gate_save, up_save, *refs):
         grad_ref, gain_ref, wide_ref, down_ref, *outs = refs
         residual, inv_rms = residual_ref[...], inv_ref[:, :1]
@@ -489,7 +478,7 @@
 
     for distances in reversed(list(tokens_at)):
         backward(distances)
-    (top_left, top_right), (bottom_left, bottom_right) = ring.scatter(back_at)
+    (top_left, top_right), (bottom_left, bottom_right), last = ring.scatter(back_at)
     token_grad = pl.pallas_call(
         sum_kernel,
         out_shape=jax.ShapeDtypeStruct(block, BF16),
@@ -497,6 +486,18 @@
         out_specs=pl.BlockSpec(memory_space=pltpu.VMEM),
         compiler_params=pltpu.CompilerParams(vmem_limit_bytes=VMEM_LIMIT),
     )(back_at[0][0], top_left, top_right, back_at[0][1], bottom_left, bottom_right)
+
+    both = after(jnp.concatenate([pooled, logit_grad], axis=1), [last])
+    if group_count == 2:
+        both = jnp.concatenate([both, lax.ppermute(both, "group", [(0, 1), (1, 0)])], axis=0)
+    else:
+        both = lax.all_gather(both, "group", axis=0, tiled=True)
+    head_grad = lax.dot_general(
+        both[:, :feature_dim],
+        both[:, feature_dim:],
+        (((0,), (0,)), ((), ())),
+        preferred_element_type=F32,
+    )
     return (token_grad, head_grad)
 
 

time: 123 us -> 126 us (1.024)
  waiting for transfers between devices: 29.2 us -> 32.3 us
    ppermute x56, waiting for transfers between devices: 25.8 us -> 28.6 us  [send(): return lax.ppermute(value, 'expert', pairs)]
  transfers between devices with their start and end apart: 62 -> 62, of which waited for: 28 -> 29; matrix products, arithmetic and copies ran while one was open for 1% -> 1% of each run, Pallas kernels for 14% -> 14%
where the time goes in v22:
time: 126 us
  starting transfers between devices  68.8 us (55%)
  waiting for transfers between devices  32.3 us (26%)
  Pallas kernels  21.8 us (17%)
  matrix products  1.71 us (1%)
    ppermute x56, starting transfers between devices, send(): return lax.ppermute(value, 'expert', pairs)  62.4 us
    ppermute x56, waiting for transfers between devices, send(): return lax.ppermute(value, 'expert', pairs)  28.6 us
    pallas_call x39, Pallas kernels, call(): pl.pallas_call(kernel, out_shape=[pltpu.VMEM(shape, dtype) for shape, dty...  17.3 us
    ppermute x4, starting transfers between devices, body(): pooled_grad = pooled_grad + lax.ppermute(mine, 'expert', pairs).astype(F32)  5.86 us
    ppermute x4, waiting for transfers between devices, body(): pooled_grad = pooled_grad + lax.ppermute(mine, 'expert', pairs).astype(F32)  3.68 us
  transfers between devices with their start and end apart: 62, of which 29 were waited for; matrix products, arithmetic and copies ran while one was open for 1% of the time, Pallas kernels for 14%

profile of v22, /device:TPU:0, one launch (start us, length us, event | category | flops | bytes accessed | tf_op | source)
XLA Modules:
  0.0 125.8 jit_solution(10098319216174236374)
XLA Ops:
  0.6 1.9 %shard_map.104 = (bf16[64,1152]{1,0:T(8,128)(2,1)S(1)}, bf16[64,1024]{1,0:T(8,128)(2,1)S(1)}, bf16[3200,384]{1,0:T(8,128)(2,1)S(1)}) custom-call(s32[8,128]{1,0:T(8,128)} %bitcast.19, f32[8,128]{1,0:T(8,128)} %bitcast.20, bf16[128,1024]{1,0:T(8,128)(2,1)} %refs_2_.2, bf16[2,512,384]{2,1,0:T(8,128)(2,1)} %refs_0_.1, bf16[2,512,384]{2,1,0:T(8,128)(2,1)} %refs_1_.1, ...), custom_call_target="tpu_custom_call" | custom-call | tf_op jit(solution)/shard_map/pallas_call | solution.py:216
  3.1 2.6 %collective-permute-start.1 = (bf16[64,1152]{1,0:T(8,128)(2,1)S(1)}, bf16[64,1152]{1,0:T(8,128)(2,1)S(1)}, u32[]{:S(2)}, u32[]{:S(2)}) collective-permute-start(bf16[64,1152]{1,0:T(8,128)(2,1)S(1)} %get-tuple-element.64.refs_0_), channel_id=1, source_target_pairs={{0,4},{4,8},{8,12},{12,14},{14,10},{10,6},{6,2},{2,0},{1,5},{5,9},... | collective-permute-start | bytes 442376 | tf_op jit(solution)/shard_map/ppermute | solution.py:68
  5.7 4.4 %collective-permute-done.1.refs_0_ = bf16[64,1152]{1,0:T(8,128)(2,1)S(1)} collective-permute-done((bf16[64,1152]{1,0:T(8,128)(2,1)S(1)}, bf16[64,1152]{1,0:T(8,128)(2,1)S(1)}, u32[]{:S(2)}, u32[]{:S(2)}) %collective-permute-start.1) | collective-permute-done | bytes 147488 | tf_op jit(solution)/shard_map/ppermute | solution.py:68
  10.1 1.8 %collective-permute-start.5 = (bf16[64,1152]{1,0:T(8,128)(2,1)S(1)}, bf16[64,1152]{1,0:T(8,128)(2,1)S(1)}, u32[]{:S(2)}, u32[]{:S(2)}) collective-permute-start(bf16[64,1152]{1,0:T(8,128)(2,1)S(1)} %collective-permute-done.1.refs_0_), channel_id=1, source_target_pairs={{0,4},{4,8},{8,12},{12,14},{14,10},{10,6},{6,2},{2,0},{1,5},{5,9},... | collective-permute-start | bytes 442376 | tf_op jit(solution)/shard_map/ppermute | solution.py:68
  12.1 1.7 %collective-permute-start.3 = (bf16[64,1152]{1,0:T(8,128)(2,1)S(1)}, bf16[64,1152]{1,0:T(8,128)(2,1)S(1)}, u32[]{:S(2)}, u32[]{:S(2)}) collective-permute-start(bf16[64,1152]{1,0:T(8,128)(2,1)S(1)} %get-tuple-element.64.refs_0_), channel_id=1, source_target_pairs={{0,2},{4,0},{8,4},{12,8},{14,12},{10,14},{6,10},{2,6},{1,3},{5,1},... | collective-permute-start | bytes 442376 | tf_op jit(solution)/shard_map/ppermute | solution.py:68
  14.2 2.0 %collective-permute-done.5.refs_0_ = bf16[64,1152]{1,0:T(8,128)(2,1)S(1)} collective-permute-done((bf16[64,1152]{1,0:T(8,128)(2,1)S(1)}, bf16[64,1152]{1,0:T(8,128)(2,1)S(1)}, u32[]{:S(2)}, u32[]{:S(2)}) %collective-permute-start.5) | collective-permute-done | bytes 147488 | tf_op jit(solution)/shard_map/ppermute | solution.py:68
  16.2 2.5 %collective-permute-start.9 = (bf16[64,1152]{1,0:T(8,128)(2,1)S(1)}, bf16[64,1152]{1,0:T(8,128)(2,1)S(1)}, u32[]{:S(2)}, u32[]{:S(2)}) collective-permute-start(bf16[64,1152]{1,0:T(8,128)(2,1)S(1)} %collective-permute-done.5.refs_0_), channel_id=1, source_target_pairs={{0,4},{4,8},{8,12},{12,14},{14,10},{10,6},{6,2},{2,0},{1,5},{5,9},... | collective-permute-start | bytes 442376 | tf_op jit(solution)/shard_map/ppermute | solution.py:68
  18.7 2.6 %collective-permute-done.3.refs_2_ = bf16[64,1152]{1,0:T(8,128)(2,1)S(1)} collective-permute-done((bf16[64,1152]{1,0:T(8,128)(2,1)S(1)}, bf16[64,1152]{1,0:T(8,128)(2,1)S(1)}, u32[]{:S(2)}, u32[]{:S(2)}) %collective-permute-start.3) | collective-permute-done | bytes 147488 | tf_op jit(solution)/shard_map/ppermute | solution.py:68
  21.4 1.9 %collective-permute-start.6 = (bf16[64,1024]{1,0:T(8,128)(2,1)S(1)}, bf16[64,1024]{1,0:T(8,128)(2,1)S(1)}, u32[]{:S(2)}, u32[]{:S(2)}) collective-permute-start(bf16[64,1024]{1,0:T(8,128)(2,1)S(1)} %collective-permute-done.2.refs_1_), channel_id=1, source_target_pairs={{0,4},{4,8},{8,12},{12,14},{14,10},{10,6},{6,2},{2,0},{1,5},{5,9},... | collective-permute-start | bytes 393224 | tf_op jit(solution)/shard_map/ppermute | solution.py:68
  23.3 1.8 %collective-permute-start.13 = (bf16[64,1152]{1,0:T(8,128)(2,1)S(1)}, bf16[64,1152]{1,0:T(8,128)(2,1)S(1)}, u32[]{:S(2)}, u32[]{:S(2)}) collective-permute-start(bf16[64,1152]{1,0:T(8,128)(2,1)S(1)} %collective-permute-done.9.refs_0_), channel_id=1, source_target_pairs={{0,4},{4,8},{8,12},{12,14},{14,10},{10,6},{6,2},{2,0},{1,5},{5,9},... | collective-permute-start | bytes 442376 | tf_op jit(solution)/shard_map/ppermute | solution.py:68
  25.3 1.9 %collective-permute-done.7.refs_2_ = bf16[64,1152]{1,0:T(8,128)(2,1)S(1)} collective-permute-done((bf16[64,1152]{1,0:T(8,128)(2,1)S(1)}, bf16[64,1152]{1,0:T(8,128)(2,1)S(1)}, u32[]{:S(2)}, u32[]{:S(2)}) %collective-permute-start.7) | collective-permute-done | bytes 147488 | tf_op jit(solution)/shard_map/ppermute | solution.py:68
  27.3 1.8 %shard_map.105 = (bf16[1024,1536]{1,0:T(8,128)(2,1)S(1)}, bf16[768,1024]{1,0:T(8,128)(2,1)S(1)}) custom-call(bf16[2,512,384]{2,1,0:T(8,128)(2,1)} %refs_0_.1, bf16[2,512,384]{2,1,0:T(8,128)(2,1)} %refs_1_.1, bf16[2,192,1024]{2,1,0:T(8,128)(2,1)} %refs_2_.3, bf16[3200,384]{1,0:T(8,128)(2,1)S(1)} %collective-permute-done.refs_3_), custom_call_target="tpu_custom_call" | custom-call | tf_op jit(solution)/shard_map/pallas_call | solution.py:271
  32.2 1.6 %collective-permute-start.15 = (bf16[64,1024]{1,0:T(8,128)(2,1)S(1)}, bf16[64,1024]{1,0:T(8,128)(2,1)S(1)}, u32[]{:S(2)}, u32[]{:S(2)}) collective-permute-start(bf16[64,1024]{1,0:T(8,128)(2,1)S(1)} %get-tuple-element.73), channel_id=1, source_target_pairs={{0,4},{4,8},{8,12},{12,14},{14,10},{10,6},{6,2},{2,0},{1,5},{5,9},... | collective-permute-start | bytes 393224 | tf_op jit(solution)/shard_map/ppermute | solution.py:68
  48.2 1.7 %collective-permute-start.27 = (bf16[64,1024]{1,0:T(8,128)(2,1)S(1)}, bf16[64,1024]{1,0:T(8,128)(2,1)S(1)}, u32[]{:S(2)}, u32[]{:S(2)}) collective-permute-start(bf16[64,1024]{1,0:T(8,128)(2,1)S(1)} %shard_map.121), channel_id=1, source_target_pairs={{0,2},{4,0},{8,4},{12,8},{14,12},{10,14},{6,10},{2,6},{1,3},{5,1},... | collective-permute-start | bytes 393224 | tf_op jit(solution)/shard_map/ppermute | solution.py:68
  51.6 2.1 %collective-permute-start.18 = (bf16[64,1024]{1,0:T(8,128)(2,1)S(1)}, bf16[64,1024]{1,0:T(8,128)(2,1)S(1)}, u32[]{:S(2)}, u32[]{:S(2)}) collective-permute-start(bf16[64,1024]{1,0:T(8,128)(2,1)S(1)} %shard_map.114), channel_id=1, source_target_pairs={{0,4},{4,8},{8,12},{12,14},{14,10},{10,6},{6,2},{2,0},{1,5},{5,9},... | collective-permute-start | bytes 393224 | tf_op jit(solution)/shard_map/ppermute | solution.py:68
  54.3 2.1 %collective-permute-start.28 = (bf16[64,1024]{1,0:T(8,128)(2,1)S(1)}, bf16[64,1024]{1,0:T(8,128)(2,1)S(1)}, u32[]{:S(2)}, u32[]{:S(2)}) collective-permute-start(bf16[64,1024]{1,0:T(8,128)(2,1)S(1)} %shard_map.122), channel_id=1, source_target_pairs={{0,2},{4,0},{8,4},{12,8},{14,12},{10,14},{6,10},{2,6},{1,3},{5,1},... | collective-permute-start | bytes 393224 | tf_op jit(solution)/shard_map/ppermute | solution.py:68
  57.9 2.1 %collective-permute-start.29 = (bf16[64,1024]{1,0:T(8,128)(2,1)S(1)}, bf16[64,1024]{1,0:T(8,128)(2,1)S(1)}, u32[]{:S(2)}, u32[]{:S(2)}) collective-permute-start(bf16[64,1024]{1,0:T(8,128)(2,1)S(1)} %shard_map.117.refs_2_), channel_id=1, source_target_pairs={{0,4},{4,8},{8,12},{12,14},{14,10},{10,6},{6,2},{2,0},{1,5},{5,9},... | collective-permute-start | bytes 393224 | tf_op jit(solution)/shard_map/ppermute | solution.py:68
  64.2 2.2 %collective-permute-start.30 = (bf16[64,1024]{1,0:T(8,128)(2,1)S(1)}, bf16[64,1024]{1,0:T(8,128)(2,1)S(1)}, u32[]{:S(2)}, u32[]{:S(2)}) collective-permute-start(bf16[64,1024]{1,0:T(8,128)(2,1)S(1)} %collective-permute-done.29.refs_4_), channel_id=1, source_target_pairs={{0,4},{4,8},{8,12},{12,14},{14,10},{10,6},{6,2},{2,0},{1,5},{5,9},... | collective-permute-start | bytes 393224 | tf_op jit(solution)/shard_map/ppermute | solution.py:68
  69.6 1.7 %collective-permute-start.41 = (bf16[64,1024]{1,0:T(8,128)(2,1)S(1)}, bf16[64,1024]{1,0:T(8,128)(2,1)S(1)}, u32[]{:S(2)}, u32[]{:S(2)}) collective-permute-start(bf16[64,1024]{1,0:T(8,128)(2,1)S(1)} %collective-permute-done.40.refs_6_), channel_id=1, source_target_pairs={{0,2},{4,0},{8,4},{12,8},{14,12},{10,14},{6,10},{2,6},{1,3},{5,1},... | collective-permute-start | bytes 393224 | tf_op jit(solution)/shard_map/ppermute | solution.py:68
  74.6 1.7 %collective-permute-start.42 = (bf16[64,1024]{1,0:T(8,128)(2,1)S(1)}, bf16[64,1024]{1,0:T(8,128)(2,1)S(1)}, u32[]{:S(2)}, u32[]{:S(2)}) collective-permute-start(bf16[64,1024]{1,0:T(8,128)(2,1)S(1)} %collective-permute-done.41.refs_6_), channel_id=1, source_target_pairs={{0,2},{4,0},{8,4},{12,8},{14,12},{10,14},{6,10},{2,6},{1,3},{5,1},... | collective-permute-start | bytes 393224 | tf_op jit(solution)/shard_map/ppermute | solution.py:68
  85.6 2.4 %collective-permute-done.43 = bf16[8,1024]{1,0:T(8,128)(2,1)S(1)} collective-permute-done((bf16[8,1024]{1,0:T(8,128)(2,1)S(1)}, bf16[8,1024]{1,0:T(8,128)(2,1)S(1)}, u32[]{:S(2)}, u32[]{:S(2)}) %collective-permute-start.43) | collective-permute-done | bytes 16416 | tf_op jit(solution)/shard_map/ppermute | solution.py:436
  88.0 2.8 %collective-permute-start.46 = (bf16[8,1024]{1,0:T(8,128)(2,1)S(1)}, bf16[8,1024]{1,0:T(8,128)(2,1)S(1)}, u32[]{:S(2)}, u32[]{:S(2)}) collective-permute-start(bf16[8,1024]{1,0:T(8,128)(2,1)S(1)} %add_convert_fusion), channel_id=1, source_target_pairs={{0,12},{2,14},{4,8},{6,10},{8,4},{10,6},{12,0},{14,2},{1,13},{3,15... | collective-permute-start | bytes 49160 | tf_op jit(solution)/shard_map/ppermute | solution.py:436
  90.8 1.6 %collective-permute-start.44 = (bf16[8,1024]{1,0:T(8,128)(2,1)S(1)}, bf16[8,1024]{1,0:T(8,128)(2,1)S(1)}, u32[]{:S(2)}, u32[]{:S(2)}) collective-permute-start(bf16[8,1024]{1,0:T(8,128)(2,1)S(1)} %add_convert_fusion), channel_id=1, source_target_pairs={{0,4},{2,6},{4,0},{6,2},{8,12},{10,14},{12,8},{14,10},{1,5},{3,7},... | collective-permute-start | bytes 49160 | tf_op jit(solution)/shard_map/ppermute | solution.py:436
  123.0 2.1 %collective-permute-done.50.refs_1_ = bf16[64,1024]{1,0:T(8,128)(2,1)S(1)} collective-permute-done((bf16[64,1024]{1,0:T(8,128)(2,1)S(1)}, bf16[64,1024]{1,0:T(8,128)(2,1)S(1)}, u32[]{:S(2)}, u32[]{:S(2)}) %collective-permute-start.50) | collective-permute-done | bytes 131104 | tf_op jit(solution)/shard_map/ppermute | solution.py:68
  (159 shorter events, 73.7 us)
Async XLA Ops:
  2.6 24.7 %collective-permute-start = (bf16[3200,384]{1,0:T(8,128)(2,1)S(1)}, bf16[3200,384]{1,0:T(8,128)(2,1)S(1)}, u32[]{:S(2)}, u32[]{:S(2)}) collective-permute-start(bf16[3200,384]{1,0:T(8,128)(2,1)S(1)} %get-tuple-element.66), channel_id=1, source_target_pairs={{0,1},{1,0},{2,3},{3,2},{4,5},{5,4},{6,7},{7,6},{8,9},{9,8},{10,11... | collective-permute-start | bytes 7372808 | tf_op jit(solution)/shard_map/ppermute | solution.py:311
  3.1 7.0 %collective-permute-start.1 = (bf16[64,1152]{1,0:T(8,128)(2,1)S(1)}, bf16[64,1152]{1,0:T(8,128)(2,1)S(1)}, u32[]{:S(2)}, u32[]{:S(2)}) collective-permute-start(bf16[64,1152]{1,0:T(8,128)(2,1)S(1)} %get-tuple-element.64.refs_0_), channel_id=1, source_target_pairs={{0,4},{4,8},{8,12},{12,14},{14,10},{10,6},{6,2},{2,0},{1,5},{5,9},... | collective-permute-start | bytes 442376 | tf_op jit(solution)/shard_map/ppermute | solution.py:68
  11.9 6.8 %collective-permute-start.8 = (bf16[64,1024]{1,0:T(8,128)(2,1)S(1)}, bf16[64,1024]{1,0:T(8,128)(2,1)S(1)}, u32[]{:S(2)}, u32[]{:S(2)}) collective-permute-start(bf16[64,1024]{1,0:T(8,128)(2,1)S(1)} %collective-permute-done.4.refs_3_), channel_id=1, source_target_pairs={{0,2},{4,0},{8,4},{12,8},{14,12},{10,14},{6,10},{2,6},{1,3},{5,1},... | collective-permute-start | bytes 393224 | tf_op jit(solution)/shard_map/ppermute | solution.py:68
  12.1 9.1 %collective-permute-start.3 = (bf16[64,1152]{1,0:T(8,128)(2,1)S(1)}, bf16[64,1152]{1,0:T(8,128)(2,1)S(1)}, u32[]{:S(2)}, u32[]{:S(2)}) collective-permute-start(bf16[64,1152]{1,0:T(8,128)(2,1)S(1)} %get-tuple-element.64.refs_0_), channel_id=1, source_target_pairs={{0,2},{4,0},{8,4},{12,8},{14,12},{10,14},{6,10},{2,6},{1,3},{5,1},... | collective-permute-start | bytes 442376 | tf_op jit(solution)/shard_map/ppermute | solution.py:68
  13.9 7.6 %collective-permute-start.2 = (bf16[64,1024]{1,0:T(8,128)(2,1)S(1)}, bf16[64,1024]{1,0:T(8,128)(2,1)S(1)}, u32[]{:S(2)}, u32[]{:S(2)}) collective-permute-start(bf16[64,1024]{1,0:T(8,128)(2,1)S(1)} %get-tuple-element.65.refs_1_), channel_id=1, source_target_pairs={{0,4},{4,8},{8,12},{12,14},{14,10},{10,6},{6,2},{2,0},{1,5},{5,9},... | collective-permute-start | bytes 393224 | tf_op jit(solution)/shard_map/ppermute | solution.py:68
  16.2 7.1 %collective-permute-start.9 = (bf16[64,1152]{1,0:T(8,128)(2,1)S(1)}, bf16[64,1152]{1,0:T(8,128)(2,1)S(1)}, u32[]{:S(2)}, u32[]{:S(2)}) collective-permute-start(bf16[64,1152]{1,0:T(8,128)(2,1)S(1)} %collective-permute-done.5.refs_0_), channel_id=1, source_target_pairs={{0,4},{4,8},{8,12},{12,14},{14,10},{10,6},{6,2},{2,0},{1,5},{5,9},... | collective-permute-start | bytes 442376 | tf_op jit(solution)/shard_map/ppermute | solution.py:68
  21.4 8.2 %collective-permute-start.6 = (bf16[64,1024]{1,0:T(8,128)(2,1)S(1)}, bf16[64,1024]{1,0:T(8,128)(2,1)S(1)}, u32[]{:S(2)}, u32[]{:S(2)}) collective-permute-start(bf16[64,1024]{1,0:T(8,128)(2,1)S(1)} %collective-permute-done.2.refs_1_), channel_id=1, source_target_pairs={{0,4},{4,8},{8,12},{12,14},{14,10},{10,6},{6,2},{2,0},{1,5},{5,9},... | collective-permute-start | bytes 393224 | tf_op jit(solution)/shard_map/ppermute | solution.py:68
  23.3 7.8 %collective-permute-start.13 = (bf16[64,1152]{1,0:T(8,128)(2,1)S(1)}, bf16[64,1152]{1,0:T(8,128)(2,1)S(1)}, u32[]{:S(2)}, u32[]{:S(2)}) collective-permute-start(bf16[64,1152]{1,0:T(8,128)(2,1)S(1)} %collective-permute-done.9.refs_0_), channel_id=1, source_target_pairs={{0,4},{4,8},{8,12},{12,14},{14,10},{10,6},{6,2},{2,0},{1,5},{5,9},... | collective-permute-start | bytes 442376 | tf_op jit(solution)/shard_map/ppermute | solution.py:68
  33.8 8.0 %collective-permute-start.25 = (bf16[64,1024]{1,0:T(8,128)(2,1)S(1)}, bf16[64,1024]{1,0:T(8,128)(2,1)S(1)}, u32[]{:S(2)}, u32[]{:S(2)}) collective-permute-start(bf16[64,1024]{1,0:T(8,128)(2,1)S(1)} %get-tuple-element.84), channel_id=1, source_target_pairs={{0,2},{4,0},{8,4},{12,8},{14,12},{10,14},{6,10},{2,6},{1,3},{5,1},... | collective-permute-start | bytes 393224 | tf_op jit(solution)/shard_map/ppermute | solution.py:68
  36.3 7.5 %collective-permute-start.19 = (bf16[64,1024]{1,0:T(8,128)(2,1)S(1)}, bf16[64,1024]{1,0:T(8,128)(2,1)S(1)}, u32[]{:S(2)}, u32[]{:S(2)}) collective-permute-start(bf16[64,1024]{1,0:T(8,128)(2,1)S(1)} %get-tuple-element.76), channel_id=1, source_target_pairs={{0,2},{4,0},{8,4},{12,8},{14,12},{10,14},{6,10},{2,6},{1,3},{5,1},... | collective-permute-start | bytes 393224 | tf_op jit(solution)/shard_map/ppermute | solution.py:68
  40.2 7.5 %collective-permute-start.22 = (bf16[64,1024]{1,0:T(8,128)(2,1)S(1)}, bf16[64,1024]{1,0:T(8,128)(2,1)S(1)}, u32[]{:S(2)}, u32[]{:S(2)}) collective-permute-start(bf16[64,1024]{1,0:T(8,128)(2,1)S(1)} %get-tuple-element.80), channel_id=1, source_target_pairs={{0,4},{4,8},{8,12},{12,14},{14,10},{10,6},{6,2},{2,0},{1,5},{5,9},... | collective-permute-start | bytes 393224 | tf_op jit(solution)/shard_map/ppermute | solution.py:68
  43.9 7.6 %collective-permute-start.20 = (bf16[64,1024]{1,0:T(8,128)(2,1)S(1)}, bf16[64,1024]{1,0:T(8,128)(2,1)S(1)}, u32[]{:S(2)}, u32[]{:S(2)}) collective-permute-start(bf16[64,1024]{1,0:T(8,128)(2,1)S(1)} %shard_map.115), channel_id=1, source_target_pairs={{0,2},{4,0},{8,4},{12,8},{14,12},{10,14},{6,10},{2,6},{1,3},{5,1},... | collective-permute-start | bytes 393224 | tf_op jit(solution)/shard_map/ppermute | solution.py:68
  45.0 6.5 %collective-permute-start.17 = (bf16[64,1024]{1,0:T(8,128)(2,1)S(1)}, bf16[64,1024]{1,0:T(8,128)(2,1)S(1)}, u32[]{:S(2)}, u32[]{:S(2)}) collective-permute-start(bf16[64,1024]{1,0:T(8,128)(2,1)S(1)} %shard_map.113), channel_id=1, source_target_pairs={{0,4},{4,8},{8,12},{12,14},{14,10},{10,6},{6,2},{2,0},{1,5},{5,9},... | collective-permute-start | bytes 393224 | tf_op jit(solution)/shard_map/ppermute | solution.py:68
  54.3 6.5 %collective-permute-start.28 = (bf16[64,1024]{1,0:T(8,128)(2,1)S(1)}, bf16[64,1024]{1,0:T(8,128)(2,1)S(1)}, u32[]{:S(2)}, u32[]{:S(2)}) collective-permute-start(bf16[64,1024]{1,0:T(8,128)(2,1)S(1)} %shard_map.122), channel_id=1, source_target_pairs={{0,2},{4,0},{8,4},{12,8},{14,12},{10,14},{6,10},{2,6},{1,3},{5,1},... | collective-permute-start | bytes 393224 | tf_op jit(solution)/shard_map/ppermute | solution.py:68
  62.2 7.5 %collective-permute-start.40 = (bf16[64,1024]{1,0:T(8,128)(2,1)S(1)}, bf16[64,1024]{1,0:T(8,128)(2,1)S(1)}, u32[]{:S(2)}, u32[]{:S(2)}) collective-permute-start(bf16[64,1024]{1,0:T(8,128)(2,1)S(1)} %shard_map.117.refs_2_), channel_id=1, source_target_pairs={{0,2},{4,0},{8,4},{12,8},{14,12},{10,14},{6,10},{2,6},{1,3},{5,1},... | collective-permute-start | bytes 393224 | tf_op jit(solution)/shard_map/ppermute | solution.py:68
  63.3 8.1 %collective-permute-start.37 = (bf16[64,1024]{1,0:T(8,128)(2,1)S(1)}, bf16[64,1024]{1,0:T(8,128)(2,1)S(1)}, u32[]{:S(2)}, u32[]{:S(2)}) collective-permute-start(bf16[64,1024]{1,0:T(8,128)(2,1)S(1)} %shard_map.123.refs_3_), channel_id=1, source_target_pairs={{0,4},{4,8},{8,12},{12,14},{14,10},{10,6},{6,2},{2,0},{1,5},{5,9},... | collective-permute-start | bytes 393224 | tf_op jit(solution)/shard_map/ppermute | solution.py:68
  64.2 8.3 %collective-permute-start.30 = (bf16[64,1024]{1,0:T(8,128)(2,1)S(1)}, bf16[64,1024]{1,0:T(8,128)(2,1)S(1)}, u32[]{:S(2)}, u32[]{:S(2)}) collective-permute-start(bf16[64,1024]{1,0:T(8,128)(2,1)S(1)} %collective-permute-done.29.refs_4_), channel_id=1, source_target_pairs={{0,4},{4,8},{8,12},{12,14},{14,10},{10,6},{6,2},{2,0},{1,5},{5,9},... | collective-permute-start | bytes 393224 | tf_op jit(solution)/shard_map/ppermute | solution.py:68
  97.4 8.7 %collective-permute-start.57 = (bf16[64,1024]{1,0:T(8,128)(2,1)S(1)}, bf16[64,1024]{1,0:T(8,128)(2,1)S(1)}, u32[]{:S(2)}, u32[]{:S(2)}) collective-permute-start(bf16[64,1024]{1,0:T(8,128)(2,1)S(1)} %get-tuple-element.125), channel_id=1, source_target_pairs={{0,2},{4,0},{8,4},{12,8},{14,12},{10,14},{6,10},{2,6},{1,3},{5,1},... | collective-permute-start | bytes 393224 | tf_op jit(solution)/shard_map/ppermute | solution.py:68
  107.6 6.6 %collective-permute-start.49 = (bf16[64,1024]{1,0:T(8,128)(2,1)S(1)}, bf16[64,1024]{1,0:T(8,128)(2,1)S(1)}, u32[]{:S(2)}, u32[]{:S(2)}) collective-permute-start(bf16[64,1024]{1,0:T(8,128)(2,1)S(1)} %shard_map.137), channel_id=1, source_target_pairs={{0,4},{4,8},{8,12},{12,14},{14,10},{10,6},{6,2},{2,0},{1,5},{5,9},... | collective-permute-start | bytes 393224 | tf_op jit(solution)/shard_map/ppermute | solution.py:68
  108.4 7.0 %collective-permute-start.52 = (bf16[64,1024]{1,0:T(8,128)(2,1)S(1)}, bf16[64,1024]{1,0:T(8,128)(2,1)S(1)}, u32[]{:S(2)}, u32[]{:S(2)}) collective-permute-start(bf16[64,1024]{1,0:T(8,128)(2,1)S(1)} %shard_map.139), channel_id=1, source_target_pairs={{0,2},{4,0},{8,4},{12,8},{14,12},{10,14},{6,10},{2,6},{1,3},{5,1},... | collective-permute-start | bytes 393224 | tf_op jit(solution)/shard_map/ppermute | solution.py:68
  109.8 6.8 %collective-permute-start.55 = (bf16[64,1024]{1,0:T(8,128)(2,1)S(1)}, bf16[64,1024]{1,0:T(8,128)(2,1)S(1)}, u32[]{:S(2)}, u32[]{:S(2)}) collective-permute-start(bf16[64,1024]{1,0:T(8,128)(2,1)S(1)} %shard_map.141), channel_id=1, source_target_pairs={{0,4},{4,8},{8,12},{12,14},{14,10},{10,6},{6,2},{2,0},{1,5},{5,9},... | collective-permute-start | bytes 393224 | tf_op jit(solution)/shard_map/ppermute | solution.py:68
  111.2 7.1 %collective-permute-start.59 = (bf16[64,1024]{1,0:T(8,128)(2,1)S(1)}, bf16[64,1024]{1,0:T(8,128)(2,1)S(1)}, u32[]{:S(2)}, u32[]{:S(2)}) collective-permute-start(bf16[64,1024]{1,0:T(8,128)(2,1)S(1)} %shard_map.144), channel_id=1, source_target_pairs={{0,2},{4,0},{8,4},{12,8},{14,12},{10,14},{6,10},{2,6},{1,3},{5,1},... | collective-permute-start | bytes 393224 | tf_op jit(solution)/shard_map/ppermute | solution.py:68
  117.6 7.4 %collective-permute-start.50 = (bf16[64,1024]{1,0:T(8,128)(2,1)S(1)}, bf16[64,1024]{1,0:T(8,128)(2,1)S(1)}, u32[]{:S(2)}, u32[]{:S(2)}) collective-permute-start(bf16[64,1024]{1,0:T(8,128)(2,1)S(1)} %shard_map.138.refs_1_), channel_id=1, source_target_pairs={{0,4},{4,8},{8,12},{12,14},{14,10},{10,6},{6,2},{2,0},{1,5},{5,9},... | collective-permute-start | bytes 393224 | tf_op jit(solution)/shard_map/ppermute | solution.py:68
  118.4 6.7 %collective-permute-start.60 = (bf16[64,1024]{1,0:T(8,128)(2,1)S(1)}, bf16[64,1024]{1,0:T(8,128)(2,1)S(1)}, u32[]{:S(2)}, u32[]{:S(2)}) collective-permute-start(bf16[64,1024]{1,0:T(8,128)(2,1)S(1)} %shard_map.145), channel_id=1, source_target_pairs={{0,2},{4,0},{8,4},{12,8},{14,12},{10,14},{6,10},{2,6},{1,3},{5,1},... | collective-permute-start | bytes 393224 | tf_op jit(solution)/shard_map/ppermute | solution.py:68
  (41 other events, 350.0 us)

commit v23 on v16

--- a/solution.py
+++ b/solution.py
@@ -55,6 +55,7 @@
     def __init__(self, expert_count, group_count):
         self.count = expert_count
         self.half = expert_count // 2
+        self.groups = group_count
         self.snake = group_count == 2
         if self.snake:
             self.order = list(range(0, expert_count, 2)) + list(range(expert_count - 1, 0, -2))
@@ -62,17 +63,21 @@
             self.order = list(range(expert_count))
 
     def send(self, value, distance):
-        pairs = [
-            (self.order[i], self.order[(i + distance) % self.count]) for i in range(self.count)
-        ]
-        return lax.ppermute(value, "expert", pairs)
+        pairs = []
+        for i in range(self.count):
+            for g in range(self.groups):
+                there = self.order[(i + (-distance if g % 2 else distance)) % self.count]
+                pairs.append((self.order[i] * self.groups + g, there * self.groups + g))
+        return lax.ppermute(value, ("expert", "group"), pairs)
 
     def device_at(self, distance):
         here = lax.axis_index("expert")
         count = self.count
         if self.snake:
             here = jnp.where(here % 2 == 0, here // 2, count - 1 - here // 2)
-        there = lax.rem(here + distance % count, count)
+        ahead = distance % count
+        step = jnp.where(lax.rem(lax.axis_index("group"), 2) == 0, ahead, count - ahead)
+        there = lax.rem(here + step, count)
         if self.snake:
             there = jnp.where(there < self.half, 2 * there, 2 * (count - 1 - there) + 1)
         return there

time: 123 us -> 124 us (level)
  waiting for transfers between devices: 29.2 us -> 32.2 us
  starting transfers between devices: 69.1 us -> 66.5 us
    ppermute x56, waiting for transfers between devices: 25.8 us -> 28.3 us  [send(): return lax.ppermute(value, ('expert', 'group'), pairs)]
    ppermute x56, starting transfers between devices: 62.6 us -> 60.8 us  [send(): return lax.ppermute(value, ('expert', 'group'), pairs)]
  transfers between devices with their start and end apart: 62 -> 62, of which waited for: 28 -> 22; matrix products, arithmetic and copies ran while one was open for 1% -> 1% of each run, Pallas kernels for 14% -> 14%
where the time goes in v23:
time: 124 us; the launch traced here: 123 us
  starting transfers between devices  66.5 us (54%)
  waiting for transfers between devices  32.2 us (26%)
  Pallas kernels  21.8 us (18%)
  matrix products  1.71 us (1%)
    ppermute x56, starting transfers between devices, send(): return lax.ppermute(value, ('expert', 'group'), pairs)  60.8 us
    ppermute x56, waiting for transfers between devices, send(): return lax.ppermute(value, ('expert', 'group'), pairs)  28.3 us
    pallas_call x39, Pallas kernels, call(): pl.pallas_call(kernel, out_shape=[pltpu.VMEM(shape, dtype) for shape, dty...  17.4 us
    ppermute x4, starting transfers between devices, body(): pooled_grad = pooled_grad + lax.ppermute(mine, 'expert', pairs).astype(F32)  5.13 us
    ppermute x4, waiting for transfers between devices, body(): pooled_grad = pooled_grad + lax.ppermute(mine, 'expert', pairs).astype(F32)  3.89 us
  transfers between devices with their start and end apart: 62, of which 22 were waited for; matrix products, arithmetic and copies ran while one was open for 1% of the time, Pallas kernels for 14%

profile of v23, /device:TPU:0, one launch (start us, length us, event | category | flops | bytes accessed | tf_op | source)
XLA Modules:
  0.0 123.4 jit_solution(13471067874167503733)
XLA Ops:
  0.6 1.9 %shard_map.104 = (bf16[64,1152]{1,0:T(8,128)(2,1)S(1)}, bf16[64,1024]{1,0:T(8,128)(2,1)S(1)}, bf16[3200,384]{1,0:T(8,128)(2,1)S(1)}) custom-call(s32[8,128]{1,0:T(8,128)} %bitcast.19, f32[8,128]{1,0:T(8,128)} %bitcast.20, bf16[128,1024]{1,0:T(8,128)(2,1)} %refs_2_.2, bf16[2,512,384]{2,1,0:T(8,128)(2,1)} %refs_0_.1, bf16[2,512,384]{2,1,0:T(8,128)(2,1)} %refs_1_.1, ...), custom_call_target="tpu_custom_call" | custom-call | tf_op jit(solution)/shard_map/pallas_call | solution.py:220
  3.1 2.6 %collective-permute-start.1 = (bf16[64,1152]{1,0:T(8,128)(2,1)S(1)}, bf16[64,1152]{1,0:T(8,128)(2,1)S(1)}, u32[]{:S(2)}, u32[]{:S(2)}) collective-permute-start(bf16[64,1152]{1,0:T(8,128)(2,1)S(1)} %get-tuple-element.64.refs_0_), channel_id=1, source_target_pairs={{0,4},{1,3},{4,8},{5,1},{8,12},{9,5},{12,14},{13,9},{14,10},{15,13... | collective-permute-start | bytes 442376 | tf_op jit(solution)/shard_map/ppermute | solution.py:71
  5.7 3.5 %collective-permute-done.1.refs_0_ = bf16[64,1152]{1,0:T(8,128)(2,1)S(1)} collective-permute-done((bf16[64,1152]{1,0:T(8,128)(2,1)S(1)}, bf16[64,1152]{1,0:T(8,128)(2,1)S(1)}, u32[]{:S(2)}, u32[]{:S(2)}) %collective-permute-start.1) | collective-permute-done | bytes 147488 | tf_op jit(solution)/shard_map/ppermute | solution.py:71
  9.3 2.5 %collective-permute-start.5 = (bf16[64,1152]{1,0:T(8,128)(2,1)S(1)}, bf16[64,1152]{1,0:T(8,128)(2,1)S(1)}, u32[]{:S(2)}, u32[]{:S(2)}) collective-permute-start(bf16[64,1152]{1,0:T(8,128)(2,1)S(1)} %collective-permute-done.1.refs_0_), channel_id=1, source_target_pairs={{0,4},{1,3},{4,8},{5,1},{8,12},{9,5},{12,14},{13,9},{14,10},{15,13... | collective-permute-start | bytes 442376 | tf_op jit(solution)/shard_map/ppermute | solution.py:71
  11.8 1.9 %collective-permute-start.3 = (bf16[64,1152]{1,0:T(8,128)(2,1)S(1)}, bf16[64,1152]{1,0:T(8,128)(2,1)S(1)}, u32[]{:S(2)}, u32[]{:S(2)}) collective-permute-start(bf16[64,1152]{1,0:T(8,128)(2,1)S(1)} %get-tuple-element.64.refs_0_), channel_id=1, source_target_pairs={{0,2},{1,5},{4,0},{5,9},{8,4},{9,13},{12,8},{13,15},{14,12},{15,11... | collective-permute-start | bytes 442376 | tf_op jit(solution)/shard_map/ppermute | solution.py:71
  13.8 2.2 %collective-permute-done.5.refs_0_ = bf16[64,1152]{1,0:T(8,128)(2,1)S(1)} collective-permute-done((bf16[64,1152]{1,0:T(8,128)(2,1)S(1)}, bf16[64,1152]{1,0:T(8,128)(2,1)S(1)}, u32[]{:S(2)}, u32[]{:S(2)}) %collective-permute-start.5) | collective-permute-done | bytes 147488 | tf_op jit(solution)/shard_map/ppermute | solution.py:71
  16.0 2.5 %collective-permute-start.9 = (bf16[64,1152]{1,0:T(8,128)(2,1)S(1)}, bf16[64,1152]{1,0:T(8,128)(2,1)S(1)}, u32[]{:S(2)}, u32[]{:S(2)}) collective-permute-start(bf16[64,1152]{1,0:T(8,128)(2,1)S(1)} %collective-permute-done.5.refs_0_), channel_id=1, source_target_pairs={{0,4},{1,3},{4,8},{5,1},{8,12},{9,5},{12,14},{13,9},{14,10},{15,13... | collective-permute-start | bytes 442376 | tf_op jit(solution)/shard_map/ppermute | solution.py:71
  18.5 2.7 %collective-permute-done.3.refs_2_ = bf16[64,1152]{1,0:T(8,128)(2,1)S(1)} collective-permute-done((bf16[64,1152]{1,0:T(8,128)(2,1)S(1)}, bf16[64,1152]{1,0:T(8,128)(2,1)S(1)}, u32[]{:S(2)}, u32[]{:S(2)}) %collective-permute-start.3) | collective-permute-done | bytes 147488 | tf_op jit(solution)/shard_map/ppermute | solution.py:71
  21.3 1.9 %collective-permute-start.6 = (bf16[64,1024]{1,0:T(8,128)(2,1)S(1)}, bf16[64,1024]{1,0:T(8,128)(2,1)S(1)}, u32[]{:S(2)}, u32[]{:S(2)}) collective-permute-start(bf16[64,1024]{1,0:T(8,128)(2,1)S(1)} %collective-permute-done.2.refs_1_), channel_id=1, source_target_pairs={{0,4},{1,3},{4,8},{5,1},{8,12},{9,5},{12,14},{13,9},{14,10},{15,13... | collective-permute-start | bytes 393224 | tf_op jit(solution)/shard_map/ppermute | solution.py:71
  25.3 1.9 %collective-permute-done.7.refs_2_ = bf16[64,1152]{1,0:T(8,128)(2,1)S(1)} collective-permute-done((bf16[64,1152]{1,0:T(8,128)(2,1)S(1)}, bf16[64,1152]{1,0:T(8,128)(2,1)S(1)}, u32[]{:S(2)}, u32[]{:S(2)}) %collective-permute-start.7) | collective-permute-done | bytes 147488 | tf_op jit(solution)/shard_map/ppermute | solution.py:71
  27.2 1.8 %shard_map.105 = (bf16[1024,1536]{1,0:T(8,128)(2,1)S(1)}, bf16[768,1024]{1,0:T(8,128)(2,1)S(1)}) custom-call(bf16[2,512,384]{2,1,0:T(8,128)(2,1)} %refs_0_.1, bf16[2,512,384]{2,1,0:T(8,128)(2,1)} %refs_1_.1, bf16[2,192,1024]{2,1,0:T(8,128)(2,1)} %refs_2_.3, bf16[3200,384]{1,0:T(8,128)(2,1)S(1)} %collective-permute-done.refs_3_), custom_call_target="tpu_custom_call" | custom-call | tf_op jit(solution)/shard_map/pallas_call | solution.py:275
  36.6 2.8 %collective-permute-start.19 = (bf16[64,1024]{1,0:T(8,128)(2,1)S(1)}, bf16[64,1024]{1,0:T(8,128)(2,1)S(1)}, u32[]{:S(2)}, u32[]{:S(2)}) collective-permute-start(bf16[64,1024]{1,0:T(8,128)(2,1)S(1)} %get-tuple-element.76), channel_id=1, source_target_pairs={{0,2},{1,5},{4,0},{5,9},{8,4},{9,13},{12,8},{13,15},{14,12},{15,11... | collective-permute-start | bytes 393224 | tf_op jit(solution)/shard_map/ppermute | solution.py:71
  43.9 1.9 %collective-permute-start.20 = (bf16[64,1024]{1,0:T(8,128)(2,1)S(1)}, bf16[64,1024]{1,0:T(8,128)(2,1)S(1)}, u32[]{:S(2)}, u32[]{:S(2)}) collective-permute-start(bf16[64,1024]{1,0:T(8,128)(2,1)S(1)} %shard_map.115), channel_id=1, source_target_pairs={{0,2},{1,5},{4,0},{5,9},{8,4},{9,13},{12,8},{13,15},{14,12},{15,11... | collective-permute-start | bytes 393224 | tf_op jit(solution)/shard_map/ppermute | solution.py:71
  47.7 1.7 %collective-permute-start.27 = (bf16[64,1024]{1,0:T(8,128)(2,1)S(1)}, bf16[64,1024]{1,0:T(8,128)(2,1)S(1)}, u32[]{:S(2)}, u32[]{:S(2)}) collective-permute-start(bf16[64,1024]{1,0:T(8,128)(2,1)S(1)} %shard_map.121), channel_id=1, source_target_pairs={{0,2},{1,5},{4,0},{5,9},{8,4},{9,13},{12,8},{13,15},{14,12},{15,11... | collective-permute-start | bytes 393224 | tf_op jit(solution)/shard_map/ppermute | solution.py:71
  56.8 2.0 %collective-permute-done.18.refs_1_ = bf16[64,1024]{1,0:T(8,128)(2,1)S(1)} collective-permute-done((bf16[64,1024]{1,0:T(8,128)(2,1)S(1)}, bf16[64,1024]{1,0:T(8,128)(2,1)S(1)}, u32[]{:S(2)}, u32[]{:S(2)}) %collective-permute-start.18) | collective-permute-done | bytes 131104 | tf_op jit(solution)/shard_map/ppermute | solution.py:71
  59.0 2.3 %collective-permute-done.24.refs_1_ = bf16[64,1024]{1,0:T(8,128)(2,1)S(1)} collective-permute-done((bf16[64,1024]{1,0:T(8,128)(2,1)S(1)}, bf16[64,1024]{1,0:T(8,128)(2,1)S(1)}, u32[]{:S(2)}, u32[]{:S(2)}) %collective-permute-start.24) | collective-permute-done | bytes 131104 | tf_op jit(solution)/shard_map/ppermute | solution.py:71
  65.6 2.3 %collective-permute-done.33.refs_7_ = bf16[64,1024]{1,0:T(8,128)(2,1)S(1)} collective-permute-done((bf16[64,1024]{1,0:T(8,128)(2,1)S(1)}, bf16[64,1024]{1,0:T(8,128)(2,1)S(1)}, u32[]{:S(2)}, u32[]{:S(2)}) %collective-permute-start.33) | collective-permute-done | bytes 131104 | tf_op jit(solution)/shard_map/ppermute | solution.py:71
  69.1 1.6 %collective-permute-done.40.refs_6_ = bf16[64,1024]{1,0:T(8,128)(2,1)S(1)} collective-permute-done((bf16[64,1024]{1,0:T(8,128)(2,1)S(1)}, bf16[64,1024]{1,0:T(8,128)(2,1)S(1)}, u32[]{:S(2)}, u32[]{:S(2)}) %collective-permute-start.40) | collective-permute-done | bytes 131104 | tf_op jit(solution)/shard_map/ppermute | solution.py:71
  85.8 3.1 %collective-permute-done.43 = bf16[8,1024]{1,0:T(8,128)(2,1)S(1)} collective-permute-done((bf16[8,1024]{1,0:T(8,128)(2,1)S(1)}, bf16[8,1024]{1,0:T(8,128)(2,1)S(1)}, u32[]{:S(2)}, u32[]{:S(2)}) %collective-permute-start.43) | collective-permute-done | bytes 16416 | tf_op jit(solution)/shard_map/ppermute | solution.py:440
  88.9 2.2 %collective-permute-start.46 = (bf16[8,1024]{1,0:T(8,128)(2,1)S(1)}, bf16[8,1024]{1,0:T(8,128)(2,1)S(1)}, u32[]{:S(2)}, u32[]{:S(2)}) collective-permute-start(bf16[8,1024]{1,0:T(8,128)(2,1)S(1)} %add_convert_fusion), channel_id=1, source_target_pairs={{0,12},{2,14},{4,8},{6,10},{8,4},{10,6},{12,0},{14,2},{1,13},{3,15... | collective-permute-start | bytes 49160 | tf_op jit(solution)/shard_map/ppermute | solution.py:440
  105.0 1.6 %shard_map.133 = (f32[64,1024]{1,0:T(8,128)S(1)}, f32[64,1024]{1,0:T(8,128)S(1)}, f32[64,1024]{1,0:T(8,128)S(1)}, f32[64,1024]{1,0:T(8,128)S(1)}) custom-call(f32[256,1024]{1,0:T(8,128)S(1)} %get-tuple-element.100.residual_ref, f32[256,128]{1,0:T(8,128)S(1)} %get-tuple-element.101.inv_ref, bf16[256,768]{1,0:T(8,128)(2,1)S(1)} %get-tuple-element.102.gate_save, ...), custom_call_target="tpu_custom_call" | custom-call | flops 1207959552 | bytes 6721536 | tf_op jit(solution)/shard_map/pallas_call | solution.py:29
  111.1 1.6 %shard_map.132 = (f32[64,1024]{1,0:T(8,128)S(1)}, f32[64,1024]{1,0:T(8,128)S(1)}, f32[64,1024]{1,0:T(8,128)S(1)}, f32[64,1024]{1,0:T(8,128)S(1)}) custom-call(f32[256,1024]{1,0:T(8,128)S(1)} %get-tuple-element.95.residual_ref, f32[256,128]{1,0:T(8,128)S(1)} %get-tuple-element.96.inv_ref, bf16[256,768]{1,0:T(8,128)(2,1)S(1)} %get-tuple-element.97.gate_save, ...), custom_call_target="tpu_custom_call" | custom-call | flops 1207959552 | bytes 6721536 | tf_op jit(solution)/shard_map/pallas_call | solution.py:29
  112.8 1.9 %collective-permute-start.53 = (bf16[64,1024]{1,0:T(8,128)(2,1)S(1)}, bf16[64,1024]{1,0:T(8,128)(2,1)S(1)}, u32[]{:S(2)}, u32[]{:S(2)}) collective-permute-start(bf16[64,1024]{1,0:T(8,128)(2,1)S(1)} %shard_map.140), channel_id=1, source_target_pairs={{0,2},{1,5},{4,0},{5,9},{8,4},{9,13},{12,8},{13,15},{14,12},{15,11... | collective-permute-start | bytes 393224 | tf_op jit(solution)/shard_map/ppermute | solution.py:71
  115.0 1.7 %collective-permute-done.49.arrived_ref = bf16[64,1024]{1,0:T(8,128)(2,1)S(1)} collective-permute-done((bf16[64,1024]{1,0:T(8,128)(2,1)S(1)}, bf16[64,1024]{1,0:T(8,128)(2,1)S(1)}, u32[]{:S(2)}, u32[]{:S(2)}) %collective-permute-start.49) | collective-permute-done | bytes 131104 | tf_op jit(solution)/shard_map/ppermute | solution.py:71
  (159 shorter events, 70.2 us)
Async XLA Ops:
  2.6 24.6 %collective-permute-start = (bf16[3200,384]{1,0:T(8,128)(2,1)S(1)}, bf16[3200,384]{1,0:T(8,128)(2,1)S(1)}, u32[]{:S(2)}, u32[]{:S(2)}) collective-permute-start(bf16[3200,384]{1,0:T(8,128)(2,1)S(1)} %get-tuple-element.66), channel_id=1, source_target_pairs={{0,1},{1,0},{2,3},{3,2},{4,5},{5,4},{6,7},{7,6},{8,9},{9,8},{10,11... | collective-permute-start | bytes 7372808 | tf_op jit(solution)/shard_map/ppermute | solution.py:315
  9.3 6.7 %collective-permute-start.5 = (bf16[64,1152]{1,0:T(8,128)(2,1)S(1)}, bf16[64,1152]{1,0:T(8,128)(2,1)S(1)}, u32[]{:S(2)}, u32[]{:S(2)}) collective-permute-start(bf16[64,1152]{1,0:T(8,128)(2,1)S(1)} %collective-permute-done.1.refs_0_), channel_id=1, source_target_pairs={{0,4},{1,3},{4,8},{5,1},{8,12},{9,5},{12,14},{13,9},{14,10},{15,13... | collective-permute-start | bytes 442376 | tf_op jit(solution)/shard_map/ppermute | solution.py:71
  11.8 6.7 %collective-permute-start.8 = (bf16[64,1024]{1,0:T(8,128)(2,1)S(1)}, bf16[64,1024]{1,0:T(8,128)(2,1)S(1)}, u32[]{:S(2)}, u32[]{:S(2)}) collective-permute-start(bf16[64,1024]{1,0:T(8,128)(2,1)S(1)} %collective-permute-done.4.refs_3_), channel_id=1, source_target_pairs={{0,2},{1,5},{4,0},{5,9},{8,4},{9,13},{12,8},{13,15},{14,12},{15,11... | collective-permute-start | bytes 393224 | tf_op jit(solution)/shard_map/ppermute | solution.py:71
  11.8 9.4 %collective-permute-start.3 = (bf16[64,1152]{1,0:T(8,128)(2,1)S(1)}, bf16[64,1152]{1,0:T(8,128)(2,1)S(1)}, u32[]{:S(2)}, u32[]{:S(2)}) collective-permute-start(bf16[64,1152]{1,0:T(8,128)(2,1)S(1)} %get-tuple-element.64.refs_0_), channel_id=1, source_target_pairs={{0,2},{1,5},{4,0},{5,9},{8,4},{9,13},{12,8},{13,15},{14,12},{15,11... | collective-permute-start | bytes 442376 | tf_op jit(solution)/shard_map/ppermute | solution.py:71
  13.7 7.7 %collective-permute-start.2 = (bf16[64,1024]{1,0:T(8,128)(2,1)S(1)}, bf16[64,1024]{1,0:T(8,128)(2,1)S(1)}, u32[]{:S(2)}, u32[]{:S(2)}) collective-permute-start(bf16[64,1024]{1,0:T(8,128)(2,1)S(1)} %get-tuple-element.65.refs_1_), channel_id=1, source_target_pairs={{0,4},{1,3},{4,8},{5,1},{8,12},{9,5},{12,14},{13,9},{14,10},{15,13... | collective-permute-start | bytes 393224 | tf_op jit(solution)/shard_map/ppermute | solution.py:71
  16.0 7.2 %collective-permute-start.9 = (bf16[64,1152]{1,0:T(8,128)(2,1)S(1)}, bf16[64,1152]{1,0:T(8,128)(2,1)S(1)}, u32[]{:S(2)}, u32[]{:S(2)}) collective-permute-start(bf16[64,1152]{1,0:T(8,128)(2,1)S(1)} %collective-permute-done.5.refs_0_), channel_id=1, source_target_pairs={{0,4},{1,3},{4,8},{5,1},{8,12},{9,5},{12,14},{13,9},{14,10},{15,13... | collective-permute-start | bytes 442376 | tf_op jit(solution)/shard_map/ppermute | solution.py:71
  21.3 8.5 %collective-permute-start.6 = (bf16[64,1024]{1,0:T(8,128)(2,1)S(1)}, bf16[64,1024]{1,0:T(8,128)(2,1)S(1)}, u32[]{:S(2)}, u32[]{:S(2)}) collective-permute-start(bf16[64,1024]{1,0:T(8,128)(2,1)S(1)} %collective-permute-done.2.refs_1_), channel_id=1, source_target_pairs={{0,4},{1,3},{4,8},{5,1},{8,12},{9,5},{12,14},{13,9},{14,10},{15,13... | collective-permute-start | bytes 393224 | tf_op jit(solution)/shard_map/ppermute | solution.py:71
  23.2 8.0 %collective-permute-start.13 = (bf16[64,1152]{1,0:T(8,128)(2,1)S(1)}, bf16[64,1152]{1,0:T(8,128)(2,1)S(1)}, u32[]{:S(2)}, u32[]{:S(2)}) collective-permute-start(bf16[64,1152]{1,0:T(8,128)(2,1)S(1)} %collective-permute-done.9.refs_0_), channel_id=1, source_target_pairs={{0,4},{1,3},{4,8},{5,1},{8,12},{9,5},{12,14},{13,9},{14,10},{15,13... | collective-permute-start | bytes 442376 | tf_op jit(solution)/shard_map/ppermute | solution.py:71
  32.2 7.2 %collective-permute-start.15 = (bf16[64,1024]{1,0:T(8,128)(2,1)S(1)}, bf16[64,1024]{1,0:T(8,128)(2,1)S(1)}, u32[]{:S(2)}, u32[]{:S(2)}) collective-permute-start(bf16[64,1024]{1,0:T(8,128)(2,1)S(1)} %get-tuple-element.73), channel_id=1, source_target_pairs={{0,4},{1,3},{4,8},{5,1},{8,12},{9,5},{12,14},{13,9},{14,10},{15,13... | collective-permute-start | bytes 393224 | tf_op jit(solution)/shard_map/ppermute | solution.py:71
  33.8 7.9 %collective-permute-start.25 = (bf16[64,1024]{1,0:T(8,128)(2,1)S(1)}, bf16[64,1024]{1,0:T(8,128)(2,1)S(1)}, u32[]{:S(2)}, u32[]{:S(2)}) collective-permute-start(bf16[64,1024]{1,0:T(8,128)(2,1)S(1)} %get-tuple-element.84), channel_id=1, source_target_pairs={{0,2},{1,5},{4,0},{5,9},{8,4},{9,13},{12,8},{13,15},{14,12},{15,11... | collective-permute-start | bytes 393224 | tf_op jit(solution)/shard_map/ppermute | solution.py:71
  36.6 7.2 %collective-permute-start.19 = (bf16[64,1024]{1,0:T(8,128)(2,1)S(1)}, bf16[64,1024]{1,0:T(8,128)(2,1)S(1)}, u32[]{:S(2)}, u32[]{:S(2)}) collective-permute-start(bf16[64,1024]{1,0:T(8,128)(2,1)S(1)} %get-tuple-element.76), channel_id=1, source_target_pairs={{0,2},{1,5},{4,0},{5,9},{8,4},{9,13},{12,8},{13,15},{14,12},{15,11... | collective-permute-start | bytes 393224 | tf_op jit(solution)/shard_map/ppermute | solution.py:71
  40.2 7.0 %collective-permute-start.22 = (bf16[64,1024]{1,0:T(8,128)(2,1)S(1)}, bf16[64,1024]{1,0:T(8,128)(2,1)S(1)}, u32[]{:S(2)}, u32[]{:S(2)}) collective-permute-start(bf16[64,1024]{1,0:T(8,128)(2,1)S(1)} %get-tuple-element.80), channel_id=1, source_target_pairs={{0,4},{1,3},{4,8},{5,1},{8,12},{9,5},{12,14},{13,9},{14,10},{15,13... | collective-permute-start | bytes 393224 | tf_op jit(solution)/shard_map/ppermute | solution.py:71
  43.9 7.1 %collective-permute-start.20 = (bf16[64,1024]{1,0:T(8,128)(2,1)S(1)}, bf16[64,1024]{1,0:T(8,128)(2,1)S(1)}, u32[]{:S(2)}, u32[]{:S(2)}) collective-permute-start(bf16[64,1024]{1,0:T(8,128)(2,1)S(1)} %shard_map.115), channel_id=1, source_target_pairs={{0,2},{1,5},{4,0},{5,9},{8,4},{9,13},{12,8},{13,15},{14,12},{15,11... | collective-permute-start | bytes 393224 | tf_op jit(solution)/shard_map/ppermute | solution.py:71
  45.8 6.6 %collective-permute-start.17 = (bf16[64,1024]{1,0:T(8,128)(2,1)S(1)}, bf16[64,1024]{1,0:T(8,128)(2,1)S(1)}, u32[]{:S(2)}, u32[]{:S(2)}) collective-permute-start(bf16[64,1024]{1,0:T(8,128)(2,1)S(1)} %shard_map.113), channel_id=1, source_target_pairs={{0,4},{1,3},{4,8},{5,1},{8,12},{9,5},{12,14},{13,9},{14,10},{15,13... | collective-permute-start | bytes 393224 | tf_op jit(solution)/shard_map/ppermute | solution.py:71
  47.7 7.3 %collective-permute-start.27 = (bf16[64,1024]{1,0:T(8,128)(2,1)S(1)}, bf16[64,1024]{1,0:T(8,128)(2,1)S(1)}, u32[]{:S(2)}, u32[]{:S(2)}) collective-permute-start(bf16[64,1024]{1,0:T(8,128)(2,1)S(1)} %shard_map.121), channel_id=1, source_target_pairs={{0,2},{1,5},{4,0},{5,9},{8,4},{9,13},{12,8},{13,15},{14,12},{15,11... | collective-permute-start | bytes 393224 | tf_op jit(solution)/shard_map/ppermute | solution.py:71
  53.6 7.6 %collective-permute-start.24 = (bf16[64,1024]{1,0:T(8,128)(2,1)S(1)}, bf16[64,1024]{1,0:T(8,128)(2,1)S(1)}, u32[]{:S(2)}, u32[]{:S(2)}) collective-permute-start(bf16[64,1024]{1,0:T(8,128)(2,1)S(1)} %shard_map.119), channel_id=1, source_target_pairs={{0,4},{1,3},{4,8},{5,1},{8,12},{9,5},{12,14},{13,9},{14,10},{15,13... | collective-permute-start | bytes 393224 | tf_op jit(solution)/shard_map/ppermute | solution.py:71
  61.5 6.4 %collective-permute-start.33 = (bf16[64,1024]{1,0:T(8,128)(2,1)S(1)}, bf16[64,1024]{1,0:T(8,128)(2,1)S(1)}, u32[]{:S(2)}, u32[]{:S(2)}) collective-permute-start(bf16[64,1024]{1,0:T(8,128)(2,1)S(1)} %shard_map.123.refs_3_), channel_id=1, source_target_pairs={{0,2},{1,5},{4,0},{5,9},{8,4},{9,13},{12,8},{13,15},{14,12},{15,11... | collective-permute-start | bytes 393224 | tf_op jit(solution)/shard_map/ppermute | solution.py:71
  62.7 8.0 %collective-permute-start.40 = (bf16[64,1024]{1,0:T(8,128)(2,1)S(1)}, bf16[64,1024]{1,0:T(8,128)(2,1)S(1)}, u32[]{:S(2)}, u32[]{:S(2)}) collective-permute-start(bf16[64,1024]{1,0:T(8,128)(2,1)S(1)} %shard_map.117.refs_2_), channel_id=1, source_target_pairs={{0,2},{1,5},{4,0},{5,9},{8,4},{9,13},{12,8},{13,15},{14,12},{15,11... | collective-permute-start | bytes 393224 | tf_op jit(solution)/shard_map/ppermute | solution.py:71
  63.5 8.1 %collective-permute-start.37 = (bf16[64,1024]{1,0:T(8,128)(2,1)S(1)}, bf16[64,1024]{1,0:T(8,128)(2,1)S(1)}, u32[]{:S(2)}, u32[]{:S(2)}) collective-permute-start(bf16[64,1024]{1,0:T(8,128)(2,1)S(1)} %shard_map.123.refs_3_), channel_id=1, source_target_pairs={{0,4},{1,3},{4,8},{5,1},{8,12},{9,5},{12,14},{13,9},{14,10},{15,13... | collective-permute-start | bytes 393224 | tf_op jit(solution)/shard_map/ppermute | solution.py:71
  64.8 8.0 %collective-permute-start.30 = (bf16[64,1024]{1,0:T(8,128)(2,1)S(1)}, bf16[64,1024]{1,0:T(8,128)(2,1)S(1)}, u32[]{:S(2)}, u32[]{:S(2)}) collective-permute-start(bf16[64,1024]{1,0:T(8,128)(2,1)S(1)} %collective-permute-done.29.refs_4_), channel_id=1, source_target_pairs={{0,4},{1,3},{4,8},{5,1},{8,12},{9,5},{12,14},{13,9},{14,10},{15,13... | collective-permute-start | bytes 393224 | tf_op jit(solution)/shard_map/ppermute | solution.py:71
  108.9 7.8 %collective-permute-start.49 = (bf16[64,1024]{1,0:T(8,128)(2,1)S(1)}, bf16[64,1024]{1,0:T(8,128)(2,1)S(1)}, u32[]{:S(2)}, u32[]{:S(2)}) collective-permute-start(bf16[64,1024]{1,0:T(8,128)(2,1)S(1)} %shard_map.137), channel_id=1, source_target_pairs={{0,4},{1,3},{4,8},{5,1},{8,12},{9,5},{12,14},{13,9},{14,10},{15,13... | collective-permute-start | bytes 393224 | tf_op jit(solution)/shard_map/ppermute | solution.py:71
  110.1 7.2 %collective-permute-start.59 = (bf16[64,1024]{1,0:T(8,128)(2,1)S(1)}, bf16[64,1024]{1,0:T(8,128)(2,1)S(1)}, u32[]{:S(2)}, u32[]{:S(2)}) collective-permute-start(bf16[64,1024]{1,0:T(8,128)(2,1)S(1)} %shard_map.144), channel_id=1, source_target_pairs={{0,2},{1,5},{4,0},{5,9},{8,4},{9,13},{12,8},{13,15},{14,12},{15,11... | collective-permute-start | bytes 393224 | tf_op jit(solution)/shard_map/ppermute | solution.py:71
  112.8 8.5 %collective-permute-start.53 = (bf16[64,1024]{1,0:T(8,128)(2,1)S(1)}, bf16[64,1024]{1,0:T(8,128)(2,1)S(1)}, u32[]{:S(2)}, u32[]{:S(2)}) collective-permute-start(bf16[64,1024]{1,0:T(8,128)(2,1)S(1)} %shard_map.140), channel_id=1, source_target_pairs={{0,2},{1,5},{4,0},{5,9},{8,4},{9,13},{12,8},{13,15},{14,12},{15,11... | collective-permute-start | bytes 393224 | tf_op jit(solution)/shard_map/ppermute | solution.py:71
  114.8 6.5 %collective-permute-start.56 = (bf16[64,1024]{1,0:T(8,128)(2,1)S(1)}, bf16[64,1024]{1,0:T(8,128)(2,1)S(1)}, u32[]{:S(2)}, u32[]{:S(2)}) collective-permute-start(bf16[64,1024]{1,0:T(8,128)(2,1)S(1)} %shard_map.142), channel_id=1, source_target_pairs={{0,4},{1,3},{4,8},{5,1},{8,12},{9,5},{12,14},{13,9},{14,10},{15,13... | collective-permute-start | bytes 393224 | tf_op jit(solution)/shard_map/ppermute | solution.py:71
  (41 other events, 349.4 us)

commit v24 on v16

--- a/solution.py
+++ b/solution.py
@@ -83,7 +83,7 @@
         use((0,), (top, bottom))
         for step in range(1, self.half):
             if guard is not None and step == self.half - 1:
-                top_right = after(top_right, [guard])
+                bottom_right = after(bottom_right, [guard])
             top_left = self.send(top_left, 1)
             top_right = self.send(top_right, -1)
             bottom_left = self.send(bottom_left, 1)
@@ -335,7 +335,7 @@
             scale = jnp.concatenate(pieces, axis=0)
             act = dot(x, wide_ref[:, pl.ds(local * pair_dim, pair_dim)])
             gate_act, up_act = act[:, :hidden_dim], act[:, hidden_dim:]
-            sigmoid_gate = jax.nn.sigmoid(gate_act)
+            sigmoid_gate = 0.5 + 0.5 * jnp.tanh(0.5 * gate_act)
             silu = gate_act * sigmoid_gate * scale
             slope = sigmoid_gate * (1.0 + gate_act * (1.0 - sigmoid_gate)) * scale
             cols = pl.ds(local * hidden_dim, hidden_dim)

time: 123 us -> 126 us (1.024)
  waiting for transfers between devices: 29.2 us -> 33.7 us
  starting transfers between devices: 69.1 us -> 67.2 us
    ppermute x56, waiting for transfers between devices: 25.8 us -> 29.3 us  [send(): return lax.ppermute(value, 'expert', pairs)]
    ppermute x56, starting transfers between devices: 62.6 us -> 61.1 us  [send(): return lax.ppermute(value, 'expert', pairs)]
  transfers between devices with their start and end apart: 62 -> 62, of which waited for: 28 -> 26; matrix products, arithmetic and copies ran while one was open for 1% -> 1% of each run, Pallas kernels for 14% -> 14%
where the time goes in v24:
time: 126 us
  starting transfers between devices  67.2 us (53%)
  waiting for transfers between devices  33.7 us (27%)
  Pallas kernels  21.8 us (17%)
  matrix products  1.71 us (1%)
    ppermute x56, starting transfers between devices, send(): return lax.ppermute(value, 'expert', pairs)  61.1 us
    ppermute x56, waiting for transfers between devices, send(): return lax.ppermute(value, 'expert', pairs)  29.3 us
    pallas_call x39, Pallas kernels, call(): pl.pallas_call(kernel, out_shape=[pltpu.VMEM(shape, dtype) for shape, dty...  17.3 us
    ppermute x4, starting transfers between devices, body(): pooled_grad = pooled_grad + lax.ppermute(mine, 'expert', pairs).astype(F32)  5.58 us
    ppermute x4, waiting for transfers between devices, body(): pooled_grad = pooled_grad + lax.ppermute(mine, 'expert', pairs).astype(F32)  4.39 us
  transfers between devices with their start and end apart: 62, of which 26 were waited for; matrix products, arithmetic and copies ran while one was open for 1% of the time, Pallas kernels for 14%

profile of v24, /device:TPU:0, one launch (start us, length us, event | category | flops | bytes accessed | tf_op | source)
XLA Modules:
  0.0 125.6 jit_solution(5642648670557499036)
XLA Ops:
  0.6 1.9 %shard_map.104 = (bf16[64,1152]{1,0:T(8,128)(2,1)S(1)}, bf16[64,1024]{1,0:T(8,128)(2,1)S(1)}, bf16[3200,384]{1,0:T(8,128)(2,1)S(1)}) custom-call(s32[8,128]{1,0:T(8,128)} %bitcast.19, f32[8,128]{1,0:T(8,128)} %bitcast.20, bf16[128,1024]{1,0:T(8,128)(2,1)} %refs_2_.2, bf16[2,512,384]{2,1,0:T(8,128)(2,1)} %refs_0_.1, bf16[2,512,384]{2,1,0:T(8,128)(2,1)} %refs_1_.1, ...), custom_call_target="tpu_custom_call" | custom-call | tf_op jit(solution)/shard_map/pallas_call | solution.py:215
  3.1 2.6 %collective-permute-start.1 = (bf16[64,1152]{1,0:T(8,128)(2,1)S(1)}, bf16[64,1152]{1,0:T(8,128)(2,1)S(1)}, u32[]{:S(2)}, u32[]{:S(2)}) collective-permute-start(bf16[64,1152]{1,0:T(8,128)(2,1)S(1)} %get-tuple-element.64.refs_0_), channel_id=1, source_target_pairs={{0,4},{4,8},{8,12},{12,14},{14,10},{10,6},{6,2},{2,0},{1,5},{5,9},... | collective-permute-start | bytes 442376 | tf_op jit(solution)/shard_map/ppermute | solution.py:68
  5.7 4.4 %collective-permute-done.1.refs_0_ = bf16[64,1152]{1,0:T(8,128)(2,1)S(1)} collective-permute-done((bf16[64,1152]{1,0:T(8,128)(2,1)S(1)}, bf16[64,1152]{1,0:T(8,128)(2,1)S(1)}, u32[]{:S(2)}, u32[]{:S(2)}) %collective-permute-start.1) | collective-permute-done | bytes 147488 | tf_op jit(solution)/shard_map/ppermute | solution.py:68
  10.1 1.8 %collective-permute-start.5 = (bf16[64,1152]{1,0:T(8,128)(2,1)S(1)}, bf16[64,1152]{1,0:T(8,128)(2,1)S(1)}, u32[]{:S(2)}, u32[]{:S(2)}) collective-permute-start(bf16[64,1152]{1,0:T(8,128)(2,1)S(1)} %collective-permute-done.1.refs_0_), channel_id=1, source_target_pairs={{0,4},{4,8},{8,12},{12,14},{14,10},{10,6},{6,2},{2,0},{1,5},{5,9},... | collective-permute-start | bytes 442376 | tf_op jit(solution)/shard_map/ppermute | solution.py:68
  12.1 1.7 %collective-permute-start.3 = (bf16[64,1152]{1,0:T(8,128)(2,1)S(1)}, bf16[64,1152]{1,0:T(8,128)(2,1)S(1)}, u32[]{:S(2)}, u32[]{:S(2)}) collective-permute-start(bf16[64,1152]{1,0:T(8,128)(2,1)S(1)} %get-tuple-element.64.refs_0_), channel_id=1, source_target_pairs={{0,2},{4,0},{8,4},{12,8},{14,12},{10,14},{6,10},{2,6},{1,3},{5,1},... | collective-permute-start | bytes 442376 | tf_op jit(solution)/shard_map/ppermute | solution.py:68
  14.2 2.0 %collective-permute-done.5.refs_0_ = bf16[64,1152]{1,0:T(8,128)(2,1)S(1)} collective-permute-done((bf16[64,1152]{1,0:T(8,128)(2,1)S(1)}, bf16[64,1152]{1,0:T(8,128)(2,1)S(1)}, u32[]{:S(2)}, u32[]{:S(2)}) %collective-permute-start.5) | collective-permute-done | bytes 147488 | tf_op jit(solution)/shard_map/ppermute | solution.py:68
  16.2 2.5 %collective-permute-start.9 = (bf16[64,1152]{1,0:T(8,128)(2,1)S(1)}, bf16[64,1152]{1,0:T(8,128)(2,1)S(1)}, u32[]{:S(2)}, u32[]{:S(2)}) collective-permute-start(bf16[64,1152]{1,0:T(8,128)(2,1)S(1)} %collective-permute-done.5.refs_0_), channel_id=1, source_target_pairs={{0,4},{4,8},{8,12},{12,14},{14,10},{10,6},{6,2},{2,0},{1,5},{5,9},... | collective-permute-start | bytes 442376 | tf_op jit(solution)/shard_map/ppermute | solution.py:68
  18.7 1.8 %shard_map.105 = (bf16[1024,1536]{1,0:T(8,128)(2,1)S(1)}, bf16[768,1024]{1,0:T(8,128)(2,1)S(1)}) custom-call(bf16[2,512,384]{2,1,0:T(8,128)(2,1)} %refs_0_.1, bf16[2,512,384]{2,1,0:T(8,128)(2,1)} %refs_1_.1, bf16[2,192,1024]{2,1,0:T(8,128)(2,1)} %refs_2_.3, bf16[3200,384]{1,0:T(8,128)(2,1)S(1)} %collective-permute-done.refs_3_), custom_call_target="tpu_custom_call" | custom-call | tf_op jit(solution)/shard_map/pallas_call | solution.py:270
  22.6 2.4 %collective-permute-start.13 = (bf16[64,1152]{1,0:T(8,128)(2,1)S(1)}, bf16[64,1152]{1,0:T(8,128)(2,1)S(1)}, u32[]{:S(2)}, u32[]{:S(2)}) collective-permute-start(bf16[64,1152]{1,0:T(8,128)(2,1)S(1)} %collective-permute-done.9.refs_0_), channel_id=1, source_target_pairs={{0,4},{4,8},{8,12},{12,14},{14,10},{10,6},{6,2},{2,0},{1,5},{5,9},... | collective-permute-start | bytes 442376 | tf_op jit(solution)/shard_map/ppermute | solution.py:68
  26.6 3.2 %collective-permute-done.7.refs_2_ = bf16[64,1152]{1,0:T(8,128)(2,1)S(1)} collective-permute-done((bf16[64,1152]{1,0:T(8,128)(2,1)S(1)}, bf16[64,1152]{1,0:T(8,128)(2,1)S(1)}, u32[]{:S(2)}, u32[]{:S(2)}) %collective-permute-start.7) | collective-permute-done | bytes 147488 | tf_op jit(solution)/shard_map/ppermute | solution.py:68
  29.8 2.0 %collective-permute-start.10 = (bf16[64,1024]{1,0:T(8,128)(2,1)S(1)}, bf16[64,1024]{1,0:T(8,128)(2,1)S(1)}, u32[]{:S(2)}, u32[]{:S(2)}) collective-permute-start(bf16[64,1024]{1,0:T(8,128)(2,1)S(1)} %collective-permute-done.6.refs_1_), channel_id=1, source_target_pairs={{0,4},{4,8},{8,12},{12,14},{14,10},{10,6},{6,2},{2,0},{1,5},{5,9},... | collective-permute-start | bytes 393224 | tf_op jit(solution)/shard_map/ppermute | solution.py:68
  38.0 1.7 %collective-permute-start.22 = (bf16[64,1024]{1,0:T(8,128)(2,1)S(1)}, bf16[64,1024]{1,0:T(8,128)(2,1)S(1)}, u32[]{:S(2)}, u32[]{:S(2)}) collective-permute-start(bf16[64,1024]{1,0:T(8,128)(2,1)S(1)} %get-tuple-element.80), channel_id=1, source_target_pairs={{0,4},{4,8},{8,12},{12,14},{14,10},{10,6},{6,2},{2,0},{1,5},{5,9},... | collective-permute-start | bytes 393224 | tf_op jit(solution)/shard_map/ppermute | solution.py:68
  39.7 1.9 %collective-permute-start.16 = (bf16[64,1024]{1,0:T(8,128)(2,1)S(1)}, bf16[64,1024]{1,0:T(8,128)(2,1)S(1)}, u32[]{:S(2)}, u32[]{:S(2)}) collective-permute-start(bf16[64,1024]{1,0:T(8,128)(2,1)S(1)} %shard_map.112), channel_id=1, source_target_pairs={{0,4},{4,8},{8,12},{12,14},{14,10},{10,6},{6,2},{2,0},{1,5},{5,9},... | collective-permute-start | bytes 393224 | tf_op jit(solution)/shard_map/ppermute | solution.py:68
  45.8 2.2 %collective-permute-start.17 = (bf16[64,1024]{1,0:T(8,128)(2,1)S(1)}, bf16[64,1024]{1,0:T(8,128)(2,1)S(1)}, u32[]{:S(2)}, u32[]{:S(2)}) collective-permute-start(bf16[64,1024]{1,0:T(8,128)(2,1)S(1)} %shard_map.113), channel_id=1, source_target_pairs={{0,4},{4,8},{8,12},{12,14},{14,10},{10,6},{6,2},{2,0},{1,5},{5,9},... | collective-permute-start | bytes 393224 | tf_op jit(solution)/shard_map/ppermute | solution.py:68
  50.7 1.8 %collective-permute-done.17.arrived_ref = bf16[64,1024]{1,0:T(8,128)(2,1)S(1)} collective-permute-done((bf16[64,1024]{1,0:T(8,128)(2,1)S(1)}, bf16[64,1024]{1,0:T(8,128)(2,1)S(1)}, u32[]{:S(2)}, u32[]{:S(2)}) %collective-permute-start.17) | collective-permute-done | bytes 131104 | tf_op jit(solution)/shard_map/ppermute | solution.py:68
  52.5 2.4 %collective-permute-start.18 = (bf16[64,1024]{1,0:T(8,128)(2,1)S(1)}, bf16[64,1024]{1,0:T(8,128)(2,1)S(1)}, u32[]{:S(2)}, u32[]{:S(2)}) collective-permute-start(bf16[64,1024]{1,0:T(8,128)(2,1)S(1)} %shard_map.114), channel_id=1, source_target_pairs={{0,4},{4,8},{8,12},{12,14},{14,10},{10,6},{6,2},{2,0},{1,5},{5,9},... | collective-permute-start | bytes 393224 | tf_op jit(solution)/shard_map/ppermute | solution.py:68
  55.0 2.0 %collective-permute-start.24 = (bf16[64,1024]{1,0:T(8,128)(2,1)S(1)}, bf16[64,1024]{1,0:T(8,128)(2,1)S(1)}, u32[]{:S(2)}, u32[]{:S(2)}) collective-permute-start(bf16[64,1024]{1,0:T(8,128)(2,1)S(1)} %shard_map.119), channel_id=1, source_target_pairs={{0,4},{4,8},{8,12},{12,14},{14,10},{10,6},{6,2},{2,0},{1,5},{5,9},... | collective-permute-start | bytes 393224 | tf_op jit(solution)/shard_map/ppermute | solution.py:68
  59.6 1.8 %collective-permute-start.29 = (bf16[64,1024]{1,0:T(8,128)(2,1)S(1)}, bf16[64,1024]{1,0:T(8,128)(2,1)S(1)}, u32[]{:S(2)}, u32[]{:S(2)}) collective-permute-start(bf16[64,1024]{1,0:T(8,128)(2,1)S(1)} %shard_map.117.refs_2_), channel_id=1, source_target_pairs={{0,4},{4,8},{8,12},{12,14},{14,10},{10,6},{6,2},{2,0},{1,5},{5,9},... | collective-permute-start | bytes 393224 | tf_op jit(solution)/shard_map/ppermute | solution.py:68
  67.5 2.3 %collective-permute-done.33.refs_7_ = bf16[64,1024]{1,0:T(8,128)(2,1)S(1)} collective-permute-done((bf16[64,1024]{1,0:T(8,128)(2,1)S(1)}, bf16[64,1024]{1,0:T(8,128)(2,1)S(1)}, u32[]{:S(2)}, u32[]{:S(2)}) %collective-permute-start.33) | collective-permute-done | bytes 131104 | tf_op jit(solution)/shard_map/ppermute | solution.py:68
  87.3 2.6 %collective-permute-done.43 = bf16[8,1024]{1,0:T(8,128)(2,1)S(1)} collective-permute-done((bf16[8,1024]{1,0:T(8,128)(2,1)S(1)}, bf16[8,1024]{1,0:T(8,128)(2,1)S(1)}, u32[]{:S(2)}, u32[]{:S(2)}) %collective-permute-start.43) | collective-permute-done | bytes 16416 | tf_op jit(solution)/shard_map/ppermute | solution.py:435
  89.9 3.4 %collective-permute-start.46 = (bf16[8,1024]{1,0:T(8,128)(2,1)S(1)}, bf16[8,1024]{1,0:T(8,128)(2,1)S(1)}, u32[]{:S(2)}, u32[]{:S(2)}) collective-permute-start(bf16[8,1024]{1,0:T(8,128)(2,1)S(1)} %add_convert_fusion), channel_id=1, source_target_pairs={{0,12},{2,14},{4,8},{6,10},{8,4},{10,6},{12,0},{14,2},{1,13},{3,15... | collective-permute-start | bytes 49160 | tf_op jit(solution)/shard_map/ppermute | solution.py:435
  96.2 1.7 %collective-permute-done.45 = bf16[8,1024]{1,0:T(8,128)(2,1)S(1)} collective-permute-done((bf16[8,1024]{1,0:T(8,128)(2,1)S(1)}, bf16[8,1024]{1,0:T(8,128)(2,1)S(1)}, u32[]{:S(2)}, u32[]{:S(2)}) %collective-permute-start.45) | collective-permute-done | bytes 16416 | tf_op jit(solution)/shard_map/ppermute | solution.py:435
  99.3 1.9 %collective-permute-start.57 = (bf16[64,1024]{1,0:T(8,128)(2,1)S(1)}, bf16[64,1024]{1,0:T(8,128)(2,1)S(1)}, u32[]{:S(2)}, u32[]{:S(2)}) collective-permute-start(bf16[64,1024]{1,0:T(8,128)(2,1)S(1)} %get-tuple-element.125), channel_id=1, source_target_pairs={{0,2},{4,0},{8,4},{12,8},{14,12},{10,14},{6,10},{2,6},{1,3},{5,1},... | collective-permute-start | bytes 393224 | tf_op jit(solution)/shard_map/ppermute | solution.py:68
  117.3 1.9 %collective-permute-done.49.arrived_ref = bf16[64,1024]{1,0:T(8,128)(2,1)S(1)} collective-permute-done((bf16[64,1024]{1,0:T(8,128)(2,1)S(1)}, bf16[64,1024]{1,0:T(8,128)(2,1)S(1)}, u32[]{:S(2)}, u32[]{:S(2)}) %collective-permute-start.49) | collective-permute-done | bytes 131104 | tf_op jit(solution)/shard_map/ppermute | solution.py:68
  (159 shorter events, 70.6 us)
Async XLA Ops:
  2.6 16.1 %collective-permute-start = (bf16[3200,384]{1,0:T(8,128)(2,1)S(1)}, bf16[3200,384]{1,0:T(8,128)(2,1)S(1)}, u32[]{:S(2)}, u32[]{:S(2)}) collective-permute-start(bf16[3200,384]{1,0:T(8,128)(2,1)S(1)} %get-tuple-element.66), channel_id=1, source_target_pairs={{0,1},{1,0},{2,3},{3,2},{4,5},{5,4},{6,7},{7,6},{8,9},{9,8},{10,11... | collective-permute-start | bytes 7372808 | tf_op jit(solution)/shard_map/ppermute | solution.py:310
  3.1 7.0 %collective-permute-start.1 = (bf16[64,1152]{1,0:T(8,128)(2,1)S(1)}, bf16[64,1152]{1,0:T(8,128)(2,1)S(1)}, u32[]{:S(2)}, u32[]{:S(2)}) collective-permute-start(bf16[64,1152]{1,0:T(8,128)(2,1)S(1)} %get-tuple-element.64.refs_0_), channel_id=1, source_target_pairs={{0,4},{4,8},{8,12},{12,14},{14,10},{10,6},{6,2},{2,0},{1,5},{5,9},... | collective-permute-start | bytes 442376 | tf_op jit(solution)/shard_map/ppermute | solution.py:68
  11.9 6.8 %collective-permute-start.8 = (bf16[64,1024]{1,0:T(8,128)(2,1)S(1)}, bf16[64,1024]{1,0:T(8,128)(2,1)S(1)}, u32[]{:S(2)}, u32[]{:S(2)}) collective-permute-start(bf16[64,1024]{1,0:T(8,128)(2,1)S(1)} %collective-permute-done.4.refs_3_), channel_id=1, source_target_pairs={{0,2},{4,0},{8,4},{12,8},{14,12},{10,14},{6,10},{2,6},{1,3},{5,1},... | collective-permute-start | bytes 393224 | tf_op jit(solution)/shard_map/ppermute | solution.py:68
  12.1 8.4 %collective-permute-start.3 = (bf16[64,1152]{1,0:T(8,128)(2,1)S(1)}, bf16[64,1152]{1,0:T(8,128)(2,1)S(1)}, u32[]{:S(2)}, u32[]{:S(2)}) collective-permute-start(bf16[64,1152]{1,0:T(8,128)(2,1)S(1)} %get-tuple-element.64.refs_0_), channel_id=1, source_target_pairs={{0,2},{4,0},{8,4},{12,8},{14,12},{10,14},{6,10},{2,6},{1,3},{5,1},... | collective-permute-start | bytes 442376 | tf_op jit(solution)/shard_map/ppermute | solution.py:68
  13.9 8.2 %collective-permute-start.2 = (bf16[64,1024]{1,0:T(8,128)(2,1)S(1)}, bf16[64,1024]{1,0:T(8,128)(2,1)S(1)}, u32[]{:S(2)}, u32[]{:S(2)}) collective-permute-start(bf16[64,1024]{1,0:T(8,128)(2,1)S(1)} %get-tuple-element.65.refs_1_), channel_id=1, source_target_pairs={{0,4},{4,8},{8,12},{12,14},{14,10},{10,6},{6,2},{2,0},{1,5},{5,9},... | collective-permute-start | bytes 393224 | tf_op jit(solution)/shard_map/ppermute | solution.py:68
  16.2 6.4 %collective-permute-start.9 = (bf16[64,1152]{1,0:T(8,128)(2,1)S(1)}, bf16[64,1152]{1,0:T(8,128)(2,1)S(1)}, u32[]{:S(2)}, u32[]{:S(2)}) collective-permute-start(bf16[64,1152]{1,0:T(8,128)(2,1)S(1)} %collective-permute-done.5.refs_0_), channel_id=1, source_target_pairs={{0,4},{4,8},{8,12},{12,14},{14,10},{10,6},{6,2},{2,0},{1,5},{5,9},... | collective-permute-start | bytes 442376 | tf_op jit(solution)/shard_map/ppermute | solution.py:68
  20.6 9.2 %collective-permute-start.7 = (bf16[64,1152]{1,0:T(8,128)(2,1)S(1)}, bf16[64,1152]{1,0:T(8,128)(2,1)S(1)}, u32[]{:S(2)}, u32[]{:S(2)}) collective-permute-start(bf16[64,1152]{1,0:T(8,128)(2,1)S(1)} %collective-permute-done.3.refs_2_), channel_id=1, source_target_pairs={{0,2},{4,0},{8,4},{12,8},{14,12},{10,14},{6,10},{2,6},{1,3},{5,1},... | collective-permute-start | bytes 442376 | tf_op jit(solution)/shard_map/ppermute | solution.py:68
  22.1 7.7 %collective-permute-start.6 = (bf16[64,1024]{1,0:T(8,128)(2,1)S(1)}, bf16[64,1024]{1,0:T(8,128)(2,1)S(1)}, u32[]{:S(2)}, u32[]{:S(2)}) collective-permute-start(bf16[64,1024]{1,0:T(8,128)(2,1)S(1)} %collective-permute-done.2.refs_1_), channel_id=1, source_target_pairs={{0,4},{4,8},{8,12},{12,14},{14,10},{10,6},{6,2},{2,0},{1,5},{5,9},... | collective-permute-start | bytes 393224 | tf_op jit(solution)/shard_map/ppermute | solution.py:68
  22.6 9.2 %collective-permute-start.13 = (bf16[64,1152]{1,0:T(8,128)(2,1)S(1)}, bf16[64,1152]{1,0:T(8,128)(2,1)S(1)}, u32[]{:S(2)}, u32[]{:S(2)}) collective-permute-start(bf16[64,1152]{1,0:T(8,128)(2,1)S(1)} %collective-permute-done.9.refs_0_), channel_id=1, source_target_pairs={{0,4},{4,8},{8,12},{12,14},{14,10},{10,6},{6,2},{2,0},{1,5},{5,9},... | collective-permute-start | bytes 442376 | tf_op jit(solution)/shard_map/ppermute | solution.py:68
  32.8 6.9 %collective-permute-start.15 = (bf16[64,1024]{1,0:T(8,128)(2,1)S(1)}, bf16[64,1024]{1,0:T(8,128)(2,1)S(1)}, u32[]{:S(2)}, u32[]{:S(2)}) collective-permute-start(bf16[64,1024]{1,0:T(8,128)(2,1)S(1)} %get-tuple-element.73), channel_id=1, source_target_pairs={{0,4},{4,8},{8,12},{12,14},{14,10},{10,6},{6,2},{2,0},{1,5},{5,9},... | collective-permute-start | bytes 393224 | tf_op jit(solution)/shard_map/ppermute | solution.py:68
  34.4 7.2 %collective-permute-start.25 = (bf16[64,1024]{1,0:T(8,128)(2,1)S(1)}, bf16[64,1024]{1,0:T(8,128)(2,1)S(1)}, u32[]{:S(2)}, u32[]{:S(2)}) collective-permute-start(bf16[64,1024]{1,0:T(8,128)(2,1)S(1)} %get-tuple-element.84), channel_id=1, source_target_pairs={{0,2},{4,0},{8,4},{12,8},{14,12},{10,14},{6,10},{2,6},{1,3},{5,1},... | collective-permute-start | bytes 393224 | tf_op jit(solution)/shard_map/ppermute | solution.py:68
  45.8 6.8 %collective-permute-start.17 = (bf16[64,1024]{1,0:T(8,128)(2,1)S(1)}, bf16[64,1024]{1,0:T(8,128)(2,1)S(1)}, u32[]{:S(2)}, u32[]{:S(2)}) collective-permute-start(bf16[64,1024]{1,0:T(8,128)(2,1)S(1)} %shard_map.113), channel_id=1, source_target_pairs={{0,4},{4,8},{8,12},{12,14},{14,10},{10,6},{6,2},{2,0},{1,5},{5,9},... | collective-permute-start | bytes 393224 | tf_op jit(solution)/shard_map/ppermute | solution.py:68
  48.1 8.9 %collective-permute-start.27 = (bf16[64,1024]{1,0:T(8,128)(2,1)S(1)}, bf16[64,1024]{1,0:T(8,128)(2,1)S(1)}, u32[]{:S(2)}, u32[]{:S(2)}) collective-permute-start(bf16[64,1024]{1,0:T(8,128)(2,1)S(1)} %shard_map.121), channel_id=1, source_target_pairs={{0,2},{4,0},{8,4},{12,8},{14,12},{10,14},{6,10},{2,6},{1,3},{5,1},... | collective-permute-start | bytes 393224 | tf_op jit(solution)/shard_map/ppermute | solution.py:68
  49.7 8.4 %collective-permute-start.21 = (bf16[64,1024]{1,0:T(8,128)(2,1)S(1)}, bf16[64,1024]{1,0:T(8,128)(2,1)S(1)}, u32[]{:S(2)}, u32[]{:S(2)}) collective-permute-start(bf16[64,1024]{1,0:T(8,128)(2,1)S(1)} %shard_map.116), channel_id=1, source_target_pairs={{0,2},{4,0},{8,4},{12,8},{14,12},{10,14},{6,10},{2,6},{1,3},{5,1},... | collective-permute-start | bytes 393224 | tf_op jit(solution)/shard_map/ppermute | solution.py:68
  52.5 7.0 %collective-permute-start.18 = (bf16[64,1024]{1,0:T(8,128)(2,1)S(1)}, bf16[64,1024]{1,0:T(8,128)(2,1)S(1)}, u32[]{:S(2)}, u32[]{:S(2)}) collective-permute-start(bf16[64,1024]{1,0:T(8,128)(2,1)S(1)} %shard_map.114), channel_id=1, source_target_pairs={{0,4},{4,8},{8,12},{12,14},{14,10},{10,6},{6,2},{2,0},{1,5},{5,9},... | collective-permute-start | bytes 393224 | tf_op jit(solution)/shard_map/ppermute | solution.py:68
  55.0 7.1 %collective-permute-start.24 = (bf16[64,1024]{1,0:T(8,128)(2,1)S(1)}, bf16[64,1024]{1,0:T(8,128)(2,1)S(1)}, u32[]{:S(2)}, u32[]{:S(2)}) collective-permute-start(bf16[64,1024]{1,0:T(8,128)(2,1)S(1)} %shard_map.119), channel_id=1, source_target_pairs={{0,4},{4,8},{8,12},{12,14},{14,10},{10,6},{6,2},{2,0},{1,5},{5,9},... | collective-permute-start | bytes 393224 | tf_op jit(solution)/shard_map/ppermute | solution.py:68
  59.6 6.6 %collective-permute-start.29 = (bf16[64,1024]{1,0:T(8,128)(2,1)S(1)}, bf16[64,1024]{1,0:T(8,128)(2,1)S(1)}, u32[]{:S(2)}, u32[]{:S(2)}) collective-permute-start(bf16[64,1024]{1,0:T(8,128)(2,1)S(1)} %shard_map.117.refs_2_), channel_id=1, source_target_pairs={{0,4},{4,8},{8,12},{12,14},{14,10},{10,6},{6,2},{2,0},{1,5},{5,9},... | collective-permute-start | bytes 393224 | tf_op jit(solution)/shard_map/ppermute | solution.py:68
  64.2 8.0 %collective-permute-start.40 = (bf16[64,1024]{1,0:T(8,128)(2,1)S(1)}, bf16[64,1024]{1,0:T(8,128)(2,1)S(1)}, u32[]{:S(2)}, u32[]{:S(2)}) collective-permute-start(bf16[64,1024]{1,0:T(8,128)(2,1)S(1)} %shard_map.117.refs_2_), channel_id=1, source_target_pairs={{0,2},{4,0},{8,4},{12,8},{14,12},{10,14},{6,10},{2,6},{1,3},{5,1},... | collective-permute-start | bytes 393224 | tf_op jit(solution)/shard_map/ppermute | solution.py:68
  65.0 8.2 %collective-permute-start.37 = (bf16[64,1024]{1,0:T(8,128)(2,1)S(1)}, bf16[64,1024]{1,0:T(8,128)(2,1)S(1)}, u32[]{:S(2)}, u32[]{:S(2)}) collective-permute-start(bf16[64,1024]{1,0:T(8,128)(2,1)S(1)} %shard_map.123.refs_3_), channel_id=1, source_target_pairs={{0,4},{4,8},{8,12},{12,14},{14,10},{10,6},{6,2},{2,0},{1,5},{5,9},... | collective-permute-start | bytes 393224 | tf_op jit(solution)/shard_map/ppermute | solution.py:68
  66.2 8.0 %collective-permute-start.30 = (bf16[64,1024]{1,0:T(8,128)(2,1)S(1)}, bf16[64,1024]{1,0:T(8,128)(2,1)S(1)}, u32[]{:S(2)}, u32[]{:S(2)}) collective-permute-start(bf16[64,1024]{1,0:T(8,128)(2,1)S(1)} %collective-permute-done.29.refs_4_), channel_id=1, source_target_pairs={{0,4},{4,8},{8,12},{12,14},{14,10},{10,6},{6,2},{2,0},{1,5},{5,9},... | collective-permute-start | bytes 393224 | tf_op jit(solution)/shard_map/ppermute | solution.py:68
  110.9 8.3 %collective-permute-start.49 = (bf16[64,1024]{1,0:T(8,128)(2,1)S(1)}, bf16[64,1024]{1,0:T(8,128)(2,1)S(1)}, u32[]{:S(2)}, u32[]{:S(2)}) collective-permute-start(bf16[64,1024]{1,0:T(8,128)(2,1)S(1)} %shard_map.137), channel_id=1, source_target_pairs={{0,4},{4,8},{8,12},{12,14},{14,10},{10,6},{6,2},{2,0},{1,5},{5,9},... | collective-permute-start | bytes 393224 | tf_op jit(solution)/shard_map/ppermute | solution.py:68
  111.7 8.1 %collective-permute-start.59 = (bf16[64,1024]{1,0:T(8,128)(2,1)S(1)}, bf16[64,1024]{1,0:T(8,128)(2,1)S(1)}, u32[]{:S(2)}, u32[]{:S(2)}) collective-permute-start(bf16[64,1024]{1,0:T(8,128)(2,1)S(1)} %shard_map.144), channel_id=1, source_target_pairs={{0,2},{4,0},{8,4},{12,8},{14,12},{10,14},{6,10},{2,6},{1,3},{5,1},... | collective-permute-start | bytes 393224 | tf_op jit(solution)/shard_map/ppermute | solution.py:68
  115.1 8.7 %collective-permute-start.53 = (bf16[64,1024]{1,0:T(8,128)(2,1)S(1)}, bf16[64,1024]{1,0:T(8,128)(2,1)S(1)}, u32[]{:S(2)}, u32[]{:S(2)}) collective-permute-start(bf16[64,1024]{1,0:T(8,128)(2,1)S(1)} %shard_map.140), channel_id=1, source_target_pairs={{0,2},{4,0},{8,4},{12,8},{14,12},{10,14},{6,10},{2,6},{1,3},{5,1},... | collective-permute-start | bytes 393224 | tf_op jit(solution)/shard_map/ppermute | solution.py:68
  116.8 7.0 %collective-permute-start.56 = (bf16[64,1024]{1,0:T(8,128)(2,1)S(1)}, bf16[64,1024]{1,0:T(8,128)(2,1)S(1)}, u32[]{:S(2)}, u32[]{:S(2)}) collective-permute-start(bf16[64,1024]{1,0:T(8,128)(2,1)S(1)} %shard_map.142), channel_id=1, source_target_pairs={{0,4},{4,8},{8,12},{12,14},{14,10},{10,6},{6,2},{2,0},{1,5},{5,9},... | collective-permute-start | bytes 393224 | tf_op jit(solution)/shard_map/ppermute | solution.py:68
  (41 other events, 348.3 us)

commit v25 on v16

--- a/solution.py
+++ b/solution.py
@@ -490,11 +490,24 @@
     for distances in reversed(list(tokens_at)):
         backward(distances)
     (top_left, top_right), (bottom_left, bottom_right) = ring.scatter(back_at)
+
+    def last_kernel(*refs):
+        out_hbm, rows_ref, sems = refs[-3:]
+        copies = Copies(sems)
+        for i in range(2):
+            own, left, right = refs[3 * i : 3 * i + 3]
+            some = pl.ds(i * mid, mid)
+            arrived = left[...].astype(F32) + right[...].astype(F32)
+            rows_ref[some, :] = (own[...] + arrived).astype(BF16)
+            copies.start(rows_ref.at[some, :], out_hbm.at[some, :])
+        copies.wait()
+
     token_grad = pl.pallas_call(
-        sum_kernel,
+        last_kernel,
         out_shape=jax.ShapeDtypeStruct(block, BF16),
         in_specs=[pl.BlockSpec(memory_space=pltpu.VMEM)] * 6,
-        out_specs=pl.BlockSpec(memory_space=pltpu.VMEM),
+        out_specs=pl.BlockSpec(memory_space=pl.ANY),
+        scratch_shapes=[pltpu.VMEM(block, BF16), pltpu.SemaphoreType.DMA((2,))],
         compiler_params=pltpu.CompilerParams(vmem_limit_bytes=VMEM_LIMIT),
     )(back_at[0][0], top_left, top_right, back_at[0][1], bottom_left, bottom_right)
     return (token_grad, head_grad)

time: 123 us -> 123 us (level)
  no operation moved by 1% of the time
where the time goes in v25:
time: 123 us
  starting transfers between devices  69.1 us (56%)
  waiting for transfers between devices  29.2 us (24%)
  Pallas kernels  21.8 us (18%)
  matrix products  1.71 us (1%)
  between operations  1.24 us (1%)
    ppermute x56, starting transfers between devices, send(): return lax.ppermute(value, 'expert', pairs)  62.6 us
    ppermute x56, waiting for transfers between devices, send(): return lax.ppermute(value, 'expert', pairs)  25.8 us
    pallas_call x39, Pallas kernels, call(): pl.pallas_call(kernel, out_shape=[pltpu.VMEM(shape, dtype) for shape, dty...  17.4 us
    ppermute x4, starting transfers between devices, body(): pooled_grad = pooled_grad + lax.ppermute(mine, 'expert', pairs).astype(F32)  5.95 us
    ppermute x4, waiting for transfers between devices, body(): pooled_grad = pooled_grad + lax.ppermute(mine, 'expert', pairs).astype(F32)  3.43 us
  transfers between devices with their start and end apart: 62, of which 28 were waited for; matrix products, arithmetic and copies ran while one was open for 1% of the time, Pallas kernels for 14%

profile of v25, /device:TPU:0, one launch (start us, length us, event | category | flops | bytes accessed | tf_op | source)
XLA Modules:
  0.0 123.1 jit_solution(16996272934563485369)
XLA Ops:
  0.6 1.9 %shard_map.104 = (bf16[64,1152]{1,0:T(8,128)(2,1)S(1)}, bf16[64,1024]{1,0:T(8,128)(2,1)S(1)}, bf16[3200,384]{1,0:T(8,128)(2,1)S(1)}) custom-call(s32[8,128]{1,0:T(8,128)} %bitcast.19, f32[8,128]{1,0:T(8,128)} %bitcast.20, bf16[128,1024]{1,0:T(8,128)(2,1)} %refs_2_.2, bf16[2,512,384]{2,1,0:T(8,128)(2,1)} %refs_0_.1, bf16[2,512,384]{2,1,0:T(8,128)(2,1)} %refs_1_.1, ...), custom_call_target="tpu_custom_call" | custom-call | tf_op jit(solution)/shard_map/pallas_call | solution.py:215
  3.1 2.6 %collective-permute-start.1 = (bf16[64,1152]{1,0:T(8,128)(2,1)S(1)}, bf16[64,1152]{1,0:T(8,128)(2,1)S(1)}, u32[]{:S(2)}, u32[]{:S(2)}) collective-permute-start(bf16[64,1152]{1,0:T(8,128)(2,1)S(1)} %get-tuple-element.64.refs_0_), channel_id=1, source_target_pairs={{0,4},{4,8},{8,12},{12,14},{14,10},{10,6},{6,2},{2,0},{1,5},{5,9},... | collective-permute-start | bytes 442376 | tf_op jit(solution)/shard_map/ppermute | solution.py:68
  5.7 4.4 %collective-permute-done.1.refs_0_ = bf16[64,1152]{1,0:T(8,128)(2,1)S(1)} collective-permute-done((bf16[64,1152]{1,0:T(8,128)(2,1)S(1)}, bf16[64,1152]{1,0:T(8,128)(2,1)S(1)}, u32[]{:S(2)}, u32[]{:S(2)}) %collective-permute-start.1) | collective-permute-done | bytes 147488 | tf_op jit(solution)/shard_map/ppermute | solution.py:68
  10.1 1.8 %collective-permute-start.5 = (bf16[64,1152]{1,0:T(8,128)(2,1)S(1)}, bf16[64,1152]{1,0:T(8,128)(2,1)S(1)}, u32[]{:S(2)}, u32[]{:S(2)}) collective-permute-start(bf16[64,1152]{1,0:T(8,128)(2,1)S(1)} %collective-permute-done.1.refs_0_), channel_id=1, source_target_pairs={{0,4},{4,8},{8,12},{12,14},{14,10},{10,6},{6,2},{2,0},{1,5},{5,9},... | collective-permute-start | bytes 442376 | tf_op jit(solution)/shard_map/ppermute | solution.py:68
  12.1 1.7 %collective-permute-start.3 = (bf16[64,1152]{1,0:T(8,128)(2,1)S(1)}, bf16[64,1152]{1,0:T(8,128)(2,1)S(1)}, u32[]{:S(2)}, u32[]{:S(2)}) collective-permute-start(bf16[64,1152]{1,0:T(8,128)(2,1)S(1)} %get-tuple-element.64.refs_0_), channel_id=1, source_target_pairs={{0,2},{4,0},{8,4},{12,8},{14,12},{10,14},{6,10},{2,6},{1,3},{5,1},... | collective-permute-start | bytes 442376 | tf_op jit(solution)/shard_map/ppermute | solution.py:68
  14.2 2.0 %collective-permute-done.5.refs_0_ = bf16[64,1152]{1,0:T(8,128)(2,1)S(1)} collective-permute-done((bf16[64,1152]{1,0:T(8,128)(2,1)S(1)}, bf16[64,1152]{1,0:T(8,128)(2,1)S(1)}, u32[]{:S(2)}, u32[]{:S(2)}) %collective-permute-start.5) | collective-permute-done | bytes 147488 | tf_op jit(solution)/shard_map/ppermute | solution.py:68
  16.2 2.5 %collective-permute-start.9 = (bf16[64,1152]{1,0:T(8,128)(2,1)S(1)}, bf16[64,1152]{1,0:T(8,128)(2,1)S(1)}, u32[]{:S(2)}, u32[]{:S(2)}) collective-permute-start(bf16[64,1152]{1,0:T(8,128)(2,1)S(1)} %collective-permute-done.5.refs_0_), channel_id=1, source_target_pairs={{0,4},{4,8},{8,12},{12,14},{14,10},{10,6},{6,2},{2,0},{1,5},{5,9},... | collective-permute-start | bytes 442376 | tf_op jit(solution)/shard_map/ppermute | solution.py:68
  18.7 2.6 %collective-permute-done.3.refs_2_ = bf16[64,1152]{1,0:T(8,128)(2,1)S(1)} collective-permute-done((bf16[64,1152]{1,0:T(8,128)(2,1)S(1)}, bf16[64,1152]{1,0:T(8,128)(2,1)S(1)}, u32[]{:S(2)}, u32[]{:S(2)}) %collective-permute-start.3) | collective-permute-done | bytes 147488 | tf_op jit(solution)/shard_map/ppermute | solution.py:68
  21.4 1.9 %collective-permute-start.6 = (bf16[64,1024]{1,0:T(8,128)(2,1)S(1)}, bf16[64,1024]{1,0:T(8,128)(2,1)S(1)}, u32[]{:S(2)}, u32[]{:S(2)}) collective-permute-start(bf16[64,1024]{1,0:T(8,128)(2,1)S(1)} %collective-permute-done.2.refs_1_), channel_id=1, source_target_pairs={{0,4},{4,8},{8,12},{12,14},{14,10},{10,6},{6,2},{2,0},{1,5},{5,9},... | collective-permute-start | bytes 393224 | tf_op jit(solution)/shard_map/ppermute | solution.py:68
  23.3 1.8 %collective-permute-start.13 = (bf16[64,1152]{1,0:T(8,128)(2,1)S(1)}, bf16[64,1152]{1,0:T(8,128)(2,1)S(1)}, u32[]{:S(2)}, u32[]{:S(2)}) collective-permute-start(bf16[64,1152]{1,0:T(8,128)(2,1)S(1)} %collective-permute-done.9.refs_0_), channel_id=1, source_target_pairs={{0,4},{4,8},{8,12},{12,14},{14,10},{10,6},{6,2},{2,0},{1,5},{5,9},... | collective-permute-start | bytes 442376 | tf_op jit(solution)/shard_map/ppermute | solution.py:68
  25.3 1.9 %collective-permute-done.7.refs_2_ = bf16[64,1152]{1,0:T(8,128)(2,1)S(1)} collective-permute-done((bf16[64,1152]{1,0:T(8,128)(2,1)S(1)}, bf16[64,1152]{1,0:T(8,128)(2,1)S(1)}, u32[]{:S(2)}, u32[]{:S(2)}) %collective-permute-start.7) | collective-permute-done | bytes 147488 | tf_op jit(solution)/shard_map/ppermute | solution.py:68
  27.3 1.8 %shard_map.105 = (bf16[1024,1536]{1,0:T(8,128)(2,1)S(1)}, bf16[768,1024]{1,0:T(8,128)(2,1)S(1)}) custom-call(bf16[2,512,384]{2,1,0:T(8,128)(2,1)} %refs_0_.1, bf16[2,512,384]{2,1,0:T(8,128)(2,1)} %refs_1_.1, bf16[2,192,1024]{2,1,0:T(8,128)(2,1)} %refs_2_.3, bf16[3200,384]{1,0:T(8,128)(2,1)S(1)} %collective-permute-done.refs_3_), custom_call_target="tpu_custom_call" | custom-call | tf_op jit(solution)/shard_map/pallas_call | solution.py:270
  32.2 1.6 %collective-permute-start.15 = (bf16[64,1024]{1,0:T(8,128)(2,1)S(1)}, bf16[64,1024]{1,0:T(8,128)(2,1)S(1)}, u32[]{:S(2)}, u32[]{:S(2)}) collective-permute-start(bf16[64,1024]{1,0:T(8,128)(2,1)S(1)} %get-tuple-element.73), channel_id=1, source_target_pairs={{0,4},{4,8},{8,12},{12,14},{14,10},{10,6},{6,2},{2,0},{1,5},{5,9},... | collective-permute-start | bytes 393224 | tf_op jit(solution)/shard_map/ppermute | solution.py:68
  48.2 1.7 %collective-permute-start.27 = (bf16[64,1024]{1,0:T(8,128)(2,1)S(1)}, bf16[64,1024]{1,0:T(8,128)(2,1)S(1)}, u32[]{:S(2)}, u32[]{:S(2)}) collective-permute-start(bf16[64,1024]{1,0:T(8,128)(2,1)S(1)} %shard_map.121), channel_id=1, source_target_pairs={{0,2},{4,0},{8,4},{12,8},{14,12},{10,14},{6,10},{2,6},{1,3},{5,1},... | collective-permute-start | bytes 393224 | tf_op jit(solution)/shard_map/ppermute | solution.py:68
  51.6 2.1 %collective-permute-start.18 = (bf16[64,1024]{1,0:T(8,128)(2,1)S(1)}, bf16[64,1024]{1,0:T(8,128)(2,1)S(1)}, u32[]{:S(2)}, u32[]{:S(2)}) collective-permute-start(bf16[64,1024]{1,0:T(8,128)(2,1)S(1)} %shard_map.114), channel_id=1, source_target_pairs={{0,4},{4,8},{8,12},{12,14},{14,10},{10,6},{6,2},{2,0},{1,5},{5,9},... | collective-permute-start | bytes 393224 | tf_op jit(solution)/shard_map/ppermute | solution.py:68
  54.3 2.1 %collective-permute-start.28 = (bf16[64,1024]{1,0:T(8,128)(2,1)S(1)}, bf16[64,1024]{1,0:T(8,128)(2,1)S(1)}, u32[]{:S(2)}, u32[]{:S(2)}) collective-permute-start(bf16[64,1024]{1,0:T(8,128)(2,1)S(1)} %shard_map.122), channel_id=1, source_target_pairs={{0,2},{4,0},{8,4},{12,8},{14,12},{10,14},{6,10},{2,6},{1,3},{5,1},... | collective-permute-start | bytes 393224 | tf_op jit(solution)/shard_map/ppermute | solution.py:68
  57.9 2.1 %collective-permute-start.29 = (bf16[64,1024]{1,0:T(8,128)(2,1)S(1)}, bf16[64,1024]{1,0:T(8,128)(2,1)S(1)}, u32[]{:S(2)}, u32[]{:S(2)}) collective-permute-start(bf16[64,1024]{1,0:T(8,128)(2,1)S(1)} %shard_map.117.refs_2_), channel_id=1, source_target_pairs={{0,4},{4,8},{8,12},{12,14},{14,10},{10,6},{6,2},{2,0},{1,5},{5,9},... | collective-permute-start | bytes 393224 | tf_op jit(solution)/shard_map/ppermute | solution.py:68
  64.3 2.2 %collective-permute-start.30 = (bf16[64,1024]{1,0:T(8,128)(2,1)S(1)}, bf16[64,1024]{1,0:T(8,128)(2,1)S(1)}, u32[]{:S(2)}, u32[]{:S(2)}) collective-permute-start(bf16[64,1024]{1,0:T(8,128)(2,1)S(1)} %collective-permute-done.29.refs_4_), channel_id=1, source_target_pairs={{0,4},{4,8},{8,12},{12,14},{14,10},{10,6},{6,2},{2,0},{1,5},{5,9},... | collective-permute-start | bytes 393224 | tf_op jit(solution)/shard_map/ppermute | solution.py:68
  69.7 1.7 %collective-permute-start.41 = (bf16[64,1024]{1,0:T(8,128)(2,1)S(1)}, bf16[64,1024]{1,0:T(8,128)(2,1)S(1)}, u32[]{:S(2)}, u32[]{:S(2)}) collective-permute-start(bf16[64,1024]{1,0:T(8,128)(2,1)S(1)} %collective-permute-done.40.refs_6_), channel_id=1, source_target_pairs={{0,2},{4,0},{8,4},{12,8},{14,12},{10,14},{6,10},{2,6},{1,3},{5,1},... | collective-permute-start | bytes 393224 | tf_op jit(solution)/shard_map/ppermute | solution.py:68
  74.6 1.8 %collective-permute-start.42 = (bf16[64,1024]{1,0:T(8,128)(2,1)S(1)}, bf16[64,1024]{1,0:T(8,128)(2,1)S(1)}, u32[]{:S(2)}, u32[]{:S(2)}) collective-permute-start(bf16[64,1024]{1,0:T(8,128)(2,1)S(1)} %collective-permute-done.41.refs_6_), channel_id=1, source_target_pairs={{0,2},{4,0},{8,4},{12,8},{14,12},{10,14},{6,10},{2,6},{1,3},{5,1},... | collective-permute-start | bytes 393224 | tf_op jit(solution)/shard_map/ppermute | solution.py:68
  78.4 1.6 %collective-permute-start.36 = (bf16[64,1024]{1,0:T(8,128)(2,1)S(1)}, bf16[64,1024]{1,0:T(8,128)(2,1)S(1)}, u32[]{:S(2)}, u32[]{:S(2)}) collective-permute-start(bf16[64,1024]{1,0:T(8,128)(2,1)S(1)} %collective-permute-done.35.refs_7_), channel_id=1, source_target_pairs={{0,2},{4,0},{8,4},{12,8},{14,12},{10,14},{6,10},{2,6},{1,3},{5,1},... | collective-permute-start | bytes 393224 | tf_op jit(solution)/shard_map/ppermute | solution.py:68
  85.7 2.3 %collective-permute-done.43 = bf16[8,1024]{1,0:T(8,128)(2,1)S(1)} collective-permute-done((bf16[8,1024]{1,0:T(8,128)(2,1)S(1)}, bf16[8,1024]{1,0:T(8,128)(2,1)S(1)}, u32[]{:S(2)}, u32[]{:S(2)}) %collective-permute-start.43) | collective-permute-done | bytes 16416 | tf_op jit(solution)/shard_map/ppermute | solution.py:435
  87.9 2.8 %collective-permute-start.46 = (bf16[8,1024]{1,0:T(8,128)(2,1)S(1)}, bf16[8,1024]{1,0:T(8,128)(2,1)S(1)}, u32[]{:S(2)}, u32[]{:S(2)}) collective-permute-start(bf16[8,1024]{1,0:T(8,128)(2,1)S(1)} %add_convert_fusion), channel_id=1, source_target_pairs={{0,12},{2,14},{4,8},{6,10},{8,4},{10,6},{12,0},{14,2},{1,13},{3,15... | collective-permute-start | bytes 49160 | tf_op jit(solution)/shard_map/ppermute | solution.py:435
  90.7 1.6 %collective-permute-start.44 = (bf16[8,1024]{1,0:T(8,128)(2,1)S(1)}, bf16[8,1024]{1,0:T(8,128)(2,1)S(1)}, u32[]{:S(2)}, u32[]{:S(2)}) collective-permute-start(bf16[8,1024]{1,0:T(8,128)(2,1)S(1)} %add_convert_fusion), channel_id=1, source_target_pairs={{0,4},{2,6},{4,0},{6,2},{8,12},{10,14},{12,8},{14,10},{1,5},{3,7},... | collective-permute-start | bytes 49160 | tf_op jit(solution)/shard_map/ppermute | solution.py:435
  (159 shorter events, 71.4 us)
Async XLA Ops:
  2.6 24.7 %collective-permute-start = (bf16[3200,384]{1,0:T(8,128)(2,1)S(1)}, bf16[3200,384]{1,0:T(8,128)(2,1)S(1)}, u32[]{:S(2)}, u32[]{:S(2)}) collective-permute-start(bf16[3200,384]{1,0:T(8,128)(2,1)S(1)} %get-tuple-element.66), channel_id=1, source_target_pairs={{0,1},{1,0},{2,3},{3,2},{4,5},{5,4},{6,7},{7,6},{8,9},{9,8},{10,11... | collective-permute-start | bytes 7372808 | tf_op jit(solution)/shard_map/ppermute | solution.py:310
  3.1 7.0 %collective-permute-start.1 = (bf16[64,1152]{1,0:T(8,128)(2,1)S(1)}, bf16[64,1152]{1,0:T(8,128)(2,1)S(1)}, u32[]{:S(2)}, u32[]{:S(2)}) collective-permute-start(bf16[64,1152]{1,0:T(8,128)(2,1)S(1)} %get-tuple-element.64.refs_0_), channel_id=1, source_target_pairs={{0,4},{4,8},{8,12},{12,14},{14,10},{10,6},{6,2},{2,0},{1,5},{5,9},... | collective-permute-start | bytes 442376 | tf_op jit(solution)/shard_map/ppermute | solution.py:68
  11.9 6.8 %collective-permute-start.8 = (bf16[64,1024]{1,0:T(8,128)(2,1)S(1)}, bf16[64,1024]{1,0:T(8,128)(2,1)S(1)}, u32[]{:S(2)}, u32[]{:S(2)}) collective-permute-start(bf16[64,1024]{1,0:T(8,128)(2,1)S(1)} %collective-permute-done.4.refs_3_), channel_id=1, source_target_pairs={{0,2},{4,0},{8,4},{12,8},{14,12},{10,14},{6,10},{2,6},{1,3},{5,1},... | collective-permute-start | bytes 393224 | tf_op jit(solution)/shard_map/ppermute | solution.py:68
  12.1 9.1 %collective-permute-start.3 = (bf16[64,1152]{1,0:T(8,128)(2,1)S(1)}, bf16[64,1152]{1,0:T(8,128)(2,1)S(1)}, u32[]{:S(2)}, u32[]{:S(2)}) collective-permute-start(bf16[64,1152]{1,0:T(8,128)(2,1)S(1)} %get-tuple-element.64.refs_0_), channel_id=1, source_target_pairs={{0,2},{4,0},{8,4},{12,8},{14,12},{10,14},{6,10},{2,6},{1,3},{5,1},... | collective-permute-start | bytes 442376 | tf_op jit(solution)/shard_map/ppermute | solution.py:68
  13.9 7.6 %collective-permute-start.2 = (bf16[64,1024]{1,0:T(8,128)(2,1)S(1)}, bf16[64,1024]{1,0:T(8,128)(2,1)S(1)}, u32[]{:S(2)}, u32[]{:S(2)}) collective-permute-start(bf16[64,1024]{1,0:T(8,128)(2,1)S(1)} %get-tuple-element.65.refs_1_), channel_id=1, source_target_pairs={{0,4},{4,8},{8,12},{12,14},{14,10},{10,6},{6,2},{2,0},{1,5},{5,9},... | collective-permute-start | bytes 393224 | tf_op jit(solution)/shard_map/ppermute | solution.py:68
  16.2 7.1 %collective-permute-start.9 = (bf16[64,1152]{1,0:T(8,128)(2,1)S(1)}, bf16[64,1152]{1,0:T(8,128)(2,1)S(1)}, u32[]{:S(2)}, u32[]{:S(2)}) collective-permute-start(bf16[64,1152]{1,0:T(8,128)(2,1)S(1)} %collective-permute-done.5.refs_0_), channel_id=1, source_target_pairs={{0,4},{4,8},{8,12},{12,14},{14,10},{10,6},{6,2},{2,0},{1,5},{5,9},... | collective-permute-start | bytes 442376 | tf_op jit(solution)/shard_map/ppermute | solution.py:68
  21.4 8.2 %collective-permute-start.6 = (bf16[64,1024]{1,0:T(8,128)(2,1)S(1)}, bf16[64,1024]{1,0:T(8,128)(2,1)S(1)}, u32[]{:S(2)}, u32[]{:S(2)}) collective-permute-start(bf16[64,1024]{1,0:T(8,128)(2,1)S(1)} %collective-permute-done.2.refs_1_), channel_id=1, source_target_pairs={{0,4},{4,8},{8,12},{12,14},{14,10},{10,6},{6,2},{2,0},{1,5},{5,9},... | collective-permute-start | bytes 393224 | tf_op jit(solution)/shard_map/ppermute | solution.py:68
  23.3 7.8 %collective-permute-start.13 = (bf16[64,1152]{1,0:T(8,128)(2,1)S(1)}, bf16[64,1152]{1,0:T(8,128)(2,1)S(1)}, u32[]{:S(2)}, u32[]{:S(2)}) collective-permute-start(bf16[64,1152]{1,0:T(8,128)(2,1)S(1)} %collective-permute-done.9.refs_0_), channel_id=1, source_target_pairs={{0,4},{4,8},{8,12},{12,14},{14,10},{10,6},{6,2},{2,0},{1,5},{5,9},... | collective-permute-start | bytes 442376 | tf_op jit(solution)/shard_map/ppermute | solution.py:68
  32.2 6.4 %collective-permute-start.15 = (bf16[64,1024]{1,0:T(8,128)(2,1)S(1)}, bf16[64,1024]{1,0:T(8,128)(2,1)S(1)}, u32[]{:S(2)}, u32[]{:S(2)}) collective-permute-start(bf16[64,1024]{1,0:T(8,128)(2,1)S(1)} %get-tuple-element.73), channel_id=1, source_target_pairs={{0,4},{4,8},{8,12},{12,14},{14,10},{10,6},{6,2},{2,0},{1,5},{5,9},... | collective-permute-start | bytes 393224 | tf_op jit(solution)/shard_map/ppermute | solution.py:68
  33.8 8.0 %collective-permute-start.25 = (bf16[64,1024]{1,0:T(8,128)(2,1)S(1)}, bf16[64,1024]{1,0:T(8,128)(2,1)S(1)}, u32[]{:S(2)}, u32[]{:S(2)}) collective-permute-start(bf16[64,1024]{1,0:T(8,128)(2,1)S(1)} %get-tuple-element.84), channel_id=1, source_target_pairs={{0,2},{4,0},{8,4},{12,8},{14,12},{10,14},{6,10},{2,6},{1,3},{5,1},... | collective-permute-start | bytes 393224 | tf_op jit(solution)/shard_map/ppermute | solution.py:68
  36.3 7.5 %collective-permute-start.19 = (bf16[64,1024]{1,0:T(8,128)(2,1)S(1)}, bf16[64,1024]{1,0:T(8,128)(2,1)S(1)}, u32[]{:S(2)}, u32[]{:S(2)}) collective-permute-start(bf16[64,1024]{1,0:T(8,128)(2,1)S(1)} %get-tuple-element.76), channel_id=1, source_target_pairs={{0,2},{4,0},{8,4},{12,8},{14,12},{10,14},{6,10},{2,6},{1,3},{5,1},... | collective-permute-start | bytes 393224 | tf_op jit(solution)/shard_map/ppermute | solution.py:68
  40.2 7.5 %collective-permute-start.22 = (bf16[64,1024]{1,0:T(8,128)(2,1)S(1)}, bf16[64,1024]{1,0:T(8,128)(2,1)S(1)}, u32[]{:S(2)}, u32[]{:S(2)}) collective-permute-start(bf16[64,1024]{1,0:T(8,128)(2,1)S(1)} %get-tuple-element.80), channel_id=1, source_target_pairs={{0,4},{4,8},{8,12},{12,14},{14,10},{10,6},{6,2},{2,0},{1,5},{5,9},... | collective-permute-start | bytes 393224 | tf_op jit(solution)/shard_map/ppermute | solution.py:68
  43.9 7.6 %collective-permute-start.20 = (bf16[64,1024]{1,0:T(8,128)(2,1)S(1)}, bf16[64,1024]{1,0:T(8,128)(2,1)S(1)}, u32[]{:S(2)}, u32[]{:S(2)}) collective-permute-start(bf16[64,1024]{1,0:T(8,128)(2,1)S(1)} %shard_map.115), channel_id=1, source_target_pairs={{0,2},{4,0},{8,4},{12,8},{14,12},{10,14},{6,10},{2,6},{1,3},{5,1},... | collective-permute-start | bytes 393224 | tf_op jit(solution)/shard_map/ppermute | solution.py:68
  45.0 6.5 %collective-permute-start.17 = (bf16[64,1024]{1,0:T(8,128)(2,1)S(1)}, bf16[64,1024]{1,0:T(8,128)(2,1)S(1)}, u32[]{:S(2)}, u32[]{:S(2)}) collective-permute-start(bf16[64,1024]{1,0:T(8,128)(2,1)S(1)} %shard_map.113), channel_id=1, source_target_pairs={{0,4},{4,8},{8,12},{12,14},{14,10},{10,6},{6,2},{2,0},{1,5},{5,9},... | collective-permute-start | bytes 393224 | tf_op jit(solution)/shard_map/ppermute | solution.py:68
  47.8 6.4 %collective-permute-start.23 = (bf16[64,1024]{1,0:T(8,128)(2,1)S(1)}, bf16[64,1024]{1,0:T(8,128)(2,1)S(1)}, u32[]{:S(2)}, u32[]{:S(2)}) collective-permute-start(bf16[64,1024]{1,0:T(8,128)(2,1)S(1)} %shard_map.118), channel_id=1, source_target_pairs={{0,4},{4,8},{8,12},{12,14},{14,10},{10,6},{6,2},{2,0},{1,5},{5,9},... | collective-permute-start | bytes 393224 | tf_op jit(solution)/shard_map/ppermute | solution.py:68
  54.2 6.5 %collective-permute-start.24 = (bf16[64,1024]{1,0:T(8,128)(2,1)S(1)}, bf16[64,1024]{1,0:T(8,128)(2,1)S(1)}, u32[]{:S(2)}, u32[]{:S(2)}) collective-permute-start(bf16[64,1024]{1,0:T(8,128)(2,1)S(1)} %shard_map.119), channel_id=1, source_target_pairs={{0,4},{4,8},{8,12},{12,14},{14,10},{10,6},{6,2},{2,0},{1,5},{5,9},... | collective-permute-start | bytes 393224 | tf_op jit(solution)/shard_map/ppermute | solution.py:68
  54.3 6.4 %collective-permute-start.28 = (bf16[64,1024]{1,0:T(8,128)(2,1)S(1)}, bf16[64,1024]{1,0:T(8,128)(2,1)S(1)}, u32[]{:S(2)}, u32[]{:S(2)}) collective-permute-start(bf16[64,1024]{1,0:T(8,128)(2,1)S(1)} %shard_map.122), channel_id=1, source_target_pairs={{0,2},{4,0},{8,4},{12,8},{14,12},{10,14},{6,10},{2,6},{1,3},{5,1},... | collective-permute-start | bytes 393224 | tf_op jit(solution)/shard_map/ppermute | solution.py:68
  62.2 7.4 %collective-permute-start.40 = (bf16[64,1024]{1,0:T(8,128)(2,1)S(1)}, bf16[64,1024]{1,0:T(8,128)(2,1)S(1)}, u32[]{:S(2)}, u32[]{:S(2)}) collective-permute-start(bf16[64,1024]{1,0:T(8,128)(2,1)S(1)} %shard_map.117.refs_2_), channel_id=1, source_target_pairs={{0,2},{4,0},{8,4},{12,8},{14,12},{10,14},{6,10},{2,6},{1,3},{5,1},... | collective-permute-start | bytes 393224 | tf_op jit(solution)/shard_map/ppermute | solution.py:68
  63.3 8.2 %collective-permute-start.37 = (bf16[64,1024]{1,0:T(8,128)(2,1)S(1)}, bf16[64,1024]{1,0:T(8,128)(2,1)S(1)}, u32[]{:S(2)}, u32[]{:S(2)}) collective-permute-start(bf16[64,1024]{1,0:T(8,128)(2,1)S(1)} %shard_map.123.refs_3_), channel_id=1, source_target_pairs={{0,4},{4,8},{8,12},{12,14},{14,10},{10,6},{6,2},{2,0},{1,5},{5,9},... | collective-permute-start | bytes 393224 | tf_op jit(solution)/shard_map/ppermute | solution.py:68
  64.3 8.2 %collective-permute-start.30 = (bf16[64,1024]{1,0:T(8,128)(2,1)S(1)}, bf16[64,1024]{1,0:T(8,128)(2,1)S(1)}, u32[]{:S(2)}, u32[]{:S(2)}) collective-permute-start(bf16[64,1024]{1,0:T(8,128)(2,1)S(1)} %collective-permute-done.29.refs_4_), channel_id=1, source_target_pairs={{0,4},{4,8},{8,12},{12,14},{14,10},{10,6},{6,2},{2,0},{1,5},{5,9},... | collective-permute-start | bytes 393224 | tf_op jit(solution)/shard_map/ppermute | solution.py:68
  108.3 7.8 %collective-permute-start.49 = (bf16[64,1024]{1,0:T(8,128)(2,1)S(1)}, bf16[64,1024]{1,0:T(8,128)(2,1)S(1)}, u32[]{:S(2)}, u32[]{:S(2)}) collective-permute-start(bf16[64,1024]{1,0:T(8,128)(2,1)S(1)} %shard_map.137), channel_id=1, source_target_pairs={{0,4},{4,8},{8,12},{12,14},{14,10},{10,6},{6,2},{2,0},{1,5},{5,9},... | collective-permute-start | bytes 393224 | tf_op jit(solution)/shard_map/ppermute | solution.py:68
  109.2 8.0 %collective-permute-start.59 = (bf16[64,1024]{1,0:T(8,128)(2,1)S(1)}, bf16[64,1024]{1,0:T(8,128)(2,1)S(1)}, u32[]{:S(2)}, u32[]{:S(2)}) collective-permute-start(bf16[64,1024]{1,0:T(8,128)(2,1)S(1)} %shard_map.144), channel_id=1, source_target_pairs={{0,2},{4,0},{8,4},{12,8},{14,12},{10,14},{6,10},{2,6},{1,3},{5,1},... | collective-permute-start | bytes 393224 | tf_op jit(solution)/shard_map/ppermute | solution.py:68
  112.5 8.3 %collective-permute-start.53 = (bf16[64,1024]{1,0:T(8,128)(2,1)S(1)}, bf16[64,1024]{1,0:T(8,128)(2,1)S(1)}, u32[]{:S(2)}, u32[]{:S(2)}) collective-permute-start(bf16[64,1024]{1,0:T(8,128)(2,1)S(1)} %shard_map.140), channel_id=1, source_target_pairs={{0,2},{4,0},{8,4},{12,8},{14,12},{10,14},{6,10},{2,6},{1,3},{5,1},... | collective-permute-start | bytes 393224 | tf_op jit(solution)/shard_map/ppermute | solution.py:68
  113.8 7.0 %collective-permute-start.56 = (bf16[64,1024]{1,0:T(8,128)(2,1)S(1)}, bf16[64,1024]{1,0:T(8,128)(2,1)S(1)}, u32[]{:S(2)}, u32[]{:S(2)}) collective-permute-start(bf16[64,1024]{1,0:T(8,128)(2,1)S(1)} %shard_map.142), channel_id=1, source_target_pairs={{0,4},{4,8},{8,12},{12,14},{14,10},{10,6},{6,2},{2,0},{1,5},{5,9},... | collective-permute-start | bytes 393224 | tf_op jit(solution)/shard_map/ppermute | solution.py:68
  (41 other events, 349.5 us)
